TPU v7x, 32 devices: a whole 2x2x4 slice. The times are simulated.
32 devices in a mesh: dp: 8 (over y, x, core), mp: 4 (over z).
Axes of the slice: x: 2, y: 2, z: 4, core: 2. Of those that a mesh axis runs over, the one named last changes fastest.
Arguments:
- replica_grads: bfloat16 [8, 512, 12288], P('dp', None, 'mp'), may hold values from -320 to 320
- owners: int32 [4, 6], P('mp'), may hold values from 0 to 7, as said below
- left_stats: float32 [8, 512, 2048], P('dp', None, 'mp'), may hold values from -1 to 5, as said below
- right_stats: float32 [8, 512, 2048], P('dp', None, 'mp'), may hold values from -1 to 5, as said below
Outputs:
- update: float32 [512, 12288], P(None, 'mp')
Inputs may be any that keep to these rules, and one draw needn't show every extreme that they name: `owners`: within one row no replica owns more than 1 block, and some replica owns exactly 1. `left_stats`: each slot's 512 x 512 block is symmetric and diagonally dominant with a positive diagonal; slots that no block names are unused. `right_stats`: each slot's 512 x 512 block is symmetric and diagonally dominant with a positive diagonal; slots that no block names are unused.
All inputs are finite; a program needn't handle non-finite values.
Results may differ from a plain program's by a relative error of at most 0.0003.
Values sent between devices are 32-bit elements; how exact they have to be, the bound alone decides.
No kernel may reach another device: no remote copies, remote signals or barrier semaphores. Data moves between devices by JAX's collectives and lax.ppermute only.
A program may use at most 64 MiB of HBM per device.

v0:
```python
import jax
import jax.numpy as jnp
from jax import lax
from jax.sharding import PartitionSpec as P

clip_level = 1.0
graft_eps = 1e-06


def mat_product(left_side, right_side):
    return jnp.matmul(left_side, right_side, precision=lax.Precision.HIGHEST)


def inverse_root(statistic):
    order_size = statistic.shape[-1]
    identity = jnp.eye(order_size, dtype=jnp.float32)
    frobenius = jnp.sqrt(jnp.sum(statistic * statistic, axis=(-2, -1), keepdims=True))
    scaled = statistic / frobenius
    factor = (5.0 * identity - scaled) * 0.25
    root = factor * frobenius ** (-0.25)
    square = mat_product(factor, factor)
    fourth = mat_product(square, square)
    scaled = mat_product(fourth, scaled)
    factor = (5.0 * identity - scaled) * 0.25
    root = mat_product(root, factor)
    return root


def block_update(block, left_prev, right_prev):
    order_size = block.shape[-1]
    transposed = jnp.swapaxes(block, -1, -2)
    left = 0.5 * left_prev + mat_product(block, transposed) / order_size
    right = 0.5 * right_prev + mat_product(transposed, block) / order_size
    pre = mat_product(mat_product(inverse_root(left), block), inverse_root(right))
    block_norm = jnp.sum(block * block, axis=(-2, -1), keepdims=True)
    pre_norm = jnp.sum(pre * pre, axis=(-2, -1), keepdims=True)
    return pre * jnp.sqrt(block_norm / (pre_norm + graft_eps))


def body(replica_grads, owners, left_stats, right_stats):
    width = left_stats.shape[1]
    slots = left_stats.shape[0]
    owner_row = owners[0]
    block_count = owner_row.shape[0]
    replica = lax.axis_index("dp")
    positions = jnp.arange(block_count, dtype=jnp.int32)
    matching = owner_row[:, None] == owner_row[None, :]
    earlier = positions[:, None] > positions[None, :]
    slot_rank = jnp.sum((matching & earlier).astype(jnp.int32), axis=1)
    slot_ids = jnp.arange(slots, dtype=jnp.int32)
    selector = ((owner_row[None, :] == replica) & (slot_rank[None, :] == slot_ids[:, None])).astype(
        jnp.float32
    )
    entry_count = width * block_count * width * lax.axis_size("mp")
    replica_count = lax.axis_size("dp")
    share_rows = width // replica_count
    local_grads = replica_grads[0]
    share = lax.psum_scatter(local_grads.astype(jnp.float32), "dp", scatter_dimension=0, tiled=True)
    squares = lax.psum(jnp.sum(share * share), ("dp", "mp"))
    clip_factor = jnp.minimum(1.0, clip_level / jnp.sqrt(squares / entry_count))
    share_blocks = jnp.transpose(share.reshape(share_rows, block_count, width), (1, 0, 2))
    targets = jnp.arange(replica_count, dtype=jnp.int32)
    routing = (
        (owner_row[None, None, :] == targets[:, None, None])
        & (slot_rank[None, None, :] == slot_ids[None, :, None])
    ).astype(jnp.float32)
    outgoing = jnp.einsum("dsb,brc->drsc", routing, share_blocks, precision=lax.Precision.HIGHEST)
    arrived = lax.all_to_all(outgoing, "dp", split_axis=0, concat_axis=1, tiled=True)
    mine = jnp.transpose(arrived[0], (1, 0, 2)) * clip_factor
    updates = block_update(mine, left_stats, right_stats)
    placed = jnp.sum(selector[:, :, None, None] * updates[:, None], axis=0)
    whole = lax.psum(placed, "dp")
    result = jnp.transpose(whole, (1, 0, 2)).reshape(width, block_count * width)
    return result


def solution(mesh):
    return jax.shard_map(
        body,
        mesh=mesh,
        in_specs=(P("dp", None, "mp"), P("mp", None), P("dp", None, "mp"), P("dp", None, "mp")),
        out_specs=P(None, "mp"),
        check_vma=False,
    )
```

profile of v0, /device:TPU:0, one launch (start us, length us, event | category | flops | bytes accessed | tf_op | source)
XLA Modules:
  0.0 284.4 jit_solution(1265977245198350391)
XLA Ops:
  6.5 5.4 %bitcast_convert_fusion = f32[512,3072]{1,0:T(8,128)} fusion(bf16[1,512,3072]{2,1,0:T(8,128)(2,1)} %param.4), kind=kLoop, calls=%fused_computation | loop fusion | flops 1572864 | bytes 9437184 | tf_op jit(solution)/shard_map/convert_element_type | solution.py:58
  11.9 0.0 reduce-scatter.2.cloned.1.call-update
  12.0 0.0 copy-start.1
  12.0 0.2 convert_reduce_fusion
  12.2 64.4 %reduce-scatter.2.cloned.1.call-done = f32[64,3072]{1,0:T(8,128)} async-done(((f32[512,3072]{1,0:T(8,128)}), f32[64,3072]{1,0:T(8,128)}) %reduce-scatter.2.cloned.1.call-update) | async-done | bytes 786448 | tf_op jit(solution)/shard_map/reduce_scatter | solution.py:58
  76.6 1.6 reshape.158
  78.2 0.6 convolution_bitcast_fusion
  78.8 1.6 copy.13
  80.4 3.6 %all-to-all-start = ((f32[8,64,1,512]{3,1,2,0:T(8,128)}), f32[8,64,1,512]{3,1,2,0:T(8,128)S(1)}, u32[]{:S(2)}, u32[]{:S(2)}) async-start(f32[8,64,1,512]{3,1,2,0:T(8,128)} %copy.13), calls=%async_computation.1 | async-start | bytes 2097152 | tf_op jit(solution)/shard_map/all_to_all | solution.py:68
  84.0 0.0 all-reduce.2.cloned.1.call-start
  84.0 0.9 multiply_reduce_fusion.4
  84.9 47.6 %psum.14 = f32[]{:T(128)} all-reduce(f32[]{:T(128)} %multiply_reduce_fusion.4), channel_id=1, replica_groups=mesh['dp'=8,'mp'=4] {'dp','mp'}, use_global_device_ids=true, to_apply=%region_3.0 | all-reduce | flops 1 | bytes 8 | tf_op jit(solution)/shard_map/psum | solution.py:59
  133.3 1.0 multiply_reduce_fusion.1
  134.3 2.6 multiply_reduce_fusion.2
  137.6 2.0 fusion.7
  139.6 1.8 fusion.53
  141.5 2.9 %fusion.3 = f32[512,512]{1,0:T(8,128)} fusion(f32[512,512]{1,0:T(8,128)S(1)} %fusion.53, f32[1,512,512]{2,1,0:T(8,128)S(1)} %get-tuple-element.10, f32[]{:T(128)S(6)} %sqrt.17), kind=kOutput, calls=%fused_computation.12 | convolution fusion | flops 1611923456 | bytes 3145732 | tf_op jit(solution)/shard_map/dot_general | solution.py:11
  144.3 2.6 multiply_reduce_fusion.3
  147.6 2.0 fusion.12
  149.6 2.1 fusion.51
  151.7 0.0 copy-start.4
  151.7 1.9 fusion.2
  153.6 2.0 fusion.14
  155.5 1.8 fusion.52
  157.4 2.0 fusion.9
  159.4 2.6 multiply_reduce_fusion
  163.3 0.1 broadcast_multiply_fusion.1
  163.4 0.3 copy.15
  163.8 3.7 %broadcast_multiply_fusion = f32[6,512,512]{1,2,0:T(8,128)} fusion(f32[512,512]{0,1:T(8,128)S(1)} %copy.15, f32[6]{0:T(128)S(1)} %fusion.40), kind=kLoop, calls=%fused_computation.1 | loop fusion | flops 1572864 | bytes 7340056 | tf_op jit(solution)/shard_map/mul | solution.py:71
  167.5 0.0 all-reduce.2.cloned.1.call-update
  167.5 103.5 %all-reduce.2.cloned.1.call-done = f32[512,3072]{0,1:T(8,128)} async-done(((f32[512,3072]{0,1:T(8,128)}), f32[512,3072]{0,1:T(8,128)}) %all-reduce.2.cloned.1.call-update) | async-done | bytes 6291472 | tf_op jit(solution)/shard_map/psum | solution.py:72
  271.0 6.6 %copy.16 = f32[512,3072]{1,0:T(8,128)} copy(f32[512,3072]{0,1:T(8,128)} %all-reduce.2.cloned.1.call-done) | data formatting | bytes 12582912 | tf_op jit(solution)/shard_map/psum | solution.py:72
  (12 shorter events, 0.0 us)
Async XLA Ops:
  6.5 5.4 %copy-start.3 = (s32[1,6]{1,0:T(1,128)S(1)}, s32[1,6]{1,0:T(1,128)}, u32[]{:S(2)}) copy-start(s32[1,6]{1,0:T(1,128)} %param.5) | copy-start | bytes 76
  6.5 70.0 %reduce-scatter.2.cloned.1.call-start = ((), (), s32[]{:S(2)}) async-start(), calls=%async_computation.2 | async-start | bytes 7077888 | tf_op jit(solution)/shard_map/reduce_scatter | solution.py:58
  12.0 122.3 %copy-start.1 = (f32[1,512,512]{2,1,0:T(8,128)S(1)}, f32[1,512,512]{2,1,0:T(8,128)}, u32[]{:S(2)}) copy-start(f32[1,512,512]{2,1,0:T(8,128)} %param.7) | copy-start | bytes 3145732
  76.6 7.4 %copy-start = (f32[64,3072]{1,0:T(8,128)S(1)}, f32[64,3072]{1,0:T(8,128)}, u32[]{:S(2)}) copy-start(f32[64,3072]{1,0:T(8,128)} %reduce-scatter.2.cloned.1.call-done) | copy-start | bytes 2359300
  80.4 52.9 %all-to-all-start = ((f32[8,64,1,512]{3,1,2,0:T(8,128)}), f32[8,64,1,512]{3,1,2,0:T(8,128)S(1)}, u32[]{:S(2)}, u32[]{:S(2)}) async-start(f32[8,64,1,512]{3,1,2,0:T(8,128)} %copy.13), calls=%async_computation.1 | async-start | bytes 2097152 | tf_op jit(solution)/shard_map/all_to_all | solution.py:68
  84.0 187.1 %all-reduce.2.cloned.1.call-start = ((), (), s32[]{:S(2)}) async-start(), calls=%async_computation.3 | async-start | bytes 12582912 | tf_op jit(solution)/shard_map/psum | solution.py:72
  137.6 6.7 %copy-start.2 = (f32[1,512,512]{2,1,0:T(8,128)S(1)}, f32[1,512,512]{2,1,0:T(8,128)}, u32[]{:S(2)}) copy-start(f32[1,512,512]{2,1,0:T(8,128)} %param.6) | copy-start | bytes 3145732
  151.7 5.7 %copy-start.4 = (f32[512,512]{1,0:T(8,128)S(1)}, f32[512,512]{1,0:T(8,128)}, u32[]{:S(2)}) copy-start(f32[512,512]{1,0:T(8,128)} %fusion.3) | copy-start | bytes 3145732
Sparse Core Ops, SparseCore 0:
  12.1 64.4 reduce-scatter.1
  167.6 103.3 all-reduce.1
where the time goes:
time: 285 us; the launch traced here: 284 us
  waiting for transfers between devices  168 us (59%)
  blocking collectives  47.6 us (17%)
  matrix products  26.8 us (9%)
  between operations  17.1 us (6%)
  other arithmetic  11.2 us (4%)
  local copies, waits for them, and re-layouts  10.1 us (4%)
  starting transfers between devices  3.6 us (1%)
    psum x1, waiting for transfers between devices, body(): whole = lax.psum(placed, 'dp')  104 us
    reduce_scatter x1, waiting for transfers between devices, body(): lax.psum_scatter(local_grads.astype(jnp.float32), 'dp', scatter_dimension...  64.4 us
    psum x1, blocking collectives, body(): squares = lax.psum(jnp.sum(share * share), ('dp', 'mp'))  47.6 us
    dot_general x12, matrix products, mat_product(): return jnp.matmul(left_side, right_side, precision=lax.Precision.HIGHEST)  26.2 us
    psum x1, local copies, waits for them, and re-layouts, body(): whole = lax.psum(placed, 'dp')  6.56 us
  transfers between devices with their start and end apart: 3, of which 2 were waited for; matrix products, arithmetic and copies ran while one was open for 0% of the time, Pallas kernels for 0%

commit v1 on v0

v1 whole, which is shorter than its diff:
```python
import jax
import jax.numpy as jnp
from jax import lax
from jax.sharding import PartitionSpec as P

clip_level = 1.0
graft_eps = 1e-06


def mat_product(left_side, right_side):
    return jnp.matmul(left_side, right_side, precision=lax.Precision.HIGH)


def inverse_root(statistic):
    order_size = statistic.shape[-1]
    identity = jnp.eye(order_size, dtype=jnp.float32)
    frobenius = jnp.sqrt(jnp.sum(statistic * statistic))
    scaled = statistic / frobenius
    square = mat_product(scaled, scaled)
    factor_square = (25.0 * identity - 10.0 * scaled + square) * 0.0625
    factor_scaled = (5.0 * scaled - square) * 0.25
    fourth = mat_product(factor_square, factor_square)
    tail = mat_product(fourth, factor_scaled)
    return (6.25 * identity - 1.25 * scaled - tail) * (0.25 * frobenius ** (-0.25))


def general_body(replica_grads, owners, left_stats, right_stats):
    width = left_stats.shape[1]
    owner_row = owners[0]
    block_count = owner_row.shape[0]
    replica = lax.axis_index("dp")
    replica_count = lax.axis_size("dp")
    entry_count = width * block_count * width * lax.axis_size("mp")
    share_rows = width // replica_count
    share = lax.psum_scatter(
        replica_grads[0].astype(jnp.float32), "dp", scatter_dimension=0, tiled=True
    )
    squares = lax.psum(jnp.sum(share * share), ("dp", "mp"))
    clip_factor = jnp.minimum(1.0, clip_level / jnp.sqrt(squares / entry_count))
    share_blocks = jnp.transpose(share.reshape(share_rows, block_count, width), (1, 0, 2))
    targets = jnp.arange(replica_count, dtype=jnp.int32)
    routing = (owner_row[None, :] == targets[:, None]).astype(jnp.float32)
    outgoing = jnp.einsum("db,brc->drc", routing, share_blocks, precision=lax.Precision.HIGHEST)
    arrived = lax.all_to_all(outgoing, "dp", split_axis=0, concat_axis=0, tiled=True)
    block = arrived.reshape(width, width) * clip_factor
    update = block_update(block, jnp.sum(block * block), 1.0, left_stats[0], right_stats[0])
    chosen = (owner_row == replica).astype(jnp.float32)
    whole = lax.psum(chosen[:, None, None] * update[None], "dp")
    return jnp.transpose(whole, (1, 0, 2)).reshape(width, block_count * width)


def block_update(block, block_norm, clip_factor, left_prev, right_prev):
    order_size = block.shape[-1]
    stat_scale = clip_factor * clip_factor / order_size
    transposed = block.T
    left = 0.5 * left_prev + mat_product(block, transposed) * stat_scale
    right = 0.5 * right_prev + mat_product(transposed, block) * stat_scale
    pre = mat_product(mat_product(inverse_root(left), block), inverse_root(right)) * clip_factor
    pre_norm = jnp.sum(pre * pre)
    return pre * (clip_factor * jnp.sqrt(block_norm / (pre_norm + graft_eps)))


def paired_body(replica_grads, owners, left_stats, right_stats):
    width = left_stats.shape[1]
    owner_row = owners[0]
    block_count = owner_row.shape[0]
    me = lax.axis_index("dp")
    core = me & 1
    entry_count = width * block_count * width * lax.axis_size("mp")
    grads = replica_grads[0]
    matches = (owner_row[None, :] == jnp.arange(8, dtype=jnp.int32)[:, None]).astype(jnp.int32)
    owned = jnp.sum(matches, axis=1)
    block_of = jnp.sum(matches * jnp.arange(block_count, dtype=jnp.int32)[None, :], axis=1)

    first_pairs = [(i, i ^ (2 if i % 2 == 0 else 4)) for i in range(8)]
    second_pairs = [(i, i ^ (4 if i % 2 == 0 else 2)) for i in range(8)]
    core_pairs = [(i, i ^ 1) for i in range(8)]

    def over(pairs, value):
        return lax.ppermute(value, "dp", pairs)

    def target(slot, device):
        device_core = device & 1
        first = jnp.where(device_core == 0, 2, 4)
        second = 6 - first
        return device ^ ((slot >> 1) * first) ^ ((slot & 1) * second)

    def own_piece(device_target):
        column = block_of[device_target] * width
        return lax.dynamic_slice(grads, (0, column), (width, width)).astype(jnp.float32)

    sums = {}
    for slot in (3, 2, 1, 0):
        arrived = over(core_pairs, own_piece(target(slot, me ^ 1)))
        sums[slot] = arrived + own_piece(target(slot, me))
    sum_one = sums[1] + over(first_pairs, sums[3])
    sum_zero = sums[0] + over(first_pairs, sums[2])
    block = sum_zero + over(second_pairs, sum_one)

    block_norm = jnp.sum(block * block)
    mine = owned[me] > 0
    squares = lax.psum(jnp.where(mine, block_norm, 0.0), ("dp", "mp"))
    clip_factor = jnp.minimum(1.0, clip_level / jnp.sqrt(squares / entry_count))
    update = block_update(block, block_norm, clip_factor, left_stats[0], right_stats[0])

    mine_near = over(second_pairs, update)
    mine_far = over(first_pairs, update)
    near_far = over(first_pairs, mine_near)
    held = [update, mine_near, mine_far, near_far]
    slots = held + [over(core_pairs, value) for value in held]
    places = jnp.stack(
        [target(slot, me) for slot in range(4)] + [target(slot, me ^ 1) for slot in range(4)]
    )
    stacked = jnp.stack(slots)
    pieces = []
    for index in range(block_count):
        place = jnp.argmax(places == owner_row[index])
        pieces.append(lax.dynamic_index_in_dim(stacked, place, 0, keepdims=False))
    return jnp.concatenate(pieces, axis=1)


def solution(mesh):
    return jax.shard_map(
        paired_body if mesh.shape["dp"] == 8 else general_body,
        mesh=mesh,
        in_specs=(P("dp", None, "mp"), P("mp", None), P("dp", None, "mp"), P("dp", None, "mp")),
        out_specs=P(None, "mp"),
        check_vma=False,
    )
```

time: 285 us -> 205 us (0.72)
  waiting for transfers between devices: 168 us -> 50.9 us
  local copies, waits for them, and re-layouts: 10.1 us -> 36.1 us
  starting transfers between devices: 3.6 us -> 15.5 us
  other arithmetic: 11.2 us -> 21.9 us
  matrix products: 26.8 us -> 18.3 us
  blocking collectives: 47.6 us -> 39.9 us
  between operations: 17.1 us -> 21.2 us
    psum x1 -> x0, waiting for transfers between devices: 104 us -> none  [body(): whole = lax.psum(placed, 'dp')]
    reduce_scatter x1 -> x0, waiting for transfers between devices: 64.4 us -> none  [body(): lax.psum_scatter(local_grads.astype(jnp.float32), 'dp', scatter_dimension...]
    ppermute x0 -> x14, waiting for transfers between devices: none -> 50.9 us  [over(): return lax.ppermute(value, 'dp', pairs)]
    unnamed x10 -> x29, local copies, waits for them, and re-layouts: 0.03 us -> 16.7 us
    dynamic_slice x0 -> x9, local copies, waits for them, and re-layouts: none -> 16.5 us  [the longest x7 15.1 us: paired_body(): pieces.append(lax.dynamic_index_in_dim(stacked, place, 0, keepdims=False))]
    ppermute x0 -> x14, starting transfers between devices: none -> 15.5 us  [over(): return lax.ppermute(value, 'dp', pairs)]
    dot_general x13 -> x10, matrix products: 26.8 us -> 18.3 us  [mat_product(): return jnp.matmul(left_side, right_side, precision=lax.Precision.HIGH)]
    another operation x0 -> x6, other arithmetic: none -> 8.21 us  [paired_body(): place = jnp.argmax(places == owner_row[index])]
  transfers between devices with their start and end apart: 3 -> 14, of which waited for: 2 -> 4; matrix products, arithmetic and copies ran while one was open for 0% -> 12% of each run, Pallas kernels for 0% -> 0%
where the time goes in v1:
time: 205 us; the launch traced here: 204 us
  waiting for transfers between devices  50.9 us (25%)
  blocking collectives  39.9 us (19%)
  local copies, waits for them, and re-layouts  36.1 us (18%)
  other arithmetic  21.9 us (11%)
  between operations  21.2 us (10%)
  matrix products  18.3 us (9%)
  starting transfers between devices  15.5 us (8%)
    ppermute x14, waiting for transfers between devices, over(): return lax.ppermute(value, 'dp', pairs)  50.9 us
    psum x1, blocking collectives, paired_body(): squares = lax.psum(jnp.where(mine, block_norm, 0.0), ('dp', 'mp'))  39.9 us
    dot_general x10, matrix products, mat_product(): return jnp.matmul(left_side, right_side, precision=lax.Precision.HIGH)  18.3 us
    unnamed x29, local copies, waits for them, and re-layouts  16.7 us
    ppermute x14, starting transfers between devices, over(): return lax.ppermute(value, 'dp', pairs)  15.5 us
    dynamic_slice x7, local copies, waits for them, and re-layouts, paired_body(): pieces.append(lax.dynamic_index_in_dim(stacked, place, 0, keepdims=False))  15.1 us
    another operation x6, other arithmetic, paired_body(): place = jnp.argmax(places == owner_row[index])  8.21 us
    add x2, other arithmetic, paired_body(): sums[slot] = arrived + own_piece(target(slot, me))  5.12 us
  transfers between devices with their start and end apart: 14, of which 4 were waited for; matrix products, arithmetic and copies ran while one was open for 12% of the time, Pallas kernels for 0%

profile of v1, /device:TPU:0, one launch (start us, length us, event | category | flops | bytes accessed | tf_op | source)
XLA Modules:
  0.0 203.7 jit_solution(14605709249596197983)
XLA Ops:
  4.1 3.4 %bitcast_convert_fusion.3 = (f32[512,512]{1,0:T(8,128)}, f32[512,512]{1,0:T(8,128)}, f32[512,512]{1,0:T(8,128)}, f32[512,512]{1,0:T(8,128)S(1)}) fusion(bf16[1,512,3072]{2,1,0:T(8,128)(2,1)} %param.4, s32[]{:T(128)S(6)} %select_n.104, s32[]{:T(128)S(6)} %select_n.114, s32[]{:T(128)S(6)} %select_n.109, s32[]{:T(128)S(6)} %select_n.118), kind=kLoop, calls=%fused_computation.56 | loop fusion | flops 1048576 | bytes 6291472 | tf_op jit(solution)/shard_map/convert_element_type | solution.py:90
  9.1 2.0 collective-permute-done.4
  12.3 3.5 %collective-permute-start.5 = (f32[512,512]{1,0:T(8,128)S(1)}, f32[512,512]{1,0:T(8,128)}, u32[]{:S(2)}, u32[]{:S(2)}) collective-permute-start(f32[512,512]{1,0:T(8,128)S(1)} %convert_add_fusion), channel_id=1, source_target_pairs={{0,8},{4,20},{8,0},{12,28},{16,24},{20,4},{24,16},{28,12},{1,9},{5... | collective-permute-start | bytes 3145736 | tf_op jit(solution)/shard_map/ppermute | solution.py:80
  17.2 11.5 %collective-permute-done.5 = f32[512,512]{1,0:T(8,128)} collective-permute-done((f32[512,512]{1,0:T(8,128)S(1)}, f32[512,512]{1,0:T(8,128)}, u32[]{:S(2)}, u32[]{:S(2)}) %collective-permute-start.5) | collective-permute-done | bytes 1048608 | tf_op jit(solution)/shard_map/ppermute | solution.py:80
  28.7 3.9 %convert_add_fusion.2 = (f32[512,512]{1,0:T(8,128)}, f32[512,512]{1,0:T(8,128)}) fusion(f32[512,512]{1,0:T(8,128)} %collective-permute-done.1, bf16[1,512,3072]{2,1,0:T(8,128)(2,1)} %param.4, s32[]{:T(128)S(6)} %select_n.112, f32[512,512]{1,0:T(8,128)} %collective-permute-done.5, f32[512,512]{1,0:T(8,128)} %collective-permute-done.3, s32[]{:T(128)S(6)} %select_n.116), kind=kLoop, calls=%fused_computation.22 | loop fusion | flops 1310720 | bytes 6291464 | tf_op jit(solution)/shard_map/add | solution.py:95
  32.7 2.0 collective-permute-start.2
  34.7 1.5 collective-permute-start.6
  38.2 20.7 %collective-permute-done.2 = f32[512,512]{1,0:T(8,128)} collective-permute-done((f32[512,512]{1,0:T(8,128)}, f32[512,512]{1,0:T(8,128)}, u32[]{:S(2)}, u32[]{:S(2)}) %collective-permute-start.2) | collective-permute-done | bytes 1048608 | tf_op jit(solution)/shard_map/ppermute | solution.py:80
  58.9 3.1 %multiply_reduce_fusion.3 = (f32[]{:T(128)}, f32[512,512]{1,0:T(8,128)S(1)}) fusion(f32[512,512]{1,0:T(8,128)} %collective-permute-done.6, f32[512,512]{1,0:T(8,128)} %collective-permute-done.2, f32[512,512]{1,0:T(8,128)} %copy-done.2, bf16[1,512,3072]{2,1,0:T(8,128)(2,1)} %param.4, s32[]{:T(128)S(6)} %select_n.106), kind=kLoop, calls=%fused_computation.51 | loop fusion | flops 1572863 | bytes 4718600 | tf_op jit(solution)/shard_map/reduce_sum | solution.py:100
  62.6 39.9 %psum.7 = f32[]{:T(128)} all-reduce(f32[]{:T(128)S(6)} %select_n.121), channel_id=1, replica_groups=mesh['dp'=8,'mp'=4] {'dp','mp'}, use_global_device_ids=true, to_apply=%region_3.4 | all-reduce | flops 1 | bytes 8 | tf_op jit(solution)/shard_map/psum | solution.py:102
  103.2 2.7 %multiply_reduce_fusion.1 = (f32[]{:T(128)}, f32[512,512]{1,0:T(8,128)}) fusion(f32[]{:T(128)S(6)} %div.23, f32[512,512]{1,0:T(8,128)S(1)} %get-tuple-element.22, f32[1,512,512]{2,1,0:T(8,128)S(1)} %copy-done), kind=kOutput, calls=%fused_computation.45 | convolution fusion | flops 806617088 | bytes 3145736 | tf_op jit(solution)/shard_map/dot_general | solution.py:11
  106.8 2.6 %fusion.48 = f32[512,512]{1,0:T(8,128)S(1)} fusion(f32[512,512]{1,0:T(8,128)} %get-tuple-element.52, f32[]{:T(128)S(6)} %sqrt.14), kind=kOutput, calls=%fused_computation.100 | convolution fusion | flops 805568512 | bytes 2097156 | tf_op jit(solution)/shard_map/dot_general | solution.py:11
  110.4 3.8 %fusion.10 = f32[512,512]{1,0:T(8,128)} fusion(f32[512,512]{1,0:T(8,128)S(1)} %fusion.48, f32[512,512]{1,0:T(8,128)} %get-tuple-element.52, f32[]{:T(128)S(6)} %sqrt.14), kind=kOutput, calls=%fused_computation.18 | convolution fusion | flops 807141376 | bytes 3145732 | tf_op jit(solution)/shard_map/dot_general | solution.py:11
  114.2 1.8 multiply_reduce_fusion.2
  122.4 1.8 multiply_reduce_fusion
  126.7 2.5 %collective-permute-start.7 = (f32[512,512]{0,1:T(8,128)S(1)}, f32[512,512]{0,1:T(8,128)S(1)}, u32[]{:S(2)}, u32[]{:S(2)}) collective-permute-start(f32[512,512]{0,1:T(8,128)S(1)} %get-tuple-element.20), channel_id=1, source_target_pairs={{0,16},{4,12},{8,24},{12,4},{16,0},{20,28},{24,8},{28,20},{1,17},{... | collective-permute-start | bytes 3145736 | tf_op jit(solution)/shard_map/ppermute | solution.py:80
  130.0 1.3 compare_reduce_fusion
  131.3 1.5 collective-permute-start.8
  132.8 1.4 compare_reduce_fusion.2
  134.2 1.5 compare_reduce_fusion.3
  135.7 16.7 %collective-permute-done.7 = f32[512,512]{0,1:T(8,128)S(1)} collective-permute-done((f32[512,512]{0,1:T(8,128)S(1)}, f32[512,512]{0,1:T(8,128)S(1)}, u32[]{:S(2)}, u32[]{:S(2)}) %collective-permute-start.7) | collective-permute-done | bytes 1048608 | tf_op jit(solution)/shard_map/ppermute | solution.py:80
  152.4 2.4 %collective-permute-start.9 = (f32[512,512]{0,1:T(8,128)S(1)}, f32[512,512]{0,1:T(8,128)}, u32[]{:S(2)}, u32[]{:S(2)}) collective-permute-start(f32[512,512]{0,1:T(8,128)S(1)} %collective-permute-done.7), channel_id=1, source_target_pairs={{0,8},{4,20},{8,0},{12,28},{16,24},{20,4},{24,16},{28,12},{1,9},{5... | collective-permute-start | bytes 3145736 | tf_op jit(solution)/shard_map/ppermute | solution.py:80
  154.8 1.3 compare_reduce_fusion.4
  163.5 1.3 compare_reduce_fusion.1
  172.9 2.3 %bitcast_dynamic-update-slice_fusion.10 = f32[8,512,512]{1,2,0:T(8,128)} fusion(f32[8,512,512]{1,2,0:T(8,128)} %bitcast_dynamic-update-slice_fusion.11, f32[512,512]{0,1:T(8,128)} %collective-permute-done.9), kind=kLoop, calls=%fused_computation.36 | loop fusion | bytes 2097152
  175.2 2.3 %bitcast_dynamic-update-slice_fusion.9 = f32[8,512,512]{1,2,0:T(8,128)} fusion(f32[8,512,512]{1,2,0:T(8,128)} %bitcast_dynamic-update-slice_fusion.10, f32[512,512]{0,1:T(8,128)} %collective-permute-done.10), kind=kLoop, calls=%fused_computation.35 | loop fusion | bytes 2097152
  180.7 5.2 %constant_dynamic-slice_fusion = (f32[1,512,512]{1,2,0:T(8,128)S(1)}, f32[1,512,512]{1,2,0:T(8,128)S(1)}, f32[1,512,512]{1,2,0:T(8,128)}, f32[1,512,512]{1,2,0:T...) fusion(f32[8,512,512]{1,2,0:T(8,128)} %bitcast_dynamic-update-slice_fusion.6, s32[]{:T(128)S(6)} %select_n.127, ...), kind=kLoop, calls=%fused_computation.75 | loop fusion | bytes 12582936 | tf_op jit(solution)/shard_map/jit(dynamic_index_in_dim)/dynamic_slice | solution.py:118
  186.6 1.6 copy.14
  188.2 2.6 %copy.13 = f32[1,512,512]{2,1,0:T(8,128)} copy(f32[1,512,512]{1,2,0:T(8,128)} %get-tuple-element.26) | data formatting | bytes 2097152 | tf_op jit(solution)/shard_map/jit(dynamic_index_in_dim)/dynamic_slice | solution.py:118
  190.7 2.6 %copy.12 = f32[1,512,512]{2,1,0:T(8,128)} copy(f32[1,512,512]{1,2,0:T(8,128)} %get-tuple-element.27) | data formatting | bytes 2097152 | tf_op jit(solution)/shard_map/jit(dynamic_index_in_dim)/dynamic_slice | solution.py:118
  193.3 2.5 %copy.11 = f32[1,512,512]{2,1,0:T(8,128)} copy(f32[1,512,512]{1,2,0:T(8,128)} %get-tuple-element.28) | data formatting | bytes 2097152 | tf_op jit(solution)/shard_map/jit(dynamic_index_in_dim)/dynamic_slice | solution.py:118
  200.0 2.7 %copy-done.4 = f32[512,3072]{1,0:T(8,128)} copy-done((f32[512,3072]{1,0:T(8,128)}, f32[512,3072]{1,0:T(8,128)S(1)}, u32[]{:S(2)}) %copy-start.4) | copy-done | bytes 6291480
  (61 shorter events, 26.6 us)
Async XLA Ops:
  7.5 95.7 %copy-start = (f32[1,512,512]{2,1,0:T(8,128)S(1)}, f32[1,512,512]{2,1,0:T(8,128)}, u32[]{:S(2)}) copy-start(f32[1,512,512]{2,1,0:T(8,128)} %param.7) | copy-start | bytes 3145732
  7.5 3.6 %collective-permute-start.4 = (f32[512,512]{1,0:T(8,128)S(1)}, f32[512,512]{1,0:T(8,128)S(1)}, u32[]{:S(2)}, u32[]{:S(2)}) collective-permute-start(f32[512,512]{1,0:T(8,128)S(1)} %get-tuple-element.32), channel_id=1, source_target_pairs={{0,4},{4,0},{8,12},{12,8},{16,20},{20,16},{24,28},{28,24},{1,5},{5... | collective-permute-start | bytes 3145736 | tf_op jit(solution)/shard_map/ppermute | solution.py:80
  8.0 9.2 %collective-permute-start.3 = (f32[512,512]{1,0:T(8,128)}, f32[512,512]{1,0:T(8,128)}, u32[]{:S(2)}, u32[]{:S(2)}) collective-permute-start(f32[512,512]{1,0:T(8,128)} %get-tuple-element.30), channel_id=1, source_target_pairs={{0,4},{4,0},{8,12},{12,8},{16,20},{20,16},{24,28},{28,24},{1,5},{5... | collective-permute-start | bytes 3145736 | tf_op jit(solution)/shard_map/ppermute | solution.py:80
  8.0 9.2 %collective-permute-start.1 = (f32[512,512]{1,0:T(8,128)}, f32[512,512]{1,0:T(8,128)}, u32[]{:S(2)}, u32[]{:S(2)}) collective-permute-start(f32[512,512]{1,0:T(8,128)} %get-tuple-element.31), channel_id=1, source_target_pairs={{0,4},{4,0},{8,12},{12,8},{16,20},{20,16},{24,28},{28,24},{1,5},{5... | collective-permute-start | bytes 3145736 | tf_op jit(solution)/shard_map/ppermute | solution.py:80
  12.3 16.4 %collective-permute-start.5 = (f32[512,512]{1,0:T(8,128)S(1)}, f32[512,512]{1,0:T(8,128)}, u32[]{:S(2)}, u32[]{:S(2)}) collective-permute-start(f32[512,512]{1,0:T(8,128)S(1)} %convert_add_fusion), channel_id=1, source_target_pairs={{0,8},{4,20},{8,0},{12,28},{16,24},{20,4},{24,16},{28,12},{1,9},{5... | collective-permute-start | bytes 3145736 | tf_op jit(solution)/shard_map/ppermute | solution.py:80
  15.8 22.4 %collective-permute-start = (f32[512,512]{1,0:T(8,128)}, f32[512,512]{1,0:T(8,128)S(1)}, u32[]{:S(2)}, u32[]{:S(2)}) collective-permute-start(f32[512,512]{1,0:T(8,128)} %get-tuple-element.29), channel_id=1, source_target_pairs={{0,4},{4,0},{8,12},{12,8},{16,20},{20,16},{24,28},{28,24},{1,5},{5... | collective-permute-start | bytes 3145736 | tf_op jit(solution)/shard_map/ppermute | solution.py:80
  32.7 26.3 %collective-permute-start.2 = (f32[512,512]{1,0:T(8,128)}, f32[512,512]{1,0:T(8,128)}, u32[]{:S(2)}, u32[]{:S(2)}) collective-permute-start(f32[512,512]{1,0:T(8,128)} %get-tuple-element.33), channel_id=1, source_target_pairs={{0,8},{4,20},{8,0},{12,28},{16,24},{20,4},{24,16},{28,12},{1,9},{5... | collective-permute-start | bytes 3145736 | tf_op jit(solution)/shard_map/ppermute | solution.py:80
  34.7 24.3 %collective-permute-start.6 = (f32[512,512]{1,0:T(8,128)}, f32[512,512]{1,0:T(8,128)}, u32[]{:S(2)}, u32[]{:S(2)}) collective-permute-start(f32[512,512]{1,0:T(8,128)} %get-tuple-element.34), channel_id=1, source_target_pairs={{0,16},{4,12},{8,24},{12,4},{16,0},{20,28},{24,8},{28,20},{1,17},{... | collective-permute-start | bytes 3145736 | tf_op jit(solution)/shard_map/ppermute | solution.py:80
  38.2 76.0 %copy-start.1 = (f32[1,512,512]{2,1,0:T(8,128)S(1)}, f32[1,512,512]{2,1,0:T(8,128)}, u32[]{:S(2)}) copy-start(f32[1,512,512]{2,1,0:T(8,128)} %param.6) | copy-start | bytes 3145732
  38.2 20.7 %copy-start.2 = (f32[512,512]{1,0:T(8,128)}, f32[512,512]{1,0:T(8,128)S(1)}, u32[]{:S(2)}) copy-start(f32[512,512]{1,0:T(8,128)S(1)} %collective-permute-done) | copy-start | bytes 3145732
  109.4 1.0 copy-start.6
  117.7 3.5 %copy-start.3 = (f32[512,512]{1,0:T(8,128)S(1)}, f32[512,512]{1,0:T(8,128)}, u32[]{:S(2)}) copy-start(f32[512,512]{1,0:T(8,128)} %get-tuple-element.52) | copy-start | bytes 3145732
  117.8 3.4 %copy-start.7 = (f32[512,512]{1,0:T(8,128)S(1)}, f32[512,512]{1,0:T(8,128)}, u32[]{:S(2)}) copy-start(f32[512,512]{1,0:T(8,128)} %copy-done.6) | copy-start | bytes 3145732
  117.8 3.4 %copy-start.8 = (f32[512,512]{1,0:T(8,128)S(1)}, f32[512,512]{1,0:T(8,128)}, u32[]{:S(2)}) copy-start(f32[512,512]{1,0:T(8,128)} %fusion.10) | copy-start | bytes 3145732
  121.2 8.1 %copy-start.5 = (s32[1,6]{1,0:T(1,128)S(1)}, s32[1,6]{1,0:T(1,128)}, u32[]{:S(2)}) copy-start(s32[1,6]{1,0:T(1,128)} %param.5) | copy-start | bytes 76
  126.7 25.7 %collective-permute-start.7 = (f32[512,512]{0,1:T(8,128)S(1)}, f32[512,512]{0,1:T(8,128)S(1)}, u32[]{:S(2)}, u32[]{:S(2)}) collective-permute-start(f32[512,512]{0,1:T(8,128)S(1)} %get-tuple-element.20), channel_id=1, source_target_pairs={{0,16},{4,12},{8,24},{12,4},{16,0},{20,28},{24,8},{28,20},{1,17},{... | collective-permute-start | bytes 3145736 | tf_op jit(solution)/shard_map/ppermute | solution.py:80
  131.3 39.0 %collective-permute-start.8 = (f32[512,512]{0,1:T(8,128)S(1)}, f32[512,512]{0,1:T(8,128)S(1)}, u32[]{:S(2)}, u32[]{:S(2)}) collective-permute-start(f32[512,512]{0,1:T(8,128)S(1)} %get-tuple-element.20), channel_id=1, source_target_pairs={{0,8},{4,20},{8,0},{12,28},{16,24},{20,4},{24,16},{28,12},{1,9},{5... | collective-permute-start | bytes 3145736 | tf_op jit(solution)/shard_map/ppermute | solution.py:80
  152.4 20.1 %collective-permute-start.9 = (f32[512,512]{0,1:T(8,128)S(1)}, f32[512,512]{0,1:T(8,128)}, u32[]{:S(2)}, u32[]{:S(2)}) collective-permute-start(f32[512,512]{0,1:T(8,128)S(1)} %collective-permute-done.7), channel_id=1, source_target_pairs={{0,8},{4,20},{8,0},{12,28},{16,24},{20,4},{24,16},{28,12},{1,9},{5... | collective-permute-start | bytes 3145736 | tf_op jit(solution)/shard_map/ppermute | solution.py:80
  163.4 11.8 %collective-permute-start.10 = (f32[512,512]{0,1:T(8,128)S(1)}, f32[512,512]{0,1:T(8,128)}, u32[]{:S(2)}, u32[]{:S(2)}) collective-permute-start(f32[512,512]{0,1:T(8,128)S(1)} %get-tuple-element.20), channel_id=1, source_target_pairs={{0,4},{4,0},{8,12},{12,8},{16,20},{20,16},{24,28},{28,24},{1,5},{5... | collective-permute-start | bytes 3145736 | tf_op jit(solution)/shard_map/ppermute | solution.py:80
  169.7 7.8 %collective-permute-start.11 = (f32[512,512]{0,1:T(8,128)S(1)}, f32[512,512]{0,1:T(8,128)S(1)}, u32[]{:S(2)}, u32[]{:S(2)}) collective-permute-start(f32[512,512]{0,1:T(8,128)S(1)} %collective-permute-done.7), channel_id=1, source_target_pairs={{0,4},{4,0},{8,12},{12,8},{16,20},{20,16},{24,28},{28,24},{1,5},{5... | collective-permute-start | bytes 3145736 | tf_op jit(solution)/shard_map/ppermute | solution.py:80
  170.3 8.3 %collective-permute-start.12 = (f32[512,512]{0,1:T(8,128)S(1)}, f32[512,512]{0,1:T(8,128)S(1)}, u32[]{:S(2)}, u32[]{:S(2)}) collective-permute-start(f32[512,512]{0,1:T(8,128)S(1)} %collective-permute-done.8), channel_id=1, source_target_pairs={{0,4},{4,0},{8,12},{12,8},{16,20},{20,16},{24,28},{28,24},{1,5},{5... | collective-permute-start | bytes 3145736 | tf_op jit(solution)/shard_map/ppermute | solution.py:80
  172.5 7.1 %collective-permute-start.13 = (f32[512,512]{0,1:T(8,128)}, f32[512,512]{0,1:T(8,128)S(1)}, u32[]{:S(2)}, u32[]{:S(2)}) collective-permute-start(f32[512,512]{0,1:T(8,128)} %collective-permute-done.9), channel_id=1, source_target_pairs={{0,4},{4,0},{8,12},{12,8},{16,20},{20,16},{24,28},{28,24},{1,5},{5... | collective-permute-start | bytes 3145736 | tf_op jit(solution)/shard_map/ppermute | solution.py:80
  200.0 2.7 %copy-start.4 = (f32[512,3072]{1,0:T(8,128)}, f32[512,3072]{1,0:T(8,128)S(1)}, u32[]{:S(2)}) copy-start(f32[512,3072]{1,0:T(8,128)S(1)} %bitcast_dynamic-update-slice_fusion.1) | copy-start | bytes 18874372

commit v2 on v1

--- a/solution.py
+++ b/solution.py
@@ -1,6 +1,8 @@
 import jax
 import jax.numpy as jnp
 from jax import lax
+from jax.experimental import pallas as pl
+from jax.experimental.pallas import tpu as pltpu
 from jax.sharding import PartitionSpec as P
 
 clip_level = 1.0
@@ -60,63 +62,235 @@
     return pre * (clip_factor * jnp.sqrt(block_norm / (pre_norm + graft_eps)))
 
 
+MIB = 1 << 20
+F32 = jnp.float32
+
+
+def split(value):
+    high = value.astype(jnp.bfloat16)
+    return high, (value - high.astype(F32)).astype(jnp.bfloat16)
+
+
+def narrow_dot(left_side, right_side, dims):
+    return lax.dot_general(left_side, right_side, (dims, ((), ())), preferred_element_type=F32)
+
+
+def split_product(left_side, right_side, dims=((1,), (0,))):
+    small = narrow_dot(left_side[0], right_side[1], dims) + narrow_dot(left_side[1], right_side[0], dims)
+    return narrow_dot(left_side[0], right_side[0], dims) + small
+
+
+def pair_target(slot, device):
+    first = 2 + 2 * (device & 1)
+    return device ^ ((slot >> 1) * first) ^ ((slot & 1) * (6 - first))
+
+
+def column_of(owners_ref, block_count, target):
+    column = 0
+    for index in range(1, block_count):
+        column = column + jnp.where(owners_ref[index] == target, index, 0)
+    return column
+
+
+def piece_call(grads, owners, me, slot, flip, arrivals, with_norm=False):
+    width = grads.shape[0]
+    block_count = grads.shape[1] // width
+    rows = width // 4
+
+    def kernel(owners_ref, me_ref, grad_ref, *refs):
+        total = grad_ref[...].astype(F32)
+        for ref in refs[: len(arrivals)]:
+            total = total + ref[...]
+        refs[len(arrivals)][...] = total
+        if with_norm:
+            norm_ref = refs[len(arrivals) + 1]
+            owned = 0
+            for index in range(block_count):
+                owned = owned + jnp.where(owners_ref[index] == me_ref[0], 1, 0)
+            part = jnp.sum(total * total, keepdims=True).reshape(1, 1) * owned.astype(F32)
+
+            @pl.when(pl.program_id(0) == 0)
+            def _():
+                norm_ref[...] = jnp.zeros_like(norm_ref)
+
+            norm_ref[...] += jnp.broadcast_to(part, norm_ref.shape)
+
+    def grad_index(step, owners_ref, me_ref):
+        return step, column_of(owners_ref, block_count, pair_target(slot, me_ref[0] ^ flip))
+
+    plain = pl.BlockSpec((rows, width), lambda step, owners_ref, me_ref: (step, 0))
+    out_specs = [plain]
+    out_shape = [jax.ShapeDtypeStruct((width, width), F32)]
+    if with_norm:
+        out_specs.append(pl.BlockSpec((8, 128), lambda step, owners_ref, me_ref: (0, 0)))
+        out_shape.append(jax.ShapeDtypeStruct((8, 128), F32))
+    result = pl.pallas_call(
+        kernel,
+        grid_spec=pltpu.PrefetchScalarGridSpec(
+            num_scalar_prefetch=2,
+            grid=(width // rows,),
+            in_specs=[pl.BlockSpec((rows, width), grad_index)] + [plain] * len(arrivals),
+            out_specs=out_specs,
+        ),
+        out_shape=out_shape,
+        cost_estimate=pl.CostEstimate(
+            flops=width * width * (len(arrivals) + 1),
+            bytes_accessed=width * width * (6 + 4 * len(arrivals)),
+            transcendentals=0,
+        ),
+        name="piece",
+    )(owners, me, grads, *arrivals)
+    return result if with_norm else result[0]
+
+
+def gram_kernel(block_ref, left_ref, right_ref):
+    block = split(block_ref[...])
+    left_ref[...] = split_product(block, block, ((1,), (1,)))
+    right_ref[...] = split_product(block, block, ((0,), (0,)))
+
+
+def gram_call(block):
+    width = block.shape[0]
+    shape = jax.ShapeDtypeStruct(block.shape, F32)
+    return pl.pallas_call(
+        gram_kernel,
+        in_specs=[pl.BlockSpec(memory_space=pltpu.VMEM)],
+        out_specs=[pl.BlockSpec(memory_space=pltpu.VMEM)] * 2,
+        out_shape=[shape, shape],
+        compiler_params=pltpu.CompilerParams(vmem_limit_bytes=24 * MIB),
+        cost_estimate=pl.CostEstimate(
+            flops=12 * width**3, bytes_accessed=12 * width * width, transcendentals=0
+        ),
+        name="gram",
+    )(block)
+
+
+def root_of(previous, gram, gram_scale):
+    order_size = previous.shape[0]
+    rows = lax.broadcasted_iota(jnp.int32, previous.shape, 0)
+    columns = lax.broadcasted_iota(jnp.int32, previous.shape, 1)
+    identity = jnp.where(rows == columns, 1.0, 0.0)
+    statistic = 0.5 * previous + gram * gram_scale
+    squares = jnp.sum(statistic * statistic, keepdims=True).reshape(1, 1)
+    frobenius = jnp.sqrt(squares)
+    scaled = statistic * (1.0 / frobenius)
+    parts = split(scaled)
+    square = split_product(parts, parts)
+    factor_square = split((25.0 * identity - 10.0 * scaled + square) * 0.0625)
+    factor_scaled = split((5.0 * scaled - square) * 0.25)
+    fourth = split(split_product(factor_square, factor_square))
+    tail = split_product(fourth, factor_scaled)
+    return (6.25 * identity - 1.25 * scaled - tail) * (0.25 * lax.rsqrt(jnp.sqrt(frobenius)))
+
+
+def update_call(block, left_gram, right_gram, left_prev, right_prev, norms, entry_count):
+    width = block.shape[0]
+
+    def kernel(block_ref, left_gram_ref, right_gram_ref, left_ref, right_ref, *refs):
+        out_ref = refs[-1]
+        squares = refs[0][...]
+        for ref in refs[1:-1]:
+            squares = squares + ref[...]
+        clip_factor = jnp.minimum(1.0, clip_level / jnp.sqrt(squares[:1, :1] / entry_count))
+        gram_scale = clip_factor * clip_factor / width
+        left_root = root_of(left_ref[...], left_gram_ref[...], gram_scale)
+        right_root = root_of(right_ref[...], right_gram_ref[...], gram_scale)
+        block = block_ref[...]
+        halfway = split_product(split(left_root), split(block))
+        pre = split_product(split(halfway), split(right_root)) * clip_factor
+        block_norm = jnp.sum(block * block, keepdims=True).reshape(1, 1) * (clip_factor * clip_factor)
+        pre_norm = jnp.sum(pre * pre, keepdims=True).reshape(1, 1)
+        out_ref[...] = pre * jnp.sqrt(block_norm / (pre_norm + graft_eps))
+
+    return pl.pallas_call(
+        kernel,
+        in_specs=[pl.BlockSpec(memory_space=pltpu.VMEM)] * (5 + len(norms)),
+        out_specs=pl.BlockSpec(memory_space=pltpu.VMEM),
+        out_shape=jax.ShapeDtypeStruct(block.shape, F32),
+        compiler_params=pltpu.CompilerParams(vmem_limit_bytes=40 * MIB),
+        cost_estimate=pl.CostEstimate(
+            flops=48 * width**3, bytes_accessed=24 * width * width, transcendentals=0
+        ),
+        name="update",
+    )(block, left_gram, right_gram, left_prev, right_prev, *norms)
+
+
+def assemble_call(owners, me, slots, block_count):
+    width = slots[0].shape[0]
+
+    def kernel(owners_ref, me_ref, *refs):
+        out_ref, sem = refs[-2:]
+        for index in range(block_count):
+            spot = out_ref.at[:, pl.ds(index * width, width)]
+            for place in range(len(slots)):
+                target = pair_target(place & 3, me_ref[0] ^ (place >> 2))
+
+                @pl.when(owners_ref[index] == target)
+                def _():
+                    pltpu.make_async_copy(refs[place], spot, sem.at[index]).start()
+
+        for index in range(block_count):
+            spot = out_ref.at[:, pl.ds(index * width, width)]
+            pltpu.make_async_copy(refs[0], spot, sem.at[index]).wait()
+
+    return pl.pallas_call(
+        kernel,
+        in_specs=[pl.BlockSpec(memory_space=pltpu.SMEM)] * 2
+        + [pl.BlockSpec(memory_space=pl.ANY)] * len(slots),
+        out_specs=pl.BlockSpec(memory_space=pl.ANY),
+        out_shape=jax.ShapeDtypeStruct((width, block_count * width), F32),
+        scratch_shapes=[pltpu.SemaphoreType.DMA((block_count,))],
+        cost_estimate=pl.CostEstimate(
+            flops=0, bytes_accessed=8 * width * width * block_count, transcendentals=0
+        ),
+        name="assemble",
+    )(owners, me, *slots)
+
+
 def paired_body(replica_grads, owners, left_stats, right_stats):
     width = left_stats.shape[1]
     owner_row = owners[0]
     block_count = owner_row.shape[0]
-    me = lax.axis_index("dp")
-    core = me & 1
-    entry_count = width * block_count * width * lax.axis_size("mp")
+    me = lax.axis_index("dp").astype(jnp.int32).reshape(1)
+    group_count = lax.axis_size("mp")
+    entry_count = width * block_count * width * group_count
     grads = replica_grads[0]
-    matches = (owner_row[None, :] == jnp.arange(8, dtype=jnp.int32)[:, None]).astype(jnp.int32)
-    owned = jnp.sum(matches, axis=1)
-    block_of = jnp.sum(matches * jnp.arange(block_count, dtype=jnp.int32)[None, :], axis=1)
-
-    first_pairs = [(i, i ^ (2 if i % 2 == 0 else 4)) for i in range(8)]
-    second_pairs = [(i, i ^ (4 if i % 2 == 0 else 2)) for i in range(8)]
+
+    first_pairs = [(i, i ^ (2 + 2 * (i % 2))) for i in range(8)]
+    second_pairs = [(i, i ^ (4 - 2 * (i % 2))) for i in range(8)]
     core_pairs = [(i, i ^ 1) for i in range(8)]
 
     def over(pairs, value):
         return lax.ppermute(value, "dp", pairs)
 
-    def target(slot, device):
-        device_core = device & 1
-        first = jnp.where(device_core == 0, 2, 4)
-        second = 6 - first
-        return device ^ ((slot >> 1) * first) ^ ((slot & 1) * second)
-
-    def own_piece(device_target):
-        column = block_of[device_target] * width
-        return lax.dynamic_slice(grads, (0, column), (width, width)).astype(jnp.float32)
-
-    sums = {}
-    for slot in (3, 2, 1, 0):
-        arrived = over(core_pairs, own_piece(target(slot, me ^ 1)))
-        sums[slot] = arrived + own_piece(target(slot, me))
-    sum_one = sums[1] + over(first_pairs, sums[3])
-    sum_zero = sums[0] + over(first_pairs, sums[2])
-    block = sum_zero + over(second_pairs, sum_one)
-
-    block_norm = jnp.sum(block * block)
-    mine = owned[me] > 0
-    squares = lax.psum(jnp.where(mine, block_norm, 0.0), ("dp", "mp"))
-    clip_factor = jnp.minimum(1.0, clip_level / jnp.sqrt(squares / entry_count))
-    update = block_update(block, block_norm, clip_factor, left_stats[0], right_stats[0])
+    def piece(slot, flip, *arrivals):
+        return piece_call(grads, owner_row, me, slot, flip, arrivals)
+
+    from_core = {slot: over(core_pairs, piece(slot, 1)) for slot in (3, 2, 1, 0)}
+    from_first_three = over(first_pairs, piece(3, 0, from_core[3]))
+    from_first_two = over(first_pairs, piece(2, 0, from_core[2]))
+    from_second = over(second_pairs, piece(1, 0, from_core[1], from_first_three))
+    arrivals = (from_core[0], from_first_two, from_second)
+    block, norm = piece_call(grads, owner_row, me, 0, 0, arrivals, with_norm=True)
+
+    group_norm = norm
+    for flip in range(1, 8):
+        group_norm = group_norm + over([(i, i ^ flip) for i in range(8)], norm)
+    norms = [group_norm]
+    for shift in range(1, group_count):
+        pairs = [(i, (i + shift) % group_count) for i in range(group_count)]
+        norms.append(lax.ppermute(group_norm, "mp", pairs))
+    left_gram, right_gram = gram_call(block)
+    update = update_call(
+        block, left_gram, right_gram, left_stats[0], right_stats[0], norms, entry_count
+    )
 
     mine_near = over(second_pairs, update)
     mine_far = over(first_pairs, update)
     near_far = over(first_pairs, mine_near)
     held = [update, mine_near, mine_far, near_far]
     slots = held + [over(core_pairs, value) for value in held]
-    places = jnp.stack(
-        [target(slot, me) for slot in range(4)] + [target(slot, me ^ 1) for slot in range(4)]
-    )
-    stacked = jnp.stack(slots)
-    pieces = []
-    for index in range(block_count):
-        place = jnp.argmax(places == owner_row[index])
-        pieces.append(lax.dynamic_index_in_dim(stacked, place, 0, keepdims=False))
-    return jnp.concatenate(pieces, axis=1)
+    return assemble_call(owner_row, me, slots, block_count)
 
 
 def solution(mesh):

time: 205 us -> 326 us (1.59)
  Pallas kernels: 0 us -> 236 us
  blocking collectives: 39.9 us -> 0 us
  local copies, waits for them, and re-layouts: 36.1 us -> 7 us
  other arithmetic: 21.9 us -> 0.68 us
  between operations: 21.2 us -> 0.11 us
  matrix products: 18.3 us -> 0 us
  waiting for transfers between devices: 50.9 us -> 58.6 us
  starting transfers between devices: 15.5 us -> 22.5 us
    pallas_call x0 -> x11, Pallas kernels: none -> 236 us  [the longest x1 192 us: assemble_call(): pl.pallas_call(kernel, in_specs=[pl.BlockSpec(memory_space=pltpu.SMEM)] *...]
    psum x1 -> x0, blocking collectives: 39.9 us -> none  [paired_body(): squares = lax.psum(jnp.where(mine, block_norm, 0.0), ('dp', 'mp'))]
    dot_general x10 -> x0, matrix products: 18.3 us -> none  [mat_product(): return jnp.matmul(left_side, right_side, precision=lax.Precision.HIGH)]
    dynamic_slice x9 -> x0, local copies, waits for them, and re-layouts: 16.5 us -> none  [the longest x7 15.1 us: paired_body(): pieces.append(lax.dynamic_index_in_dim(stacked, place, 0, keepdims=False))]
    unnamed x29 -> x30, local copies, waits for them, and re-layouts: 16.7 us -> 7 us
    another operation x6 -> x0, other arithmetic: 8.21 us -> none  [paired_body(): place = jnp.argmax(places == owner_row[index])]
    ppermute x14 -> x21, waiting for transfers between devices: 50.9 us -> 57.3 us  [over(): return lax.ppermute(value, 'dp', pairs)]
    ppermute x0 -> x3, starting transfers between devices: none -> 4.61 us  [paired_body(): norms.append(lax.ppermute(group_norm, 'mp', pairs))]
  transfers between devices with their start and end apart: 14 -> 24, of which waited for: 4 -> 11; matrix products, arithmetic and copies ran while one was open for 12% -> 0% of each run, Pallas kernels for 0% -> 8%
where the time goes in v2:
time: 326 us; the launch traced here: 325 us
  Pallas kernels  236 us (72%)
  waiting for transfers between devices  58.6 us (18%)
  starting transfers between devices  22.5 us (7%)
  local copies, waits for them, and re-layouts  7 us (2%)
    pallas_call x1, Pallas kernels, assemble_call(): pl.pallas_call(kernel, in_specs=[pl.BlockSpec(memory_space=pltpu.SMEM)] *...  192 us
    ppermute x21, waiting for transfers between devices, over(): return lax.ppermute(value, 'dp', pairs)  57.3 us
    pallas_call x8, Pallas kernels, piece_call(): pl.pallas_call(kernel, grid_spec=pltpu.PrefetchScalarGridSpec(num_scalar_...  33.5 us
    ppermute x21, starting transfers between devices, over(): return lax.ppermute(value, 'dp', pairs)  17.9 us
    pallas_call x1, Pallas kernels, update_call(): pl.pallas_call(kernel, in_specs=[pl.BlockSpec(memory_space=pltpu.VMEM)] *...  8.15 us
    unnamed x30, local copies, waits for them, and re-layouts  7 us
  transfers between devices with their start and end apart: 24, of which 11 were waited for; matrix products, arithmetic and copies ran while one was open for 0% of the time, Pallas kernels for 8%

profile of v2, /device:TPU:0, one launch (start us, length us, event | category | flops | bytes accessed | tf_op | source)
XLA Modules:
  0.0 324.8 jit_solution(13282730010832616149)
XLA Ops:
  0.0 3.9 %piece.12 = f32[512,512]{1,0:T(8,128)} custom-call(s32[6]{0:T(128)} %bitcast.15, s32[1]{0:T(128)} %bitcast.1.me_ref, bf16[512,3072]{1,0:T(8,128)(2,1)} %bitcast.7), custom_call_target="tpu_custom_call" | custom-call | flops 262144 | bytes 1572864 | tf_op jit(solution)/shard_map/piece/pallas_call | solution.py:127
  4.4 3.9 %piece.9 = f32[512,512]{1,0:T(8,128)} custom-call(s32[6]{0:T(128)} %bitcast.16, s32[1]{0:T(128)} %bitcast.1.me_ref, bf16[512,3072]{1,0:T(8,128)(2,1)} %bitcast.8), custom_call_target="tpu_custom_call" | custom-call | flops 262144 | bytes 1572864 | tf_op jit(solution)/shard_map/piece/pallas_call | solution.py:127
  8.4 4.0 %piece.11 = f32[512,512]{1,0:T(8,128)} custom-call(s32[6]{0:T(128)} %bitcast.17, s32[1]{0:T(128)} %bitcast.1.me_ref, bf16[512,3072]{1,0:T(8,128)(2,1)} %bitcast.9), custom_call_target="tpu_custom_call" | custom-call | flops 262144 | bytes 1572864 | tf_op jit(solution)/shard_map/piece/pallas_call | solution.py:127
  12.8 1.0 copy-done.8
  13.8 4.2 %piece.13 = f32[512,512]{1,0:T(8,128)} custom-call(s32[6]{0:T(128)} %bitcast.18, s32[1]{0:T(128)} %bitcast.1.me_ref, bf16[512,3072]{1,0:T(8,128)(2,1)} %bitcast.10, f32[512,512]{1,0:T(8,128)} %copy-done.8), custom_call_target="tpu_custom_call" | custom-call | flops 524288 | bytes 2621440 | tf_op jit(solution)/shard_map/piece/pallas_call | solution.py:127
  18.0 2.5 collective-permute-start.5
  20.5 3.9 %piece.8 = f32[512,512]{1,0:T(8,128)} custom-call(s32[6]{0:T(128)} %bitcast.19, s32[1]{0:T(128)} %bitcast.1.me_ref, bf16[512,3072]{1,0:T(8,128)(2,1)} %bitcast.11), custom_call_target="tpu_custom_call" | custom-call | flops 262144 | bytes 1572864 | tf_op jit(solution)/shard_map/piece/pallas_call | solution.py:127
  24.7 1.0 copy-done.7
  25.7 4.2 %piece.10 = f32[512,512]{1,0:T(8,128)} custom-call(s32[6]{0:T(128)} %bitcast.20, s32[1]{0:T(128)} %bitcast.1.me_ref, bf16[512,3072]{1,0:T(8,128)(2,1)} %bitcast.12, f32[512,512]{1,0:T(8,128)} %copy-done.7), custom_call_target="tpu_custom_call" | custom-call | flops 524288 | bytes 2621440 | tf_op jit(solution)/shard_map/piece/pallas_call | solution.py:127
  29.9 1.5 collective-permute-start.2
  31.4 2.2 collective-permute-done.5.refs_1_
  33.6 4.4 %piece.14 = f32[512,512]{1,0:T(8,128)} custom-call(s32[6]{0:T(128)} %bitcast.21, s32[1]{0:T(128)} %bitcast.1.me_ref, bf16[512,3072]{1,0:T(8,128)(2,1)} %bitcast.13, f32[512,512]{1,0:T(8,128)} %copy-done.6, f32[512,512]{1,0:T(8,128)} %collective-permute-done.5.refs_1_), custom_call_target="tpu_custom_call" | custom-call | flops 786432 | bytes 3670016 | tf_op jit(solution)/shard_map/piece/pallas_call | solution.py:127
  38.0 2.1 collective-permute-start.6
  40.0 9.0 %collective-permute-done.2.refs_1_ = f32[512,512]{1,0:T(8,128)} collective-permute-done((f32[512,512]{1,0:T(8,128)}, f32[512,512]{1,0:T(8,128)}, u32[]{:S(2)}, u32[]{:S(2)}) %collective-permute-start.2) | collective-permute-done | bytes 1048608 | tf_op jit(solution)/shard_map/ppermute | solution.py:264
  49.0 6.9 %collective-permute-done.6.refs_2_ = f32[512,512]{1,0:T(8,128)} collective-permute-done((f32[512,512]{1,0:T(8,128)}, f32[512,512]{1,0:T(8,128)}, u32[]{:S(2)}, u32[]{:S(2)}) %collective-permute-start.6) | collective-permute-done | bytes 1048608 | tf_op jit(solution)/shard_map/ppermute | solution.py:264
  55.9 4.9 %piece.15 = (f32[512,512]{1,0:T(8,128)}, f32[8,128]{1,0:T(8,128)}) custom-call(s32[6]{0:T(128)} %bitcast.22, s32[1]{0:T(128)} %bitcast.1.me_ref, bf16[512,3072]{1,0:T(8,128)(2,1)} %bitcast.14, f32[512,512]{1,0:T(8,128)} %copy-done.5, f32[512,512]{1,0:T(8,128)} %collective-permute-done.2.refs_1_, f32[512,512]{1,0:T(8,128)} %collective-permute-done.6.refs_2_), custom_call_target="tpu_custom_call" | custom-call | flops 1048576 | bytes 4718592 | tf_op jit(solution)/shard_map/piece/pallas_call | solution.py:127
  60.8 2.6 collective-permute-start.13
  63.6 1.4 collective-permute-start.11
  65.4 1.4 collective-permute-start.9
  68.8 1.9 collective-permute-done.8
  71.4 3.6 %collective-permute-start.16 = (f32[8,128]{1,0:T(8,128)S(1)}, f32[8,128]{1,0:T(8,128)S(1)}, u32[]{:S(2)}, u32[]{:S(2)}) collective-permute-start(f32[8,128]{1,0:T(8,128)S(1)} %add_add_fusion.refs_0_), channel_id=1, source_target_pairs={{0,3},{1,0},{2,1},{3,2},{4,7},{5,4},{6,5},{7,6},{8,11},{9,8},{10,9... | collective-permute-start | bytes 12296 | tf_op jit(solution)/shard_map/ppermute | solution.py:282
  75.0 1.0 collective-permute-start.14
  76.0 1.2 copy-done.3
  77.2 1.8 gram.1
  80.4 1.2 copy-done.4
  81.6 8.1 %update.1.refs_0_ = f32[512,512]{1,0:T(8,128)S(1)} custom-call(f32[512,512]{1,0:T(8,128)S(1)} %copy-done.4, f32[512,512]{1,0:T(8,128)S(1)} %get-tuple-element.10.left_gram_ref, f32[512,512]{1,0:T(8,128)S(1)} %get-tuple-element.11.right_gram_ref, f32[512,512]{1,0:T(8,128)S(1)} %bitcast.5, f32[512,512]{1,0:T(8,128)S(1)} %bitcast.6, ...), custom_call_target="tpu_custom_call" | custom-call | flops 6442450944 | bytes 6291456 | tf_op jit(solution)/shard_map/update/pallas_call | solution.py:205
  89.8 1.6 collective-permute-start.17
  91.9 22.9 %collective-permute-done.17.refs_1_ = f32[512,512]{1,0:T(8,128)S(1)} collective-permute-done((f32[512,512]{1,0:T(8,128)S(1)}, f32[512,512]{1,0:T(8,128)S(1)}, u32[]{:S(2)}, u32[]{:S(2)}) %collective-permute-start.17) | collective-permute-done | bytes 1048608 | tf_op jit(solution)/shard_map/ppermute | solution.py:264
  114.8 1.6 collective-permute-start.19
  117.0 12.6 %collective-permute-done.19.refs_3_ = f32[512,512]{1,0:T(8,128)S(1)} collective-permute-done((f32[512,512]{1,0:T(8,128)S(1)}, f32[512,512]{1,0:T(8,128)S(1)}, u32[]{:S(2)}, u32[]{:S(2)}) %collective-permute-start.19) | collective-permute-done | bytes 1048608 | tf_op jit(solution)/shard_map/ppermute | solution.py:264
  131.2 1.0 copy-done.13
  132.4 192.4 %assemble.1 = f32[512,3072]{1,0:T(8,128)} custom-call(s32[6]{0:T(128)} %bitcast.23, s32[1]{0:T(128)} %bitcast.1.me_ref, f32[512,512]{1,0:T(8,128)} %copy-done, f32[512,512]{1,0:T(8,128)} %copy-done.9, f32[512,512]{1,0:T(8,128)} %copy-done.10, f32[512,512]{1,0:T(8,128)} %copy-done.11, f32[512,512]{1,0:T(8,128)} %copy-done.12, f32[512,512]{1,0:T(8,128)} %copy-done.13, ...), custom_call_target="tpu_custom_call" | custom-call | bytes 12582912 | tf_op jit(solution)/shard_map/assemble/pallas_call | solution.py:236
  (58 shorter events, 8.7 us)
Async XLA Ops:
  3.9 8.9 %collective-permute-start.4 = (f32[512,512]{1,0:T(8,128)}, f32[512,512]{1,0:T(8,128)S(1)}, u32[]{:S(2)}, u32[]{:S(2)}) collective-permute-start(f32[512,512]{1,0:T(8,128)} %piece.12), channel_id=1, source_target_pairs={{0,4},{4,0},{8,12},{12,8},{16,20},{20,16},{24,28},{28,24},{1,5},{5... | collective-permute-start | bytes 3145736 | tf_op jit(solution)/shard_map/ppermute | solution.py:264
  8.3 16.4 %collective-permute-start.1 = (f32[512,512]{1,0:T(8,128)}, f32[512,512]{1,0:T(8,128)S(1)}, u32[]{:S(2)}, u32[]{:S(2)}) collective-permute-start(f32[512,512]{1,0:T(8,128)} %piece.9), channel_id=1, source_target_pairs={{0,4},{4,0},{8,12},{12,8},{16,20},{20,16},{24,28},{28,24},{1,5},{5... | collective-permute-start | bytes 3145736 | tf_op jit(solution)/shard_map/ppermute | solution.py:264
  12.4 19.0 %collective-permute-start.3 = (f32[512,512]{1,0:T(8,128)}, f32[512,512]{1,0:T(8,128)S(1)}, u32[]{:S(2)}, u32[]{:S(2)}) collective-permute-start(f32[512,512]{1,0:T(8,128)} %piece.11), channel_id=1, source_target_pairs={{0,4},{4,0},{8,12},{12,8},{16,20},{20,16},{24,28},{28,24},{1,5},{5... | collective-permute-start | bytes 3145736 | tf_op jit(solution)/shard_map/ppermute | solution.py:264
  18.0 15.6 %collective-permute-start.5 = (f32[512,512]{1,0:T(8,128)}, f32[512,512]{1,0:T(8,128)}, u32[]{:S(2)}, u32[]{:S(2)}) collective-permute-start(f32[512,512]{1,0:T(8,128)} %piece.13), channel_id=1, source_target_pairs={{0,8},{4,20},{8,0},{12,28},{16,24},{20,4},{24,16},{28,12},{1,9},{5... | collective-permute-start | bytes 3145736 | tf_op jit(solution)/shard_map/ppermute | solution.py:264
  24.4 15.6 %collective-permute-start = (f32[512,512]{1,0:T(8,128)}, f32[512,512]{1,0:T(8,128)S(1)}, u32[]{:S(2)}, u32[]{:S(2)}) collective-permute-start(f32[512,512]{1,0:T(8,128)} %piece.8), channel_id=1, source_target_pairs={{0,4},{4,0},{8,12},{12,8},{16,20},{20,16},{24,28},{28,24},{1,5},{5... | collective-permute-start | bytes 3145736 | tf_op jit(solution)/shard_map/ppermute | solution.py:264
  29.9 19.2 %collective-permute-start.2 = (f32[512,512]{1,0:T(8,128)}, f32[512,512]{1,0:T(8,128)}, u32[]{:S(2)}, u32[]{:S(2)}) collective-permute-start(f32[512,512]{1,0:T(8,128)} %piece.10), channel_id=1, source_target_pairs={{0,8},{4,20},{8,0},{12,28},{16,24},{20,4},{24,16},{28,12},{1,9},{5... | collective-permute-start | bytes 3145736 | tf_op jit(solution)/shard_map/ppermute | solution.py:264
  31.4 2.2 copy-start.6
  38.0 42.4 %copy-start.1 = (f32[1,512,512]{2,1,0:T(8,128)S(1)}, f32[1,512,512]{2,1,0:T(8,128)}, u32[]{:S(2)}) copy-start(f32[1,512,512]{2,1,0:T(8,128)} %param.6) | copy-start | bytes 3145732
  38.0 42.4 %copy-start.2 = (f32[1,512,512]{2,1,0:T(8,128)S(1)}, f32[1,512,512]{2,1,0:T(8,128)}, u32[]{:S(2)}) copy-start(f32[1,512,512]{2,1,0:T(8,128)} %param.7) | copy-start | bytes 3145732
  38.0 17.9 %collective-permute-start.6 = (f32[512,512]{1,0:T(8,128)}, f32[512,512]{1,0:T(8,128)}, u32[]{:S(2)}, u32[]{:S(2)}) collective-permute-start(f32[512,512]{1,0:T(8,128)} %piece.14), channel_id=1, source_target_pairs={{0,16},{4,12},{8,24},{12,4},{16,0},{20,28},{24,8},{28,20},{1,17},{... | collective-permute-start | bytes 3145736 | tf_op jit(solution)/shard_map/ppermute | solution.py:264
  40.0 15.9 %copy-start.5 = (f32[512,512]{1,0:T(8,128)}, f32[512,512]{1,0:T(8,128)S(1)}, u32[]{:S(2)}) copy-start(f32[512,512]{1,0:T(8,128)S(1)} %collective-permute-done.refs_0_) | copy-start | bytes 3145732
  60.8 6.0 %collective-permute-start.13 = (f32[8,128]{1,0:T(8,128)}, f32[8,128]{1,0:T(8,128)S(1)}, u32[]{:S(2)}, u32[]{:S(2)}) collective-permute-start(f32[8,128]{1,0:T(8,128)} %get-tuple-element.12), channel_id=1, source_target_pairs={{0,28},{4,24},{8,20},{12,16},{16,12},{20,8},{24,4},{28,0},{1,29},{... | collective-permute-start | bytes 12296 | tf_op jit(solution)/shard_map/ppermute | solution.py:264
  63.4 4.7 %collective-permute-start.12 = (f32[8,128]{1,0:T(8,128)}, f32[8,128]{1,0:T(8,128)S(1)}, u32[]{:S(2)}, u32[]{:S(2)}) collective-permute-start(f32[8,128]{1,0:T(8,128)} %get-tuple-element.12), channel_id=1, source_target_pairs={{0,24},{4,28},{8,16},{12,20},{16,8},{20,12},{24,0},{28,4},{1,25},{... | collective-permute-start | bytes 12296 | tf_op jit(solution)/shard_map/ppermute | solution.py:264
  63.6 4.6 %collective-permute-start.11 = (f32[8,128]{1,0:T(8,128)}, f32[8,128]{1,0:T(8,128)S(1)}, u32[]{:S(2)}, u32[]{:S(2)}) collective-permute-start(f32[8,128]{1,0:T(8,128)} %get-tuple-element.12), channel_id=1, source_target_pairs={{0,20},{4,16},{8,28},{12,24},{16,4},{20,0},{24,12},{28,8},{1,21},{... | collective-permute-start | bytes 12296 | tf_op jit(solution)/shard_map/ppermute | solution.py:264
  65.0 3.8 %collective-permute-start.10 = (f32[8,128]{1,0:T(8,128)}, f32[8,128]{1,0:T(8,128)S(1)}, u32[]{:S(2)}, u32[]{:S(2)}) collective-permute-start(f32[8,128]{1,0:T(8,128)} %get-tuple-element.12), channel_id=1, source_target_pairs={{0,16},{4,20},{8,24},{12,28},{16,0},{20,4},{24,8},{28,12},{1,17},{... | collective-permute-start | bytes 12296 | tf_op jit(solution)/shard_map/ppermute | solution.py:264
  65.4 3.3 %collective-permute-start.9 = (f32[8,128]{1,0:T(8,128)}, f32[8,128]{1,0:T(8,128)S(1)}, u32[]{:S(2)}, u32[]{:S(2)}) collective-permute-start(f32[8,128]{1,0:T(8,128)} %get-tuple-element.12), channel_id=1, source_target_pairs={{0,12},{4,8},{8,4},{12,0},{16,28},{20,24},{24,20},{28,16},{1,13},{... | collective-permute-start | bytes 12296 | tf_op jit(solution)/shard_map/ppermute | solution.py:264
  66.8 3.8 %collective-permute-start.8 = (f32[8,128]{1,0:T(8,128)}, f32[8,128]{1,0:T(8,128)S(1)}, u32[]{:S(2)}, u32[]{:S(2)}) collective-permute-start(f32[8,128]{1,0:T(8,128)} %get-tuple-element.12), channel_id=1, source_target_pairs={{0,8},{4,12},{8,0},{12,4},{16,24},{20,28},{24,16},{28,20},{1,9},{5... | collective-permute-start | bytes 12296 | tf_op jit(solution)/shard_map/ppermute | solution.py:264
  68.1 2.5 collective-permute-start.7
  71.4 7.7 %collective-permute-start.16 = (f32[8,128]{1,0:T(8,128)S(1)}, f32[8,128]{1,0:T(8,128)S(1)}, u32[]{:S(2)}, u32[]{:S(2)}) collective-permute-start(f32[8,128]{1,0:T(8,128)S(1)} %add_add_fusion.refs_0_), channel_id=1, source_target_pairs={{0,3},{1,0},{2,1},{3,2},{4,7},{5,4},{6,5},{7,6},{8,11},{9,8},{10,9... | collective-permute-start | bytes 12296 | tf_op jit(solution)/shard_map/ppermute | solution.py:282
  75.0 4.5 %collective-permute-start.15 = (f32[8,128]{1,0:T(8,128)S(1)}, f32[8,128]{1,0:T(8,128)S(1)}, u32[]{:S(2)}, u32[]{:S(2)}) collective-permute-start(f32[8,128]{1,0:T(8,128)S(1)} %add_add_fusion.refs_0_), channel_id=1, source_target_pairs={{0,2},{1,3},{2,0},{3,1},{4,6},{5,7},{6,4},{7,5},{8,10},{9,11},{10,... | collective-permute-start | bytes 12296 | tf_op jit(solution)/shard_map/ppermute | solution.py:282
  75.0 5.4 %collective-permute-start.14 = (f32[8,128]{1,0:T(8,128)S(1)}, f32[8,128]{1,0:T(8,128)S(1)}, u32[]{:S(2)}, u32[]{:S(2)}) collective-permute-start(f32[8,128]{1,0:T(8,128)S(1)} %add_add_fusion.refs_0_), channel_id=1, source_target_pairs={{0,1},{1,2},{2,3},{3,0},{4,5},{5,6},{6,7},{7,4},{8,9},{9,10},{10,1... | collective-permute-start | bytes 12296 | tf_op jit(solution)/shard_map/ppermute | solution.py:282
  89.8 42.7 %copy-start = (f32[512,512]{1,0:T(8,128)}, f32[512,512]{1,0:T(8,128)S(1)}, u32[]{:S(2)}) copy-start(f32[512,512]{1,0:T(8,128)S(1)} %update.1.refs_0_) | copy-start | bytes 3145732
  89.8 25.1 %collective-permute-start.17 = (f32[512,512]{1,0:T(8,128)S(1)}, f32[512,512]{1,0:T(8,128)S(1)}, u32[]{:S(2)}, u32[]{:S(2)}) collective-permute-start(f32[512,512]{1,0:T(8,128)S(1)} %update.1.refs_0_), channel_id=1, source_target_pairs={{0,16},{4,12},{8,24},{12,4},{16,0},{20,28},{24,8},{28,20},{1,17},{... | collective-permute-start | bytes 3145736 | tf_op jit(solution)/shard_map/ppermute | solution.py:264
  91.3 25.6 %collective-permute-start.18 = (f32[512,512]{1,0:T(8,128)S(1)}, f32[512,512]{1,0:T(8,128)S(1)}, u32[]{:S(2)}, u32[]{:S(2)}) collective-permute-start(f32[512,512]{1,0:T(8,128)S(1)} %update.1.refs_0_), channel_id=1, source_target_pairs={{0,8},{4,20},{8,0},{12,28},{16,24},{20,4},{24,16},{28,12},{1,9},{5... | collective-permute-start | bytes 3145736 | tf_op jit(solution)/shard_map/ppermute | solution.py:264
  114.8 17.6 %copy-start.9 = (f32[512,512]{1,0:T(8,128)}, f32[512,512]{1,0:T(8,128)S(1)}, u32[]{:S(2)}) copy-start(f32[512,512]{1,0:T(8,128)S(1)} %collective-permute-done.17.refs_1_) | copy-start | bytes 3145732
  114.8 14.8 %collective-permute-start.19 = (f32[512,512]{1,0:T(8,128)S(1)}, f32[512,512]{1,0:T(8,128)S(1)}, u32[]{:S(2)}, u32[]{:S(2)}) collective-permute-start(f32[512,512]{1,0:T(8,128)S(1)} %collective-permute-done.17.refs_1_), channel_id=1, source_target_pairs={{0,8},{4,20},{8,0},{12,28},{16,24},{20,4},{24,16},{28,12},{1,9},{5... | collective-permute-start | bytes 3145736 | tf_op jit(solution)/shard_map/ppermute | solution.py:264
  116.5 13.2 %collective-permute-start.20 = (f32[512,512]{1,0:T(8,128)S(1)}, f32[512,512]{1,0:T(8,128)S(1)}, u32[]{:S(2)}, u32[]{:S(2)}) collective-permute-start(f32[512,512]{1,0:T(8,128)S(1)} %update.1.refs_0_), channel_id=1, source_target_pairs={{0,4},{4,0},{8,12},{12,8},{16,20},{20,16},{24,28},{28,24},{1,5},{5... | collective-permute-start | bytes 3145736 | tf_op jit(solution)/shard_map/ppermute | solution.py:264
  116.5 13.2 %collective-permute-start.21 = (f32[512,512]{1,0:T(8,128)S(1)}, f32[512,512]{1,0:T(8,128)S(1)}, u32[]{:S(2)}, u32[]{:S(2)}) collective-permute-start(f32[512,512]{1,0:T(8,128)S(1)} %collective-permute-done.17.refs_1_), channel_id=1, source_target_pairs={{0,4},{4,0},{8,12},{12,8},{16,20},{20,16},{24,28},{28,24},{1,5},{5... | collective-permute-start | bytes 3145736 | tf_op jit(solution)/shard_map/ppermute | solution.py:264
  117.0 15.4 %copy-start.10 = (f32[512,512]{1,0:T(8,128)}, f32[512,512]{1,0:T(8,128)S(1)}, u32[]{:S(2)}) copy-start(f32[512,512]{1,0:T(8,128)S(1)} %collective-permute-done.18.refs_2_) | copy-start | bytes 3145732
  117.0 12.7 %collective-permute-start.22 = (f32[512,512]{1,0:T(8,128)S(1)}, f32[512,512]{1,0:T(8,128)S(1)}, u32[]{:S(2)}, u32[]{:S(2)}) collective-permute-start(f32[512,512]{1,0:T(8,128)S(1)} %collective-permute-done.18.refs_2_), channel_id=1, source_target_pairs={{0,4},{4,0},{8,12},{12,8},{16,20},{20,16},{24,28},{28,24},{1,5},{5... | collective-permute-start | bytes 3145736 | tf_op jit(solution)/shard_map/ppermute | solution.py:264
  129.6 2.8 collective-permute-start.23
  129.6 1.6 copy-start.14
  (7 other events, 7.7 us)

commit v3 on v1

--- a/solution.py
+++ b/solution.py
@@ -1,6 +1,8 @@
 import jax
 import jax.numpy as jnp
 from jax import lax
+from jax.experimental import pallas as pl
+from jax.experimental.pallas import tpu as pltpu
 from jax.sharding import PartitionSpec as P
 
 clip_level = 1.0
@@ -60,63 +62,240 @@
     return pre * (clip_factor * jnp.sqrt(block_norm / (pre_norm + graft_eps)))
 
 
+MIB = 1 << 20
+F32 = jnp.float32
+HALVES = (0, 1)
+
+
+def split(value):
+    high = value.astype(jnp.bfloat16)
+    return high, (value - high.astype(F32)).astype(jnp.bfloat16)
+
+
+def narrow_dot(left_side, right_side, dims):
+    return lax.dot_general(left_side, right_side, (dims, ((), ())), preferred_element_type=F32)
+
+
+def split_product(left_side, right_side, dims=((1,), (0,))):
+    small = narrow_dot(left_side[0], right_side[1], dims) + narrow_dot(left_side[1], right_side[0], dims)
+    return narrow_dot(left_side[0], right_side[0], dims) + small
+
+
+def pair_target(slot, device):
+    first = 2 + 2 * (device & 1)
+    return device ^ ((slot >> 1) * first) ^ ((slot & 1) * (6 - first))
+
+
+def local_call(kernel, name, out_shape, operands, scalars=(), flops=0, vmem=None, **options):
+    whole = pl.BlockSpec(memory_space=pltpu.VMEM)
+    arrays = list(operands) + (list(out_shape) if isinstance(out_shape, (list, tuple)) else [out_shape])
+    moved = sum(array.size * array.dtype.itemsize for array in arrays)
+    return pl.pallas_call(
+        kernel,
+        in_specs=[pl.BlockSpec(memory_space=pltpu.SMEM)] * len(scalars) + [whole] * len(operands),
+        out_specs=jax.tree.map(lambda _: whole, out_shape),
+        out_shape=out_shape,
+        compiler_params=pltpu.CompilerParams(vmem_limit_bytes=vmem),
+        cost_estimate=pl.CostEstimate(flops=flops, bytes_accessed=moved, transcendentals=0),
+        name=name,
+        **options,
+    )(*scalars, *operands)
+
+
+def owner_block(owners_ref, grad_ref, rows, width, target):
+    column = 0
+    for index in range(1, grad_ref.shape[1] // width):
+        column = column + jnp.where(owners_ref[index] == target, index * width, 0)
+    columns = pl.ds(pl.multiple_of(column, width), width)
+    return grad_ref[rows, columns].astype(F32)
+
+
+def half_rows(half, width):
+    return pl.ds(half * (width // 2), width // 2)
+
+
+def half_shape(width):
+    return jax.ShapeDtypeStruct((width // 2, width), F32)
+
+
+def pack_call(owners, me, grads, slots, width):
+    def kernel(owners_ref, me_ref, grad_ref, *out_refs):
+        place = 0
+        for slot in slots:
+            target = pair_target(slot, me_ref[0] ^ 1)
+            for half in HALVES:
+                out_refs[place][...] = owner_block(owners_ref, grad_ref, half_rows(half, width), width, target)
+                place += 1
+
+    shapes = [half_shape(width)] * (2 * len(slots))
+    return local_call(kernel, "pack", shapes, (grads,), (owners, me), vmem=8 * MIB)
+
+
+def add_call(owners, me, grads, slot, half, arrivals, width):
+    def kernel(owners_ref, me_ref, grad_ref, *refs):
+        target = pair_target(slot, me_ref[0])
+        total = owner_block(owners_ref, grad_ref, half_rows(half, width), width, target)
+        for ref in refs[:-1]:
+            total = total + ref[...]
+        refs[-1][...] = total
+
+    return local_call(kernel, "add", half_shape(width), (grads, *arrivals), (owners, me), vmem=8 * MIB)
+
+
+def join_call(owners, me, grads, arrivals, width, device_count):
+    block_count = grads.shape[1] // width
+
+    def kernel(owners_ref, me_ref, grad_ref, *refs):
+        block_ref, norm_ref = refs[-2:]
+        squares = jnp.zeros((1, 1), F32)
+        for half in HALVES:
+            rows = half_rows(half, width)
+            total = owner_block(owners_ref, grad_ref, rows, width, me_ref[0])
+            for ref in refs[half:-2:2]:
+                total = total + ref[...]
+            block_ref[rows, :] = total
+            squares = squares + jnp.sum(total * total, keepdims=True).reshape(1, 1)
+        owned = 0
+        for index in range(block_count):
+            owned = owned + jnp.where(owners_ref[index] == me_ref[0], 1, 0)
+        norm_ref[...] = jnp.broadcast_to(squares * owned.astype(F32), norm_ref.shape)
+
+    shapes = [jax.ShapeDtypeStruct((width, width), F32), jax.ShapeDtypeStruct((device_count, 128), F32)]
+    return local_call(kernel, "join", shapes, (grads, *arrivals), (owners, me), vmem=8 * MIB)
+
+
+def gram_kernel(block_ref, left_ref, right_ref):
+    block = split(block_ref[...])
+    left_ref[...] = split_product(block, block, ((1,), (1,)))
+    right_ref[...] = split_product(block, block, ((0,), (0,)))
+
+
+def gram_call(block):
+    shape = jax.ShapeDtypeStruct(block.shape, F32)
+    flops = 12 * block.shape[0] ** 3
+    return local_call(gram_kernel, "gram", [shape, shape], (block,), flops=flops, vmem=16 * MIB)
+
+
+def root_of(previous, gram, gram_scale):
+    rows = lax.broadcasted_iota(jnp.int32, previous.shape, 0)
+    columns = lax.broadcasted_iota(jnp.int32, previous.shape, 1)
+    identity = jnp.where(rows == columns, 1.0, 0.0)
+    statistic = 0.5 * previous + gram * gram_scale
+    squares = jnp.sum(statistic * statistic, keepdims=True).reshape(1, 1)
+    frobenius = jnp.sqrt(squares)
+    scaled = statistic * (1.0 / frobenius)
+    parts = split(scaled)
+    square = split_product(parts, parts)
+    factor_square = split((25.0 * identity - 10.0 * scaled + square) * 0.0625)
+    factor_scaled = split((5.0 * scaled - square) * 0.25)
+    fourth = split(split_product(factor_square, factor_square))
+    tail = split_product(fourth, factor_scaled)
+    return (6.25 * identity - 1.25 * scaled - tail) * (0.25 * lax.rsqrt(jnp.sqrt(frobenius)))
+
+
+def update_call(block, left_gram, right_gram, left_prev, right_prev, norms, entry_count):
+    width = block.shape[0]
+
+    def kernel(block_ref, left_gram_ref, right_gram_ref, left_ref, right_ref, norm_ref, *out_refs):
+        squares = jnp.sum(norm_ref[:, :1], axis=0, keepdims=True)
+        clip_factor = jnp.minimum(1.0, clip_level / jnp.sqrt(squares / entry_count))
+        gram_scale = clip_factor * clip_factor / width
+        left_root = root_of(left_ref[...], left_gram_ref[...], gram_scale)
+        right_root = root_of(right_ref[...], right_gram_ref[...], gram_scale)
+        block = block_ref[...]
+        halfway = split_product(split(left_root), split(block))
+        pre = split_product(split(halfway), split(right_root)) * clip_factor
+        block_norm = jnp.sum(block * block, keepdims=True).reshape(1, 1) * (clip_factor * clip_factor)
+        pre_norm = jnp.sum(pre * pre, keepdims=True).reshape(1, 1)
+        update = pre * jnp.sqrt(block_norm / (pre_norm + graft_eps))
+        for half in HALVES:
+            out_refs[half][...] = update[half * (width // 2) : (half + 1) * (width // 2)]
+
+    operands = (block, left_gram, right_gram, left_prev, right_prev, norms)
+    shapes = [half_shape(width)] * 2
+    return local_call(kernel, "update", shapes, operands, flops=48 * width**3, vmem=24 * MIB)
+
+
+def assemble_call(owners, me, slots, block_count):
+    width = slots[0].shape[1]
+
+    def kernel(owners_ref, me_ref, *refs):
+        out_ref, sem = refs[-2:]
+
+        def spot(index, half):
+            return out_ref.at[half_rows(half, width), pl.ds(index * width, width)]
+
+        for index in range(block_count):
+            for place in range(8):
+                target = pair_target(place & 3, me_ref[0] ^ (place >> 2))
+
+                @pl.when(owners_ref[index] == target)
+                def _():
+                    for half in HALVES:
+                        source = refs[2 * place + half]
+                        pltpu.make_async_copy(source, spot(index, half), sem.at[index, half]).start()
+
+        for index in range(block_count):
+            for half in HALVES:
+                pltpu.make_async_copy(refs[half], spot(index, half), sem.at[index, half]).wait()
+
+    return pl.pallas_call(
+        kernel,
+        in_specs=[pl.BlockSpec(memory_space=pltpu.SMEM)] * 2
+        + [pl.BlockSpec(memory_space=pltpu.VMEM)] * len(slots),
+        out_specs=pl.BlockSpec(memory_space=pl.ANY),
+        out_shape=jax.ShapeDtypeStruct((width, block_count * width), F32),
+        scratch_shapes=[pltpu.SemaphoreType.DMA((block_count, 2))],
+        cost_estimate=pl.CostEstimate(
+            flops=0, bytes_accessed=8 * width * width * block_count, transcendentals=0
+        ),
+        name="assemble",
+    )(owners, me, *slots)
+
+
 def paired_body(replica_grads, owners, left_stats, right_stats):
     width = left_stats.shape[1]
     owner_row = owners[0]
     block_count = owner_row.shape[0]
-    me = lax.axis_index("dp")
-    core = me & 1
+    me = lax.axis_index("dp").astype(jnp.int32).reshape(1)
+    device_count = 8 * lax.axis_size("mp")
     entry_count = width * block_count * width * lax.axis_size("mp")
     grads = replica_grads[0]
-    matches = (owner_row[None, :] == jnp.arange(8, dtype=jnp.int32)[:, None]).astype(jnp.int32)
-    owned = jnp.sum(matches, axis=1)
-    block_of = jnp.sum(matches * jnp.arange(block_count, dtype=jnp.int32)[None, :], axis=1)
-
-    first_pairs = [(i, i ^ (2 if i % 2 == 0 else 4)) for i in range(8)]
-    second_pairs = [(i, i ^ (4 if i % 2 == 0 else 2)) for i in range(8)]
+
+    first_pairs = [(i, i ^ (2 + 2 * (i % 2))) for i in range(8)]
+    second_pairs = [(i, i ^ (4 - 2 * (i % 2))) for i in range(8)]
     core_pairs = [(i, i ^ 1) for i in range(8)]
 
     def over(pairs, value):
         return lax.ppermute(value, "dp", pairs)
 
-    def target(slot, device):
-        device_core = device & 1
-        first = jnp.where(device_core == 0, 2, 4)
-        second = 6 - first
-        return device ^ ((slot >> 1) * first) ^ ((slot & 1) * second)
-
-    def own_piece(device_target):
-        column = block_of[device_target] * width
-        return lax.dynamic_slice(grads, (0, column), (width, width)).astype(jnp.float32)
-
-    sums = {}
-    for slot in (3, 2, 1, 0):
-        arrived = over(core_pairs, own_piece(target(slot, me ^ 1)))
-        sums[slot] = arrived + own_piece(target(slot, me))
-    sum_one = sums[1] + over(first_pairs, sums[3])
-    sum_zero = sums[0] + over(first_pairs, sums[2])
-    block = sum_zero + over(second_pairs, sum_one)
-
-    block_norm = jnp.sum(block * block)
-    mine = owned[me] > 0
-    squares = lax.psum(jnp.where(mine, block_norm, 0.0), ("dp", "mp"))
-    clip_factor = jnp.minimum(1.0, clip_level / jnp.sqrt(squares / entry_count))
-    update = block_update(block, block_norm, clip_factor, left_stats[0], right_stats[0])
-
-    mine_near = over(second_pairs, update)
-    mine_far = over(first_pairs, update)
-    near_far = over(first_pairs, mine_near)
-    held = [update, mine_near, mine_far, near_far]
+    def own_plus(slot, half, *arrivals):
+        return add_call(owner_row, me, grads, slot, half, arrivals, width)
+
+    packed = {}
+    for slots in ((3, 2), (1, 0)):
+        pieces = pack_call(owner_row, me, grads, slots, width)
+        packed.update(zip([(slot, half) for slot in slots for half in HALVES], pieces))
+    from_core = {key: over(core_pairs, value) for key, value in packed.items()}
+    from_first = {}
+    for slot in (3, 2):
+        for half in HALVES:
+            from_first[slot, half] = over(first_pairs, own_plus(slot, half, from_core[slot, half]))
+    from_second = [
+        over(second_pairs, own_plus(1, half, from_core[1, half], from_first[3, half])) for half in HALVES
+    ]
+    arrivals = [from_core[0, half] for half in HALVES] + [from_first[2, half] for half in HALVES]
+    block, norm = join_call(owner_row, me, grads, arrivals + from_second, width, device_count)
+    norms = lax.all_to_all(norm, ("dp", "mp"), split_axis=0, concat_axis=0, tiled=True)
+    left_gram, right_gram = gram_call(block)
+    update = update_call(block, left_gram, right_gram, left_stats[0], right_stats[0], norms, entry_count)
+
+    near = [over(second_pairs, value) for value in update]
+    far = [over(first_pairs, value) for value in update]
+    relayed = [over(first_pairs, value) for value in near]
+    held = list(update) + near + far + relayed
     slots = held + [over(core_pairs, value) for value in held]
-    places = jnp.stack(
-        [target(slot, me) for slot in range(4)] + [target(slot, me ^ 1) for slot in range(4)]
-    )
-    stacked = jnp.stack(slots)
-    pieces = []
-    for index in range(block_count):
-        place = jnp.argmax(places == owner_row[index])
-        pieces.append(lax.dynamic_index_in_dim(stacked, place, 0, keepdims=False))
-    return jnp.concatenate(pieces, axis=1)
+    return assemble_call(owner_row, me, slots, block_count)
 
 
 def solution(mesh):

time: 205 us -> 117 us (0.57)
  blocking collectives: 39.9 us -> 0 us
  local copies, waits for them, and re-layouts: 36.1 us -> 10.3 us
  Pallas kernels: 0 us -> 23 us
  other arithmetic: 21.9 us -> 0 us
  between operations: 21.2 us -> 0.37 us
  matrix products: 18.3 us -> 0 us
  starting transfers between devices: 15.5 us -> 24.7 us
  waiting for transfers between devices: 50.9 us -> 58 us
    psum x1 -> x0, blocking collectives: 39.9 us -> none  [paired_body(): squares = lax.psum(jnp.where(mine, block_norm, 0.0), ('dp', 'mp'))]
    pallas_call x0 -> x12, Pallas kernels: none -> 23 us  [the longest x11 16.9 us: local_call(): pl.pallas_call(kernel, in_specs=[pl.BlockSpec(memory_space=pltpu.SMEM)] *...]
    dot_general x10 -> x0, matrix products: 18.3 us -> none  [mat_product(): return jnp.matmul(left_side, right_side, precision=lax.Precision.HIGH)]
    dynamic_slice x9 -> x0, local copies, waits for them, and re-layouts: 16.5 us -> none  [the longest x7 15.1 us: paired_body(): pieces.append(lax.dynamic_index_in_dim(stacked, place, 0, keepdims=False))]
    another operation x6 -> x0, other arithmetic: 8.21 us -> none  [paired_body(): place = jnp.argmax(places == owner_row[index])]
    unnamed x29 -> x50, local copies, waits for them, and re-layouts: 16.7 us -> 10.3 us
    all_to_all x0 -> x1, starting transfers between devices: none -> 6.1 us  [paired_body(): lax.all_to_all(norm, ('dp', 'mp'), split_axis=0, concat_axis=0, tiled=True)]
    add x2 -> x0, other arithmetic: 5.12 us -> none  [paired_body(): sums[slot] = arrived + own_piece(target(slot, me))]
  transfers between devices with their start and end apart: 14 -> 29, of which waited for: 4 -> 11; matrix products, arithmetic and copies ran while one was open for 12% -> 0% of each run, Pallas kernels for 0% -> 5%
where the time goes in v3:
time: 117 us; the launch traced here: 116 us
  waiting for transfers between devices  58 us (50%)
  starting transfers between devices  24.7 us (21%)
  Pallas kernels  23 us (20%)
  local copies, waits for them, and re-layouts  10.3 us (9%)
    ppermute x28, waiting for transfers between devices, over(): return lax.ppermute(value, 'dp', pairs)  54.7 us
    ppermute x28, starting transfers between devices, over(): return lax.ppermute(value, 'dp', pairs)  18.6 us
    pallas_call x11, Pallas kernels, local_call(): pl.pallas_call(kernel, in_specs=[pl.BlockSpec(memory_space=pltpu.SMEM)] *...  16.9 us
    unnamed x50, local copies, waits for them, and re-layouts  10.3 us
    pallas_call x1, Pallas kernels, assemble_call(): pl.pallas_call(kernel, in_specs=[pl.BlockSpec(memory_space=pltpu.SMEM)] *...  6.16 us
    all_to_all x1, starting transfers between devices, paired_body(): lax.all_to_all(norm, ('dp', 'mp'), split_axis=0, concat_axis=0, tiled=True)  6.1 us
    all_to_all x1, waiting for transfers between devices, paired_body(): lax.all_to_all(norm, ('dp', 'mp'), split_axis=0, concat_axis=0, tiled=True)  3.31 us
  transfers between devices with their start and end apart: 29, of which 11 were waited for; matrix products, arithmetic and copies ran while one was open for 0% of the time, Pallas kernels for 5%

profile of v3, /device:TPU:0, one launch (start us, length us, event | category | flops | bytes accessed | tf_op | source)
XLA Modules:
  0.0 116.4 jit_solution(2234638197686711850)
XLA Ops:
  0.0 1.9 %copy-done = bf16[1,512,3072]{2,1,0:T(8,128)(2,1)S(1)} copy-done((bf16[1,512,3072]{2,1,0:T(8,128)(2,1)S(1)}, bf16[1,512,3072]{2,1,0:T(8,128)(2,1)}, u32[]{:S(2)}) %copy-start) | copy-done | bytes 3145752
  2.5 0.7 pack.3
  6.1 2.7 %collective-permute-start.8 = (f32[256,512]{1,0:T(8,128)S(1)}, f32[256,512]{1,0:T(8,128)S(1)}, u32[]{:S(2)}, u32[]{:S(2)}) collective-permute-start(f32[256,512]{1,0:T(8,128)S(1)} %add.8), channel_id=1, source_target_pairs={{0,8},{4,20},{8,0},{12,28},{16,24},{20,4},{24,16},{28,12},{1,9},{5... | collective-permute-start | bytes 1572872 | tf_op jit(solution)/shard_map/ppermute | solution.py:270
  9.6 1.6 %collective-permute-start.12 = (f32[256,512]{1,0:T(8,128)S(1)}, f32[256,512]{1,0:T(8,128)S(1)}, u32[]{:S(2)}, u32[]{:S(2)}) collective-permute-start(f32[256,512]{1,0:T(8,128)S(1)} %add.10), channel_id=1, source_target_pairs={{0,8},{4,20},{8,0},{12,28},{16,24},{20,4},{24,16},{28,12},{1,9},{5... | collective-permute-start | bytes 1572872 | tf_op jit(solution)/shard_map/ppermute | solution.py:270
  12.9 3.1 %collective-permute-done.8.refs_1_ = f32[256,512]{1,0:T(8,128)S(1)} collective-permute-done((f32[256,512]{1,0:T(8,128)S(1)}, f32[256,512]{1,0:T(8,128)S(1)}, u32[]{:S(2)}, u32[]{:S(2)}) %collective-permute-start.8) | collective-permute-done | bytes 524320 | tf_op jit(solution)/shard_map/ppermute | solution.py:270
  16.0 2.0 %collective-permute-start.3 = (f32[256,512]{1,0:T(8,128)S(1)}, f32[256,512]{1,0:T(8,128)S(1)}, u32[]{:S(2)}, u32[]{:S(2)}) collective-permute-start(f32[256,512]{1,0:T(8,128)S(1)} %add.6), channel_id=1, source_target_pairs={{0,8},{4,20},{8,0},{12,28},{16,24},{20,4},{24,16},{28,12},{1,9},{5... | collective-permute-start | bytes 1572872 | tf_op jit(solution)/shard_map/ppermute | solution.py:270
  18.7 2.9 %collective-permute-done.12.refs_1_ = f32[256,512]{1,0:T(8,128)S(1)} collective-permute-done((f32[256,512]{1,0:T(8,128)S(1)}, f32[256,512]{1,0:T(8,128)S(1)}, u32[]{:S(2)}, u32[]{:S(2)}) %collective-permute-start.12) | collective-permute-done | bytes 524320 | tf_op jit(solution)/shard_map/ppermute | solution.py:270
  21.6 2.0 %collective-permute-start.9 = (f32[256,512]{1,0:T(8,128)S(1)}, f32[256,512]{1,0:T(8,128)S(1)}, u32[]{:S(2)}, u32[]{:S(2)}) collective-permute-start(f32[256,512]{1,0:T(8,128)S(1)} %add.9), channel_id=1, source_target_pairs={{0,16},{4,12},{8,24},{12,4},{16,0},{20,28},{24,8},{28,20},{1,17},{... | collective-permute-start | bytes 1572872 | tf_op jit(solution)/shard_map/ppermute | solution.py:270
  24.4 5.9 %collective-permute-done.3.refs_2_ = f32[256,512]{1,0:T(8,128)S(1)} collective-permute-done((f32[256,512]{1,0:T(8,128)S(1)}, f32[256,512]{1,0:T(8,128)S(1)}, u32[]{:S(2)}, u32[]{:S(2)}) %collective-permute-start.3) | collective-permute-done | bytes 524320 | tf_op jit(solution)/shard_map/ppermute | solution.py:270
  30.3 11.2 %collective-permute-done.5.refs_3_ = f32[256,512]{1,0:T(8,128)S(1)} collective-permute-done((f32[256,512]{1,0:T(8,128)S(1)}, f32[256,512]{1,0:T(8,128)S(1)}, u32[]{:S(2)}, u32[]{:S(2)}) %collective-permute-start.5) | collective-permute-done | bytes 524320 | tf_op jit(solution)/shard_map/ppermute | solution.py:270
  41.6 2.2 %collective-permute-done.13.refs_5_ = f32[256,512]{1,0:T(8,128)S(1)} collective-permute-done((f32[256,512]{1,0:T(8,128)S(1)}, f32[256,512]{1,0:T(8,128)S(1)}, u32[]{:S(2)}, u32[]{:S(2)}) %collective-permute-start.13) | collective-permute-done | bytes 524320 | tf_op jit(solution)/shard_map/ppermute | solution.py:270
  43.8 1.8 %join.1 = (f32[512,512]{1,0:T(8,128)S(1)}, f32[32,128]{1,0:T(8,128)}) custom-call(s32[6]{0:T(128)S(1)} %bitcast.27, s32[1]{0:T(128)} %bitcast.1.me_ref, bf16[512,3072]{1,0:T(8,128)(2,1)S(1)} %bitcast.17, f32[256,512]{1,0:T(8,128)S(1)} %collective-permute-done.refs_0_, f32[256,512]{1,0:T(8,128)S(1)} %collective-permute-done.1.refs_1_, ...), custom_call_target="tpu_custom_call" | custom-call | bytes 7356416 | tf_op jit(solution)/shard_map/join/pallas_call | solution.py:93
  45.6 6.1 %all-to-all-start = ((f32[32,1,128]{2,1,0:T(1,128)}), f32[32,1,128]{2,1,0:T(1,128)S(1)}, u32[]{:S(2)}, u32[]{:S(2)}) async-start(f32[32,1,128]{2,1,0:T(1,128)} %bitcast.6), calls=%async_computation | async-start | bytes 32768 | tf_op jit(solution)/shard_map/all_to_all | solution.py:289
  51.7 1.8 %gram.1 = (f32[512,512]{1,0:T(8,128)S(1)}, f32[512,512]{1,0:T(8,128)S(1)}) custom-call(f32[512,512]{1,0:T(8,128)S(1)} %get-tuple-element.27.block_ref), custom_call_target="tpu_custom_call" | custom-call | flops 1610612736 | bytes 3145728 | tf_op jit(solution)/shard_map/gram/pallas_call | solution.py:93
  53.5 1.0 copy-done.8
  54.6 1.0 copy-done.10
  55.5 3.3 %all-to-all-done = f32[32,1,128]{2,1,0:T(1,128)S(1)} async-done(((f32[32,1,128]{2,1,0:T(1,128)}), f32[32,1,128]{2,1,0:T(1,128)S(1)}, u32[]{:S(2)}, u32[]{:S(2)}) %all-to-all-start) | async-done | bytes 16416 | tf_op jit(solution)/shard_map/all_to_all | solution.py:289
  58.9 1.2 %copy-done.7 = f32[512,512]{1,0:T(8,128)S(1)} copy-done((f32[512,512]{1,0:T(8,128)S(1)}, f32[512,512]{1,0:T(8,128)}, u32[]{:S(2)}) %copy-start.7) | copy-done | bytes 1048600
  60.1 1.2 %copy-done.9 = f32[512,512]{1,0:T(8,128)S(1)} copy-done((f32[512,512]{1,0:T(8,128)S(1)}, f32[512,512]{1,0:T(8,128)}, u32[]{:S(2)}) %copy-start.9) | copy-done | bytes 1048600
  61.3 1.2 %copy-done.11 = f32[512,512]{1,0:T(8,128)S(1)} copy-done((f32[512,512]{1,0:T(8,128)S(1)}, f32[512,512]{1,0:T(8,128)}, u32[]{:S(2)}) %copy-start.11) | copy-done | bytes 1048600
  62.5 8.3 %update.1 = (f32[256,512]{1,0:T(8,128)S(1)}, f32[256,512]{1,0:T(8,128)S(1)}) custom-call(f32[512,512]{1,0:T(8,128)S(1)} %copy-done.7, f32[512,512]{1,0:T(8,128)S(1)} %copy-done.9, f32[512,512]{1,0:T(8,128)S(1)} %copy-done.11, f32[512,512]{1,0:T(8,128)S(1)} %bitcast.29, f32[512,512]{1,0:T(8,128)S(1)} %bitcast.30, f32[32,128]{1,0:T(8,128)S(1)} %bitcast.28), custom_call_target="tpu_custom_call" | custom-call | flops 6442450944 | bytes 6307840 | tf_op jit(solution)/shard_map/update/pallas_call | solution.py:93
  72.1 1.5 %collective-permute-start.15 = (f32[256,512]{1,0:T(8,128)S(1)}, f32[256,512]{1,0:T(8,128)S(1)}, u32[]{:S(2)}, u32[]{:S(2)}) collective-permute-start(f32[256,512]{1,0:T(8,128)S(1)} %get-tuple-element.32.refs_1_), channel_id=1, source_target_pairs={{0,16},{4,12},{8,24},{12,4},{16,0},{20,28},{24,8},{28,20},{1,17},{... | collective-permute-start | bytes 1572872 | tf_op jit(solution)/shard_map/ppermute | solution.py:270
  73.6 1.5 %collective-permute-start.17 = (f32[256,512]{1,0:T(8,128)S(1)}, f32[256,512]{1,0:T(8,128)S(1)}, u32[]{:S(2)}, u32[]{:S(2)}) collective-permute-start(f32[256,512]{1,0:T(8,128)S(1)} %get-tuple-element.32.refs_1_), channel_id=1, source_target_pairs={{0,8},{4,20},{8,0},{12,28},{16,24},{20,4},{24,16},{28,12},{1,9},{5... | collective-permute-start | bytes 1572872 | tf_op jit(solution)/shard_map/ppermute | solution.py:270
  75.1 10.7 %collective-permute-done.16.refs_4_ = f32[256,512]{1,0:T(8,128)S(1)} collective-permute-done((f32[256,512]{1,0:T(8,128)S(1)}, f32[256,512]{1,0:T(8,128)S(1)}, u32[]{:S(2)}, u32[]{:S(2)}) %collective-permute-start.16) | collective-permute-done | bytes 524320 | tf_op jit(solution)/shard_map/ppermute | solution.py:270
  86.4 1.5 %collective-permute-start.18 = (f32[256,512]{1,0:T(8,128)S(1)}, f32[256,512]{1,0:T(8,128)S(1)}, u32[]{:S(2)}, u32[]{:S(2)}) collective-permute-start(f32[256,512]{1,0:T(8,128)S(1)} %collective-permute-done.14.refs_2_), channel_id=1, source_target_pairs={{0,8},{4,20},{8,0},{12,28},{16,24},{20,4},{24,16},{28,12},{1,9},{5... | collective-permute-start | bytes 1572872 | tf_op jit(solution)/shard_map/ppermute | solution.py:270
  87.9 9.7 %collective-permute-done.15.refs_3_ = f32[256,512]{1,0:T(8,128)S(1)} collective-permute-done((f32[256,512]{1,0:T(8,128)S(1)}, f32[256,512]{1,0:T(8,128)S(1)}, u32[]{:S(2)}, u32[]{:S(2)}) %collective-permute-start.15) | collective-permute-done | bytes 524320 | tf_op jit(solution)/shard_map/ppermute | solution.py:270
  97.6 1.5 %collective-permute-start.19 = (f32[256,512]{1,0:T(8,128)S(1)}, f32[256,512]{1,0:T(8,128)S(1)}, u32[]{:S(2)}, u32[]{:S(2)}) collective-permute-start(f32[256,512]{1,0:T(8,128)S(1)} %collective-permute-done.15.refs_3_), channel_id=1, source_target_pairs={{0,8},{4,20},{8,0},{12,28},{16,24},{20,4},{24,16},{28,12},{1,9},{5... | collective-permute-start | bytes 1572872 | tf_op jit(solution)/shard_map/ppermute | solution.py:270
  99.7 2.7 %collective-permute-done.18.refs_6_ = f32[256,512]{1,0:T(8,128)S(1)} collective-permute-done((f32[256,512]{1,0:T(8,128)S(1)}, f32[256,512]{1,0:T(8,128)S(1)}, u32[]{:S(2)}, u32[]{:S(2)}) %collective-permute-start.18) | collective-permute-done | bytes 524320 | tf_op jit(solution)/shard_map/ppermute | solution.py:270
  102.4 5.6 %collective-permute-done.19.refs_7_ = f32[256,512]{1,0:T(8,128)S(1)} collective-permute-done((f32[256,512]{1,0:T(8,128)S(1)}, f32[256,512]{1,0:T(8,128)S(1)}, u32[]{:S(2)}, u32[]{:S(2)}) %collective-permute-start.19) | collective-permute-done | bytes 524320 | tf_op jit(solution)/shard_map/ppermute | solution.py:270
  108.1 0.7 copy-done.20
  109.4 0.8 copy-done.24
  110.3 6.2 %assemble.1 = f32[512,3072]{1,0:T(8,128)} custom-call(s32[6]{0:T(128)} %bitcast.18, s32[1]{0:T(128)} %bitcast.1.me_ref, f32[256,512]{1,0:T(8,128)} %copy-done.1, f32[256,512]{1,0:T(8,128)} %copy-done.2, f32[256,512]{1,0:T(8,128)} %copy-done.14, f32[256,512]{1,0:T(8,128)} %copy-done.15, f32[256,512]{1,0:T(8,128)} %copy-done.13, f32[256,512]{1,0:T(8,128)} %copy-done.17, ...), custom_call_target="tpu_custom_call" | custom-call | bytes 12582912 | tf_op jit(solution)/shard_map/assemble/pallas_call | solution.py:242
  (88 shorter events, 10.5 us)
Async XLA Ops:
  3.2 2.3 %collective-permute-start.7 = (f32[256,512]{1,0:T(8,128)S(1)}, f32[256,512]{1,0:T(8,128)S(1)}, u32[]{:S(2)}, u32[]{:S(2)}) collective-permute-start(f32[256,512]{1,0:T(8,128)S(1)} %get-tuple-element.24), channel_id=1, source_target_pairs={{0,4},{4,0},{8,12},{12,8},{16,20},{20,16},{24,28},{28,24},{1,5},{5... | collective-permute-start | bytes 1572872 | tf_op jit(solution)/shard_map/ppermute | solution.py:270
  3.8 5.1 %collective-permute-start.11 = (f32[256,512]{1,0:T(8,128)S(1)}, f32[256,512]{1,0:T(8,128)S(1)}, u32[]{:S(2)}, u32[]{:S(2)}) collective-permute-start(f32[256,512]{1,0:T(8,128)S(1)} %get-tuple-element.26), channel_id=1, source_target_pairs={{0,4},{4,0},{8,12},{12,8},{16,20},{20,16},{24,28},{28,24},{1,5},{5... | collective-permute-start | bytes 1572872 | tf_op jit(solution)/shard_map/ppermute | solution.py:270
  3.8 5.7 %collective-permute-start.2 = (f32[256,512]{1,0:T(8,128)S(1)}, f32[256,512]{1,0:T(8,128)S(1)}, u32[]{:S(2)}, u32[]{:S(2)}) collective-permute-start(f32[256,512]{1,0:T(8,128)S(1)} %get-tuple-element.21), channel_id=1, source_target_pairs={{0,4},{4,0},{8,12},{12,8},{16,20},{20,16},{24,28},{28,24},{1,5},{5... | collective-permute-start | bytes 1572872 | tf_op jit(solution)/shard_map/ppermute | solution.py:270
  4.3 6.9 %collective-permute-start.4 = (f32[256,512]{1,0:T(8,128)S(1)}, f32[256,512]{1,0:T(8,128)S(1)}, u32[]{:S(2)}, u32[]{:S(2)}) collective-permute-start(f32[256,512]{1,0:T(8,128)S(1)} %get-tuple-element.22), channel_id=1, source_target_pairs={{0,4},{4,0},{8,12},{12,8},{16,20},{20,16},{24,28},{28,24},{1,5},{5... | collective-permute-start | bytes 1572872 | tf_op jit(solution)/shard_map/ppermute | solution.py:270
  5.0 7.4 %collective-permute-start.6 = (f32[256,512]{1,0:T(8,128)S(1)}, f32[256,512]{1,0:T(8,128)S(1)}, u32[]{:S(2)}, u32[]{:S(2)}) collective-permute-start(f32[256,512]{1,0:T(8,128)S(1)} %get-tuple-element.23), channel_id=1, source_target_pairs={{0,4},{4,0},{8,12},{12,8},{16,20},{20,16},{24,28},{28,24},{1,5},{5... | collective-permute-start | bytes 1572872 | tf_op jit(solution)/shard_map/ppermute | solution.py:270
  6.1 9.8 %collective-permute-start.8 = (f32[256,512]{1,0:T(8,128)S(1)}, f32[256,512]{1,0:T(8,128)S(1)}, u32[]{:S(2)}, u32[]{:S(2)}) collective-permute-start(f32[256,512]{1,0:T(8,128)S(1)} %add.8), channel_id=1, source_target_pairs={{0,8},{4,20},{8,0},{12,28},{16,24},{20,4},{24,16},{28,12},{1,9},{5... | collective-permute-start | bytes 1572872 | tf_op jit(solution)/shard_map/ppermute | solution.py:270
  8.8 9.8 %collective-permute-start.10 = (f32[256,512]{1,0:T(8,128)S(1)}, f32[256,512]{1,0:T(8,128)S(1)}, u32[]{:S(2)}, u32[]{:S(2)}) collective-permute-start(f32[256,512]{1,0:T(8,128)S(1)} %get-tuple-element.25), channel_id=1, source_target_pairs={{0,4},{4,0},{8,12},{12,8},{16,20},{20,16},{24,28},{28,24},{1,5},{5... | collective-permute-start | bytes 1572872 | tf_op jit(solution)/shard_map/ppermute | solution.py:270
  9.6 12.0 %collective-permute-start.12 = (f32[256,512]{1,0:T(8,128)S(1)}, f32[256,512]{1,0:T(8,128)S(1)}, u32[]{:S(2)}, u32[]{:S(2)}) collective-permute-start(f32[256,512]{1,0:T(8,128)S(1)} %add.10), channel_id=1, source_target_pairs={{0,8},{4,20},{8,0},{12,28},{16,24},{20,4},{24,16},{28,12},{1,9},{5... | collective-permute-start | bytes 1572872 | tf_op jit(solution)/shard_map/ppermute | solution.py:270
  11.1 13.2 %collective-permute-start = (f32[256,512]{1,0:T(8,128)S(1)}, f32[256,512]{1,0:T(8,128)S(1)}, u32[]{:S(2)}, u32[]{:S(2)}) collective-permute-start(f32[256,512]{1,0:T(8,128)S(1)} %get-tuple-element.19), channel_id=1, source_target_pairs={{0,4},{4,0},{8,12},{12,8},{16,20},{20,16},{24,28},{28,24},{1,5},{5... | collective-permute-start | bytes 1572872 | tf_op jit(solution)/shard_map/ppermute | solution.py:270
  12.5 11.9 %collective-permute-start.1 = (f32[256,512]{1,0:T(8,128)S(1)}, f32[256,512]{1,0:T(8,128)S(1)}, u32[]{:S(2)}, u32[]{:S(2)}) collective-permute-start(f32[256,512]{1,0:T(8,128)S(1)} %get-tuple-element.20), channel_id=1, source_target_pairs={{0,4},{4,0},{8,12},{12,8},{16,20},{20,16},{24,28},{28,24},{1,5},{5... | collective-permute-start | bytes 1572872 | tf_op jit(solution)/shard_map/ppermute | solution.py:270
  16.0 14.4 %collective-permute-start.3 = (f32[256,512]{1,0:T(8,128)S(1)}, f32[256,512]{1,0:T(8,128)S(1)}, u32[]{:S(2)}, u32[]{:S(2)}) collective-permute-start(f32[256,512]{1,0:T(8,128)S(1)} %add.6), channel_id=1, source_target_pairs={{0,8},{4,20},{8,0},{12,28},{16,24},{20,4},{24,16},{28,12},{1,9},{5... | collective-permute-start | bytes 1572872 | tf_op jit(solution)/shard_map/ppermute | solution.py:270
  18.6 22.9 %collective-permute-start.5 = (f32[256,512]{1,0:T(8,128)S(1)}, f32[256,512]{1,0:T(8,128)S(1)}, u32[]{:S(2)}, u32[]{:S(2)}) collective-permute-start(f32[256,512]{1,0:T(8,128)S(1)} %add.7), channel_id=1, source_target_pairs={{0,8},{4,20},{8,0},{12,28},{16,24},{20,4},{24,16},{28,12},{1,9},{5... | collective-permute-start | bytes 1572872 | tf_op jit(solution)/shard_map/ppermute | solution.py:270
  21.6 20.0 %collective-permute-start.9 = (f32[256,512]{1,0:T(8,128)S(1)}, f32[256,512]{1,0:T(8,128)S(1)}, u32[]{:S(2)}, u32[]{:S(2)}) collective-permute-start(f32[256,512]{1,0:T(8,128)S(1)} %add.9), channel_id=1, source_target_pairs={{0,16},{4,12},{8,24},{12,4},{16,0},{20,28},{24,8},{28,20},{1,17},{... | collective-permute-start | bytes 1572872 | tf_op jit(solution)/shard_map/ppermute | solution.py:270
  24.3 19.5 %collective-permute-start.13 = (f32[256,512]{1,0:T(8,128)S(1)}, f32[256,512]{1,0:T(8,128)S(1)}, u32[]{:S(2)}, u32[]{:S(2)}) collective-permute-start(f32[256,512]{1,0:T(8,128)S(1)} %add.11), channel_id=1, source_target_pairs={{0,16},{4,12},{8,24},{12,4},{16,0},{20,28},{24,8},{28,20},{1,17},{... | collective-permute-start | bytes 1572872 | tf_op jit(solution)/shard_map/ppermute | solution.py:270
  45.6 13.3 %all-to-all-start = ((f32[32,1,128]{2,1,0:T(1,128)}), f32[32,1,128]{2,1,0:T(1,128)S(1)}, u32[]{:S(2)}, u32[]{:S(2)}) async-start(f32[32,1,128]{2,1,0:T(1,128)} %bitcast.6), calls=%async_computation | async-start | bytes 32768 | tf_op jit(solution)/shard_map/all_to_all | solution.py:289
  70.8 39.4 %copy-start.1 = (f32[256,512]{1,0:T(8,128)}, f32[256,512]{1,0:T(8,128)S(1)}, u32[]{:S(2)}) copy-start(f32[256,512]{1,0:T(8,128)S(1)} %get-tuple-element.31.refs_0_) | copy-start | bytes 1572868
  70.8 39.4 %copy-start.2 = (f32[256,512]{1,0:T(8,128)}, f32[256,512]{1,0:T(8,128)S(1)}, u32[]{:S(2)}) copy-start(f32[256,512]{1,0:T(8,128)S(1)} %get-tuple-element.32.refs_1_) | copy-start | bytes 1572868
  70.8 2.8 %collective-permute-start.20 = (f32[256,512]{1,0:T(8,128)S(1)}, f32[256,512]{1,0:T(8,128)S(1)}, u32[]{:S(2)}, u32[]{:S(2)}) collective-permute-start(f32[256,512]{1,0:T(8,128)S(1)} %get-tuple-element.31.refs_0_), channel_id=1, source_target_pairs={{0,4},{4,0},{8,12},{12,8},{16,20},{20,16},{24,28},{28,24},{1,5},{5... | collective-permute-start | bytes 1572872 | tf_op jit(solution)/shard_map/ppermute | solution.py:270
  70.9 14.9 %collective-permute-start.16 = (f32[256,512]{1,0:T(8,128)S(1)}, f32[256,512]{1,0:T(8,128)S(1)}, u32[]{:S(2)}, u32[]{:S(2)}) collective-permute-start(f32[256,512]{1,0:T(8,128)S(1)} %get-tuple-element.31.refs_0_), channel_id=1, source_target_pairs={{0,8},{4,20},{8,0},{12,28},{16,24},{20,4},{24,16},{28,12},{1,9},{5... | collective-permute-start | bytes 1572872 | tf_op jit(solution)/shard_map/ppermute | solution.py:270
  71.6 14.8 %collective-permute-start.14 = (f32[256,512]{1,0:T(8,128)S(1)}, f32[256,512]{1,0:T(8,128)S(1)}, u32[]{:S(2)}, u32[]{:S(2)}) collective-permute-start(f32[256,512]{1,0:T(8,128)S(1)} %get-tuple-element.31.refs_0_), channel_id=1, source_target_pairs={{0,16},{4,12},{8,24},{12,4},{16,0},{20,28},{24,8},{28,20},{1,17},{... | collective-permute-start | bytes 1572872 | tf_op jit(solution)/shard_map/ppermute | solution.py:270
  72.1 25.5 %collective-permute-start.15 = (f32[256,512]{1,0:T(8,128)S(1)}, f32[256,512]{1,0:T(8,128)S(1)}, u32[]{:S(2)}, u32[]{:S(2)}) collective-permute-start(f32[256,512]{1,0:T(8,128)S(1)} %get-tuple-element.32.refs_1_), channel_id=1, source_target_pairs={{0,16},{4,12},{8,24},{12,4},{16,0},{20,28},{24,8},{28,20},{1,17},{... | collective-permute-start | bytes 1572872 | tf_op jit(solution)/shard_map/ppermute | solution.py:270
  73.6 25.5 %collective-permute-start.21 = (f32[256,512]{1,0:T(8,128)S(1)}, f32[256,512]{1,0:T(8,128)S(1)}, u32[]{:S(2)}, u32[]{:S(2)}) collective-permute-start(f32[256,512]{1,0:T(8,128)S(1)} %get-tuple-element.32.refs_1_), channel_id=1, source_target_pairs={{0,4},{4,0},{8,12},{12,8},{16,20},{20,16},{24,28},{28,24},{1,5},{5... | collective-permute-start | bytes 1572872 | tf_op jit(solution)/shard_map/ppermute | solution.py:270
  73.6 36.6 %copy-start.12 = (f32[256,512]{1,0:T(8,128)}, f32[256,512]{1,0:T(8,128)S(1)}, u32[]{:S(2)}) copy-start(f32[256,512]{1,0:T(8,128)S(1)} %collective-permute-done.20.refs_8_) | copy-start | bytes 1572868
  73.6 25.5 %collective-permute-start.17 = (f32[256,512]{1,0:T(8,128)S(1)}, f32[256,512]{1,0:T(8,128)S(1)}, u32[]{:S(2)}, u32[]{:S(2)}) collective-permute-start(f32[256,512]{1,0:T(8,128)S(1)} %get-tuple-element.32.refs_1_), channel_id=1, source_target_pairs={{0,8},{4,20},{8,0},{12,28},{16,24},{20,4},{24,16},{28,12},{1,9},{5... | collective-permute-start | bytes 1572872 | tf_op jit(solution)/shard_map/ppermute | solution.py:270
  85.8 13.9 %collective-permute-start.24 = (f32[256,512]{1,0:T(8,128)S(1)}, f32[256,512]{1,0:T(8,128)S(1)}, u32[]{:S(2)}, u32[]{:S(2)}) collective-permute-start(f32[256,512]{1,0:T(8,128)S(1)} %collective-permute-done.16.refs_4_), channel_id=1, source_target_pairs={{0,4},{4,0},{8,12},{12,8},{16,20},{20,16},{24,28},{28,24},{1,5},{5... | collective-permute-start | bytes 1572872 | tf_op jit(solution)/shard_map/ppermute | solution.py:270
  86.4 16.0 %collective-permute-start.18 = (f32[256,512]{1,0:T(8,128)S(1)}, f32[256,512]{1,0:T(8,128)S(1)}, u32[]{:S(2)}, u32[]{:S(2)}) collective-permute-start(f32[256,512]{1,0:T(8,128)S(1)} %collective-permute-done.14.refs_2_), channel_id=1, source_target_pairs={{0,8},{4,20},{8,0},{12,28},{16,24},{20,4},{24,16},{28,12},{1,9},{5... | collective-permute-start | bytes 1572872 | tf_op jit(solution)/shard_map/ppermute | solution.py:270
  97.6 10.4 %collective-permute-start.19 = (f32[256,512]{1,0:T(8,128)S(1)}, f32[256,512]{1,0:T(8,128)S(1)}, u32[]{:S(2)}, u32[]{:S(2)}) collective-permute-start(f32[256,512]{1,0:T(8,128)S(1)} %collective-permute-done.15.refs_3_), channel_id=1, source_target_pairs={{0,8},{4,20},{8,0},{12,28},{16,24},{20,4},{24,16},{28,12},{1,9},{5... | collective-permute-start | bytes 1572872 | tf_op jit(solution)/shard_map/ppermute | solution.py:270
  99.1 8.9 %collective-permute-start.22 = (f32[256,512]{1,0:T(8,128)S(1)}, f32[256,512]{1,0:T(8,128)S(1)}, u32[]{:S(2)}, u32[]{:S(2)}) collective-permute-start(f32[256,512]{1,0:T(8,128)S(1)} %collective-permute-done.14.refs_2_), channel_id=1, source_target_pairs={{0,4},{4,0},{8,12},{12,8},{16,20},{20,16},{24,28},{28,24},{1,5},{5... | collective-permute-start | bytes 1572872 | tf_op jit(solution)/shard_map/ppermute | solution.py:270
  99.1 8.9 %collective-permute-start.23 = (f32[256,512]{1,0:T(8,128)S(1)}, f32[256,512]{1,0:T(8,128)S(1)}, u32[]{:S(2)}, u32[]{:S(2)}) collective-permute-start(f32[256,512]{1,0:T(8,128)S(1)} %collective-permute-done.15.refs_3_), channel_id=1, source_target_pairs={{0,4},{4,0},{8,12},{12,8},{16,20},{20,16},{24,28},{28,24},{1,5},{5... | collective-permute-start | bytes 1572872 | tf_op jit(solution)/shard_map/ppermute | solution.py:270
  99.6 8.4 %collective-permute-start.25 = (f32[256,512]{1,0:T(8,128)S(1)}, f32[256,512]{1,0:T(8,128)S(1)}, u32[]{:S(2)}, u32[]{:S(2)}) collective-permute-start(f32[256,512]{1,0:T(8,128)S(1)} %collective-permute-done.17.refs_5_), channel_id=1, source_target_pairs={{0,4},{4,0},{8,12},{12,8},{16,20},{20,16},{24,28},{28,24},{1,5},{5... | collective-permute-start | bytes 1572872 | tf_op jit(solution)/shard_map/ppermute | solution.py:270
  102.4 5.7 %collective-permute-start.26 = (f32[256,512]{1,0:T(8,128)S(1)}, f32[256,512]{1,0:T(8,128)S(1)}, u32[]{:S(2)}, u32[]{:S(2)}) collective-permute-start(f32[256,512]{1,0:T(8,128)S(1)} %collective-permute-done.18.refs_6_), channel_id=1, source_target_pairs={{0,4},{4,0},{8,12},{12,8},{16,20},{20,16},{24,28},{28,24},{1,5},{5... | collective-permute-start | bytes 1572872 | tf_op jit(solution)/shard_map/ppermute | solution.py:270
  108.0 2.2 %collective-permute-start.27 = (f32[256,512]{1,0:T(8,128)S(1)}, f32[256,512]{1,0:T(8,128)}, u32[]{:S(2)}, u32[]{:S(2)}) collective-permute-start(f32[256,512]{1,0:T(8,128)S(1)} %collective-permute-done.19.refs_7_), channel_id=1, source_target_pairs={{0,4},{4,0},{8,12},{12,8},{16,20},{20,16},{24,28},{28,24},{1,5},{5... | collective-permute-start | bytes 1572872 | tf_op jit(solution)/shard_map/ppermute | solution.py:270
  (22 other events, 188.7 us)

commit v4 on v3

--- a/solution.py
+++ b/solution.py
@@ -1,3 +1,5 @@
+import functools
+
 import jax
 import jax.numpy as jnp
 from jax import lax
@@ -62,7 +64,8 @@
     return pre * (clip_factor * jnp.sqrt(block_norm / (pre_norm + graft_eps)))
 
 
-MIB = 1 << 20
+SMALL = 2 << 20
+LARGE = 14 << 20
 F32 = jnp.float32
 HALVES = (0, 1)
 
@@ -95,7 +98,7 @@
         in_specs=[pl.BlockSpec(memory_space=pltpu.SMEM)] * len(scalars) + [whole] * len(operands),
         out_specs=jax.tree.map(lambda _: whole, out_shape),
         out_shape=out_shape,
-        compiler_params=pltpu.CompilerParams(vmem_limit_bytes=vmem),
+        compiler_params=pltpu.CompilerParams(vmem_limit_bytes=vmem or SMALL),
         cost_estimate=pl.CostEstimate(flops=flops, bytes_accessed=moved, transcendentals=0),
         name=name,
         **options,
@@ -118,17 +121,19 @@
     return jax.ShapeDtypeStruct((width // 2, width), F32)
 
 
+def pack_kernel(slots, width, owners_ref, me_ref, grad_ref, *out_refs):
+    place = 0
+    for slot in slots:
+        target = pair_target(slot, me_ref[0] ^ 1)
+        for half in HALVES:
+            out_refs[place][...] = owner_block(owners_ref, grad_ref, half_rows(half, width), width, target)
+            place += 1
+
+
 def pack_call(owners, me, grads, slots, width):
-    def kernel(owners_ref, me_ref, grad_ref, *out_refs):
-        place = 0
-        for slot in slots:
-            target = pair_target(slot, me_ref[0] ^ 1)
-            for half in HALVES:
-                out_refs[place][...] = owner_block(owners_ref, grad_ref, half_rows(half, width), width, target)
-                place += 1
-
     shapes = [half_shape(width)] * (2 * len(slots))
-    return local_call(kernel, "pack", shapes, (grads,), (owners, me), vmem=8 * MIB)
+    kernel = functools.partial(pack_kernel, slots, width)
+    return local_call(kernel, "pack", shapes, (grads,), (owners, me))
 
 
 def add_call(owners, me, grads, slot, half, arrivals, width):
@@ -139,41 +144,41 @@
             total = total + ref[...]
         refs[-1][...] = total
 
-    return local_call(kernel, "add", half_shape(width), (grads, *arrivals), (owners, me), vmem=8 * MIB)
-
-
-def join_call(owners, me, grads, arrivals, width, device_count):
-    block_count = grads.shape[1] // width
-
-    def kernel(owners_ref, me_ref, grad_ref, *refs):
+    return local_call(kernel, "add", half_shape(width), (grads, *arrivals), (owners, me))
+
+
+def join_call(owners, me, total, arrival, norm, block_count, device_count):
+    def kernel(owners_ref, me_ref, total_ref, arrival_ref, *refs):
         block_ref, norm_ref = refs[-2:]
-        squares = jnp.zeros((1, 1), F32)
-        for half in HALVES:
-            rows = half_rows(half, width)
-            total = owner_block(owners_ref, grad_ref, rows, width, me_ref[0])
-            for ref in refs[half:-2:2]:
-                total = total + ref[...]
-            block_ref[rows, :] = total
-            squares = squares + jnp.sum(total * total, keepdims=True).reshape(1, 1)
+        block = total_ref[...] + arrival_ref[...]
+        block_ref[...] = block
         owned = 0
         for index in range(block_count):
             owned = owned + jnp.where(owners_ref[index] == me_ref[0], 1, 0)
-        norm_ref[...] = jnp.broadcast_to(squares * owned.astype(F32), norm_ref.shape)
-
-    shapes = [jax.ShapeDtypeStruct((width, width), F32), jax.ShapeDtypeStruct((device_count, 128), F32)]
-    return local_call(kernel, "join", shapes, (grads, *arrivals), (owners, me), vmem=8 * MIB)
-
-
-def gram_kernel(block_ref, left_ref, right_ref):
-    block = split(block_ref[...])
+        squares = jnp.sum(block * block, keepdims=True).reshape(1, 1) * owned.astype(F32)
+        if norm is not None:
+            squares = squares + refs[0][:1, :1]
+        norm_ref[...] = jnp.broadcast_to(squares, norm_ref.shape)
+
+    shapes = [half_shape(total.shape[1]), jax.ShapeDtypeStruct((device_count, 128), F32)]
+    operands = (total, arrival) if norm is None else (total, arrival, norm)
+    return local_call(kernel, "join", shapes, operands, (owners, me))
+
+
+def whole_block(block_refs):
+    return jnp.concatenate([ref[...] for ref in block_refs], axis=0)
+
+
+def gram_kernel(upper_ref, lower_ref, left_ref, right_ref):
+    block = split(whole_block((upper_ref, lower_ref)))
     left_ref[...] = split_product(block, block, ((1,), (1,)))
     right_ref[...] = split_product(block, block, ((0,), (0,)))
 
 
 def gram_call(block):
-    shape = jax.ShapeDtypeStruct(block.shape, F32)
-    flops = 12 * block.shape[0] ** 3
-    return local_call(gram_kernel, "gram", [shape, shape], (block,), flops=flops, vmem=16 * MIB)
+    width = block[0].shape[1]
+    shape = jax.ShapeDtypeStruct((width, width), F32)
+    return local_call(gram_kernel, "gram", [shape, shape], block, flops=12 * width**3, vmem=LARGE)
 
 
 def root_of(previous, gram, gram_scale):
@@ -194,15 +199,15 @@
 
 
 def update_call(block, left_gram, right_gram, left_prev, right_prev, norms, entry_count):
-    width = block.shape[0]
-
-    def kernel(block_ref, left_gram_ref, right_gram_ref, left_ref, right_ref, norm_ref, *out_refs):
+    width = block[0].shape[1]
+
+    def kernel(upper_ref, lower_ref, left_gram_ref, right_gram_ref, left_ref, right_ref, norm_ref, *out_refs):
         squares = jnp.sum(norm_ref[:, :1], axis=0, keepdims=True)
         clip_factor = jnp.minimum(1.0, clip_level / jnp.sqrt(squares / entry_count))
         gram_scale = clip_factor * clip_factor / width
         left_root = root_of(left_ref[...], left_gram_ref[...], gram_scale)
         right_root = root_of(right_ref[...], right_gram_ref[...], gram_scale)
-        block = block_ref[...]
+        block = whole_block((upper_ref, lower_ref))
         halfway = split_product(split(left_root), split(block))
         pre = split_product(split(halfway), split(right_root)) * clip_factor
         block_norm = jnp.sum(block * block, keepdims=True).reshape(1, 1) * (clip_factor * clip_factor)
@@ -211,46 +216,53 @@
         for half in HALVES:
             out_refs[half][...] = update[half * (width // 2) : (half + 1) * (width // 2)]
 
-    operands = (block, left_gram, right_gram, left_prev, right_prev, norms)
+    operands = (*block, left_gram, right_gram, left_prev, right_prev, norms)
     shapes = [half_shape(width)] * 2
-    return local_call(kernel, "update", shapes, operands, flops=48 * width**3, vmem=24 * MIB)
-
-
-def assemble_call(owners, me, slots, block_count):
+    return local_call(kernel, "update", shapes, operands, flops=48 * width**3, vmem=LARGE)
+
+
+def assemble_call(owners, me, places, slots, block_count, started):
     width = slots[0].shape[1]
 
     def kernel(owners_ref, me_ref, *refs):
         out_ref, sem = refs[-2:]
-
-        def spot(index, half):
-            return out_ref.at[half_rows(half, width), pl.ds(index * width, width)]
-
-        for index in range(block_count):
-            for place in range(8):
-                target = pair_target(place & 3, me_ref[0] ^ (place >> 2))
-
-                @pl.when(owners_ref[index] == target)
-                def _():
-                    for half in HALVES:
-                        source = refs[2 * place + half]
-                        pltpu.make_async_copy(source, spot(index, half), sem.at[index, half]).start()
-
-        for index in range(block_count):
-            for half in HALVES:
-                pltpu.make_async_copy(refs[half], spot(index, half), sem.at[index, half]).wait()
-
+        copies = []
+        for number, (place, half) in enumerate(places):
+            target = pair_target(place & 3, me_ref[0] ^ (place >> 2))
+            owned, column = 0, 0
+            for index in range(block_count):
+                matches = owners_ref[index] == target
+                owned = owned + jnp.where(matches, 1, 0)
+                column = column + jnp.where(matches, index * width, 0)
+            columns = pl.ds(pl.multiple_of(column, width), width)
+            spot = out_ref.at[half_rows(half, width), columns]
+            copies.append((owned, pltpu.make_async_copy(refs[number], spot, sem.at[number])))
+        for owned, copy in copies:
+            pl.when(owned == 1)(copy.start)
+        for owned, copy in copies:
+            pl.when(owned == 1)(copy.wait)
+
+    in_specs = [pl.BlockSpec(memory_space=pltpu.SMEM)] * 2
+    in_specs += [pl.BlockSpec(memory_space=pltpu.VMEM)] * len(slots)
+    operands = [owners, me, *slots]
+    aliases = {}
+    if started is not None:
+        aliases = {len(operands): 0}
+        in_specs.append(pl.BlockSpec(memory_space=pltpu.HBM))
+        operands.append(started)
     return pl.pallas_call(
         kernel,
-        in_specs=[pl.BlockSpec(memory_space=pltpu.SMEM)] * 2
-        + [pl.BlockSpec(memory_space=pltpu.VMEM)] * len(slots),
-        out_specs=pl.BlockSpec(memory_space=pl.ANY),
+        in_specs=in_specs,
+        out_specs=pl.BlockSpec(memory_space=pltpu.HBM),
         out_shape=jax.ShapeDtypeStruct((width, block_count * width), F32),
-        scratch_shapes=[pltpu.SemaphoreType.DMA((block_count, 2))],
+        scratch_shapes=[pltpu.SemaphoreType.DMA((len(slots),))],
+        input_output_aliases=aliases,
+        compiler_params=pltpu.CompilerParams(vmem_limit_bytes=SMALL),
         cost_estimate=pl.CostEstimate(
-            flops=0, bytes_accessed=8 * width * width * block_count, transcendentals=0
+            flops=0, bytes_accessed=8 * slots[0].size * len(slots), transcendentals=0
         ),
         name="assemble",
-    )(owners, me, *slots)
+    )(*operands)
 
 
 def paired_body(replica_grads, owners, left_stats, right_stats):
@@ -260,7 +272,6 @@
     me = lax.axis_index("dp").astype(jnp.int32).reshape(1)
     device_count = 8 * lax.axis_size("mp")
     entry_count = width * block_count * width * lax.axis_size("mp")
-    grads = replica_grads[0]
 
     first_pairs = [(i, i ^ (2 + 2 * (i % 2))) for i in range(8)]
     second_pairs = [(i, i ^ (4 - 2 * (i % 2))) for i in range(8)]
@@ -272,11 +283,11 @@
     def own_plus(slot, half, *arrivals):
         return add_call(owner_row, me, grads, slot, half, arrivals, width)
 
-    packed = {}
-    for slots in ((3, 2), (1, 0)):
-        pieces = pack_call(owner_row, me, grads, slots, width)
-        packed.update(zip([(slot, half) for slot in slots for half in HALVES], pieces))
-    from_core = {key: over(core_pairs, value) for key, value in packed.items()}
+    grads = replica_grads[0]
+    pieces = pack_call(owner_row, me, grads, (3, 2), width)
+    pieces += pack_call(owner_row, me, grads, (1, 0), width)
+    keys = [(slot, half) for slot in (3, 2, 1, 0) for half in HALVES]
+    from_core = {key: over(core_pairs, value) for key, value in zip(keys, pieces)}
     from_first = {}
     for slot in (3, 2):
         for half in HALVES:
@@ -284,8 +295,11 @@
     from_second = [
         over(second_pairs, own_plus(1, half, from_core[1, half], from_first[3, half])) for half in HALVES
     ]
-    arrivals = [from_core[0, half] for half in HALVES] + [from_first[2, half] for half in HALVES]
-    block, norm = join_call(owner_row, me, grads, arrivals + from_second, width, device_count)
+    norm, block = None, []
+    for half in HALVES:
+        total = own_plus(0, half, from_core[0, half], from_first[2, half])
+        joined, norm = join_call(owner_row, me, total, from_second[half], norm, block_count, device_count)
+        block.append(joined)
     norms = lax.all_to_all(norm, ("dp", "mp"), split_axis=0, concat_axis=0, tiled=True)
     left_gram, right_gram = gram_call(block)
     update = update_call(block, left_gram, right_gram, left_stats[0], right_stats[0], norms, entry_count)
@@ -293,9 +307,16 @@
     near = [over(second_pairs, value) for value in update]
     far = [over(first_pairs, value) for value in update]
     relayed = [over(first_pairs, value) for value in near]
-    held = list(update) + near + far + relayed
-    slots = held + [over(core_pairs, value) for value in held]
-    return assemble_call(owner_row, me, slots, block_count)
+    held = dict(zip([(place, half) for place in range(4) for half in HALVES], [*update, *near, *far, *relayed]))
+    held.update({(place + 4, half): over(core_pairs, value) for (place, half), value in held.items()})
+    result = None
+    for places in (
+        [key for key in held if key[0] & 3 != 3],
+        [(3, 0), (7, 0)],
+        [(3, 1), (7, 1)],
+    ):
+        result = assemble_call(owner_row, me, places, [held[key] for key in places], block_count, result)
+    return result
 
 
 def solution(mesh):

time: 117 us -> 116 us (level)
  local copies, waits for them, and re-layouts: 10.3 us -> 6.96 us
  waiting for transfers between devices: 58 us -> 60.5 us
  Pallas kernels: 23 us -> 24.4 us
    unnamed x50 -> x18, local copies, waits for them, and re-layouts: 10.3 us -> 6.96 us
    ppermute x28, waiting for transfers between devices: 54.7 us -> 57.2 us  [over(): return lax.ppermute(value, 'dp', pairs)]
    pallas_call x11 -> x14, Pallas kernels: 16.9 us -> 18.6 us  [local_call(): pl.pallas_call(kernel, in_specs=[pl.BlockSpec(memory_space=pltpu.SMEM)] *...]
    pallas_call x1 -> x3, Pallas kernels: 6.16 us -> 5.78 us  [assemble_call(): pl.pallas_call(kernel, in_specs=in_specs, out_specs=pl.BlockSpec(memory_s...]
  transfers between devices with their start and end apart: 29 -> 29, of which waited for: 11 -> 10; matrix products, arithmetic and copies ran while one was open for 0% -> 0% of each run, Pallas kernels for 5% -> 11%
where the time goes in v4:
time: 116 us
  waiting for transfers between devices  60.5 us (52%)
  Pallas kernels  24.4 us (21%)
  starting transfers between devices  23.6 us (20%)
  local copies, waits for them, and re-layouts  6.96 us (6%)
    ppermute x28, waiting for transfers between devices, over(): return lax.ppermute(value, 'dp', pairs)  57.2 us
    pallas_call x14, Pallas kernels, local_call(): pl.pallas_call(kernel, in_specs=[pl.BlockSpec(memory_space=pltpu.SMEM)] *...  18.6 us
    ppermute x28, starting transfers between devices, over(): return lax.ppermute(value, 'dp', pairs)  17.5 us
    unnamed x18, local copies, waits for them, and re-layouts  6.96 us
    all_to_all x1, starting transfers between devices, paired_body(): lax.all_to_all(norm, ('dp', 'mp'), split_axis=0, concat_axis=0, tiled=True)  6.1 us
    pallas_call x3, Pallas kernels, assemble_call(): pl.pallas_call(kernel, in_specs=in_specs, out_specs=pl.BlockSpec(memory_s...  5.78 us
    all_to_all x1, waiting for transfers between devices, paired_body(): lax.all_to_all(norm, ('dp', 'mp'), split_axis=0, concat_axis=0, tiled=True)  3.37 us
  transfers between devices with their start and end apart: 29, of which 10 were waited for; matrix products, arithmetic and copies ran while one was open for 0% of the time, Pallas kernels for 11%

profile of v4, /device:TPU:0, one launch (start us, length us, event | category | flops | bytes accessed | tf_op | source)
XLA Modules:
  0.0 115.8 jit_solution(8137227516275495413)
XLA Ops:
  0.0 1.9 %copy-done = bf16[1,512,3072]{2,1,0:T(8,128)(2,1)S(1)} copy-done((bf16[1,512,3072]{2,1,0:T(8,128)(2,1)S(1)}, bf16[1,512,3072]{2,1,0:T(8,128)(2,1)}, u32[]{:S(2)}) %copy-start) | copy-done | bytes 3145752
  2.5 0.7 pack.3
  4.3 0.7 pack.2
  6.1 2.7 %collective-permute-start.5 = (f32[256,512]{1,0:T(8,128)S(1)}, f32[256,512]{1,0:T(8,128)S(1)}, u32[]{:S(2)}, u32[]{:S(2)}) collective-permute-start(f32[256,512]{1,0:T(8,128)S(1)} %add.10), channel_id=1, source_target_pairs={{0,8},{4,20},{8,0},{12,28},{16,24},{20,4},{24,16},{28,12},{1,9},{5... | collective-permute-start | bytes 1572872 | tf_op jit(solution)/shard_map/ppermute | solution.py:281
  9.6 1.6 %collective-permute-start.12 = (f32[256,512]{1,0:T(8,128)S(1)}, f32[256,512]{1,0:T(8,128)S(1)}, u32[]{:S(2)}, u32[]{:S(2)}) collective-permute-start(f32[256,512]{1,0:T(8,128)S(1)} %add.14), channel_id=1, source_target_pairs={{0,8},{4,20},{8,0},{12,28},{16,24},{20,4},{24,16},{28,12},{1,9},{5... | collective-permute-start | bytes 1572872 | tf_op jit(solution)/shard_map/ppermute | solution.py:281
  12.9 3.1 %collective-permute-done.5.refs_1_ = f32[256,512]{1,0:T(8,128)S(1)} collective-permute-done((f32[256,512]{1,0:T(8,128)S(1)}, f32[256,512]{1,0:T(8,128)S(1)}, u32[]{:S(2)}, u32[]{:S(2)}) %collective-permute-start.5) | collective-permute-done | bytes 524320 | tf_op jit(solution)/shard_map/ppermute | solution.py:281
  16.0 2.0 %collective-permute-start.2 = (f32[256,512]{1,0:T(8,128)S(1)}, f32[256,512]{1,0:T(8,128)S(1)}, u32[]{:S(2)}, u32[]{:S(2)}) collective-permute-start(f32[256,512]{1,0:T(8,128)S(1)} %add.8), channel_id=1, source_target_pairs={{0,8},{4,20},{8,0},{12,28},{16,24},{20,4},{24,16},{28,12},{1,9},{5... | collective-permute-start | bytes 1572872 | tf_op jit(solution)/shard_map/ppermute | solution.py:281
  18.7 2.9 %collective-permute-done.12.refs_1_ = f32[256,512]{1,0:T(8,128)S(1)} collective-permute-done((f32[256,512]{1,0:T(8,128)S(1)}, f32[256,512]{1,0:T(8,128)S(1)}, u32[]{:S(2)}, u32[]{:S(2)}) %collective-permute-start.12) | collective-permute-done | bytes 524320 | tf_op jit(solution)/shard_map/ppermute | solution.py:281
  21.6 2.0 %collective-permute-start.6 = (f32[256,512]{1,0:T(8,128)S(1)}, f32[256,512]{1,0:T(8,128)S(1)}, u32[]{:S(2)}, u32[]{:S(2)}) collective-permute-start(f32[256,512]{1,0:T(8,128)S(1)} %add.11), channel_id=1, source_target_pairs={{0,16},{4,12},{8,24},{12,4},{16,0},{20,28},{24,8},{28,20},{1,17},{... | collective-permute-start | bytes 1572872 | tf_op jit(solution)/shard_map/ppermute | solution.py:281
  24.4 6.0 %collective-permute-done.2.refs_1_ = f32[256,512]{1,0:T(8,128)S(1)} collective-permute-done((f32[256,512]{1,0:T(8,128)S(1)}, f32[256,512]{1,0:T(8,128)S(1)}, u32[]{:S(2)}, u32[]{:S(2)}) %collective-permute-start.2) | collective-permute-done | bytes 524320 | tf_op jit(solution)/shard_map/ppermute | solution.py:281
  31.0 10.6 %collective-permute-done.9.refs_1_ = f32[256,512]{1,0:T(8,128)S(1)} collective-permute-done((f32[256,512]{1,0:T(8,128)S(1)}, f32[256,512]{1,0:T(8,128)S(1)}, u32[]{:S(2)}, u32[]{:S(2)}) %collective-permute-start.9) | collective-permute-done | bytes 524320 | tf_op jit(solution)/shard_map/ppermute | solution.py:281
  42.2 0.9 join.2
  43.1 0.7 collective-permute-done.13.arrival_ref
  43.8 1.5 %join.3 = (f32[256,512]{1,0:T(8,128)S(1)}, f32[32,128]{1,0:T(8,128)}) custom-call(s32[6]{0:T(128)S(1)} %bitcast.30, s32[1]{0:T(128)} %bitcast.1.me_ref, f32[256,512]{1,0:T(8,128)S(1)} %add.13.total_ref, f32[256,512]{1,0:T(8,128)S(1)} %collective-permute-done.13.arrival_ref, f32[32,128]{1,0:T(8,128)S(1)} %get-tuple-element.30.refs_0_), custom_call_target="tpu_custom_call" | custom-call | bytes 1605632 | tf_op jit(solution)/shard_map/join/pallas_call | solution.py:96
  45.3 6.1 %all-to-all-start = ((f32[32,1,128]{2,1,0:T(1,128)}), f32[32,1,128]{2,1,0:T(1,128)S(1)}, u32[]{:S(2)}, u32[]{:S(2)}) async-start(f32[32,1,128]{2,1,0:T(1,128)} %bitcast.6), calls=%async_computation | async-start | bytes 32768 | tf_op jit(solution)/shard_map/all_to_all | solution.py:303
  51.4 1.8 %gram.1 = (f32[512,512]{1,0:T(8,128)S(1)}, f32[512,512]{1,0:T(8,128)S(1)}) custom-call(f32[256,512]{1,0:T(8,128)S(1)} %get-tuple-element.25.upper_ref, f32[256,512]{1,0:T(8,128)S(1)} %get-tuple-element.31.lower_ref), custom_call_target="tpu_custom_call" | custom-call | flops 1610612736 | bytes 3145728 | tf_op jit(solution)/shard_map/gram/pallas_call | solution.py:96
  53.2 1.0 copy-done.5
  54.2 1.0 copy-done.7
  55.2 3.4 %all-to-all-done = f32[32,1,128]{2,1,0:T(1,128)S(1)} async-done(((f32[32,1,128]{2,1,0:T(1,128)}), f32[32,1,128]{2,1,0:T(1,128)S(1)}, u32[]{:S(2)}, u32[]{:S(2)}) %all-to-all-start) | async-done | bytes 16416 | tf_op jit(solution)/shard_map/all_to_all | solution.py:303
  58.6 1.2 %copy-done.6 = f32[512,512]{1,0:T(8,128)S(1)} copy-done((f32[512,512]{1,0:T(8,128)S(1)}, f32[512,512]{1,0:T(8,128)}, u32[]{:S(2)}) %copy-start.6) | copy-done | bytes 1048600
  59.8 1.2 %copy-done.8 = f32[512,512]{1,0:T(8,128)S(1)} copy-done((f32[512,512]{1,0:T(8,128)S(1)}, f32[512,512]{1,0:T(8,128)}, u32[]{:S(2)}) %copy-start.8) | copy-done | bytes 1048600
  61.0 8.3 %update.1 = (f32[256,512]{1,0:T(8,128)S(1)}, f32[256,512]{1,0:T(8,128)S(1)}) custom-call(f32[256,512]{1,0:T(8,128)S(1)} %get-tuple-element.25.upper_ref, f32[256,512]{1,0:T(8,128)S(1)} %get-tuple-element.31.lower_ref, f32[512,512]{1,0:T(8,128)S(1)} %copy-done.6, f32[512,512]{1,0:T(8,128)S(1)} %copy-done.8, f32[512,512]{1,0:T(8,128)S(1)} %bitcast.35, ...), custom_call_target="tpu_custom_call" | custom-call | flops 6442450944 | bytes 6307840 | tf_op jit(solution)/shard_map/update/pallas_call | solution.py:96
  70.0 1.4 %collective-permute-start.14 = (f32[256,512]{1,0:T(8,128)S(1)}, f32[256,512]{1,0:T(8,128)S(1)}, u32[]{:S(2)}, u32[]{:S(2)}) collective-permute-start(f32[256,512]{1,0:T(8,128)S(1)} %get-tuple-element.35.refs_1_), channel_id=1, source_target_pairs={{0,16},{4,12},{8,24},{12,4},{16,0},{20,28},{24,8},{28,20},{1,17},{... | collective-permute-start | bytes 1572872 | tf_op jit(solution)/shard_map/ppermute | solution.py:281
  72.0 1.4 %collective-permute-start.21 = (f32[256,512]{1,0:T(8,128)S(1)}, f32[256,512]{1,0:T(8,128)S(1)}, u32[]{:S(2)}, u32[]{:S(2)}) collective-permute-start(f32[256,512]{1,0:T(8,128)S(1)} %get-tuple-element.35.refs_1_), channel_id=1, source_target_pairs={{0,8},{4,20},{8,0},{12,28},{16,24},{20,4},{24,16},{28,12},{1,9},{5... | collective-permute-start | bytes 1572872 | tf_op jit(solution)/shard_map/ppermute | solution.py:281
  73.4 10.5 %collective-permute-done.17.refs_2_ = f32[256,512]{1,0:T(8,128)S(1)} collective-permute-done((f32[256,512]{1,0:T(8,128)S(1)}, f32[256,512]{1,0:T(8,128)S(1)}, u32[]{:S(2)}, u32[]{:S(2)}) %collective-permute-start.17) | collective-permute-done | bytes 524320 | tf_op jit(solution)/shard_map/ppermute | solution.py:281
  83.9 11.2 %collective-permute-done.14.refs_3_ = f32[256,512]{1,0:T(8,128)S(1)} collective-permute-done((f32[256,512]{1,0:T(8,128)S(1)}, f32[256,512]{1,0:T(8,128)S(1)}, u32[]{:S(2)}, u32[]{:S(2)}) %collective-permute-start.14) | collective-permute-done | bytes 524320 | tf_op jit(solution)/shard_map/ppermute | solution.py:281
  95.7 1.4 %collective-permute-start.15 = (f32[256,512]{1,0:T(8,128)S(1)}, f32[256,512]{1,0:T(8,128)S(1)}, u32[]{:S(2)}, u32[]{:S(2)}) collective-permute-start(f32[256,512]{1,0:T(8,128)S(1)} %collective-permute-done.14.refs_3_), channel_id=1, source_target_pairs={{0,8},{4,20},{8,0},{12,28},{16,24},{20,4},{24,16},{28,12},{1,9},{5... | collective-permute-start | bytes 1572872 | tf_op jit(solution)/shard_map/ppermute | solution.py:281
  97.8 6.6 %collective-permute-done.18.refs_0_ = f32[256,512]{1,0:T(8,128)S(1)} collective-permute-done((f32[256,512]{1,0:T(8,128)S(1)}, f32[256,512]{1,0:T(8,128)S(1)}, u32[]{:S(2)}, u32[]{:S(2)}) %collective-permute-start.18) | collective-permute-done | bytes 524320 | tf_op jit(solution)/shard_map/ppermute | solution.py:281
  104.3 5.6 %collective-permute-done.15.refs_0_ = f32[256,512]{1,0:T(8,128)S(1)} collective-permute-done((f32[256,512]{1,0:T(8,128)S(1)}, f32[256,512]{1,0:T(8,128)S(1)}, u32[]{:S(2)}, u32[]{:S(2)}) %collective-permute-start.15) | collective-permute-done | bytes 524320 | tf_op jit(solution)/shard_map/ppermute | solution.py:281
  110.0 2.7 %assemble.3.refs_2_ = f32[512,3072]{1,0:T(8,128)} custom-call(s32[6]{0:T(128)S(1)} %bitcast.31, s32[1]{0:T(128)} %bitcast.1.me_ref, f32[256,512]{1,0:T(8,128)S(1)} %get-tuple-element.36.refs_0_, f32[256,512]{1,0:T(8,128)S(1)} %get-tuple-element.35.refs_1_, f32[256,512]{1,0:T(8,128)S(1)} %collective-permute-done.17.refs_2_, ...), custom_call_target="tpu_custom_call" | custom-call | bytes 12582912 | tf_op jit(solution)/shard_map/assemble/pallas_call | solution.py:253
  112.7 1.5 %assemble.4.refs_2_ = f32[512,3072]{1,0:T(8,128)} custom-call(s32[6]{0:T(128)S(1)} %bitcast.32, s32[1]{0:T(128)} %bitcast.1.me_ref, f32[256,512]{1,0:T(8,128)S(1)} %collective-permute-done.18.refs_0_, f32[256,512]{1,0:T(8,128)S(1)} %collective-permute-done.19.refs_1_, f32[512,3072]{1,0:T(8,128)} %assemble.3.refs_2_), custom_call_target="tpu_custom_call", output_to_operand_aliasing={{}: (4, {})} | custom-call | bytes 2097152 | tf_op jit(solution)/shard_map/assemble/pallas_call | solution.py:253
  114.3 1.5 %assemble.5 = f32[512,3072]{1,0:T(8,128)} custom-call(s32[6]{0:T(128)S(1)} %bitcast.33, s32[1]{0:T(128)} %bitcast.1.me_ref, f32[256,512]{1,0:T(8,128)S(1)} %collective-permute-done.15.refs_0_, f32[256,512]{1,0:T(8,128)S(1)} %collective-permute-done.16.refs_1_, f32[512,3072]{1,0:T(8,128)} %assemble.4.refs_2_), custom_call_target="tpu_custom_call", output_to_operand_aliasing={{}: (4, {})} | custom-call | bytes 2097152 | tf_op jit(solution)/shard_map/assemble/pallas_call | solution.py:253
  (61 shorter events, 10.4 us)
Async XLA Ops:
  3.2 2.3 %collective-permute-start.4 = (f32[256,512]{1,0:T(8,128)S(1)}, f32[256,512]{1,0:T(8,128)S(1)}, u32[]{:S(2)}, u32[]{:S(2)}) collective-permute-start(f32[256,512]{1,0:T(8,128)S(1)} %get-tuple-element.24), channel_id=1, source_target_pairs={{0,4},{4,0},{8,12},{12,8},{16,20},{20,16},{24,28},{28,24},{1,5},{5... | collective-permute-start | bytes 1572872 | tf_op jit(solution)/shard_map/ppermute | solution.py:281
  3.8 5.1 %collective-permute-start.11 = (f32[256,512]{1,0:T(8,128)S(1)}, f32[256,512]{1,0:T(8,128)S(1)}, u32[]{:S(2)}, u32[]{:S(2)}) collective-permute-start(f32[256,512]{1,0:T(8,128)S(1)} %get-tuple-element.29), channel_id=1, source_target_pairs={{0,4},{4,0},{8,12},{12,8},{16,20},{20,16},{24,28},{28,24},{1,5},{5... | collective-permute-start | bytes 1572872 | tf_op jit(solution)/shard_map/ppermute | solution.py:281
  3.8 5.7 %collective-permute-start.1 = (f32[256,512]{1,0:T(8,128)S(1)}, f32[256,512]{1,0:T(8,128)S(1)}, u32[]{:S(2)}, u32[]{:S(2)}) collective-permute-start(f32[256,512]{1,0:T(8,128)S(1)} %get-tuple-element.22), channel_id=1, source_target_pairs={{0,4},{4,0},{8,12},{12,8},{16,20},{20,16},{24,28},{28,24},{1,5},{5... | collective-permute-start | bytes 1572872 | tf_op jit(solution)/shard_map/ppermute | solution.py:281
  4.3 6.9 %collective-permute-start.8 = (f32[256,512]{1,0:T(8,128)S(1)}, f32[256,512]{1,0:T(8,128)S(1)}, u32[]{:S(2)}, u32[]{:S(2)}) collective-permute-start(f32[256,512]{1,0:T(8,128)S(1)} %get-tuple-element.27), channel_id=1, source_target_pairs={{0,4},{4,0},{8,12},{12,8},{16,20},{20,16},{24,28},{28,24},{1,5},{5... | collective-permute-start | bytes 1572872 | tf_op jit(solution)/shard_map/ppermute | solution.py:281
  5.0 7.4 %collective-permute-start.3 = (f32[256,512]{1,0:T(8,128)S(1)}, f32[256,512]{1,0:T(8,128)S(1)}, u32[]{:S(2)}, u32[]{:S(2)}) collective-permute-start(f32[256,512]{1,0:T(8,128)S(1)} %get-tuple-element.23), channel_id=1, source_target_pairs={{0,4},{4,0},{8,12},{12,8},{16,20},{20,16},{24,28},{28,24},{1,5},{5... | collective-permute-start | bytes 1572872 | tf_op jit(solution)/shard_map/ppermute | solution.py:281
  6.1 9.8 %collective-permute-start.5 = (f32[256,512]{1,0:T(8,128)S(1)}, f32[256,512]{1,0:T(8,128)S(1)}, u32[]{:S(2)}, u32[]{:S(2)}) collective-permute-start(f32[256,512]{1,0:T(8,128)S(1)} %add.10), channel_id=1, source_target_pairs={{0,8},{4,20},{8,0},{12,28},{16,24},{20,4},{24,16},{28,12},{1,9},{5... | collective-permute-start | bytes 1572872 | tf_op jit(solution)/shard_map/ppermute | solution.py:281
  8.8 9.8 %collective-permute-start.10 = (f32[256,512]{1,0:T(8,128)S(1)}, f32[256,512]{1,0:T(8,128)S(1)}, u32[]{:S(2)}, u32[]{:S(2)}) collective-permute-start(f32[256,512]{1,0:T(8,128)S(1)} %get-tuple-element.28), channel_id=1, source_target_pairs={{0,4},{4,0},{8,12},{12,8},{16,20},{20,16},{24,28},{28,24},{1,5},{5... | collective-permute-start | bytes 1572872 | tf_op jit(solution)/shard_map/ppermute | solution.py:281
  9.6 12.0 %collective-permute-start.12 = (f32[256,512]{1,0:T(8,128)S(1)}, f32[256,512]{1,0:T(8,128)S(1)}, u32[]{:S(2)}, u32[]{:S(2)}) collective-permute-start(f32[256,512]{1,0:T(8,128)S(1)} %add.14), channel_id=1, source_target_pairs={{0,8},{4,20},{8,0},{12,28},{16,24},{20,4},{24,16},{28,12},{1,9},{5... | collective-permute-start | bytes 1572872 | tf_op jit(solution)/shard_map/ppermute | solution.py:281
  11.1 13.1 %collective-permute-start = (f32[256,512]{1,0:T(8,128)S(1)}, f32[256,512]{1,0:T(8,128)S(1)}, u32[]{:S(2)}, u32[]{:S(2)}) collective-permute-start(f32[256,512]{1,0:T(8,128)S(1)} %get-tuple-element.21), channel_id=1, source_target_pairs={{0,4},{4,0},{8,12},{12,8},{16,20},{20,16},{24,28},{28,24},{1,5},{5... | collective-permute-start | bytes 1572872 | tf_op jit(solution)/shard_map/ppermute | solution.py:281
  12.5 18.5 %collective-permute-start.7 = (f32[256,512]{1,0:T(8,128)S(1)}, f32[256,512]{1,0:T(8,128)S(1)}, u32[]{:S(2)}, u32[]{:S(2)}) collective-permute-start(f32[256,512]{1,0:T(8,128)S(1)} %get-tuple-element.26), channel_id=1, source_target_pairs={{0,4},{4,0},{8,12},{12,8},{16,20},{20,16},{24,28},{28,24},{1,5},{5... | collective-permute-start | bytes 1572872 | tf_op jit(solution)/shard_map/ppermute | solution.py:281
  16.0 14.4 %collective-permute-start.2 = (f32[256,512]{1,0:T(8,128)S(1)}, f32[256,512]{1,0:T(8,128)S(1)}, u32[]{:S(2)}, u32[]{:S(2)}) collective-permute-start(f32[256,512]{1,0:T(8,128)S(1)} %add.8), channel_id=1, source_target_pairs={{0,8},{4,20},{8,0},{12,28},{16,24},{20,4},{24,16},{28,12},{1,9},{5... | collective-permute-start | bytes 1572872 | tf_op jit(solution)/shard_map/ppermute | solution.py:281
  18.6 22.9 %collective-permute-start.9 = (f32[256,512]{1,0:T(8,128)S(1)}, f32[256,512]{1,0:T(8,128)S(1)}, u32[]{:S(2)}, u32[]{:S(2)}) collective-permute-start(f32[256,512]{1,0:T(8,128)S(1)} %add.12), channel_id=1, source_target_pairs={{0,8},{4,20},{8,0},{12,28},{16,24},{20,4},{24,16},{28,12},{1,9},{5... | collective-permute-start | bytes 1572872 | tf_op jit(solution)/shard_map/ppermute | solution.py:281
  21.6 20.6 %collective-permute-start.6 = (f32[256,512]{1,0:T(8,128)S(1)}, f32[256,512]{1,0:T(8,128)S(1)}, u32[]{:S(2)}, u32[]{:S(2)}) collective-permute-start(f32[256,512]{1,0:T(8,128)S(1)} %add.11), channel_id=1, source_target_pairs={{0,16},{4,12},{8,24},{12,4},{16,0},{20,28},{24,8},{28,20},{1,17},{... | collective-permute-start | bytes 1572872 | tf_op jit(solution)/shard_map/ppermute | solution.py:281
  24.3 19.5 %collective-permute-start.13 = (f32[256,512]{1,0:T(8,128)S(1)}, f32[256,512]{1,0:T(8,128)S(1)}, u32[]{:S(2)}, u32[]{:S(2)}) collective-permute-start(f32[256,512]{1,0:T(8,128)S(1)} %add.15), channel_id=1, source_target_pairs={{0,16},{4,12},{8,24},{12,4},{16,0},{20,28},{24,8},{28,20},{1,17},{... | collective-permute-start | bytes 1572872 | tf_op jit(solution)/shard_map/ppermute | solution.py:281
  31.0 27.6 %copy-start.3 = (f32[1,512,512]{2,1,0:T(8,128)S(1)}, f32[1,512,512]{2,1,0:T(8,128)}, u32[]{:S(2)}) copy-start(f32[1,512,512]{2,1,0:T(8,128)} %param.6) | copy-start | bytes 3145732
  31.0 27.6 %copy-start.4 = (f32[1,512,512]{2,1,0:T(8,128)S(1)}, f32[1,512,512]{2,1,0:T(8,128)}, u32[]{:S(2)}) copy-start(f32[1,512,512]{2,1,0:T(8,128)} %param.7) | copy-start | bytes 3145732
  45.3 13.3 %all-to-all-start = ((f32[32,1,128]{2,1,0:T(1,128)}), f32[32,1,128]{2,1,0:T(1,128)S(1)}, u32[]{:S(2)}, u32[]{:S(2)}) async-start(f32[32,1,128]{2,1,0:T(1,128)} %bitcast.6), calls=%async_computation | async-start | bytes 32768 | tf_op jit(solution)/shard_map/all_to_all | solution.py:303
  61.0 49.0 %copy-start.2 = (s32[1,6]{1,0:T(1,128)S(1)}, s32[1,6]{1,0:T(1,128)}, u32[]{:S(2)}) copy-start(s32[1,6]{1,0:T(1,128)} %param.5) | copy-start | bytes 76
  69.3 14.6 %collective-permute-start.17 = (f32[256,512]{1,0:T(8,128)S(1)}, f32[256,512]{1,0:T(8,128)S(1)}, u32[]{:S(2)}, u32[]{:S(2)}) collective-permute-start(f32[256,512]{1,0:T(8,128)S(1)} %get-tuple-element.36.refs_0_), channel_id=1, source_target_pairs={{0,16},{4,12},{8,24},{12,4},{16,0},{20,28},{24,8},{28,20},{1,17},{... | collective-permute-start | bytes 1572872 | tf_op jit(solution)/shard_map/ppermute | solution.py:281
  70.0 25.2 %collective-permute-start.14 = (f32[256,512]{1,0:T(8,128)S(1)}, f32[256,512]{1,0:T(8,128)S(1)}, u32[]{:S(2)}, u32[]{:S(2)}) collective-permute-start(f32[256,512]{1,0:T(8,128)S(1)} %get-tuple-element.35.refs_1_), channel_id=1, source_target_pairs={{0,16},{4,12},{8,24},{12,4},{16,0},{20,28},{24,8},{28,20},{1,17},{... | collective-permute-start | bytes 1572872 | tf_op jit(solution)/shard_map/ppermute | solution.py:281
  71.4 23.8 %collective-permute-start.20 = (f32[256,512]{1,0:T(8,128)S(1)}, f32[256,512]{1,0:T(8,128)S(1)}, u32[]{:S(2)}, u32[]{:S(2)}) collective-permute-start(f32[256,512]{1,0:T(8,128)S(1)} %get-tuple-element.36.refs_0_), channel_id=1, source_target_pairs={{0,8},{4,20},{8,0},{12,28},{16,24},{20,4},{24,16},{28,12},{1,9},{5... | collective-permute-start | bytes 1572872 | tf_op jit(solution)/shard_map/ppermute | solution.py:281
  72.0 23.8 %collective-permute-start.21 = (f32[256,512]{1,0:T(8,128)S(1)}, f32[256,512]{1,0:T(8,128)S(1)}, u32[]{:S(2)}, u32[]{:S(2)}) collective-permute-start(f32[256,512]{1,0:T(8,128)S(1)} %get-tuple-element.35.refs_1_), channel_id=1, source_target_pairs={{0,8},{4,20},{8,0},{12,28},{16,24},{20,4},{24,16},{28,12},{1,9},{5... | collective-permute-start | bytes 1572872 | tf_op jit(solution)/shard_map/ppermute | solution.py:281
  73.4 23.8 %collective-permute-start.22 = (f32[256,512]{1,0:T(8,128)S(1)}, f32[256,512]{1,0:T(8,128)S(1)}, u32[]{:S(2)}, u32[]{:S(2)}) collective-permute-start(f32[256,512]{1,0:T(8,128)S(1)} %get-tuple-element.36.refs_0_), channel_id=1, source_target_pairs={{0,4},{4,0},{8,12},{12,8},{16,20},{20,16},{24,28},{28,24},{1,5},{5... | collective-permute-start | bytes 1572872 | tf_op jit(solution)/shard_map/ppermute | solution.py:281
  83.9 13.3 %collective-permute-start.23 = (f32[256,512]{1,0:T(8,128)S(1)}, f32[256,512]{1,0:T(8,128)S(1)}, u32[]{:S(2)}, u32[]{:S(2)}) collective-permute-start(f32[256,512]{1,0:T(8,128)S(1)} %get-tuple-element.35.refs_1_), channel_id=1, source_target_pairs={{0,4},{4,0},{8,12},{12,8},{16,20},{20,16},{24,28},{28,24},{1,5},{5... | collective-permute-start | bytes 1572872 | tf_op jit(solution)/shard_map/ppermute | solution.py:281
  95.1 2.6 %collective-permute-start.24 = (f32[256,512]{1,0:T(8,128)S(1)}, f32[256,512]{1,0:T(8,128)S(1)}, u32[]{:S(2)}, u32[]{:S(2)}) collective-permute-start(f32[256,512]{1,0:T(8,128)S(1)} %collective-permute-done.17.refs_2_), channel_id=1, source_target_pairs={{0,4},{4,0},{8,12},{12,8},{16,20},{20,16},{24,28},{28,24},{1,5},{5... | collective-permute-start | bytes 1572872 | tf_op jit(solution)/shard_map/ppermute | solution.py:281
  95.1 9.2 %collective-permute-start.18 = (f32[256,512]{1,0:T(8,128)S(1)}, f32[256,512]{1,0:T(8,128)S(1)}, u32[]{:S(2)}, u32[]{:S(2)}) collective-permute-start(f32[256,512]{1,0:T(8,128)S(1)} %collective-permute-done.17.refs_2_), channel_id=1, source_target_pairs={{0,8},{4,20},{8,0},{12,28},{16,24},{20,4},{24,16},{28,12},{1,9},{5... | collective-permute-start | bytes 1572872 | tf_op jit(solution)/shard_map/ppermute | solution.py:281
  95.7 14.2 %collective-permute-start.15 = (f32[256,512]{1,0:T(8,128)S(1)}, f32[256,512]{1,0:T(8,128)S(1)}, u32[]{:S(2)}, u32[]{:S(2)}) collective-permute-start(f32[256,512]{1,0:T(8,128)S(1)} %collective-permute-done.14.refs_3_), channel_id=1, source_target_pairs={{0,8},{4,20},{8,0},{12,28},{16,24},{20,4},{24,16},{28,12},{1,9},{5... | collective-permute-start | bytes 1572872 | tf_op jit(solution)/shard_map/ppermute | solution.py:281
  97.2 12.8 %collective-permute-start.25 = (f32[256,512]{1,0:T(8,128)S(1)}, f32[256,512]{1,0:T(8,128)S(1)}, u32[]{:S(2)}, u32[]{:S(2)}) collective-permute-start(f32[256,512]{1,0:T(8,128)S(1)} %collective-permute-done.14.refs_3_), channel_id=1, source_target_pairs={{0,4},{4,0},{8,12},{12,8},{16,20},{20,16},{24,28},{28,24},{1,5},{5... | collective-permute-start | bytes 1572872 | tf_op jit(solution)/shard_map/ppermute | solution.py:281
  97.2 12.8 %collective-permute-start.26 = (f32[256,512]{1,0:T(8,128)S(1)}, f32[256,512]{1,0:T(8,128)S(1)}, u32[]{:S(2)}, u32[]{:S(2)}) collective-permute-start(f32[256,512]{1,0:T(8,128)S(1)} %collective-permute-done.20.refs_4_), channel_id=1, source_target_pairs={{0,4},{4,0},{8,12},{12,8},{16,20},{20,16},{24,28},{28,24},{1,5},{5... | collective-permute-start | bytes 1572872 | tf_op jit(solution)/shard_map/ppermute | solution.py:281
  97.7 12.3 %collective-permute-start.27 = (f32[256,512]{1,0:T(8,128)S(1)}, f32[256,512]{1,0:T(8,128)S(1)}, u32[]{:S(2)}, u32[]{:S(2)}) collective-permute-start(f32[256,512]{1,0:T(8,128)S(1)} %collective-permute-done.21.refs_5_), channel_id=1, source_target_pairs={{0,4},{4,0},{8,12},{12,8},{16,20},{20,16},{24,28},{28,24},{1,5},{5... | collective-permute-start | bytes 1572872 | tf_op jit(solution)/shard_map/ppermute | solution.py:281
  104.3 8.4 %collective-permute-start.19 = (f32[256,512]{1,0:T(8,128)S(1)}, f32[256,512]{1,0:T(8,128)S(1)}, u32[]{:S(2)}, u32[]{:S(2)}) collective-permute-start(f32[256,512]{1,0:T(8,128)S(1)} %collective-permute-done.18.refs_0_), channel_id=1, source_target_pairs={{0,4},{4,0},{8,12},{12,8},{16,20},{20,16},{24,28},{28,24},{1,5},{5... | collective-permute-start | bytes 1572872 | tf_op jit(solution)/shard_map/ppermute | solution.py:281
  109.9 4.3 %collective-permute-start.16 = (f32[256,512]{1,0:T(8,128)S(1)}, f32[256,512]{1,0:T(8,128)S(1)}, u32[]{:S(2)}, u32[]{:S(2)}) collective-permute-start(f32[256,512]{1,0:T(8,128)S(1)} %collective-permute-done.15.refs_0_), channel_id=1, source_target_pairs={{0,4},{4,0},{8,12},{12,8},{16,20},{20,16},{24,28},{28,24},{1,5},{5... | collective-permute-start | bytes 1572872 | tf_op jit(solution)/shard_map/ppermute | solution.py:281
  (6 other events, 7.0 us)

commit v5 on v4

--- a/solution.py
+++ b/solution.py
@@ -113,44 +113,45 @@
     return grad_ref[rows, columns].astype(F32)
 
 
-def half_rows(half, width):
-    return pl.ds(half * (width // 2), width // 2)
-
-
-def half_shape(width):
-    return jax.ShapeDtypeStruct((width // 2, width), F32)
-
-
-def pack_kernel(slots, width, owners_ref, me_ref, grad_ref, *out_refs):
-    place = 0
-    for slot in slots:
-        target = pair_target(slot, me_ref[0] ^ 1)
-        for half in HALVES:
-            out_refs[place][...] = owner_block(owners_ref, grad_ref, half_rows(half, width), width, target)
-            place += 1
-
-
-def pack_call(owners, me, grads, slots, width):
-    shapes = [half_shape(width)] * (2 * len(slots))
-    kernel = functools.partial(pack_kernel, slots, width)
+def rows_of(half, width):
+    return pl.ds(0, width) if half is None else pl.ds(half * (width // 2), width // 2)
+
+
+def piece_shape(half, width):
+    return jax.ShapeDtypeStruct((width if half is None else width // 2, width), F32)
+
+
+def piece_of(ref, half, width):
+    return ref[rows_of(half, width), :] if ref.shape[0] == width else ref[...]
+
+
+def pack_call(owners, me, grads, pieces, width):
+    def kernel(owners_ref, me_ref, grad_ref, *out_refs):
+        for (slot, half), out_ref in zip(pieces, out_refs):
+            target = pair_target(slot, me_ref[0] ^ 1)
+            out_ref[...] = owner_block(owners_ref, grad_ref, rows_of(half, width), width, target)
+
+    shapes = [piece_shape(half, width) for _, half in pieces]
     return local_call(kernel, "pack", shapes, (grads,), (owners, me))
 
 
 def add_call(owners, me, grads, slot, half, arrivals, width):
     def kernel(owners_ref, me_ref, grad_ref, *refs):
         target = pair_target(slot, me_ref[0])
-        total = owner_block(owners_ref, grad_ref, half_rows(half, width), width, target)
+        total = owner_block(owners_ref, grad_ref, rows_of(half, width), width, target)
         for ref in refs[:-1]:
-            total = total + ref[...]
+            total = total + piece_of(ref, half, width)
         refs[-1][...] = total
 
-    return local_call(kernel, "add", half_shape(width), (grads, *arrivals), (owners, me))
-
-
-def join_call(owners, me, total, arrival, norm, block_count, device_count):
+    return local_call(kernel, "add", piece_shape(half, width), (grads, *arrivals), (owners, me))
+
+
+def join_call(owners, me, total, half, arrival, norm, block_count):
+    width = total.shape[1]
+
     def kernel(owners_ref, me_ref, total_ref, arrival_ref, *refs):
         block_ref, norm_ref = refs[-2:]
-        block = total_ref[...] + arrival_ref[...]
+        block = piece_of(total_ref, half, width) + arrival_ref[...]
         block_ref[...] = block
         owned = 0
         for index in range(block_count):
@@ -158,9 +159,10 @@
         squares = jnp.sum(block * block, keepdims=True).reshape(1, 1) * owned.astype(F32)
         if norm is not None:
             squares = squares + refs[0][:1, :1]
-        norm_ref[...] = jnp.broadcast_to(squares, norm_ref.shape)
-
-    shapes = [half_shape(total.shape[1]), jax.ShapeDtypeStruct((device_count, 128), F32)]
+        rows = lax.broadcasted_iota(jnp.int32, norm_ref.shape, 0)
+        norm_ref[...] = jnp.where(rows == 0, squares, 0.0)
+
+    shapes = [piece_shape(half, width), jax.ShapeDtypeStruct((8, 128), F32)]
     operands = (total, arrival) if norm is None else (total, arrival, norm)
     return local_call(kernel, "join", shapes, operands, (owners, me))
 
@@ -213,11 +215,12 @@
         block_norm = jnp.sum(block * block, keepdims=True).reshape(1, 1) * (clip_factor * clip_factor)
         pre_norm = jnp.sum(pre * pre, keepdims=True).reshape(1, 1)
         update = pre * jnp.sqrt(block_norm / (pre_norm + graft_eps))
+        out_refs[0][...] = update
         for half in HALVES:
-            out_refs[half][...] = update[half * (width // 2) : (half + 1) * (width // 2)]
+            out_refs[1 + half][...] = update[half * (width // 2) : (half + 1) * (width // 2)]
 
     operands = (*block, left_gram, right_gram, left_prev, right_prev, norms)
-    shapes = [half_shape(width)] * 2
+    shapes = [piece_shape(half, width) for half in (None, *HALVES)]
     return local_call(kernel, "update", shapes, operands, flops=48 * width**3, vmem=LARGE)
 
 
@@ -235,7 +238,7 @@
                 owned = owned + jnp.where(matches, 1, 0)
                 column = column + jnp.where(matches, index * width, 0)
             columns = pl.ds(pl.multiple_of(column, width), width)
-            spot = out_ref.at[half_rows(half, width), columns]
+            spot = out_ref.at[rows_of(half, width), columns]
             copies.append((owned, pltpu.make_async_copy(refs[number], spot, sem.at[number])))
         for owned, copy in copies:
             pl.when(owned == 1)(copy.start)
@@ -270,52 +273,58 @@
     owner_row = owners[0]
     block_count = owner_row.shape[0]
     me = lax.axis_index("dp").astype(jnp.int32).reshape(1)
-    device_count = 8 * lax.axis_size("mp")
     entry_count = width * block_count * width * lax.axis_size("mp")
 
     first_pairs = [(i, i ^ (2 + 2 * (i % 2))) for i in range(8)]
     second_pairs = [(i, i ^ (4 - 2 * (i % 2))) for i in range(8)]
     core_pairs = [(i, i ^ 1) for i in range(8)]
 
-    def over(pairs, value):
-        return lax.ppermute(value, "dp", pairs)
+    def over(pairs, value, label="move"):
+        with jax.named_scope(label):
+            return lax.ppermute(value, "dp", pairs)
 
     def own_plus(slot, half, *arrivals):
         return add_call(owner_row, me, grads, slot, half, arrivals, width)
 
+    def after(value, *others):
+        return lax.optimization_barrier((value, *others))[0]
+
     grads = replica_grads[0]
-    pieces = pack_call(owner_row, me, grads, (3, 2), width)
-    pieces += pack_call(owner_row, me, grads, (1, 0), width)
-    keys = [(slot, half) for slot in (3, 2, 1, 0) for half in HALVES]
-    from_core = {key: over(core_pairs, value) for key, value in zip(keys, pieces)}
-    from_first = {}
-    for slot in (3, 2):
-        for half in HALVES:
-            from_first[slot, half] = over(first_pairs, own_plus(slot, half, from_core[slot, half]))
-    from_second = [
-        over(second_pairs, own_plus(1, half, from_core[1, half], from_first[3, half])) for half in HALVES
-    ]
+    early = pack_call(owner_row, me, grads, [(3, 0), (3, 1)], width)
+    core_three = [over(core_pairs, early[h], "core3%d"%h) for h in HALVES]
+    sums_three = [own_plus(3, h, core_three[h]) for h in HALVES]
+    first_three = [over(first_pairs, sums_three[h], "first3%d"%h) for h in HALVES]
+    late = pack_call(owner_row, after(me, *sums_three), grads, [(2, None)], width)
+    core_two = over(core_pairs, late[0], "core2")
+    late += pack_call(owner_row, after(me, core_two), grads, [(1, None), (0, None)], width)
+    core_one = over(core_pairs, late[1], "core1")
+    first_two = over(first_pairs, own_plus(2, None, core_two), "first2")
+    core_zero = over(core_pairs, after(late[2], first_three[1]), "core0")
+    second = [over(second_pairs, own_plus(1, h, core_one, first_three[h]), "second%d"%h) for h in HALVES]
+    total = own_plus(0, None, core_zero, first_two)
     norm, block = None, []
     for half in HALVES:
-        total = own_plus(0, half, from_core[0, half], from_first[2, half])
-        joined, norm = join_call(owner_row, me, total, from_second[half], norm, block_count, device_count)
+        joined, norm = join_call(owner_row, me, total, half, second[half], norm, block_count)
         block.append(joined)
-    norms = lax.all_to_all(norm, ("dp", "mp"), split_axis=0, concat_axis=0, tiled=True)
+    norms = lax.all_gather(norm, ("dp", "mp"), axis=0, tiled=True)
     left_gram, right_gram = gram_call(block)
-    update = update_call(block, left_gram, right_gram, left_stats[0], right_stats[0], norms, entry_count)
-
-    near = [over(second_pairs, value) for value in update]
-    far = [over(first_pairs, value) for value in update]
-    relayed = [over(first_pairs, value) for value in near]
-    held = dict(zip([(place, half) for place in range(4) for half in HALVES], [*update, *near, *far, *relayed]))
-    held.update({(place + 4, half): over(core_pairs, value) for (place, half), value in held.items()})
+    whole, *own = update_call(block, left_gram, right_gram, left_stats[0], right_stats[0], norms, entry_count)
+
+    near = [over(second_pairs, own[h], "near%d"%h) for h in HALVES]
+    far = over(first_pairs, after(whole, near[1]), "far")
+    relayed = [over(first_pairs, near[h], "relay%d"%h) for h in HALVES]
+    w = after(whole, near[0])
+    n = [after(near[h], far) for h in HALVES]
+    core_own = over(core_pairs, w, "core_own")
+    core_near = [over(core_pairs, n[h], "core_near%d"%h) for h in HALVES]
+    core_far = over(core_pairs, far, "core_far")
+    core_relay = [over(core_pairs, relayed[h], "core_relay%d"%h) for h in HALVES]
+    groups = [{(0,None):w, (4,None):core_own, (1,0):n[0],(1,1):n[1],(5,0):core_near[0],(5,1):core_near[1],(2,None):far,(6,None):core_far}, {(3,0):relayed[0],(7,0):core_relay[0],(3,1):relayed[1],(7,1):core_relay[1]}]
+
     result = None
-    for places in (
-        [key for key in held if key[0] & 3 != 3],
-        [(3, 0), (7, 0)],
-        [(3, 1), (7, 1)],
-    ):
-        result = assemble_call(owner_row, me, places, [held[key] for key in places], block_count, result)
+    for group in groups:
+        keys, here = zip(*group.items())
+        result = assemble_call(owner_row, me, keys, here, block_count, result)
     return result
 
 

time: 116 us -> 170 us (1.47)
  blocking collectives: 0 us -> 70 us
  starting transfers between devices: 23.6 us -> 13.8 us
  local copies, waits for them, and re-layouts: 6.96 us -> 2.56 us
  Pallas kernels: 24.4 us -> 22.2 us
    all_gather x0 -> x1, blocking collectives: none -> 70 us  [paired_body(): norms = lax.all_gather(norm, ('dp', 'mp'), axis=0, tiled=True)]
    all_to_all x1 -> x0, starting transfers between devices: 6.1 us -> none  [paired_body(): lax.all_to_all(norm, ('dp', 'mp'), split_axis=0, concat_axis=0, tiled=True)]
    unnamed x18 -> x10, local copies, waits for them, and re-layouts: 6.96 us -> 2.56 us
    ppermute x28 -> x21, waiting for transfers between devices: 57.2 us -> 61.3 us  [over(): return lax.ppermute(value, 'dp', pairs)]
    ppermute x28 -> x21, starting transfers between devices: 17.5 us -> 13.8 us  [over(): return lax.ppermute(value, 'dp', pairs)]
    all_to_all x1 -> x0, waiting for transfers between devices: 3.37 us -> none  [paired_body(): lax.all_to_all(norm, ('dp', 'mp'), split_axis=0, concat_axis=0, tiled=True)]
    pallas_call x3 -> x2, Pallas kernels: 5.78 us -> 4.54 us  [assemble_call(): pl.pallas_call(kernel, in_specs=in_specs, out_specs=pl.BlockSpec(memory_s...]
    pallas_call x14 -> x13, Pallas kernels: 18.6 us -> 17.6 us  [local_call(): pl.pallas_call(kernel, in_specs=[pl.BlockSpec(memory_space=pltpu.SMEM)] *...]
  transfers between devices with their start and end apart: 29 -> 21, of which waited for: 10 -> 11; matrix products, arithmetic and copies ran while one was open for 0% -> 0% of each run, Pallas kernels for 11% -> 5%
where the time goes in v5:
time: 170 us
  blocking collectives  70 us (41%)
  waiting for transfers between devices  61.3 us (36%)
  Pallas kernels  22.2 us (13%)
  starting transfers between devices  13.8 us (8%)
  local copies, waits for them, and re-layouts  2.56 us (2%)
    all_gather x1, blocking collectives, paired_body(): norms = lax.all_gather(norm, ('dp', 'mp'), axis=0, tiled=True)  70 us
    ppermute x21, waiting for transfers between devices, over(): return lax.ppermute(value, 'dp', pairs)  61.3 us
    pallas_call x13, Pallas kernels, local_call(): pl.pallas_call(kernel, in_specs=[pl.BlockSpec(memory_space=pltpu.SMEM)] *...  17.6 us
    ppermute x21, starting transfers between devices, over(): return lax.ppermute(value, 'dp', pairs)  13.8 us
    pallas_call x2, Pallas kernels, assemble_call(): pl.pallas_call(kernel, in_specs=in_specs, out_specs=pl.BlockSpec(memory_s...  4.54 us
  transfers between devices with their start and end apart: 21, of which 11 were waited for; matrix products, arithmetic and copies ran while one was open for 0% of the time, Pallas kernels for 5%

profile of v5, /device:TPU:0, one launch (start us, length us, event | category | flops | bytes accessed | tf_op | source)
XLA Modules:
  0.0 170.1 jit_solution(3527046213931855935)
XLA Ops:
  0.0 1.9 %copy-done = bf16[1,512,3072]{2,1,0:T(8,128)(2,1)S(1)} copy-done((bf16[1,512,3072]{2,1,0:T(8,128)(2,1)S(1)}, bf16[1,512,3072]{2,1,0:T(8,128)(2,1)}, u32[]{:S(2)}) %copy-start) | copy-done | bytes 3145752
  1.9 0.7 copy-done.1
  2.5 0.6 pack.3
  3.8 1.5 collective-permute-done.refs_0_
  5.2 0.6 add.6
  6.6 0.6 pack.4
  7.6 2.6 %collective-permute-start.3 = (f32[256,512]{1,0:T(8,128)S(1)}, f32[256,512]{1,0:T(8,128)S(1)}, u32[]{:S(2)}, u32[]{:S(2)}) collective-permute-start(f32[256,512]{1,0:T(8,128)S(1)} %add.7), channel_id=1, source_target_pairs={{0,8},{4,20},{8,0},{12,28},{16,24},{20,4},{24,16},{28,12},{1,9},{5... | collective-permute-start | bytes 1572872 | tf_op jit(solution)/shard_map/first31/ppermute | solution.py:284
  10.3 0.7 pack.5
  11.2 2.5 %collective-permute-start.7 = (f32[256,512]{1,0:T(8,128)S(1)}, f32[256,512]{1,0:T(8,128)S(1)}, u32[]{:S(2)}, u32[]{:S(2)}) collective-permute-start(f32[256,512]{1,0:T(8,128)S(1)} %add.6), channel_id=1, source_target_pairs={{0,8},{4,20},{8,0},{12,28},{16,24},{20,4},{24,16},{28,12},{1,9},{5... | collective-permute-start | bytes 1572872 | tf_op jit(solution)/shard_map/first30/ppermute | solution.py:284
  13.7 0.7 add.8
  14.4 3.0 %collective-permute-done.3.refs_1_ = f32[256,512]{1,0:T(8,128)S(1)} collective-permute-done((f32[256,512]{1,0:T(8,128)S(1)}, f32[256,512]{1,0:T(8,128)S(1)}, u32[]{:S(2)}, u32[]{:S(2)}) %collective-permute-start.3) | collective-permute-done | bytes 524320 | tf_op jit(solution)/shard_map/first31/ppermute | solution.py:284
  17.4 5.6 %collective-permute-done.7.refs_1_ = f32[256,512]{1,0:T(8,128)S(1)} collective-permute-done((f32[256,512]{1,0:T(8,128)S(1)}, f32[256,512]{1,0:T(8,128)S(1)}, u32[]{:S(2)}, u32[]{:S(2)}) %collective-permute-start.7) | collective-permute-done | bytes 524320 | tf_op jit(solution)/shard_map/first30/ppermute | solution.py:284
  23.1 0.6 add.10
  23.7 2.1 %collective-permute-start.8 = (f32[256,512]{1,0:T(8,128)S(1)}, f32[256,512]{1,0:T(8,128)S(1)}, u32[]{:S(2)}, u32[]{:S(2)}) collective-permute-start(f32[256,512]{1,0:T(8,128)S(1)} %add.10), channel_id=1, source_target_pairs={{0,16},{4,12},{8,24},{12,4},{16,0},{20,28},{24,8},{28,20},{1,17},{... | collective-permute-start | bytes 1572872 | tf_op jit(solution)/shard_map/second0/ppermute | solution.py:284
  25.8 0.6 add.11
  26.5 15.8 %collective-permute-done.5.refs_1_ = f32[512,512]{1,0:T(8,128)S(1)} collective-permute-done((f32[512,512]{1,0:T(8,128)S(1)}, f32[512,512]{1,0:T(8,128)S(1)}, u32[]{:S(2)}, u32[]{:S(2)}) %collective-permute-start.5) | collective-permute-done | bytes 1048608 | tf_op jit(solution)/shard_map/first2/ppermute | solution.py:284
  42.3 0.7 add.9.total_ref
  43.0 0.9 join.2
  43.9 1.3 collective-permute-done.9.arrival_ref
  45.2 0.9 join.3
  46.1 70.0 %all_gather.3.norm_ref = f32[256,128]{1,0:T(8,128)S(1)} all-gather(f32[8,128]{1,0:T(8,128)S(1)} %get-tuple-element.37), channel_id=1, replica_groups=mesh['dp'=8,'mp'=4] {'dp','mp'}, dimensions={0}, use_global_device_ids=true | all-gather | bytes 135168 | tf_op jit(solution)/shard_map/all_gather | solution.py:309
  116.2 1.8 %gram.1 = (f32[512,512]{1,0:T(8,128)S(1)}, f32[512,512]{1,0:T(8,128)S(1)}) custom-call(f32[256,512]{1,0:T(8,128)S(1)} %get-tuple-element.32.upper_ref, f32[256,512]{1,0:T(8,128)S(1)} %get-tuple-element.34.lower_ref), custom_call_target="tpu_custom_call" | custom-call | flops 1610612736 | bytes 3145728 | tf_op jit(solution)/shard_map/gram/pallas_call | solution.py:96
  118.0 8.4 %update.1 = (f32[512,512]{1,0:T(8,128)S(1)}, f32[256,512]{1,0:T(8,128)S(1)}, f32[256,512]{1,0:T(8,128)S(1)}) custom-call(f32[256,512]{1,0:T(8,128)S(1)} %get-tuple-element.32.upper_ref, f32[256,512]{1,0:T(8,128)S(1)} %get-tuple-element.34.lower_ref, f32[512,512]{1,0:T(8,128)S(1)} %get-tuple-element.35.left_gram_ref, ...), custom_call_target="tpu_custom_call" | custom-call | flops 6442450944 | bytes 7471104 | tf_op jit(solution)/shard_map/update/pallas_call | solution.py:96
  127.0 1.5 collective-permute-start.10
  128.5 10.5 %collective-permute-done.13.refs_3_ = f32[256,512]{1,0:T(8,128)S(1)} collective-permute-done((f32[256,512]{1,0:T(8,128)S(1)}, f32[256,512]{1,0:T(8,128)S(1)}, u32[]{:S(2)}, u32[]{:S(2)}) %collective-permute-start.13) | collective-permute-done | bytes 524320 | tf_op jit(solution)/shard_map/near1/ppermute | solution.py:284
  139.0 11.2 %collective-permute-done.10.refs_2_ = f32[256,512]{1,0:T(8,128)S(1)} collective-permute-done((f32[256,512]{1,0:T(8,128)S(1)}, f32[256,512]{1,0:T(8,128)S(1)}, u32[]{:S(2)}, u32[]{:S(2)}) %collective-permute-start.10) | collective-permute-done | bytes 524320 | tf_op jit(solution)/shard_map/near0/ppermute | solution.py:284
  150.2 2.0 %collective-permute-start.14 = (f32[256,512]{1,0:T(8,128)S(1)}, f32[256,512]{1,0:T(8,128)S(1)}, u32[]{:S(2)}, u32[]{:S(2)}) collective-permute-start(f32[256,512]{1,0:T(8,128)S(1)} %collective-permute-done.13.refs_3_), channel_id=1, source_target_pairs={{0,8},{4,20},{8,0},{12,28},{16,24},{20,4},{24,16},{28,12},{1,9},{5... | collective-permute-start | bytes 1572872 | tf_op jit(solution)/shard_map/relay1/ppermute | solution.py:284
  152.2 1.5 collective-permute-done.17.refs_6_
  154.3 5.1 %collective-permute-done.11.refs_0_ = f32[256,512]{1,0:T(8,128)S(1)} collective-permute-done((f32[256,512]{1,0:T(8,128)S(1)}, f32[256,512]{1,0:T(8,128)S(1)}, u32[]{:S(2)}, u32[]{:S(2)}) %collective-permute-start.11) | collective-permute-done | bytes 524320 | tf_op jit(solution)/shard_map/relay0/ppermute | solution.py:284
  159.4 5.6 %collective-permute-done.14.refs_2_ = f32[256,512]{1,0:T(8,128)S(1)} collective-permute-done((f32[256,512]{1,0:T(8,128)S(1)}, f32[256,512]{1,0:T(8,128)S(1)}, u32[]{:S(2)}, u32[]{:S(2)}) %collective-permute-start.14) | collective-permute-done | bytes 524320 | tf_op jit(solution)/shard_map/relay1/ppermute | solution.py:284
  165.6 3.0 %assemble.2.refs_4_ = f32[512,3072]{1,0:T(8,128)} custom-call(s32[6]{0:T(128)S(1)} %bitcast.25, s32[1]{0:T(128)} %bitcast.1.me_ref, f32[512,512]{1,0:T(8,128)S(1)} %get-tuple-element.42.refs_0_, f32[512,512]{1,0:T(8,128)S(1)} %collective-permute-done.16.refs_1_, f32[256,512]{1,0:T(8,128)S(1)} %collective-permute-done.10.refs_2_, ...), custom_call_target="tpu_custom_call" | custom-call | bytes 16777216 | tf_op jit(solution)/shard_map/assemble/pallas_call | solution.py:256
  168.6 1.6 assemble.3
  (36 shorter events, 3.8 us)
Async XLA Ops:
  0.0 1.9 %copy-start = (bf16[1,512,3072]{2,1,0:T(8,128)(2,1)S(1)}, bf16[1,512,3072]{2,1,0:T(8,128)(2,1)}, u32[]{:S(2)}) copy-start(bf16[1,512,3072]{2,1,0:T(8,128)(2,1)} %param.4) | copy-start | bytes 9437188
  1.9 0.7 copy-start.1
  3.2 2.1 %collective-permute-start = (f32[256,512]{1,0:T(8,128)S(1)}, f32[256,512]{1,0:T(8,128)S(1)}, u32[]{:S(2)}, u32[]{:S(2)}) collective-permute-start(f32[256,512]{1,0:T(8,128)S(1)} %get-tuple-element.25), channel_id=1, source_target_pairs={{0,4},{4,0},{8,12},{12,8},{16,20},{20,16},{24,28},{28,24},{1,5},{5... | collective-permute-start | bytes 1572872 | tf_op jit(solution)/shard_map/core30/ppermute | solution.py:284
  3.7 2.3 %collective-permute-start.1 = (f32[256,512]{1,0:T(8,128)S(1)}, f32[256,512]{1,0:T(8,128)S(1)}, u32[]{:S(2)}, u32[]{:S(2)}) collective-permute-start(f32[256,512]{1,0:T(8,128)S(1)} %get-tuple-element.26), channel_id=1, source_target_pairs={{0,4},{4,0},{8,12},{12,8},{16,20},{20,16},{24,28},{28,24},{1,5},{5... | collective-permute-start | bytes 1572872 | tf_op jit(solution)/shard_map/core31/ppermute | solution.py:284
  7.2 3.1 %collective-permute-start.2 = (f32[512,512]{1,0:T(8,128)S(1)}, f32[512,512]{1,0:T(8,128)S(1)}, u32[]{:S(2)}, u32[]{:S(2)}) collective-permute-start(f32[512,512]{1,0:T(8,128)S(1)} %pack.4), channel_id=1, source_target_pairs={{0,4},{4,0},{8,12},{12,8},{16,20},{20,16},{24,28},{28,24},{1,5},{5... | collective-permute-start | bytes 3145736 | tf_op jit(solution)/shard_map/core2/ppermute | solution.py:284
  7.6 9.8 %collective-permute-start.3 = (f32[256,512]{1,0:T(8,128)S(1)}, f32[256,512]{1,0:T(8,128)S(1)}, u32[]{:S(2)}, u32[]{:S(2)}) collective-permute-start(f32[256,512]{1,0:T(8,128)S(1)} %add.7), channel_id=1, source_target_pairs={{0,8},{4,20},{8,0},{12,28},{16,24},{20,4},{24,16},{28,12},{1,9},{5... | collective-permute-start | bytes 1572872 | tf_op jit(solution)/shard_map/first31/ppermute | solution.py:284
  11.0 12.1 %collective-permute-start.6 = (f32[512,512]{1,0:T(8,128)S(1)}, f32[512,512]{1,0:T(8,128)S(1)}, u32[]{:S(2)}, u32[]{:S(2)}) collective-permute-start(f32[512,512]{1,0:T(8,128)S(1)} %get-tuple-element.31), channel_id=1, source_target_pairs={{0,4},{4,0},{8,12},{12,8},{16,20},{20,16},{24,28},{28,24},{1,5},{5... | collective-permute-start | bytes 3145736 | tf_op jit(solution)/shard_map/core1/ppermute | solution.py:284
  11.2 11.9 %collective-permute-start.7 = (f32[256,512]{1,0:T(8,128)S(1)}, f32[256,512]{1,0:T(8,128)S(1)}, u32[]{:S(2)}, u32[]{:S(2)}) collective-permute-start(f32[256,512]{1,0:T(8,128)S(1)} %add.6), channel_id=1, source_target_pairs={{0,8},{4,20},{8,0},{12,28},{16,24},{20,4},{24,16},{28,12},{1,9},{5... | collective-permute-start | bytes 1572872 | tf_op jit(solution)/shard_map/first30/ppermute | solution.py:284
  14.3 28.0 %collective-permute-start.5 = (f32[512,512]{1,0:T(8,128)S(1)}, f32[512,512]{1,0:T(8,128)S(1)}, u32[]{:S(2)}, u32[]{:S(2)}) collective-permute-start(f32[512,512]{1,0:T(8,128)S(1)} %add.8), channel_id=1, source_target_pairs={{0,8},{4,20},{8,0},{12,28},{16,24},{20,4},{24,16},{28,12},{1,9},{5... | collective-permute-start | bytes 3145736 | tf_op jit(solution)/shard_map/first2/ppermute | solution.py:284
  17.4 24.9 %collective-permute-start.4 = (f32[512,512]{1,0:T(8,128)S(1)}, f32[512,512]{1,0:T(8,128)S(1)}, u32[]{:S(2)}, u32[]{:S(2)}) collective-permute-start(f32[512,512]{1,0:T(8,128)S(1)} %get-tuple-element.30), channel_id=1, source_target_pairs={{0,4},{4,0},{8,12},{12,8},{16,20},{20,16},{24,28},{28,24},{1,5},{5... | collective-permute-start | bytes 3145736 | tf_op jit(solution)/shard_map/core0/ppermute | solution.py:284
  23.7 19.4 %collective-permute-start.8 = (f32[256,512]{1,0:T(8,128)S(1)}, f32[256,512]{1,0:T(8,128)S(1)}, u32[]{:S(2)}, u32[]{:S(2)}) collective-permute-start(f32[256,512]{1,0:T(8,128)S(1)} %add.10), channel_id=1, source_target_pairs={{0,16},{4,12},{8,24},{12,4},{16,0},{20,28},{24,8},{28,20},{1,17},{... | collective-permute-start | bytes 1572872 | tf_op jit(solution)/shard_map/second0/ppermute | solution.py:284
  26.4 91.6 %copy-start.3 = (f32[1,512,512]{2,1,0:T(8,128)S(1)}, f32[1,512,512]{2,1,0:T(8,128)}, u32[]{:S(2)}) copy-start(f32[1,512,512]{2,1,0:T(8,128)} %param.6) | copy-start | bytes 3145732
  26.4 91.6 %copy-start.4 = (f32[1,512,512]{2,1,0:T(8,128)S(1)}, f32[1,512,512]{2,1,0:T(8,128)}, u32[]{:S(2)}) copy-start(f32[1,512,512]{2,1,0:T(8,128)} %param.7) | copy-start | bytes 3145732
  26.4 18.8 %collective-permute-start.9 = (f32[256,512]{1,0:T(8,128)S(1)}, f32[256,512]{1,0:T(8,128)S(1)}, u32[]{:S(2)}, u32[]{:S(2)}) collective-permute-start(f32[256,512]{1,0:T(8,128)S(1)} %add.11), channel_id=1, source_target_pairs={{0,16},{4,12},{8,24},{12,4},{16,0},{20,28},{24,8},{28,20},{1,17},{... | collective-permute-start | bytes 1572872 | tf_op jit(solution)/shard_map/second1/ppermute | solution.py:284
  118.0 47.5 %copy-start.2 = (s32[1,6]{1,0:T(1,128)S(1)}, s32[1,6]{1,0:T(1,128)}, u32[]{:S(2)}) copy-start(s32[1,6]{1,0:T(1,128)} %param.5) | copy-start | bytes 76
  126.4 12.6 %collective-permute-start.13 = (f32[256,512]{1,0:T(8,128)S(1)}, f32[256,512]{1,0:T(8,128)S(1)}, u32[]{:S(2)}, u32[]{:S(2)}) collective-permute-start(f32[256,512]{1,0:T(8,128)S(1)} %get-tuple-element.39), channel_id=1, source_target_pairs={{0,16},{4,12},{8,24},{12,4},{16,0},{20,28},{24,8},{28,20},{1,17},{... | collective-permute-start | bytes 1572872 | tf_op jit(solution)/shard_map/near1/ppermute | solution.py:284
  127.0 23.2 %collective-permute-start.10 = (f32[256,512]{1,0:T(8,128)S(1)}, f32[256,512]{1,0:T(8,128)S(1)}, u32[]{:S(2)}, u32[]{:S(2)}) collective-permute-start(f32[256,512]{1,0:T(8,128)S(1)} %get-tuple-element.38), channel_id=1, source_target_pairs={{0,16},{4,12},{8,24},{12,4},{16,0},{20,28},{24,8},{28,20},{1,17},{... | collective-permute-start | bytes 1572872 | tf_op jit(solution)/shard_map/near0/ppermute | solution.py:284
  139.0 14.8 %collective-permute-start.17 = (f32[512,512]{1,0:T(8,128)S(1)}, f32[512,512]{1,0:T(8,128)S(1)}, u32[]{:S(2)}, u32[]{:S(2)}) collective-permute-start(f32[512,512]{1,0:T(8,128)S(1)} %get-tuple-element.42.refs_0_), channel_id=1, source_target_pairs={{0,8},{4,20},{8,0},{12,28},{16,24},{20,4},{24,16},{28,12},{1,9},{5... | collective-permute-start | bytes 3145736 | tf_op jit(solution)/shard_map/far/ppermute | solution.py:284
  150.2 14.8 %collective-permute-start.16 = (f32[512,512]{1,0:T(8,128)S(1)}, f32[512,512]{1,0:T(8,128)S(1)}, u32[]{:S(2)}, u32[]{:S(2)}) collective-permute-start(f32[512,512]{1,0:T(8,128)S(1)} %get-tuple-element.42.refs_0_), channel_id=1, source_target_pairs={{0,4},{4,0},{8,12},{12,8},{16,20},{20,16},{24,28},{28,24},{1,5},{5... | collective-permute-start | bytes 3145736 | tf_op jit(solution)/shard_map/core_own/ppermute | solution.py:284
  150.2 9.2 %collective-permute-start.11 = (f32[256,512]{1,0:T(8,128)S(1)}, f32[256,512]{1,0:T(8,128)S(1)}, u32[]{:S(2)}, u32[]{:S(2)}) collective-permute-start(f32[256,512]{1,0:T(8,128)S(1)} %collective-permute-done.10.refs_2_), channel_id=1, source_target_pairs={{0,8},{4,20},{8,0},{12,28},{16,24},{20,4},{24,16},{28,12},{1,9},{5... | collective-permute-start | bytes 1572872 | tf_op jit(solution)/shard_map/relay0/ppermute | solution.py:284
  150.2 14.8 %collective-permute-start.14 = (f32[256,512]{1,0:T(8,128)S(1)}, f32[256,512]{1,0:T(8,128)S(1)}, u32[]{:S(2)}, u32[]{:S(2)}) collective-permute-start(f32[256,512]{1,0:T(8,128)S(1)} %collective-permute-done.13.refs_3_), channel_id=1, source_target_pairs={{0,8},{4,20},{8,0},{12,28},{16,24},{20,4},{24,16},{28,12},{1,9},{5... | collective-permute-start | bytes 1572872 | tf_op jit(solution)/shard_map/relay1/ppermute | solution.py:284
  153.8 11.8 %collective-permute-start.20 = (f32[512,512]{1,0:T(8,128)S(1)}, f32[512,512]{1,0:T(8,128)S(1)}, u32[]{:S(2)}, u32[]{:S(2)}) collective-permute-start(f32[512,512]{1,0:T(8,128)S(1)} %collective-permute-done.17.refs_6_), channel_id=1, source_target_pairs={{0,4},{4,0},{8,12},{12,8},{16,20},{20,16},{24,28},{28,24},{1,5},{5... | collective-permute-start | bytes 3145736 | tf_op jit(solution)/shard_map/core_far/ppermute | solution.py:284
  153.8 11.8 %collective-permute-start.18 = (f32[256,512]{1,0:T(8,128)S(1)}, f32[256,512]{1,0:T(8,128)S(1)}, u32[]{:S(2)}, u32[]{:S(2)}) collective-permute-start(f32[256,512]{1,0:T(8,128)S(1)} %collective-permute-done.10.refs_2_), channel_id=1, source_target_pairs={{0,4},{4,0},{8,12},{12,8},{16,20},{20,16},{24,28},{28,24},{1,5},{5... | collective-permute-start | bytes 1572872 | tf_op jit(solution)/shard_map/core_near0/ppermute | solution.py:284
  159.4 6.1 %collective-permute-start.19 = (f32[256,512]{1,0:T(8,128)S(1)}, f32[256,512]{1,0:T(8,128)S(1)}, u32[]{:S(2)}, u32[]{:S(2)}) collective-permute-start(f32[256,512]{1,0:T(8,128)S(1)} %collective-permute-done.13.refs_3_), channel_id=1, source_target_pairs={{0,4},{4,0},{8,12},{12,8},{16,20},{20,16},{24,28},{28,24},{1,5},{5... | collective-permute-start | bytes 1572872 | tf_op jit(solution)/shard_map/core_near1/ppermute | solution.py:284
  165.0 3.5 %collective-permute-start.12 = (f32[256,512]{1,0:T(8,128)S(1)}, f32[256,512]{1,0:T(8,128)S(1)}, u32[]{:S(2)}, u32[]{:S(2)}) collective-permute-start(f32[256,512]{1,0:T(8,128)S(1)} %collective-permute-done.11.refs_0_), channel_id=1, source_target_pairs={{0,4},{4,0},{8,12},{12,8},{16,20},{20,16},{24,28},{28,24},{1,5},{5... | collective-permute-start | bytes 1572872 | tf_op jit(solution)/shard_map/core_relay0/ppermute | solution.py:284
  165.0 3.5 %collective-permute-start.15 = (f32[256,512]{1,0:T(8,128)S(1)}, f32[256,512]{1,0:T(8,128)S(1)}, u32[]{:S(2)}, u32[]{:S(2)}) collective-permute-start(f32[256,512]{1,0:T(8,128)S(1)} %collective-permute-done.14.refs_2_), channel_id=1, source_target_pairs={{0,4},{4,0},{8,12},{12,8},{16,20},{20,16},{24,28},{28,24},{1,5},{5... | collective-permute-start | bytes 1572872 | tf_op jit(solution)/shard_map/core_relay1/ppermute | solution.py:284

commit v6 on v5

--- a/solution.py
+++ b/solution.py
@@ -84,9 +84,9 @@
     return narrow_dot(left_side[0], right_side[0], dims) + small
 
 
-def pair_target(slot, device):
-    first = 2 + 2 * (device & 1)
-    return device ^ ((slot >> 1) * first) ^ ((slot & 1) * (6 - first))
+def piece_target(kind, device):
+    along = 2 + 2 * (device & 1)
+    return {"self": device, "straight": device ^ along, "cross": device ^ along ^ 1, "diagonal": device ^ 7}[kind]
 
 
 def local_call(kernel, name, out_shape, operands, scalars=(), flops=0, vmem=None, **options):
@@ -127,17 +127,17 @@
 
 def pack_call(owners, me, grads, pieces, width):
     def kernel(owners_ref, me_ref, grad_ref, *out_refs):
-        for (slot, half), out_ref in zip(pieces, out_refs):
-            target = pair_target(slot, me_ref[0] ^ 1)
+        for (kind, half), out_ref in zip(pieces, out_refs):
+            target = piece_target(kind, me_ref[0] ^ 1)
             out_ref[...] = owner_block(owners_ref, grad_ref, rows_of(half, width), width, target)
 
     shapes = [piece_shape(half, width) for _, half in pieces]
     return local_call(kernel, "pack", shapes, (grads,), (owners, me))
 
 
-def add_call(owners, me, grads, slot, half, arrivals, width):
+def add_call(owners, me, grads, kind, half, arrivals, width):
     def kernel(owners_ref, me_ref, grad_ref, *refs):
-        target = pair_target(slot, me_ref[0])
+        target = piece_target(kind, me_ref[0])
         total = owner_block(owners_ref, grad_ref, rows_of(half, width), width, target)
         for ref in refs[:-1]:
             total = total + piece_of(ref, half, width)
@@ -157,14 +157,23 @@
         for index in range(block_count):
             owned = owned + jnp.where(owners_ref[index] == me_ref[0], 1, 0)
         squares = jnp.sum(block * block, keepdims=True).reshape(1, 1) * owned.astype(F32)
-        if norm is not None:
-            squares = squares + refs[0][:1, :1]
-        rows = lax.broadcasted_iota(jnp.int32, norm_ref.shape, 0)
-        norm_ref[...] = jnp.where(rows == 0, squares, 0.0)
+        total_squares = jnp.broadcast_to(squares, norm_ref.shape)
+        norm_ref[...] = total_squares if norm is None else total_squares + refs[0][...]
 
     shapes = [piece_shape(half, width), jax.ShapeDtypeStruct((8, 128), F32)]
     operands = (total, arrival) if norm is None else (total, arrival, norm)
     return local_call(kernel, "join", shapes, operands, (owners, me))
+
+
+def sum_kernel(*refs):
+    total = refs[0][...]
+    for ref in refs[1:-1]:
+        total = total + ref[...]
+    refs[-1][...] = total
+
+
+def sum_call(*tiles):
+    return local_call(sum_kernel, "sum", jax.ShapeDtypeStruct(tiles[0].shape, F32), tiles)
 
 
 def whole_block(block_refs):
@@ -203,8 +212,9 @@
 def update_call(block, left_gram, right_gram, left_prev, right_prev, norms, entry_count):
     width = block[0].shape[1]
 
-    def kernel(upper_ref, lower_ref, left_gram_ref, right_gram_ref, left_ref, right_ref, norm_ref, *out_refs):
-        squares = jnp.sum(norm_ref[:, :1], axis=0, keepdims=True)
+    def kernel(upper_ref, lower_ref, left_gram_ref, right_gram_ref, left_ref, right_ref, *refs):
+        norm_refs, out_refs = refs[:-3], refs[-3:]
+        squares = sum(ref[:1, :1] for ref in norm_refs)
         clip_factor = jnp.minimum(1.0, clip_level / jnp.sqrt(squares / entry_count))
         gram_scale = clip_factor * clip_factor / width
         left_root = root_of(left_ref[...], left_gram_ref[...], gram_scale)
@@ -219,7 +229,7 @@
         for half in HALVES:
             out_refs[1 + half][...] = update[half * (width // 2) : (half + 1) * (width // 2)]
 
-    operands = (*block, left_gram, right_gram, left_prev, right_prev, norms)
+    operands = (*block, left_gram, right_gram, left_prev, right_prev, *norms)
     shapes = [piece_shape(half, width) for half in (None, *HALVES)]
     return local_call(kernel, "update", shapes, operands, flops=48 * width**3, vmem=LARGE)
 
@@ -230,8 +240,8 @@
     def kernel(owners_ref, me_ref, *refs):
         out_ref, sem = refs[-2:]
         copies = []
-        for number, (place, half) in enumerate(places):
-            target = pair_target(place & 3, me_ref[0] ^ (place >> 2))
+        for number, (kind, flip, half) in enumerate(places):
+            target = piece_target(kind, me_ref[0] ^ flip)
             owned, column = 0, 0
             for index in range(block_count):
                 matches = owners_ref[index] == target
@@ -273,58 +283,76 @@
     owner_row = owners[0]
     block_count = owner_row.shape[0]
     me = lax.axis_index("dp").astype(jnp.int32).reshape(1)
-    entry_count = width * block_count * width * lax.axis_size("mp")
-
-    first_pairs = [(i, i ^ (2 + 2 * (i % 2))) for i in range(8)]
-    second_pairs = [(i, i ^ (4 - 2 * (i % 2))) for i in range(8)]
-    core_pairs = [(i, i ^ 1) for i in range(8)]
-
-    def over(pairs, value, label="move"):
+    group_count = lax.axis_size("mp")
+    entry_count = width * block_count * width * group_count
+    grads = replica_grads[0]
+
+    def flipped(mask):
+        return [(i, i ^ mask) for i in range(8)]
+
+    def over(pairs, value, label):
         with jax.named_scope(label):
             return lax.ppermute(value, "dp", pairs)
 
-    def own_plus(slot, half, *arrivals):
-        return add_call(owner_row, me, grads, slot, half, arrivals, width)
+    def to_core(value, label):
+        return over(flipped(1), value, "core_" + label)
+
+    def to_link(value, label):
+        return over([(i, i ^ (2 + 2 * (i % 2))) for i in range(8)], value, "link_" + label)
+
+    def own_plus(kind, half, *arrivals):
+        return add_call(owner_row, me, grads, kind, half, arrivals, width)
 
     def after(value, *others):
         return lax.optimization_barrier((value, *others))[0]
 
-    grads = replica_grads[0]
-    early = pack_call(owner_row, me, grads, [(3, 0), (3, 1)], width)
-    core_three = [over(core_pairs, early[h], "core3%d"%h) for h in HALVES]
-    sums_three = [own_plus(3, h, core_three[h]) for h in HALVES]
-    first_three = [over(first_pairs, sums_three[h], "first3%d"%h) for h in HALVES]
-    late = pack_call(owner_row, after(me, *sums_three), grads, [(2, None)], width)
-    core_two = over(core_pairs, late[0], "core2")
-    late += pack_call(owner_row, after(me, core_two), grads, [(1, None), (0, None)], width)
-    core_one = over(core_pairs, late[1], "core1")
-    first_two = over(first_pairs, own_plus(2, None, core_two), "first2")
-    core_zero = over(core_pairs, after(late[2], first_three[1]), "core0")
-    second = [over(second_pairs, own_plus(1, h, core_one, first_three[h]), "second%d"%h) for h in HALVES]
-    total = own_plus(0, None, core_zero, first_two)
+    early = pack_call(owner_row, me, grads, [("diagonal", half) for half in HALVES], width)
+    core_diagonal = [to_core(value, "diagonal") for value in early]
+    sums = [own_plus("diagonal", half, core_diagonal[half]) for half in HALVES]
+    diagonal = [to_link(value, "diagonal") for value in sums]
+    later = pack_call(owner_row, after(me, *sums), grads, [("cross", None)], width)
+    core_cross = to_core(later[0], "cross")
+    cross = to_link(own_plus("cross", None, after(core_cross, diagonal[0])), "cross")
+    later = pack_call(owner_row, after(me, core_cross), grads, [("straight", None), ("self", None)], width)
+    core_straight = to_core(later[0], "straight")
+    core_self = to_core(later[1], "self")
+    handed = [to_core(value, "handed") for value in diagonal]
+    straight = [
+        to_link(own_plus("straight", half, core_straight, handed[half]), "straight") for half in HALVES
+    ]
+    total = own_plus("self", None, core_self, to_core(cross, "handed_cross"))
     norm, block = None, []
     for half in HALVES:
-        joined, norm = join_call(owner_row, me, total, half, second[half], norm, block_count)
+        joined, norm = join_call(owner_row, me, total, half, straight[half], norm, block_count)
         block.append(joined)
-    norms = lax.all_gather(norm, ("dp", "mp"), axis=0, tiled=True)
+    norm = sum_call(norm, to_core(norm, "norm"))
+    norm = sum_call(norm, *[over(flipped(mask), norm, "chip_norm") for mask in (2, 4, 6)])
+    norms = [norm]
+    for shift in range(1, group_count):
+        pairs = [(i, (i + shift) % group_count) for i in range(group_count)]
+        with jax.named_scope("group_norm"):
+            norms.append(lax.ppermute(norm, "mp", pairs))
     left_gram, right_gram = gram_call(block)
     whole, *own = update_call(block, left_gram, right_gram, left_stats[0], right_stats[0], norms, entry_count)
 
-    near = [over(second_pairs, own[h], "near%d"%h) for h in HALVES]
-    far = over(first_pairs, after(whole, near[1]), "far")
-    relayed = [over(first_pairs, near[h], "relay%d"%h) for h in HALVES]
-    w = after(whole, near[0])
-    n = [after(near[h], far) for h in HALVES]
-    core_own = over(core_pairs, w, "core_own")
-    core_near = [over(core_pairs, n[h], "core_near%d"%h) for h in HALVES]
-    core_far = over(core_pairs, far, "core_far")
-    core_relay = [over(core_pairs, relayed[h], "core_relay%d"%h) for h in HALVES]
-    groups = [{(0,None):w, (4,None):core_own, (1,0):n[0],(1,1):n[1],(5,0):core_near[0],(5,1):core_near[1],(2,None):far,(6,None):core_far}, {(3,0):relayed[0],(7,0):core_relay[0],(3,1):relayed[1],(7,1):core_relay[1]}]
-
+    core_own = to_core(whole, "own")
+    first = [to_link(value, "own") for value in own]
+    core_first = [to_core(after(value, core_own), "first") for value in first]
+    second = to_link(after(core_own, first[0]), "sibling")
+    core_second = to_core(second, "second")
+    relayed = [to_link(value, "relayed") for value in core_first]
+    core_relayed = [to_core(value, "relayed") for value in relayed]
+    groups = [
+        [(("self", 0, None), whole), (("self", 1, None), core_own)]
+        + [(("straight", 0, half), first[half]) for half in HALVES]
+        + [(("straight", 1, half), core_first[half]) for half in HALVES]
+        + [(("cross", 0, None), second), (("cross", 1, None), core_second)],
+        [(("diagonal", 0, half), relayed[half]) for half in HALVES]
+        + [(("diagonal", 1, half), core_relayed[half]) for half in HALVES],
+    ]
     result = None
     for group in groups:
-        keys, here = zip(*group.items())
-        result = assemble_call(owner_row, me, keys, here, block_count, result)
+        result = assemble_call(owner_row, me, *zip(*group), block_count, result)
     return result
 
 

time: 170 us -> 123 us (0.72)
  blocking collectives: 70 us -> 0 us
  waiting for transfers between devices: 61.3 us -> 74.5 us
  starting transfers between devices: 13.8 us -> 23.2 us
    all_gather x1 -> x0, blocking collectives: 70 us -> none  [paired_body(): norms = lax.all_gather(norm, ('dp', 'mp'), axis=0, tiled=True)]
    ppermute x21 -> x28, waiting for transfers between devices: 61.3 us -> 72 us  [over(): return lax.ppermute(value, 'dp', pairs)]
    ppermute x21 -> x28, starting transfers between devices: 13.8 us -> 18.6 us  [over(): return lax.ppermute(value, 'dp', pairs)]
    ppermute x0 -> x3, starting transfers between devices: none -> 4.61 us  [paired_body(): norms.append(lax.ppermute(norm, 'mp', pairs))]
    ppermute x0 -> x3, waiting for transfers between devices: none -> 2.56 us  [paired_body(): norms.append(lax.ppermute(norm, 'mp', pairs))]
    pallas_call x13 -> x15, Pallas kernels: 17.6 us -> 17.4 us  [local_call(): pl.pallas_call(kernel, in_specs=[pl.BlockSpec(memory_space=pltpu.SMEM)] *...]
  transfers between devices with their start and end apart: 21 -> 31, of which waited for: 11 -> 18; matrix products, arithmetic and copies ran while one was open for 0% -> 0% of each run, Pallas kernels for 5% -> 7%
where the time goes in v6:
time: 123 us
  waiting for transfers between devices  74.5 us (61%)
  starting transfers between devices  23.2 us (19%)
  Pallas kernels  22 us (18%)
  local copies, waits for them, and re-layouts  2.56 us (2%)
    ppermute x28, waiting for transfers between devices, over(): return lax.ppermute(value, 'dp', pairs)  72 us
    ppermute x28, starting transfers between devices, over(): return lax.ppermute(value, 'dp', pairs)  18.6 us
    pallas_call x15, Pallas kernels, local_call(): pl.pallas_call(kernel, in_specs=[pl.BlockSpec(memory_space=pltpu.SMEM)] *...  17.4 us
    ppermute x3, starting transfers between devices, paired_body(): norms.append(lax.ppermute(norm, 'mp', pairs))  4.61 us
    pallas_call x2, Pallas kernels, assemble_call(): pl.pallas_call(kernel, in_specs=in_specs, out_specs=pl.BlockSpec(memory_s...  4.54 us
    unnamed x10, local copies, waits for them, and re-layouts  2.56 us
    ppermute x3, waiting for transfers between devices, paired_body(): norms.append(lax.ppermute(norm, 'mp', pairs))  2.56 us
  transfers between devices with their start and end apart: 31, of which 18 were waited for; matrix products, arithmetic and copies ran while one was open for 0% of the time, Pallas kernels for 7%

profile of v6, /device:TPU:0, one launch (start us, length us, event | category | flops | bytes accessed | tf_op | source)
XLA Modules:
  0.0 122.5 jit_solution(6620877359398529653)
XLA Ops:
  0.0 1.9 %copy-done = bf16[1,512,3072]{2,1,0:T(8,128)(2,1)S(1)} copy-done((bf16[1,512,3072]{2,1,0:T(8,128)(2,1)S(1)}, bf16[1,512,3072]{2,1,0:T(8,128)(2,1)}, u32[]{:S(2)}) %copy-start) | copy-done | bytes 3145752
  3.8 1.5 %collective-permute-done.refs_0_ = f32[256,512]{1,0:T(8,128)S(1)} collective-permute-done((f32[256,512]{1,0:T(8,128)S(1)}, f32[256,512]{1,0:T(8,128)S(1)}, u32[]{:S(2)}, u32[]{:S(2)}) %collective-permute-start) | collective-permute-done | bytes 524320 | tf_op jit(solution)/shard_map/core_diagonal/ppermute | solution.py:295
  7.6 2.6 %collective-permute-start.4 = (f32[256,512]{1,0:T(8,128)S(1)}, f32[256,512]{1,0:T(8,128)S(1)}, u32[]{:S(2)}, u32[]{:S(2)}) collective-permute-start(f32[256,512]{1,0:T(8,128)S(1)} %add.6), channel_id=1, source_target_pairs={{0,8},{4,20},{8,0},{12,28},{16,24},{20,4},{24,16},{28,12},{1,9},{5... | collective-permute-start | bytes 1572872 | tf_op jit(solution)/shard_map/link_diagonal/ppermute | solution.py:295
  10.3 7.2 %collective-permute-done.4 = f32[256,512]{1,0:T(8,128)S(1)} collective-permute-done((f32[256,512]{1,0:T(8,128)S(1)}, f32[256,512]{1,0:T(8,128)S(1)}, u32[]{:S(2)}, u32[]{:S(2)}) %collective-permute-start.4) | collective-permute-done | bytes 524320 | tf_op jit(solution)/shard_map/link_diagonal/ppermute | solution.py:295
  18.1 2.1 %collective-permute-start.5 = (f32[512,512]{1,0:T(8,128)S(1)}, f32[512,512]{1,0:T(8,128)S(1)}, u32[]{:S(2)}, u32[]{:S(2)}) collective-permute-start(f32[512,512]{1,0:T(8,128)S(1)} %add.8), channel_id=1, source_target_pairs={{0,8},{4,20},{8,0},{12,28},{16,24},{20,4},{24,16},{28,12},{1,9},{5... | collective-permute-start | bytes 3145736 | tf_op jit(solution)/shard_map/link_cross/ppermute | solution.py:295
  21.7 1.0 collective-permute-start.8
  22.7 10.3 %collective-permute-done.5 = f32[512,512]{1,0:T(8,128)S(1)} collective-permute-done((f32[512,512]{1,0:T(8,128)S(1)}, f32[512,512]{1,0:T(8,128)S(1)}, u32[]{:S(2)}, u32[]{:S(2)}) %collective-permute-start.5) | collective-permute-done | bytes 1048608 | tf_op jit(solution)/shard_map/link_cross/ppermute | solution.py:295
  32.9 5.6 %collective-permute-done.10 = f32[256,512]{1,0:T(8,128)S(1)} collective-permute-done((f32[256,512]{1,0:T(8,128)S(1)}, f32[256,512]{1,0:T(8,128)S(1)}, u32[]{:S(2)}, u32[]{:S(2)}) %collective-permute-start.10) | collective-permute-done | bytes 524320 | tf_op jit(solution)/shard_map/link_diagonal/ppermute | solution.py:295
  39.2 2.1 %collective-permute-start.9 = (f32[256,512]{1,0:T(8,128)S(1)}, f32[256,512]{1,0:T(8,128)S(1)}, u32[]{:S(2)}, u32[]{:S(2)}) collective-permute-start(f32[256,512]{1,0:T(8,128)S(1)} %add.10), channel_id=1, source_target_pairs={{0,8},{4,20},{8,0},{12,28},{16,24},{20,4},{24,16},{28,12},{1,9},{5... | collective-permute-start | bytes 1572872 | tf_op jit(solution)/shard_map/link_straight/ppermute | solution.py:295
  41.9 1.3 %collective-permute-start.12 = (f32[256,512]{1,0:T(8,128)S(1)}, f32[256,512]{1,0:T(8,128)S(1)}, u32[]{:S(2)}, u32[]{:S(2)}) collective-permute-start(f32[256,512]{1,0:T(8,128)S(1)} %add.11), channel_id=1, source_target_pairs={{0,8},{4,20},{8,0},{12,28},{16,24},{20,4},{24,16},{28,12},{1,9},{5... | collective-permute-start | bytes 1572872 | tf_op jit(solution)/shard_map/link_straight/ppermute | solution.py:295
  43.9 4.5 %collective-permute-done.9.arrival_ref = f32[256,512]{1,0:T(8,128)S(1)} collective-permute-done((f32[256,512]{1,0:T(8,128)S(1)}, f32[256,512]{1,0:T(8,128)S(1)}, u32[]{:S(2)}, u32[]{:S(2)}) %collective-permute-start.9) | collective-permute-done | bytes 524320 | tf_op jit(solution)/shard_map/link_straight/ppermute | solution.py:295
  48.4 0.9 join.2
  49.3 4.8 %collective-permute-done.12.arrival_ref = f32[256,512]{1,0:T(8,128)S(1)} collective-permute-done((f32[256,512]{1,0:T(8,128)S(1)}, f32[256,512]{1,0:T(8,128)S(1)}, u32[]{:S(2)}, u32[]{:S(2)}) %collective-permute-start.12) | collective-permute-done | bytes 524320 | tf_op jit(solution)/shard_map/link_straight/ppermute | solution.py:295
  54.1 0.9 join.3
  55.0 1.2 collective-permute-done.13.refs_1_
  56.2 3.0 %collective-permute-start.16 = (f32[8,128]{1,0:T(8,128)S(1)}, f32[8,128]{1,0:T(8,128)S(1)}, u32[]{:S(2)}, u32[]{:S(2)}) collective-permute-start(f32[8,128]{1,0:T(8,128)S(1)} %sum.2.refs_0_), channel_id=1, source_target_pairs={{0,24},{4,28},{8,16},{12,20},{16,8},{20,12},{24,0},{28,4},{1,25},{... | collective-permute-start | bytes 12296 | tf_op jit(solution)/shard_map/chip_norm/ppermute | solution.py:295
  59.7 1.0 collective-permute-done.16.refs_3_
  60.7 2.0 %collective-permute-done.15.refs_2_ = f32[8,128]{1,0:T(8,128)S(1)} collective-permute-done((f32[8,128]{1,0:T(8,128)S(1)}, f32[8,128]{1,0:T(8,128)S(1)}, u32[]{:S(2)}, u32[]{:S(2)}) %collective-permute-start.15) | collective-permute-done | bytes 4128 | tf_op jit(solution)/shard_map/chip_norm/ppermute | solution.py:295
  63.3 3.6 %collective-permute-start.19 = (f32[8,128]{1,0:T(8,128)S(1)}, f32[8,128]{1,0:T(8,128)S(1)}, u32[]{:S(2)}, u32[]{:S(2)}) collective-permute-start(f32[8,128]{1,0:T(8,128)S(1)} %sum.3.refs_0_), channel_id=1, source_target_pairs={{0,3},{1,0},{2,1},{3,2},{4,7},{5,4},{6,5},{7,6},{8,11},{9,8},{10,9... | collective-permute-start | bytes 12296 | tf_op jit(solution)/shard_map/group_norm/ppermute | solution.py:334
  66.9 1.0 collective-permute-start.17
  67.9 1.8 %gram.1 = (f32[512,512]{1,0:T(8,128)S(1)}, f32[512,512]{1,0:T(8,128)S(1)}) custom-call(f32[256,512]{1,0:T(8,128)S(1)} %get-tuple-element.31.upper_ref, f32[256,512]{1,0:T(8,128)S(1)} %get-tuple-element.33.lower_ref), custom_call_target="tpu_custom_call" | custom-call | flops 1610612736 | bytes 3145728 | tf_op jit(solution)/shard_map/gram/pallas_call | solution.py:96
  69.7 1.7 %collective-permute-done.18.refs_2_ = f32[8,128]{1,0:T(8,128)S(1)} collective-permute-done((f32[8,128]{1,0:T(8,128)S(1)}, f32[8,128]{1,0:T(8,128)S(1)}, u32[]{:S(2)}, u32[]{:S(2)}) %collective-permute-start.18) | collective-permute-done | bytes 4128 | tf_op jit(solution)/shard_map/group_norm/ppermute | solution.py:334
  71.4 0.9 collective-permute-done.17.refs_1_
  72.3 8.2 %update.1 = (f32[512,512]{1,0:T(8,128)S(1)}, f32[256,512]{1,0:T(8,128)S(1)}, f32[256,512]{1,0:T(8,128)S(1)}) custom-call(f32[256,512]{1,0:T(8,128)S(1)} %get-tuple-element.31.upper_ref, f32[256,512]{1,0:T(8,128)S(1)} %get-tuple-element.33.lower_ref, f32[512,512]{1,0:T(8,128)S(1)} %get-tuple-element.34.left_gram_ref, ...), custom_call_target="tpu_custom_call" | custom-call | flops 6442450944 | bytes 7356416 | tf_op jit(solution)/shard_map/update/pallas_call | solution.py:96
  81.2 1.5 %collective-permute-start.24 = (f32[256,512]{1,0:T(8,128)S(1)}, f32[256,512]{1,0:T(8,128)S(1)}, u32[]{:S(2)}, u32[]{:S(2)}) collective-permute-start(f32[256,512]{1,0:T(8,128)S(1)} %get-tuple-element.40), channel_id=1, source_target_pairs={{0,8},{4,20},{8,0},{12,28},{16,24},{20,4},{24,16},{28,12},{1,9},{5... | collective-permute-start | bytes 1572872 | tf_op jit(solution)/shard_map/link_own/ppermute | solution.py:295
  82.7 7.2 %collective-permute-done.20.refs_2_ = f32[256,512]{1,0:T(8,128)S(1)} collective-permute-done((f32[256,512]{1,0:T(8,128)S(1)}, f32[256,512]{1,0:T(8,128)S(1)}, u32[]{:S(2)}, u32[]{:S(2)}) %collective-permute-start.20) | collective-permute-done | bytes 524320 | tf_op jit(solution)/shard_map/link_own/ppermute | solution.py:295
  90.7 4.8 %collective-permute-done.24.refs_3_ = f32[256,512]{1,0:T(8,128)S(1)} collective-permute-done((f32[256,512]{1,0:T(8,128)S(1)}, f32[256,512]{1,0:T(8,128)S(1)}, u32[]{:S(2)}, u32[]{:S(2)}) %collective-permute-start.24) | collective-permute-done | bytes 524320 | tf_op jit(solution)/shard_map/link_own/ppermute | solution.py:295
  96.0 10.7 %collective-permute-done.29.refs_6_ = f32[512,512]{1,0:T(8,128)S(1)} collective-permute-done((f32[512,512]{1,0:T(8,128)S(1)}, f32[512,512]{1,0:T(8,128)S(1)}, u32[]{:S(2)}, u32[]{:S(2)}) %collective-permute-start.29) | collective-permute-done | bytes 1048608 | tf_op jit(solution)/shard_map/link_sibling/ppermute | solution.py:295
  107.2 5.1 %collective-permute-done.23.refs_0_ = f32[256,512]{1,0:T(8,128)S(1)} collective-permute-done((f32[256,512]{1,0:T(8,128)S(1)}, f32[256,512]{1,0:T(8,128)S(1)}, u32[]{:S(2)}, u32[]{:S(2)}) %collective-permute-start.23) | collective-permute-done | bytes 524320 | tf_op jit(solution)/shard_map/link_relayed/ppermute | solution.py:295
  112.3 5.6 %collective-permute-done.26.refs_1_ = f32[256,512]{1,0:T(8,128)S(1)} collective-permute-done((f32[256,512]{1,0:T(8,128)S(1)}, f32[256,512]{1,0:T(8,128)S(1)}, u32[]{:S(2)}, u32[]{:S(2)}) %collective-permute-start.26) | collective-permute-done | bytes 524320 | tf_op jit(solution)/shard_map/link_relayed/ppermute | solution.py:295
  117.9 2.6 %assemble.2.refs_4_ = f32[512,3072]{1,0:T(8,128)} custom-call(s32[6]{0:T(128)S(1)} %bitcast.25, s32[1]{0:T(128)} %bitcast.1.me_ref, f32[512,512]{1,0:T(8,128)S(1)} %get-tuple-element.38.refs_0_, f32[512,512]{1,0:T(8,128)S(1)} %collective-permute-done.21.refs_1_, f32[256,512]{1,0:T(8,128)S(1)} %collective-permute-done.20.refs_2_, ...), custom_call_target="tpu_custom_call" | custom-call | bytes 16777216 | tf_op jit(solution)/shard_map/assemble/pallas_call | solution.py:266
  120.6 1.9 %assemble.3 = f32[512,3072]{1,0:T(8,128)} custom-call(s32[6]{0:T(128)S(1)} %bitcast.26, s32[1]{0:T(128)} %bitcast.1.me_ref, f32[256,512]{1,0:T(8,128)S(1)} %collective-permute-done.23.refs_0_, f32[256,512]{1,0:T(8,128)S(1)} %collective-permute-done.26.refs_1_, f32[256,512]{1,0:T(8,128)S(1)} %collective-permute-done.27.refs_2_, ...), custom_call_target="tpu_custom_call", output_to_operand_aliasing={{}: (6, {})} | custom-call | bytes 4194304 | tf_op jit(solution)/shard_map/assemble/pallas_call | solution.py:266
  (57 shorter events, 12.1 us)
Async XLA Ops:
  3.2 2.1 %collective-permute-start = (f32[256,512]{1,0:T(8,128)S(1)}, f32[256,512]{1,0:T(8,128)S(1)}, u32[]{:S(2)}, u32[]{:S(2)}) collective-permute-start(f32[256,512]{1,0:T(8,128)S(1)} %get-tuple-element.24), channel_id=1, source_target_pairs={{0,4},{4,0},{8,12},{12,8},{16,20},{20,16},{24,28},{28,24},{1,5},{5... | collective-permute-start | bytes 1572872 | tf_op jit(solution)/shard_map/core_diagonal/ppermute | solution.py:295
  3.7 2.3 %collective-permute-start.1 = (f32[256,512]{1,0:T(8,128)S(1)}, f32[256,512]{1,0:T(8,128)S(1)}, u32[]{:S(2)}, u32[]{:S(2)}) collective-permute-start(f32[256,512]{1,0:T(8,128)S(1)} %get-tuple-element.25), channel_id=1, source_target_pairs={{0,4},{4,0},{8,12},{12,8},{16,20},{20,16},{24,28},{28,24},{1,5},{5... | collective-permute-start | bytes 1572872 | tf_op jit(solution)/shard_map/core_diagonal/ppermute | solution.py:295
  7.2 10.2 %collective-permute-start.2 = (f32[512,512]{1,0:T(8,128)S(1)}, f32[512,512]{1,0:T(8,128)S(1)}, u32[]{:S(2)}, u32[]{:S(2)}) collective-permute-start(f32[512,512]{1,0:T(8,128)S(1)} %pack.4), channel_id=1, source_target_pairs={{0,4},{4,0},{8,12},{12,8},{16,20},{20,16},{24,28},{28,24},{1,5},{5... | collective-permute-start | bytes 3145736 | tf_op jit(solution)/shard_map/core_cross/ppermute | solution.py:295
  7.6 9.8 %collective-permute-start.4 = (f32[256,512]{1,0:T(8,128)S(1)}, f32[256,512]{1,0:T(8,128)S(1)}, u32[]{:S(2)}, u32[]{:S(2)}) collective-permute-start(f32[256,512]{1,0:T(8,128)S(1)} %add.6), channel_id=1, source_target_pairs={{0,8},{4,20},{8,0},{12,28},{16,24},{20,4},{24,16},{28,12},{1,9},{5... | collective-permute-start | bytes 1572872 | tf_op jit(solution)/shard_map/link_diagonal/ppermute | solution.py:295
  18.1 14.9 %collective-permute-start.5 = (f32[512,512]{1,0:T(8,128)S(1)}, f32[512,512]{1,0:T(8,128)S(1)}, u32[]{:S(2)}, u32[]{:S(2)}) collective-permute-start(f32[512,512]{1,0:T(8,128)S(1)} %add.8), channel_id=1, source_target_pairs={{0,8},{4,20},{8,0},{12,28},{16,24},{20,4},{24,16},{28,12},{1,9},{5... | collective-permute-start | bytes 3145736 | tf_op jit(solution)/shard_map/link_cross/ppermute | solution.py:295
  20.9 17.7 %collective-permute-start.7 = (f32[512,512]{1,0:T(8,128)S(1)}, f32[512,512]{1,0:T(8,128)S(1)}, u32[]{:S(2)}, u32[]{:S(2)}) collective-permute-start(f32[512,512]{1,0:T(8,128)S(1)} %get-tuple-element.30), channel_id=1, source_target_pairs={{0,4},{4,0},{8,12},{12,8},{16,20},{20,16},{24,28},{28,24},{1,5},{5... | collective-permute-start | bytes 3145736 | tf_op jit(solution)/shard_map/core_straight/ppermute | solution.py:295
  20.9 17.6 %collective-permute-start.10 = (f32[256,512]{1,0:T(8,128)S(1)}, f32[256,512]{1,0:T(8,128)S(1)}, u32[]{:S(2)}, u32[]{:S(2)}) collective-permute-start(f32[256,512]{1,0:T(8,128)S(1)} %add.7), channel_id=1, source_target_pairs={{0,8},{4,20},{8,0},{12,28},{16,24},{20,4},{24,16},{28,12},{1,9},{5... | collective-permute-start | bytes 1572872 | tf_op jit(solution)/shard_map/link_diagonal/ppermute | solution.py:295
  21.7 16.9 %collective-permute-start.8 = (f32[256,512]{1,0:T(8,128)S(1)}, f32[256,512]{1,0:T(8,128)S(1)}, u32[]{:S(2)}, u32[]{:S(2)}) collective-permute-start(f32[256,512]{1,0:T(8,128)S(1)} %collective-permute-done.4), channel_id=1, source_target_pairs={{0,4},{4,0},{8,12},{12,8},{16,20},{20,16},{24,28},{28,24},{1,5},{5... | collective-permute-start | bytes 1572872 | tf_op jit(solution)/shard_map/core_handed/ppermute | solution.py:295
  22.7 20.5 %collective-permute-start.3 = (f32[512,512]{1,0:T(8,128)S(1)}, f32[512,512]{1,0:T(8,128)S(1)}, u32[]{:S(2)}, u32[]{:S(2)}) collective-permute-start(f32[512,512]{1,0:T(8,128)S(1)} %get-tuple-element.28), channel_id=1, source_target_pairs={{0,4},{4,0},{8,12},{12,8},{16,20},{20,16},{24,28},{28,24},{1,5},{5... | collective-permute-start | bytes 3145736 | tf_op jit(solution)/shard_map/core_self/ppermute | solution.py:295
  32.9 10.3 %collective-permute-start.6 = (f32[512,512]{1,0:T(8,128)S(1)}, f32[512,512]{1,0:T(8,128)S(1)}, u32[]{:S(2)}, u32[]{:S(2)}) collective-permute-start(f32[512,512]{1,0:T(8,128)S(1)} %collective-permute-done.5), channel_id=1, source_target_pairs={{0,4},{4,0},{8,12},{12,8},{16,20},{20,16},{24,28},{28,24},{1,5},{5... | collective-permute-start | bytes 3145736 | tf_op jit(solution)/shard_map/core_handed_cross/ppermute | solution.py:295
  38.6 2.7 %collective-permute-start.11 = (f32[256,512]{1,0:T(8,128)S(1)}, f32[256,512]{1,0:T(8,128)S(1)}, u32[]{:S(2)}, u32[]{:S(2)}) collective-permute-start(f32[256,512]{1,0:T(8,128)S(1)} %collective-permute-done.10), channel_id=1, source_target_pairs={{0,4},{4,0},{8,12},{12,8},{16,20},{20,16},{24,28},{28,24},{1,5},{5... | collective-permute-start | bytes 1572872 | tf_op jit(solution)/shard_map/core_handed/ppermute | solution.py:295
  39.2 9.3 %collective-permute-start.9 = (f32[256,512]{1,0:T(8,128)S(1)}, f32[256,512]{1,0:T(8,128)S(1)}, u32[]{:S(2)}, u32[]{:S(2)}) collective-permute-start(f32[256,512]{1,0:T(8,128)S(1)} %add.10), channel_id=1, source_target_pairs={{0,8},{4,20},{8,0},{12,28},{16,24},{20,4},{24,16},{28,12},{1,9},{5... | collective-permute-start | bytes 1572872 | tf_op jit(solution)/shard_map/link_straight/ppermute | solution.py:295
  41.9 12.1 %collective-permute-start.12 = (f32[256,512]{1,0:T(8,128)S(1)}, f32[256,512]{1,0:T(8,128)S(1)}, u32[]{:S(2)}, u32[]{:S(2)}) collective-permute-start(f32[256,512]{1,0:T(8,128)S(1)} %add.11), channel_id=1, source_target_pairs={{0,8},{4,20},{8,0},{12,28},{16,24},{20,4},{24,16},{28,12},{1,9},{5... | collective-permute-start | bytes 1572872 | tf_op jit(solution)/shard_map/link_straight/ppermute | solution.py:295
  54.9 1.2 %collective-permute-start.13 = (f32[8,128]{1,0:T(8,128)S(1)}, f32[8,128]{1,0:T(8,128)S(1)}, u32[]{:S(2)}, u32[]{:S(2)}) collective-permute-start(f32[8,128]{1,0:T(8,128)S(1)} %get-tuple-element.36.refs_0_), channel_id=1, source_target_pairs={{0,4},{4,0},{8,12},{12,8},{16,20},{20,16},{24,28},{28,24},{1,5},{5... | collective-permute-start | bytes 12296 | tf_op jit(solution)/shard_map/core_norm/ppermute | solution.py:295
  56.2 4.6 %collective-permute-start.16 = (f32[8,128]{1,0:T(8,128)S(1)}, f32[8,128]{1,0:T(8,128)S(1)}, u32[]{:S(2)}, u32[]{:S(2)}) collective-permute-start(f32[8,128]{1,0:T(8,128)S(1)} %sum.2.refs_0_), channel_id=1, source_target_pairs={{0,24},{4,28},{8,16},{12,20},{16,8},{20,12},{24,0},{28,4},{1,25},{... | collective-permute-start | bytes 12296 | tf_op jit(solution)/shard_map/chip_norm/ppermute | solution.py:295
  59.1 3.6 %collective-permute-start.15 = (f32[8,128]{1,0:T(8,128)S(1)}, f32[8,128]{1,0:T(8,128)S(1)}, u32[]{:S(2)}, u32[]{:S(2)}) collective-permute-start(f32[8,128]{1,0:T(8,128)S(1)} %sum.2.refs_0_), channel_id=1, source_target_pairs={{0,16},{4,20},{8,24},{12,28},{16,0},{20,4},{24,8},{28,12},{1,17},{... | collective-permute-start | bytes 12296 | tf_op jit(solution)/shard_map/chip_norm/ppermute | solution.py:295
  59.6 3.6 %collective-permute-start.14 = (f32[8,128]{1,0:T(8,128)S(1)}, f32[8,128]{1,0:T(8,128)S(1)}, u32[]{:S(2)}, u32[]{:S(2)}) collective-permute-start(f32[8,128]{1,0:T(8,128)S(1)} %sum.2.refs_0_), channel_id=1, source_target_pairs={{0,8},{4,12},{8,0},{12,4},{16,24},{20,28},{24,16},{28,20},{1,9},{5... | collective-permute-start | bytes 12296 | tf_op jit(solution)/shard_map/chip_norm/ppermute | solution.py:295
  63.3 6.4 %collective-permute-start.19 = (f32[8,128]{1,0:T(8,128)S(1)}, f32[8,128]{1,0:T(8,128)S(1)}, u32[]{:S(2)}, u32[]{:S(2)}) collective-permute-start(f32[8,128]{1,0:T(8,128)S(1)} %sum.3.refs_0_), channel_id=1, source_target_pairs={{0,3},{1,0},{2,1},{3,2},{4,7},{5,4},{6,5},{7,6},{8,11},{9,8},{10,9... | collective-permute-start | bytes 12296 | tf_op jit(solution)/shard_map/group_norm/ppermute | solution.py:334
  66.9 4.5 %collective-permute-start.18 = (f32[8,128]{1,0:T(8,128)S(1)}, f32[8,128]{1,0:T(8,128)S(1)}, u32[]{:S(2)}, u32[]{:S(2)}) collective-permute-start(f32[8,128]{1,0:T(8,128)S(1)} %sum.3.refs_0_), channel_id=1, source_target_pairs={{0,2},{1,3},{2,0},{3,1},{4,6},{5,7},{6,4},{7,5},{8,10},{9,11},{10,... | collective-permute-start | bytes 12296 | tf_op jit(solution)/shard_map/group_norm/ppermute | solution.py:334
  66.9 5.4 %collective-permute-start.17 = (f32[8,128]{1,0:T(8,128)S(1)}, f32[8,128]{1,0:T(8,128)S(1)}, u32[]{:S(2)}, u32[]{:S(2)}) collective-permute-start(f32[8,128]{1,0:T(8,128)S(1)} %sum.3.refs_0_), channel_id=1, source_target_pairs={{0,1},{1,2},{2,3},{3,0},{4,5},{5,6},{6,7},{7,4},{8,9},{9,10},{10,1... | collective-permute-start | bytes 12296 | tf_op jit(solution)/shard_map/group_norm/ppermute | solution.py:334
  72.3 45.7 %copy-start.2 = (s32[1,6]{1,0:T(1,128)S(1)}, s32[1,6]{1,0:T(1,128)}, u32[]{:S(2)}) copy-start(s32[1,6]{1,0:T(1,128)} %param.5) | copy-start | bytes 76
  80.5 9.3 %collective-permute-start.21 = (f32[512,512]{1,0:T(8,128)S(1)}, f32[512,512]{1,0:T(8,128)S(1)}, u32[]{:S(2)}, u32[]{:S(2)}) collective-permute-start(f32[512,512]{1,0:T(8,128)S(1)} %get-tuple-element.38.refs_0_), channel_id=1, source_target_pairs={{0,4},{4,0},{8,12},{12,8},{16,20},{20,16},{24,28},{28,24},{1,5},{5... | collective-permute-start | bytes 3145736 | tf_op jit(solution)/shard_map/core_own/ppermute | solution.py:295
  80.6 9.2 %collective-permute-start.20 = (f32[256,512]{1,0:T(8,128)S(1)}, f32[256,512]{1,0:T(8,128)S(1)}, u32[]{:S(2)}, u32[]{:S(2)}) collective-permute-start(f32[256,512]{1,0:T(8,128)S(1)} %get-tuple-element.37), channel_id=1, source_target_pairs={{0,8},{4,20},{8,0},{12,28},{16,24},{20,4},{24,16},{28,12},{1,9},{5... | collective-permute-start | bytes 1572872 | tf_op jit(solution)/shard_map/link_own/ppermute | solution.py:295
  81.2 14.3 %collective-permute-start.24 = (f32[256,512]{1,0:T(8,128)S(1)}, f32[256,512]{1,0:T(8,128)S(1)}, u32[]{:S(2)}, u32[]{:S(2)}) collective-permute-start(f32[256,512]{1,0:T(8,128)S(1)} %get-tuple-element.40), channel_id=1, source_target_pairs={{0,8},{4,20},{8,0},{12,28},{16,24},{20,4},{24,16},{28,12},{1,9},{5... | collective-permute-start | bytes 1572872 | tf_op jit(solution)/shard_map/link_own/ppermute | solution.py:295
  89.8 16.8 %collective-permute-start.29 = (f32[512,512]{1,0:T(8,128)S(1)}, f32[512,512]{1,0:T(8,128)S(1)}, u32[]{:S(2)}, u32[]{:S(2)}) collective-permute-start(f32[512,512]{1,0:T(8,128)S(1)} %collective-permute-done.21.refs_1_), channel_id=1, source_target_pairs={{0,8},{4,20},{8,0},{12,28},{16,24},{20,4},{24,16},{28,12},{1,9},{5... | collective-permute-start | bytes 3145736 | tf_op jit(solution)/shard_map/link_sibling/ppermute | solution.py:295
  90.4 5.1 %collective-permute-start.22 = (f32[256,512]{1,0:T(8,128)S(1)}, f32[256,512]{1,0:T(8,128)S(1)}, u32[]{:S(2)}, u32[]{:S(2)}) collective-permute-start(f32[256,512]{1,0:T(8,128)S(1)} %collective-permute-done.20.refs_2_), channel_id=1, source_target_pairs={{0,4},{4,0},{8,12},{12,8},{16,20},{20,16},{24,28},{28,24},{1,5},{5... | collective-permute-start | bytes 1572872 | tf_op jit(solution)/shard_map/core_first/ppermute | solution.py:295
  95.5 11.2 %collective-permute-start.25 = (f32[256,512]{1,0:T(8,128)S(1)}, f32[256,512]{1,0:T(8,128)S(1)}, u32[]{:S(2)}, u32[]{:S(2)}) collective-permute-start(f32[256,512]{1,0:T(8,128)S(1)} %collective-permute-done.24.refs_3_), channel_id=1, source_target_pairs={{0,4},{4,0},{8,12},{12,8},{16,20},{20,16},{24,28},{28,24},{1,5},{5... | collective-permute-start | bytes 1572872 | tf_op jit(solution)/shard_map/core_first/ppermute | solution.py:295
  95.5 16.8 %collective-permute-start.23 = (f32[256,512]{1,0:T(8,128)S(1)}, f32[256,512]{1,0:T(8,128)S(1)}, u32[]{:S(2)}, u32[]{:S(2)}) collective-permute-start(f32[256,512]{1,0:T(8,128)S(1)} %collective-permute-done.22.refs_4_), channel_id=1, source_target_pairs={{0,8},{4,20},{8,0},{12,28},{16,24},{20,4},{24,16},{28,12},{1,9},{5... | collective-permute-start | bytes 1572872 | tf_op jit(solution)/shard_map/link_relayed/ppermute | solution.py:295
  106.7 11.2 %collective-permute-start.30 = (f32[512,512]{1,0:T(8,128)S(1)}, f32[512,512]{1,0:T(8,128)S(1)}, u32[]{:S(2)}, u32[]{:S(2)}) collective-permute-start(f32[512,512]{1,0:T(8,128)S(1)} %collective-permute-done.29.refs_6_), channel_id=1, source_target_pairs={{0,4},{4,0},{8,12},{12,8},{16,20},{20,16},{24,28},{28,24},{1,5},{5... | collective-permute-start | bytes 3145736 | tf_op jit(solution)/shard_map/core_second/ppermute | solution.py:295
  106.7 11.2 %collective-permute-start.26 = (f32[256,512]{1,0:T(8,128)S(1)}, f32[256,512]{1,0:T(8,128)S(1)}, u32[]{:S(2)}, u32[]{:S(2)}) collective-permute-start(f32[256,512]{1,0:T(8,128)S(1)} %collective-permute-done.25.refs_5_), channel_id=1, source_target_pairs={{0,8},{4,20},{8,0},{12,28},{16,24},{20,4},{24,16},{28,12},{1,9},{5... | collective-permute-start | bytes 1572872 | tf_op jit(solution)/shard_map/link_relayed/ppermute | solution.py:295
  112.3 8.3 %collective-permute-start.27 = (f32[256,512]{1,0:T(8,128)S(1)}, f32[256,512]{1,0:T(8,128)S(1)}, u32[]{:S(2)}, u32[]{:S(2)}) collective-permute-start(f32[256,512]{1,0:T(8,128)S(1)} %collective-permute-done.23.refs_0_), channel_id=1, source_target_pairs={{0,4},{4,0},{8,12},{12,8},{16,20},{20,16},{24,28},{28,24},{1,5},{5... | collective-permute-start | bytes 1572872 | tf_op jit(solution)/shard_map/core_relayed/ppermute | solution.py:295
  117.9 2.7 %collective-permute-start.28 = (f32[256,512]{1,0:T(8,128)S(1)}, f32[256,512]{1,0:T(8,128)S(1)}, u32[]{:S(2)}, u32[]{:S(2)}) collective-permute-start(f32[256,512]{1,0:T(8,128)S(1)} %collective-permute-done.26.refs_1_), channel_id=1, source_target_pairs={{0,4},{4,0},{8,12},{12,8},{16,20},{20,16},{24,28},{28,24},{1,5},{5... | collective-permute-start | bytes 1572872 | tf_op jit(solution)/shard_map/core_relayed/ppermute | solution.py:295
  (4 other events, 63.3 us)

commit v7 on v6

--- a/solution.py
+++ b/solution.py
@@ -86,7 +86,8 @@
 
 def piece_target(kind, device):
     along = 2 + 2 * (device & 1)
-    return {"self": device, "straight": device ^ along, "cross": device ^ along ^ 1, "diagonal": device ^ 7}[kind]
+    flips = {"self": 0, "straight": along, "side": 6 - along, "corner": 6, "cross": along ^ 1, "diagonal": 7}
+    return device ^ flips[kind]
 
 
 def local_call(kernel, name, out_shape, operands, scalars=(), flops=0, vmem=None, **options):
@@ -136,14 +137,26 @@
 
 
 def add_call(owners, me, grads, kind, half, arrivals, width):
+    flat = [value for arrival in arrivals for value in (arrival if isinstance(arrival, list) else [arrival])]
+
     def kernel(owners_ref, me_ref, grad_ref, *refs):
         target = piece_target(kind, me_ref[0])
-        total = owner_block(owners_ref, grad_ref, rows_of(half, width), width, target)
-        for ref in refs[:-1]:
-            total = total + piece_of(ref, half, width)
-        refs[-1][...] = total
-
-    return local_call(kernel, "add", piece_shape(half, width), (grads, *arrivals), (owners, me))
+        for part in HALVES if half is None else (half,):
+            total = owner_block(owners_ref, grad_ref, rows_of(part, width), width, target)
+            place = 0
+            for arrival in arrivals:
+                if isinstance(arrival, list):
+                    total = total + refs[place + part][...]
+                    place += 2
+                else:
+                    total = total + piece_of(refs[place], part, width)
+                    place += 1
+            if half is None:
+                refs[-1][rows_of(part, width), :] = total
+            else:
+                refs[-1][...] = total
+
+    return local_call(kernel, "add", piece_shape(half, width), (grads, *flat), (owners, me))
 
 
 def join_call(owners, me, total, half, arrival, norm, block_count):
@@ -300,30 +313,37 @@
     def to_link(value, label):
         return over([(i, i ^ (2 + 2 * (i % 2))) for i in range(8)], value, "link_" + label)
 
+    def to_side(value, label):
+        return over([(i, i ^ (4 - 2 * (i % 2))) for i in range(8)], value, "side_" + label)
+
     def own_plus(kind, half, *arrivals):
         return add_call(owner_row, me, grads, kind, half, arrivals, width)
 
+    def assemble(result, *pieces):
+        return assemble_call(owner_row, me, *zip(*pieces), block_count, result)
+
     def after(value, *others):
         return lax.optimization_barrier((value, *others))[0]
 
-    early = pack_call(owner_row, me, grads, [("diagonal", half) for half in HALVES], width)
-    core_diagonal = [to_core(value, "diagonal") for value in early]
-    sums = [own_plus("diagonal", half, core_diagonal[half]) for half in HALVES]
-    diagonal = [to_link(value, "diagonal") for value in sums]
-    later = pack_call(owner_row, after(me, *sums), grads, [("cross", None)], width)
-    core_cross = to_core(later[0], "cross")
-    cross = to_link(own_plus("cross", None, after(core_cross, diagonal[0])), "cross")
-    later = pack_call(owner_row, after(me, core_cross), grads, [("straight", None), ("self", None)], width)
-    core_straight = to_core(later[0], "straight")
-    core_self = to_core(later[1], "self")
-    handed = [to_core(value, "handed") for value in diagonal]
-    straight = [
-        to_link(own_plus("straight", half, core_straight, handed[half]), "straight") for half in HALVES
+    kinds = ("corner", "straight", "side", "self")
+    pieces = []
+    for pair in (kinds[:2], kinds[2:]):
+        pieces += pack_call(owner_row, me, grads, [(kind, half) for kind in pair for half in HALVES], width)
+    keys = [(kind, half) for kind in kinds for half in HALVES]
+    from_core = {key: to_core(value, key[0]) for key, value in zip(keys, pieces)}
+    from_link = {
+        key: to_link(own_plus(*key, from_core[key]), key[0]) for key in keys if key[0] in kinds[:2]
+    }
+    arrived = [
+        to_side(own_plus("side", half, from_core["side", half], from_link["corner", half]), "side")
+        for half in HALVES
     ]
-    total = own_plus("self", None, core_self, to_core(cross, "handed_cross"))
+    totals = [
+        own_plus("self", half, from_core["self", half], from_link["straight", half]) for half in HALVES
+    ]
     norm, block = None, []
     for half in HALVES:
-        joined, norm = join_call(owner_row, me, total, half, straight[half], norm, block_count)
+        joined, norm = join_call(owner_row, me, totals[half], half, arrived[half], norm, block_count)
         block.append(joined)
     norm = sum_call(norm, to_core(norm, "norm"))
     norm = sum_call(norm, *[over(flipped(mask), norm, "chip_norm") for mask in (2, 4, 6)])
@@ -341,19 +361,14 @@
     second = to_link(after(core_own, first[0]), "sibling")
     core_second = to_core(second, "second")
     relayed = [to_link(value, "relayed") for value in core_first]
-    core_relayed = [to_core(value, "relayed") for value in relayed]
-    groups = [
-        [(("self", 0, None), whole), (("self", 1, None), core_own)]
-        + [(("straight", 0, half), first[half]) for half in HALVES]
-        + [(("straight", 1, half), core_first[half]) for half in HALVES]
-        + [(("cross", 0, None), second), (("cross", 1, None), core_second)],
-        [(("diagonal", 0, half), relayed[half]) for half in HALVES]
-        + [(("diagonal", 1, half), core_relayed[half]) for half in HALVES],
-    ]
-    result = None
-    for group in groups:
-        result = assemble_call(owner_row, me, *zip(*group), block_count, result)
-    return result
+    held = [(("self", 0, None), whole), (("self", 1, None), core_own)]
+    held += [(("straight", 0, half), first[half]) for half in HALVES]
+    held += [(("straight", 1, half), core_first[half]) for half in HALVES]
+    crossed = [(("cross", 0, None), second), (("cross", 1, None), core_second)]
+    result = assemble(None, *held)
+    core_relayed = [to_core(after(relayed[0], result), "relayed"), to_core(relayed[1], "relayed")]
+    result = assemble(result, *crossed, *[(("diagonal", 0, half), relayed[half]) for half in HALVES])
+    return assemble(result, *[(("diagonal", 1, half), core_relayed[half]) for half in HALVES])
 
 
 def solution(mesh):

time: 123 us -> 110 us (0.89)
  waiting for transfers between devices: 74.5 us -> 60.4 us
  Pallas kernels: 22 us -> 23.7 us
    ppermute x28 -> x29, waiting for transfers between devices: 72 us -> 60 us  [over(): return lax.ppermute(value, 'dp', pairs)]
    ppermute x3, waiting for transfers between devices: 2.56 us -> 0.4 us  [paired_body(): norms.append(lax.ppermute(norm, 'mp', pairs))]
    pallas_call x2 -> x3, Pallas kernels: 4.54 us -> 5.71 us  [assemble_call(): pl.pallas_call(kernel, in_specs=in_specs, out_specs=pl.BlockSpec(memory_s...]
    pallas_call x15 -> x16, Pallas kernels: 17.4 us -> 18 us  [local_call(): pl.pallas_call(kernel, in_specs=[pl.BlockSpec(memory_space=pltpu.SMEM)] *...]
    ppermute x28 -> x29, starting transfers between devices: 18.6 us -> 18.2 us  [over(): return lax.ppermute(value, 'dp', pairs)]
  transfers between devices with their start and end apart: 31 -> 32, of which waited for: 18 -> 15; matrix products, arithmetic and copies ran while one was open for 0% -> 0% of each run, Pallas kernels for 7% -> 11%
where the time goes in v7:
time: 110 us; the launch traced here: 111 us
  waiting for transfers between devices  60.4 us (55%)
  Pallas kernels  23.7 us (22%)
  starting transfers between devices  23.7 us (22%)
  local copies, waits for them, and re-layouts  2.56 us (2%)
    ppermute x29, waiting for transfers between devices, over(): return lax.ppermute(value, 'dp', pairs)  60 us
    ppermute x29, starting transfers between devices, over(): return lax.ppermute(value, 'dp', pairs)  18.2 us
    pallas_call x16, Pallas kernels, local_call(): pl.pallas_call(kernel, in_specs=[pl.BlockSpec(memory_space=pltpu.SMEM)] *...  18 us
    pallas_call x3, Pallas kernels, assemble_call(): pl.pallas_call(kernel, in_specs=in_specs, out_specs=pl.BlockSpec(memory_s...  5.71 us
    ppermute x3, starting transfers between devices, paired_body(): norms.append(lax.ppermute(norm, 'mp', pairs))  5.51 us
    unnamed x10, local copies, waits for them, and re-layouts  2.56 us
  transfers between devices with their start and end apart: 32, of which 15 were waited for; matrix products, arithmetic and copies ran while one was open for 0% of the time, Pallas kernels for 11%

profile of v7, /device:TPU:0, one launch (start us, length us, event | category | flops | bytes accessed | tf_op | source)
XLA Modules:
  0.0 110.6 jit_solution(11593609830834925475)
XLA Ops:
  0.0 1.9 %copy-done = bf16[1,512,3072]{2,1,0:T(8,128)(2,1)S(1)} copy-done((bf16[1,512,3072]{2,1,0:T(8,128)(2,1)S(1)}, bf16[1,512,3072]{2,1,0:T(8,128)(2,1)}, u32[]{:S(2)}) %copy-start) | copy-done | bytes 3145752
  4.3 0.7 pack.2
  6.1 2.7 %collective-permute-start.5 = (f32[256,512]{1,0:T(8,128)S(1)}, f32[256,512]{1,0:T(8,128)S(1)}, u32[]{:S(2)}, u32[]{:S(2)}) collective-permute-start(f32[256,512]{1,0:T(8,128)S(1)} %add.10), channel_id=1, source_target_pairs={{0,8},{4,20},{8,0},{12,28},{16,24},{20,4},{24,16},{28,12},{1,9},{5... | collective-permute-start | bytes 1572872 | tf_op jit(solution)/shard_map/link_corner/ppermute | solution.py:308
  9.6 1.6 %collective-permute-start.12 = (f32[256,512]{1,0:T(8,128)S(1)}, f32[256,512]{1,0:T(8,128)S(1)}, u32[]{:S(2)}, u32[]{:S(2)}) collective-permute-start(f32[256,512]{1,0:T(8,128)S(1)} %add.14), channel_id=1, source_target_pairs={{0,8},{4,20},{8,0},{12,28},{16,24},{20,4},{24,16},{28,12},{1,9},{5... | collective-permute-start | bytes 1572872 | tf_op jit(solution)/shard_map/link_corner/ppermute | solution.py:308
  12.9 3.1 %collective-permute-done.5.refs_1_ = f32[256,512]{1,0:T(8,128)S(1)} collective-permute-done((f32[256,512]{1,0:T(8,128)S(1)}, f32[256,512]{1,0:T(8,128)S(1)}, u32[]{:S(2)}, u32[]{:S(2)}) %collective-permute-start.5) | collective-permute-done | bytes 524320 | tf_op jit(solution)/shard_map/link_corner/ppermute | solution.py:308
  16.0 2.0 %collective-permute-start.2 = (f32[256,512]{1,0:T(8,128)S(1)}, f32[256,512]{1,0:T(8,128)S(1)}, u32[]{:S(2)}, u32[]{:S(2)}) collective-permute-start(f32[256,512]{1,0:T(8,128)S(1)} %add.8), channel_id=1, source_target_pairs={{0,8},{4,20},{8,0},{12,28},{16,24},{20,4},{24,16},{28,12},{1,9},{5... | collective-permute-start | bytes 1572872 | tf_op jit(solution)/shard_map/link_straight/ppermute | solution.py:308
  18.7 2.9 %collective-permute-done.12.refs_1_ = f32[256,512]{1,0:T(8,128)S(1)} collective-permute-done((f32[256,512]{1,0:T(8,128)S(1)}, f32[256,512]{1,0:T(8,128)S(1)}, u32[]{:S(2)}, u32[]{:S(2)}) %collective-permute-start.12) | collective-permute-done | bytes 524320 | tf_op jit(solution)/shard_map/link_corner/ppermute | solution.py:308
  21.6 2.0 %collective-permute-start.6 = (f32[256,512]{1,0:T(8,128)S(1)}, f32[256,512]{1,0:T(8,128)S(1)}, u32[]{:S(2)}, u32[]{:S(2)}) collective-permute-start(f32[256,512]{1,0:T(8,128)S(1)} %add.11), channel_id=1, source_target_pairs={{0,16},{4,12},{8,24},{12,4},{16,0},{20,28},{24,8},{28,20},{1,17},{... | collective-permute-start | bytes 1572872 | tf_op jit(solution)/shard_map/side_side/ppermute | solution.py:308
  24.4 6.0 %collective-permute-done.2.refs_1_ = f32[256,512]{1,0:T(8,128)S(1)} collective-permute-done((f32[256,512]{1,0:T(8,128)S(1)}, f32[256,512]{1,0:T(8,128)S(1)}, u32[]{:S(2)}, u32[]{:S(2)}) %collective-permute-start.2) | collective-permute-done | bytes 524320 | tf_op jit(solution)/shard_map/link_straight/ppermute | solution.py:308
  31.0 10.6 %collective-permute-done.9.refs_1_ = f32[256,512]{1,0:T(8,128)S(1)} collective-permute-done((f32[256,512]{1,0:T(8,128)S(1)}, f32[256,512]{1,0:T(8,128)S(1)}, u32[]{:S(2)}, u32[]{:S(2)}) %collective-permute-start.9) | collective-permute-done | bytes 524320 | tf_op jit(solution)/shard_map/link_straight/ppermute | solution.py:308
  42.2 0.9 join.2
  43.1 0.7 collective-permute-done.13.arrival_ref
  43.8 0.9 join.3
  44.8 1.1 collective-permute-done.14.refs_1_
  45.9 1.8 %collective-permute-start.15 = (f32[8,128]{1,0:T(8,128)S(1)}, f32[8,128]{1,0:T(8,128)S(1)}, u32[]{:S(2)}, u32[]{:S(2)}) collective-permute-start(f32[8,128]{1,0:T(8,128)S(1)} %sum.2.refs_0_), channel_id=1, source_target_pairs={{0,8},{4,12},{8,0},{12,4},{16,24},{20,28},{24,16},{28,20},{1,9},{5... | collective-permute-start | bytes 12296 | tf_op jit(solution)/shard_map/chip_norm/ppermute | solution.py:308
  47.7 1.5 %collective-permute-start.16 = (f32[8,128]{1,0:T(8,128)S(1)}, f32[8,128]{1,0:T(8,128)S(1)}, u32[]{:S(2)}, u32[]{:S(2)}) collective-permute-start(f32[8,128]{1,0:T(8,128)S(1)} %sum.2.refs_0_), channel_id=1, source_target_pairs={{0,16},{4,20},{8,24},{12,28},{16,0},{20,4},{24,8},{28,12},{1,17},{... | collective-permute-start | bytes 12296 | tf_op jit(solution)/shard_map/chip_norm/ppermute | solution.py:308
  49.5 1.8 %collective-permute-done.16.refs_2_ = f32[8,128]{1,0:T(8,128)S(1)} collective-permute-done((f32[8,128]{1,0:T(8,128)S(1)}, f32[8,128]{1,0:T(8,128)S(1)}, u32[]{:S(2)}, u32[]{:S(2)}) %collective-permute-start.16) | collective-permute-done | bytes 4128 | tf_op jit(solution)/shard_map/chip_norm/ppermute | solution.py:308
  51.3 2.4 %collective-permute-done.17.refs_3_ = f32[8,128]{1,0:T(8,128)S(1)} collective-permute-done((f32[8,128]{1,0:T(8,128)S(1)}, f32[8,128]{1,0:T(8,128)S(1)}, u32[]{:S(2)}, u32[]{:S(2)}) %collective-permute-start.17) | collective-permute-done | bytes 4128 | tf_op jit(solution)/shard_map/chip_norm/ppermute | solution.py:308
  53.7 1.6 %collective-permute-start.18 = (f32[8,128]{1,0:T(8,128)S(1)}, f32[8,128]{1,0:T(8,128)S(1)}, u32[]{:S(2)}, u32[]{:S(2)}) collective-permute-start(f32[8,128]{1,0:T(8,128)S(1)} %sum.3.refs_0_), channel_id=1, source_target_pairs={{0,1},{1,2},{2,3},{3,0},{4,5},{5,6},{6,7},{7,4},{8,9},{9,10},{10,1... | collective-permute-start | bytes 12296 | tf_op jit(solution)/shard_map/group_norm/ppermute | solution.py:354
  55.3 2.6 %collective-permute-start.19 = (f32[8,128]{1,0:T(8,128)S(1)}, f32[8,128]{1,0:T(8,128)S(1)}, u32[]{:S(2)}, u32[]{:S(2)}) collective-permute-start(f32[8,128]{1,0:T(8,128)S(1)} %sum.3.refs_0_), channel_id=1, source_target_pairs={{0,2},{1,3},{2,0},{3,1},{4,6},{5,7},{6,4},{7,5},{8,10},{9,11},{10,... | collective-permute-start | bytes 12296 | tf_op jit(solution)/shard_map/group_norm/ppermute | solution.py:354
  57.9 1.3 %collective-permute-start.20 = (f32[8,128]{1,0:T(8,128)S(1)}, f32[8,128]{1,0:T(8,128)S(1)}, u32[]{:S(2)}, u32[]{:S(2)}) collective-permute-start(f32[8,128]{1,0:T(8,128)S(1)} %sum.3.refs_0_), channel_id=1, source_target_pairs={{0,3},{1,0},{2,1},{3,2},{4,7},{5,4},{6,5},{7,6},{8,11},{9,8},{10,9... | collective-permute-start | bytes 12296 | tf_op jit(solution)/shard_map/group_norm/ppermute | solution.py:354
  59.2 1.8 %gram.1 = (f32[512,512]{1,0:T(8,128)S(1)}, f32[512,512]{1,0:T(8,128)S(1)}) custom-call(f32[256,512]{1,0:T(8,128)S(1)} %get-tuple-element.30.upper_ref, f32[256,512]{1,0:T(8,128)S(1)} %get-tuple-element.36.lower_ref), custom_call_target="tpu_custom_call" | custom-call | flops 1610612736 | bytes 3145728 | tf_op jit(solution)/shard_map/gram/pallas_call | solution.py:97
  61.5 8.2 %update.1 = (f32[512,512]{1,0:T(8,128)S(1)}, f32[256,512]{1,0:T(8,128)S(1)}, f32[256,512]{1,0:T(8,128)S(1)}) custom-call(f32[256,512]{1,0:T(8,128)S(1)} %get-tuple-element.30.upper_ref, f32[256,512]{1,0:T(8,128)S(1)} %get-tuple-element.36.lower_ref, f32[512,512]{1,0:T(8,128)S(1)} %get-tuple-element.37.left_gram_ref, ...), custom_call_target="tpu_custom_call" | custom-call | flops 6442450944 | bytes 7356416 | tf_op jit(solution)/shard_map/update/pallas_call | solution.py:97
  70.4 1.5 %collective-permute-start.25 = (f32[256,512]{1,0:T(8,128)S(1)}, f32[256,512]{1,0:T(8,128)S(1)}, u32[]{:S(2)}, u32[]{:S(2)}) collective-permute-start(f32[256,512]{1,0:T(8,128)S(1)} %get-tuple-element.43), channel_id=1, source_target_pairs={{0,8},{4,20},{8,0},{12,28},{16,24},{20,4},{24,16},{28,12},{1,9},{5... | collective-permute-start | bytes 1572872 | tf_op jit(solution)/shard_map/link_own/ppermute | solution.py:308
  71.9 7.2 %collective-permute-done.21.refs_2_ = f32[256,512]{1,0:T(8,128)S(1)} collective-permute-done((f32[256,512]{1,0:T(8,128)S(1)}, f32[256,512]{1,0:T(8,128)S(1)}, u32[]{:S(2)}, u32[]{:S(2)}) %collective-permute-start.21) | collective-permute-done | bytes 524320 | tf_op jit(solution)/shard_map/link_own/ppermute | solution.py:308
  79.6 5.1 %collective-permute-done.25.refs_3_ = f32[256,512]{1,0:T(8,128)S(1)} collective-permute-done((f32[256,512]{1,0:T(8,128)S(1)}, f32[256,512]{1,0:T(8,128)S(1)}, u32[]{:S(2)}, u32[]{:S(2)}) %collective-permute-start.25) | collective-permute-done | bytes 524320 | tf_op jit(solution)/shard_map/link_own/ppermute | solution.py:308
  85.2 10.7 %collective-permute-done.30.refs_0_ = f32[512,512]{1,0:T(8,128)S(1)} collective-permute-done((f32[512,512]{1,0:T(8,128)S(1)}, f32[512,512]{1,0:T(8,128)S(1)}, u32[]{:S(2)}, u32[]{:S(2)}) %collective-permute-start.30) | collective-permute-done | bytes 1048608 | tf_op jit(solution)/shard_map/link_sibling/ppermute | solution.py:308
  96.4 2.3 %assemble.3.refs_4_ = f32[512,3072]{1,0:T(8,128)} custom-call(s32[6]{0:T(128)S(1)} %bitcast.27, s32[1]{0:T(128)} %bitcast.1.me_ref, f32[512,512]{1,0:T(8,128)S(1)} %get-tuple-element.41.refs_0_, f32[512,512]{1,0:T(8,128)S(1)} %collective-permute-done.22.refs_1_, f32[256,512]{1,0:T(8,128)S(1)} %collective-permute-done.21.refs_2_, ...), custom_call_target="tpu_custom_call" | custom-call | bytes 12582912 | tf_op jit(solution)/shard_map/assemble/pallas_call | solution.py:279
  98.7 2.8 %collective-permute-done.24.refs_2_ = f32[256,512]{1,0:T(8,128)S(1)} collective-permute-done((f32[256,512]{1,0:T(8,128)S(1)}, f32[256,512]{1,0:T(8,128)S(1)}, u32[]{:S(2)}, u32[]{:S(2)}) %collective-permute-start.24) | collective-permute-done | bytes 524320 | tf_op jit(solution)/shard_map/link_relayed/ppermute | solution.py:308
  101.5 5.6 %collective-permute-done.28.refs_3_ = f32[256,512]{1,0:T(8,128)S(1)} collective-permute-done((f32[256,512]{1,0:T(8,128)S(1)}, f32[256,512]{1,0:T(8,128)S(1)}, u32[]{:S(2)}, u32[]{:S(2)}) %collective-permute-start.28) | collective-permute-done | bytes 524320 | tf_op jit(solution)/shard_map/link_relayed/ppermute | solution.py:308
  107.1 1.9 %assemble.4.refs_2_ = f32[512,3072]{1,0:T(8,128)} custom-call(s32[6]{0:T(128)S(1)} %bitcast.28, s32[1]{0:T(128)} %bitcast.1.me_ref, f32[512,512]{1,0:T(8,128)S(1)} %collective-permute-done.30.refs_0_, f32[512,512]{1,0:T(8,128)S(1)} %collective-permute-done.31.refs_1_, ...), custom_call_target="tpu_custom_call", output_to_operand_aliasing={{}: (6, {})} | custom-call | bytes 8388608 | tf_op jit(solution)/shard_map/assemble/pallas_call | solution.py:279
  109.1 1.5 %assemble.5 = f32[512,3072]{1,0:T(8,128)} custom-call(s32[6]{0:T(128)S(1)} %bitcast.29, s32[1]{0:T(128)} %bitcast.1.me_ref, f32[256,512]{1,0:T(8,128)S(1)} %collective-permute-done.27.refs_0_, f32[256,512]{1,0:T(8,128)S(1)} %collective-permute-done.29.refs_1_, f32[512,3072]{1,0:T(8,128)} %assemble.4.refs_2_), custom_call_target="tpu_custom_call", output_to_operand_aliasing={{}: (4, {})} | custom-call | bytes 2097152 | tf_op jit(solution)/shard_map/assemble/pallas_call | solution.py:279
  (61 shorter events, 11.9 us)
Async XLA Ops:
  3.2 2.3 %collective-permute-start.4 = (f32[256,512]{1,0:T(8,128)S(1)}, f32[256,512]{1,0:T(8,128)S(1)}, u32[]{:S(2)}, u32[]{:S(2)}) collective-permute-start(f32[256,512]{1,0:T(8,128)S(1)} %get-tuple-element.29), channel_id=1, source_target_pairs={{0,4},{4,0},{8,12},{12,8},{16,20},{20,16},{24,28},{28,24},{1,5},{5... | collective-permute-start | bytes 1572872 | tf_op jit(solution)/shard_map/core_corner/ppermute | solution.py:308
  3.8 5.1 %collective-permute-start.11 = (f32[256,512]{1,0:T(8,128)S(1)}, f32[256,512]{1,0:T(8,128)S(1)}, u32[]{:S(2)}, u32[]{:S(2)}) collective-permute-start(f32[256,512]{1,0:T(8,128)S(1)} %get-tuple-element.34), channel_id=1, source_target_pairs={{0,4},{4,0},{8,12},{12,8},{16,20},{20,16},{24,28},{28,24},{1,5},{5... | collective-permute-start | bytes 1572872 | tf_op jit(solution)/shard_map/core_corner/ppermute | solution.py:308
  3.8 5.7 %collective-permute-start.1 = (f32[256,512]{1,0:T(8,128)S(1)}, f32[256,512]{1,0:T(8,128)S(1)}, u32[]{:S(2)}, u32[]{:S(2)}) collective-permute-start(f32[256,512]{1,0:T(8,128)S(1)} %get-tuple-element.27), channel_id=1, source_target_pairs={{0,4},{4,0},{8,12},{12,8},{16,20},{20,16},{24,28},{28,24},{1,5},{5... | collective-permute-start | bytes 1572872 | tf_op jit(solution)/shard_map/core_straight/ppermute | solution.py:308
  4.3 6.9 %collective-permute-start.8 = (f32[256,512]{1,0:T(8,128)S(1)}, f32[256,512]{1,0:T(8,128)S(1)}, u32[]{:S(2)}, u32[]{:S(2)}) collective-permute-start(f32[256,512]{1,0:T(8,128)S(1)} %get-tuple-element.32), channel_id=1, source_target_pairs={{0,4},{4,0},{8,12},{12,8},{16,20},{20,16},{24,28},{28,24},{1,5},{5... | collective-permute-start | bytes 1572872 | tf_op jit(solution)/shard_map/core_straight/ppermute | solution.py:308
  5.0 7.4 %collective-permute-start.3 = (f32[256,512]{1,0:T(8,128)S(1)}, f32[256,512]{1,0:T(8,128)S(1)}, u32[]{:S(2)}, u32[]{:S(2)}) collective-permute-start(f32[256,512]{1,0:T(8,128)S(1)} %get-tuple-element.28), channel_id=1, source_target_pairs={{0,4},{4,0},{8,12},{12,8},{16,20},{20,16},{24,28},{28,24},{1,5},{5... | collective-permute-start | bytes 1572872 | tf_op jit(solution)/shard_map/core_side/ppermute | solution.py:308
  6.1 9.8 %collective-permute-start.5 = (f32[256,512]{1,0:T(8,128)S(1)}, f32[256,512]{1,0:T(8,128)S(1)}, u32[]{:S(2)}, u32[]{:S(2)}) collective-permute-start(f32[256,512]{1,0:T(8,128)S(1)} %add.10), channel_id=1, source_target_pairs={{0,8},{4,20},{8,0},{12,28},{16,24},{20,4},{24,16},{28,12},{1,9},{5... | collective-permute-start | bytes 1572872 | tf_op jit(solution)/shard_map/link_corner/ppermute | solution.py:308
  8.8 9.8 %collective-permute-start.10 = (f32[256,512]{1,0:T(8,128)S(1)}, f32[256,512]{1,0:T(8,128)S(1)}, u32[]{:S(2)}, u32[]{:S(2)}) collective-permute-start(f32[256,512]{1,0:T(8,128)S(1)} %get-tuple-element.33), channel_id=1, source_target_pairs={{0,4},{4,0},{8,12},{12,8},{16,20},{20,16},{24,28},{28,24},{1,5},{5... | collective-permute-start | bytes 1572872 | tf_op jit(solution)/shard_map/core_side/ppermute | solution.py:308
  9.6 12.0 %collective-permute-start.12 = (f32[256,512]{1,0:T(8,128)S(1)}, f32[256,512]{1,0:T(8,128)S(1)}, u32[]{:S(2)}, u32[]{:S(2)}) collective-permute-start(f32[256,512]{1,0:T(8,128)S(1)} %add.14), channel_id=1, source_target_pairs={{0,8},{4,20},{8,0},{12,28},{16,24},{20,4},{24,16},{28,12},{1,9},{5... | collective-permute-start | bytes 1572872 | tf_op jit(solution)/shard_map/link_corner/ppermute | solution.py:308
  11.1 13.1 %collective-permute-start = (f32[256,512]{1,0:T(8,128)S(1)}, f32[256,512]{1,0:T(8,128)S(1)}, u32[]{:S(2)}, u32[]{:S(2)}) collective-permute-start(f32[256,512]{1,0:T(8,128)S(1)} %get-tuple-element.26), channel_id=1, source_target_pairs={{0,4},{4,0},{8,12},{12,8},{16,20},{20,16},{24,28},{28,24},{1,5},{5... | collective-permute-start | bytes 1572872 | tf_op jit(solution)/shard_map/core_self/ppermute | solution.py:308
  12.5 18.5 %collective-permute-start.7 = (f32[256,512]{1,0:T(8,128)S(1)}, f32[256,512]{1,0:T(8,128)S(1)}, u32[]{:S(2)}, u32[]{:S(2)}) collective-permute-start(f32[256,512]{1,0:T(8,128)S(1)} %get-tuple-element.31), channel_id=1, source_target_pairs={{0,4},{4,0},{8,12},{12,8},{16,20},{20,16},{24,28},{28,24},{1,5},{5... | collective-permute-start | bytes 1572872 | tf_op jit(solution)/shard_map/core_self/ppermute | solution.py:308
  16.0 14.4 %collective-permute-start.2 = (f32[256,512]{1,0:T(8,128)S(1)}, f32[256,512]{1,0:T(8,128)S(1)}, u32[]{:S(2)}, u32[]{:S(2)}) collective-permute-start(f32[256,512]{1,0:T(8,128)S(1)} %add.8), channel_id=1, source_target_pairs={{0,8},{4,20},{8,0},{12,28},{16,24},{20,4},{24,16},{28,12},{1,9},{5... | collective-permute-start | bytes 1572872 | tf_op jit(solution)/shard_map/link_straight/ppermute | solution.py:308
  18.6 22.9 %collective-permute-start.9 = (f32[256,512]{1,0:T(8,128)S(1)}, f32[256,512]{1,0:T(8,128)S(1)}, u32[]{:S(2)}, u32[]{:S(2)}) collective-permute-start(f32[256,512]{1,0:T(8,128)S(1)} %add.12), channel_id=1, source_target_pairs={{0,8},{4,20},{8,0},{12,28},{16,24},{20,4},{24,16},{28,12},{1,9},{5... | collective-permute-start | bytes 1572872 | tf_op jit(solution)/shard_map/link_straight/ppermute | solution.py:308
  21.6 20.6 %collective-permute-start.6 = (f32[256,512]{1,0:T(8,128)S(1)}, f32[256,512]{1,0:T(8,128)S(1)}, u32[]{:S(2)}, u32[]{:S(2)}) collective-permute-start(f32[256,512]{1,0:T(8,128)S(1)} %add.11), channel_id=1, source_target_pairs={{0,16},{4,12},{8,24},{12,4},{16,0},{20,28},{24,8},{28,20},{1,17},{... | collective-permute-start | bytes 1572872 | tf_op jit(solution)/shard_map/side_side/ppermute | solution.py:308
  24.3 19.5 %collective-permute-start.13 = (f32[256,512]{1,0:T(8,128)S(1)}, f32[256,512]{1,0:T(8,128)S(1)}, u32[]{:S(2)}, u32[]{:S(2)}) collective-permute-start(f32[256,512]{1,0:T(8,128)S(1)} %add.15), channel_id=1, source_target_pairs={{0,16},{4,12},{8,24},{12,4},{16,0},{20,28},{24,8},{28,20},{1,17},{... | collective-permute-start | bytes 1572872 | tf_op jit(solution)/shard_map/side_side/ppermute | solution.py:308
  44.7 1.2 %collective-permute-start.14 = (f32[8,128]{1,0:T(8,128)S(1)}, f32[8,128]{1,0:T(8,128)S(1)}, u32[]{:S(2)}, u32[]{:S(2)}) collective-permute-start(f32[8,128]{1,0:T(8,128)S(1)} %get-tuple-element.39.refs_0_), channel_id=1, source_target_pairs={{0,4},{4,0},{8,12},{12,8},{16,20},{20,16},{24,28},{28,24},{1,5},{5... | collective-permute-start | bytes 12296 | tf_op jit(solution)/shard_map/core_norm/ppermute | solution.py:308
  45.9 3.6 %collective-permute-start.15 = (f32[8,128]{1,0:T(8,128)S(1)}, f32[8,128]{1,0:T(8,128)S(1)}, u32[]{:S(2)}, u32[]{:S(2)}) collective-permute-start(f32[8,128]{1,0:T(8,128)S(1)} %sum.2.refs_0_), channel_id=1, source_target_pairs={{0,8},{4,12},{8,0},{12,4},{16,24},{20,28},{24,16},{28,20},{1,9},{5... | collective-permute-start | bytes 12296 | tf_op jit(solution)/shard_map/chip_norm/ppermute | solution.py:308
  47.7 3.6 %collective-permute-start.16 = (f32[8,128]{1,0:T(8,128)S(1)}, f32[8,128]{1,0:T(8,128)S(1)}, u32[]{:S(2)}, u32[]{:S(2)}) collective-permute-start(f32[8,128]{1,0:T(8,128)S(1)} %sum.2.refs_0_), channel_id=1, source_target_pairs={{0,16},{4,20},{8,24},{12,28},{16,0},{20,4},{24,8},{28,12},{1,17},{... | collective-permute-start | bytes 12296 | tf_op jit(solution)/shard_map/chip_norm/ppermute | solution.py:308
  49.2 4.5 %collective-permute-start.17 = (f32[8,128]{1,0:T(8,128)S(1)}, f32[8,128]{1,0:T(8,128)S(1)}, u32[]{:S(2)}, u32[]{:S(2)}) collective-permute-start(f32[8,128]{1,0:T(8,128)S(1)} %sum.2.refs_0_), channel_id=1, source_target_pairs={{0,24},{4,28},{8,16},{12,20},{16,8},{20,12},{24,0},{28,4},{1,25},{... | collective-permute-start | bytes 12296 | tf_op jit(solution)/shard_map/chip_norm/ppermute | solution.py:308
  53.7 7.4 %collective-permute-start.18 = (f32[8,128]{1,0:T(8,128)S(1)}, f32[8,128]{1,0:T(8,128)S(1)}, u32[]{:S(2)}, u32[]{:S(2)}) collective-permute-start(f32[8,128]{1,0:T(8,128)S(1)} %sum.3.refs_0_), channel_id=1, source_target_pairs={{0,1},{1,2},{2,3},{3,0},{4,5},{5,6},{6,7},{7,4},{8,9},{9,10},{10,1... | collective-permute-start | bytes 12296 | tf_op jit(solution)/shard_map/group_norm/ppermute | solution.py:354
  55.3 5.8 %collective-permute-start.19 = (f32[8,128]{1,0:T(8,128)S(1)}, f32[8,128]{1,0:T(8,128)S(1)}, u32[]{:S(2)}, u32[]{:S(2)}) collective-permute-start(f32[8,128]{1,0:T(8,128)S(1)} %sum.3.refs_0_), channel_id=1, source_target_pairs={{0,2},{1,3},{2,0},{3,1},{4,6},{5,7},{6,4},{7,5},{8,10},{9,11},{10,... | collective-permute-start | bytes 12296 | tf_op jit(solution)/shard_map/group_norm/ppermute | solution.py:354
  57.9 3.6 %collective-permute-start.20 = (f32[8,128]{1,0:T(8,128)S(1)}, f32[8,128]{1,0:T(8,128)S(1)}, u32[]{:S(2)}, u32[]{:S(2)}) collective-permute-start(f32[8,128]{1,0:T(8,128)S(1)} %sum.3.refs_0_), channel_id=1, source_target_pairs={{0,3},{1,0},{2,1},{3,2},{4,7},{5,4},{6,5},{7,6},{8,11},{9,8},{10,9... | collective-permute-start | bytes 12296 | tf_op jit(solution)/shard_map/group_norm/ppermute | solution.py:354
  69.7 9.3 %collective-permute-start.22 = (f32[512,512]{1,0:T(8,128)S(1)}, f32[512,512]{1,0:T(8,128)S(1)}, u32[]{:S(2)}, u32[]{:S(2)}) collective-permute-start(f32[512,512]{1,0:T(8,128)S(1)} %get-tuple-element.41.refs_0_), channel_id=1, source_target_pairs={{0,4},{4,0},{8,12},{12,8},{16,20},{20,16},{24,28},{28,24},{1,5},{5... | collective-permute-start | bytes 3145736 | tf_op jit(solution)/shard_map/core_own/ppermute | solution.py:308
  69.8 9.2 %collective-permute-start.21 = (f32[256,512]{1,0:T(8,128)S(1)}, f32[256,512]{1,0:T(8,128)S(1)}, u32[]{:S(2)}, u32[]{:S(2)}) collective-permute-start(f32[256,512]{1,0:T(8,128)S(1)} %get-tuple-element.40), channel_id=1, source_target_pairs={{0,8},{4,20},{8,0},{12,28},{16,24},{20,4},{24,16},{28,12},{1,9},{5... | collective-permute-start | bytes 1572872 | tf_op jit(solution)/shard_map/link_own/ppermute | solution.py:308
  70.4 14.3 %collective-permute-start.25 = (f32[256,512]{1,0:T(8,128)S(1)}, f32[256,512]{1,0:T(8,128)S(1)}, u32[]{:S(2)}, u32[]{:S(2)}) collective-permute-start(f32[256,512]{1,0:T(8,128)S(1)} %get-tuple-element.43), channel_id=1, source_target_pairs={{0,8},{4,20},{8,0},{12,28},{16,24},{20,4},{24,16},{28,12},{1,9},{5... | collective-permute-start | bytes 1572872 | tf_op jit(solution)/shard_map/link_own/ppermute | solution.py:308
  79.0 16.8 %collective-permute-start.30 = (f32[512,512]{1,0:T(8,128)S(1)}, f32[512,512]{1,0:T(8,128)S(1)}, u32[]{:S(2)}, u32[]{:S(2)}) collective-permute-start(f32[512,512]{1,0:T(8,128)S(1)} %collective-permute-done.22.refs_1_), channel_id=1, source_target_pairs={{0,8},{4,20},{8,0},{12,28},{16,24},{20,4},{24,16},{28,12},{1,9},{5... | collective-permute-start | bytes 3145736 | tf_op jit(solution)/shard_map/link_sibling/ppermute | solution.py:308
  79.6 5.1 %collective-permute-start.23 = (f32[256,512]{1,0:T(8,128)S(1)}, f32[256,512]{1,0:T(8,128)S(1)}, u32[]{:S(2)}, u32[]{:S(2)}) collective-permute-start(f32[256,512]{1,0:T(8,128)S(1)} %collective-permute-done.21.refs_2_), channel_id=1, source_target_pairs={{0,4},{4,0},{8,12},{12,8},{16,20},{20,16},{24,28},{28,24},{1,5},{5... | collective-permute-start | bytes 1572872 | tf_op jit(solution)/shard_map/core_first/ppermute | solution.py:308
  84.7 11.2 %collective-permute-start.26 = (f32[256,512]{1,0:T(8,128)S(1)}, f32[256,512]{1,0:T(8,128)S(1)}, u32[]{:S(2)}, u32[]{:S(2)}) collective-permute-start(f32[256,512]{1,0:T(8,128)S(1)} %collective-permute-done.25.refs_3_), channel_id=1, source_target_pairs={{0,4},{4,0},{8,12},{12,8},{16,20},{20,16},{24,28},{28,24},{1,5},{5... | collective-permute-start | bytes 1572872 | tf_op jit(solution)/shard_map/core_first/ppermute | solution.py:308
  84.7 16.8 %collective-permute-start.24 = (f32[256,512]{1,0:T(8,128)S(1)}, f32[256,512]{1,0:T(8,128)S(1)}, u32[]{:S(2)}, u32[]{:S(2)}) collective-permute-start(f32[256,512]{1,0:T(8,128)S(1)} %collective-permute-done.23.refs_4_), channel_id=1, source_target_pairs={{0,8},{4,20},{8,0},{12,28},{16,24},{20,4},{24,16},{28,12},{1,9},{5... | collective-permute-start | bytes 1572872 | tf_op jit(solution)/shard_map/link_relayed/ppermute | solution.py:308
  95.9 11.2 %collective-permute-start.31 = (f32[512,512]{1,0:T(8,128)S(1)}, f32[512,512]{1,0:T(8,128)S(1)}, u32[]{:S(2)}, u32[]{:S(2)}) collective-permute-start(f32[512,512]{1,0:T(8,128)S(1)} %collective-permute-done.30.refs_0_), channel_id=1, source_target_pairs={{0,4},{4,0},{8,12},{12,8},{16,20},{20,16},{24,28},{28,24},{1,5},{5... | collective-permute-start | bytes 3145736 | tf_op jit(solution)/shard_map/core_second/ppermute | solution.py:308
  95.9 11.2 %collective-permute-start.28 = (f32[256,512]{1,0:T(8,128)S(1)}, f32[256,512]{1,0:T(8,128)S(1)}, u32[]{:S(2)}, u32[]{:S(2)}) collective-permute-start(f32[256,512]{1,0:T(8,128)S(1)} %collective-permute-done.26.refs_5_), channel_id=1, source_target_pairs={{0,8},{4,20},{8,0},{12,28},{16,24},{20,4},{24,16},{28,12},{1,9},{5... | collective-permute-start | bytes 1572872 | tf_op jit(solution)/shard_map/link_relayed/ppermute | solution.py:308
  101.5 7.5 %collective-permute-start.27 = (f32[256,512]{1,0:T(8,128)S(1)}, f32[256,512]{1,0:T(8,128)S(1)}, u32[]{:S(2)}, u32[]{:S(2)}) collective-permute-start(f32[256,512]{1,0:T(8,128)S(1)} %collective-permute-done.24.refs_2_), channel_id=1, source_target_pairs={{0,4},{4,0},{8,12},{12,8},{16,20},{20,16},{24,28},{28,24},{1,5},{5... | collective-permute-start | bytes 1572872 | tf_op jit(solution)/shard_map/core_relayed/ppermute | solution.py:308
  107.1 1.9 %collective-permute-start.29 = (f32[256,512]{1,0:T(8,128)S(1)}, f32[256,512]{1,0:T(8,128)S(1)}, u32[]{:S(2)}, u32[]{:S(2)}) collective-permute-start(f32[256,512]{1,0:T(8,128)S(1)} %collective-permute-done.28.refs_3_), channel_id=1, source_target_pairs={{0,4},{4,0},{8,12},{12,8},{16,20},{20,16},{24,28},{28,24},{1,5},{5... | collective-permute-start | bytes 1572872 | tf_op jit(solution)/shard_map/core_relayed/ppermute | solution.py:308
  (5 other events, 98.5 us)

commit v8 on v7

--- a/solution.py
+++ b/solution.py
@@ -65,7 +65,7 @@
 
 
 SMALL = 2 << 20
-LARGE = 14 << 20
+LARGE = 20 << 20
 F32 = jnp.float32
 HALVES = (0, 1)
 
@@ -75,13 +75,32 @@
     return high, (value - high.astype(F32)).astype(jnp.bfloat16)
 
 
-def narrow_dot(left_side, right_side, dims):
-    return lax.dot_general(left_side, right_side, (dims, ((), ())), preferred_element_type=F32)
-
-
-def split_product(left_side, right_side, dims=((1,), (0,))):
-    small = narrow_dot(left_side[0], right_side[1], dims) + narrow_dot(left_side[1], right_side[0], dims)
-    return narrow_dot(left_side[0], right_side[0], dims) + small
+def left_operand(value):
+    high, low = split(value)
+    return jnp.concatenate([high, high, low], axis=1)
+
+
+def right_operand(value):
+    high, low = split(value)
+    return jnp.concatenate([high, low, high], axis=0)
+
+
+def triple_dot(left_side, right_side):
+    return jnp.dot(left_side, right_side, preferred_element_type=F32)
+
+
+def add_identity(value, amount):
+    tile = 128
+    rows = lax.broadcasted_iota(jnp.int32, (tile, tile), 0)
+    columns = lax.broadcasted_iota(jnp.int32, (tile, tile), 1)
+    diagonal = jnp.where(rows == columns, amount, 0.0)
+    lines = []
+    for i in range(value.shape[0] // tile):
+        line = value[i * tile : (i + 1) * tile]
+        parts = [line[:, j * tile : (j + 1) * tile] for j in range(value.shape[1] // tile)]
+        parts[i] = parts[i] + diagonal
+        lines.append(jnp.concatenate(parts, axis=1))
+    return jnp.concatenate(lines, axis=0)
 
 
 def piece_target(kind, device):
@@ -194,9 +213,14 @@
 
 
 def gram_kernel(upper_ref, lower_ref, left_ref, right_ref):
-    block = split(whole_block((upper_ref, lower_ref)))
-    left_ref[...] = split_product(block, block, ((1,), (1,)))
-    right_ref[...] = split_product(block, block, ((0,), (0,)))
+    block = whole_block((upper_ref, lower_ref))
+    high, low = split(block)
+    across = jnp.concatenate([high, high, low], axis=1)
+    across_other = jnp.concatenate([high, low, high], axis=1)
+    down = jnp.concatenate([high, high, low], axis=0)
+    down_other = jnp.concatenate([high, low, high], axis=0)
+    left_ref[...] = lax.dot_general(across, across_other, (((1,), (1,)), ((), ())), preferred_element_type=F32)
+    right_ref[...] = lax.dot_general(down, down_other, (((0,), (0,)), ((), ())), preferred_element_type=F32)
 
 
 def gram_call(block):
@@ -205,44 +229,40 @@
     return local_call(gram_kernel, "gram", [shape, shape], block, flops=12 * width**3, vmem=LARGE)
 
 
-def root_of(previous, gram, gram_scale):
-    rows = lax.broadcasted_iota(jnp.int32, previous.shape, 0)
-    columns = lax.broadcasted_iota(jnp.int32, previous.shape, 1)
-    identity = jnp.where(rows == columns, 1.0, 0.0)
-    statistic = 0.5 * previous + gram * gram_scale
-    squares = jnp.sum(statistic * statistic, keepdims=True).reshape(1, 1)
-    frobenius = jnp.sqrt(squares)
-    scaled = statistic * (1.0 / frobenius)
-    parts = split(scaled)
-    square = split_product(parts, parts)
-    factor_square = split((25.0 * identity - 10.0 * scaled + square) * 0.0625)
-    factor_scaled = split((5.0 * scaled - square) * 0.25)
-    fourth = split(split_product(factor_square, factor_square))
-    tail = split_product(fourth, factor_scaled)
-    return (6.25 * identity - 1.25 * scaled - tail) * (0.25 * lax.rsqrt(jnp.sqrt(frobenius)))
-
-
-def update_call(block, left_gram, right_gram, left_prev, right_prev, norms, entry_count):
+def roots_of(previous, grams, gram_scale):
+    statistics = [0.5 * prev + gram * gram_scale for prev, gram in zip(previous, grams)]
+    frobenius = [jnp.sqrt(jnp.sum(value * value, keepdims=True).reshape(1, 1)) for value in statistics]
+    scaled = [value * (1.0 / norm) for value, norm in zip(statistics, frobenius)]
+    square = [triple_dot(left_operand(value), right_operand(value)) for value in scaled]
+    factor_square = [add_identity(0.0625 * q - 0.625 * m, 1.5625) for q, m in zip(square, scaled)]
+    factor_scaled = [1.25 * m - 0.25 * q for q, m in zip(square, scaled)]
+    fourth = [triple_dot(left_operand(value), right_operand(value)) for value in factor_square]
+    tail = [triple_dot(left_operand(f), right_operand(m)) for f, m in zip(fourth, factor_scaled)]
+    roots = [add_identity(-1.25 * m - t, 6.25) for m, t in zip(scaled, tail)]
+    return roots, [0.25 * lax.rsqrt(jnp.sqrt(norm)) for norm in frobenius]
+
+
+def update_call(block, block_norm, left_gram, right_gram, left_prev, right_prev, norms, entry_count):
     width = block[0].shape[1]
 
-    def kernel(upper_ref, lower_ref, left_gram_ref, right_gram_ref, left_ref, right_ref, *refs):
+    def kernel(upper_ref, lower_ref, block_norm_ref, left_gram_ref, right_gram_ref, left_ref, right_ref, *refs):
         norm_refs, out_refs = refs[:-3], refs[-3:]
         squares = sum(ref[:1, :1] for ref in norm_refs)
         clip_factor = jnp.minimum(1.0, clip_level / jnp.sqrt(squares / entry_count))
         gram_scale = clip_factor * clip_factor / width
-        left_root = root_of(left_ref[...], left_gram_ref[...], gram_scale)
-        right_root = root_of(right_ref[...], right_gram_ref[...], gram_scale)
-        block = whole_block((upper_ref, lower_ref))
-        halfway = split_product(split(left_root), split(block))
-        pre = split_product(split(halfway), split(right_root)) * clip_factor
-        block_norm = jnp.sum(block * block, keepdims=True).reshape(1, 1) * (clip_factor * clip_factor)
-        pre_norm = jnp.sum(pre * pre, keepdims=True).reshape(1, 1)
-        update = pre * jnp.sqrt(block_norm / (pre_norm + graft_eps))
+        previous, grams = (left_ref[...], right_ref[...]), (left_gram_ref[...], right_gram_ref[...])
+        roots, scales = roots_of(previous, grams, gram_scale)
+        halfway = triple_dot(left_operand(roots[0]), right_operand(whole_block((upper_ref, lower_ref))))
+        pre = triple_dot(left_operand(halfway), right_operand(roots[1]))
+        pre_scale = scales[0] * scales[1] * clip_factor
+        pre_norm = jnp.sum(pre * pre, keepdims=True).reshape(1, 1) * (pre_scale * pre_scale)
+        clipped_norm = block_norm_ref[:1, :1] * (clip_factor * clip_factor)
+        update = pre * (pre_scale * jnp.sqrt(clipped_norm / (pre_norm + graft_eps)))
         out_refs[0][...] = update
         for half in HALVES:
             out_refs[1 + half][...] = update[half * (width // 2) : (half + 1) * (width // 2)]
 
-    operands = (*block, left_gram, right_gram, left_prev, right_prev, *norms)
+    operands = (*block, block_norm, left_gram, right_gram, left_prev, right_prev, *norms)
     shapes = [piece_shape(half, width) for half in (None, *HALVES)]
     return local_call(kernel, "update", shapes, operands, flops=48 * width**3, vmem=LARGE)
 
@@ -345,15 +365,19 @@
     for half in HALVES:
         joined, norm = join_call(owner_row, me, totals[half], half, arrived[half], norm, block_count)
         block.append(joined)
+    block_norm = norm
     norm = sum_call(norm, to_core(norm, "norm"))
     norm = sum_call(norm, *[over(flipped(mask), norm, "chip_norm") for mask in (2, 4, 6)])
     norms = [norm]
     for shift in range(1, group_count):
-        pairs = [(i, (i + shift) % group_count) for i in range(group_count)]
+        both_ways = group_count & (group_count - 1) == 0
+        pairs = [(i, i ^ shift if both_ways else (i + shift) % group_count) for i in range(group_count)]
         with jax.named_scope("group_norm"):
             norms.append(lax.ppermute(norm, "mp", pairs))
     left_gram, right_gram = gram_call(block)
-    whole, *own = update_call(block, left_gram, right_gram, left_stats[0], right_stats[0], norms, entry_count)
+    whole, *own = update_call(
+        block, block_norm, left_gram, right_gram, left_stats[0], right_stats[0], norms, entry_count
+    )
 
     core_own = to_core(whole, "own")
     first = [to_link(value, "own") for value in own]

time: 110 us -> 113 us (1.027); the launches traced: 111 us -> 112 us
  waiting for transfers between devices: 60.4 us -> 63.3 us
    ppermute x3, waiting for transfers between devices: 0.4 us -> 3.33 us  [paired_body(): norms.append(lax.ppermute(norm, 'mp', pairs))]
  transfers between devices with their start and end apart: 32 -> 32, of which waited for: 15 -> 16; matrix products, arithmetic and copies ran while one was open for 0% -> 0% of each run, Pallas kernels for 11% -> 11%
where the time goes in v8:
time: 113 us; the launch traced here: 112 us
  waiting for transfers between devices  63.3 us (56%)
  Pallas kernels  23.5 us (21%)
  starting transfers between devices  22.6 us (20%)
  local copies, waits for them, and re-layouts  2.56 us (2%)
    ppermute x29, waiting for transfers between devices, over(): return lax.ppermute(value, 'dp', pairs)  60 us
    ppermute x29, starting transfers between devices, over(): return lax.ppermute(value, 'dp', pairs)  18.2 us
    pallas_call x16, Pallas kernels, local_call(): pl.pallas_call(kernel, in_specs=[pl.BlockSpec(memory_space=pltpu.SMEM)] *...  17.8 us
    pallas_call x3, Pallas kernels, assemble_call(): pl.pallas_call(kernel, in_specs=in_specs, out_specs=pl.BlockSpec(memory_s...  5.73 us
    ppermute x3, starting transfers between devices, paired_body(): norms.append(lax.ppermute(norm, 'mp', pairs))  4.39 us
    ppermute x3, waiting for transfers between devices, paired_body(): norms.append(lax.ppermute(norm, 'mp', pairs))  3.33 us
    unnamed x10, local copies, waits for them, and re-layouts  2.56 us
  transfers between devices with their start and end apart: 32, of which 16 were waited for; matrix products, arithmetic and copies ran while one was open for 0% of the time, Pallas kernels for 11%

profile of v8, /device:TPU:0, one launch (start us, length us, event | category | flops | bytes accessed | tf_op | source)
XLA Modules:
  0.0 112.2 jit_solution(14223347835437593583)
XLA Ops:
  0.0 1.9 %copy-done = bf16[1,512,3072]{2,1,0:T(8,128)(2,1)S(1)} copy-done((bf16[1,512,3072]{2,1,0:T(8,128)(2,1)S(1)}, bf16[1,512,3072]{2,1,0:T(8,128)(2,1)}, u32[]{:S(2)}) %copy-start) | copy-done | bytes 3145752
  4.3 0.7 pack.2
  6.1 2.7 %collective-permute-start.5 = (f32[256,512]{1,0:T(8,128)S(1)}, f32[256,512]{1,0:T(8,128)S(1)}, u32[]{:S(2)}, u32[]{:S(2)}) collective-permute-start(f32[256,512]{1,0:T(8,128)S(1)} %add.10), channel_id=1, source_target_pairs={{0,8},{4,20},{8,0},{12,28},{16,24},{20,4},{24,16},{28,12},{1,9},{5... | collective-permute-start | bytes 1572872 | tf_op jit(solution)/shard_map/link_corner/ppermute | solution.py:328
  9.6 1.6 %collective-permute-start.12 = (f32[256,512]{1,0:T(8,128)S(1)}, f32[256,512]{1,0:T(8,128)S(1)}, u32[]{:S(2)}, u32[]{:S(2)}) collective-permute-start(f32[256,512]{1,0:T(8,128)S(1)} %add.14), channel_id=1, source_target_pairs={{0,8},{4,20},{8,0},{12,28},{16,24},{20,4},{24,16},{28,12},{1,9},{5... | collective-permute-start | bytes 1572872 | tf_op jit(solution)/shard_map/link_corner/ppermute | solution.py:328
  12.9 3.1 %collective-permute-done.5.refs_1_ = f32[256,512]{1,0:T(8,128)S(1)} collective-permute-done((f32[256,512]{1,0:T(8,128)S(1)}, f32[256,512]{1,0:T(8,128)S(1)}, u32[]{:S(2)}, u32[]{:S(2)}) %collective-permute-start.5) | collective-permute-done | bytes 524320 | tf_op jit(solution)/shard_map/link_corner/ppermute | solution.py:328
  16.0 2.0 %collective-permute-start.2 = (f32[256,512]{1,0:T(8,128)S(1)}, f32[256,512]{1,0:T(8,128)S(1)}, u32[]{:S(2)}, u32[]{:S(2)}) collective-permute-start(f32[256,512]{1,0:T(8,128)S(1)} %add.8), channel_id=1, source_target_pairs={{0,8},{4,20},{8,0},{12,28},{16,24},{20,4},{24,16},{28,12},{1,9},{5... | collective-permute-start | bytes 1572872 | tf_op jit(solution)/shard_map/link_straight/ppermute | solution.py:328
  18.7 2.9 %collective-permute-done.12.refs_1_ = f32[256,512]{1,0:T(8,128)S(1)} collective-permute-done((f32[256,512]{1,0:T(8,128)S(1)}, f32[256,512]{1,0:T(8,128)S(1)}, u32[]{:S(2)}, u32[]{:S(2)}) %collective-permute-start.12) | collective-permute-done | bytes 524320 | tf_op jit(solution)/shard_map/link_corner/ppermute | solution.py:328
  21.6 2.0 %collective-permute-start.6 = (f32[256,512]{1,0:T(8,128)S(1)}, f32[256,512]{1,0:T(8,128)S(1)}, u32[]{:S(2)}, u32[]{:S(2)}) collective-permute-start(f32[256,512]{1,0:T(8,128)S(1)} %add.11), channel_id=1, source_target_pairs={{0,16},{4,12},{8,24},{12,4},{16,0},{20,28},{24,8},{28,20},{1,17},{... | collective-permute-start | bytes 1572872 | tf_op jit(solution)/shard_map/side_side/ppermute | solution.py:328
  24.4 6.0 %collective-permute-done.2.refs_1_ = f32[256,512]{1,0:T(8,128)S(1)} collective-permute-done((f32[256,512]{1,0:T(8,128)S(1)}, f32[256,512]{1,0:T(8,128)S(1)}, u32[]{:S(2)}, u32[]{:S(2)}) %collective-permute-start.2) | collective-permute-done | bytes 524320 | tf_op jit(solution)/shard_map/link_straight/ppermute | solution.py:328
  31.0 10.6 %collective-permute-done.9.refs_1_ = f32[256,512]{1,0:T(8,128)S(1)} collective-permute-done((f32[256,512]{1,0:T(8,128)S(1)}, f32[256,512]{1,0:T(8,128)S(1)}, u32[]{:S(2)}, u32[]{:S(2)}) %collective-permute-start.9) | collective-permute-done | bytes 524320 | tf_op jit(solution)/shard_map/link_straight/ppermute | solution.py:328
  42.2 0.9 join.2
  43.1 0.7 collective-permute-done.13.arrival_ref
  43.8 0.9 join.3
  44.8 1.1 collective-permute-done.14.refs_1_
  45.9 1.8 %collective-permute-start.15 = (f32[8,128]{1,0:T(8,128)S(1)}, f32[8,128]{1,0:T(8,128)S(1)}, u32[]{:S(2)}, u32[]{:S(2)}) collective-permute-start(f32[8,128]{1,0:T(8,128)S(1)} %sum.2.refs_0_), channel_id=1, source_target_pairs={{0,8},{4,12},{8,0},{12,4},{16,24},{20,28},{24,16},{28,20},{1,9},{5... | collective-permute-start | bytes 12296 | tf_op jit(solution)/shard_map/chip_norm/ppermute | solution.py:328
  47.7 1.5 %collective-permute-start.16 = (f32[8,128]{1,0:T(8,128)S(1)}, f32[8,128]{1,0:T(8,128)S(1)}, u32[]{:S(2)}, u32[]{:S(2)}) collective-permute-start(f32[8,128]{1,0:T(8,128)S(1)} %sum.2.refs_0_), channel_id=1, source_target_pairs={{0,16},{4,20},{8,24},{12,28},{16,0},{20,4},{24,8},{28,12},{1,17},{... | collective-permute-start | bytes 12296 | tf_op jit(solution)/shard_map/chip_norm/ppermute | solution.py:328
  49.5 1.8 %collective-permute-done.16.refs_2_ = f32[8,128]{1,0:T(8,128)S(1)} collective-permute-done((f32[8,128]{1,0:T(8,128)S(1)}, f32[8,128]{1,0:T(8,128)S(1)}, u32[]{:S(2)}, u32[]{:S(2)}) %collective-permute-start.16) | collective-permute-done | bytes 4128 | tf_op jit(solution)/shard_map/chip_norm/ppermute | solution.py:328
  51.3 2.4 %collective-permute-done.17.refs_3_ = f32[8,128]{1,0:T(8,128)S(1)} collective-permute-done((f32[8,128]{1,0:T(8,128)S(1)}, f32[8,128]{1,0:T(8,128)S(1)}, u32[]{:S(2)}, u32[]{:S(2)}) %collective-permute-start.17) | collective-permute-done | bytes 4128 | tf_op jit(solution)/shard_map/chip_norm/ppermute | solution.py:328
  53.7 1.6 %collective-permute-start.18 = (f32[8,128]{1,0:T(8,128)S(1)}, f32[8,128]{1,0:T(8,128)S(1)}, u32[]{:S(2)}, u32[]{:S(2)}) collective-permute-start(f32[8,128]{1,0:T(8,128)S(1)} %sum.3.refs_0_), channel_id=1, source_target_pairs={{0,1},{1,0},{2,3},{3,2},{4,5},{5,4},{6,7},{7,6},{8,9},{9,8},{10,11... | collective-permute-start | bytes 12296 | tf_op jit(solution)/shard_map/group_norm/ppermute | solution.py:376
  55.3 2.6 %collective-permute-start.19 = (f32[8,128]{1,0:T(8,128)S(1)}, f32[8,128]{1,0:T(8,128)S(1)}, u32[]{:S(2)}, u32[]{:S(2)}) collective-permute-start(f32[8,128]{1,0:T(8,128)S(1)} %sum.3.refs_0_), channel_id=1, source_target_pairs={{0,2},{1,3},{2,0},{3,1},{4,6},{5,7},{6,4},{7,5},{8,10},{9,11},{10,... | collective-permute-start | bytes 12296 | tf_op jit(solution)/shard_map/group_norm/ppermute | solution.py:376
  58.1 1.8 %gram.1 = (f32[512,512]{1,0:T(8,128)S(1)}, f32[512,512]{1,0:T(8,128)S(1)}) custom-call(f32[256,512]{1,0:T(8,128)S(1)} %get-tuple-element.30.upper_ref, f32[256,512]{1,0:T(8,128)S(1)} %get-tuple-element.36.lower_ref), custom_call_target="tpu_custom_call" | custom-call | flops 1610612736 | bytes 3145728 | tf_op jit(solution)/shard_map/gram/pallas_call | solution.py:116
  59.9 3.3 %collective-permute-done.20.refs_3_ = f32[8,128]{1,0:T(8,128)S(1)} collective-permute-done((f32[8,128]{1,0:T(8,128)S(1)}, f32[8,128]{1,0:T(8,128)S(1)}, u32[]{:S(2)}, u32[]{:S(2)}) %collective-permute-start.20) | collective-permute-done | bytes 4128 | tf_op jit(solution)/shard_map/group_norm/ppermute | solution.py:376
  63.3 8.0 %update.1 = (f32[512,512]{1,0:T(8,128)S(1)}, f32[256,512]{1,0:T(8,128)S(1)}, f32[256,512]{1,0:T(8,128)S(1)}) custom-call(f32[256,512]{1,0:T(8,128)S(1)} %get-tuple-element.30.upper_ref, f32[256,512]{1,0:T(8,128)S(1)} %get-tuple-element.36.lower_ref, f32[8,128]{1,0:T(8,128)S(1)} %get-tuple-element.37.refs_0_.block_norm_ref, ...), custom_call_target="tpu_custom_call" | custom-call | flops 6442450944 | bytes 7360512 | tf_op jit(solution)/shard_map/update/pallas_call | solution.py:116
  72.0 1.5 %collective-permute-start.25 = (f32[256,512]{1,0:T(8,128)S(1)}, f32[256,512]{1,0:T(8,128)S(1)}, u32[]{:S(2)}, u32[]{:S(2)}) collective-permute-start(f32[256,512]{1,0:T(8,128)S(1)} %get-tuple-element.43), channel_id=1, source_target_pairs={{0,8},{4,20},{8,0},{12,28},{16,24},{20,4},{24,16},{28,12},{1,9},{5... | collective-permute-start | bytes 1572872 | tf_op jit(solution)/shard_map/link_own/ppermute | solution.py:328
  73.5 7.2 %collective-permute-done.21.refs_2_ = f32[256,512]{1,0:T(8,128)S(1)} collective-permute-done((f32[256,512]{1,0:T(8,128)S(1)}, f32[256,512]{1,0:T(8,128)S(1)}, u32[]{:S(2)}, u32[]{:S(2)}) %collective-permute-start.21) | collective-permute-done | bytes 524320 | tf_op jit(solution)/shard_map/link_own/ppermute | solution.py:328
  81.2 5.1 %collective-permute-done.25.refs_3_ = f32[256,512]{1,0:T(8,128)S(1)} collective-permute-done((f32[256,512]{1,0:T(8,128)S(1)}, f32[256,512]{1,0:T(8,128)S(1)}, u32[]{:S(2)}, u32[]{:S(2)}) %collective-permute-start.25) | collective-permute-done | bytes 524320 | tf_op jit(solution)/shard_map/link_own/ppermute | solution.py:328
  86.8 10.7 %collective-permute-done.30.refs_0_ = f32[512,512]{1,0:T(8,128)S(1)} collective-permute-done((f32[512,512]{1,0:T(8,128)S(1)}, f32[512,512]{1,0:T(8,128)S(1)}, u32[]{:S(2)}, u32[]{:S(2)}) %collective-permute-start.30) | collective-permute-done | bytes 1048608 | tf_op jit(solution)/shard_map/link_sibling/ppermute | solution.py:328
  98.0 2.6 %assemble.3.refs_4_ = f32[512,3072]{1,0:T(8,128)} custom-call(s32[6]{0:T(128)S(1)} %bitcast.27, s32[1]{0:T(128)} %bitcast.1.me_ref, f32[512,512]{1,0:T(8,128)S(1)} %get-tuple-element.41.refs_0_, f32[512,512]{1,0:T(8,128)S(1)} %collective-permute-done.22.refs_1_, f32[256,512]{1,0:T(8,128)S(1)} %collective-permute-done.21.refs_2_, ...), custom_call_target="tpu_custom_call" | custom-call | bytes 12582912 | tf_op jit(solution)/shard_map/assemble/pallas_call | solution.py:299
  100.7 2.5 %collective-permute-done.24.refs_2_ = f32[256,512]{1,0:T(8,128)S(1)} collective-permute-done((f32[256,512]{1,0:T(8,128)S(1)}, f32[256,512]{1,0:T(8,128)S(1)}, u32[]{:S(2)}, u32[]{:S(2)}) %collective-permute-start.24) | collective-permute-done | bytes 524320 | tf_op jit(solution)/shard_map/link_relayed/ppermute | solution.py:328
  103.1 5.6 %collective-permute-done.28.refs_3_ = f32[256,512]{1,0:T(8,128)S(1)} collective-permute-done((f32[256,512]{1,0:T(8,128)S(1)}, f32[256,512]{1,0:T(8,128)S(1)}, u32[]{:S(2)}, u32[]{:S(2)}) %collective-permute-start.28) | collective-permute-done | bytes 524320 | tf_op jit(solution)/shard_map/link_relayed/ppermute | solution.py:328
  108.7 1.6 %assemble.4.refs_2_ = f32[512,3072]{1,0:T(8,128)} custom-call(s32[6]{0:T(128)S(1)} %bitcast.28, s32[1]{0:T(128)} %bitcast.1.me_ref, f32[512,512]{1,0:T(8,128)S(1)} %collective-permute-done.30.refs_0_, f32[512,512]{1,0:T(8,128)S(1)} %collective-permute-done.31.refs_1_, ...), custom_call_target="tpu_custom_call", output_to_operand_aliasing={{}: (6, {})} | custom-call | bytes 8388608 | tf_op jit(solution)/shard_map/assemble/pallas_call | solution.py:299
  110.7 1.5 %assemble.5 = f32[512,3072]{1,0:T(8,128)} custom-call(s32[6]{0:T(128)S(1)} %bitcast.29, s32[1]{0:T(128)} %bitcast.1.me_ref, f32[256,512]{1,0:T(8,128)S(1)} %collective-permute-done.27.refs_0_, f32[256,512]{1,0:T(8,128)S(1)} %collective-permute-done.29.refs_1_, f32[512,3072]{1,0:T(8,128)} %assemble.4.refs_2_), custom_call_target="tpu_custom_call", output_to_operand_aliasing={{}: (4, {})} | custom-call | bytes 2097152 | tf_op jit(solution)/shard_map/assemble/pallas_call | solution.py:299
  (61 shorter events, 12.0 us)
Async XLA Ops:
  3.2 2.3 %collective-permute-start.4 = (f32[256,512]{1,0:T(8,128)S(1)}, f32[256,512]{1,0:T(8,128)S(1)}, u32[]{:S(2)}, u32[]{:S(2)}) collective-permute-start(f32[256,512]{1,0:T(8,128)S(1)} %get-tuple-element.29), channel_id=1, source_target_pairs={{0,4},{4,0},{8,12},{12,8},{16,20},{20,16},{24,28},{28,24},{1,5},{5... | collective-permute-start | bytes 1572872 | tf_op jit(solution)/shard_map/core_corner/ppermute | solution.py:328
  3.8 5.1 %collective-permute-start.11 = (f32[256,512]{1,0:T(8,128)S(1)}, f32[256,512]{1,0:T(8,128)S(1)}, u32[]{:S(2)}, u32[]{:S(2)}) collective-permute-start(f32[256,512]{1,0:T(8,128)S(1)} %get-tuple-element.34), channel_id=1, source_target_pairs={{0,4},{4,0},{8,12},{12,8},{16,20},{20,16},{24,28},{28,24},{1,5},{5... | collective-permute-start | bytes 1572872 | tf_op jit(solution)/shard_map/core_corner/ppermute | solution.py:328
  3.8 5.7 %collective-permute-start.1 = (f32[256,512]{1,0:T(8,128)S(1)}, f32[256,512]{1,0:T(8,128)S(1)}, u32[]{:S(2)}, u32[]{:S(2)}) collective-permute-start(f32[256,512]{1,0:T(8,128)S(1)} %get-tuple-element.27), channel_id=1, source_target_pairs={{0,4},{4,0},{8,12},{12,8},{16,20},{20,16},{24,28},{28,24},{1,5},{5... | collective-permute-start | bytes 1572872 | tf_op jit(solution)/shard_map/core_straight/ppermute | solution.py:328
  4.3 6.9 %collective-permute-start.8 = (f32[256,512]{1,0:T(8,128)S(1)}, f32[256,512]{1,0:T(8,128)S(1)}, u32[]{:S(2)}, u32[]{:S(2)}) collective-permute-start(f32[256,512]{1,0:T(8,128)S(1)} %get-tuple-element.32), channel_id=1, source_target_pairs={{0,4},{4,0},{8,12},{12,8},{16,20},{20,16},{24,28},{28,24},{1,5},{5... | collective-permute-start | bytes 1572872 | tf_op jit(solution)/shard_map/core_straight/ppermute | solution.py:328
  5.0 7.4 %collective-permute-start.3 = (f32[256,512]{1,0:T(8,128)S(1)}, f32[256,512]{1,0:T(8,128)S(1)}, u32[]{:S(2)}, u32[]{:S(2)}) collective-permute-start(f32[256,512]{1,0:T(8,128)S(1)} %get-tuple-element.28), channel_id=1, source_target_pairs={{0,4},{4,0},{8,12},{12,8},{16,20},{20,16},{24,28},{28,24},{1,5},{5... | collective-permute-start | bytes 1572872 | tf_op jit(solution)/shard_map/core_side/ppermute | solution.py:328
  6.1 9.8 %collective-permute-start.5 = (f32[256,512]{1,0:T(8,128)S(1)}, f32[256,512]{1,0:T(8,128)S(1)}, u32[]{:S(2)}, u32[]{:S(2)}) collective-permute-start(f32[256,512]{1,0:T(8,128)S(1)} %add.10), channel_id=1, source_target_pairs={{0,8},{4,20},{8,0},{12,28},{16,24},{20,4},{24,16},{28,12},{1,9},{5... | collective-permute-start | bytes 1572872 | tf_op jit(solution)/shard_map/link_corner/ppermute | solution.py:328
  8.8 9.8 %collective-permute-start.10 = (f32[256,512]{1,0:T(8,128)S(1)}, f32[256,512]{1,0:T(8,128)S(1)}, u32[]{:S(2)}, u32[]{:S(2)}) collective-permute-start(f32[256,512]{1,0:T(8,128)S(1)} %get-tuple-element.33), channel_id=1, source_target_pairs={{0,4},{4,0},{8,12},{12,8},{16,20},{20,16},{24,28},{28,24},{1,5},{5... | collective-permute-start | bytes 1572872 | tf_op jit(solution)/shard_map/core_side/ppermute | solution.py:328
  9.6 12.0 %collective-permute-start.12 = (f32[256,512]{1,0:T(8,128)S(1)}, f32[256,512]{1,0:T(8,128)S(1)}, u32[]{:S(2)}, u32[]{:S(2)}) collective-permute-start(f32[256,512]{1,0:T(8,128)S(1)} %add.14), channel_id=1, source_target_pairs={{0,8},{4,20},{8,0},{12,28},{16,24},{20,4},{24,16},{28,12},{1,9},{5... | collective-permute-start | bytes 1572872 | tf_op jit(solution)/shard_map/link_corner/ppermute | solution.py:328
  11.1 13.1 %collective-permute-start = (f32[256,512]{1,0:T(8,128)S(1)}, f32[256,512]{1,0:T(8,128)S(1)}, u32[]{:S(2)}, u32[]{:S(2)}) collective-permute-start(f32[256,512]{1,0:T(8,128)S(1)} %get-tuple-element.26), channel_id=1, source_target_pairs={{0,4},{4,0},{8,12},{12,8},{16,20},{20,16},{24,28},{28,24},{1,5},{5... | collective-permute-start | bytes 1572872 | tf_op jit(solution)/shard_map/core_self/ppermute | solution.py:328
  12.5 18.5 %collective-permute-start.7 = (f32[256,512]{1,0:T(8,128)S(1)}, f32[256,512]{1,0:T(8,128)S(1)}, u32[]{:S(2)}, u32[]{:S(2)}) collective-permute-start(f32[256,512]{1,0:T(8,128)S(1)} %get-tuple-element.31), channel_id=1, source_target_pairs={{0,4},{4,0},{8,12},{12,8},{16,20},{20,16},{24,28},{28,24},{1,5},{5... | collective-permute-start | bytes 1572872 | tf_op jit(solution)/shard_map/core_self/ppermute | solution.py:328
  16.0 14.4 %collective-permute-start.2 = (f32[256,512]{1,0:T(8,128)S(1)}, f32[256,512]{1,0:T(8,128)S(1)}, u32[]{:S(2)}, u32[]{:S(2)}) collective-permute-start(f32[256,512]{1,0:T(8,128)S(1)} %add.8), channel_id=1, source_target_pairs={{0,8},{4,20},{8,0},{12,28},{16,24},{20,4},{24,16},{28,12},{1,9},{5... | collective-permute-start | bytes 1572872 | tf_op jit(solution)/shard_map/link_straight/ppermute | solution.py:328
  18.6 22.9 %collective-permute-start.9 = (f32[256,512]{1,0:T(8,128)S(1)}, f32[256,512]{1,0:T(8,128)S(1)}, u32[]{:S(2)}, u32[]{:S(2)}) collective-permute-start(f32[256,512]{1,0:T(8,128)S(1)} %add.12), channel_id=1, source_target_pairs={{0,8},{4,20},{8,0},{12,28},{16,24},{20,4},{24,16},{28,12},{1,9},{5... | collective-permute-start | bytes 1572872 | tf_op jit(solution)/shard_map/link_straight/ppermute | solution.py:328
  21.6 20.6 %collective-permute-start.6 = (f32[256,512]{1,0:T(8,128)S(1)}, f32[256,512]{1,0:T(8,128)S(1)}, u32[]{:S(2)}, u32[]{:S(2)}) collective-permute-start(f32[256,512]{1,0:T(8,128)S(1)} %add.11), channel_id=1, source_target_pairs={{0,16},{4,12},{8,24},{12,4},{16,0},{20,28},{24,8},{28,20},{1,17},{... | collective-permute-start | bytes 1572872 | tf_op jit(solution)/shard_map/side_side/ppermute | solution.py:328
  24.3 19.5 %collective-permute-start.13 = (f32[256,512]{1,0:T(8,128)S(1)}, f32[256,512]{1,0:T(8,128)S(1)}, u32[]{:S(2)}, u32[]{:S(2)}) collective-permute-start(f32[256,512]{1,0:T(8,128)S(1)} %add.15), channel_id=1, source_target_pairs={{0,16},{4,12},{8,24},{12,4},{16,0},{20,28},{24,8},{28,20},{1,17},{... | collective-permute-start | bytes 1572872 | tf_op jit(solution)/shard_map/side_side/ppermute | solution.py:328
  44.7 1.2 %collective-permute-start.14 = (f32[8,128]{1,0:T(8,128)S(1)}, f32[8,128]{1,0:T(8,128)S(1)}, u32[]{:S(2)}, u32[]{:S(2)}) collective-permute-start(f32[8,128]{1,0:T(8,128)S(1)} %get-tuple-element.37.refs_0_.block_norm_ref), channel_id=1, source_target_pairs={{0,4},{4,0},{8,12},{12,8},{16,20},{20,16},{24,28},{28,24},{1,5},{5... | collective-permute-start | bytes 12296 | tf_op jit(solution)/shard_map/core_norm/ppermute | solution.py:328
  45.9 3.6 %collective-permute-start.15 = (f32[8,128]{1,0:T(8,128)S(1)}, f32[8,128]{1,0:T(8,128)S(1)}, u32[]{:S(2)}, u32[]{:S(2)}) collective-permute-start(f32[8,128]{1,0:T(8,128)S(1)} %sum.2.refs_0_), channel_id=1, source_target_pairs={{0,8},{4,12},{8,0},{12,4},{16,24},{20,28},{24,16},{28,20},{1,9},{5... | collective-permute-start | bytes 12296 | tf_op jit(solution)/shard_map/chip_norm/ppermute | solution.py:328
  47.7 3.6 %collective-permute-start.16 = (f32[8,128]{1,0:T(8,128)S(1)}, f32[8,128]{1,0:T(8,128)S(1)}, u32[]{:S(2)}, u32[]{:S(2)}) collective-permute-start(f32[8,128]{1,0:T(8,128)S(1)} %sum.2.refs_0_), channel_id=1, source_target_pairs={{0,16},{4,20},{8,24},{12,28},{16,0},{20,4},{24,8},{28,12},{1,17},{... | collective-permute-start | bytes 12296 | tf_op jit(solution)/shard_map/chip_norm/ppermute | solution.py:328
  49.2 4.5 %collective-permute-start.17 = (f32[8,128]{1,0:T(8,128)S(1)}, f32[8,128]{1,0:T(8,128)S(1)}, u32[]{:S(2)}, u32[]{:S(2)}) collective-permute-start(f32[8,128]{1,0:T(8,128)S(1)} %sum.2.refs_0_), channel_id=1, source_target_pairs={{0,24},{4,28},{8,16},{12,20},{16,8},{20,12},{24,0},{28,4},{1,25},{... | collective-permute-start | bytes 12296 | tf_op jit(solution)/shard_map/chip_norm/ppermute | solution.py:328
  53.7 6.2 %collective-permute-start.18 = (f32[8,128]{1,0:T(8,128)S(1)}, f32[8,128]{1,0:T(8,128)S(1)}, u32[]{:S(2)}, u32[]{:S(2)}) collective-permute-start(f32[8,128]{1,0:T(8,128)S(1)} %sum.3.refs_0_), channel_id=1, source_target_pairs={{0,1},{1,0},{2,3},{3,2},{4,5},{5,4},{6,7},{7,6},{8,9},{9,8},{10,11... | collective-permute-start | bytes 12296 | tf_op jit(solution)/shard_map/group_norm/ppermute | solution.py:376
  55.3 4.7 %collective-permute-start.19 = (f32[8,128]{1,0:T(8,128)S(1)}, f32[8,128]{1,0:T(8,128)S(1)}, u32[]{:S(2)}, u32[]{:S(2)}) collective-permute-start(f32[8,128]{1,0:T(8,128)S(1)} %sum.3.refs_0_), channel_id=1, source_target_pairs={{0,2},{1,3},{2,0},{3,1},{4,6},{5,7},{6,4},{7,5},{8,10},{9,11},{10,... | collective-permute-start | bytes 12296 | tf_op jit(solution)/shard_map/group_norm/ppermute | solution.py:376
  57.9 5.4 %collective-permute-start.20 = (f32[8,128]{1,0:T(8,128)S(1)}, f32[8,128]{1,0:T(8,128)S(1)}, u32[]{:S(2)}, u32[]{:S(2)}) collective-permute-start(f32[8,128]{1,0:T(8,128)S(1)} %sum.3.refs_0_), channel_id=1, source_target_pairs={{0,3},{1,2},{2,1},{3,0},{4,7},{5,6},{6,5},{7,4},{8,11},{9,10},{10,... | collective-permute-start | bytes 12296 | tf_op jit(solution)/shard_map/group_norm/ppermute | solution.py:376
  71.3 9.3 %collective-permute-start.22 = (f32[512,512]{1,0:T(8,128)S(1)}, f32[512,512]{1,0:T(8,128)S(1)}, u32[]{:S(2)}, u32[]{:S(2)}) collective-permute-start(f32[512,512]{1,0:T(8,128)S(1)} %get-tuple-element.41.refs_0_), channel_id=1, source_target_pairs={{0,4},{4,0},{8,12},{12,8},{16,20},{20,16},{24,28},{28,24},{1,5},{5... | collective-permute-start | bytes 3145736 | tf_op jit(solution)/shard_map/core_own/ppermute | solution.py:328
  71.4 9.2 %collective-permute-start.21 = (f32[256,512]{1,0:T(8,128)S(1)}, f32[256,512]{1,0:T(8,128)S(1)}, u32[]{:S(2)}, u32[]{:S(2)}) collective-permute-start(f32[256,512]{1,0:T(8,128)S(1)} %get-tuple-element.40), channel_id=1, source_target_pairs={{0,8},{4,20},{8,0},{12,28},{16,24},{20,4},{24,16},{28,12},{1,9},{5... | collective-permute-start | bytes 1572872 | tf_op jit(solution)/shard_map/link_own/ppermute | solution.py:328
  72.0 14.3 %collective-permute-start.25 = (f32[256,512]{1,0:T(8,128)S(1)}, f32[256,512]{1,0:T(8,128)S(1)}, u32[]{:S(2)}, u32[]{:S(2)}) collective-permute-start(f32[256,512]{1,0:T(8,128)S(1)} %get-tuple-element.43), channel_id=1, source_target_pairs={{0,8},{4,20},{8,0},{12,28},{16,24},{20,4},{24,16},{28,12},{1,9},{5... | collective-permute-start | bytes 1572872 | tf_op jit(solution)/shard_map/link_own/ppermute | solution.py:328
  80.7 16.8 %collective-permute-start.30 = (f32[512,512]{1,0:T(8,128)S(1)}, f32[512,512]{1,0:T(8,128)S(1)}, u32[]{:S(2)}, u32[]{:S(2)}) collective-permute-start(f32[512,512]{1,0:T(8,128)S(1)} %collective-permute-done.22.refs_1_), channel_id=1, source_target_pairs={{0,8},{4,20},{8,0},{12,28},{16,24},{20,4},{24,16},{28,12},{1,9},{5... | collective-permute-start | bytes 3145736 | tf_op jit(solution)/shard_map/link_sibling/ppermute | solution.py:328
  81.2 5.1 %collective-permute-start.23 = (f32[256,512]{1,0:T(8,128)S(1)}, f32[256,512]{1,0:T(8,128)S(1)}, u32[]{:S(2)}, u32[]{:S(2)}) collective-permute-start(f32[256,512]{1,0:T(8,128)S(1)} %collective-permute-done.21.refs_2_), channel_id=1, source_target_pairs={{0,4},{4,0},{8,12},{12,8},{16,20},{20,16},{24,28},{28,24},{1,5},{5... | collective-permute-start | bytes 1572872 | tf_op jit(solution)/shard_map/core_first/ppermute | solution.py:328
  86.3 11.2 %collective-permute-start.26 = (f32[256,512]{1,0:T(8,128)S(1)}, f32[256,512]{1,0:T(8,128)S(1)}, u32[]{:S(2)}, u32[]{:S(2)}) collective-permute-start(f32[256,512]{1,0:T(8,128)S(1)} %collective-permute-done.25.refs_3_), channel_id=1, source_target_pairs={{0,4},{4,0},{8,12},{12,8},{16,20},{20,16},{24,28},{28,24},{1,5},{5... | collective-permute-start | bytes 1572872 | tf_op jit(solution)/shard_map/core_first/ppermute | solution.py:328
  86.3 16.8 %collective-permute-start.24 = (f32[256,512]{1,0:T(8,128)S(1)}, f32[256,512]{1,0:T(8,128)S(1)}, u32[]{:S(2)}, u32[]{:S(2)}) collective-permute-start(f32[256,512]{1,0:T(8,128)S(1)} %collective-permute-done.23.refs_4_), channel_id=1, source_target_pairs={{0,8},{4,20},{8,0},{12,28},{16,24},{20,4},{24,16},{28,12},{1,9},{5... | collective-permute-start | bytes 1572872 | tf_op jit(solution)/shard_map/link_relayed/ppermute | solution.py:328
  97.5 11.2 %collective-permute-start.31 = (f32[512,512]{1,0:T(8,128)S(1)}, f32[512,512]{1,0:T(8,128)S(1)}, u32[]{:S(2)}, u32[]{:S(2)}) collective-permute-start(f32[512,512]{1,0:T(8,128)S(1)} %collective-permute-done.30.refs_0_), channel_id=1, source_target_pairs={{0,4},{4,0},{8,12},{12,8},{16,20},{20,16},{24,28},{28,24},{1,5},{5... | collective-permute-start | bytes 3145736 | tf_op jit(solution)/shard_map/core_second/ppermute | solution.py:328
  97.5 11.2 %collective-permute-start.28 = (f32[256,512]{1,0:T(8,128)S(1)}, f32[256,512]{1,0:T(8,128)S(1)}, u32[]{:S(2)}, u32[]{:S(2)}) collective-permute-start(f32[256,512]{1,0:T(8,128)S(1)} %collective-permute-done.26.refs_5_), channel_id=1, source_target_pairs={{0,8},{4,20},{8,0},{12,28},{16,24},{20,4},{24,16},{28,12},{1,9},{5... | collective-permute-start | bytes 1572872 | tf_op jit(solution)/shard_map/link_relayed/ppermute | solution.py:328
  103.1 7.2 %collective-permute-start.27 = (f32[256,512]{1,0:T(8,128)S(1)}, f32[256,512]{1,0:T(8,128)S(1)}, u32[]{:S(2)}, u32[]{:S(2)}) collective-permute-start(f32[256,512]{1,0:T(8,128)S(1)} %collective-permute-done.24.refs_2_), channel_id=1, source_target_pairs={{0,4},{4,0},{8,12},{12,8},{16,20},{20,16},{24,28},{28,24},{1,5},{5... | collective-permute-start | bytes 1572872 | tf_op jit(solution)/shard_map/core_relayed/ppermute | solution.py:328
  108.7 1.9 %collective-permute-start.29 = (f32[256,512]{1,0:T(8,128)S(1)}, f32[256,512]{1,0:T(8,128)S(1)}, u32[]{:S(2)}, u32[]{:S(2)}) collective-permute-start(f32[256,512]{1,0:T(8,128)S(1)} %collective-permute-done.28.refs_3_), channel_id=1, source_target_pairs={{0,4},{4,0},{8,12},{12,8},{16,20},{20,16},{24,28},{28,24},{1,5},{5... | collective-permute-start | bytes 1572872 | tf_op jit(solution)/shard_map/core_relayed/ppermute | solution.py:328
  (5 other events, 101.9 us)

commit v9 on v8

--- a/solution.py
+++ b/solution.py
@@ -89,6 +89,18 @@
     return jnp.dot(left_side, right_side, preferred_element_type=F32)
 
 
+def mirrored(upper, corner):
+    half = corner.shape[0]
+    lower = jnp.concatenate([upper[:, half:].T, corner], axis=1)
+    return jnp.concatenate([upper, lower], axis=0)
+
+
+def symmetric_dot(left_side, right_side):
+    half = left_side.shape[0] // 2
+    upper = triple_dot(left_side[:half], right_side)
+    return mirrored(upper, triple_dot(left_side[half:], right_side[:, half:]))
+
+
 def add_identity(value, amount):
     tile = 128
     rows = lax.broadcasted_iota(jnp.int32, (tile, tile), 0)
@@ -213,14 +225,18 @@
 
 
 def gram_kernel(upper_ref, lower_ref, left_ref, right_ref):
-    block = whole_block((upper_ref, lower_ref))
-    high, low = split(block)
-    across = jnp.concatenate([high, high, low], axis=1)
-    across_other = jnp.concatenate([high, low, high], axis=1)
-    down = jnp.concatenate([high, high, low], axis=0)
-    down_other = jnp.concatenate([high, low, high], axis=0)
-    left_ref[...] = lax.dot_general(across, across_other, (((1,), (1,)), ((), ())), preferred_element_type=F32)
-    right_ref[...] = lax.dot_general(down, down_other, (((0,), (0,)), ((), ())), preferred_element_type=F32)
+    high, low = split(whole_block((upper_ref, lower_ref)))
+    for axis, out_ref in ((1, left_ref), (0, right_ref)):
+        first = jnp.concatenate([high, high, low], axis=axis)
+        second = jnp.concatenate([high, low, high], axis=axis)
+        half = high.shape[0] // 2
+        dims = (((axis,), (axis,)), ((), ()))
+        first_upper = first[:half] if axis == 1 else first[:, :half]
+        first_lower = first[half:] if axis == 1 else first[:, half:]
+        second_lower = second[half:] if axis == 1 else second[:, half:]
+        upper = lax.dot_general(first_upper, second, dims, preferred_element_type=F32)
+        corner = lax.dot_general(first_lower, second_lower, dims, preferred_element_type=F32)
+        out_ref[...] = mirrored(upper, corner)
 
 
 def gram_call(block):
@@ -229,29 +245,59 @@
     return local_call(gram_kernel, "gram", [shape, shape], block, flops=12 * width**3, vmem=LARGE)
 
 
-def roots_of(previous, grams, gram_scale):
-    statistics = [0.5 * prev + gram * gram_scale for prev, gram in zip(previous, grams)]
-    frobenius = [jnp.sqrt(jnp.sum(value * value, keepdims=True).reshape(1, 1)) for value in statistics]
-    scaled = [value * (1.0 / norm) for value, norm in zip(statistics, frobenius)]
-    square = [triple_dot(left_operand(value), right_operand(value)) for value in scaled]
-    factor_square = [add_identity(0.0625 * q - 0.625 * m, 1.5625) for q, m in zip(square, scaled)]
-    factor_scaled = [1.25 * m - 0.25 * q for q, m in zip(square, scaled)]
-    fourth = [triple_dot(left_operand(value), right_operand(value)) for value in factor_square]
-    tail = [triple_dot(left_operand(f), right_operand(m)) for f, m in zip(fourth, factor_scaled)]
-    roots = [add_identity(-1.25 * m - t, 6.25) for m, t in zip(scaled, tail)]
-    return roots, [0.25 * lax.rsqrt(jnp.sqrt(norm)) for norm in frobenius]
-
-
-def update_call(block, block_norm, left_gram, right_gram, left_prev, right_prev, norms, entry_count):
+def square_kernel(*refs):
+    for ref, out_ref in zip(refs[: len(refs) // 2], refs[len(refs) // 2 :]):
+        value = ref[...]
+        out_ref[...] = symmetric_dot(left_operand(value), right_operand(value))
+
+
+def square_call(*statistics):
+    shapes = [jax.ShapeDtypeStruct(value.shape, F32) for value in statistics]
+    flops = 6 * len(statistics) * statistics[0].shape[0] ** 3
+    return local_call(square_kernel, "square", shapes, statistics, flops=flops, vmem=LARGE)
+
+
+def mix_kernel(previous_ref, gram_ref, mixed_ref, square_ref):
+    gram = gram_ref[...]
+    gram_right = right_operand(gram)
+    product = triple_dot(left_operand(previous_ref[...]), gram_right)
+    square_ref[...] = symmetric_dot(left_operand(gram), gram_right)
+    mixed_ref[...] = product + product.T
+
+
+def mix_call(previous, gram):
+    shape = jax.ShapeDtypeStruct(gram.shape, F32)
+    flops = 12 * gram.shape[0] ** 3
+    return local_call(mix_kernel, "mix", [shape, shape], (previous, gram), flops=flops, vmem=LARGE)
+
+
+def roots_of(sides, gram_scale):
+    statistics = [0.5 * previous[...] + gram[...] * gram_scale for previous, gram, _, _, _ in sides]
+    norms = [jnp.sum(value * value, keepdims=True).reshape(1, 1) for value in statistics]
+    factor_square, factor_scaled, kept = [], [], []
+    for statistic, norm, (_, _, previous_square, mixed, gram_square) in zip(statistics, norms, sides):
+        inverse = 1.0 / norm
+        scaled = statistic * jnp.sqrt(inverse)
+        square = previous_square[...] * (0.25 * inverse) + mixed[...] * (0.5 * gram_scale * inverse)
+        square = square + gram_square[...] * (gram_scale * gram_scale * inverse)
+        factor_square.append(add_identity(0.0625 * square - 0.625 * scaled, 1.5625))
+        factor_scaled.append(1.25 * scaled - 0.25 * square)
+        kept.append(scaled)
+    fourth = [symmetric_dot(left_operand(value), right_operand(value)) for value in factor_square]
+    tail = [symmetric_dot(left_operand(f), right_operand(m)) for f, m in zip(fourth, factor_scaled)]
+    roots = [add_identity(-1.25 * m - t, 6.25) for m, t in zip(kept, tail)]
+    return roots, [0.25 * lax.rsqrt(jnp.sqrt(jnp.sqrt(norm))) for norm in norms]
+
+
+def update_call(block, block_norm, left, right, norms, entry_count):
     width = block[0].shape[1]
 
-    def kernel(upper_ref, lower_ref, block_norm_ref, left_gram_ref, right_gram_ref, left_ref, right_ref, *refs):
-        norm_refs, out_refs = refs[:-3], refs[-3:]
+    def kernel(upper_ref, lower_ref, block_norm_ref, *refs):
+        left_refs, right_refs, norm_refs, out_refs = refs[:5], refs[5:10], refs[10:-3], refs[-3:]
         squares = sum(ref[:1, :1] for ref in norm_refs)
         clip_factor = jnp.minimum(1.0, clip_level / jnp.sqrt(squares / entry_count))
         gram_scale = clip_factor * clip_factor / width
-        previous, grams = (left_ref[...], right_ref[...]), (left_gram_ref[...], right_gram_ref[...])
-        roots, scales = roots_of(previous, grams, gram_scale)
+        roots, scales = roots_of((left_refs, right_refs), gram_scale)
         halfway = triple_dot(left_operand(roots[0]), right_operand(whole_block((upper_ref, lower_ref))))
         pre = triple_dot(left_operand(halfway), right_operand(roots[1]))
         pre_scale = scales[0] * scales[1] * clip_factor
@@ -262,9 +308,9 @@
         for half in HALVES:
             out_refs[1 + half][...] = update[half * (width // 2) : (half + 1) * (width // 2)]
 
-    operands = (*block, block_norm, left_gram, right_gram, left_prev, right_prev, *norms)
+    operands = (*block, block_norm, *left, *right, *norms)
     shapes = [piece_shape(half, width) for half in (None, *HALVES)]
-    return local_call(kernel, "update", shapes, operands, flops=48 * width**3, vmem=LARGE)
+    return local_call(kernel, "update", shapes, operands, flops=36 * width**3, vmem=LARGE)
 
 
 def assemble_call(owners, me, places, slots, block_count, started):
@@ -361,23 +407,27 @@
     totals = [
         own_plus("self", half, from_core["self", half], from_link["straight", half]) for half in HALVES
     ]
+    sides = [(left_stats[0],), (right_stats[0],)]
+    squares = square_call(*[after(previous, totals[0]) for previous, in sides])
+    totals[0] = after(totals[0], *squares)
     norm, block = None, []
     for half in HALVES:
         joined, norm = join_call(owner_row, me, totals[half], half, arrived[half], norm, block_count)
         block.append(joined)
     block_norm = norm
     norm = sum_call(norm, to_core(norm, "norm"))
-    norm = sum_call(norm, *[over(flipped(mask), norm, "chip_norm") for mask in (2, 4, 6)])
+    chip_norms = [over(flipped(mask), norm, "chip_norm") for mask in (2, 4, 6)]
+    grams = gram_call([after(block[0], norm), block[1]])
+    sides = [(previous, gram, square) for (previous,), gram, square in zip(sides, grams, squares)]
+    sides[0] += tuple(mix_call(*sides[0][:2]))
+    norm = sum_call(after(norm, sides[0][4]), *chip_norms)
     norms = [norm]
     for shift in range(1, group_count):
-        both_ways = group_count & (group_count - 1) == 0
-        pairs = [(i, i ^ shift if both_ways else (i + shift) % group_count) for i in range(group_count)]
+        pairs = [(i, (i + shift) % group_count) for i in range(group_count)]
         with jax.named_scope("group_norm"):
             norms.append(lax.ppermute(norm, "mp", pairs))
-    left_gram, right_gram = gram_call(block)
-    whole, *own = update_call(
-        block, block_norm, left_gram, right_gram, left_stats[0], right_stats[0], norms, entry_count
-    )
+    sides[1] += tuple(mix_call(*sides[1][:2]))
+    whole, *own = update_call(block, block_norm, *sides, norms, entry_count)
 
     core_own = to_core(whole, "own")
     first = [to_link(value, "own") for value in own]

time: 113 us -> 109 us (0.965)
  waiting for transfers between devices: 63.3 us -> 54.9 us
  Pallas kernels: 23.5 us -> 25.9 us
  starting transfers between devices: 22.6 us -> 24.6 us
    ppermute x29, waiting for transfers between devices: 60 us -> 54.4 us  [over(): return lax.ppermute(value, 'dp', pairs)]
    ppermute x3, waiting for transfers between devices: 3.33 us -> 0.53 us  [paired_body(): norms.append(lax.ppermute(norm, 'mp', pairs))]
    pallas_call x16 -> x19, Pallas kernels: 17.8 us -> 20.2 us  [local_call(): pl.pallas_call(kernel, in_specs=[pl.BlockSpec(memory_space=pltpu.SMEM)] *...]
    unnamed x10 -> x12, local copies, waits for them, and re-layouts: 2.56 us -> 2.56 us
  transfers between devices with their start and end apart: 32 -> 32, of which waited for: 16 -> 14; matrix products, arithmetic and copies ran while one was open for 0% -> 0% of each run, Pallas kernels for 11% -> 16%
where the time goes in v9:
time: 109 us; the launch traced here: 108 us
  waiting for transfers between devices  54.9 us (50%)
  Pallas kernels  25.9 us (24%)
  starting transfers between devices  24.6 us (23%)
  local copies, waits for them, and re-layouts  2.56 us (2%)
    ppermute x29, waiting for transfers between devices, over(): return lax.ppermute(value, 'dp', pairs)  54.4 us
    pallas_call x19, Pallas kernels, local_call(): pl.pallas_call(kernel, in_specs=[pl.BlockSpec(memory_space=pltpu.SMEM)] *...  20.2 us
    ppermute x29, starting transfers between devices, over(): return lax.ppermute(value, 'dp', pairs)  19.1 us
    pallas_call x3, Pallas kernels, assemble_call(): pl.pallas_call(kernel, in_specs=in_specs, out_specs=pl.BlockSpec(memory_s...  5.72 us
    ppermute x3, starting transfers between devices, paired_body(): norms.append(lax.ppermute(norm, 'mp', pairs))  5.51 us
    unnamed x12, local copies, waits for them, and re-layouts  2.56 us
  transfers between devices with their start and end apart: 32, of which 14 were waited for; matrix products, arithmetic and copies ran while one was open for 0% of the time, Pallas kernels for 16%

profile of v9, /device:TPU:0, one launch (start us, length us, event | category | flops | bytes accessed | tf_op | source)
XLA Modules:
  0.0 108.4 jit_solution(16485836676286770944)
XLA Ops:
  0.0 1.9 %copy-done = bf16[1,512,3072]{2,1,0:T(8,128)(2,1)S(1)} copy-done((bf16[1,512,3072]{2,1,0:T(8,128)(2,1)S(1)}, bf16[1,512,3072]{2,1,0:T(8,128)(2,1)}, u32[]{:S(2)}) %copy-start) | copy-done | bytes 3145752
  6.1 2.7 %collective-permute-start.5 = (f32[256,512]{1,0:T(8,128)S(1)}, f32[256,512]{1,0:T(8,128)S(1)}, u32[]{:S(2)}, u32[]{:S(2)}) collective-permute-start(f32[256,512]{1,0:T(8,128)S(1)} %add.10), channel_id=1, source_target_pairs={{0,8},{4,20},{8,0},{12,28},{16,24},{20,4},{24,16},{28,12},{1,9},{5... | collective-permute-start | bytes 1572872 | tf_op jit(solution)/shard_map/link_corner/ppermute | solution.py:374
  9.6 1.6 %collective-permute-start.12 = (f32[256,512]{1,0:T(8,128)S(1)}, f32[256,512]{1,0:T(8,128)S(1)}, u32[]{:S(2)}, u32[]{:S(2)}) collective-permute-start(f32[256,512]{1,0:T(8,128)S(1)} %add.14), channel_id=1, source_target_pairs={{0,8},{4,20},{8,0},{12,28},{16,24},{20,4},{24,16},{28,12},{1,9},{5... | collective-permute-start | bytes 1572872 | tf_op jit(solution)/shard_map/link_corner/ppermute | solution.py:374
  13.1 2.9 %collective-permute-done.5.refs_1_ = f32[256,512]{1,0:T(8,128)S(1)} collective-permute-done((f32[256,512]{1,0:T(8,128)S(1)}, f32[256,512]{1,0:T(8,128)S(1)}, u32[]{:S(2)}, u32[]{:S(2)}) %collective-permute-start.5) | collective-permute-done | bytes 524320 | tf_op jit(solution)/shard_map/link_corner/ppermute | solution.py:374
  16.6 2.1 %collective-permute-start.9 = (f32[256,512]{1,0:T(8,128)S(1)}, f32[256,512]{1,0:T(8,128)S(1)}, u32[]{:S(2)}, u32[]{:S(2)}) collective-permute-start(f32[256,512]{1,0:T(8,128)S(1)} %add.12), channel_id=1, source_target_pairs={{0,8},{4,20},{8,0},{12,28},{16,24},{20,4},{24,16},{28,12},{1,9},{5... | collective-permute-start | bytes 1572872 | tf_op jit(solution)/shard_map/link_straight/ppermute | solution.py:374
  18.7 2.9 %collective-permute-done.12.refs_1_ = f32[256,512]{1,0:T(8,128)S(1)} collective-permute-done((f32[256,512]{1,0:T(8,128)S(1)}, f32[256,512]{1,0:T(8,128)S(1)}, u32[]{:S(2)}, u32[]{:S(2)}) %collective-permute-start.12) | collective-permute-done | bytes 524320 | tf_op jit(solution)/shard_map/link_corner/ppermute | solution.py:374
  21.6 2.0 %collective-permute-start.6 = (f32[256,512]{1,0:T(8,128)S(1)}, f32[256,512]{1,0:T(8,128)S(1)}, u32[]{:S(2)}, u32[]{:S(2)}) collective-permute-start(f32[256,512]{1,0:T(8,128)S(1)} %add.11), channel_id=1, source_target_pairs={{0,16},{4,12},{8,24},{12,4},{16,0},{20,28},{24,8},{28,20},{1,17},{... | collective-permute-start | bytes 1572872 | tf_op jit(solution)/shard_map/side_side/ppermute | solution.py:374
  24.4 5.9 %collective-permute-done.2.refs_1_ = f32[256,512]{1,0:T(8,128)S(1)} collective-permute-done((f32[256,512]{1,0:T(8,128)S(1)}, f32[256,512]{1,0:T(8,128)S(1)}, u32[]{:S(2)}, u32[]{:S(2)}) %collective-permute-start.2) | collective-permute-done | bytes 524320 | tf_op jit(solution)/shard_map/link_straight/ppermute | solution.py:374
  31.0 1.5 %square.1 = (f32[512,512]{1,0:T(8,128)S(1)}, f32[512,512]{1,0:T(8,128)S(1)}) custom-call(f32[512,512]{1,0:T(8,128)S(1)} %bitcast.30, f32[512,512]{1,0:T(8,128)S(1)} %bitcast.33), custom_call_target="tpu_custom_call" | custom-call | flops 1610612736 | bytes 4194304 | tf_op jit(solution)/shard_map/square/pallas_call | solution.py:128
  32.4 9.1 %collective-permute-done.9.refs_1_ = f32[256,512]{1,0:T(8,128)S(1)} collective-permute-done((f32[256,512]{1,0:T(8,128)S(1)}, f32[256,512]{1,0:T(8,128)S(1)}, u32[]{:S(2)}, u32[]{:S(2)}) %collective-permute-start.9) | collective-permute-done | bytes 524320 | tf_op jit(solution)/shard_map/link_straight/ppermute | solution.py:374
  42.2 0.9 join.2
  43.8 0.9 join.3
  44.8 1.1 collective-permute-done.14.refs_1_
  45.9 1.8 %collective-permute-start.15 = (f32[8,128]{1,0:T(8,128)S(1)}, f32[8,128]{1,0:T(8,128)S(1)}, u32[]{:S(2)}, u32[]{:S(2)}) collective-permute-start(f32[8,128]{1,0:T(8,128)S(1)} %sum.2.refs_0_), channel_id=1, source_target_pairs={{0,8},{4,12},{8,0},{12,4},{16,24},{20,28},{24,16},{28,20},{1,9},{5... | collective-permute-start | bytes 12296 | tf_op jit(solution)/shard_map/chip_norm/ppermute | solution.py:374
  47.7 1.5 %collective-permute-start.16 = (f32[8,128]{1,0:T(8,128)S(1)}, f32[8,128]{1,0:T(8,128)S(1)}, u32[]{:S(2)}, u32[]{:S(2)}) collective-permute-start(f32[8,128]{1,0:T(8,128)S(1)} %sum.2.refs_0_), channel_id=1, source_target_pairs={{0,16},{4,20},{8,24},{12,28},{16,0},{20,4},{24,8},{28,12},{1,17},{... | collective-permute-start | bytes 12296 | tf_op jit(solution)/shard_map/chip_norm/ppermute | solution.py:374
  49.4 1.5 %gram.1 = (f32[512,512]{1,0:T(8,128)S(1)}, f32[512,512]{1,0:T(8,128)S(1)}) custom-call(f32[256,512]{1,0:T(8,128)S(1)} %get-tuple-element.54.upper_ref, f32[256,512]{1,0:T(8,128)S(1)} %get-tuple-element.52.lower_ref), custom_call_target="tpu_custom_call" | custom-call | flops 1610612736 | bytes 3145728 | tf_op jit(solution)/shard_map/gram/pallas_call | solution.py:128
  50.9 1.7 %mix.2 = (f32[512,512]{1,0:T(8,128)S(1)}, f32[512,512]{1,0:T(8,128)S(1)}) custom-call(f32[512,512]{1,0:T(8,128)S(1)} %bitcast.31, f32[512,512]{1,0:T(8,128)S(1)} %get-tuple-element.55.gram_ref.refs_1_), custom_call_target="tpu_custom_call" | custom-call | flops 1610612736 | bytes 4194304 | tf_op jit(solution)/shard_map/mix/pallas_call | solution.py:128
  52.6 1.1 %collective-permute-done.17.refs_3_ = f32[8,128]{1,0:T(8,128)S(1)} collective-permute-done((f32[8,128]{1,0:T(8,128)S(1)}, f32[8,128]{1,0:T(8,128)S(1)}, u32[]{:S(2)}, u32[]{:S(2)}) %collective-permute-start.17) | collective-permute-done | bytes 4128 | tf_op jit(solution)/shard_map/chip_norm/ppermute | solution.py:374
  53.7 1.6 %collective-permute-start.18 = (f32[8,128]{1,0:T(8,128)S(1)}, f32[8,128]{1,0:T(8,128)S(1)}, u32[]{:S(2)}, u32[]{:S(2)}) collective-permute-start(f32[8,128]{1,0:T(8,128)S(1)} %sum.3.refs_10_), channel_id=1, source_target_pairs={{0,1},{1,2},{2,3},{3,0},{4,5},{5,6},{6,7},{7,4},{8,9},{9,10},{10,1... | collective-permute-start | bytes 12296 | tf_op jit(solution)/shard_map/group_norm/ppermute | solution.py:428
  55.3 2.6 %collective-permute-start.19 = (f32[8,128]{1,0:T(8,128)S(1)}, f32[8,128]{1,0:T(8,128)S(1)}, u32[]{:S(2)}, u32[]{:S(2)}) collective-permute-start(f32[8,128]{1,0:T(8,128)S(1)} %sum.3.refs_10_), channel_id=1, source_target_pairs={{0,2},{1,3},{2,0},{3,1},{4,6},{5,7},{6,4},{7,5},{8,10},{9,11},{10,... | collective-permute-start | bytes 12296 | tf_op jit(solution)/shard_map/group_norm/ppermute | solution.py:428
  57.9 1.3 %collective-permute-start.20 = (f32[8,128]{1,0:T(8,128)S(1)}, f32[8,128]{1,0:T(8,128)S(1)}, u32[]{:S(2)}, u32[]{:S(2)}) collective-permute-start(f32[8,128]{1,0:T(8,128)S(1)} %sum.3.refs_10_), channel_id=1, source_target_pairs={{0,3},{1,0},{2,1},{3,2},{4,7},{5,4},{6,5},{7,6},{8,11},{9,8},{10,9... | collective-permute-start | bytes 12296 | tf_op jit(solution)/shard_map/group_norm/ppermute | solution.py:428
  59.2 1.7 %mix.3 = (f32[512,512]{1,0:T(8,128)S(1)}, f32[512,512]{1,0:T(8,128)S(1)}) custom-call(f32[512,512]{1,0:T(8,128)S(1)} %bitcast.34, f32[512,512]{1,0:T(8,128)S(1)} %get-tuple-element.58.gram_ref.refs_6_), custom_call_target="tpu_custom_call" | custom-call | flops 1610612736 | bytes 4194304 | tf_op jit(solution)/shard_map/mix/pallas_call | solution.py:128
  61.5 5.9 %update.1 = (f32[512,512]{1,0:T(8,128)S(1)}, f32[256,512]{1,0:T(8,128)S(1)}, f32[256,512]{1,0:T(8,128)S(1)}) custom-call(f32[256,512]{1,0:T(8,128)S(1)} %get-tuple-element.54.upper_ref, f32[256,512]{1,0:T(8,128)S(1)} %get-tuple-element.52.lower_ref, f32[8,128]{1,0:T(8,128)S(1)} %get-tuple-element.53.refs_0_.block_norm_ref, f32[512,512]{1,0:T(8,128)S(1)} %bitcast.32, ...), custom_call_target="tpu_custom_call" | custom-call | flops 4831838208 | bytes 13651968 | tf_op jit(solution)/shard_map/update/pallas_call | solution.py:128
  68.3 1.3 %collective-permute-start.25 = (f32[256,512]{1,0:T(8,128)S(1)}, f32[256,512]{1,0:T(8,128)S(1)}, u32[]{:S(2)}, u32[]{:S(2)}) collective-permute-start(f32[256,512]{1,0:T(8,128)S(1)} %get-tuple-element.65), channel_id=1, source_target_pairs={{0,8},{4,20},{8,0},{12,28},{16,24},{20,4},{24,16},{28,12},{1,9},{5... | collective-permute-start | bytes 1572872 | tf_op jit(solution)/shard_map/link_own/ppermute | solution.py:374
  69.6 7.2 %collective-permute-done.21.refs_2_ = f32[256,512]{1,0:T(8,128)S(1)} collective-permute-done((f32[256,512]{1,0:T(8,128)S(1)}, f32[256,512]{1,0:T(8,128)S(1)}, u32[]{:S(2)}, u32[]{:S(2)}) %collective-permute-start.21) | collective-permute-done | bytes 524320 | tf_op jit(solution)/shard_map/link_own/ppermute | solution.py:374
  77.5 4.8 %collective-permute-done.25.refs_3_ = f32[256,512]{1,0:T(8,128)S(1)} collective-permute-done((f32[256,512]{1,0:T(8,128)S(1)}, f32[256,512]{1,0:T(8,128)S(1)}, u32[]{:S(2)}, u32[]{:S(2)}) %collective-permute-start.25) | collective-permute-done | bytes 524320 | tf_op jit(solution)/shard_map/link_own/ppermute | solution.py:374
  83.1 10.5 %collective-permute-done.30.refs_0_ = f32[512,512]{1,0:T(8,128)S(1)} collective-permute-done((f32[512,512]{1,0:T(8,128)S(1)}, f32[512,512]{1,0:T(8,128)S(1)}, u32[]{:S(2)}, u32[]{:S(2)}) %collective-permute-start.30) | collective-permute-done | bytes 1048608 | tf_op jit(solution)/shard_map/link_sibling/ppermute | solution.py:374
  94.4 2.6 %assemble.3.refs_4_ = f32[512,3072]{1,0:T(8,128)} custom-call(s32[6]{0:T(128)S(1)} %bitcast.27, s32[1]{0:T(128)} %bitcast.1.me_ref, f32[512,512]{1,0:T(8,128)S(1)} %get-tuple-element.63.refs_0_, f32[512,512]{1,0:T(8,128)S(1)} %collective-permute-done.22.refs_1_, f32[256,512]{1,0:T(8,128)S(1)} %collective-permute-done.21.refs_2_, ...), custom_call_target="tpu_custom_call" | custom-call | bytes 12582912 | tf_op jit(solution)/shard_map/assemble/pallas_call | solution.py:345
  97.0 2.2 %collective-permute-done.24.refs_2_ = f32[256,512]{1,0:T(8,128)S(1)} collective-permute-done((f32[256,512]{1,0:T(8,128)S(1)}, f32[256,512]{1,0:T(8,128)S(1)}, u32[]{:S(2)}, u32[]{:S(2)}) %collective-permute-start.24) | collective-permute-done | bytes 524320 | tf_op jit(solution)/shard_map/link_relayed/ppermute | solution.py:374
  99.2 5.6 %collective-permute-done.28.refs_3_ = f32[256,512]{1,0:T(8,128)S(1)} collective-permute-done((f32[256,512]{1,0:T(8,128)S(1)}, f32[256,512]{1,0:T(8,128)S(1)}, u32[]{:S(2)}, u32[]{:S(2)}) %collective-permute-start.28) | collective-permute-done | bytes 524320 | tf_op jit(solution)/shard_map/link_relayed/ppermute | solution.py:374
  104.8 1.6 %assemble.4.refs_2_ = f32[512,3072]{1,0:T(8,128)} custom-call(s32[6]{0:T(128)S(1)} %bitcast.28, s32[1]{0:T(128)} %bitcast.1.me_ref, f32[512,512]{1,0:T(8,128)S(1)} %collective-permute-done.30.refs_0_, f32[512,512]{1,0:T(8,128)S(1)} %collective-permute-done.31.refs_1_, ...), custom_call_target="tpu_custom_call", output_to_operand_aliasing={{}: (6, {})} | custom-call | bytes 8388608 | tf_op jit(solution)/shard_map/assemble/pallas_call | solution.py:345
  106.7 1.5 %assemble.5 = f32[512,3072]{1,0:T(8,128)} custom-call(s32[6]{0:T(128)S(1)} %bitcast.29, s32[1]{0:T(128)} %bitcast.1.me_ref, f32[256,512]{1,0:T(8,128)S(1)} %collective-permute-done.27.refs_0_, f32[256,512]{1,0:T(8,128)S(1)} %collective-permute-done.29.refs_1_, f32[512,3072]{1,0:T(8,128)} %assemble.4.refs_2_), custom_call_target="tpu_custom_call", output_to_operand_aliasing={{}: (4, {})} | custom-call | bytes 2097152 | tf_op jit(solution)/shard_map/assemble/pallas_call | solution.py:345
  (66 shorter events, 14.7 us)
Async XLA Ops:
  3.2 2.3 %collective-permute-start.4 = (f32[256,512]{1,0:T(8,128)S(1)}, f32[256,512]{1,0:T(8,128)S(1)}, u32[]{:S(2)}, u32[]{:S(2)}) collective-permute-start(f32[256,512]{1,0:T(8,128)S(1)} %get-tuple-element.45), channel_id=1, source_target_pairs={{0,4},{4,0},{8,12},{12,8},{16,20},{20,16},{24,28},{28,24},{1,5},{5... | collective-permute-start | bytes 1572872 | tf_op jit(solution)/shard_map/core_corner/ppermute | solution.py:374
  3.8 5.1 %collective-permute-start.11 = (f32[256,512]{1,0:T(8,128)S(1)}, f32[256,512]{1,0:T(8,128)S(1)}, u32[]{:S(2)}, u32[]{:S(2)}) collective-permute-start(f32[256,512]{1,0:T(8,128)S(1)} %get-tuple-element.50), channel_id=1, source_target_pairs={{0,4},{4,0},{8,12},{12,8},{16,20},{20,16},{24,28},{28,24},{1,5},{5... | collective-permute-start | bytes 1572872 | tf_op jit(solution)/shard_map/core_corner/ppermute | solution.py:374
  3.8 5.7 %collective-permute-start.1 = (f32[256,512]{1,0:T(8,128)S(1)}, f32[256,512]{1,0:T(8,128)S(1)}, u32[]{:S(2)}, u32[]{:S(2)}) collective-permute-start(f32[256,512]{1,0:T(8,128)S(1)} %get-tuple-element.38), channel_id=1, source_target_pairs={{0,4},{4,0},{8,12},{12,8},{16,20},{20,16},{24,28},{28,24},{1,5},{5... | collective-permute-start | bytes 1572872 | tf_op jit(solution)/shard_map/core_straight/ppermute | solution.py:374
  5.0 6.2 %collective-permute-start.3 = (f32[256,512]{1,0:T(8,128)S(1)}, f32[256,512]{1,0:T(8,128)S(1)}, u32[]{:S(2)}, u32[]{:S(2)}) collective-permute-start(f32[256,512]{1,0:T(8,128)S(1)} %get-tuple-element.44), channel_id=1, source_target_pairs={{0,4},{4,0},{8,12},{12,8},{16,20},{20,16},{24,28},{28,24},{1,5},{5... | collective-permute-start | bytes 1572872 | tf_op jit(solution)/shard_map/core_side/ppermute | solution.py:374
  5.1 6.8 %collective-permute-start.8 = (f32[256,512]{1,0:T(8,128)S(1)}, f32[256,512]{1,0:T(8,128)S(1)}, u32[]{:S(2)}, u32[]{:S(2)}) collective-permute-start(f32[256,512]{1,0:T(8,128)S(1)} %get-tuple-element.48), channel_id=1, source_target_pairs={{0,4},{4,0},{8,12},{12,8},{16,20},{20,16},{24,28},{28,24},{1,5},{5... | collective-permute-start | bytes 1572872 | tf_op jit(solution)/shard_map/core_straight/ppermute | solution.py:374
  6.1 9.8 %collective-permute-start.5 = (f32[256,512]{1,0:T(8,128)S(1)}, f32[256,512]{1,0:T(8,128)S(1)}, u32[]{:S(2)}, u32[]{:S(2)}) collective-permute-start(f32[256,512]{1,0:T(8,128)S(1)} %add.10), channel_id=1, source_target_pairs={{0,8},{4,20},{8,0},{12,28},{16,24},{20,4},{24,16},{28,12},{1,9},{5... | collective-permute-start | bytes 1572872 | tf_op jit(solution)/shard_map/link_corner/ppermute | solution.py:374
  8.8 7.8 %collective-permute-start.10 = (f32[256,512]{1,0:T(8,128)S(1)}, f32[256,512]{1,0:T(8,128)S(1)}, u32[]{:S(2)}, u32[]{:S(2)}) collective-permute-start(f32[256,512]{1,0:T(8,128)S(1)} %get-tuple-element.49), channel_id=1, source_target_pairs={{0,4},{4,0},{8,12},{12,8},{16,20},{20,16},{24,28},{28,24},{1,5},{5... | collective-permute-start | bytes 1572872 | tf_op jit(solution)/shard_map/core_side/ppermute | solution.py:374
  9.6 12.0 %collective-permute-start.12 = (f32[256,512]{1,0:T(8,128)S(1)}, f32[256,512]{1,0:T(8,128)S(1)}, u32[]{:S(2)}, u32[]{:S(2)}) collective-permute-start(f32[256,512]{1,0:T(8,128)S(1)} %add.14), channel_id=1, source_target_pairs={{0,8},{4,20},{8,0},{12,28},{16,24},{20,4},{24,16},{28,12},{1,9},{5... | collective-permute-start | bytes 1572872 | tf_op jit(solution)/shard_map/link_corner/ppermute | solution.py:374
  11.1 13.2 %collective-permute-start = (f32[256,512]{1,0:T(8,128)S(1)}, f32[256,512]{1,0:T(8,128)S(1)}, u32[]{:S(2)}, u32[]{:S(2)}) collective-permute-start(f32[256,512]{1,0:T(8,128)S(1)} %get-tuple-element.37), channel_id=1, source_target_pairs={{0,4},{4,0},{8,12},{12,8},{16,20},{20,16},{24,28},{28,24},{1,5},{5... | collective-permute-start | bytes 1572872 | tf_op jit(solution)/shard_map/core_self/ppermute | solution.py:374
  11.9 18.5 %collective-permute-start.2 = (f32[256,512]{1,0:T(8,128)S(1)}, f32[256,512]{1,0:T(8,128)S(1)}, u32[]{:S(2)}, u32[]{:S(2)}) collective-permute-start(f32[256,512]{1,0:T(8,128)S(1)} %add.8), channel_id=1, source_target_pairs={{0,8},{4,20},{8,0},{12,28},{16,24},{20,4},{24,16},{28,12},{1,9},{5... | collective-permute-start | bytes 1572872 | tf_op jit(solution)/shard_map/link_straight/ppermute | solution.py:374
  16.0 16.4 %collective-permute-start.7 = (f32[256,512]{1,0:T(8,128)S(1)}, f32[256,512]{1,0:T(8,128)S(1)}, u32[]{:S(2)}, u32[]{:S(2)}) collective-permute-start(f32[256,512]{1,0:T(8,128)S(1)} %get-tuple-element.47), channel_id=1, source_target_pairs={{0,4},{4,0},{8,12},{12,8},{16,20},{20,16},{24,28},{28,24},{1,5},{5... | collective-permute-start | bytes 1572872 | tf_op jit(solution)/shard_map/core_self/ppermute | solution.py:374
  16.6 24.9 %collective-permute-start.9 = (f32[256,512]{1,0:T(8,128)S(1)}, f32[256,512]{1,0:T(8,128)S(1)}, u32[]{:S(2)}, u32[]{:S(2)}) collective-permute-start(f32[256,512]{1,0:T(8,128)S(1)} %add.12), channel_id=1, source_target_pairs={{0,8},{4,20},{8,0},{12,28},{16,24},{20,4},{24,16},{28,12},{1,9},{5... | collective-permute-start | bytes 1572872 | tf_op jit(solution)/shard_map/link_straight/ppermute | solution.py:374
  21.6 20.6 %collective-permute-start.6 = (f32[256,512]{1,0:T(8,128)S(1)}, f32[256,512]{1,0:T(8,128)S(1)}, u32[]{:S(2)}, u32[]{:S(2)}) collective-permute-start(f32[256,512]{1,0:T(8,128)S(1)} %add.11), channel_id=1, source_target_pairs={{0,16},{4,12},{8,24},{12,4},{16,0},{20,28},{24,8},{28,20},{1,17},{... | collective-permute-start | bytes 1572872 | tf_op jit(solution)/shard_map/side_side/ppermute | solution.py:374
  24.3 19.5 %collective-permute-start.13 = (f32[256,512]{1,0:T(8,128)S(1)}, f32[256,512]{1,0:T(8,128)S(1)}, u32[]{:S(2)}, u32[]{:S(2)}) collective-permute-start(f32[256,512]{1,0:T(8,128)S(1)} %add.15), channel_id=1, source_target_pairs={{0,16},{4,12},{8,24},{12,4},{16,0},{20,28},{24,8},{28,20},{1,17},{... | collective-permute-start | bytes 1572872 | tf_op jit(solution)/shard_map/side_side/ppermute | solution.py:374
  44.7 1.2 %collective-permute-start.14 = (f32[8,128]{1,0:T(8,128)S(1)}, f32[8,128]{1,0:T(8,128)S(1)}, u32[]{:S(2)}, u32[]{:S(2)}) collective-permute-start(f32[8,128]{1,0:T(8,128)S(1)} %get-tuple-element.53.refs_0_.block_norm_ref), channel_id=1, source_target_pairs={{0,4},{4,0},{8,12},{12,8},{16,20},{20,16},{24,28},{28,24},{1,5},{5... | collective-permute-start | bytes 12296 | tf_op jit(solution)/shard_map/core_norm/ppermute | solution.py:374
  45.9 6.7 %collective-permute-start.15 = (f32[8,128]{1,0:T(8,128)S(1)}, f32[8,128]{1,0:T(8,128)S(1)}, u32[]{:S(2)}, u32[]{:S(2)}) collective-permute-start(f32[8,128]{1,0:T(8,128)S(1)} %sum.2.refs_0_), channel_id=1, source_target_pairs={{0,8},{4,12},{8,0},{12,4},{16,24},{20,28},{24,16},{28,20},{1,9},{5... | collective-permute-start | bytes 12296 | tf_op jit(solution)/shard_map/chip_norm/ppermute | solution.py:374
  47.7 4.9 %collective-permute-start.16 = (f32[8,128]{1,0:T(8,128)S(1)}, f32[8,128]{1,0:T(8,128)S(1)}, u32[]{:S(2)}, u32[]{:S(2)}) collective-permute-start(f32[8,128]{1,0:T(8,128)S(1)} %sum.2.refs_0_), channel_id=1, source_target_pairs={{0,16},{4,20},{8,24},{12,28},{16,0},{20,4},{24,8},{28,12},{1,17},{... | collective-permute-start | bytes 12296 | tf_op jit(solution)/shard_map/chip_norm/ppermute | solution.py:374
  49.2 4.5 %collective-permute-start.17 = (f32[8,128]{1,0:T(8,128)S(1)}, f32[8,128]{1,0:T(8,128)S(1)}, u32[]{:S(2)}, u32[]{:S(2)}) collective-permute-start(f32[8,128]{1,0:T(8,128)S(1)} %sum.2.refs_0_), channel_id=1, source_target_pairs={{0,24},{4,28},{8,16},{12,20},{16,8},{20,12},{24,0},{28,4},{1,25},{... | collective-permute-start | bytes 12296 | tf_op jit(solution)/shard_map/chip_norm/ppermute | solution.py:374
  53.7 7.2 %collective-permute-start.18 = (f32[8,128]{1,0:T(8,128)S(1)}, f32[8,128]{1,0:T(8,128)S(1)}, u32[]{:S(2)}, u32[]{:S(2)}) collective-permute-start(f32[8,128]{1,0:T(8,128)S(1)} %sum.3.refs_10_), channel_id=1, source_target_pairs={{0,1},{1,2},{2,3},{3,0},{4,5},{5,6},{6,7},{7,4},{8,9},{9,10},{10,1... | collective-permute-start | bytes 12296 | tf_op jit(solution)/shard_map/group_norm/ppermute | solution.py:428
  55.3 5.7 %collective-permute-start.19 = (f32[8,128]{1,0:T(8,128)S(1)}, f32[8,128]{1,0:T(8,128)S(1)}, u32[]{:S(2)}, u32[]{:S(2)}) collective-permute-start(f32[8,128]{1,0:T(8,128)S(1)} %sum.3.refs_10_), channel_id=1, source_target_pairs={{0,2},{1,3},{2,0},{3,1},{4,6},{5,7},{6,4},{7,5},{8,10},{9,11},{10,... | collective-permute-start | bytes 12296 | tf_op jit(solution)/shard_map/group_norm/ppermute | solution.py:428
  57.9 3.6 %collective-permute-start.20 = (f32[8,128]{1,0:T(8,128)S(1)}, f32[8,128]{1,0:T(8,128)S(1)}, u32[]{:S(2)}, u32[]{:S(2)}) collective-permute-start(f32[8,128]{1,0:T(8,128)S(1)} %sum.3.refs_10_), channel_id=1, source_target_pairs={{0,3},{1,0},{2,1},{3,2},{4,7},{5,4},{6,5},{7,6},{8,11},{9,8},{10,9... | collective-permute-start | bytes 12296 | tf_op jit(solution)/shard_map/group_norm/ppermute | solution.py:428
  67.4 9.3 %collective-permute-start.22 = (f32[512,512]{1,0:T(8,128)S(1)}, f32[512,512]{1,0:T(8,128)S(1)}, u32[]{:S(2)}, u32[]{:S(2)}) collective-permute-start(f32[512,512]{1,0:T(8,128)S(1)} %get-tuple-element.63.refs_0_), channel_id=1, source_target_pairs={{0,4},{4,0},{8,12},{12,8},{16,20},{20,16},{24,28},{28,24},{1,5},{5... | collective-permute-start | bytes 3145736 | tf_op jit(solution)/shard_map/core_own/ppermute | solution.py:374
  67.5 9.2 %collective-permute-start.21 = (f32[256,512]{1,0:T(8,128)S(1)}, f32[256,512]{1,0:T(8,128)S(1)}, u32[]{:S(2)}, u32[]{:S(2)}) collective-permute-start(f32[256,512]{1,0:T(8,128)S(1)} %get-tuple-element.62), channel_id=1, source_target_pairs={{0,8},{4,20},{8,0},{12,28},{16,24},{20,4},{24,16},{28,12},{1,9},{5... | collective-permute-start | bytes 1572872 | tf_op jit(solution)/shard_map/link_own/ppermute | solution.py:374
  68.3 14.0 %collective-permute-start.25 = (f32[256,512]{1,0:T(8,128)S(1)}, f32[256,512]{1,0:T(8,128)S(1)}, u32[]{:S(2)}, u32[]{:S(2)}) collective-permute-start(f32[256,512]{1,0:T(8,128)S(1)} %get-tuple-element.65), channel_id=1, source_target_pairs={{0,8},{4,20},{8,0},{12,28},{16,24},{20,4},{24,16},{28,12},{1,9},{5... | collective-permute-start | bytes 1572872 | tf_op jit(solution)/shard_map/link_own/ppermute | solution.py:374
  76.7 16.8 %collective-permute-start.30 = (f32[512,512]{1,0:T(8,128)S(1)}, f32[512,512]{1,0:T(8,128)S(1)}, u32[]{:S(2)}, u32[]{:S(2)}) collective-permute-start(f32[512,512]{1,0:T(8,128)S(1)} %collective-permute-done.22.refs_1_), channel_id=1, source_target_pairs={{0,8},{4,20},{8,0},{12,28},{16,24},{20,4},{24,16},{28,12},{1,9},{5... | collective-permute-start | bytes 3145736 | tf_op jit(solution)/shard_map/link_sibling/ppermute | solution.py:374
  77.5 4.8 %collective-permute-start.23 = (f32[256,512]{1,0:T(8,128)S(1)}, f32[256,512]{1,0:T(8,128)S(1)}, u32[]{:S(2)}, u32[]{:S(2)}) collective-permute-start(f32[256,512]{1,0:T(8,128)S(1)} %collective-permute-done.21.refs_2_), channel_id=1, source_target_pairs={{0,4},{4,0},{8,12},{12,8},{16,20},{20,16},{24,28},{28,24},{1,5},{5... | collective-permute-start | bytes 1572872 | tf_op jit(solution)/shard_map/core_first/ppermute | solution.py:374
  82.3 11.2 %collective-permute-start.26 = (f32[256,512]{1,0:T(8,128)S(1)}, f32[256,512]{1,0:T(8,128)S(1)}, u32[]{:S(2)}, u32[]{:S(2)}) collective-permute-start(f32[256,512]{1,0:T(8,128)S(1)} %collective-permute-done.25.refs_3_), channel_id=1, source_target_pairs={{0,4},{4,0},{8,12},{12,8},{16,20},{20,16},{24,28},{28,24},{1,5},{5... | collective-permute-start | bytes 1572872 | tf_op jit(solution)/shard_map/core_first/ppermute | solution.py:374
  82.4 16.8 %collective-permute-start.24 = (f32[256,512]{1,0:T(8,128)S(1)}, f32[256,512]{1,0:T(8,128)S(1)}, u32[]{:S(2)}, u32[]{:S(2)}) collective-permute-start(f32[256,512]{1,0:T(8,128)S(1)} %collective-permute-done.23.refs_4_), channel_id=1, source_target_pairs={{0,8},{4,20},{8,0},{12,28},{16,24},{20,4},{24,16},{28,12},{1,9},{5... | collective-permute-start | bytes 1572872 | tf_op jit(solution)/shard_map/link_relayed/ppermute | solution.py:374
  93.6 11.2 %collective-permute-start.31 = (f32[512,512]{1,0:T(8,128)S(1)}, f32[512,512]{1,0:T(8,128)S(1)}, u32[]{:S(2)}, u32[]{:S(2)}) collective-permute-start(f32[512,512]{1,0:T(8,128)S(1)} %collective-permute-done.30.refs_0_), channel_id=1, source_target_pairs={{0,4},{4,0},{8,12},{12,8},{16,20},{20,16},{24,28},{28,24},{1,5},{5... | collective-permute-start | bytes 3145736 | tf_op jit(solution)/shard_map/core_second/ppermute | solution.py:374
  93.6 11.2 %collective-permute-start.28 = (f32[256,512]{1,0:T(8,128)S(1)}, f32[256,512]{1,0:T(8,128)S(1)}, u32[]{:S(2)}, u32[]{:S(2)}) collective-permute-start(f32[256,512]{1,0:T(8,128)S(1)} %collective-permute-done.26.refs_5_), channel_id=1, source_target_pairs={{0,8},{4,20},{8,0},{12,28},{16,24},{20,4},{24,16},{28,12},{1,9},{5... | collective-permute-start | bytes 1572872 | tf_op jit(solution)/shard_map/link_relayed/ppermute | solution.py:374
  99.2 7.2 %collective-permute-start.27 = (f32[256,512]{1,0:T(8,128)S(1)}, f32[256,512]{1,0:T(8,128)S(1)}, u32[]{:S(2)}, u32[]{:S(2)}) collective-permute-start(f32[256,512]{1,0:T(8,128)S(1)} %collective-permute-done.24.refs_2_), channel_id=1, source_target_pairs={{0,4},{4,0},{8,12},{12,8},{16,20},{20,16},{24,28},{28,24},{1,5},{5... | collective-permute-start | bytes 1572872 | tf_op jit(solution)/shard_map/core_relayed/ppermute | solution.py:374
  104.8 1.9 %collective-permute-start.29 = (f32[256,512]{1,0:T(8,128)S(1)}, f32[256,512]{1,0:T(8,128)S(1)}, u32[]{:S(2)}, u32[]{:S(2)}) collective-permute-start(f32[256,512]{1,0:T(8,128)S(1)} %collective-permute-done.28.refs_3_), channel_id=1, source_target_pairs={{0,4},{4,0},{8,12},{12,8},{16,20},{20,16},{24,28},{28,24},{1,5},{5... | collective-permute-start | bytes 1572872 | tf_op jit(solution)/shard_map/core_relayed/ppermute | solution.py:374
  (6 other events, 67.1 us)

commit v10 on v9

--- a/solution.py
+++ b/solution.py
@@ -416,17 +416,33 @@
         block.append(joined)
     block_norm = norm
     norm = sum_call(norm, to_core(norm, "norm"))
-    chip_norms = [over(flipped(mask), norm, "chip_norm") for mask in (2, 4, 6)]
+    def group_over(step, value):
+        with jax.named_scope("group_norm"):
+            return lax.ppermute(value, "mp", [(i, step(i)) for i in range(group_count)])
+
+    chip_norm = over(flipped(2), norm, "x_norm")
     grams = gram_call([after(block[0], norm), block[1]])
+    norm = sum_call(after(norm, grams[0]), chip_norm)
+    chip_norm = over(flipped(4), norm, "y_norm")
     sides = [(previous, gram, square) for (previous,), gram, square in zip(sides, grams, squares)]
-    sides[0] += tuple(mix_call(*sides[0][:2]))
-    norm = sum_call(after(norm, sides[0][4]), *chip_norms)
-    norms = [norm]
-    for shift in range(1, group_count):
-        pairs = [(i, (i + shift) % group_count) for i in range(group_count)]
-        with jax.named_scope("group_norm"):
-            norms.append(lax.ppermute(norm, "mp", pairs))
-    sides[1] += tuple(mix_call(*sides[1][:2]))
+    sides[0] += tuple(mix_call(sides[0][0], after(sides[0][1], norm)))
+    norm = sum_call(after(norm, sides[0][3]), chip_norm)
+    if group_count & (group_count - 1) == 0:
+        step = 1
+        right_gram = sides[1][1]
+        while step < group_count:
+            other = group_over(lambda i: i ^ step, norm)
+            if step == 1:
+                sides[1] += tuple(mix_call(sides[1][0], after(right_gram, norm)))
+                norm = after(norm, sides[1][3])
+            norm = sum_call(norm, other)
+            step *= 2
+        norms = [norm]
+    else:
+        norms = [norm]
+        for shift in range(1, group_count):
+            norms.append(group_over(lambda i: (i + shift) % group_count, norm))
+        sides[1] += tuple(mix_call(*sides[1][:2]))
     whole, *own = update_call(block, block_norm, *sides, norms, entry_count)
 
     core_own = to_core(whole, "own")
@@ -441,8 +457,8 @@
     crossed = [(("cross", 0, None), second), (("cross", 1, None), core_second)]
     result = assemble(None, *held)
     core_relayed = [to_core(after(relayed[0], result), "relayed"), to_core(relayed[1], "relayed")]
-    result = assemble(result, *crossed, *[(("diagonal", 0, half), relayed[half]) for half in HALVES])
-    return assemble(result, *[(("diagonal", 1, half), core_relayed[half]) for half in HALVES])
+    result = assemble(result, *crossed, *[(("diagonal", 0, half), relayed[half]) for half in HALVES], (("diagonal", 1, 0), core_relayed[0]))
+    return assemble(result, (("diagonal", 1, 1), core_relayed[1]))
 
 
 def solution(mesh):

time: 109 us -> 108 us (level)
  waiting for transfers between devices: 54.9 us -> 52.5 us
  starting transfers between devices: 24.6 us -> 26.8 us
    ppermute x29 -> x28, waiting for transfers between devices: 54.4 us -> 50.8 us  [over(): return lax.ppermute(value, 'dp', pairs)]
    ppermute x29 -> x28, starting transfers between devices: 19.1 us -> 22.1 us  [over(): return lax.ppermute(value, 'dp', pairs)]
    ppermute x3 -> x2, waiting for transfers between devices: 0.53 us -> 1.75 us  [group_over(): return lax.ppermute(value, 'mp', [(i, step(i)) for i in range(group_count)])]
    ppermute x3 -> x2, starting transfers between devices: 5.51 us -> 4.7 us  [group_over(): return lax.ppermute(value, 'mp', [(i, step(i)) for i in range(group_count)])]
    pallas_call x19 -> x22, Pallas kernels: 20.2 us -> 20.3 us  [local_call(): pl.pallas_call(kernel, in_specs=[pl.BlockSpec(memory_space=pltpu.SMEM)] *...]
  transfers between devices with their start and end apart: 32 -> 30, of which waited for: 14 -> 15; matrix products, arithmetic and copies ran while one was open for 0% -> 0% of each run, Pallas kernels for 16% -> 16%
where the time goes in v10:
time: 108 us
  waiting for transfers between devices  52.5 us (49%)
  starting transfers between devices  26.8 us (25%)
  Pallas kernels  26.1 us (24%)
  local copies, waits for them, and re-layouts  2.56 us (2%)
    ppermute x28, waiting for transfers between devices, over(): return lax.ppermute(value, 'dp', pairs)  50.8 us
    ppermute x28, starting transfers between devices, over(): return lax.ppermute(value, 'dp', pairs)  22.1 us
    pallas_call x22, Pallas kernels, local_call(): pl.pallas_call(kernel, in_specs=[pl.BlockSpec(memory_space=pltpu.SMEM)] *...  20.3 us
    pallas_call x3, Pallas kernels, assemble_call(): pl.pallas_call(kernel, in_specs=in_specs, out_specs=pl.BlockSpec(memory_s...  5.73 us
    ppermute x2, starting transfers between devices, group_over(): return lax.ppermute(value, 'mp', [(i, step(i)) for i in range(group_count)])  4.7 us
    unnamed x12, local copies, waits for them, and re-layouts  2.56 us
  transfers between devices with their start and end apart: 30, of which 15 were waited for; matrix products, arithmetic and copies ran while one was open for 0% of the time, Pallas kernels for 16%

profile of v10, /device:TPU:0, one launch (start us, length us, event | category | flops | bytes accessed | tf_op | source)
XLA Modules:
  0.0 108.2 jit_solution(10500117639868171728)
XLA Ops:
  0.0 1.9 %copy-done = bf16[1,512,3072]{2,1,0:T(8,128)(2,1)S(1)} copy-done((bf16[1,512,3072]{2,1,0:T(8,128)(2,1)S(1)}, bf16[1,512,3072]{2,1,0:T(8,128)(2,1)}, u32[]{:S(2)}) %copy-start) | copy-done | bytes 3145752
  6.1 2.7 %collective-permute-start.5 = (f32[256,512]{1,0:T(8,128)S(1)}, f32[256,512]{1,0:T(8,128)S(1)}, u32[]{:S(2)}, u32[]{:S(2)}) collective-permute-start(f32[256,512]{1,0:T(8,128)S(1)} %add.10), channel_id=1, source_target_pairs={{0,8},{4,20},{8,0},{12,28},{16,24},{20,4},{24,16},{28,12},{1,9},{5... | collective-permute-start | bytes 1572872 | tf_op jit(solution)/shard_map/link_corner/ppermute | solution.py:374
  9.6 1.6 %collective-permute-start.12 = (f32[256,512]{1,0:T(8,128)S(1)}, f32[256,512]{1,0:T(8,128)S(1)}, u32[]{:S(2)}, u32[]{:S(2)}) collective-permute-start(f32[256,512]{1,0:T(8,128)S(1)} %add.14), channel_id=1, source_target_pairs={{0,8},{4,20},{8,0},{12,28},{16,24},{20,4},{24,16},{28,12},{1,9},{5... | collective-permute-start | bytes 1572872 | tf_op jit(solution)/shard_map/link_corner/ppermute | solution.py:374
  13.1 2.9 %collective-permute-done.5.refs_1_ = f32[256,512]{1,0:T(8,128)S(1)} collective-permute-done((f32[256,512]{1,0:T(8,128)S(1)}, f32[256,512]{1,0:T(8,128)S(1)}, u32[]{:S(2)}, u32[]{:S(2)}) %collective-permute-start.5) | collective-permute-done | bytes 524320 | tf_op jit(solution)/shard_map/link_corner/ppermute | solution.py:374
  16.6 2.1 %collective-permute-start.9 = (f32[256,512]{1,0:T(8,128)S(1)}, f32[256,512]{1,0:T(8,128)S(1)}, u32[]{:S(2)}, u32[]{:S(2)}) collective-permute-start(f32[256,512]{1,0:T(8,128)S(1)} %add.12), channel_id=1, source_target_pairs={{0,8},{4,20},{8,0},{12,28},{16,24},{20,4},{24,16},{28,12},{1,9},{5... | collective-permute-start | bytes 1572872 | tf_op jit(solution)/shard_map/link_straight/ppermute | solution.py:374
  18.7 2.9 %collective-permute-done.12.refs_1_ = f32[256,512]{1,0:T(8,128)S(1)} collective-permute-done((f32[256,512]{1,0:T(8,128)S(1)}, f32[256,512]{1,0:T(8,128)S(1)}, u32[]{:S(2)}, u32[]{:S(2)}) %collective-permute-start.12) | collective-permute-done | bytes 524320 | tf_op jit(solution)/shard_map/link_corner/ppermute | solution.py:374
  21.6 2.0 %collective-permute-start.6 = (f32[256,512]{1,0:T(8,128)S(1)}, f32[256,512]{1,0:T(8,128)S(1)}, u32[]{:S(2)}, u32[]{:S(2)}) collective-permute-start(f32[256,512]{1,0:T(8,128)S(1)} %add.11), channel_id=1, source_target_pairs={{0,16},{4,12},{8,24},{12,4},{16,0},{20,28},{24,8},{28,20},{1,17},{... | collective-permute-start | bytes 1572872 | tf_op jit(solution)/shard_map/side_side/ppermute | solution.py:374
  24.4 5.9 %collective-permute-done.2.refs_1_ = f32[256,512]{1,0:T(8,128)S(1)} collective-permute-done((f32[256,512]{1,0:T(8,128)S(1)}, f32[256,512]{1,0:T(8,128)S(1)}, u32[]{:S(2)}, u32[]{:S(2)}) %collective-permute-start.2) | collective-permute-done | bytes 524320 | tf_op jit(solution)/shard_map/link_straight/ppermute | solution.py:374
  31.0 1.5 %square.1 = (f32[512,512]{1,0:T(8,128)S(1)}, f32[512,512]{1,0:T(8,128)S(1)}) custom-call(f32[512,512]{1,0:T(8,128)S(1)} %bitcast.30, f32[512,512]{1,0:T(8,128)S(1)} %bitcast.33), custom_call_target="tpu_custom_call" | custom-call | flops 1610612736 | bytes 4194304 | tf_op jit(solution)/shard_map/square/pallas_call | solution.py:128
  32.4 9.1 %collective-permute-done.9.refs_1_ = f32[256,512]{1,0:T(8,128)S(1)} collective-permute-done((f32[256,512]{1,0:T(8,128)S(1)}, f32[256,512]{1,0:T(8,128)S(1)}, u32[]{:S(2)}, u32[]{:S(2)}) %collective-permute-start.9) | collective-permute-done | bytes 524320 | tf_op jit(solution)/shard_map/link_straight/ppermute | solution.py:374
  44.8 1.1 collective-permute-done.14.refs_1_
  45.9 1.8 %collective-permute-start.15 = (f32[8,128]{1,0:T(8,128)S(1)}, f32[8,128]{1,0:T(8,128)S(1)}, u32[]{:S(2)}, u32[]{:S(2)}) collective-permute-start(f32[8,128]{1,0:T(8,128)S(1)} %sum.5.refs_0_), channel_id=1, source_target_pairs={{0,8},{4,12},{8,0},{12,4},{16,24},{20,28},{24,16},{28,20},{1,9},{5... | collective-permute-start | bytes 12296 | tf_op jit(solution)/shard_map/x_norm/ppermute | solution.py:374
  47.7 1.5 %gram.1 = (f32[512,512]{1,0:T(8,128)S(1)}, f32[512,512]{1,0:T(8,128)S(1)}) custom-call(f32[256,512]{1,0:T(8,128)S(1)} %get-tuple-element.58.upper_ref, f32[256,512]{1,0:T(8,128)S(1)} %get-tuple-element.56.lower_ref), custom_call_target="tpu_custom_call" | custom-call | flops 1610612736 | bytes 3145728 | tf_op jit(solution)/shard_map/gram/pallas_call | solution.py:128
  49.5 1.8 %collective-permute-start.16 = (f32[8,128]{1,0:T(8,128)S(1)}, f32[8,128]{1,0:T(8,128)S(1)}, u32[]{:S(2)}, u32[]{:S(2)}) collective-permute-start(f32[8,128]{1,0:T(8,128)S(1)} %sum.6.refs_0_), channel_id=1, source_target_pairs={{0,16},{4,20},{8,24},{12,28},{16,0},{20,4},{24,8},{28,12},{1,17},{... | collective-permute-start | bytes 12296 | tf_op jit(solution)/shard_map/y_norm/ppermute | solution.py:374
  51.3 1.7 %mix.2 = (f32[512,512]{1,0:T(8,128)S(1)}, f32[512,512]{1,0:T(8,128)S(1)}) custom-call(f32[512,512]{1,0:T(8,128)S(1)} %bitcast.31, f32[512,512]{1,0:T(8,128)S(1)} %get-tuple-element.61.gram_ref.refs_1_), custom_call_target="tpu_custom_call" | custom-call | flops 1610612736 | bytes 4194304 | tf_op jit(solution)/shard_map/mix/pallas_call | solution.py:128
  53.1 1.9 %collective-permute-start.17 = (f32[8,128]{1,0:T(8,128)S(1)}, f32[8,128]{1,0:T(8,128)S(1)}, u32[]{:S(2)}, u32[]{:S(2)}) collective-permute-start(f32[8,128]{1,0:T(8,128)S(1)} %sum.7.refs_0_), channel_id=1, source_target_pairs={{0,1},{1,0},{2,3},{3,2},{4,5},{5,4},{6,7},{7,6},{8,9},{9,8},{10,11... | collective-permute-start | bytes 12296 | tf_op jit(solution)/shard_map/group_norm/ppermute | solution.py:421
  55.0 1.7 %mix.3 = (f32[512,512]{1,0:T(8,128)S(1)}, f32[512,512]{1,0:T(8,128)S(1)}) custom-call(f32[512,512]{1,0:T(8,128)S(1)} %bitcast.34, f32[512,512]{1,0:T(8,128)S(1)} %get-tuple-element.66.gram_ref.refs_6_), custom_call_target="tpu_custom_call" | custom-call | flops 1610612736 | bytes 4194304 | tf_op jit(solution)/shard_map/mix/pallas_call | solution.py:128
  56.8 2.8 %collective-permute-start.18 = (f32[8,128]{1,0:T(8,128)S(1)}, f32[8,128]{1,0:T(8,128)S(1)}, u32[]{:S(2)}, u32[]{:S(2)}) collective-permute-start(f32[8,128]{1,0:T(8,128)S(1)} %sum.8.refs_0_), channel_id=1, source_target_pairs={{0,2},{1,3},{2,0},{3,1},{4,6},{5,7},{6,4},{7,5},{8,10},{9,11},{10,... | collective-permute-start | bytes 12296 | tf_op jit(solution)/shard_map/group_norm/ppermute | solution.py:421
  59.6 1.7 %collective-permute-done.18.refs_1_ = f32[8,128]{1,0:T(8,128)S(1)} collective-permute-done((f32[8,128]{1,0:T(8,128)S(1)}, f32[8,128]{1,0:T(8,128)S(1)}, u32[]{:S(2)}, u32[]{:S(2)}) %collective-permute-start.18) | collective-permute-done | bytes 4128 | tf_op jit(solution)/shard_map/group_norm/ppermute | solution.py:421
  61.3 6.0 %update.1 = (f32[512,512]{1,0:T(8,128)S(1)}, f32[256,512]{1,0:T(8,128)S(1)}, f32[256,512]{1,0:T(8,128)S(1)}) custom-call(f32[256,512]{1,0:T(8,128)S(1)} %get-tuple-element.58.upper_ref, f32[256,512]{1,0:T(8,128)S(1)} %get-tuple-element.56.lower_ref, f32[8,128]{1,0:T(8,128)S(1)} %get-tuple-element.57.refs_0_.block_norm_ref, f32[512,512]{1,0:T(8,128)S(1)} %bitcast.32, ...), custom_call_target="tpu_custom_call" | custom-call | flops 4831838208 | bytes 13639680 | tf_op jit(solution)/shard_map/update/pallas_call | solution.py:128
  67.3 1.8 %collective-permute-start.24 = (f32[256,512]{1,0:T(8,128)S(1)}, f32[256,512]{1,0:T(8,128)S(1)}, u32[]{:S(2)}, u32[]{:S(2)}) collective-permute-start(f32[256,512]{1,0:T(8,128)S(1)} %get-tuple-element.73), channel_id=1, source_target_pairs={{0,8},{4,20},{8,0},{12,28},{16,24},{20,4},{24,16},{28,12},{1,9},{5... | collective-permute-start | bytes 1572872 | tf_op jit(solution)/shard_map/link_own/ppermute | solution.py:374
  69.4 7.2 %collective-permute-done.24.refs_2_ = f32[256,512]{1,0:T(8,128)S(1)} collective-permute-done((f32[256,512]{1,0:T(8,128)S(1)}, f32[256,512]{1,0:T(8,128)S(1)}, u32[]{:S(2)}, u32[]{:S(2)}) %collective-permute-start.24) | collective-permute-done | bytes 524320 | tf_op jit(solution)/shard_map/link_own/ppermute | solution.py:374
  76.6 1.7 %collective-permute-start.25 = (f32[512,512]{1,0:T(8,128)S(1)}, f32[512,512]{1,0:T(8,128)S(1)}, u32[]{:S(2)}, u32[]{:S(2)}) collective-permute-start(f32[512,512]{1,0:T(8,128)S(1)} %collective-permute-done.20.refs_1_), channel_id=1, source_target_pairs={{0,8},{4,20},{8,0},{12,28},{16,24},{20,4},{24,16},{28,12},{1,9},{5... | collective-permute-start | bytes 3145736 | tf_op jit(solution)/shard_map/link_sibling/ppermute | solution.py:374
  78.3 3.9 %collective-permute-done.19.refs_3_ = f32[256,512]{1,0:T(8,128)S(1)} collective-permute-done((f32[256,512]{1,0:T(8,128)S(1)}, f32[256,512]{1,0:T(8,128)S(1)}, u32[]{:S(2)}, u32[]{:S(2)}) %collective-permute-start.19) | collective-permute-done | bytes 524320 | tf_op jit(solution)/shard_map/link_own/ppermute | solution.py:374
  82.2 1.7 %collective-permute-start.28 = (f32[256,512]{1,0:T(8,128)S(1)}, f32[256,512]{1,0:T(8,128)S(1)}, u32[]{:S(2)}, u32[]{:S(2)}) collective-permute-start(f32[256,512]{1,0:T(8,128)S(1)} %collective-permute-done.27.refs_4_), channel_id=1, source_target_pairs={{0,8},{4,20},{8,0},{12,28},{16,24},{20,4},{24,16},{28,12},{1,9},{5... | collective-permute-start | bytes 1572872 | tf_op jit(solution)/shard_map/link_relayed/ppermute | solution.py:374
  84.0 9.5 %collective-permute-done.25.refs_0_ = f32[512,512]{1,0:T(8,128)S(1)} collective-permute-done((f32[512,512]{1,0:T(8,128)S(1)}, f32[512,512]{1,0:T(8,128)S(1)}, u32[]{:S(2)}, u32[]{:S(2)}) %collective-permute-start.25) | collective-permute-done | bytes 1048608 | tf_op jit(solution)/shard_map/link_sibling/ppermute | solution.py:374
  93.5 1.7 %collective-permute-start.22 = (f32[256,512]{1,0:T(8,128)S(1)}, f32[256,512]{1,0:T(8,128)S(1)}, u32[]{:S(2)}, u32[]{:S(2)}) collective-permute-start(f32[256,512]{1,0:T(8,128)S(1)} %collective-permute-done.21.refs_5_), channel_id=1, source_target_pairs={{0,8},{4,20},{8,0},{12,28},{16,24},{20,4},{24,16},{28,12},{1,9},{5... | collective-permute-start | bytes 1572872 | tf_op jit(solution)/shard_map/link_relayed/ppermute | solution.py:374
  95.2 2.3 %assemble.3.refs_5_ = f32[512,3072]{1,0:T(8,128)} custom-call(s32[6]{0:T(128)S(1)} %bitcast.27, s32[1]{0:T(128)} %bitcast.1.me_ref, f32[512,512]{1,0:T(8,128)S(1)} %get-tuple-element.71.refs_0_, f32[512,512]{1,0:T(8,128)S(1)} %collective-permute-done.20.refs_1_, f32[256,512]{1,0:T(8,128)S(1)} %collective-permute-done.24.refs_2_, ...), custom_call_target="tpu_custom_call" | custom-call | bytes 12582912 | tf_op jit(solution)/shard_map/assemble/pallas_call | solution.py:345
  97.5 1.6 %collective-permute-done.28.refs_2_ = f32[256,512]{1,0:T(8,128)S(1)} collective-permute-done((f32[256,512]{1,0:T(8,128)S(1)}, f32[256,512]{1,0:T(8,128)S(1)}, u32[]{:S(2)}, u32[]{:S(2)}) %collective-permute-start.28) | collective-permute-done | bytes 524320 | tf_op jit(solution)/shard_map/link_relayed/ppermute | solution.py:374
  99.1 5.6 %collective-permute-done.22.refs_3_ = f32[256,512]{1,0:T(8,128)S(1)} collective-permute-done((f32[256,512]{1,0:T(8,128)S(1)}, f32[256,512]{1,0:T(8,128)S(1)}, u32[]{:S(2)}, u32[]{:S(2)}) %collective-permute-start.22) | collective-permute-done | bytes 524320 | tf_op jit(solution)/shard_map/link_relayed/ppermute | solution.py:374
  104.7 2.1 %assemble.4.refs_1_ = f32[512,3072]{1,0:T(8,128)} custom-call(s32[6]{0:T(128)S(1)} %bitcast.28, s32[1]{0:T(128)} %bitcast.1.me_ref, f32[512,512]{1,0:T(8,128)S(1)} %collective-permute-done.25.refs_0_, f32[512,512]{1,0:T(8,128)S(1)} %collective-permute-done.26.refs_1_, ...), custom_call_target="tpu_custom_call", output_to_operand_aliasing={{}: (7, {})} | custom-call | bytes 10485760 | tf_op jit(solution)/shard_map/assemble/pallas_call | solution.py:345
  106.8 1.4 %assemble.5 = f32[512,3072]{1,0:T(8,128)} custom-call(s32[6]{0:T(128)S(1)} %bitcast.29, s32[1]{0:T(128)} %bitcast.1.me_ref, f32[256,512]{1,0:T(8,128)S(1)} %collective-permute-done.23.refs_0_, f32[512,3072]{1,0:T(8,128)} %assemble.4.refs_1_), custom_call_target="tpu_custom_call", output_to_operand_aliasing={{}: (3, {})} | custom-call | bytes 1048576 | tf_op jit(solution)/shard_map/assemble/pallas_call | solution.py:345
  (65 shorter events, 12.9 us)
Async XLA Ops:
  3.2 2.3 %collective-permute-start.4 = (f32[256,512]{1,0:T(8,128)S(1)}, f32[256,512]{1,0:T(8,128)S(1)}, u32[]{:S(2)}, u32[]{:S(2)}) collective-permute-start(f32[256,512]{1,0:T(8,128)S(1)} %get-tuple-element.49), channel_id=1, source_target_pairs={{0,4},{4,0},{8,12},{12,8},{16,20},{20,16},{24,28},{28,24},{1,5},{5... | collective-permute-start | bytes 1572872 | tf_op jit(solution)/shard_map/core_corner/ppermute | solution.py:374
  3.8 5.1 %collective-permute-start.11 = (f32[256,512]{1,0:T(8,128)S(1)}, f32[256,512]{1,0:T(8,128)S(1)}, u32[]{:S(2)}, u32[]{:S(2)}) collective-permute-start(f32[256,512]{1,0:T(8,128)S(1)} %get-tuple-element.54), channel_id=1, source_target_pairs={{0,4},{4,0},{8,12},{12,8},{16,20},{20,16},{24,28},{28,24},{1,5},{5... | collective-permute-start | bytes 1572872 | tf_op jit(solution)/shard_map/core_corner/ppermute | solution.py:374
  3.8 5.7 %collective-permute-start.1 = (f32[256,512]{1,0:T(8,128)S(1)}, f32[256,512]{1,0:T(8,128)S(1)}, u32[]{:S(2)}, u32[]{:S(2)}) collective-permute-start(f32[256,512]{1,0:T(8,128)S(1)} %get-tuple-element.42), channel_id=1, source_target_pairs={{0,4},{4,0},{8,12},{12,8},{16,20},{20,16},{24,28},{28,24},{1,5},{5... | collective-permute-start | bytes 1572872 | tf_op jit(solution)/shard_map/core_straight/ppermute | solution.py:374
  5.0 6.2 %collective-permute-start.3 = (f32[256,512]{1,0:T(8,128)S(1)}, f32[256,512]{1,0:T(8,128)S(1)}, u32[]{:S(2)}, u32[]{:S(2)}) collective-permute-start(f32[256,512]{1,0:T(8,128)S(1)} %get-tuple-element.48), channel_id=1, source_target_pairs={{0,4},{4,0},{8,12},{12,8},{16,20},{20,16},{24,28},{28,24},{1,5},{5... | collective-permute-start | bytes 1572872 | tf_op jit(solution)/shard_map/core_side/ppermute | solution.py:374
  5.1 6.8 %collective-permute-start.8 = (f32[256,512]{1,0:T(8,128)S(1)}, f32[256,512]{1,0:T(8,128)S(1)}, u32[]{:S(2)}, u32[]{:S(2)}) collective-permute-start(f32[256,512]{1,0:T(8,128)S(1)} %get-tuple-element.52), channel_id=1, source_target_pairs={{0,4},{4,0},{8,12},{12,8},{16,20},{20,16},{24,28},{28,24},{1,5},{5... | collective-permute-start | bytes 1572872 | tf_op jit(solution)/shard_map/core_straight/ppermute | solution.py:374
  6.1 9.8 %collective-permute-start.5 = (f32[256,512]{1,0:T(8,128)S(1)}, f32[256,512]{1,0:T(8,128)S(1)}, u32[]{:S(2)}, u32[]{:S(2)}) collective-permute-start(f32[256,512]{1,0:T(8,128)S(1)} %add.10), channel_id=1, source_target_pairs={{0,8},{4,20},{8,0},{12,28},{16,24},{20,4},{24,16},{28,12},{1,9},{5... | collective-permute-start | bytes 1572872 | tf_op jit(solution)/shard_map/link_corner/ppermute | solution.py:374
  8.8 7.8 %collective-permute-start.10 = (f32[256,512]{1,0:T(8,128)S(1)}, f32[256,512]{1,0:T(8,128)S(1)}, u32[]{:S(2)}, u32[]{:S(2)}) collective-permute-start(f32[256,512]{1,0:T(8,128)S(1)} %get-tuple-element.53), channel_id=1, source_target_pairs={{0,4},{4,0},{8,12},{12,8},{16,20},{20,16},{24,28},{28,24},{1,5},{5... | collective-permute-start | bytes 1572872 | tf_op jit(solution)/shard_map/core_side/ppermute | solution.py:374
  9.6 12.0 %collective-permute-start.12 = (f32[256,512]{1,0:T(8,128)S(1)}, f32[256,512]{1,0:T(8,128)S(1)}, u32[]{:S(2)}, u32[]{:S(2)}) collective-permute-start(f32[256,512]{1,0:T(8,128)S(1)} %add.14), channel_id=1, source_target_pairs={{0,8},{4,20},{8,0},{12,28},{16,24},{20,4},{24,16},{28,12},{1,9},{5... | collective-permute-start | bytes 1572872 | tf_op jit(solution)/shard_map/link_corner/ppermute | solution.py:374
  11.1 13.2 %collective-permute-start = (f32[256,512]{1,0:T(8,128)S(1)}, f32[256,512]{1,0:T(8,128)S(1)}, u32[]{:S(2)}, u32[]{:S(2)}) collective-permute-start(f32[256,512]{1,0:T(8,128)S(1)} %get-tuple-element.41), channel_id=1, source_target_pairs={{0,4},{4,0},{8,12},{12,8},{16,20},{20,16},{24,28},{28,24},{1,5},{5... | collective-permute-start | bytes 1572872 | tf_op jit(solution)/shard_map/core_self/ppermute | solution.py:374
  11.9 18.5 %collective-permute-start.2 = (f32[256,512]{1,0:T(8,128)S(1)}, f32[256,512]{1,0:T(8,128)S(1)}, u32[]{:S(2)}, u32[]{:S(2)}) collective-permute-start(f32[256,512]{1,0:T(8,128)S(1)} %add.8), channel_id=1, source_target_pairs={{0,8},{4,20},{8,0},{12,28},{16,24},{20,4},{24,16},{28,12},{1,9},{5... | collective-permute-start | bytes 1572872 | tf_op jit(solution)/shard_map/link_straight/ppermute | solution.py:374
  16.0 16.5 %collective-permute-start.7 = (f32[256,512]{1,0:T(8,128)S(1)}, f32[256,512]{1,0:T(8,128)S(1)}, u32[]{:S(2)}, u32[]{:S(2)}) collective-permute-start(f32[256,512]{1,0:T(8,128)S(1)} %get-tuple-element.51), channel_id=1, source_target_pairs={{0,4},{4,0},{8,12},{12,8},{16,20},{20,16},{24,28},{28,24},{1,5},{5... | collective-permute-start | bytes 1572872 | tf_op jit(solution)/shard_map/core_self/ppermute | solution.py:374
  16.6 24.9 %collective-permute-start.9 = (f32[256,512]{1,0:T(8,128)S(1)}, f32[256,512]{1,0:T(8,128)S(1)}, u32[]{:S(2)}, u32[]{:S(2)}) collective-permute-start(f32[256,512]{1,0:T(8,128)S(1)} %add.12), channel_id=1, source_target_pairs={{0,8},{4,20},{8,0},{12,28},{16,24},{20,4},{24,16},{28,12},{1,9},{5... | collective-permute-start | bytes 1572872 | tf_op jit(solution)/shard_map/link_straight/ppermute | solution.py:374
  21.6 20.6 %collective-permute-start.6 = (f32[256,512]{1,0:T(8,128)S(1)}, f32[256,512]{1,0:T(8,128)S(1)}, u32[]{:S(2)}, u32[]{:S(2)}) collective-permute-start(f32[256,512]{1,0:T(8,128)S(1)} %add.11), channel_id=1, source_target_pairs={{0,16},{4,12},{8,24},{12,4},{16,0},{20,28},{24,8},{28,20},{1,17},{... | collective-permute-start | bytes 1572872 | tf_op jit(solution)/shard_map/side_side/ppermute | solution.py:374
  24.3 17.3 %copy-start.1 = (bf16[1,512,3072]{2,1,0:T(8,128)(2,1)S(1)}, bf16[1,512,3072]{2,1,0:T(8,128)(2,1)}, u32[]{:S(2)}) copy-start(bf16[1,512,3072]{2,1,0:T(8,128)(2,1)} %param.4) | copy-start | bytes 9437188
  24.3 17.3 %copy-start.3 = (s32[1,6]{1,0:T(1,128)S(1)}, s32[1,6]{1,0:T(1,128)}, u32[]{:S(2)}) copy-start(s32[1,6]{1,0:T(1,128)} %param.5) | copy-start | bytes 76
  24.3 19.5 %collective-permute-start.13 = (f32[256,512]{1,0:T(8,128)S(1)}, f32[256,512]{1,0:T(8,128)S(1)}, u32[]{:S(2)}, u32[]{:S(2)}) collective-permute-start(f32[256,512]{1,0:T(8,128)S(1)} %add.15), channel_id=1, source_target_pairs={{0,16},{4,12},{8,24},{12,4},{16,0},{20,28},{24,8},{28,20},{1,17},{... | collective-permute-start | bytes 1572872 | tf_op jit(solution)/shard_map/side_side/ppermute | solution.py:374
  44.7 1.2 %collective-permute-start.14 = (f32[8,128]{1,0:T(8,128)S(1)}, f32[8,128]{1,0:T(8,128)S(1)}, u32[]{:S(2)}, u32[]{:S(2)}) collective-permute-start(f32[8,128]{1,0:T(8,128)S(1)} %get-tuple-element.57.refs_0_.block_norm_ref), channel_id=1, source_target_pairs={{0,4},{4,0},{8,12},{12,8},{16,20},{20,16},{24,28},{28,24},{1,5},{5... | collective-permute-start | bytes 12296 | tf_op jit(solution)/shard_map/core_norm/ppermute | solution.py:374
  45.9 3.6 %collective-permute-start.15 = (f32[8,128]{1,0:T(8,128)S(1)}, f32[8,128]{1,0:T(8,128)S(1)}, u32[]{:S(2)}, u32[]{:S(2)}) collective-permute-start(f32[8,128]{1,0:T(8,128)S(1)} %sum.5.refs_0_), channel_id=1, source_target_pairs={{0,8},{4,12},{8,0},{12,4},{16,24},{20,28},{24,16},{28,20},{1,9},{5... | collective-permute-start | bytes 12296 | tf_op jit(solution)/shard_map/x_norm/ppermute | solution.py:374
  49.5 3.6 %collective-permute-start.16 = (f32[8,128]{1,0:T(8,128)S(1)}, f32[8,128]{1,0:T(8,128)S(1)}, u32[]{:S(2)}, u32[]{:S(2)}) collective-permute-start(f32[8,128]{1,0:T(8,128)S(1)} %sum.6.refs_0_), channel_id=1, source_target_pairs={{0,16},{4,20},{8,24},{12,28},{16,0},{20,4},{24,8},{28,12},{1,17},{... | collective-permute-start | bytes 12296 | tf_op jit(solution)/shard_map/y_norm/ppermute | solution.py:374
  53.1 3.6 %collective-permute-start.17 = (f32[8,128]{1,0:T(8,128)S(1)}, f32[8,128]{1,0:T(8,128)S(1)}, u32[]{:S(2)}, u32[]{:S(2)}) collective-permute-start(f32[8,128]{1,0:T(8,128)S(1)} %sum.7.refs_0_), channel_id=1, source_target_pairs={{0,1},{1,0},{2,3},{3,2},{4,5},{5,4},{6,7},{7,6},{8,9},{9,8},{10,11... | collective-permute-start | bytes 12296 | tf_op jit(solution)/shard_map/group_norm/ppermute | solution.py:421
  56.8 4.5 %collective-permute-start.18 = (f32[8,128]{1,0:T(8,128)S(1)}, f32[8,128]{1,0:T(8,128)S(1)}, u32[]{:S(2)}, u32[]{:S(2)}) collective-permute-start(f32[8,128]{1,0:T(8,128)S(1)} %sum.8.refs_0_), channel_id=1, source_target_pairs={{0,2},{1,3},{2,0},{3,1},{4,6},{5,7},{6,4},{7,5},{8,10},{9,11},{10,... | collective-permute-start | bytes 12296 | tf_op jit(solution)/shard_map/group_norm/ppermute | solution.py:421
  67.3 9.3 %collective-permute-start.20 = (f32[512,512]{1,0:T(8,128)S(1)}, f32[512,512]{1,0:T(8,128)S(1)}, u32[]{:S(2)}, u32[]{:S(2)}) collective-permute-start(f32[512,512]{1,0:T(8,128)S(1)} %get-tuple-element.71.refs_0_), channel_id=1, source_target_pairs={{0,4},{4,0},{8,12},{12,8},{16,20},{20,16},{24,28},{28,24},{1,5},{5... | collective-permute-start | bytes 3145736 | tf_op jit(solution)/shard_map/core_own/ppermute | solution.py:374
  67.3 9.2 %collective-permute-start.24 = (f32[256,512]{1,0:T(8,128)S(1)}, f32[256,512]{1,0:T(8,128)S(1)}, u32[]{:S(2)}, u32[]{:S(2)}) collective-permute-start(f32[256,512]{1,0:T(8,128)S(1)} %get-tuple-element.73), channel_id=1, source_target_pairs={{0,8},{4,20},{8,0},{12,28},{16,24},{20,4},{24,16},{28,12},{1,9},{5... | collective-permute-start | bytes 1572872 | tf_op jit(solution)/shard_map/link_own/ppermute | solution.py:374
  69.2 13.1 %collective-permute-start.19 = (f32[256,512]{1,0:T(8,128)S(1)}, f32[256,512]{1,0:T(8,128)S(1)}, u32[]{:S(2)}, u32[]{:S(2)}) collective-permute-start(f32[256,512]{1,0:T(8,128)S(1)} %get-tuple-element.70), channel_id=1, source_target_pairs={{0,8},{4,20},{8,0},{12,28},{16,24},{20,4},{24,16},{28,12},{1,9},{5... | collective-permute-start | bytes 1572872 | tf_op jit(solution)/shard_map/link_own/ppermute | solution.py:374
  76.6 16.8 %collective-permute-start.25 = (f32[512,512]{1,0:T(8,128)S(1)}, f32[512,512]{1,0:T(8,128)S(1)}, u32[]{:S(2)}, u32[]{:S(2)}) collective-permute-start(f32[512,512]{1,0:T(8,128)S(1)} %collective-permute-done.20.refs_1_), channel_id=1, source_target_pairs={{0,8},{4,20},{8,0},{12,28},{16,24},{20,4},{24,16},{28,12},{1,9},{5... | collective-permute-start | bytes 3145736 | tf_op jit(solution)/shard_map/link_sibling/ppermute | solution.py:374
  78.3 3.9 %collective-permute-start.27 = (f32[256,512]{1,0:T(8,128)S(1)}, f32[256,512]{1,0:T(8,128)S(1)}, u32[]{:S(2)}, u32[]{:S(2)}) collective-permute-start(f32[256,512]{1,0:T(8,128)S(1)} %collective-permute-done.24.refs_2_), channel_id=1, source_target_pairs={{0,4},{4,0},{8,12},{12,8},{16,20},{20,16},{24,28},{28,24},{1,5},{5... | collective-permute-start | bytes 1572872 | tf_op jit(solution)/shard_map/core_first/ppermute | solution.py:374
  82.2 11.2 %collective-permute-start.21 = (f32[256,512]{1,0:T(8,128)S(1)}, f32[256,512]{1,0:T(8,128)S(1)}, u32[]{:S(2)}, u32[]{:S(2)}) collective-permute-start(f32[256,512]{1,0:T(8,128)S(1)} %collective-permute-done.19.refs_3_), channel_id=1, source_target_pairs={{0,4},{4,0},{8,12},{12,8},{16,20},{20,16},{24,28},{28,24},{1,5},{5... | collective-permute-start | bytes 1572872 | tf_op jit(solution)/shard_map/core_first/ppermute | solution.py:374
  82.2 16.8 %collective-permute-start.28 = (f32[256,512]{1,0:T(8,128)S(1)}, f32[256,512]{1,0:T(8,128)S(1)}, u32[]{:S(2)}, u32[]{:S(2)}) collective-permute-start(f32[256,512]{1,0:T(8,128)S(1)} %collective-permute-done.27.refs_4_), channel_id=1, source_target_pairs={{0,8},{4,20},{8,0},{12,28},{16,24},{20,4},{24,16},{28,12},{1,9},{5... | collective-permute-start | bytes 1572872 | tf_op jit(solution)/shard_map/link_relayed/ppermute | solution.py:374
  93.4 11.2 %collective-permute-start.26 = (f32[512,512]{1,0:T(8,128)S(1)}, f32[512,512]{1,0:T(8,128)S(1)}, u32[]{:S(2)}, u32[]{:S(2)}) collective-permute-start(f32[512,512]{1,0:T(8,128)S(1)} %collective-permute-done.25.refs_0_), channel_id=1, source_target_pairs={{0,4},{4,0},{8,12},{12,8},{16,20},{20,16},{24,28},{28,24},{1,5},{5... | collective-permute-start | bytes 3145736 | tf_op jit(solution)/shard_map/core_second/ppermute | solution.py:374
  93.5 11.2 %collective-permute-start.22 = (f32[256,512]{1,0:T(8,128)S(1)}, f32[256,512]{1,0:T(8,128)S(1)}, u32[]{:S(2)}, u32[]{:S(2)}) collective-permute-start(f32[256,512]{1,0:T(8,128)S(1)} %collective-permute-done.21.refs_5_), channel_id=1, source_target_pairs={{0,8},{4,20},{8,0},{12,28},{16,24},{20,4},{24,16},{28,12},{1,9},{5... | collective-permute-start | bytes 1572872 | tf_op jit(solution)/shard_map/link_relayed/ppermute | solution.py:374
  99.1 5.6 %collective-permute-start.29 = (f32[256,512]{1,0:T(8,128)S(1)}, f32[256,512]{1,0:T(8,128)S(1)}, u32[]{:S(2)}, u32[]{:S(2)}) collective-permute-start(f32[256,512]{1,0:T(8,128)S(1)} %collective-permute-done.28.refs_2_), channel_id=1, source_target_pairs={{0,4},{4,0},{8,12},{12,8},{16,20},{20,16},{24,28},{28,24},{1,5},{5... | collective-permute-start | bytes 1572872 | tf_op jit(solution)/shard_map/core_relayed/ppermute | solution.py:374
  104.7 2.1 %collective-permute-start.23 = (f32[256,512]{1,0:T(8,128)S(1)}, f32[256,512]{1,0:T(8,128)S(1)}, u32[]{:S(2)}, u32[]{:S(2)}) collective-permute-start(f32[256,512]{1,0:T(8,128)S(1)} %collective-permute-done.22.refs_3_), channel_id=1, source_target_pairs={{0,4},{4,0},{8,12},{12,8},{16,20},{20,16},{24,28},{28,24},{1,5},{5... | collective-permute-start | bytes 1572872 | tf_op jit(solution)/shard_map/core_relayed/ppermute | solution.py:374
  (4 other events, 32.5 us)

commit v11 on v9

--- a/solution.py
+++ b/solution.py
@@ -392,14 +392,21 @@
         return lax.optimization_barrier((value, *others))[0]
 
     kinds = ("corner", "straight", "side", "self")
-    pieces = []
-    for pair in (kinds[:2], kinds[2:]):
-        pieces += pack_call(owner_row, me, grads, [(kind, half) for kind in pair for half in HALVES], width)
-    keys = [(kind, half) for kind in kinds for half in HALVES]
-    from_core = {key: to_core(value, key[0]) for key, value in zip(keys, pieces)}
-    from_link = {
-        key: to_link(own_plus(*key, from_core[key]), key[0]) for key in keys if key[0] in kinds[:2]
-    }
+    from_core, sums, from_link = {}, {}, {}
+
+    def exchange(kind, gate):
+        pieces = pack_call(owner_row, gate, grads, [(kind, half) for half in HALVES], width)
+        for half, value in zip(HALVES, pieces):
+            from_core[kind, half] = to_core(value, kind)
+
+    exchange("corner", me)
+    exchange("straight", after(me, from_core["corner", 0]))
+    for kind in kinds[:2]:
+        for half in HALVES:
+            sums[kind, half] = own_plus(kind, half, from_core[kind, half])
+            from_link[kind, half] = to_link(sums[kind, half], kind)
+    exchange("side", after(me, sums["corner", 1]))
+    exchange("self", after(me, from_link["corner", 0]))
     arrived = [
         to_side(own_plus("side", half, from_core["side", half], from_link["corner", half]), "side")
         for half in HALVES

time: 109 us -> 110 us (level)
  waiting for transfers between devices: 54.9 us -> 52.8 us
  starting transfers between devices: 24.6 us -> 26.6 us
  Pallas kernels: 25.9 us -> 27.1 us
    ppermute x29, waiting for transfers between devices: 54.4 us -> 52.2 us  [over(): return lax.ppermute(value, 'dp', pairs)]
    ppermute x29, starting transfers between devices: 19.1 us -> 21.1 us  [over(): return lax.ppermute(value, 'dp', pairs)]
    pallas_call x19 -> x21, Pallas kernels: 20.2 us -> 21.3 us  [local_call(): pl.pallas_call(kernel, in_specs=[pl.BlockSpec(memory_space=pltpu.SMEM)] *...]
  transfers between devices with their start and end apart: 32 -> 32, of which waited for: 14 -> 15; matrix products, arithmetic and copies ran while one was open for 0% -> 0% of each run, Pallas kernels for 16% -> 17%
where the time goes in v11:
time: 110 us
  waiting for transfers between devices  52.8 us (48%)
  Pallas kernels  27.1 us (25%)
  starting transfers between devices  26.6 us (24%)
  local copies, waits for them, and re-layouts  2.57 us (2%)
    ppermute x29, waiting for transfers between devices, over(): return lax.ppermute(value, 'dp', pairs)  52.2 us
    pallas_call x21, Pallas kernels, local_call(): pl.pallas_call(kernel, in_specs=[pl.BlockSpec(memory_space=pltpu.SMEM)] *...  21.3 us
    ppermute x29, starting transfers between devices, over(): return lax.ppermute(value, 'dp', pairs)  21.1 us
    pallas_call x3, Pallas kernels, assemble_call(): pl.pallas_call(kernel, in_specs=in_specs, out_specs=pl.BlockSpec(memory_s...  5.73 us
    ppermute x3, starting transfers between devices, paired_body(): norms.append(lax.ppermute(norm, 'mp', pairs))  5.51 us
    unnamed x12, local copies, waits for them, and re-layouts  2.57 us
  transfers between devices with their start and end apart: 32, of which 15 were waited for; matrix products, arithmetic and copies ran while one was open for 0% of the time, Pallas kernels for 17%

profile of v11, /device:TPU:0, one launch (start us, length us, event | category | flops | bytes accessed | tf_op | source)
XLA Modules:
  0.0 109.5 jit_solution(8240305970065493959)
XLA Ops:
  0.0 1.9 %copy-done = bf16[1,512,3072]{2,1,0:T(8,128)(2,1)S(1)} copy-done((bf16[1,512,3072]{2,1,0:T(8,128)(2,1)S(1)}, bf16[1,512,3072]{2,1,0:T(8,128)(2,1)}, u32[]{:S(2)}) %copy-start) | copy-done | bytes 3145752
  3.8 1.5 %collective-permute-done.refs_0_ = f32[256,512]{1,0:T(8,128)S(1)} collective-permute-done((f32[256,512]{1,0:T(8,128)S(1)}, f32[256,512]{1,0:T(8,128)S(1)}, u32[]{:S(2)}, u32[]{:S(2)}) %collective-permute-start) | collective-permute-done | bytes 524320 | tf_op jit(solution)/shard_map/core_corner/ppermute | solution.py:374
  5.8 2.9 %collective-permute-start.1 = (f32[256,512]{1,0:T(8,128)S(1)}, f32[256,512]{1,0:T(8,128)S(1)}, u32[]{:S(2)}, u32[]{:S(2)}) collective-permute-start(f32[256,512]{1,0:T(8,128)S(1)} %add.8), channel_id=1, source_target_pairs={{0,8},{4,20},{8,0},{12,28},{16,24},{20,4},{24,16},{28,12},{1,9},{5... | collective-permute-start | bytes 1572872 | tf_op jit(solution)/shard_map/link_corner/ppermute | solution.py:374
  11.3 0.9 collective-permute-start.12
  12.6 3.3 %collective-permute-done.1.refs_1_ = f32[256,512]{1,0:T(8,128)S(1)} collective-permute-done((f32[256,512]{1,0:T(8,128)S(1)}, f32[256,512]{1,0:T(8,128)S(1)}, u32[]{:S(2)}, u32[]{:S(2)}) %collective-permute-start.1) | collective-permute-done | bytes 524320 | tf_op jit(solution)/shard_map/link_corner/ppermute | solution.py:374
  17.7 2.1 %collective-permute-start.4 = (f32[256,512]{1,0:T(8,128)S(1)}, f32[256,512]{1,0:T(8,128)S(1)}, u32[]{:S(2)}, u32[]{:S(2)}) collective-permute-start(f32[256,512]{1,0:T(8,128)S(1)} %add.9), channel_id=1, source_target_pairs={{0,8},{4,20},{8,0},{12,28},{16,24},{20,4},{24,16},{28,12},{1,9},{5... | collective-permute-start | bytes 1572872 | tf_op jit(solution)/shard_map/link_straight/ppermute | solution.py:374
  20.5 1.6 %collective-permute-start.7 = (f32[256,512]{1,0:T(8,128)S(1)}, f32[256,512]{1,0:T(8,128)S(1)}, u32[]{:S(2)}, u32[]{:S(2)}) collective-permute-start(f32[256,512]{1,0:T(8,128)S(1)} %add.12), channel_id=1, source_target_pairs={{0,16},{4,12},{8,24},{12,4},{16,0},{20,28},{24,8},{28,20},{1,17},{... | collective-permute-start | bytes 1572872 | tf_op jit(solution)/shard_map/side_side/ppermute | solution.py:374
  24.2 1.7 %collective-permute-start.13 = (f32[256,512]{1,0:T(8,128)S(1)}, f32[256,512]{1,0:T(8,128)S(1)}, u32[]{:S(2)}, u32[]{:S(2)}) collective-permute-start(f32[256,512]{1,0:T(8,128)S(1)} %add.15), channel_id=1, source_target_pairs={{0,16},{4,12},{8,24},{12,4},{16,0},{20,28},{24,8},{28,20},{1,17},{... | collective-permute-start | bytes 1572872 | tf_op jit(solution)/shard_map/side_side/ppermute | solution.py:374
  25.9 5.5 %collective-permute-done.4.refs_1_ = f32[256,512]{1,0:T(8,128)S(1)} collective-permute-done((f32[256,512]{1,0:T(8,128)S(1)}, f32[256,512]{1,0:T(8,128)S(1)}, u32[]{:S(2)}, u32[]{:S(2)}) %collective-permute-start.4) | collective-permute-done | bytes 524320 | tf_op jit(solution)/shard_map/link_straight/ppermute | solution.py:374
  32.0 1.5 %square.1 = (f32[512,512]{1,0:T(8,128)S(1)}, f32[512,512]{1,0:T(8,128)S(1)}) custom-call(f32[512,512]{1,0:T(8,128)S(1)} %bitcast.34, f32[512,512]{1,0:T(8,128)S(1)} %bitcast.37), custom_call_target="tpu_custom_call" | custom-call | flops 1610612736 | bytes 4194304 | tf_op jit(solution)/shard_map/square/pallas_call | solution.py:128
  33.5 1.9 %collective-permute-done.7.arrival_ref = f32[256,512]{1,0:T(8,128)S(1)} collective-permute-done((f32[256,512]{1,0:T(8,128)S(1)}, f32[256,512]{1,0:T(8,128)S(1)}, u32[]{:S(2)}, u32[]{:S(2)}) %collective-permute-start.7) | collective-permute-done | bytes 524320 | tf_op jit(solution)/shard_map/side_side/ppermute | solution.py:374
  36.3 6.4 %collective-permute-done.10.refs_1_ = f32[256,512]{1,0:T(8,128)S(1)} collective-permute-done((f32[256,512]{1,0:T(8,128)S(1)}, f32[256,512]{1,0:T(8,128)S(1)}, u32[]{:S(2)}, u32[]{:S(2)}) %collective-permute-start.10) | collective-permute-done | bytes 524320 | tf_op jit(solution)/shard_map/link_straight/ppermute | solution.py:374
  43.5 0.9 join.3
  45.6 2.3 %collective-permute-start.15 = (f32[8,128]{1,0:T(8,128)S(1)}, f32[8,128]{1,0:T(8,128)S(1)}, u32[]{:S(2)}, u32[]{:S(2)}) collective-permute-start(f32[8,128]{1,0:T(8,128)S(1)} %sum.2.refs_0_), channel_id=1, source_target_pairs={{0,8},{4,12},{8,0},{12,4},{16,24},{20,28},{24,16},{28,20},{1,9},{5... | collective-permute-start | bytes 12296 | tf_op jit(solution)/shard_map/chip_norm/ppermute | solution.py:374
  47.9 2.4 %collective-permute-start.16 = (f32[8,128]{1,0:T(8,128)S(1)}, f32[8,128]{1,0:T(8,128)S(1)}, u32[]{:S(2)}, u32[]{:S(2)}) collective-permute-start(f32[8,128]{1,0:T(8,128)S(1)} %sum.2.refs_0_), channel_id=1, source_target_pairs={{0,16},{4,20},{8,24},{12,28},{16,0},{20,4},{24,8},{28,12},{1,17},{... | collective-permute-start | bytes 12296 | tf_op jit(solution)/shard_map/chip_norm/ppermute | solution.py:374
  50.3 1.5 %gram.1 = (f32[512,512]{1,0:T(8,128)S(1)}, f32[512,512]{1,0:T(8,128)S(1)}) custom-call(f32[256,512]{1,0:T(8,128)S(1)} %get-tuple-element.60.upper_ref, f32[256,512]{1,0:T(8,128)S(1)} %get-tuple-element.58.lower_ref), custom_call_target="tpu_custom_call" | custom-call | flops 1610612736 | bytes 3145728 | tf_op jit(solution)/shard_map/gram/pallas_call | solution.py:128
  51.8 1.7 %mix.2 = (f32[512,512]{1,0:T(8,128)S(1)}, f32[512,512]{1,0:T(8,128)S(1)}) custom-call(f32[512,512]{1,0:T(8,128)S(1)} %bitcast.35, f32[512,512]{1,0:T(8,128)S(1)} %get-tuple-element.61.gram_ref.refs_1_), custom_call_target="tpu_custom_call" | custom-call | flops 1610612736 | bytes 4194304 | tf_op jit(solution)/shard_map/mix/pallas_call | solution.py:128
  53.5 1.3 %collective-permute-done.17.refs_3_ = f32[8,128]{1,0:T(8,128)S(1)} collective-permute-done((f32[8,128]{1,0:T(8,128)S(1)}, f32[8,128]{1,0:T(8,128)S(1)}, u32[]{:S(2)}, u32[]{:S(2)}) %collective-permute-start.17) | collective-permute-done | bytes 4128 | tf_op jit(solution)/shard_map/chip_norm/ppermute | solution.py:374
  54.8 1.6 %collective-permute-start.18 = (f32[8,128]{1,0:T(8,128)S(1)}, f32[8,128]{1,0:T(8,128)S(1)}, u32[]{:S(2)}, u32[]{:S(2)}) collective-permute-start(f32[8,128]{1,0:T(8,128)S(1)} %sum.3.refs_10_), channel_id=1, source_target_pairs={{0,1},{1,2},{2,3},{3,0},{4,5},{5,6},{6,7},{7,4},{8,9},{9,10},{10,1... | collective-permute-start | bytes 12296 | tf_op jit(solution)/shard_map/group_norm/ppermute | solution.py:435
  56.4 2.6 %collective-permute-start.19 = (f32[8,128]{1,0:T(8,128)S(1)}, f32[8,128]{1,0:T(8,128)S(1)}, u32[]{:S(2)}, u32[]{:S(2)}) collective-permute-start(f32[8,128]{1,0:T(8,128)S(1)} %sum.3.refs_10_), channel_id=1, source_target_pairs={{0,2},{1,3},{2,0},{3,1},{4,6},{5,7},{6,4},{7,5},{8,10},{9,11},{10,... | collective-permute-start | bytes 12296 | tf_op jit(solution)/shard_map/group_norm/ppermute | solution.py:435
  59.0 1.3 %collective-permute-start.20 = (f32[8,128]{1,0:T(8,128)S(1)}, f32[8,128]{1,0:T(8,128)S(1)}, u32[]{:S(2)}, u32[]{:S(2)}) collective-permute-start(f32[8,128]{1,0:T(8,128)S(1)} %sum.3.refs_10_), channel_id=1, source_target_pairs={{0,3},{1,0},{2,1},{3,2},{4,7},{5,4},{6,5},{7,6},{8,11},{9,8},{10,9... | collective-permute-start | bytes 12296 | tf_op jit(solution)/shard_map/group_norm/ppermute | solution.py:435
  60.3 1.7 %mix.3 = (f32[512,512]{1,0:T(8,128)S(1)}, f32[512,512]{1,0:T(8,128)S(1)}) custom-call(f32[512,512]{1,0:T(8,128)S(1)} %bitcast.38, f32[512,512]{1,0:T(8,128)S(1)} %get-tuple-element.64.gram_ref.refs_6_), custom_call_target="tpu_custom_call" | custom-call | flops 1610612736 | bytes 4194304 | tf_op jit(solution)/shard_map/mix/pallas_call | solution.py:128
  62.6 5.9 %update.1 = (f32[512,512]{1,0:T(8,128)S(1)}, f32[256,512]{1,0:T(8,128)S(1)}, f32[256,512]{1,0:T(8,128)S(1)}) custom-call(f32[256,512]{1,0:T(8,128)S(1)} %get-tuple-element.60.upper_ref, f32[256,512]{1,0:T(8,128)S(1)} %get-tuple-element.58.lower_ref, f32[8,128]{1,0:T(8,128)S(1)} %get-tuple-element.59.refs_0_.block_norm_ref, f32[512,512]{1,0:T(8,128)S(1)} %bitcast.36, ...), custom_call_target="tpu_custom_call" | custom-call | flops 4831838208 | bytes 13651968 | tf_op jit(solution)/shard_map/update/pallas_call | solution.py:128
  69.2 1.5 %collective-permute-start.25 = (f32[256,512]{1,0:T(8,128)S(1)}, f32[256,512]{1,0:T(8,128)S(1)}, u32[]{:S(2)}, u32[]{:S(2)}) collective-permute-start(f32[256,512]{1,0:T(8,128)S(1)} %get-tuple-element.71), channel_id=1, source_target_pairs={{0,8},{4,20},{8,0},{12,28},{16,24},{20,4},{24,16},{28,12},{1,9},{5... | collective-permute-start | bytes 1572872 | tf_op jit(solution)/shard_map/link_own/ppermute | solution.py:374
  70.7 7.2 %collective-permute-done.21.refs_2_ = f32[256,512]{1,0:T(8,128)S(1)} collective-permute-done((f32[256,512]{1,0:T(8,128)S(1)}, f32[256,512]{1,0:T(8,128)S(1)}, u32[]{:S(2)}, u32[]{:S(2)}) %collective-permute-start.21) | collective-permute-done | bytes 524320 | tf_op jit(solution)/shard_map/link_own/ppermute | solution.py:374
  78.4 5.1 %collective-permute-done.25.refs_3_ = f32[256,512]{1,0:T(8,128)S(1)} collective-permute-done((f32[256,512]{1,0:T(8,128)S(1)}, f32[256,512]{1,0:T(8,128)S(1)}, u32[]{:S(2)}, u32[]{:S(2)}) %collective-permute-start.25) | collective-permute-done | bytes 524320 | tf_op jit(solution)/shard_map/link_own/ppermute | solution.py:374
  84.0 10.7 %collective-permute-done.30.refs_0_ = f32[512,512]{1,0:T(8,128)S(1)} collective-permute-done((f32[512,512]{1,0:T(8,128)S(1)}, f32[512,512]{1,0:T(8,128)S(1)}, u32[]{:S(2)}, u32[]{:S(2)}) %collective-permute-start.30) | collective-permute-done | bytes 1048608 | tf_op jit(solution)/shard_map/link_sibling/ppermute | solution.py:374
  95.2 2.6 %assemble.3.refs_4_ = f32[512,3072]{1,0:T(8,128)} custom-call(s32[6]{0:T(128)S(1)} %bitcast.31, s32[1]{0:T(128)} %bitcast.1.me_ref, f32[512,512]{1,0:T(8,128)S(1)} %get-tuple-element.69.refs_0_, f32[512,512]{1,0:T(8,128)S(1)} %collective-permute-done.22.refs_1_, f32[256,512]{1,0:T(8,128)S(1)} %collective-permute-done.21.refs_2_, ...), custom_call_target="tpu_custom_call" | custom-call | bytes 12582912 | tf_op jit(solution)/shard_map/assemble/pallas_call | solution.py:345
  97.8 2.5 %collective-permute-done.24.refs_2_ = f32[256,512]{1,0:T(8,128)S(1)} collective-permute-done((f32[256,512]{1,0:T(8,128)S(1)}, f32[256,512]{1,0:T(8,128)S(1)}, u32[]{:S(2)}, u32[]{:S(2)}) %collective-permute-start.24) | collective-permute-done | bytes 524320 | tf_op jit(solution)/shard_map/link_relayed/ppermute | solution.py:374
  100.3 5.6 %collective-permute-done.28.refs_3_ = f32[256,512]{1,0:T(8,128)S(1)} collective-permute-done((f32[256,512]{1,0:T(8,128)S(1)}, f32[256,512]{1,0:T(8,128)S(1)}, u32[]{:S(2)}, u32[]{:S(2)}) %collective-permute-start.28) | collective-permute-done | bytes 524320 | tf_op jit(solution)/shard_map/link_relayed/ppermute | solution.py:374
  105.9 1.6 %assemble.4.refs_2_ = f32[512,3072]{1,0:T(8,128)} custom-call(s32[6]{0:T(128)S(1)} %bitcast.32, s32[1]{0:T(128)} %bitcast.1.me_ref, f32[512,512]{1,0:T(8,128)S(1)} %collective-permute-done.30.refs_0_, f32[512,512]{1,0:T(8,128)S(1)} %collective-permute-done.31.refs_1_, ...), custom_call_target="tpu_custom_call", output_to_operand_aliasing={{}: (6, {})} | custom-call | bytes 8388608 | tf_op jit(solution)/shard_map/assemble/pallas_call | solution.py:345
  107.8 1.5 %assemble.5 = f32[512,3072]{1,0:T(8,128)} custom-call(s32[6]{0:T(128)S(1)} %bitcast.33, s32[1]{0:T(128)} %bitcast.1.me_ref, f32[256,512]{1,0:T(8,128)S(1)} %collective-permute-done.27.refs_0_, f32[256,512]{1,0:T(8,128)S(1)} %collective-permute-done.29.refs_1_, f32[512,3072]{1,0:T(8,128)} %assemble.4.refs_2_), custom_call_target="tpu_custom_call", output_to_operand_aliasing={{}: (4, {})} | custom-call | bytes 2097152 | tf_op jit(solution)/shard_map/assemble/pallas_call | solution.py:345
  (68 shorter events, 16.5 us)
Async XLA Ops:
  3.2 2.1 %collective-permute-start = (f32[256,512]{1,0:T(8,128)S(1)}, f32[256,512]{1,0:T(8,128)S(1)}, u32[]{:S(2)}, u32[]{:S(2)}) collective-permute-start(f32[256,512]{1,0:T(8,128)S(1)} %get-tuple-element.40), channel_id=1, source_target_pairs={{0,4},{4,0},{8,12},{12,8},{16,20},{20,16},{24,28},{28,24},{1,5},{5... | collective-permute-start | bytes 1572872 | tf_op jit(solution)/shard_map/core_corner/ppermute | solution.py:374
  3.7 5.8 %collective-permute-start.5 = (f32[256,512]{1,0:T(8,128)S(1)}, f32[256,512]{1,0:T(8,128)S(1)}, u32[]{:S(2)}, u32[]{:S(2)}) collective-permute-start(f32[256,512]{1,0:T(8,128)S(1)} %get-tuple-element.50), channel_id=1, source_target_pairs={{0,4},{4,0},{8,12},{12,8},{16,20},{20,16},{24,28},{28,24},{1,5},{5... | collective-permute-start | bytes 1572872 | tf_op jit(solution)/shard_map/core_corner/ppermute | solution.py:374
  5.8 10.1 %collective-permute-start.1 = (f32[256,512]{1,0:T(8,128)S(1)}, f32[256,512]{1,0:T(8,128)S(1)}, u32[]{:S(2)}, u32[]{:S(2)}) collective-permute-start(f32[256,512]{1,0:T(8,128)S(1)} %add.8), channel_id=1, source_target_pairs={{0,8},{4,20},{8,0},{12,28},{16,24},{20,4},{24,16},{28,12},{1,9},{5... | collective-permute-start | bytes 1572872 | tf_op jit(solution)/shard_map/link_corner/ppermute | solution.py:374
  9.4 7.2 %collective-permute-start.3 = (f32[256,512]{1,0:T(8,128)S(1)}, f32[256,512]{1,0:T(8,128)S(1)}, u32[]{:S(2)}, u32[]{:S(2)}) collective-permute-start(f32[256,512]{1,0:T(8,128)S(1)} %get-tuple-element.44), channel_id=1, source_target_pairs={{0,4},{4,0},{8,12},{12,8},{16,20},{20,16},{24,28},{28,24},{1,5},{5... | collective-permute-start | bytes 1572872 | tf_op jit(solution)/shard_map/core_straight/ppermute | solution.py:374
  10.7 7.0 %collective-permute-start.6 = (f32[256,512]{1,0:T(8,128)S(1)}, f32[256,512]{1,0:T(8,128)S(1)}, u32[]{:S(2)}, u32[]{:S(2)}) collective-permute-start(f32[256,512]{1,0:T(8,128)S(1)} %get-tuple-element.52), channel_id=1, source_target_pairs={{0,4},{4,0},{8,12},{12,8},{16,20},{20,16},{24,28},{28,24},{1,5},{5... | collective-permute-start | bytes 1572872 | tf_op jit(solution)/shard_map/core_side/ppermute | solution.py:374
  11.3 11.5 %collective-permute-start.12 = (f32[256,512]{1,0:T(8,128)S(1)}, f32[256,512]{1,0:T(8,128)S(1)}, u32[]{:S(2)}, u32[]{:S(2)}) collective-permute-start(f32[256,512]{1,0:T(8,128)S(1)} %add.11), channel_id=1, source_target_pairs={{0,8},{4,20},{8,0},{12,28},{16,24},{20,4},{24,16},{28,12},{1,9},{5... | collective-permute-start | bytes 1572872 | tf_op jit(solution)/shard_map/link_corner/ppermute | solution.py:374
  12.2 8.3 %collective-permute-start.9 = (f32[256,512]{1,0:T(8,128)S(1)}, f32[256,512]{1,0:T(8,128)S(1)}, u32[]{:S(2)}, u32[]{:S(2)}) collective-permute-start(f32[256,512]{1,0:T(8,128)S(1)} %get-tuple-element.55), channel_id=1, source_target_pairs={{0,4},{4,0},{8,12},{12,8},{16,20},{20,16},{24,28},{28,24},{1,5},{5... | collective-permute-start | bytes 1572872 | tf_op jit(solution)/shard_map/core_straight/ppermute | solution.py:374
  15.9 6.8 %collective-permute-start.11 = (f32[256,512]{1,0:T(8,128)S(1)}, f32[256,512]{1,0:T(8,128)S(1)}, u32[]{:S(2)}, u32[]{:S(2)}) collective-permute-start(f32[256,512]{1,0:T(8,128)S(1)} %get-tuple-element.56), channel_id=1, source_target_pairs={{0,4},{4,0},{8,12},{12,8},{16,20},{20,16},{24,28},{28,24},{1,5},{5... | collective-permute-start | bytes 1572872 | tf_op jit(solution)/shard_map/core_side/ppermute | solution.py:374
  16.6 7.6 %collective-permute-start.2 = (f32[256,512]{1,0:T(8,128)S(1)}, f32[256,512]{1,0:T(8,128)S(1)}, u32[]{:S(2)}, u32[]{:S(2)}) collective-permute-start(f32[256,512]{1,0:T(8,128)S(1)} %get-tuple-element.42), channel_id=1, source_target_pairs={{0,4},{4,0},{8,12},{12,8},{16,20},{20,16},{24,28},{28,24},{1,5},{5... | collective-permute-start | bytes 1572872 | tf_op jit(solution)/shard_map/core_self/ppermute | solution.py:374
  17.7 13.7 %collective-permute-start.4 = (f32[256,512]{1,0:T(8,128)S(1)}, f32[256,512]{1,0:T(8,128)S(1)}, u32[]{:S(2)}, u32[]{:S(2)}) collective-permute-start(f32[256,512]{1,0:T(8,128)S(1)} %add.9), channel_id=1, source_target_pairs={{0,8},{4,20},{8,0},{12,28},{16,24},{20,4},{24,16},{28,12},{1,9},{5... | collective-permute-start | bytes 1572872 | tf_op jit(solution)/shard_map/link_straight/ppermute | solution.py:374
  20.5 14.9 %collective-permute-start.7 = (f32[256,512]{1,0:T(8,128)S(1)}, f32[256,512]{1,0:T(8,128)S(1)}, u32[]{:S(2)}, u32[]{:S(2)}) collective-permute-start(f32[256,512]{1,0:T(8,128)S(1)} %add.12), channel_id=1, source_target_pairs={{0,16},{4,12},{8,24},{12,4},{16,0},{20,28},{24,8},{28,20},{1,17},{... | collective-permute-start | bytes 1572872 | tf_op jit(solution)/shard_map/side_side/ppermute | solution.py:374
  22.7 13.6 %collective-permute-start.8 = (f32[256,512]{1,0:T(8,128)S(1)}, f32[256,512]{1,0:T(8,128)S(1)}, u32[]{:S(2)}, u32[]{:S(2)}) collective-permute-start(f32[256,512]{1,0:T(8,128)S(1)} %get-tuple-element.54), channel_id=1, source_target_pairs={{0,4},{4,0},{8,12},{12,8},{16,20},{20,16},{24,28},{28,24},{1,5},{5... | collective-permute-start | bytes 1572872 | tf_op jit(solution)/shard_map/core_self/ppermute | solution.py:374
  22.8 19.9 %collective-permute-start.10 = (f32[256,512]{1,0:T(8,128)S(1)}, f32[256,512]{1,0:T(8,128)S(1)}, u32[]{:S(2)}, u32[]{:S(2)}) collective-permute-start(f32[256,512]{1,0:T(8,128)S(1)} %add.13), channel_id=1, source_target_pairs={{0,8},{4,20},{8,0},{12,28},{16,24},{20,4},{24,16},{28,12},{1,9},{5... | collective-permute-start | bytes 1572872 | tf_op jit(solution)/shard_map/link_straight/ppermute | solution.py:374
  24.2 19.3 %collective-permute-start.13 = (f32[256,512]{1,0:T(8,128)S(1)}, f32[256,512]{1,0:T(8,128)S(1)}, u32[]{:S(2)}, u32[]{:S(2)}) collective-permute-start(f32[256,512]{1,0:T(8,128)S(1)} %add.15), channel_id=1, source_target_pairs={{0,16},{4,12},{8,24},{12,4},{16,0},{20,28},{24,8},{28,20},{1,17},{... | collective-permute-start | bytes 1572872 | tf_op jit(solution)/shard_map/side_side/ppermute | solution.py:374
  44.3 1.2 %collective-permute-start.14 = (f32[8,128]{1,0:T(8,128)S(1)}, f32[8,128]{1,0:T(8,128)S(1)}, u32[]{:S(2)}, u32[]{:S(2)}) collective-permute-start(f32[8,128]{1,0:T(8,128)S(1)} %get-tuple-element.59.refs_0_.block_norm_ref), channel_id=1, source_target_pairs={{0,4},{4,0},{8,12},{12,8},{16,20},{20,16},{24,28},{28,24},{1,5},{5... | collective-permute-start | bytes 12296 | tf_op jit(solution)/shard_map/core_norm/ppermute | solution.py:374
  45.6 7.9 %collective-permute-start.15 = (f32[8,128]{1,0:T(8,128)S(1)}, f32[8,128]{1,0:T(8,128)S(1)}, u32[]{:S(2)}, u32[]{:S(2)}) collective-permute-start(f32[8,128]{1,0:T(8,128)S(1)} %sum.2.refs_0_), channel_id=1, source_target_pairs={{0,8},{4,12},{8,0},{12,4},{16,24},{20,28},{24,16},{28,20},{1,9},{5... | collective-permute-start | bytes 12296 | tf_op jit(solution)/shard_map/chip_norm/ppermute | solution.py:374
  47.9 5.7 %collective-permute-start.16 = (f32[8,128]{1,0:T(8,128)S(1)}, f32[8,128]{1,0:T(8,128)S(1)}, u32[]{:S(2)}, u32[]{:S(2)}) collective-permute-start(f32[8,128]{1,0:T(8,128)S(1)} %sum.2.refs_0_), channel_id=1, source_target_pairs={{0,16},{4,20},{8,24},{12,28},{16,0},{20,4},{24,8},{28,12},{1,17},{... | collective-permute-start | bytes 12296 | tf_op jit(solution)/shard_map/chip_norm/ppermute | solution.py:374
  50.3 4.5 %collective-permute-start.17 = (f32[8,128]{1,0:T(8,128)S(1)}, f32[8,128]{1,0:T(8,128)S(1)}, u32[]{:S(2)}, u32[]{:S(2)}) collective-permute-start(f32[8,128]{1,0:T(8,128)S(1)} %sum.2.refs_0_), channel_id=1, source_target_pairs={{0,24},{4,28},{8,16},{12,20},{16,8},{20,12},{24,0},{28,4},{1,25},{... | collective-permute-start | bytes 12296 | tf_op jit(solution)/shard_map/chip_norm/ppermute | solution.py:374
  54.8 7.2 %collective-permute-start.18 = (f32[8,128]{1,0:T(8,128)S(1)}, f32[8,128]{1,0:T(8,128)S(1)}, u32[]{:S(2)}, u32[]{:S(2)}) collective-permute-start(f32[8,128]{1,0:T(8,128)S(1)} %sum.3.refs_10_), channel_id=1, source_target_pairs={{0,1},{1,2},{2,3},{3,0},{4,5},{5,6},{6,7},{7,4},{8,9},{9,10},{10,1... | collective-permute-start | bytes 12296 | tf_op jit(solution)/shard_map/group_norm/ppermute | solution.py:435
  56.4 5.7 %collective-permute-start.19 = (f32[8,128]{1,0:T(8,128)S(1)}, f32[8,128]{1,0:T(8,128)S(1)}, u32[]{:S(2)}, u32[]{:S(2)}) collective-permute-start(f32[8,128]{1,0:T(8,128)S(1)} %sum.3.refs_10_), channel_id=1, source_target_pairs={{0,2},{1,3},{2,0},{3,1},{4,6},{5,7},{6,4},{7,5},{8,10},{9,11},{10,... | collective-permute-start | bytes 12296 | tf_op jit(solution)/shard_map/group_norm/ppermute | solution.py:435
  59.0 3.6 %collective-permute-start.20 = (f32[8,128]{1,0:T(8,128)S(1)}, f32[8,128]{1,0:T(8,128)S(1)}, u32[]{:S(2)}, u32[]{:S(2)}) collective-permute-start(f32[8,128]{1,0:T(8,128)S(1)} %sum.3.refs_10_), channel_id=1, source_target_pairs={{0,3},{1,0},{2,1},{3,2},{4,7},{5,4},{6,5},{7,6},{8,11},{9,8},{10,9... | collective-permute-start | bytes 12296 | tf_op jit(solution)/shard_map/group_norm/ppermute | solution.py:435
  68.5 9.3 %collective-permute-start.22 = (f32[512,512]{1,0:T(8,128)S(1)}, f32[512,512]{1,0:T(8,128)S(1)}, u32[]{:S(2)}, u32[]{:S(2)}) collective-permute-start(f32[512,512]{1,0:T(8,128)S(1)} %get-tuple-element.69.refs_0_), channel_id=1, source_target_pairs={{0,4},{4,0},{8,12},{12,8},{16,20},{20,16},{24,28},{28,24},{1,5},{5... | collective-permute-start | bytes 3145736 | tf_op jit(solution)/shard_map/core_own/ppermute | solution.py:374
  68.6 9.2 %collective-permute-start.21 = (f32[256,512]{1,0:T(8,128)S(1)}, f32[256,512]{1,0:T(8,128)S(1)}, u32[]{:S(2)}, u32[]{:S(2)}) collective-permute-start(f32[256,512]{1,0:T(8,128)S(1)} %get-tuple-element.68), channel_id=1, source_target_pairs={{0,8},{4,20},{8,0},{12,28},{16,24},{20,4},{24,16},{28,12},{1,9},{5... | collective-permute-start | bytes 1572872 | tf_op jit(solution)/shard_map/link_own/ppermute | solution.py:374
  69.2 14.3 %collective-permute-start.25 = (f32[256,512]{1,0:T(8,128)S(1)}, f32[256,512]{1,0:T(8,128)S(1)}, u32[]{:S(2)}, u32[]{:S(2)}) collective-permute-start(f32[256,512]{1,0:T(8,128)S(1)} %get-tuple-element.71), channel_id=1, source_target_pairs={{0,8},{4,20},{8,0},{12,28},{16,24},{20,4},{24,16},{28,12},{1,9},{5... | collective-permute-start | bytes 1572872 | tf_op jit(solution)/shard_map/link_own/ppermute | solution.py:374
  77.8 16.8 %collective-permute-start.30 = (f32[512,512]{1,0:T(8,128)S(1)}, f32[512,512]{1,0:T(8,128)S(1)}, u32[]{:S(2)}, u32[]{:S(2)}) collective-permute-start(f32[512,512]{1,0:T(8,128)S(1)} %collective-permute-done.22.refs_1_), channel_id=1, source_target_pairs={{0,8},{4,20},{8,0},{12,28},{16,24},{20,4},{24,16},{28,12},{1,9},{5... | collective-permute-start | bytes 3145736 | tf_op jit(solution)/shard_map/link_sibling/ppermute | solution.py:374
  78.4 5.1 %collective-permute-start.23 = (f32[256,512]{1,0:T(8,128)S(1)}, f32[256,512]{1,0:T(8,128)S(1)}, u32[]{:S(2)}, u32[]{:S(2)}) collective-permute-start(f32[256,512]{1,0:T(8,128)S(1)} %collective-permute-done.21.refs_2_), channel_id=1, source_target_pairs={{0,4},{4,0},{8,12},{12,8},{16,20},{20,16},{24,28},{28,24},{1,5},{5... | collective-permute-start | bytes 1572872 | tf_op jit(solution)/shard_map/core_first/ppermute | solution.py:374
  83.5 11.2 %collective-permute-start.26 = (f32[256,512]{1,0:T(8,128)S(1)}, f32[256,512]{1,0:T(8,128)S(1)}, u32[]{:S(2)}, u32[]{:S(2)}) collective-permute-start(f32[256,512]{1,0:T(8,128)S(1)} %collective-permute-done.25.refs_3_), channel_id=1, source_target_pairs={{0,4},{4,0},{8,12},{12,8},{16,20},{20,16},{24,28},{28,24},{1,5},{5... | collective-permute-start | bytes 1572872 | tf_op jit(solution)/shard_map/core_first/ppermute | solution.py:374
  83.5 16.8 %collective-permute-start.24 = (f32[256,512]{1,0:T(8,128)S(1)}, f32[256,512]{1,0:T(8,128)S(1)}, u32[]{:S(2)}, u32[]{:S(2)}) collective-permute-start(f32[256,512]{1,0:T(8,128)S(1)} %collective-permute-done.23.refs_4_), channel_id=1, source_target_pairs={{0,8},{4,20},{8,0},{12,28},{16,24},{20,4},{24,16},{28,12},{1,9},{5... | collective-permute-start | bytes 1572872 | tf_op jit(solution)/shard_map/link_relayed/ppermute | solution.py:374
  94.7 11.2 %collective-permute-start.31 = (f32[512,512]{1,0:T(8,128)S(1)}, f32[512,512]{1,0:T(8,128)S(1)}, u32[]{:S(2)}, u32[]{:S(2)}) collective-permute-start(f32[512,512]{1,0:T(8,128)S(1)} %collective-permute-done.30.refs_0_), channel_id=1, source_target_pairs={{0,4},{4,0},{8,12},{12,8},{16,20},{20,16},{24,28},{28,24},{1,5},{5... | collective-permute-start | bytes 3145736 | tf_op jit(solution)/shard_map/core_second/ppermute | solution.py:374
  94.7 11.2 %collective-permute-start.28 = (f32[256,512]{1,0:T(8,128)S(1)}, f32[256,512]{1,0:T(8,128)S(1)}, u32[]{:S(2)}, u32[]{:S(2)}) collective-permute-start(f32[256,512]{1,0:T(8,128)S(1)} %collective-permute-done.26.refs_5_), channel_id=1, source_target_pairs={{0,8},{4,20},{8,0},{12,28},{16,24},{20,4},{24,16},{28,12},{1,9},{5... | collective-permute-start | bytes 1572872 | tf_op jit(solution)/shard_map/link_relayed/ppermute | solution.py:374
  100.3 7.2 %collective-permute-start.27 = (f32[256,512]{1,0:T(8,128)S(1)}, f32[256,512]{1,0:T(8,128)S(1)}, u32[]{:S(2)}, u32[]{:S(2)}) collective-permute-start(f32[256,512]{1,0:T(8,128)S(1)} %collective-permute-done.24.refs_2_), channel_id=1, source_target_pairs={{0,4},{4,0},{8,12},{12,8},{16,20},{20,16},{24,28},{28,24},{1,5},{5... | collective-permute-start | bytes 1572872 | tf_op jit(solution)/shard_map/core_relayed/ppermute | solution.py:374
  105.9 1.9 %collective-permute-start.29 = (f32[256,512]{1,0:T(8,128)S(1)}, f32[256,512]{1,0:T(8,128)S(1)}, u32[]{:S(2)}, u32[]{:S(2)}) collective-permute-start(f32[256,512]{1,0:T(8,128)S(1)} %collective-permute-done.28.refs_3_), channel_id=1, source_target_pairs={{0,4},{4,0},{8,12},{12,8},{16,20},{20,16},{24,28},{28,24},{1,5},{5... | collective-permute-start | bytes 1572872 | tf_op jit(solution)/shard_map/core_relayed/ppermute | solution.py:374
  (6 other events, 55.4 us)

commit v12 on v9

--- a/solution.py
+++ b/solution.py
@@ -423,7 +423,8 @@
     norm = sum_call(after(norm, sides[0][4]), *chip_norms)
     norms = [norm]
     for shift in range(1, group_count):
-        pairs = [(i, (i + shift) % group_count) for i in range(group_count)]
+        both_ways = group_count & (group_count - 1) == 0
+        pairs = [(i, i ^ shift if both_ways else (i + shift) % group_count) for i in range(group_count)]
         with jax.named_scope("group_norm"):
             norms.append(lax.ppermute(norm, "mp", pairs))
     sides[1] += tuple(mix_call(*sides[1][:2]))

time: 109 us -> 110 us (level)
  waiting for transfers between devices: 54.9 us -> 57.5 us
  starting transfers between devices: 24.6 us -> 23.4 us
    ppermute x3, waiting for transfers between devices: 0.53 us -> 3.46 us  [paired_body(): norms.append(lax.ppermute(norm, 'mp', pairs))]
    ppermute x3, starting transfers between devices: 5.51 us -> 4.39 us  [paired_body(): norms.append(lax.ppermute(norm, 'mp', pairs))]
  transfers between devices with their start and end apart: 32 -> 32, of which waited for: 14 -> 13; matrix products, arithmetic and copies ran while one was open for 0% -> 0% of each run, Pallas kernels for 16% -> 16%
where the time goes in v12:
time: 110 us; the launch traced here: 109 us
  waiting for transfers between devices  57.5 us (52%)
  Pallas kernels  25.3 us (23%)
  starting transfers between devices  23.4 us (21%)
  local copies, waits for them, and re-layouts  2.56 us (2%)
    ppermute x29, waiting for transfers between devices, over(): return lax.ppermute(value, 'dp', pairs)  54.1 us
    pallas_call x19, Pallas kernels, local_call(): pl.pallas_call(kernel, in_specs=[pl.BlockSpec(memory_space=pltpu.SMEM)] *...  20.2 us
    ppermute x29, starting transfers between devices, over(): return lax.ppermute(value, 'dp', pairs)  19 us
    pallas_call x3, Pallas kernels, assemble_call(): pl.pallas_call(kernel, in_specs=in_specs, out_specs=pl.BlockSpec(memory_s...  5.11 us
    ppermute x3, starting transfers between devices, paired_body(): norms.append(lax.ppermute(norm, 'mp', pairs))  4.39 us
    ppermute x3, waiting for transfers between devices, paired_body(): norms.append(lax.ppermute(norm, 'mp', pairs))  3.46 us
    unnamed x12, local copies, waits for them, and re-layouts  2.56 us
  transfers between devices with their start and end apart: 32, of which 13 were waited for; matrix products, arithmetic and copies ran while one was open for 0% of the time, Pallas kernels for 16%

profile of v12, /device:TPU:0, one launch (start us, length us, event | category | flops | bytes accessed | tf_op | source)
XLA Modules:
  0.0 109.1 jit_solution(18327982521368658141)
XLA Ops:
  0.0 1.9 %copy-done = bf16[1,512,3072]{2,1,0:T(8,128)(2,1)S(1)} copy-done((bf16[1,512,3072]{2,1,0:T(8,128)(2,1)S(1)}, bf16[1,512,3072]{2,1,0:T(8,128)(2,1)}, u32[]{:S(2)}) %copy-start) | copy-done | bytes 3145752
  6.1 2.7 %collective-permute-start.5 = (f32[256,512]{1,0:T(8,128)S(1)}, f32[256,512]{1,0:T(8,128)S(1)}, u32[]{:S(2)}, u32[]{:S(2)}) collective-permute-start(f32[256,512]{1,0:T(8,128)S(1)} %add.10), channel_id=1, source_target_pairs={{0,8},{4,20},{8,0},{12,28},{16,24},{20,4},{24,16},{28,12},{1,9},{5... | collective-permute-start | bytes 1572872 | tf_op jit(solution)/shard_map/link_corner/ppermute | solution.py:374
  9.6 1.6 %collective-permute-start.12 = (f32[256,512]{1,0:T(8,128)S(1)}, f32[256,512]{1,0:T(8,128)S(1)}, u32[]{:S(2)}, u32[]{:S(2)}) collective-permute-start(f32[256,512]{1,0:T(8,128)S(1)} %add.14), channel_id=1, source_target_pairs={{0,8},{4,20},{8,0},{12,28},{16,24},{20,4},{24,16},{28,12},{1,9},{5... | collective-permute-start | bytes 1572872 | tf_op jit(solution)/shard_map/link_corner/ppermute | solution.py:374
  13.1 2.9 %collective-permute-done.5.refs_1_ = f32[256,512]{1,0:T(8,128)S(1)} collective-permute-done((f32[256,512]{1,0:T(8,128)S(1)}, f32[256,512]{1,0:T(8,128)S(1)}, u32[]{:S(2)}, u32[]{:S(2)}) %collective-permute-start.5) | collective-permute-done | bytes 524320 | tf_op jit(solution)/shard_map/link_corner/ppermute | solution.py:374
  16.6 2.1 %collective-permute-start.9 = (f32[256,512]{1,0:T(8,128)S(1)}, f32[256,512]{1,0:T(8,128)S(1)}, u32[]{:S(2)}, u32[]{:S(2)}) collective-permute-start(f32[256,512]{1,0:T(8,128)S(1)} %add.12), channel_id=1, source_target_pairs={{0,8},{4,20},{8,0},{12,28},{16,24},{20,4},{24,16},{28,12},{1,9},{5... | collective-permute-start | bytes 1572872 | tf_op jit(solution)/shard_map/link_straight/ppermute | solution.py:374
  18.7 2.9 %collective-permute-done.12.refs_1_ = f32[256,512]{1,0:T(8,128)S(1)} collective-permute-done((f32[256,512]{1,0:T(8,128)S(1)}, f32[256,512]{1,0:T(8,128)S(1)}, u32[]{:S(2)}, u32[]{:S(2)}) %collective-permute-start.12) | collective-permute-done | bytes 524320 | tf_op jit(solution)/shard_map/link_corner/ppermute | solution.py:374
  21.6 2.0 %collective-permute-start.6 = (f32[256,512]{1,0:T(8,128)S(1)}, f32[256,512]{1,0:T(8,128)S(1)}, u32[]{:S(2)}, u32[]{:S(2)}) collective-permute-start(f32[256,512]{1,0:T(8,128)S(1)} %add.11), channel_id=1, source_target_pairs={{0,16},{4,12},{8,24},{12,4},{16,0},{20,28},{24,8},{28,20},{1,17},{... | collective-permute-start | bytes 1572872 | tf_op jit(solution)/shard_map/side_side/ppermute | solution.py:374
  24.4 5.9 %collective-permute-done.2.refs_1_ = f32[256,512]{1,0:T(8,128)S(1)} collective-permute-done((f32[256,512]{1,0:T(8,128)S(1)}, f32[256,512]{1,0:T(8,128)S(1)}, u32[]{:S(2)}, u32[]{:S(2)}) %collective-permute-start.2) | collective-permute-done | bytes 524320 | tf_op jit(solution)/shard_map/link_straight/ppermute | solution.py:374
  31.0 1.5 %square.1 = (f32[512,512]{1,0:T(8,128)S(1)}, f32[512,512]{1,0:T(8,128)S(1)}) custom-call(f32[512,512]{1,0:T(8,128)S(1)} %bitcast.30, f32[512,512]{1,0:T(8,128)S(1)} %bitcast.33), custom_call_target="tpu_custom_call" | custom-call | flops 1610612736 | bytes 4194304 | tf_op jit(solution)/shard_map/square/pallas_call | solution.py:128
  32.4 9.1 %collective-permute-done.9.refs_1_ = f32[256,512]{1,0:T(8,128)S(1)} collective-permute-done((f32[256,512]{1,0:T(8,128)S(1)}, f32[256,512]{1,0:T(8,128)S(1)}, u32[]{:S(2)}, u32[]{:S(2)}) %collective-permute-start.9) | collective-permute-done | bytes 524320 | tf_op jit(solution)/shard_map/link_straight/ppermute | solution.py:374
  42.2 0.9 join.2
  43.8 0.9 join.3
  44.8 1.1 collective-permute-done.14.refs_1_
  45.9 1.8 %collective-permute-start.15 = (f32[8,128]{1,0:T(8,128)S(1)}, f32[8,128]{1,0:T(8,128)S(1)}, u32[]{:S(2)}, u32[]{:S(2)}) collective-permute-start(f32[8,128]{1,0:T(8,128)S(1)} %sum.2.refs_0_), channel_id=1, source_target_pairs={{0,8},{4,12},{8,0},{12,4},{16,24},{20,28},{24,16},{28,20},{1,9},{5... | collective-permute-start | bytes 12296 | tf_op jit(solution)/shard_map/chip_norm/ppermute | solution.py:374
  47.7 1.5 %collective-permute-start.16 = (f32[8,128]{1,0:T(8,128)S(1)}, f32[8,128]{1,0:T(8,128)S(1)}, u32[]{:S(2)}, u32[]{:S(2)}) collective-permute-start(f32[8,128]{1,0:T(8,128)S(1)} %sum.2.refs_0_), channel_id=1, source_target_pairs={{0,16},{4,20},{8,24},{12,28},{16,0},{20,4},{24,8},{28,12},{1,17},{... | collective-permute-start | bytes 12296 | tf_op jit(solution)/shard_map/chip_norm/ppermute | solution.py:374
  49.4 1.5 %gram.1 = (f32[512,512]{1,0:T(8,128)S(1)}, f32[512,512]{1,0:T(8,128)S(1)}) custom-call(f32[256,512]{1,0:T(8,128)S(1)} %get-tuple-element.54.upper_ref, f32[256,512]{1,0:T(8,128)S(1)} %get-tuple-element.52.lower_ref), custom_call_target="tpu_custom_call" | custom-call | flops 1610612736 | bytes 3145728 | tf_op jit(solution)/shard_map/gram/pallas_call | solution.py:128
  50.9 1.7 %mix.2 = (f32[512,512]{1,0:T(8,128)S(1)}, f32[512,512]{1,0:T(8,128)S(1)}) custom-call(f32[512,512]{1,0:T(8,128)S(1)} %bitcast.31, f32[512,512]{1,0:T(8,128)S(1)} %get-tuple-element.55.gram_ref.refs_1_), custom_call_target="tpu_custom_call" | custom-call | flops 1610612736 | bytes 4194304 | tf_op jit(solution)/shard_map/mix/pallas_call | solution.py:128
  52.6 1.1 collective-permute-done.17.refs_3_
  53.7 1.6 %collective-permute-start.18 = (f32[8,128]{1,0:T(8,128)S(1)}, f32[8,128]{1,0:T(8,128)S(1)}, u32[]{:S(2)}, u32[]{:S(2)}) collective-permute-start(f32[8,128]{1,0:T(8,128)S(1)} %sum.3.refs_10_), channel_id=1, source_target_pairs={{0,1},{1,0},{2,3},{3,2},{4,5},{5,4},{6,7},{7,6},{8,9},{9,8},{10,11... | collective-permute-start | bytes 12296 | tf_op jit(solution)/shard_map/group_norm/ppermute | solution.py:429
  55.3 2.6 %collective-permute-start.19 = (f32[8,128]{1,0:T(8,128)S(1)}, f32[8,128]{1,0:T(8,128)S(1)}, u32[]{:S(2)}, u32[]{:S(2)}) collective-permute-start(f32[8,128]{1,0:T(8,128)S(1)} %sum.3.refs_10_), channel_id=1, source_target_pairs={{0,2},{1,3},{2,0},{3,1},{4,6},{5,7},{6,4},{7,5},{8,10},{9,11},{10,... | collective-permute-start | bytes 12296 | tf_op jit(solution)/shard_map/group_norm/ppermute | solution.py:429
  58.1 1.7 %mix.3 = (f32[512,512]{1,0:T(8,128)S(1)}, f32[512,512]{1,0:T(8,128)S(1)}) custom-call(f32[512,512]{1,0:T(8,128)S(1)} %bitcast.34, f32[512,512]{1,0:T(8,128)S(1)} %get-tuple-element.58.gram_ref.refs_6_), custom_call_target="tpu_custom_call" | custom-call | flops 1610612736 | bytes 4194304 | tf_op jit(solution)/shard_map/mix/pallas_call | solution.py:128
  59.8 3.5 %collective-permute-done.20.refs_13_ = f32[8,128]{1,0:T(8,128)S(1)} collective-permute-done((f32[8,128]{1,0:T(8,128)S(1)}, f32[8,128]{1,0:T(8,128)S(1)}, u32[]{:S(2)}, u32[]{:S(2)}) %collective-permute-start.20) | collective-permute-done | bytes 4128 | tf_op jit(solution)/shard_map/group_norm/ppermute | solution.py:429
  63.3 5.9 %update.1 = (f32[512,512]{1,0:T(8,128)S(1)}, f32[256,512]{1,0:T(8,128)S(1)}, f32[256,512]{1,0:T(8,128)S(1)}) custom-call(f32[256,512]{1,0:T(8,128)S(1)} %get-tuple-element.54.upper_ref, f32[256,512]{1,0:T(8,128)S(1)} %get-tuple-element.52.lower_ref, f32[8,128]{1,0:T(8,128)S(1)} %get-tuple-element.53.refs_0_.block_norm_ref, f32[512,512]{1,0:T(8,128)S(1)} %bitcast.32, ...), custom_call_target="tpu_custom_call" | custom-call | flops 4831838208 | bytes 13651968 | tf_op jit(solution)/shard_map/update/pallas_call | solution.py:128
  69.3 0.8 collective-permute-start.21
  70.1 1.3 %collective-permute-start.25 = (f32[256,512]{1,0:T(8,128)S(1)}, f32[256,512]{1,0:T(8,128)S(1)}, u32[]{:S(2)}, u32[]{:S(2)}) collective-permute-start(f32[256,512]{1,0:T(8,128)S(1)} %get-tuple-element.65), channel_id=1, source_target_pairs={{0,8},{4,20},{8,0},{12,28},{16,24},{20,4},{24,16},{28,12},{1,9},{5... | collective-permute-start | bytes 1572872 | tf_op jit(solution)/shard_map/link_own/ppermute | solution.py:374
  71.4 7.2 %collective-permute-done.21.refs_2_ = f32[256,512]{1,0:T(8,128)S(1)} collective-permute-done((f32[256,512]{1,0:T(8,128)S(1)}, f32[256,512]{1,0:T(8,128)S(1)}, u32[]{:S(2)}, u32[]{:S(2)}) %collective-permute-start.21) | collective-permute-done | bytes 524320 | tf_op jit(solution)/shard_map/link_own/ppermute | solution.py:374
  79.3 4.8 %collective-permute-done.25.refs_3_ = f32[256,512]{1,0:T(8,128)S(1)} collective-permute-done((f32[256,512]{1,0:T(8,128)S(1)}, f32[256,512]{1,0:T(8,128)S(1)}, u32[]{:S(2)}, u32[]{:S(2)}) %collective-permute-start.25) | collective-permute-done | bytes 524320 | tf_op jit(solution)/shard_map/link_own/ppermute | solution.py:374
  84.9 10.5 %collective-permute-done.30.refs_0_ = f32[512,512]{1,0:T(8,128)S(1)} collective-permute-done((f32[512,512]{1,0:T(8,128)S(1)}, f32[512,512]{1,0:T(8,128)S(1)}, u32[]{:S(2)}, u32[]{:S(2)}) %collective-permute-start.30) | collective-permute-done | bytes 1048608 | tf_op jit(solution)/shard_map/link_sibling/ppermute | solution.py:374
  96.2 2.6 %assemble.3.refs_4_ = f32[512,3072]{1,0:T(8,128)} custom-call(s32[6]{0:T(128)S(1)} %bitcast.27, s32[1]{0:T(128)} %bitcast.1.me_ref, f32[512,512]{1,0:T(8,128)S(1)} %get-tuple-element.63.refs_0_, f32[512,512]{1,0:T(8,128)S(1)} %collective-permute-done.22.refs_1_, f32[256,512]{1,0:T(8,128)S(1)} %collective-permute-done.21.refs_2_, ...), custom_call_target="tpu_custom_call" | custom-call | bytes 12582912 | tf_op jit(solution)/shard_map/assemble/pallas_call | solution.py:345
  98.8 2.2 %collective-permute-done.24.refs_2_ = f32[256,512]{1,0:T(8,128)S(1)} collective-permute-done((f32[256,512]{1,0:T(8,128)S(1)}, f32[256,512]{1,0:T(8,128)S(1)}, u32[]{:S(2)}, u32[]{:S(2)}) %collective-permute-start.24) | collective-permute-done | bytes 524320 | tf_op jit(solution)/shard_map/link_relayed/ppermute | solution.py:374
  101.0 5.6 %collective-permute-done.28.refs_3_ = f32[256,512]{1,0:T(8,128)S(1)} collective-permute-done((f32[256,512]{1,0:T(8,128)S(1)}, f32[256,512]{1,0:T(8,128)S(1)}, u32[]{:S(2)}, u32[]{:S(2)}) %collective-permute-start.28) | collective-permute-done | bytes 524320 | tf_op jit(solution)/shard_map/link_relayed/ppermute | solution.py:374
  106.6 1.9 %assemble.4.refs_2_ = f32[512,3072]{1,0:T(8,128)} custom-call(s32[6]{0:T(128)S(1)} %bitcast.28, s32[1]{0:T(128)} %bitcast.1.me_ref, f32[512,512]{1,0:T(8,128)S(1)} %collective-permute-done.30.refs_0_, f32[512,512]{1,0:T(8,128)S(1)} %collective-permute-done.31.refs_1_, ...), custom_call_target="tpu_custom_call", output_to_operand_aliasing={{}: (6, {})} | custom-call | bytes 8388608 | tf_op jit(solution)/shard_map/assemble/pallas_call | solution.py:345
  (66 shorter events, 13.8 us)
Async XLA Ops:
  3.2 2.3 %collective-permute-start.4 = (f32[256,512]{1,0:T(8,128)S(1)}, f32[256,512]{1,0:T(8,128)S(1)}, u32[]{:S(2)}, u32[]{:S(2)}) collective-permute-start(f32[256,512]{1,0:T(8,128)S(1)} %get-tuple-element.45), channel_id=1, source_target_pairs={{0,4},{4,0},{8,12},{12,8},{16,20},{20,16},{24,28},{28,24},{1,5},{5... | collective-permute-start | bytes 1572872 | tf_op jit(solution)/shard_map/core_corner/ppermute | solution.py:374
  3.8 5.1 %collective-permute-start.11 = (f32[256,512]{1,0:T(8,128)S(1)}, f32[256,512]{1,0:T(8,128)S(1)}, u32[]{:S(2)}, u32[]{:S(2)}) collective-permute-start(f32[256,512]{1,0:T(8,128)S(1)} %get-tuple-element.50), channel_id=1, source_target_pairs={{0,4},{4,0},{8,12},{12,8},{16,20},{20,16},{24,28},{28,24},{1,5},{5... | collective-permute-start | bytes 1572872 | tf_op jit(solution)/shard_map/core_corner/ppermute | solution.py:374
  3.8 5.7 %collective-permute-start.1 = (f32[256,512]{1,0:T(8,128)S(1)}, f32[256,512]{1,0:T(8,128)S(1)}, u32[]{:S(2)}, u32[]{:S(2)}) collective-permute-start(f32[256,512]{1,0:T(8,128)S(1)} %get-tuple-element.38), channel_id=1, source_target_pairs={{0,4},{4,0},{8,12},{12,8},{16,20},{20,16},{24,28},{28,24},{1,5},{5... | collective-permute-start | bytes 1572872 | tf_op jit(solution)/shard_map/core_straight/ppermute | solution.py:374
  5.0 6.2 %collective-permute-start.3 = (f32[256,512]{1,0:T(8,128)S(1)}, f32[256,512]{1,0:T(8,128)S(1)}, u32[]{:S(2)}, u32[]{:S(2)}) collective-permute-start(f32[256,512]{1,0:T(8,128)S(1)} %get-tuple-element.44), channel_id=1, source_target_pairs={{0,4},{4,0},{8,12},{12,8},{16,20},{20,16},{24,28},{28,24},{1,5},{5... | collective-permute-start | bytes 1572872 | tf_op jit(solution)/shard_map/core_side/ppermute | solution.py:374
  5.1 6.7 %collective-permute-start.8 = (f32[256,512]{1,0:T(8,128)S(1)}, f32[256,512]{1,0:T(8,128)S(1)}, u32[]{:S(2)}, u32[]{:S(2)}) collective-permute-start(f32[256,512]{1,0:T(8,128)S(1)} %get-tuple-element.48), channel_id=1, source_target_pairs={{0,4},{4,0},{8,12},{12,8},{16,20},{20,16},{24,28},{28,24},{1,5},{5... | collective-permute-start | bytes 1572872 | tf_op jit(solution)/shard_map/core_straight/ppermute | solution.py:374
  6.1 9.8 %collective-permute-start.5 = (f32[256,512]{1,0:T(8,128)S(1)}, f32[256,512]{1,0:T(8,128)S(1)}, u32[]{:S(2)}, u32[]{:S(2)}) collective-permute-start(f32[256,512]{1,0:T(8,128)S(1)} %add.10), channel_id=1, source_target_pairs={{0,8},{4,20},{8,0},{12,28},{16,24},{20,4},{24,16},{28,12},{1,9},{5... | collective-permute-start | bytes 1572872 | tf_op jit(solution)/shard_map/link_corner/ppermute | solution.py:374
  8.8 7.8 %collective-permute-start.10 = (f32[256,512]{1,0:T(8,128)S(1)}, f32[256,512]{1,0:T(8,128)S(1)}, u32[]{:S(2)}, u32[]{:S(2)}) collective-permute-start(f32[256,512]{1,0:T(8,128)S(1)} %get-tuple-element.49), channel_id=1, source_target_pairs={{0,4},{4,0},{8,12},{12,8},{16,20},{20,16},{24,28},{28,24},{1,5},{5... | collective-permute-start | bytes 1572872 | tf_op jit(solution)/shard_map/core_side/ppermute | solution.py:374
  9.6 12.0 %collective-permute-start.12 = (f32[256,512]{1,0:T(8,128)S(1)}, f32[256,512]{1,0:T(8,128)S(1)}, u32[]{:S(2)}, u32[]{:S(2)}) collective-permute-start(f32[256,512]{1,0:T(8,128)S(1)} %add.14), channel_id=1, source_target_pairs={{0,8},{4,20},{8,0},{12,28},{16,24},{20,4},{24,16},{28,12},{1,9},{5... | collective-permute-start | bytes 1572872 | tf_op jit(solution)/shard_map/link_corner/ppermute | solution.py:374
  11.1 13.2 %collective-permute-start = (f32[256,512]{1,0:T(8,128)S(1)}, f32[256,512]{1,0:T(8,128)S(1)}, u32[]{:S(2)}, u32[]{:S(2)}) collective-permute-start(f32[256,512]{1,0:T(8,128)S(1)} %get-tuple-element.37), channel_id=1, source_target_pairs={{0,4},{4,0},{8,12},{12,8},{16,20},{20,16},{24,28},{28,24},{1,5},{5... | collective-permute-start | bytes 1572872 | tf_op jit(solution)/shard_map/core_self/ppermute | solution.py:374
  11.9 18.5 %collective-permute-start.2 = (f32[256,512]{1,0:T(8,128)S(1)}, f32[256,512]{1,0:T(8,128)S(1)}, u32[]{:S(2)}, u32[]{:S(2)}) collective-permute-start(f32[256,512]{1,0:T(8,128)S(1)} %add.8), channel_id=1, source_target_pairs={{0,8},{4,20},{8,0},{12,28},{16,24},{20,4},{24,16},{28,12},{1,9},{5... | collective-permute-start | bytes 1572872 | tf_op jit(solution)/shard_map/link_straight/ppermute | solution.py:374
  16.0 16.4 %collective-permute-start.7 = (f32[256,512]{1,0:T(8,128)S(1)}, f32[256,512]{1,0:T(8,128)S(1)}, u32[]{:S(2)}, u32[]{:S(2)}) collective-permute-start(f32[256,512]{1,0:T(8,128)S(1)} %get-tuple-element.47), channel_id=1, source_target_pairs={{0,4},{4,0},{8,12},{12,8},{16,20},{20,16},{24,28},{28,24},{1,5},{5... | collective-permute-start | bytes 1572872 | tf_op jit(solution)/shard_map/core_self/ppermute | solution.py:374
  16.6 24.9 %collective-permute-start.9 = (f32[256,512]{1,0:T(8,128)S(1)}, f32[256,512]{1,0:T(8,128)S(1)}, u32[]{:S(2)}, u32[]{:S(2)}) collective-permute-start(f32[256,512]{1,0:T(8,128)S(1)} %add.12), channel_id=1, source_target_pairs={{0,8},{4,20},{8,0},{12,28},{16,24},{20,4},{24,16},{28,12},{1,9},{5... | collective-permute-start | bytes 1572872 | tf_op jit(solution)/shard_map/link_straight/ppermute | solution.py:374
  21.6 20.6 %collective-permute-start.6 = (f32[256,512]{1,0:T(8,128)S(1)}, f32[256,512]{1,0:T(8,128)S(1)}, u32[]{:S(2)}, u32[]{:S(2)}) collective-permute-start(f32[256,512]{1,0:T(8,128)S(1)} %add.11), channel_id=1, source_target_pairs={{0,16},{4,12},{8,24},{12,4},{16,0},{20,28},{24,8},{28,20},{1,17},{... | collective-permute-start | bytes 1572872 | tf_op jit(solution)/shard_map/side_side/ppermute | solution.py:374
  24.3 19.5 %collective-permute-start.13 = (f32[256,512]{1,0:T(8,128)S(1)}, f32[256,512]{1,0:T(8,128)S(1)}, u32[]{:S(2)}, u32[]{:S(2)}) collective-permute-start(f32[256,512]{1,0:T(8,128)S(1)} %add.15), channel_id=1, source_target_pairs={{0,16},{4,12},{8,24},{12,4},{16,0},{20,28},{24,8},{28,20},{1,17},{... | collective-permute-start | bytes 1572872 | tf_op jit(solution)/shard_map/side_side/ppermute | solution.py:374
  44.7 1.2 %collective-permute-start.14 = (f32[8,128]{1,0:T(8,128)S(1)}, f32[8,128]{1,0:T(8,128)S(1)}, u32[]{:S(2)}, u32[]{:S(2)}) collective-permute-start(f32[8,128]{1,0:T(8,128)S(1)} %get-tuple-element.53.refs_0_.block_norm_ref), channel_id=1, source_target_pairs={{0,4},{4,0},{8,12},{12,8},{16,20},{20,16},{24,28},{28,24},{1,5},{5... | collective-permute-start | bytes 12296 | tf_op jit(solution)/shard_map/core_norm/ppermute | solution.py:374
  45.9 6.7 %collective-permute-start.15 = (f32[8,128]{1,0:T(8,128)S(1)}, f32[8,128]{1,0:T(8,128)S(1)}, u32[]{:S(2)}, u32[]{:S(2)}) collective-permute-start(f32[8,128]{1,0:T(8,128)S(1)} %sum.2.refs_0_), channel_id=1, source_target_pairs={{0,8},{4,12},{8,0},{12,4},{16,24},{20,28},{24,16},{28,20},{1,9},{5... | collective-permute-start | bytes 12296 | tf_op jit(solution)/shard_map/chip_norm/ppermute | solution.py:374
  47.7 4.9 %collective-permute-start.16 = (f32[8,128]{1,0:T(8,128)S(1)}, f32[8,128]{1,0:T(8,128)S(1)}, u32[]{:S(2)}, u32[]{:S(2)}) collective-permute-start(f32[8,128]{1,0:T(8,128)S(1)} %sum.2.refs_0_), channel_id=1, source_target_pairs={{0,16},{4,20},{8,24},{12,28},{16,0},{20,4},{24,8},{28,12},{1,17},{... | collective-permute-start | bytes 12296 | tf_op jit(solution)/shard_map/chip_norm/ppermute | solution.py:374
  49.2 4.5 %collective-permute-start.17 = (f32[8,128]{1,0:T(8,128)S(1)}, f32[8,128]{1,0:T(8,128)S(1)}, u32[]{:S(2)}, u32[]{:S(2)}) collective-permute-start(f32[8,128]{1,0:T(8,128)S(1)} %sum.2.refs_0_), channel_id=1, source_target_pairs={{0,24},{4,28},{8,16},{12,20},{16,8},{20,12},{24,0},{28,4},{1,25},{... | collective-permute-start | bytes 12296 | tf_op jit(solution)/shard_map/chip_norm/ppermute | solution.py:374
  53.7 6.1 %collective-permute-start.18 = (f32[8,128]{1,0:T(8,128)S(1)}, f32[8,128]{1,0:T(8,128)S(1)}, u32[]{:S(2)}, u32[]{:S(2)}) collective-permute-start(f32[8,128]{1,0:T(8,128)S(1)} %sum.3.refs_10_), channel_id=1, source_target_pairs={{0,1},{1,0},{2,3},{3,2},{4,5},{5,4},{6,7},{7,6},{8,9},{9,8},{10,11... | collective-permute-start | bytes 12296 | tf_op jit(solution)/shard_map/group_norm/ppermute | solution.py:429
  55.3 4.5 %collective-permute-start.19 = (f32[8,128]{1,0:T(8,128)S(1)}, f32[8,128]{1,0:T(8,128)S(1)}, u32[]{:S(2)}, u32[]{:S(2)}) collective-permute-start(f32[8,128]{1,0:T(8,128)S(1)} %sum.3.refs_10_), channel_id=1, source_target_pairs={{0,2},{1,3},{2,0},{3,1},{4,6},{5,7},{6,4},{7,5},{8,10},{9,11},{10,... | collective-permute-start | bytes 12296 | tf_op jit(solution)/shard_map/group_norm/ppermute | solution.py:429
  57.9 5.4 %collective-permute-start.20 = (f32[8,128]{1,0:T(8,128)S(1)}, f32[8,128]{1,0:T(8,128)S(1)}, u32[]{:S(2)}, u32[]{:S(2)}) collective-permute-start(f32[8,128]{1,0:T(8,128)S(1)} %sum.3.refs_10_), channel_id=1, source_target_pairs={{0,3},{1,2},{2,1},{3,0},{4,7},{5,6},{6,5},{7,4},{8,11},{9,10},{10,... | collective-permute-start | bytes 12296 | tf_op jit(solution)/shard_map/group_norm/ppermute | solution.py:429
  69.2 9.3 %collective-permute-start.22 = (f32[512,512]{1,0:T(8,128)S(1)}, f32[512,512]{1,0:T(8,128)S(1)}, u32[]{:S(2)}, u32[]{:S(2)}) collective-permute-start(f32[512,512]{1,0:T(8,128)S(1)} %get-tuple-element.63.refs_0_), channel_id=1, source_target_pairs={{0,4},{4,0},{8,12},{12,8},{16,20},{20,16},{24,28},{28,24},{1,5},{5... | collective-permute-start | bytes 3145736 | tf_op jit(solution)/shard_map/core_own/ppermute | solution.py:374
  69.3 9.2 %collective-permute-start.21 = (f32[256,512]{1,0:T(8,128)S(1)}, f32[256,512]{1,0:T(8,128)S(1)}, u32[]{:S(2)}, u32[]{:S(2)}) collective-permute-start(f32[256,512]{1,0:T(8,128)S(1)} %get-tuple-element.62), channel_id=1, source_target_pairs={{0,8},{4,20},{8,0},{12,28},{16,24},{20,4},{24,16},{28,12},{1,9},{5... | collective-permute-start | bytes 1572872 | tf_op jit(solution)/shard_map/link_own/ppermute | solution.py:374
  70.1 14.0 %collective-permute-start.25 = (f32[256,512]{1,0:T(8,128)S(1)}, f32[256,512]{1,0:T(8,128)S(1)}, u32[]{:S(2)}, u32[]{:S(2)}) collective-permute-start(f32[256,512]{1,0:T(8,128)S(1)} %get-tuple-element.65), channel_id=1, source_target_pairs={{0,8},{4,20},{8,0},{12,28},{16,24},{20,4},{24,16},{28,12},{1,9},{5... | collective-permute-start | bytes 1572872 | tf_op jit(solution)/shard_map/link_own/ppermute | solution.py:374
  78.5 16.8 %collective-permute-start.30 = (f32[512,512]{1,0:T(8,128)S(1)}, f32[512,512]{1,0:T(8,128)S(1)}, u32[]{:S(2)}, u32[]{:S(2)}) collective-permute-start(f32[512,512]{1,0:T(8,128)S(1)} %collective-permute-done.22.refs_1_), channel_id=1, source_target_pairs={{0,8},{4,20},{8,0},{12,28},{16,24},{20,4},{24,16},{28,12},{1,9},{5... | collective-permute-start | bytes 3145736 | tf_op jit(solution)/shard_map/link_sibling/ppermute | solution.py:374
  79.3 4.9 %collective-permute-start.23 = (f32[256,512]{1,0:T(8,128)S(1)}, f32[256,512]{1,0:T(8,128)S(1)}, u32[]{:S(2)}, u32[]{:S(2)}) collective-permute-start(f32[256,512]{1,0:T(8,128)S(1)} %collective-permute-done.21.refs_2_), channel_id=1, source_target_pairs={{0,4},{4,0},{8,12},{12,8},{16,20},{20,16},{24,28},{28,24},{1,5},{5... | collective-permute-start | bytes 1572872 | tf_op jit(solution)/shard_map/core_first/ppermute | solution.py:374
  84.1 11.2 %collective-permute-start.26 = (f32[256,512]{1,0:T(8,128)S(1)}, f32[256,512]{1,0:T(8,128)S(1)}, u32[]{:S(2)}, u32[]{:S(2)}) collective-permute-start(f32[256,512]{1,0:T(8,128)S(1)} %collective-permute-done.25.refs_3_), channel_id=1, source_target_pairs={{0,4},{4,0},{8,12},{12,8},{16,20},{20,16},{24,28},{28,24},{1,5},{5... | collective-permute-start | bytes 1572872 | tf_op jit(solution)/shard_map/core_first/ppermute | solution.py:374
  84.1 16.8 %collective-permute-start.24 = (f32[256,512]{1,0:T(8,128)S(1)}, f32[256,512]{1,0:T(8,128)S(1)}, u32[]{:S(2)}, u32[]{:S(2)}) collective-permute-start(f32[256,512]{1,0:T(8,128)S(1)} %collective-permute-done.23.refs_4_), channel_id=1, source_target_pairs={{0,8},{4,20},{8,0},{12,28},{16,24},{20,4},{24,16},{28,12},{1,9},{5... | collective-permute-start | bytes 1572872 | tf_op jit(solution)/shard_map/link_relayed/ppermute | solution.py:374
  95.4 11.2 %collective-permute-start.31 = (f32[512,512]{1,0:T(8,128)S(1)}, f32[512,512]{1,0:T(8,128)S(1)}, u32[]{:S(2)}, u32[]{:S(2)}) collective-permute-start(f32[512,512]{1,0:T(8,128)S(1)} %collective-permute-done.30.refs_0_), channel_id=1, source_target_pairs={{0,4},{4,0},{8,12},{12,8},{16,20},{20,16},{24,28},{28,24},{1,5},{5... | collective-permute-start | bytes 3145736 | tf_op jit(solution)/shard_map/core_second/ppermute | solution.py:374
  95.4 11.2 %collective-permute-start.28 = (f32[256,512]{1,0:T(8,128)S(1)}, f32[256,512]{1,0:T(8,128)S(1)}, u32[]{:S(2)}, u32[]{:S(2)}) collective-permute-start(f32[256,512]{1,0:T(8,128)S(1)} %collective-permute-done.26.refs_5_), channel_id=1, source_target_pairs={{0,8},{4,20},{8,0},{12,28},{16,24},{20,4},{24,16},{28,12},{1,9},{5... | collective-permute-start | bytes 1572872 | tf_op jit(solution)/shard_map/link_relayed/ppermute | solution.py:374
  101.0 7.5 %collective-permute-start.27 = (f32[256,512]{1,0:T(8,128)S(1)}, f32[256,512]{1,0:T(8,128)S(1)}, u32[]{:S(2)}, u32[]{:S(2)}) collective-permute-start(f32[256,512]{1,0:T(8,128)S(1)} %collective-permute-done.24.refs_2_), channel_id=1, source_target_pairs={{0,4},{4,0},{8,12},{12,8},{16,20},{20,16},{24,28},{28,24},{1,5},{5... | collective-permute-start | bytes 1572872 | tf_op jit(solution)/shard_map/core_relayed/ppermute | solution.py:374
  106.6 1.9 %collective-permute-start.29 = (f32[256,512]{1,0:T(8,128)S(1)}, f32[256,512]{1,0:T(8,128)S(1)}, u32[]{:S(2)}, u32[]{:S(2)}) collective-permute-start(f32[256,512]{1,0:T(8,128)S(1)} %collective-permute-done.28.refs_3_), channel_id=1, source_target_pairs={{0,4},{4,0},{8,12},{12,8},{16,20},{20,16},{24,28},{28,24},{1,5},{5... | collective-permute-start | bytes 1572872 | tf_op jit(solution)/shard_map/core_relayed/ppermute | solution.py:374
  (6 other events, 67.1 us)

commit v13 on v12

--- a/solution.py
+++ b/solution.py
@@ -416,13 +416,13 @@
         block.append(joined)
     block_norm = norm
     norm = sum_call(norm, to_core(norm, "norm"))
-    chip_norms = [over(flipped(mask), norm, "chip_norm") for mask in (2, 4, 6)]
+    chip_norms = [over(flipped(mask), norm, "chip_norm") for mask in (6, 4, 2)]
     grams = gram_call([after(block[0], norm), block[1]])
     sides = [(previous, gram, square) for (previous,), gram, square in zip(sides, grams, squares)]
     sides[0] += tuple(mix_call(*sides[0][:2]))
     norm = sum_call(after(norm, sides[0][4]), *chip_norms)
     norms = [norm]
-    for shift in range(1, group_count):
+    for shift in reversed(range(1, group_count)):
         both_ways = group_count & (group_count - 1) == 0
         pairs = [(i, i ^ shift if both_ways else (i + shift) % group_count) for i in range(group_count)]
         with jax.named_scope("group_norm"):

time: 110 us -> 108 us (0.982)
  waiting for transfers between devices: 57.5 us -> 53.5 us
  starting transfers between devices: 23.4 us -> 25.7 us
    ppermute x29, waiting for transfers between devices: 54.1 us -> 51.3 us  [over(): return lax.ppermute(value, 'dp', pairs)]
    ppermute x29, starting transfers between devices: 19 us -> 21.2 us  [over(): return lax.ppermute(value, 'dp', pairs)]
    ppermute x3, waiting for transfers between devices: 3.46 us -> 2.15 us  [paired_body(): norms.append(lax.ppermute(norm, 'mp', pairs))]
where the time goes in v13:
time: 108 us
  waiting for transfers between devices  53.5 us (50%)
  Pallas kernels  25.9 us (24%)
  starting transfers between devices  25.7 us (24%)
  local copies, waits for them, and re-layouts  2.56 us (2%)
    ppermute x29, waiting for transfers between devices, over(): return lax.ppermute(value, 'dp', pairs)  51.3 us
    ppermute x29, starting transfers between devices, over(): return lax.ppermute(value, 'dp', pairs)  21.2 us
    pallas_call x19, Pallas kernels, local_call(): pl.pallas_call(kernel, in_specs=[pl.BlockSpec(memory_space=pltpu.SMEM)] *...  20.2 us
    pallas_call x3, Pallas kernels, assemble_call(): pl.pallas_call(kernel, in_specs=in_specs, out_specs=pl.BlockSpec(memory_s...  5.72 us
    ppermute x3, starting transfers between devices, paired_body(): norms.append(lax.ppermute(norm, 'mp', pairs))  4.48 us
    unnamed x12, local copies, waits for them, and re-layouts  2.56 us
  transfers between devices with their start and end apart: 32, of which 13 were waited for; matrix products, arithmetic and copies ran while one was open for 0% of the time, Pallas kernels for 16%

profile of v13, /device:TPU:0, one launch (start us, length us, event | category | flops | bytes accessed | tf_op | source)
XLA Modules:
  0.0 107.9 jit_solution(2595628227727349751)
XLA Ops:
  0.0 1.9 %copy-done = bf16[1,512,3072]{2,1,0:T(8,128)(2,1)S(1)} copy-done((bf16[1,512,3072]{2,1,0:T(8,128)(2,1)S(1)}, bf16[1,512,3072]{2,1,0:T(8,128)(2,1)}, u32[]{:S(2)}) %copy-start) | copy-done | bytes 3145752
  6.1 2.7 %collective-permute-start.5 = (f32[256,512]{1,0:T(8,128)S(1)}, f32[256,512]{1,0:T(8,128)S(1)}, u32[]{:S(2)}, u32[]{:S(2)}) collective-permute-start(f32[256,512]{1,0:T(8,128)S(1)} %add.10), channel_id=1, source_target_pairs={{0,8},{4,20},{8,0},{12,28},{16,24},{20,4},{24,16},{28,12},{1,9},{5... | collective-permute-start | bytes 1572872 | tf_op jit(solution)/shard_map/link_corner/ppermute | solution.py:374
  9.6 1.6 %collective-permute-start.12 = (f32[256,512]{1,0:T(8,128)S(1)}, f32[256,512]{1,0:T(8,128)S(1)}, u32[]{:S(2)}, u32[]{:S(2)}) collective-permute-start(f32[256,512]{1,0:T(8,128)S(1)} %add.14), channel_id=1, source_target_pairs={{0,8},{4,20},{8,0},{12,28},{16,24},{20,4},{24,16},{28,12},{1,9},{5... | collective-permute-start | bytes 1572872 | tf_op jit(solution)/shard_map/link_corner/ppermute | solution.py:374
  13.1 2.9 %collective-permute-done.5.refs_1_ = f32[256,512]{1,0:T(8,128)S(1)} collective-permute-done((f32[256,512]{1,0:T(8,128)S(1)}, f32[256,512]{1,0:T(8,128)S(1)}, u32[]{:S(2)}, u32[]{:S(2)}) %collective-permute-start.5) | collective-permute-done | bytes 524320 | tf_op jit(solution)/shard_map/link_corner/ppermute | solution.py:374
  16.6 2.1 %collective-permute-start.9 = (f32[256,512]{1,0:T(8,128)S(1)}, f32[256,512]{1,0:T(8,128)S(1)}, u32[]{:S(2)}, u32[]{:S(2)}) collective-permute-start(f32[256,512]{1,0:T(8,128)S(1)} %add.12), channel_id=1, source_target_pairs={{0,8},{4,20},{8,0},{12,28},{16,24},{20,4},{24,16},{28,12},{1,9},{5... | collective-permute-start | bytes 1572872 | tf_op jit(solution)/shard_map/link_straight/ppermute | solution.py:374
  18.7 2.9 %collective-permute-done.12.refs_1_ = f32[256,512]{1,0:T(8,128)S(1)} collective-permute-done((f32[256,512]{1,0:T(8,128)S(1)}, f32[256,512]{1,0:T(8,128)S(1)}, u32[]{:S(2)}, u32[]{:S(2)}) %collective-permute-start.12) | collective-permute-done | bytes 524320 | tf_op jit(solution)/shard_map/link_corner/ppermute | solution.py:374
  21.6 2.0 %collective-permute-start.6 = (f32[256,512]{1,0:T(8,128)S(1)}, f32[256,512]{1,0:T(8,128)S(1)}, u32[]{:S(2)}, u32[]{:S(2)}) collective-permute-start(f32[256,512]{1,0:T(8,128)S(1)} %add.11), channel_id=1, source_target_pairs={{0,16},{4,12},{8,24},{12,4},{16,0},{20,28},{24,8},{28,20},{1,17},{... | collective-permute-start | bytes 1572872 | tf_op jit(solution)/shard_map/side_side/ppermute | solution.py:374
  24.4 5.9 %collective-permute-done.2.refs_1_ = f32[256,512]{1,0:T(8,128)S(1)} collective-permute-done((f32[256,512]{1,0:T(8,128)S(1)}, f32[256,512]{1,0:T(8,128)S(1)}, u32[]{:S(2)}, u32[]{:S(2)}) %collective-permute-start.2) | collective-permute-done | bytes 524320 | tf_op jit(solution)/shard_map/link_straight/ppermute | solution.py:374
  31.0 1.5 %square.1 = (f32[512,512]{1,0:T(8,128)S(1)}, f32[512,512]{1,0:T(8,128)S(1)}) custom-call(f32[512,512]{1,0:T(8,128)S(1)} %bitcast.30, f32[512,512]{1,0:T(8,128)S(1)} %bitcast.33), custom_call_target="tpu_custom_call" | custom-call | flops 1610612736 | bytes 4194304 | tf_op jit(solution)/shard_map/square/pallas_call | solution.py:128
  32.4 9.1 %collective-permute-done.9.refs_1_ = f32[256,512]{1,0:T(8,128)S(1)} collective-permute-done((f32[256,512]{1,0:T(8,128)S(1)}, f32[256,512]{1,0:T(8,128)S(1)}, u32[]{:S(2)}, u32[]{:S(2)}) %collective-permute-start.9) | collective-permute-done | bytes 524320 | tf_op jit(solution)/shard_map/link_straight/ppermute | solution.py:374
  42.2 0.9 join.2
  43.8 0.9 join.3
  44.8 1.1 collective-permute-done.14.refs_1_
  45.9 2.7 %collective-permute-start.15 = (f32[8,128]{1,0:T(8,128)S(1)}, f32[8,128]{1,0:T(8,128)S(1)}, u32[]{:S(2)}, u32[]{:S(2)}) collective-permute-start(f32[8,128]{1,0:T(8,128)S(1)} %sum.2.refs_0_), channel_id=1, source_target_pairs={{0,24},{4,28},{8,16},{12,20},{16,8},{20,12},{24,0},{28,4},{1,25},{... | collective-permute-start | bytes 12296 | tf_op jit(solution)/shard_map/chip_norm/ppermute | solution.py:374
  49.4 1.5 %gram.1 = (f32[512,512]{1,0:T(8,128)S(1)}, f32[512,512]{1,0:T(8,128)S(1)}) custom-call(f32[256,512]{1,0:T(8,128)S(1)} %get-tuple-element.54.upper_ref, f32[256,512]{1,0:T(8,128)S(1)} %get-tuple-element.52.lower_ref), custom_call_target="tpu_custom_call" | custom-call | flops 1610612736 | bytes 3145728 | tf_op jit(solution)/shard_map/gram/pallas_call | solution.py:128
  50.9 1.7 %mix.2 = (f32[512,512]{1,0:T(8,128)S(1)}, f32[512,512]{1,0:T(8,128)S(1)}) custom-call(f32[512,512]{1,0:T(8,128)S(1)} %bitcast.31, f32[512,512]{1,0:T(8,128)S(1)} %get-tuple-element.55.gram_ref.refs_1_), custom_call_target="tpu_custom_call" | custom-call | flops 1610612736 | bytes 4194304 | tf_op jit(solution)/shard_map/mix/pallas_call | solution.py:128
  52.7 3.8 %collective-permute-start.18 = (f32[8,128]{1,0:T(8,128)S(1)}, f32[8,128]{1,0:T(8,128)S(1)}, u32[]{:S(2)}, u32[]{:S(2)}) collective-permute-start(f32[8,128]{1,0:T(8,128)S(1)} %sum.3.refs_10_), channel_id=1, source_target_pairs={{0,3},{1,2},{2,1},{3,0},{4,7},{5,6},{6,5},{7,4},{8,11},{9,10},{10,... | collective-permute-start | bytes 12296 | tf_op jit(solution)/shard_map/group_norm/ppermute | solution.py:429
  57.2 1.7 %mix.3 = (f32[512,512]{1,0:T(8,128)S(1)}, f32[512,512]{1,0:T(8,128)S(1)}) custom-call(f32[512,512]{1,0:T(8,128)S(1)} %bitcast.34, f32[512,512]{1,0:T(8,128)S(1)} %get-tuple-element.58.gram_ref.refs_6_), custom_call_target="tpu_custom_call" | custom-call | flops 1610612736 | bytes 4194304 | tf_op jit(solution)/shard_map/mix/pallas_call | solution.py:128
  59.0 2.1 %collective-permute-done.19.refs_12_ = f32[8,128]{1,0:T(8,128)S(1)} collective-permute-done((f32[8,128]{1,0:T(8,128)S(1)}, f32[8,128]{1,0:T(8,128)S(1)}, u32[]{:S(2)}, u32[]{:S(2)}) %collective-permute-start.19) | collective-permute-done | bytes 4128 | tf_op jit(solution)/shard_map/group_norm/ppermute | solution.py:429
  61.1 5.9 %update.1 = (f32[512,512]{1,0:T(8,128)S(1)}, f32[256,512]{1,0:T(8,128)S(1)}, f32[256,512]{1,0:T(8,128)S(1)}) custom-call(f32[256,512]{1,0:T(8,128)S(1)} %get-tuple-element.54.upper_ref, f32[256,512]{1,0:T(8,128)S(1)} %get-tuple-element.52.lower_ref, f32[8,128]{1,0:T(8,128)S(1)} %get-tuple-element.53.refs_0_.block_norm_ref, f32[512,512]{1,0:T(8,128)S(1)} %bitcast.32, ...), custom_call_target="tpu_custom_call" | custom-call | flops 4831838208 | bytes 13651968 | tf_op jit(solution)/shard_map/update/pallas_call | solution.py:128
  67.1 1.6 %collective-permute-start.21 = (f32[256,512]{1,0:T(8,128)S(1)}, f32[256,512]{1,0:T(8,128)S(1)}, u32[]{:S(2)}, u32[]{:S(2)}) collective-permute-start(f32[256,512]{1,0:T(8,128)S(1)} %get-tuple-element.62), channel_id=1, source_target_pairs={{0,8},{4,20},{8,0},{12,28},{16,24},{20,4},{24,16},{28,12},{1,9},{5... | collective-permute-start | bytes 1572872 | tf_op jit(solution)/shard_map/link_own/ppermute | solution.py:374
  69.2 7.2 %collective-permute-done.21.refs_2_ = f32[256,512]{1,0:T(8,128)S(1)} collective-permute-done((f32[256,512]{1,0:T(8,128)S(1)}, f32[256,512]{1,0:T(8,128)S(1)}, u32[]{:S(2)}, u32[]{:S(2)}) %collective-permute-start.21) | collective-permute-done | bytes 524320 | tf_op jit(solution)/shard_map/link_own/ppermute | solution.py:374
  76.4 1.5 %collective-permute-start.30 = (f32[512,512]{1,0:T(8,128)S(1)}, f32[512,512]{1,0:T(8,128)S(1)}, u32[]{:S(2)}, u32[]{:S(2)}) collective-permute-start(f32[512,512]{1,0:T(8,128)S(1)} %collective-permute-done.22.refs_1_), channel_id=1, source_target_pairs={{0,8},{4,20},{8,0},{12,28},{16,24},{20,4},{24,16},{28,12},{1,9},{5... | collective-permute-start | bytes 3145736 | tf_op jit(solution)/shard_map/link_sibling/ppermute | solution.py:374
  77.8 4.1 %collective-permute-done.25.refs_3_ = f32[256,512]{1,0:T(8,128)S(1)} collective-permute-done((f32[256,512]{1,0:T(8,128)S(1)}, f32[256,512]{1,0:T(8,128)S(1)}, u32[]{:S(2)}, u32[]{:S(2)}) %collective-permute-start.25) | collective-permute-done | bytes 524320 | tf_op jit(solution)/shard_map/link_own/ppermute | solution.py:374
  82.0 1.5 %collective-permute-start.24 = (f32[256,512]{1,0:T(8,128)S(1)}, f32[256,512]{1,0:T(8,128)S(1)}, u32[]{:S(2)}, u32[]{:S(2)}) collective-permute-start(f32[256,512]{1,0:T(8,128)S(1)} %collective-permute-done.23.refs_4_), channel_id=1, source_target_pairs={{0,8},{4,20},{8,0},{12,28},{16,24},{20,4},{24,16},{28,12},{1,9},{5... | collective-permute-start | bytes 1572872 | tf_op jit(solution)/shard_map/link_relayed/ppermute | solution.py:374
  83.5 9.7 %collective-permute-done.30.refs_0_ = f32[512,512]{1,0:T(8,128)S(1)} collective-permute-done((f32[512,512]{1,0:T(8,128)S(1)}, f32[512,512]{1,0:T(8,128)S(1)}, u32[]{:S(2)}, u32[]{:S(2)}) %collective-permute-start.30) | collective-permute-done | bytes 1048608 | tf_op jit(solution)/shard_map/link_sibling/ppermute | solution.py:374
  93.2 1.5 %collective-permute-start.28 = (f32[256,512]{1,0:T(8,128)S(1)}, f32[256,512]{1,0:T(8,128)S(1)}, u32[]{:S(2)}, u32[]{:S(2)}) collective-permute-start(f32[256,512]{1,0:T(8,128)S(1)} %collective-permute-done.26.refs_5_), channel_id=1, source_target_pairs={{0,8},{4,20},{8,0},{12,28},{16,24},{20,4},{24,16},{28,12},{1,9},{5... | collective-permute-start | bytes 1572872 | tf_op jit(solution)/shard_map/link_relayed/ppermute | solution.py:374
  94.7 2.3 %assemble.3.refs_4_ = f32[512,3072]{1,0:T(8,128)} custom-call(s32[6]{0:T(128)S(1)} %bitcast.27, s32[1]{0:T(128)} %bitcast.1.me_ref, f32[512,512]{1,0:T(8,128)S(1)} %get-tuple-element.63.refs_0_, f32[512,512]{1,0:T(8,128)S(1)} %collective-permute-done.22.refs_1_, f32[256,512]{1,0:T(8,128)S(1)} %collective-permute-done.21.refs_2_, ...), custom_call_target="tpu_custom_call" | custom-call | bytes 12582912 | tf_op jit(solution)/shard_map/assemble/pallas_call | solution.py:345
  97.0 1.9 %collective-permute-done.24.refs_2_ = f32[256,512]{1,0:T(8,128)S(1)} collective-permute-done((f32[256,512]{1,0:T(8,128)S(1)}, f32[256,512]{1,0:T(8,128)S(1)}, u32[]{:S(2)}, u32[]{:S(2)}) %collective-permute-start.24) | collective-permute-done | bytes 524320 | tf_op jit(solution)/shard_map/link_relayed/ppermute | solution.py:374
  98.8 5.6 %collective-permute-done.28.refs_3_ = f32[256,512]{1,0:T(8,128)S(1)} collective-permute-done((f32[256,512]{1,0:T(8,128)S(1)}, f32[256,512]{1,0:T(8,128)S(1)}, u32[]{:S(2)}, u32[]{:S(2)}) %collective-permute-start.28) | collective-permute-done | bytes 524320 | tf_op jit(solution)/shard_map/link_relayed/ppermute | solution.py:374
  104.4 1.9 %assemble.4.refs_2_ = f32[512,3072]{1,0:T(8,128)} custom-call(s32[6]{0:T(128)S(1)} %bitcast.28, s32[1]{0:T(128)} %bitcast.1.me_ref, f32[512,512]{1,0:T(8,128)S(1)} %collective-permute-done.30.refs_0_, f32[512,512]{1,0:T(8,128)S(1)} %collective-permute-done.31.refs_1_, ...), custom_call_target="tpu_custom_call", output_to_operand_aliasing={{}: (6, {})} | custom-call | bytes 8388608 | tf_op jit(solution)/shard_map/assemble/pallas_call | solution.py:345
  106.4 1.5 %assemble.5 = f32[512,3072]{1,0:T(8,128)} custom-call(s32[6]{0:T(128)S(1)} %bitcast.29, s32[1]{0:T(128)} %bitcast.1.me_ref, f32[256,512]{1,0:T(8,128)S(1)} %collective-permute-done.27.refs_0_, f32[256,512]{1,0:T(8,128)S(1)} %collective-permute-done.29.refs_1_, f32[512,3072]{1,0:T(8,128)} %assemble.4.refs_2_), custom_call_target="tpu_custom_call", output_to_operand_aliasing={{}: (4, {})} | custom-call | bytes 2097152 | tf_op jit(solution)/shard_map/assemble/pallas_call | solution.py:345
  (66 shorter events, 12.6 us)
Async XLA Ops:
  3.2 2.3 %collective-permute-start.4 = (f32[256,512]{1,0:T(8,128)S(1)}, f32[256,512]{1,0:T(8,128)S(1)}, u32[]{:S(2)}, u32[]{:S(2)}) collective-permute-start(f32[256,512]{1,0:T(8,128)S(1)} %get-tuple-element.45), channel_id=1, source_target_pairs={{0,4},{4,0},{8,12},{12,8},{16,20},{20,16},{24,28},{28,24},{1,5},{5... | collective-permute-start | bytes 1572872 | tf_op jit(solution)/shard_map/core_corner/ppermute | solution.py:374
  3.8 5.1 %collective-permute-start.11 = (f32[256,512]{1,0:T(8,128)S(1)}, f32[256,512]{1,0:T(8,128)S(1)}, u32[]{:S(2)}, u32[]{:S(2)}) collective-permute-start(f32[256,512]{1,0:T(8,128)S(1)} %get-tuple-element.50), channel_id=1, source_target_pairs={{0,4},{4,0},{8,12},{12,8},{16,20},{20,16},{24,28},{28,24},{1,5},{5... | collective-permute-start | bytes 1572872 | tf_op jit(solution)/shard_map/core_corner/ppermute | solution.py:374
  3.8 5.7 %collective-permute-start.1 = (f32[256,512]{1,0:T(8,128)S(1)}, f32[256,512]{1,0:T(8,128)S(1)}, u32[]{:S(2)}, u32[]{:S(2)}) collective-permute-start(f32[256,512]{1,0:T(8,128)S(1)} %get-tuple-element.38), channel_id=1, source_target_pairs={{0,4},{4,0},{8,12},{12,8},{16,20},{20,16},{24,28},{28,24},{1,5},{5... | collective-permute-start | bytes 1572872 | tf_op jit(solution)/shard_map/core_straight/ppermute | solution.py:374
  5.0 6.2 %collective-permute-start.3 = (f32[256,512]{1,0:T(8,128)S(1)}, f32[256,512]{1,0:T(8,128)S(1)}, u32[]{:S(2)}, u32[]{:S(2)}) collective-permute-start(f32[256,512]{1,0:T(8,128)S(1)} %get-tuple-element.44), channel_id=1, source_target_pairs={{0,4},{4,0},{8,12},{12,8},{16,20},{20,16},{24,28},{28,24},{1,5},{5... | collective-permute-start | bytes 1572872 | tf_op jit(solution)/shard_map/core_side/ppermute | solution.py:374
  5.1 6.7 %collective-permute-start.8 = (f32[256,512]{1,0:T(8,128)S(1)}, f32[256,512]{1,0:T(8,128)S(1)}, u32[]{:S(2)}, u32[]{:S(2)}) collective-permute-start(f32[256,512]{1,0:T(8,128)S(1)} %get-tuple-element.48), channel_id=1, source_target_pairs={{0,4},{4,0},{8,12},{12,8},{16,20},{20,16},{24,28},{28,24},{1,5},{5... | collective-permute-start | bytes 1572872 | tf_op jit(solution)/shard_map/core_straight/ppermute | solution.py:374
  6.1 9.8 %collective-permute-start.5 = (f32[256,512]{1,0:T(8,128)S(1)}, f32[256,512]{1,0:T(8,128)S(1)}, u32[]{:S(2)}, u32[]{:S(2)}) collective-permute-start(f32[256,512]{1,0:T(8,128)S(1)} %add.10), channel_id=1, source_target_pairs={{0,8},{4,20},{8,0},{12,28},{16,24},{20,4},{24,16},{28,12},{1,9},{5... | collective-permute-start | bytes 1572872 | tf_op jit(solution)/shard_map/link_corner/ppermute | solution.py:374
  8.8 7.8 %collective-permute-start.10 = (f32[256,512]{1,0:T(8,128)S(1)}, f32[256,512]{1,0:T(8,128)S(1)}, u32[]{:S(2)}, u32[]{:S(2)}) collective-permute-start(f32[256,512]{1,0:T(8,128)S(1)} %get-tuple-element.49), channel_id=1, source_target_pairs={{0,4},{4,0},{8,12},{12,8},{16,20},{20,16},{24,28},{28,24},{1,5},{5... | collective-permute-start | bytes 1572872 | tf_op jit(solution)/shard_map/core_side/ppermute | solution.py:374
  9.6 12.0 %collective-permute-start.12 = (f32[256,512]{1,0:T(8,128)S(1)}, f32[256,512]{1,0:T(8,128)S(1)}, u32[]{:S(2)}, u32[]{:S(2)}) collective-permute-start(f32[256,512]{1,0:T(8,128)S(1)} %add.14), channel_id=1, source_target_pairs={{0,8},{4,20},{8,0},{12,28},{16,24},{20,4},{24,16},{28,12},{1,9},{5... | collective-permute-start | bytes 1572872 | tf_op jit(solution)/shard_map/link_corner/ppermute | solution.py:374
  11.1 13.2 %collective-permute-start = (f32[256,512]{1,0:T(8,128)S(1)}, f32[256,512]{1,0:T(8,128)S(1)}, u32[]{:S(2)}, u32[]{:S(2)}) collective-permute-start(f32[256,512]{1,0:T(8,128)S(1)} %get-tuple-element.37), channel_id=1, source_target_pairs={{0,4},{4,0},{8,12},{12,8},{16,20},{20,16},{24,28},{28,24},{1,5},{5... | collective-permute-start | bytes 1572872 | tf_op jit(solution)/shard_map/core_self/ppermute | solution.py:374
  11.9 18.5 %collective-permute-start.2 = (f32[256,512]{1,0:T(8,128)S(1)}, f32[256,512]{1,0:T(8,128)S(1)}, u32[]{:S(2)}, u32[]{:S(2)}) collective-permute-start(f32[256,512]{1,0:T(8,128)S(1)} %add.8), channel_id=1, source_target_pairs={{0,8},{4,20},{8,0},{12,28},{16,24},{20,4},{24,16},{28,12},{1,9},{5... | collective-permute-start | bytes 1572872 | tf_op jit(solution)/shard_map/link_straight/ppermute | solution.py:374
  16.0 16.4 %collective-permute-start.7 = (f32[256,512]{1,0:T(8,128)S(1)}, f32[256,512]{1,0:T(8,128)S(1)}, u32[]{:S(2)}, u32[]{:S(2)}) collective-permute-start(f32[256,512]{1,0:T(8,128)S(1)} %get-tuple-element.47), channel_id=1, source_target_pairs={{0,4},{4,0},{8,12},{12,8},{16,20},{20,16},{24,28},{28,24},{1,5},{5... | collective-permute-start | bytes 1572872 | tf_op jit(solution)/shard_map/core_self/ppermute | solution.py:374
  16.6 24.9 %collective-permute-start.9 = (f32[256,512]{1,0:T(8,128)S(1)}, f32[256,512]{1,0:T(8,128)S(1)}, u32[]{:S(2)}, u32[]{:S(2)}) collective-permute-start(f32[256,512]{1,0:T(8,128)S(1)} %add.12), channel_id=1, source_target_pairs={{0,8},{4,20},{8,0},{12,28},{16,24},{20,4},{24,16},{28,12},{1,9},{5... | collective-permute-start | bytes 1572872 | tf_op jit(solution)/shard_map/link_straight/ppermute | solution.py:374
  21.6 20.6 %collective-permute-start.6 = (f32[256,512]{1,0:T(8,128)S(1)}, f32[256,512]{1,0:T(8,128)S(1)}, u32[]{:S(2)}, u32[]{:S(2)}) collective-permute-start(f32[256,512]{1,0:T(8,128)S(1)} %add.11), channel_id=1, source_target_pairs={{0,16},{4,12},{8,24},{12,4},{16,0},{20,28},{24,8},{28,20},{1,17},{... | collective-permute-start | bytes 1572872 | tf_op jit(solution)/shard_map/side_side/ppermute | solution.py:374
  24.3 19.5 %collective-permute-start.13 = (f32[256,512]{1,0:T(8,128)S(1)}, f32[256,512]{1,0:T(8,128)S(1)}, u32[]{:S(2)}, u32[]{:S(2)}) collective-permute-start(f32[256,512]{1,0:T(8,128)S(1)} %add.15), channel_id=1, source_target_pairs={{0,16},{4,12},{8,24},{12,4},{16,0},{20,28},{24,8},{28,20},{1,17},{... | collective-permute-start | bytes 1572872 | tf_op jit(solution)/shard_map/side_side/ppermute | solution.py:374
  44.7 1.2 %collective-permute-start.14 = (f32[8,128]{1,0:T(8,128)S(1)}, f32[8,128]{1,0:T(8,128)S(1)}, u32[]{:S(2)}, u32[]{:S(2)}) collective-permute-start(f32[8,128]{1,0:T(8,128)S(1)} %get-tuple-element.53.refs_0_.block_norm_ref), channel_id=1, source_target_pairs={{0,4},{4,0},{8,12},{12,8},{16,20},{20,16},{24,28},{28,24},{1,5},{5... | collective-permute-start | bytes 12296 | tf_op jit(solution)/shard_map/core_norm/ppermute | solution.py:374
  45.9 6.7 %collective-permute-start.15 = (f32[8,128]{1,0:T(8,128)S(1)}, f32[8,128]{1,0:T(8,128)S(1)}, u32[]{:S(2)}, u32[]{:S(2)}) collective-permute-start(f32[8,128]{1,0:T(8,128)S(1)} %sum.2.refs_0_), channel_id=1, source_target_pairs={{0,24},{4,28},{8,16},{12,20},{16,8},{20,12},{24,0},{28,4},{1,25},{... | collective-permute-start | bytes 12296 | tf_op jit(solution)/shard_map/chip_norm/ppermute | solution.py:374
  48.6 4.0 %collective-permute-start.16 = (f32[8,128]{1,0:T(8,128)S(1)}, f32[8,128]{1,0:T(8,128)S(1)}, u32[]{:S(2)}, u32[]{:S(2)}) collective-permute-start(f32[8,128]{1,0:T(8,128)S(1)} %sum.2.refs_0_), channel_id=1, source_target_pairs={{0,16},{4,20},{8,24},{12,28},{16,0},{20,4},{24,8},{28,12},{1,17},{... | collective-permute-start | bytes 12296 | tf_op jit(solution)/shard_map/chip_norm/ppermute | solution.py:374
  49.1 3.6 %collective-permute-start.17 = (f32[8,128]{1,0:T(8,128)S(1)}, f32[8,128]{1,0:T(8,128)S(1)}, u32[]{:S(2)}, u32[]{:S(2)}) collective-permute-start(f32[8,128]{1,0:T(8,128)S(1)} %sum.2.refs_0_), channel_id=1, source_target_pairs={{0,8},{4,12},{8,0},{12,4},{16,24},{20,28},{24,16},{28,20},{1,9},{5... | collective-permute-start | bytes 12296 | tf_op jit(solution)/shard_map/chip_norm/ppermute | solution.py:374
  52.7 6.2 %collective-permute-start.18 = (f32[8,128]{1,0:T(8,128)S(1)}, f32[8,128]{1,0:T(8,128)S(1)}, u32[]{:S(2)}, u32[]{:S(2)}) collective-permute-start(f32[8,128]{1,0:T(8,128)S(1)} %sum.3.refs_10_), channel_id=1, source_target_pairs={{0,3},{1,2},{2,1},{3,0},{4,7},{5,6},{6,5},{7,4},{8,11},{9,10},{10,... | collective-permute-start | bytes 12296 | tf_op jit(solution)/shard_map/group_norm/ppermute | solution.py:429
  56.6 4.5 %collective-permute-start.19 = (f32[8,128]{1,0:T(8,128)S(1)}, f32[8,128]{1,0:T(8,128)S(1)}, u32[]{:S(2)}, u32[]{:S(2)}) collective-permute-start(f32[8,128]{1,0:T(8,128)S(1)} %sum.3.refs_10_), channel_id=1, source_target_pairs={{0,2},{1,3},{2,0},{3,1},{4,6},{5,7},{6,4},{7,5},{8,10},{9,11},{10,... | collective-permute-start | bytes 12296 | tf_op jit(solution)/shard_map/group_norm/ppermute | solution.py:429
  56.6 4.5 %collective-permute-start.20 = (f32[8,128]{1,0:T(8,128)S(1)}, f32[8,128]{1,0:T(8,128)S(1)}, u32[]{:S(2)}, u32[]{:S(2)}) collective-permute-start(f32[8,128]{1,0:T(8,128)S(1)} %sum.3.refs_10_), channel_id=1, source_target_pairs={{0,1},{1,0},{2,3},{3,2},{4,5},{5,4},{6,7},{7,6},{8,9},{9,8},{10,11... | collective-permute-start | bytes 12296 | tf_op jit(solution)/shard_map/group_norm/ppermute | solution.py:429
  67.0 9.3 %collective-permute-start.22 = (f32[512,512]{1,0:T(8,128)S(1)}, f32[512,512]{1,0:T(8,128)S(1)}, u32[]{:S(2)}, u32[]{:S(2)}) collective-permute-start(f32[512,512]{1,0:T(8,128)S(1)} %get-tuple-element.63.refs_0_), channel_id=1, source_target_pairs={{0,4},{4,0},{8,12},{12,8},{16,20},{20,16},{24,28},{28,24},{1,5},{5... | collective-permute-start | bytes 3145736 | tf_op jit(solution)/shard_map/core_own/ppermute | solution.py:374
  67.1 9.2 %collective-permute-start.21 = (f32[256,512]{1,0:T(8,128)S(1)}, f32[256,512]{1,0:T(8,128)S(1)}, u32[]{:S(2)}, u32[]{:S(2)}) collective-permute-start(f32[256,512]{1,0:T(8,128)S(1)} %get-tuple-element.62), channel_id=1, source_target_pairs={{0,8},{4,20},{8,0},{12,28},{16,24},{20,4},{24,16},{28,12},{1,9},{5... | collective-permute-start | bytes 1572872 | tf_op jit(solution)/shard_map/link_own/ppermute | solution.py:374
  68.7 13.3 %collective-permute-start.25 = (f32[256,512]{1,0:T(8,128)S(1)}, f32[256,512]{1,0:T(8,128)S(1)}, u32[]{:S(2)}, u32[]{:S(2)}) collective-permute-start(f32[256,512]{1,0:T(8,128)S(1)} %get-tuple-element.65), channel_id=1, source_target_pairs={{0,8},{4,20},{8,0},{12,28},{16,24},{20,4},{24,16},{28,12},{1,9},{5... | collective-permute-start | bytes 1572872 | tf_op jit(solution)/shard_map/link_own/ppermute | solution.py:374
  76.4 16.8 %collective-permute-start.30 = (f32[512,512]{1,0:T(8,128)S(1)}, f32[512,512]{1,0:T(8,128)S(1)}, u32[]{:S(2)}, u32[]{:S(2)}) collective-permute-start(f32[512,512]{1,0:T(8,128)S(1)} %collective-permute-done.22.refs_1_), channel_id=1, source_target_pairs={{0,8},{4,20},{8,0},{12,28},{16,24},{20,4},{24,16},{28,12},{1,9},{5... | collective-permute-start | bytes 3145736 | tf_op jit(solution)/shard_map/link_sibling/ppermute | solution.py:374
  77.8 4.1 %collective-permute-start.23 = (f32[256,512]{1,0:T(8,128)S(1)}, f32[256,512]{1,0:T(8,128)S(1)}, u32[]{:S(2)}, u32[]{:S(2)}) collective-permute-start(f32[256,512]{1,0:T(8,128)S(1)} %collective-permute-done.21.refs_2_), channel_id=1, source_target_pairs={{0,4},{4,0},{8,12},{12,8},{16,20},{20,16},{24,28},{28,24},{1,5},{5... | collective-permute-start | bytes 1572872 | tf_op jit(solution)/shard_map/core_first/ppermute | solution.py:374
  82.0 11.2 %collective-permute-start.26 = (f32[256,512]{1,0:T(8,128)S(1)}, f32[256,512]{1,0:T(8,128)S(1)}, u32[]{:S(2)}, u32[]{:S(2)}) collective-permute-start(f32[256,512]{1,0:T(8,128)S(1)} %collective-permute-done.25.refs_3_), channel_id=1, source_target_pairs={{0,4},{4,0},{8,12},{12,8},{16,20},{20,16},{24,28},{28,24},{1,5},{5... | collective-permute-start | bytes 1572872 | tf_op jit(solution)/shard_map/core_first/ppermute | solution.py:374
  82.0 16.8 %collective-permute-start.24 = (f32[256,512]{1,0:T(8,128)S(1)}, f32[256,512]{1,0:T(8,128)S(1)}, u32[]{:S(2)}, u32[]{:S(2)}) collective-permute-start(f32[256,512]{1,0:T(8,128)S(1)} %collective-permute-done.23.refs_4_), channel_id=1, source_target_pairs={{0,8},{4,20},{8,0},{12,28},{16,24},{20,4},{24,16},{28,12},{1,9},{5... | collective-permute-start | bytes 1572872 | tf_op jit(solution)/shard_map/link_relayed/ppermute | solution.py:374
  93.2 11.2 %collective-permute-start.31 = (f32[512,512]{1,0:T(8,128)S(1)}, f32[512,512]{1,0:T(8,128)S(1)}, u32[]{:S(2)}, u32[]{:S(2)}) collective-permute-start(f32[512,512]{1,0:T(8,128)S(1)} %collective-permute-done.30.refs_0_), channel_id=1, source_target_pairs={{0,4},{4,0},{8,12},{12,8},{16,20},{20,16},{24,28},{28,24},{1,5},{5... | collective-permute-start | bytes 3145736 | tf_op jit(solution)/shard_map/core_second/ppermute | solution.py:374
  93.2 11.2 %collective-permute-start.28 = (f32[256,512]{1,0:T(8,128)S(1)}, f32[256,512]{1,0:T(8,128)S(1)}, u32[]{:S(2)}, u32[]{:S(2)}) collective-permute-start(f32[256,512]{1,0:T(8,128)S(1)} %collective-permute-done.26.refs_5_), channel_id=1, source_target_pairs={{0,8},{4,20},{8,0},{12,28},{16,24},{20,4},{24,16},{28,12},{1,9},{5... | collective-permute-start | bytes 1572872 | tf_op jit(solution)/shard_map/link_relayed/ppermute | solution.py:374
  98.8 7.5 %collective-permute-start.27 = (f32[256,512]{1,0:T(8,128)S(1)}, f32[256,512]{1,0:T(8,128)S(1)}, u32[]{:S(2)}, u32[]{:S(2)}) collective-permute-start(f32[256,512]{1,0:T(8,128)S(1)} %collective-permute-done.24.refs_2_), channel_id=1, source_target_pairs={{0,4},{4,0},{8,12},{12,8},{16,20},{20,16},{24,28},{28,24},{1,5},{5... | collective-permute-start | bytes 1572872 | tf_op jit(solution)/shard_map/core_relayed/ppermute | solution.py:374
  104.4 1.9 %collective-permute-start.29 = (f32[256,512]{1,0:T(8,128)S(1)}, f32[256,512]{1,0:T(8,128)S(1)}, u32[]{:S(2)}, u32[]{:S(2)}) collective-permute-start(f32[256,512]{1,0:T(8,128)S(1)} %collective-permute-done.28.refs_3_), channel_id=1, source_target_pairs={{0,4},{4,0},{8,12},{12,8},{16,20},{20,16},{24,28},{28,24},{1,5},{5... | collective-permute-start | bytes 1572872 | tf_op jit(solution)/shard_map/core_relayed/ppermute | solution.py:374
  (6 other events, 67.1 us)

commit v14 on v13

--- a/solution.py
+++ b/solution.py
@@ -65,6 +65,7 @@
 
 
 SMALL = 2 << 20
+CHUNK = 32
 LARGE = 20 << 20
 F32 = jnp.float32
 HALVES = (0, 1)
@@ -137,12 +138,17 @@
     )(*scalars, *operands)
 
 
-def owner_block(owners_ref, grad_ref, rows, width, target):
+def owner_columns(owners_ref, grad_ref, width, target):
     column = 0
     for index in range(1, grad_ref.shape[1] // width):
         column = column + jnp.where(owners_ref[index] == target, index * width, 0)
-    columns = pl.ds(pl.multiple_of(column, width), width)
-    return grad_ref[rows, columns].astype(F32)
+    return pl.ds(pl.multiple_of(column, width), width)
+
+
+def row_chunks(half, width):
+    first = 0 if half is None else half * (width // 2)
+    count = width if half is None else width // 2
+    return [(pl.ds(first + row, CHUNK), pl.ds(row, CHUNK)) for row in range(0, count, CHUNK)]
 
 
 def rows_of(half, width):
@@ -151,60 +157,49 @@
 
 def piece_shape(half, width):
     return jax.ShapeDtypeStruct((width if half is None else width // 2, width), F32)
-
-
-def piece_of(ref, half, width):
-    return ref[rows_of(half, width), :] if ref.shape[0] == width else ref[...]
 
 
 def pack_call(owners, me, grads, pieces, width):
     def kernel(owners_ref, me_ref, grad_ref, *out_refs):
         for (kind, half), out_ref in zip(pieces, out_refs):
-            target = piece_target(kind, me_ref[0] ^ 1)
-            out_ref[...] = owner_block(owners_ref, grad_ref, rows_of(half, width), width, target)
+            columns = owner_columns(owners_ref, grad_ref, width, piece_target(kind, me_ref[0] ^ 1))
+            for block_rows, piece_rows in row_chunks(half, width):
+                out_ref[piece_rows, :] = grad_ref[block_rows, columns].astype(F32)
 
     shapes = [piece_shape(half, width) for _, half in pieces]
     return local_call(kernel, "pack", shapes, (grads,), (owners, me))
 
 
 def add_call(owners, me, grads, kind, half, arrivals, width):
-    flat = [value for arrival in arrivals for value in (arrival if isinstance(arrival, list) else [arrival])]
-
     def kernel(owners_ref, me_ref, grad_ref, *refs):
-        target = piece_target(kind, me_ref[0])
-        for part in HALVES if half is None else (half,):
-            total = owner_block(owners_ref, grad_ref, rows_of(part, width), width, target)
-            place = 0
-            for arrival in arrivals:
-                if isinstance(arrival, list):
-                    total = total + refs[place + part][...]
-                    place += 2
-                else:
-                    total = total + piece_of(refs[place], part, width)
-                    place += 1
-            if half is None:
-                refs[-1][rows_of(part, width), :] = total
-            else:
-                refs[-1][...] = total
-
-    return local_call(kernel, "add", piece_shape(half, width), (grads, *flat), (owners, me))
-
-
-def join_call(owners, me, total, half, arrival, norm, block_count):
-    width = total.shape[1]
+        columns = owner_columns(owners_ref, grad_ref, width, piece_target(kind, me_ref[0]))
+        for block_rows, piece_rows in row_chunks(half, width):
+            total = grad_ref[block_rows, columns].astype(F32)
+            for ref in refs[:-1]:
+                total = total + ref[piece_rows, :]
+            refs[-1][piece_rows, :] = total
+
+    return local_call(kernel, "add", piece_shape(half, width), (grads, *arrivals), (owners, me))
+
+
+def join_call(owners, me, total, arrival, norm, block_count):
+    rows, width = total.shape
 
     def kernel(owners_ref, me_ref, total_ref, arrival_ref, *refs):
         block_ref, norm_ref = refs[-2:]
-        block = piece_of(total_ref, half, width) + arrival_ref[...]
-        block_ref[...] = block
+        squares = jnp.zeros((8, width), F32)
+        for row in range(0, rows, CHUNK):
+            block = total_ref[row : row + CHUNK, :] + arrival_ref[row : row + CHUNK, :]
+            block_ref[row : row + CHUNK, :] = block
+            squares = squares + jnp.sum((block * block).reshape(CHUNK // 8, 8, width), axis=0)
         owned = 0
         for index in range(block_count):
             owned = owned + jnp.where(owners_ref[index] == me_ref[0], 1, 0)
-        squares = jnp.sum(block * block, keepdims=True).reshape(1, 1) * owned.astype(F32)
+        squares = jnp.sum(squares, keepdims=True).reshape(1, 1) * owned.astype(F32)
         total_squares = jnp.broadcast_to(squares, norm_ref.shape)
         norm_ref[...] = total_squares if norm is None else total_squares + refs[0][...]
 
-    shapes = [piece_shape(half, width), jax.ShapeDtypeStruct((8, 128), F32)]
+    shapes = [jax.ShapeDtypeStruct((rows, width), F32), jax.ShapeDtypeStruct((8, 128), F32)]
     operands = (total, arrival) if norm is None else (total, arrival, norm)
     return local_call(kernel, "join", shapes, operands, (owners, me))
 
@@ -245,16 +240,14 @@
     return local_call(gram_kernel, "gram", [shape, shape], block, flops=12 * width**3, vmem=LARGE)
 
 
-def square_kernel(*refs):
-    for ref, out_ref in zip(refs[: len(refs) // 2], refs[len(refs) // 2 :]):
-        value = ref[...]
-        out_ref[...] = symmetric_dot(left_operand(value), right_operand(value))
-
-
-def square_call(*statistics):
-    shapes = [jax.ShapeDtypeStruct(value.shape, F32) for value in statistics]
-    flops = 6 * len(statistics) * statistics[0].shape[0] ** 3
-    return local_call(square_kernel, "square", shapes, statistics, flops=flops, vmem=LARGE)
+def square_kernel(value_ref, out_ref):
+    value = value_ref[...]
+    out_ref[...] = symmetric_dot(left_operand(value), right_operand(value))
+
+
+def square_call(value):
+    shape = jax.ShapeDtypeStruct(value.shape, F32)
+    return local_call(square_kernel, "square", shape, (value,), flops=6 * value.shape[0] ** 3, vmem=LARGE)
 
 
 def mix_kernel(previous_ref, gram_ref, mixed_ref, square_ref):
@@ -271,21 +264,23 @@
     return local_call(mix_kernel, "mix", [shape, shape], (previous, gram), flops=flops, vmem=LARGE)
 
 
-def roots_of(sides, gram_scale):
-    statistics = [0.5 * previous[...] + gram[...] * gram_scale for previous, gram, _, _, _ in sides]
+def roots_of(left, right, gram_scale):
+    statistics = [0.5 * side[0][...] + side[1][...] * gram_scale for side in (left, right)]
     norms = [jnp.sum(value * value, keepdims=True).reshape(1, 1) for value in statistics]
-    factor_square, factor_scaled, kept = [], [], []
-    for statistic, norm, (_, _, previous_square, mixed, gram_square) in zip(statistics, norms, sides):
-        inverse = 1.0 / norm
-        scaled = statistic * jnp.sqrt(inverse)
-        square = previous_square[...] * (0.25 * inverse) + mixed[...] * (0.5 * gram_scale * inverse)
-        square = square + gram_square[...] * (gram_scale * gram_scale * inverse)
-        factor_square.append(add_identity(0.0625 * square - 0.625 * scaled, 1.5625))
-        factor_scaled.append(1.25 * scaled - 0.25 * square)
-        kept.append(scaled)
-    fourth = [symmetric_dot(left_operand(value), right_operand(value)) for value in factor_square]
-    tail = [symmetric_dot(left_operand(f), right_operand(m)) for f, m in zip(fourth, factor_scaled)]
-    roots = [add_identity(-1.25 * m - t, 6.25) for m, t in zip(kept, tail)]
+    inverses = [1.0 / norm for norm in norms]
+    scaled = [value * jnp.sqrt(inverse) for value, inverse in zip(statistics, inverses)]
+    left_square = symmetric_dot(left_operand(scaled[0]), right_operand(scaled[0]))
+    right_square = right[2][...] * (0.25 * inverses[1]) + right[3][...] * (0.5 * gram_scale * inverses[1])
+    right_square = right_square + right[4][...] * (gram_scale * gram_scale * inverses[1])
+    square = (left_square, right_square)
+    factor_square = [add_identity(0.0625 * q - 0.625 * m, 1.5625) for q, m in zip(square, scaled)]
+    factor_scaled = [1.25 * m - 0.25 * q for q, m in zip(square, scaled)]
+    fourth, tail = [None, None], [None, None]
+    for side in (1, 0):
+        fourth[side] = symmetric_dot(left_operand(factor_square[side]), right_operand(factor_square[side]))
+    for side in (1, 0):
+        tail[side] = symmetric_dot(left_operand(fourth[side]), right_operand(factor_scaled[side]))
+    roots = [add_identity(-1.25 * m - t, 6.25) for m, t in zip(scaled, tail)]
     return roots, [0.25 * lax.rsqrt(jnp.sqrt(jnp.sqrt(norm))) for norm in norms]
 
 
@@ -293,11 +288,11 @@
     width = block[0].shape[1]
 
     def kernel(upper_ref, lower_ref, block_norm_ref, *refs):
-        left_refs, right_refs, norm_refs, out_refs = refs[:5], refs[5:10], refs[10:-3], refs[-3:]
+        left_refs, right_refs, norm_refs, out_refs = refs[:2], refs[2:7], refs[7:-3], refs[-3:]
         squares = sum(ref[:1, :1] for ref in norm_refs)
         clip_factor = jnp.minimum(1.0, clip_level / jnp.sqrt(squares / entry_count))
         gram_scale = clip_factor * clip_factor / width
-        roots, scales = roots_of((left_refs, right_refs), gram_scale)
+        roots, scales = roots_of(left_refs, right_refs, gram_scale)
         halfway = triple_dot(left_operand(roots[0]), right_operand(whole_block((upper_ref, lower_ref))))
         pre = triple_dot(left_operand(halfway), right_operand(roots[1]))
         pre_scale = scales[0] * scales[1] * clip_factor
@@ -407,28 +402,26 @@
     totals = [
         own_plus("self", half, from_core["self", half], from_link["straight", half]) for half in HALVES
     ]
-    sides = [(left_stats[0],), (right_stats[0],)]
-    squares = square_call(*[after(previous, totals[0]) for previous, in sides])
-    totals[0] = after(totals[0], *squares)
+    right_square = square_call(after(right_stats[0], totals[0]))
+    totals[0] = after(totals[0], right_square)
     norm, block = None, []
     for half in HALVES:
-        joined, norm = join_call(owner_row, me, totals[half], half, arrived[half], norm, block_count)
+        joined, norm = join_call(owner_row, me, totals[half], arrived[half], norm, block_count)
         block.append(joined)
     block_norm = norm
     norm = sum_call(norm, to_core(norm, "norm"))
     chip_norms = [over(flipped(mask), norm, "chip_norm") for mask in (6, 4, 2)]
     grams = gram_call([after(block[0], norm), block[1]])
-    sides = [(previous, gram, square) for (previous,), gram, square in zip(sides, grams, squares)]
-    sides[0] += tuple(mix_call(*sides[0][:2]))
-    norm = sum_call(after(norm, sides[0][4]), *chip_norms)
+    norm = sum_call(after(norm, grams[0]), *chip_norms)
     norms = [norm]
     for shift in reversed(range(1, group_count)):
         both_ways = group_count & (group_count - 1) == 0
         pairs = [(i, i ^ shift if both_ways else (i + shift) % group_count) for i in range(group_count)]
         with jax.named_scope("group_norm"):
             norms.append(lax.ppermute(norm, "mp", pairs))
-    sides[1] += tuple(mix_call(*sides[1][:2]))
-    whole, *own = update_call(block, block_norm, *sides, norms, entry_count)
+    left = (left_stats[0], grams[0])
+    right = (right_stats[0], grams[1], right_square, *mix_call(right_stats[0], grams[1]))
+    whole, *own = update_call(block, block_norm, left, right, norms, entry_count)
 
     core_own = to_core(whole, "own")
     first = [to_link(value, "own") for value in own]

time: 108 us -> 108 us (level)
  waiting for transfers between devices: 53.5 us -> 58.3 us
  starting transfers between devices: 25.7 us -> 23 us
  Pallas kernels: 25.9 us -> 23.7 us
    ppermute x29, waiting for transfers between devices: 51.3 us -> 56.3 us  [over(): return lax.ppermute(value, 'dp', pairs)]
    ppermute x29, starting transfers between devices: 21.2 us -> 18.7 us  [over(): return lax.ppermute(value, 'dp', pairs)]
    pallas_call x19 -> x18, Pallas kernels: 20.2 us -> 18 us  [local_call(): pl.pallas_call(kernel, in_specs=[pl.BlockSpec(memory_space=pltpu.SMEM)] *...]
  transfers between devices with their start and end apart: 32 -> 32, of which waited for: 13 -> 14; matrix products, arithmetic and copies ran while one was open for 0% -> 0% of each run, Pallas kernels for 16% -> 13%
where the time goes in v14:
time: 108 us
  waiting for transfers between devices  58.3 us (54%)
  Pallas kernels  23.7 us (22%)
  starting transfers between devices  23 us (21%)
  local copies, waits for them, and re-layouts  2.56 us (2%)
    ppermute x29, waiting for transfers between devices, over(): return lax.ppermute(value, 'dp', pairs)  56.3 us
    ppermute x29, starting transfers between devices, over(): return lax.ppermute(value, 'dp', pairs)  18.7 us
    pallas_call x18, Pallas kernels, local_call(): pl.pallas_call(kernel, in_specs=[pl.BlockSpec(memory_space=pltpu.SMEM)] *...  18 us
    pallas_call x3, Pallas kernels, assemble_call(): pl.pallas_call(kernel, in_specs=in_specs, out_specs=pl.BlockSpec(memory_s...  5.71 us
    ppermute x3, starting transfers between devices, paired_body(): norms.append(lax.ppermute(norm, 'mp', pairs))  4.39 us
    unnamed x12, local copies, waits for them, and re-layouts  2.56 us
  transfers between devices with their start and end apart: 32, of which 14 were waited for; matrix products, arithmetic and copies ran while one was open for 0% of the time, Pallas kernels for 13%

profile of v14, /device:TPU:0, one launch (start us, length us, event | category | flops | bytes accessed | tf_op | source)
XLA Modules:
  0.0 107.9 jit_solution(9175147487739314925)
XLA Ops:
  0.0 1.9 %copy-done = bf16[1,512,3072]{2,1,0:T(8,128)(2,1)S(1)} copy-done((bf16[1,512,3072]{2,1,0:T(8,128)(2,1)S(1)}, bf16[1,512,3072]{2,1,0:T(8,128)(2,1)}, u32[]{:S(2)}) %copy-start) | copy-done | bytes 3145752
  4.3 0.7 pack.2
  6.1 2.7 %collective-permute-start.5 = (f32[256,512]{1,0:T(8,128)S(1)}, f32[256,512]{1,0:T(8,128)S(1)}, u32[]{:S(2)}, u32[]{:S(2)}) collective-permute-start(f32[256,512]{1,0:T(8,128)S(1)} %add.10), channel_id=1, source_target_pairs={{0,8},{4,20},{8,0},{12,28},{16,24},{20,4},{24,16},{28,12},{1,9},{5... | collective-permute-start | bytes 1572872 | tf_op jit(solution)/shard_map/link_corner/ppermute | solution.py:369
  9.6 1.6 %collective-permute-start.12 = (f32[256,512]{1,0:T(8,128)S(1)}, f32[256,512]{1,0:T(8,128)S(1)}, u32[]{:S(2)}, u32[]{:S(2)}) collective-permute-start(f32[256,512]{1,0:T(8,128)S(1)} %add.14), channel_id=1, source_target_pairs={{0,8},{4,20},{8,0},{12,28},{16,24},{20,4},{24,16},{28,12},{1,9},{5... | collective-permute-start | bytes 1572872 | tf_op jit(solution)/shard_map/link_corner/ppermute | solution.py:369
  13.1 2.9 %collective-permute-done.5.refs_1_ = f32[256,512]{1,0:T(8,128)S(1)} collective-permute-done((f32[256,512]{1,0:T(8,128)S(1)}, f32[256,512]{1,0:T(8,128)S(1)}, u32[]{:S(2)}, u32[]{:S(2)}) %collective-permute-start.5) | collective-permute-done | bytes 524320 | tf_op jit(solution)/shard_map/link_corner/ppermute | solution.py:369
  16.6 2.1 %collective-permute-start.9 = (f32[256,512]{1,0:T(8,128)S(1)}, f32[256,512]{1,0:T(8,128)S(1)}, u32[]{:S(2)}, u32[]{:S(2)}) collective-permute-start(f32[256,512]{1,0:T(8,128)S(1)} %add.12), channel_id=1, source_target_pairs={{0,8},{4,20},{8,0},{12,28},{16,24},{20,4},{24,16},{28,12},{1,9},{5... | collective-permute-start | bytes 1572872 | tf_op jit(solution)/shard_map/link_straight/ppermute | solution.py:369
  18.7 2.9 %collective-permute-done.12.refs_1_ = f32[256,512]{1,0:T(8,128)S(1)} collective-permute-done((f32[256,512]{1,0:T(8,128)S(1)}, f32[256,512]{1,0:T(8,128)S(1)}, u32[]{:S(2)}, u32[]{:S(2)}) %collective-permute-start.12) | collective-permute-done | bytes 524320 | tf_op jit(solution)/shard_map/link_corner/ppermute | solution.py:369
  21.6 2.0 %collective-permute-start.6 = (f32[256,512]{1,0:T(8,128)S(1)}, f32[256,512]{1,0:T(8,128)S(1)}, u32[]{:S(2)}, u32[]{:S(2)}) collective-permute-start(f32[256,512]{1,0:T(8,128)S(1)} %add.11), channel_id=1, source_target_pairs={{0,16},{4,12},{8,24},{12,4},{16,0},{20,28},{24,8},{28,20},{1,17},{... | collective-permute-start | bytes 1572872 | tf_op jit(solution)/shard_map/side_side/ppermute | solution.py:369
  24.4 6.0 %collective-permute-done.2.refs_1_ = f32[256,512]{1,0:T(8,128)S(1)} collective-permute-done((f32[256,512]{1,0:T(8,128)S(1)}, f32[256,512]{1,0:T(8,128)S(1)}, u32[]{:S(2)}, u32[]{:S(2)}) %collective-permute-start.2) | collective-permute-done | bytes 524320 | tf_op jit(solution)/shard_map/link_straight/ppermute | solution.py:369
  31.0 0.8 square.1.refs_4_
  31.8 9.7 %collective-permute-done.9.refs_1_ = f32[256,512]{1,0:T(8,128)S(1)} collective-permute-done((f32[256,512]{1,0:T(8,128)S(1)}, f32[256,512]{1,0:T(8,128)S(1)}, u32[]{:S(2)}, u32[]{:S(2)}) %collective-permute-start.9) | collective-permute-done | bytes 524320 | tf_op jit(solution)/shard_map/link_straight/ppermute | solution.py:369
  42.2 0.7 join.2
  42.9 0.9 collective-permute-done.13.arrival_ref
  43.8 0.7 join.3
  44.7 1.1 collective-permute-done.14.refs_1_
  45.8 2.7 %collective-permute-start.15 = (f32[8,128]{1,0:T(8,128)S(1)}, f32[8,128]{1,0:T(8,128)S(1)}, u32[]{:S(2)}, u32[]{:S(2)}) collective-permute-start(f32[8,128]{1,0:T(8,128)S(1)} %sum.2.refs_0_), channel_id=1, source_target_pairs={{0,24},{4,28},{8,16},{12,20},{16,8},{20,12},{24,0},{28,4},{1,25},{... | collective-permute-start | bytes 12296 | tf_op jit(solution)/shard_map/chip_norm/ppermute | solution.py:369
  49.3 1.5 %gram.1 = (f32[512,512]{1,0:T(8,128)S(1)}, f32[512,512]{1,0:T(8,128)S(1)}) custom-call(f32[256,512]{1,0:T(8,128)S(1)} %get-tuple-element.46.upper_ref, f32[256,512]{1,0:T(8,128)S(1)} %get-tuple-element.44.lower_ref), custom_call_target="tpu_custom_call" | custom-call | flops 1610612736 | bytes 3145728 | tf_op jit(solution)/shard_map/gram/pallas_call | solution.py:129
  50.8 1.3 %collective-permute-done.16.refs_2_ = f32[8,128]{1,0:T(8,128)S(1)} collective-permute-done((f32[8,128]{1,0:T(8,128)S(1)}, f32[8,128]{1,0:T(8,128)S(1)}, u32[]{:S(2)}, u32[]{:S(2)}) %collective-permute-start.16) | collective-permute-done | bytes 4128 | tf_op jit(solution)/shard_map/chip_norm/ppermute | solution.py:369
  52.6 3.6 %collective-permute-start.18 = (f32[8,128]{1,0:T(8,128)S(1)}, f32[8,128]{1,0:T(8,128)S(1)}, u32[]{:S(2)}, u32[]{:S(2)}) collective-permute-start(f32[8,128]{1,0:T(8,128)S(1)} %sum.3.refs_7_), channel_id=1, source_target_pairs={{0,3},{1,2},{2,1},{3,0},{4,7},{5,6},{6,5},{7,4},{8,11},{9,10},{10,... | collective-permute-start | bytes 12296 | tf_op jit(solution)/shard_map/group_norm/ppermute | solution.py:421
  56.2 0.8 collective-permute-start.20
  57.0 1.7 %mix.1 = (f32[512,512]{1,0:T(8,128)S(1)}, f32[512,512]{1,0:T(8,128)S(1)}) custom-call(f32[512,512]{1,0:T(8,128)S(1)} %bitcast.32, f32[512,512]{1,0:T(8,128)S(1)} %get-tuple-element.48.gram_ref.refs_3_), custom_call_target="tpu_custom_call" | custom-call | flops 1610612736 | bytes 4194304 | tf_op jit(solution)/shard_map/mix/pallas_call | solution.py:129
  58.7 2.0 %collective-permute-done.19.refs_9_ = f32[8,128]{1,0:T(8,128)S(1)} collective-permute-done((f32[8,128]{1,0:T(8,128)S(1)}, f32[8,128]{1,0:T(8,128)S(1)}, u32[]{:S(2)}, u32[]{:S(2)}) %collective-permute-start.19) | collective-permute-done | bytes 4128 | tf_op jit(solution)/shard_map/group_norm/ppermute | solution.py:421
  60.7 6.3 %update.1 = (f32[512,512]{1,0:T(8,128)S(1)}, f32[256,512]{1,0:T(8,128)S(1)}, f32[256,512]{1,0:T(8,128)S(1)}) custom-call(f32[256,512]{1,0:T(8,128)S(1)} %get-tuple-element.46.upper_ref, f32[256,512]{1,0:T(8,128)S(1)} %get-tuple-element.44.lower_ref, f32[8,128]{1,0:T(8,128)S(1)} %get-tuple-element.45.refs_0_.block_norm_ref, f32[512,512]{1,0:T(8,128)S(1)} %bitcast.30, ...), custom_call_target="tpu_custom_call" | custom-call | flops 4831838208 | bytes 10506240 | tf_op jit(solution)/shard_map/update/pallas_call | solution.py:129
  67.7 1.5 %collective-permute-start.25 = (f32[256,512]{1,0:T(8,128)S(1)}, f32[256,512]{1,0:T(8,128)S(1)}, u32[]{:S(2)}, u32[]{:S(2)}) collective-permute-start(f32[256,512]{1,0:T(8,128)S(1)} %get-tuple-element.55), channel_id=1, source_target_pairs={{0,8},{4,20},{8,0},{12,28},{16,24},{20,4},{24,16},{28,12},{1,9},{5... | collective-permute-start | bytes 1572872 | tf_op jit(solution)/shard_map/link_own/ppermute | solution.py:369
  69.2 7.2 %collective-permute-done.21.refs_2_ = f32[256,512]{1,0:T(8,128)S(1)} collective-permute-done((f32[256,512]{1,0:T(8,128)S(1)}, f32[256,512]{1,0:T(8,128)S(1)}, u32[]{:S(2)}, u32[]{:S(2)}) %collective-permute-start.21) | collective-permute-done | bytes 524320 | tf_op jit(solution)/shard_map/link_own/ppermute | solution.py:369
  77.2 4.8 %collective-permute-done.25.refs_3_ = f32[256,512]{1,0:T(8,128)S(1)} collective-permute-done((f32[256,512]{1,0:T(8,128)S(1)}, f32[256,512]{1,0:T(8,128)S(1)}, u32[]{:S(2)}, u32[]{:S(2)}) %collective-permute-start.25) | collective-permute-done | bytes 524320 | tf_op jit(solution)/shard_map/link_own/ppermute | solution.py:369
  82.5 10.7 %collective-permute-done.30.refs_0_ = f32[512,512]{1,0:T(8,128)S(1)} collective-permute-done((f32[512,512]{1,0:T(8,128)S(1)}, f32[512,512]{1,0:T(8,128)S(1)}, u32[]{:S(2)}, u32[]{:S(2)}) %collective-permute-start.30) | collective-permute-done | bytes 1048608 | tf_op jit(solution)/shard_map/link_sibling/ppermute | solution.py:369
  93.8 2.3 %assemble.3.refs_4_ = f32[512,3072]{1,0:T(8,128)} custom-call(s32[6]{0:T(128)S(1)} %bitcast.27, s32[1]{0:T(128)} %bitcast.1.me_ref, f32[512,512]{1,0:T(8,128)S(1)} %get-tuple-element.53.refs_0_, f32[512,512]{1,0:T(8,128)S(1)} %collective-permute-done.22.refs_1_, f32[256,512]{1,0:T(8,128)S(1)} %collective-permute-done.21.refs_2_, ...), custom_call_target="tpu_custom_call" | custom-call | bytes 12582912 | tf_op jit(solution)/shard_map/assemble/pallas_call | solution.py:340
  96.0 2.8 %collective-permute-done.24.refs_2_ = f32[256,512]{1,0:T(8,128)S(1)} collective-permute-done((f32[256,512]{1,0:T(8,128)S(1)}, f32[256,512]{1,0:T(8,128)S(1)}, u32[]{:S(2)}, u32[]{:S(2)}) %collective-permute-start.24) | collective-permute-done | bytes 524320 | tf_op jit(solution)/shard_map/link_relayed/ppermute | solution.py:369
  98.8 5.6 %collective-permute-done.28.refs_3_ = f32[256,512]{1,0:T(8,128)S(1)} collective-permute-done((f32[256,512]{1,0:T(8,128)S(1)}, f32[256,512]{1,0:T(8,128)S(1)}, u32[]{:S(2)}, u32[]{:S(2)}) %collective-permute-start.28) | collective-permute-done | bytes 524320 | tf_op jit(solution)/shard_map/link_relayed/ppermute | solution.py:369
  104.5 1.9 %assemble.4.refs_2_ = f32[512,3072]{1,0:T(8,128)} custom-call(s32[6]{0:T(128)S(1)} %bitcast.28, s32[1]{0:T(128)} %bitcast.1.me_ref, f32[512,512]{1,0:T(8,128)S(1)} %collective-permute-done.30.refs_0_, f32[512,512]{1,0:T(8,128)S(1)} %collective-permute-done.31.refs_1_, ...), custom_call_target="tpu_custom_call", output_to_operand_aliasing={{}: (6, {})} | custom-call | bytes 8388608 | tf_op jit(solution)/shard_map/assemble/pallas_call | solution.py:340
  106.4 1.5 %assemble.5 = f32[512,3072]{1,0:T(8,128)} custom-call(s32[6]{0:T(128)S(1)} %bitcast.29, s32[1]{0:T(128)} %bitcast.1.me_ref, f32[256,512]{1,0:T(8,128)S(1)} %collective-permute-done.27.refs_0_, f32[256,512]{1,0:T(8,128)S(1)} %collective-permute-done.29.refs_1_, f32[512,3072]{1,0:T(8,128)} %assemble.4.refs_2_), custom_call_target="tpu_custom_call", output_to_operand_aliasing={{}: (4, {})} | custom-call | bytes 2097152 | tf_op jit(solution)/shard_map/assemble/pallas_call | solution.py:340
  (65 shorter events, 12.8 us)
Async XLA Ops:
  3.2 2.3 %collective-permute-start.4 = (f32[256,512]{1,0:T(8,128)S(1)}, f32[256,512]{1,0:T(8,128)S(1)}, u32[]{:S(2)}, u32[]{:S(2)}) collective-permute-start(f32[256,512]{1,0:T(8,128)S(1)} %get-tuple-element.37), channel_id=1, source_target_pairs={{0,4},{4,0},{8,12},{12,8},{16,20},{20,16},{24,28},{28,24},{1,5},{5... | collective-permute-start | bytes 1572872 | tf_op jit(solution)/shard_map/core_corner/ppermute | solution.py:369
  3.8 5.1 %collective-permute-start.11 = (f32[256,512]{1,0:T(8,128)S(1)}, f32[256,512]{1,0:T(8,128)S(1)}, u32[]{:S(2)}, u32[]{:S(2)}) collective-permute-start(f32[256,512]{1,0:T(8,128)S(1)} %get-tuple-element.42), channel_id=1, source_target_pairs={{0,4},{4,0},{8,12},{12,8},{16,20},{20,16},{24,28},{28,24},{1,5},{5... | collective-permute-start | bytes 1572872 | tf_op jit(solution)/shard_map/core_corner/ppermute | solution.py:369
  3.8 5.7 %collective-permute-start.1 = (f32[256,512]{1,0:T(8,128)S(1)}, f32[256,512]{1,0:T(8,128)S(1)}, u32[]{:S(2)}, u32[]{:S(2)}) collective-permute-start(f32[256,512]{1,0:T(8,128)S(1)} %get-tuple-element.33), channel_id=1, source_target_pairs={{0,4},{4,0},{8,12},{12,8},{16,20},{20,16},{24,28},{28,24},{1,5},{5... | collective-permute-start | bytes 1572872 | tf_op jit(solution)/shard_map/core_straight/ppermute | solution.py:369
  5.0 6.2 %collective-permute-start.3 = (f32[256,512]{1,0:T(8,128)S(1)}, f32[256,512]{1,0:T(8,128)S(1)}, u32[]{:S(2)}, u32[]{:S(2)}) collective-permute-start(f32[256,512]{1,0:T(8,128)S(1)} %get-tuple-element.36), channel_id=1, source_target_pairs={{0,4},{4,0},{8,12},{12,8},{16,20},{20,16},{24,28},{28,24},{1,5},{5... | collective-permute-start | bytes 1572872 | tf_op jit(solution)/shard_map/core_side/ppermute | solution.py:369
  5.1 6.8 %collective-permute-start.8 = (f32[256,512]{1,0:T(8,128)S(1)}, f32[256,512]{1,0:T(8,128)S(1)}, u32[]{:S(2)}, u32[]{:S(2)}) collective-permute-start(f32[256,512]{1,0:T(8,128)S(1)} %get-tuple-element.40), channel_id=1, source_target_pairs={{0,4},{4,0},{8,12},{12,8},{16,20},{20,16},{24,28},{28,24},{1,5},{5... | collective-permute-start | bytes 1572872 | tf_op jit(solution)/shard_map/core_straight/ppermute | solution.py:369
  6.1 9.8 %collective-permute-start.5 = (f32[256,512]{1,0:T(8,128)S(1)}, f32[256,512]{1,0:T(8,128)S(1)}, u32[]{:S(2)}, u32[]{:S(2)}) collective-permute-start(f32[256,512]{1,0:T(8,128)S(1)} %add.10), channel_id=1, source_target_pairs={{0,8},{4,20},{8,0},{12,28},{16,24},{20,4},{24,16},{28,12},{1,9},{5... | collective-permute-start | bytes 1572872 | tf_op jit(solution)/shard_map/link_corner/ppermute | solution.py:369
  8.8 7.8 %collective-permute-start.10 = (f32[256,512]{1,0:T(8,128)S(1)}, f32[256,512]{1,0:T(8,128)S(1)}, u32[]{:S(2)}, u32[]{:S(2)}) collective-permute-start(f32[256,512]{1,0:T(8,128)S(1)} %get-tuple-element.41), channel_id=1, source_target_pairs={{0,4},{4,0},{8,12},{12,8},{16,20},{20,16},{24,28},{28,24},{1,5},{5... | collective-permute-start | bytes 1572872 | tf_op jit(solution)/shard_map/core_side/ppermute | solution.py:369
  9.6 12.0 %collective-permute-start.12 = (f32[256,512]{1,0:T(8,128)S(1)}, f32[256,512]{1,0:T(8,128)S(1)}, u32[]{:S(2)}, u32[]{:S(2)}) collective-permute-start(f32[256,512]{1,0:T(8,128)S(1)} %add.14), channel_id=1, source_target_pairs={{0,8},{4,20},{8,0},{12,28},{16,24},{20,4},{24,16},{28,12},{1,9},{5... | collective-permute-start | bytes 1572872 | tf_op jit(solution)/shard_map/link_corner/ppermute | solution.py:369
  11.1 13.1 %collective-permute-start = (f32[256,512]{1,0:T(8,128)S(1)}, f32[256,512]{1,0:T(8,128)S(1)}, u32[]{:S(2)}, u32[]{:S(2)}) collective-permute-start(f32[256,512]{1,0:T(8,128)S(1)} %get-tuple-element.32), channel_id=1, source_target_pairs={{0,4},{4,0},{8,12},{12,8},{16,20},{20,16},{24,28},{28,24},{1,5},{5... | collective-permute-start | bytes 1572872 | tf_op jit(solution)/shard_map/core_self/ppermute | solution.py:369
  11.9 18.5 %collective-permute-start.2 = (f32[256,512]{1,0:T(8,128)S(1)}, f32[256,512]{1,0:T(8,128)S(1)}, u32[]{:S(2)}, u32[]{:S(2)}) collective-permute-start(f32[256,512]{1,0:T(8,128)S(1)} %add.8), channel_id=1, source_target_pairs={{0,8},{4,20},{8,0},{12,28},{16,24},{20,4},{24,16},{28,12},{1,9},{5... | collective-permute-start | bytes 1572872 | tf_op jit(solution)/shard_map/link_straight/ppermute | solution.py:369
  16.0 15.8 %collective-permute-start.7 = (f32[256,512]{1,0:T(8,128)S(1)}, f32[256,512]{1,0:T(8,128)S(1)}, u32[]{:S(2)}, u32[]{:S(2)}) collective-permute-start(f32[256,512]{1,0:T(8,128)S(1)} %get-tuple-element.39), channel_id=1, source_target_pairs={{0,4},{4,0},{8,12},{12,8},{16,20},{20,16},{24,28},{28,24},{1,5},{5... | collective-permute-start | bytes 1572872 | tf_op jit(solution)/shard_map/core_self/ppermute | solution.py:369
  16.6 24.9 %collective-permute-start.9 = (f32[256,512]{1,0:T(8,128)S(1)}, f32[256,512]{1,0:T(8,128)S(1)}, u32[]{:S(2)}, u32[]{:S(2)}) collective-permute-start(f32[256,512]{1,0:T(8,128)S(1)} %add.12), channel_id=1, source_target_pairs={{0,8},{4,20},{8,0},{12,28},{16,24},{20,4},{24,16},{28,12},{1,9},{5... | collective-permute-start | bytes 1572872 | tf_op jit(solution)/shard_map/link_straight/ppermute | solution.py:369
  21.6 20.6 %collective-permute-start.6 = (f32[256,512]{1,0:T(8,128)S(1)}, f32[256,512]{1,0:T(8,128)S(1)}, u32[]{:S(2)}, u32[]{:S(2)}) collective-permute-start(f32[256,512]{1,0:T(8,128)S(1)} %add.11), channel_id=1, source_target_pairs={{0,16},{4,12},{8,24},{12,4},{16,0},{20,28},{24,8},{28,20},{1,17},{... | collective-permute-start | bytes 1572872 | tf_op jit(solution)/shard_map/side_side/ppermute | solution.py:369
  24.3 19.5 %collective-permute-start.13 = (f32[256,512]{1,0:T(8,128)S(1)}, f32[256,512]{1,0:T(8,128)S(1)}, u32[]{:S(2)}, u32[]{:S(2)}) collective-permute-start(f32[256,512]{1,0:T(8,128)S(1)} %add.15), channel_id=1, source_target_pairs={{0,16},{4,12},{8,24},{12,4},{16,0},{20,28},{24,8},{28,20},{1,17},{... | collective-permute-start | bytes 1572872 | tf_op jit(solution)/shard_map/side_side/ppermute | solution.py:369
  44.5 1.2 %collective-permute-start.14 = (f32[8,128]{1,0:T(8,128)S(1)}, f32[8,128]{1,0:T(8,128)S(1)}, u32[]{:S(2)}, u32[]{:S(2)}) collective-permute-start(f32[8,128]{1,0:T(8,128)S(1)} %get-tuple-element.45.refs_0_.block_norm_ref), channel_id=1, source_target_pairs={{0,4},{4,0},{8,12},{12,8},{16,20},{20,16},{24,28},{28,24},{1,5},{5... | collective-permute-start | bytes 12296 | tf_op jit(solution)/shard_map/core_norm/ppermute | solution.py:369
  45.8 5.0 %collective-permute-start.15 = (f32[8,128]{1,0:T(8,128)S(1)}, f32[8,128]{1,0:T(8,128)S(1)}, u32[]{:S(2)}, u32[]{:S(2)}) collective-permute-start(f32[8,128]{1,0:T(8,128)S(1)} %sum.2.refs_0_), channel_id=1, source_target_pairs={{0,24},{4,28},{8,16},{12,20},{16,8},{20,12},{24,0},{28,4},{1,25},{... | collective-permute-start | bytes 12296 | tf_op jit(solution)/shard_map/chip_norm/ppermute | solution.py:369
  48.5 3.6 %collective-permute-start.16 = (f32[8,128]{1,0:T(8,128)S(1)}, f32[8,128]{1,0:T(8,128)S(1)}, u32[]{:S(2)}, u32[]{:S(2)}) collective-permute-start(f32[8,128]{1,0:T(8,128)S(1)} %sum.2.refs_0_), channel_id=1, source_target_pairs={{0,16},{4,20},{8,24},{12,28},{16,0},{20,4},{24,8},{28,12},{1,17},{... | collective-permute-start | bytes 12296 | tf_op jit(solution)/shard_map/chip_norm/ppermute | solution.py:369
  49.0 3.6 %collective-permute-start.17 = (f32[8,128]{1,0:T(8,128)S(1)}, f32[8,128]{1,0:T(8,128)S(1)}, u32[]{:S(2)}, u32[]{:S(2)}) collective-permute-start(f32[8,128]{1,0:T(8,128)S(1)} %sum.2.refs_0_), channel_id=1, source_target_pairs={{0,8},{4,12},{8,0},{12,4},{16,24},{20,28},{24,16},{28,20},{1,9},{5... | collective-permute-start | bytes 12296 | tf_op jit(solution)/shard_map/chip_norm/ppermute | solution.py:369
  52.6 6.1 %collective-permute-start.18 = (f32[8,128]{1,0:T(8,128)S(1)}, f32[8,128]{1,0:T(8,128)S(1)}, u32[]{:S(2)}, u32[]{:S(2)}) collective-permute-start(f32[8,128]{1,0:T(8,128)S(1)} %sum.3.refs_7_), channel_id=1, source_target_pairs={{0,3},{1,2},{2,1},{3,0},{4,7},{5,6},{6,5},{7,4},{8,11},{9,10},{10,... | collective-permute-start | bytes 12296 | tf_op jit(solution)/shard_map/group_norm/ppermute | solution.py:421
  56.2 4.5 %collective-permute-start.19 = (f32[8,128]{1,0:T(8,128)S(1)}, f32[8,128]{1,0:T(8,128)S(1)}, u32[]{:S(2)}, u32[]{:S(2)}) collective-permute-start(f32[8,128]{1,0:T(8,128)S(1)} %sum.3.refs_7_), channel_id=1, source_target_pairs={{0,2},{1,3},{2,0},{3,1},{4,6},{5,7},{6,4},{7,5},{8,10},{9,11},{10,... | collective-permute-start | bytes 12296 | tf_op jit(solution)/shard_map/group_norm/ppermute | solution.py:421
  56.2 4.5 %collective-permute-start.20 = (f32[8,128]{1,0:T(8,128)S(1)}, f32[8,128]{1,0:T(8,128)S(1)}, u32[]{:S(2)}, u32[]{:S(2)}) collective-permute-start(f32[8,128]{1,0:T(8,128)S(1)} %sum.3.refs_7_), channel_id=1, source_target_pairs={{0,1},{1,0},{2,3},{3,2},{4,5},{5,4},{6,7},{7,6},{8,9},{9,8},{10,11... | collective-permute-start | bytes 12296 | tf_op jit(solution)/shard_map/group_norm/ppermute | solution.py:421
  67.0 9.3 %collective-permute-start.22 = (f32[512,512]{1,0:T(8,128)S(1)}, f32[512,512]{1,0:T(8,128)S(1)}, u32[]{:S(2)}, u32[]{:S(2)}) collective-permute-start(f32[512,512]{1,0:T(8,128)S(1)} %get-tuple-element.53.refs_0_), channel_id=1, source_target_pairs={{0,4},{4,0},{8,12},{12,8},{16,20},{20,16},{24,28},{28,24},{1,5},{5... | collective-permute-start | bytes 3145736 | tf_op jit(solution)/shard_map/core_own/ppermute | solution.py:369
  67.1 9.2 %collective-permute-start.21 = (f32[256,512]{1,0:T(8,128)S(1)}, f32[256,512]{1,0:T(8,128)S(1)}, u32[]{:S(2)}, u32[]{:S(2)}) collective-permute-start(f32[256,512]{1,0:T(8,128)S(1)} %get-tuple-element.52), channel_id=1, source_target_pairs={{0,8},{4,20},{8,0},{12,28},{16,24},{20,4},{24,16},{28,12},{1,9},{5... | collective-permute-start | bytes 1572872 | tf_op jit(solution)/shard_map/link_own/ppermute | solution.py:369
  67.7 14.3 %collective-permute-start.25 = (f32[256,512]{1,0:T(8,128)S(1)}, f32[256,512]{1,0:T(8,128)S(1)}, u32[]{:S(2)}, u32[]{:S(2)}) collective-permute-start(f32[256,512]{1,0:T(8,128)S(1)} %get-tuple-element.55), channel_id=1, source_target_pairs={{0,8},{4,20},{8,0},{12,28},{16,24},{20,4},{24,16},{28,12},{1,9},{5... | collective-permute-start | bytes 1572872 | tf_op jit(solution)/shard_map/link_own/ppermute | solution.py:369
  76.4 16.8 %collective-permute-start.30 = (f32[512,512]{1,0:T(8,128)S(1)}, f32[512,512]{1,0:T(8,128)S(1)}, u32[]{:S(2)}, u32[]{:S(2)}) collective-permute-start(f32[512,512]{1,0:T(8,128)S(1)} %collective-permute-done.22.refs_1_), channel_id=1, source_target_pairs={{0,8},{4,20},{8,0},{12,28},{16,24},{20,4},{24,16},{28,12},{1,9},{5... | collective-permute-start | bytes 3145736 | tf_op jit(solution)/shard_map/link_sibling/ppermute | solution.py:369
  76.9 5.1 %collective-permute-start.23 = (f32[256,512]{1,0:T(8,128)S(1)}, f32[256,512]{1,0:T(8,128)S(1)}, u32[]{:S(2)}, u32[]{:S(2)}) collective-permute-start(f32[256,512]{1,0:T(8,128)S(1)} %collective-permute-done.21.refs_2_), channel_id=1, source_target_pairs={{0,4},{4,0},{8,12},{12,8},{16,20},{20,16},{24,28},{28,24},{1,5},{5... | collective-permute-start | bytes 1572872 | tf_op jit(solution)/shard_map/core_first/ppermute | solution.py:369
  82.0 11.2 %collective-permute-start.26 = (f32[256,512]{1,0:T(8,128)S(1)}, f32[256,512]{1,0:T(8,128)S(1)}, u32[]{:S(2)}, u32[]{:S(2)}) collective-permute-start(f32[256,512]{1,0:T(8,128)S(1)} %collective-permute-done.25.refs_3_), channel_id=1, source_target_pairs={{0,4},{4,0},{8,12},{12,8},{16,20},{20,16},{24,28},{28,24},{1,5},{5... | collective-permute-start | bytes 1572872 | tf_op jit(solution)/shard_map/core_first/ppermute | solution.py:369
  82.0 16.8 %collective-permute-start.24 = (f32[256,512]{1,0:T(8,128)S(1)}, f32[256,512]{1,0:T(8,128)S(1)}, u32[]{:S(2)}, u32[]{:S(2)}) collective-permute-start(f32[256,512]{1,0:T(8,128)S(1)} %collective-permute-done.23.refs_4_), channel_id=1, source_target_pairs={{0,8},{4,20},{8,0},{12,28},{16,24},{20,4},{24,16},{28,12},{1,9},{5... | collective-permute-start | bytes 1572872 | tf_op jit(solution)/shard_map/link_relayed/ppermute | solution.py:369
  93.2 11.2 %collective-permute-start.31 = (f32[512,512]{1,0:T(8,128)S(1)}, f32[512,512]{1,0:T(8,128)S(1)}, u32[]{:S(2)}, u32[]{:S(2)}) collective-permute-start(f32[512,512]{1,0:T(8,128)S(1)} %collective-permute-done.30.refs_0_), channel_id=1, source_target_pairs={{0,4},{4,0},{8,12},{12,8},{16,20},{20,16},{24,28},{28,24},{1,5},{5... | collective-permute-start | bytes 3145736 | tf_op jit(solution)/shard_map/core_second/ppermute | solution.py:369
  93.2 11.2 %collective-permute-start.28 = (f32[256,512]{1,0:T(8,128)S(1)}, f32[256,512]{1,0:T(8,128)S(1)}, u32[]{:S(2)}, u32[]{:S(2)}) collective-permute-start(f32[256,512]{1,0:T(8,128)S(1)} %collective-permute-done.26.refs_5_), channel_id=1, source_target_pairs={{0,8},{4,20},{8,0},{12,28},{16,24},{20,4},{24,16},{28,12},{1,9},{5... | collective-permute-start | bytes 1572872 | tf_op jit(solution)/shard_map/link_relayed/ppermute | solution.py:369
  98.8 7.5 %collective-permute-start.27 = (f32[256,512]{1,0:T(8,128)S(1)}, f32[256,512]{1,0:T(8,128)S(1)}, u32[]{:S(2)}, u32[]{:S(2)}) collective-permute-start(f32[256,512]{1,0:T(8,128)S(1)} %collective-permute-done.24.refs_2_), channel_id=1, source_target_pairs={{0,4},{4,0},{8,12},{12,8},{16,20},{20,16},{24,28},{28,24},{1,5},{5... | collective-permute-start | bytes 1572872 | tf_op jit(solution)/shard_map/core_relayed/ppermute | solution.py:369
  104.5 1.9 %collective-permute-start.29 = (f32[256,512]{1,0:T(8,128)S(1)}, f32[256,512]{1,0:T(8,128)S(1)}, u32[]{:S(2)}, u32[]{:S(2)}) collective-permute-start(f32[256,512]{1,0:T(8,128)S(1)} %collective-permute-done.28.refs_3_), channel_id=1, source_target_pairs={{0,4},{4,0},{8,12},{12,8},{16,20},{20,16},{24,28},{28,24},{1,5},{5... | collective-permute-start | bytes 1572872 | tf_op jit(solution)/shard_map/core_relayed/ppermute | solution.py:369
  (6 other events, 84.4 us)

commit v15 on v13

--- a/solution.py
+++ b/solution.py
@@ -65,6 +65,7 @@
 
 
 SMALL = 2 << 20
+CHUNK = 32
 LARGE = 20 << 20
 F32 = jnp.float32
 HALVES = (0, 1)
@@ -137,12 +138,17 @@
     )(*scalars, *operands)
 
 
-def owner_block(owners_ref, grad_ref, rows, width, target):
+def owner_columns(places_ref, grad_ref, width, target):
     column = 0
     for index in range(1, grad_ref.shape[1] // width):
-        column = column + jnp.where(owners_ref[index] == target, index * width, 0)
-    columns = pl.ds(pl.multiple_of(column, width), width)
-    return grad_ref[rows, columns].astype(F32)
+        column = column + jnp.where(places_ref[index] == target, index * width, 0)
+    return pl.ds(pl.multiple_of(column, width), width)
+
+
+def row_chunks(half, width):
+    first = 0 if half is None else half * (width // 2)
+    count = width if half is None else width // 2
+    return [(pl.ds(first + row, CHUNK), pl.ds(row, CHUNK)) for row in range(0, count, CHUNK)]
 
 
 def rows_of(half, width):
@@ -153,60 +159,56 @@
     return jax.ShapeDtypeStruct((width if half is None else width // 2, width), F32)
 
 
-def piece_of(ref, half, width):
-    return ref[rows_of(half, width), :] if ref.shape[0] == width else ref[...]
-
-
-def pack_call(owners, me, grads, pieces, width):
-    def kernel(owners_ref, me_ref, grad_ref, *out_refs):
-        for (kind, half), out_ref in zip(pieces, out_refs):
-            target = piece_target(kind, me_ref[0] ^ 1)
-            out_ref[...] = owner_block(owners_ref, grad_ref, rows_of(half, width), width, target)
-
-    shapes = [piece_shape(half, width) for _, half in pieces]
-    return local_call(kernel, "pack", shapes, (grads,), (owners, me))
-
-
-def add_call(owners, me, grads, kind, half, arrivals, width):
-    flat = [value for arrival in arrivals for value in (arrival if isinstance(arrival, list) else [arrival])]
-
-    def kernel(owners_ref, me_ref, grad_ref, *refs):
-        target = piece_target(kind, me_ref[0])
-        for part in HALVES if half is None else (half,):
-            total = owner_block(owners_ref, grad_ref, rows_of(part, width), width, target)
-            place = 0
-            for arrival in arrivals:
-                if isinstance(arrival, list):
-                    total = total + refs[place + part][...]
-                    place += 2
-                else:
-                    total = total + piece_of(refs[place], part, width)
-                    place += 1
-            if half is None:
-                refs[-1][rows_of(part, width), :] = total
-            else:
-                refs[-1][...] = total
-
-    return local_call(kernel, "add", piece_shape(half, width), (grads, *flat), (owners, me))
-
-
-def join_call(owners, me, total, half, arrival, norm, block_count):
-    width = total.shape[1]
-
-    def kernel(owners_ref, me_ref, total_ref, arrival_ref, *refs):
+def pack_call(places, grads, pieces, width, with_owned=False):
+    block_count = grads.shape[1] // width
+
+    def kernel(places_ref, grad_ref, *out_refs):
+        me = places_ref[block_count]
+        for (kind, flip, half), out_ref in zip(pieces, out_refs):
+            columns = owner_columns(places_ref, grad_ref, width, piece_target(kind, me ^ flip))
+            for block_rows, piece_rows in row_chunks(half, width):
+                out_ref[piece_rows, :] = grad_ref[block_rows, columns].astype(F32)
+        if with_owned:
+            owned = 0
+            for index in range(block_count):
+                owned = owned + jnp.where(places_ref[index] == me, 1, 0)
+            out_refs[-1][...] = jnp.full((8, 128), owned.astype(F32))
+
+    shapes = [piece_shape(half, width) for _, _, half in pieces]
+    if with_owned:
+        shapes.append(jax.ShapeDtypeStruct((8, 128), F32))
+    return local_call(kernel, "pack", shapes, (grads,), (places,))
+
+
+def add_kernel(*refs):
+    for row in range(0, refs[-1].shape[0], CHUNK):
+        total = refs[0][row : row + CHUNK, :]
+        for ref in refs[1:-1]:
+            total = total + ref[row : row + CHUNK, :]
+        refs[-1][row : row + CHUNK, :] = total
+
+
+def add_call(*pieces):
+    return local_call(add_kernel, "add", jax.ShapeDtypeStruct(pieces[0].shape, F32), pieces)
+
+
+def join_call(total, arrival, owned, norm):
+    rows, width = total.shape
+
+    def kernel(total_ref, arrival_ref, owned_ref, *refs):
         block_ref, norm_ref = refs[-2:]
-        block = piece_of(total_ref, half, width) + arrival_ref[...]
-        block_ref[...] = block
-        owned = 0
-        for index in range(block_count):
-            owned = owned + jnp.where(owners_ref[index] == me_ref[0], 1, 0)
-        squares = jnp.sum(block * block, keepdims=True).reshape(1, 1) * owned.astype(F32)
-        total_squares = jnp.broadcast_to(squares, norm_ref.shape)
+        squares = jnp.zeros((8, width), F32)
+        for row in range(0, rows, CHUNK):
+            block = total_ref[row : row + CHUNK, :] + arrival_ref[row : row + CHUNK, :]
+            block_ref[row : row + CHUNK, :] = block
+            squares = squares + jnp.sum((block * block).reshape(CHUNK // 8, 8, width), axis=0)
+        squares = jnp.sum(squares, keepdims=True).reshape(1, 1)
+        total_squares = squares * owned_ref[...]
         norm_ref[...] = total_squares if norm is None else total_squares + refs[0][...]
 
-    shapes = [piece_shape(half, width), jax.ShapeDtypeStruct((8, 128), F32)]
-    operands = (total, arrival) if norm is None else (total, arrival, norm)
-    return local_call(kernel, "join", shapes, operands, (owners, me))
+    shapes = [jax.ShapeDtypeStruct((rows, width), F32), jax.ShapeDtypeStruct((8, 128), F32)]
+    operands = (total, arrival, owned) if norm is None else (total, arrival, owned, norm)
+    return local_call(kernel, "join", shapes, operands)
 
 
 def sum_kernel(*refs):
@@ -313,17 +315,17 @@
     return local_call(kernel, "update", shapes, operands, flops=36 * width**3, vmem=LARGE)
 
 
-def assemble_call(owners, me, places, slots, block_count, started):
+def assemble_call(places, sources, slots, block_count, started):
     width = slots[0].shape[1]
 
-    def kernel(owners_ref, me_ref, *refs):
+    def kernel(places_ref, *refs):
         out_ref, sem = refs[-2:]
         copies = []
-        for number, (kind, flip, half) in enumerate(places):
-            target = piece_target(kind, me_ref[0] ^ flip)
+        for number, (kind, flip, half) in enumerate(sources):
+            target = piece_target(kind, places_ref[block_count] ^ flip)
             owned, column = 0, 0
             for index in range(block_count):
-                matches = owners_ref[index] == target
+                matches = places_ref[index] == target
                 owned = owned + jnp.where(matches, 1, 0)
                 column = column + jnp.where(matches, index * width, 0)
             columns = pl.ds(pl.multiple_of(column, width), width)
@@ -334,9 +336,9 @@
         for owned, copy in copies:
             pl.when(owned == 1)(copy.wait)
 
-    in_specs = [pl.BlockSpec(memory_space=pltpu.SMEM)] * 2
+    in_specs = [pl.BlockSpec(memory_space=pltpu.SMEM)]
     in_specs += [pl.BlockSpec(memory_space=pltpu.VMEM)] * len(slots)
-    operands = [owners, me, *slots]
+    operands = [places, *slots]
     aliases = {}
     if started is not None:
         aliases = {len(operands): 0}
@@ -361,7 +363,7 @@
     width = left_stats.shape[1]
     owner_row = owners[0]
     block_count = owner_row.shape[0]
-    me = lax.axis_index("dp").astype(jnp.int32).reshape(1)
+    places = jnp.concatenate([owner_row, lax.axis_index("dp").astype(jnp.int32).reshape(1)])
     group_count = lax.axis_size("mp")
     entry_count = width * block_count * width * group_count
     grads = replica_grads[0]
@@ -382,37 +384,38 @@
     def to_side(value, label):
         return over([(i, i ^ (4 - 2 * (i % 2))) for i in range(8)], value, "side_" + label)
 
-    def own_plus(kind, half, *arrivals):
-        return add_call(owner_row, me, grads, kind, half, arrivals, width)
-
     def assemble(result, *pieces):
-        return assemble_call(owner_row, me, *zip(*pieces), block_count, result)
+        return assemble_call(places, *zip(*pieces), block_count, result)
 
     def after(value, *others):
         return lax.optimization_barrier((value, *others))[0]
 
     kinds = ("corner", "straight", "side", "self")
-    pieces = []
-    for pair in (kinds[:2], kinds[2:]):
-        pieces += pack_call(owner_row, me, grads, [(kind, half) for kind in pair for half in HALVES], width)
     keys = [(kind, half) for kind in kinds for half in HALVES]
+
+    def cut(gate, for_other, for_own, **options):
+        pieces = [(kind, 1, half) for kind, half in for_other] + [(kind, 0, half) for kind, half in for_own]
+        return pack_call(gate, grads, pieces, width, **options)
+
+    *pieces, own_first, own_second = cut(places, keys[:4], keys[:2])
+    pieces += cut(places, keys[4:], [])
     from_core = {key: to_core(value, key[0]) for key, value in zip(keys, pieces)}
-    from_link = {
-        key: to_link(own_plus(*key, from_core[key]), key[0]) for key in keys if key[0] in kinds[:2]
-    }
+    sums = [add_call(own_first, from_core[keys[0]]), add_call(own_second, from_core[keys[1]])]
+    *own, owned = cut(after(places, sums[1]), [], keys[2:], with_owned=True)
+    own = dict(zip(keys[2:], own))
+    sums += [add_call(own[key], from_core[key]) for key in keys[2:4]]
+    from_link = {key: to_link(value, key[0]) for key, value in zip(keys[:4], sums)}
     arrived = [
-        to_side(own_plus("side", half, from_core["side", half], from_link["corner", half]), "side")
+        to_side(add_call(own["side", half], from_core["side", half], from_link["corner", half]), "side")
         for half in HALVES
     ]
-    totals = [
-        own_plus("self", half, from_core["self", half], from_link["straight", half]) for half in HALVES
-    ]
+    totals = [add_call(own["self", half], from_core["self", half], from_link["straight", half]) for half in HALVES]
     sides = [(left_stats[0],), (right_stats[0],)]
     squares = square_call(*[after(previous, totals[0]) for previous, in sides])
     totals[0] = after(totals[0], *squares)
     norm, block = None, []
     for half in HALVES:
-        joined, norm = join_call(owner_row, me, totals[half], half, arrived[half], norm, block_count)
+        joined, norm = join_call(totals[half], arrived[half], owned, norm)
         block.append(joined)
     block_norm = norm
     norm = sum_call(norm, to_core(norm, "norm"))

time: 108 us -> 108 us (level)
  Pallas kernels: 25.9 us -> 20.7 us
  waiting for transfers between devices: 53.5 us -> 56.9 us
    pallas_call x19 -> x20, Pallas kernels: 20.2 us -> 15.6 us  [local_call(): pl.pallas_call(kernel, in_specs=[pl.BlockSpec(memory_space=pltpu.SMEM)] *...]
    ppermute x29, waiting for transfers between devices: 51.3 us -> 54.8 us  [over(): return lax.ppermute(value, 'dp', pairs)]
    unnamed x12 -> x8, local copies, waits for them, and re-layouts: 2.56 us -> 1.9 us
  transfers between devices with their start and end apart: 32 -> 32, of which waited for: 13 -> 14; matrix products, arithmetic and copies ran while one was open for 0% -> 0% of each run, Pallas kernels for 16% -> 12%
where the time goes in v15:
time: 108 us; the launch traced here: 107 us
  waiting for transfers between devices  56.9 us (53%)
  starting transfers between devices  26.4 us (24%)
  Pallas kernels  20.7 us (19%)
  local copies, waits for them, and re-layouts  1.9 us (2%)
    ppermute x29, waiting for transfers between devices, over(): return lax.ppermute(value, 'dp', pairs)  54.8 us
    ppermute x29, starting transfers between devices, over(): return lax.ppermute(value, 'dp', pairs)  21.9 us
    pallas_call x20, Pallas kernels, local_call(): pl.pallas_call(kernel, in_specs=[pl.BlockSpec(memory_space=pltpu.SMEM)] *...  15.6 us
    pallas_call x3, Pallas kernels, assemble_call(): pl.pallas_call(kernel, in_specs=in_specs, out_specs=pl.BlockSpec(memory_s...  5.09 us
    ppermute x3, starting transfers between devices, paired_body(): norms.append(lax.ppermute(norm, 'mp', pairs))  4.54 us
  transfers between devices with their start and end apart: 32, of which 14 were waited for; matrix products, arithmetic and copies ran while one was open for 0% of the time, Pallas kernels for 12%

profile of v15, /device:TPU:0, one launch (start us, length us, event | category | flops | bytes accessed | tf_op | source)
XLA Modules:
  0.0 107.0 jit_solution(3639696261440373501)
XLA Ops:
  0.7 1.9 %copy-done = bf16[1,512,3072]{2,1,0:T(8,128)(2,1)S(1)} copy-done((bf16[1,512,3072]{2,1,0:T(8,128)(2,1)S(1)}, bf16[1,512,3072]{2,1,0:T(8,128)(2,1)}, u32[]{:S(2)}) %copy-start) | copy-done | bytes 3145752
  2.6 0.8 pack.3
  6.2 2.9 %collective-permute-start.6 = (f32[256,512]{1,0:T(8,128)S(1)}, f32[256,512]{1,0:T(8,128)S(1)}, u32[]{:S(2)}, u32[]{:S(2)}) collective-permute-start(f32[256,512]{1,0:T(8,128)S(1)} %add.13), channel_id=1, source_target_pairs={{0,8},{4,20},{8,0},{12,28},{16,24},{20,4},{24,16},{28,12},{1,9},{5... | collective-permute-start | bytes 1572872 | tf_op jit(solution)/shard_map/link_corner/ppermute | solution.py:376
  9.8 0.8 pack.4
  10.7 1.5 %collective-permute-start.3 = (f32[256,512]{1,0:T(8,128)S(1)}, f32[256,512]{1,0:T(8,128)S(1)}, u32[]{:S(2)}, u32[]{:S(2)}) collective-permute-start(f32[256,512]{1,0:T(8,128)S(1)} %add.11), channel_id=1, source_target_pairs={{0,8},{4,20},{8,0},{12,28},{16,24},{20,4},{24,16},{28,12},{1,9},{5... | collective-permute-start | bytes 1572872 | tf_op jit(solution)/shard_map/link_straight/ppermute | solution.py:376
  12.6 3.6 %collective-permute-done.6.refs_2_ = f32[256,512]{1,0:T(8,128)S(1)} collective-permute-done((f32[256,512]{1,0:T(8,128)S(1)}, f32[256,512]{1,0:T(8,128)S(1)}, u32[]{:S(2)}, u32[]{:S(2)}) %collective-permute-start.6) | collective-permute-done | bytes 524320 | tf_op jit(solution)/shard_map/link_corner/ppermute | solution.py:376
  16.2 2.0 %collective-permute-start.10 = (f32[256,512]{1,0:T(8,128)S(1)}, f32[256,512]{1,0:T(8,128)S(1)}, u32[]{:S(2)}, u32[]{:S(2)}) collective-permute-start(f32[256,512]{1,0:T(8,128)S(1)} %add.15), channel_id=1, source_target_pairs={{0,8},{4,20},{8,0},{12,28},{16,24},{20,4},{24,16},{28,12},{1,9},{5... | collective-permute-start | bytes 1572872 | tf_op jit(solution)/shard_map/link_straight/ppermute | solution.py:376
  18.3 3.5 %collective-permute-done.12.refs_2_ = f32[256,512]{1,0:T(8,128)S(1)} collective-permute-done((f32[256,512]{1,0:T(8,128)S(1)}, f32[256,512]{1,0:T(8,128)S(1)}, u32[]{:S(2)}, u32[]{:S(2)}) %collective-permute-start.12) | collective-permute-done | bytes 524320 | tf_op jit(solution)/shard_map/link_corner/ppermute | solution.py:376
  21.8 2.1 %collective-permute-start.7 = (f32[256,512]{1,0:T(8,128)S(1)}, f32[256,512]{1,0:T(8,128)S(1)}, u32[]{:S(2)}, u32[]{:S(2)}) collective-permute-start(f32[256,512]{1,0:T(8,128)S(1)} %add.14), channel_id=1, source_target_pairs={{0,16},{4,12},{8,24},{12,4},{16,0},{20,28},{24,8},{28,20},{1,17},{... | collective-permute-start | bytes 1572872 | tf_op jit(solution)/shard_map/side_side/ppermute | solution.py:376
  24.1 6.7 %collective-permute-done.3.refs_2_ = f32[256,512]{1,0:T(8,128)S(1)} collective-permute-done((f32[256,512]{1,0:T(8,128)S(1)}, f32[256,512]{1,0:T(8,128)S(1)}, u32[]{:S(2)}, u32[]{:S(2)}) %collective-permute-start.3) | collective-permute-done | bytes 524320 | tf_op jit(solution)/shard_map/link_straight/ppermute | solution.py:376
  30.9 1.5 %square.1 = (f32[512,512]{1,0:T(8,128)S(1)}, f32[512,512]{1,0:T(8,128)S(1)}) custom-call(f32[512,512]{1,0:T(8,128)S(1)} %bitcast.8, f32[512,512]{1,0:T(8,128)S(1)} %bitcast.11), custom_call_target="tpu_custom_call" | custom-call | flops 1610612736 | bytes 4194304 | tf_op jit(solution)/shard_map/square/pallas_call | solution.py:129
  32.4 9.7 %collective-permute-done.10.refs_2_ = f32[256,512]{1,0:T(8,128)S(1)} collective-permute-done((f32[256,512]{1,0:T(8,128)S(1)}, f32[256,512]{1,0:T(8,128)S(1)}, u32[]{:S(2)}, u32[]{:S(2)}) %collective-permute-start.10) | collective-permute-done | bytes 524320 | tf_op jit(solution)/shard_map/link_straight/ppermute | solution.py:376
  42.3 1.4 %collective-permute-done.13.arrival_ref = f32[256,512]{1,0:T(8,128)S(1)} collective-permute-done((f32[256,512]{1,0:T(8,128)S(1)}, f32[256,512]{1,0:T(8,128)S(1)}, u32[]{:S(2)}, u32[]{:S(2)}) %collective-permute-start.13) | collective-permute-done | bytes 524320 | tf_op jit(solution)/shard_map/side_side/ppermute | solution.py:376
  44.4 0.8 collective-permute-done.14.refs_1_
  45.2 3.0 %collective-permute-start.15 = (f32[8,128]{1,0:T(8,128)S(1)}, f32[8,128]{1,0:T(8,128)S(1)}, u32[]{:S(2)}, u32[]{:S(2)}) collective-permute-start(f32[8,128]{1,0:T(8,128)S(1)} %sum.2.refs_0_), channel_id=1, source_target_pairs={{0,24},{4,28},{8,16},{12,20},{16,8},{20,12},{24,0},{28,4},{1,25},{... | collective-permute-start | bytes 12296 | tf_op jit(solution)/shard_map/chip_norm/ppermute | solution.py:376
  48.8 1.5 %gram.1 = (f32[512,512]{1,0:T(8,128)S(1)}, f32[512,512]{1,0:T(8,128)S(1)}) custom-call(f32[256,512]{1,0:T(8,128)S(1)} %get-tuple-element.74.upper_ref, f32[256,512]{1,0:T(8,128)S(1)} %get-tuple-element.72.lower_ref), custom_call_target="tpu_custom_call" | custom-call | flops 1610612736 | bytes 3145728 | tf_op jit(solution)/shard_map/gram/pallas_call | solution.py:129
  50.3 1.7 %mix.2 = (f32[512,512]{1,0:T(8,128)S(1)}, f32[512,512]{1,0:T(8,128)S(1)}) custom-call(f32[512,512]{1,0:T(8,128)S(1)} %bitcast.9, f32[512,512]{1,0:T(8,128)S(1)} %get-tuple-element.75.gram_ref.refs_1_), custom_call_target="tpu_custom_call" | custom-call | flops 1610612736 | bytes 4194304 | tf_op jit(solution)/shard_map/mix/pallas_call | solution.py:129
  52.3 3.9 %collective-permute-start.18 = (f32[8,128]{1,0:T(8,128)S(1)}, f32[8,128]{1,0:T(8,128)S(1)}, u32[]{:S(2)}, u32[]{:S(2)}) collective-permute-start(f32[8,128]{1,0:T(8,128)S(1)} %sum.3.refs_10_), channel_id=1, source_target_pairs={{0,3},{1,2},{2,1},{3,0},{4,7},{5,6},{6,5},{7,4},{8,11},{9,10},{10,... | collective-permute-start | bytes 12296 | tf_op jit(solution)/shard_map/group_norm/ppermute | solution.py:432
  56.9 1.7 %mix.3 = (f32[512,512]{1,0:T(8,128)S(1)}, f32[512,512]{1,0:T(8,128)S(1)}) custom-call(f32[512,512]{1,0:T(8,128)S(1)} %bitcast.12, f32[512,512]{1,0:T(8,128)S(1)} %get-tuple-element.78.gram_ref.refs_6_), custom_call_target="tpu_custom_call" | custom-call | flops 1610612736 | bytes 4194304 | tf_op jit(solution)/shard_map/mix/pallas_call | solution.py:129
  58.6 2.1 %collective-permute-done.19.refs_12_ = f32[8,128]{1,0:T(8,128)S(1)} collective-permute-done((f32[8,128]{1,0:T(8,128)S(1)}, f32[8,128]{1,0:T(8,128)S(1)}, u32[]{:S(2)}, u32[]{:S(2)}) %collective-permute-start.19) | collective-permute-done | bytes 4128 | tf_op jit(solution)/shard_map/group_norm/ppermute | solution.py:432
  60.7 6.0 %update.1 = (f32[512,512]{1,0:T(8,128)S(1)}, f32[256,512]{1,0:T(8,128)S(1)}, f32[256,512]{1,0:T(8,128)S(1)}) custom-call(f32[256,512]{1,0:T(8,128)S(1)} %get-tuple-element.74.upper_ref, f32[256,512]{1,0:T(8,128)S(1)} %get-tuple-element.72.lower_ref, f32[8,128]{1,0:T(8,128)S(1)} %get-tuple-element.73.refs_0_.block_norm_ref, f32[512,512]{1,0:T(8,128)S(1)} %bitcast.10, ...), custom_call_target="tpu_custom_call" | custom-call | flops 4831838208 | bytes 13651968 | tf_op jit(solution)/shard_map/update/pallas_call | solution.py:129
  66.8 1.6 %collective-permute-start.21 = (f32[256,512]{1,0:T(8,128)S(1)}, f32[256,512]{1,0:T(8,128)S(1)}, u32[]{:S(2)}, u32[]{:S(2)}) collective-permute-start(f32[256,512]{1,0:T(8,128)S(1)} %get-tuple-element.82), channel_id=1, source_target_pairs={{0,8},{4,20},{8,0},{12,28},{16,24},{20,4},{24,16},{28,12},{1,9},{5... | collective-permute-start | bytes 1572872 | tf_op jit(solution)/shard_map/link_own/ppermute | solution.py:376
  68.9 7.2 %collective-permute-done.21.refs_2_ = f32[256,512]{1,0:T(8,128)S(1)} collective-permute-done((f32[256,512]{1,0:T(8,128)S(1)}, f32[256,512]{1,0:T(8,128)S(1)}, u32[]{:S(2)}, u32[]{:S(2)}) %collective-permute-start.21) | collective-permute-done | bytes 524320 | tf_op jit(solution)/shard_map/link_own/ppermute | solution.py:376
  76.0 1.5 %collective-permute-start.30 = (f32[512,512]{1,0:T(8,128)S(1)}, f32[512,512]{1,0:T(8,128)S(1)}, u32[]{:S(2)}, u32[]{:S(2)}) collective-permute-start(f32[512,512]{1,0:T(8,128)S(1)} %collective-permute-done.22.refs_1_), channel_id=1, source_target_pairs={{0,8},{4,20},{8,0},{12,28},{16,24},{20,4},{24,16},{28,12},{1,9},{5... | collective-permute-start | bytes 3145736 | tf_op jit(solution)/shard_map/link_sibling/ppermute | solution.py:376
  77.6 4.1 %collective-permute-done.25.refs_3_ = f32[256,512]{1,0:T(8,128)S(1)} collective-permute-done((f32[256,512]{1,0:T(8,128)S(1)}, f32[256,512]{1,0:T(8,128)S(1)}, u32[]{:S(2)}, u32[]{:S(2)}) %collective-permute-start.25) | collective-permute-done | bytes 524320 | tf_op jit(solution)/shard_map/link_own/ppermute | solution.py:376
  81.7 1.5 %collective-permute-start.24 = (f32[256,512]{1,0:T(8,128)S(1)}, f32[256,512]{1,0:T(8,128)S(1)}, u32[]{:S(2)}, u32[]{:S(2)}) collective-permute-start(f32[256,512]{1,0:T(8,128)S(1)} %collective-permute-done.23.refs_4_), channel_id=1, source_target_pairs={{0,8},{4,20},{8,0},{12,28},{16,24},{20,4},{24,16},{28,12},{1,9},{5... | collective-permute-start | bytes 1572872 | tf_op jit(solution)/shard_map/link_relayed/ppermute | solution.py:376
  83.2 9.7 %collective-permute-done.30.refs_0_ = f32[512,512]{1,0:T(8,128)S(1)} collective-permute-done((f32[512,512]{1,0:T(8,128)S(1)}, f32[512,512]{1,0:T(8,128)S(1)}, u32[]{:S(2)}, u32[]{:S(2)}) %collective-permute-start.30) | collective-permute-done | bytes 1048608 | tf_op jit(solution)/shard_map/link_sibling/ppermute | solution.py:376
  92.9 1.5 %collective-permute-start.28 = (f32[256,512]{1,0:T(8,128)S(1)}, f32[256,512]{1,0:T(8,128)S(1)}, u32[]{:S(2)}, u32[]{:S(2)}) collective-permute-start(f32[256,512]{1,0:T(8,128)S(1)} %collective-permute-done.26.refs_5_), channel_id=1, source_target_pairs={{0,8},{4,20},{8,0},{12,28},{16,24},{20,4},{24,16},{28,12},{1,9},{5... | collective-permute-start | bytes 1572872 | tf_op jit(solution)/shard_map/link_relayed/ppermute | solution.py:376
  94.4 2.3 %assemble.3.refs_4_ = f32[512,3072]{1,0:T(8,128)} custom-call(s32[7]{0:T(128)S(1)} %pad_add_fusion.places_ref, f32[512,512]{1,0:T(8,128)S(1)} %get-tuple-element.83.refs_0_, f32[512,512]{1,0:T(8,128)S(1)} %collective-permute-done.22.refs_1_, f32[256,512]{1,0:T(8,128)S(1)} %collective-permute-done.21.refs_2_, f32[256,512]{1,0:T(8,128)S(1)} %collective-permute-done.25.refs_3_, ...), custom_call_target="tpu_custom_call" | custom-call | bytes 12582912 | tf_op jit(solution)/shard_map/assemble/pallas_call | solution.py:347
  96.7 1.8 %collective-permute-done.24.refs_2_ = f32[256,512]{1,0:T(8,128)S(1)} collective-permute-done((f32[256,512]{1,0:T(8,128)S(1)}, f32[256,512]{1,0:T(8,128)S(1)}, u32[]{:S(2)}, u32[]{:S(2)}) %collective-permute-start.24) | collective-permute-done | bytes 524320 | tf_op jit(solution)/shard_map/link_relayed/ppermute | solution.py:376
  98.5 5.6 %collective-permute-done.28.refs_3_ = f32[256,512]{1,0:T(8,128)S(1)} collective-permute-done((f32[256,512]{1,0:T(8,128)S(1)}, f32[256,512]{1,0:T(8,128)S(1)}, u32[]{:S(2)}, u32[]{:S(2)}) %collective-permute-start.28) | collective-permute-done | bytes 524320 | tf_op jit(solution)/shard_map/link_relayed/ppermute | solution.py:376
  104.1 2.2 %assemble.4.refs_2_ = f32[512,3072]{1,0:T(8,128)} custom-call(s32[7]{0:T(128)S(1)} %pad_add_fusion.places_ref, f32[512,512]{1,0:T(8,128)S(1)} %collective-permute-done.30.refs_0_, f32[512,512]{1,0:T(8,128)S(1)} %collective-permute-done.31.refs_1_, f32[256,512]{1,0:T(8,128)S(1)} %collective-permute-done.24.refs_2_, ...), custom_call_target="tpu_custom_call", output_to_operand_aliasing={{}: (5, {})} | custom-call | bytes 8388608 | tf_op jit(solution)/shard_map/assemble/pallas_call | solution.py:347
  (64 shorter events, 8.7 us)
Async XLA Ops:
  3.4 2.3 %collective-permute-start.5 = (f32[256,512]{1,0:T(8,128)S(1)}, f32[256,512]{1,0:T(8,128)S(1)}, u32[]{:S(2)}, u32[]{:S(2)}) collective-permute-start(f32[256,512]{1,0:T(8,128)S(1)} %get-tuple-element.62), channel_id=1, source_target_pairs={{0,4},{4,0},{8,12},{12,8},{16,20},{20,16},{24,28},{28,24},{1,5},{5... | collective-permute-start | bytes 1572872 | tf_op jit(solution)/shard_map/core_corner/ppermute | solution.py:376
  3.9 2.3 %collective-permute-start = (f32[256,512]{1,0:T(8,128)S(1)}, f32[256,512]{1,0:T(8,128)S(1)}, u32[]{:S(2)}, u32[]{:S(2)}) collective-permute-start(f32[256,512]{1,0:T(8,128)S(1)} %get-tuple-element.48), channel_id=1, source_target_pairs={{0,4},{4,0},{8,12},{12,8},{16,20},{20,16},{24,28},{28,24},{1,5},{5... | collective-permute-start | bytes 1572872 | tf_op jit(solution)/shard_map/core_corner/ppermute | solution.py:376
  4.0 5.1 %collective-permute-start.2 = (f32[256,512]{1,0:T(8,128)S(1)}, f32[256,512]{1,0:T(8,128)S(1)}, u32[]{:S(2)}, u32[]{:S(2)}) collective-permute-start(f32[256,512]{1,0:T(8,128)S(1)} %get-tuple-element.53), channel_id=1, source_target_pairs={{0,4},{4,0},{8,12},{12,8},{16,20},{20,16},{24,28},{28,24},{1,5},{5... | collective-permute-start | bytes 1572872 | tf_op jit(solution)/shard_map/core_straight/ppermute | solution.py:376
  5.1 4.7 %collective-permute-start.4 = (f32[256,512]{1,0:T(8,128)S(1)}, f32[256,512]{1,0:T(8,128)S(1)}, u32[]{:S(2)}, u32[]{:S(2)}) collective-permute-start(f32[256,512]{1,0:T(8,128)S(1)} %get-tuple-element.60), channel_id=1, source_target_pairs={{0,4},{4,0},{8,12},{12,8},{16,20},{20,16},{24,28},{28,24},{1,5},{5... | collective-permute-start | bytes 1572872 | tf_op jit(solution)/shard_map/core_side/ppermute | solution.py:376
  5.3 5.4 %collective-permute-start.9 = (f32[256,512]{1,0:T(8,128)S(1)}, f32[256,512]{1,0:T(8,128)S(1)}, u32[]{:S(2)}, u32[]{:S(2)}) collective-permute-start(f32[256,512]{1,0:T(8,128)S(1)} %get-tuple-element.68), channel_id=1, source_target_pairs={{0,4},{4,0},{8,12},{12,8},{16,20},{20,16},{24,28},{28,24},{1,5},{5... | collective-permute-start | bytes 1572872 | tf_op jit(solution)/shard_map/core_straight/ppermute | solution.py:376
  5.7 6.5 %collective-permute-start.11 = (f32[256,512]{1,0:T(8,128)S(1)}, f32[256,512]{1,0:T(8,128)S(1)}, u32[]{:S(2)}, u32[]{:S(2)}) collective-permute-start(f32[256,512]{1,0:T(8,128)S(1)} %get-tuple-element.70), channel_id=1, source_target_pairs={{0,4},{4,0},{8,12},{12,8},{16,20},{20,16},{24,28},{28,24},{1,5},{5... | collective-permute-start | bytes 1572872 | tf_op jit(solution)/shard_map/core_side/ppermute | solution.py:376
  6.2 10.0 %collective-permute-start.6 = (f32[256,512]{1,0:T(8,128)S(1)}, f32[256,512]{1,0:T(8,128)S(1)}, u32[]{:S(2)}, u32[]{:S(2)}) collective-permute-start(f32[256,512]{1,0:T(8,128)S(1)} %add.13), channel_id=1, source_target_pairs={{0,8},{4,20},{8,0},{12,28},{16,24},{20,4},{24,16},{28,12},{1,9},{5... | collective-permute-start | bytes 1572872 | tf_op jit(solution)/shard_map/link_corner/ppermute | solution.py:376
  9.1 12.7 %collective-permute-start.12 = (f32[256,512]{1,0:T(8,128)S(1)}, f32[256,512]{1,0:T(8,128)S(1)}, u32[]{:S(2)}, u32[]{:S(2)}) collective-permute-start(f32[256,512]{1,0:T(8,128)S(1)} %add.10), channel_id=1, source_target_pairs={{0,8},{4,20},{8,0},{12,28},{16,24},{20,4},{24,16},{28,12},{1,9},{5... | collective-permute-start | bytes 1572872 | tf_op jit(solution)/shard_map/link_corner/ppermute | solution.py:376
  9.8 14.2 %collective-permute-start.1 = (f32[256,512]{1,0:T(8,128)S(1)}, f32[256,512]{1,0:T(8,128)S(1)}, u32[]{:S(2)}, u32[]{:S(2)}) collective-permute-start(f32[256,512]{1,0:T(8,128)S(1)} %get-tuple-element.51), channel_id=1, source_target_pairs={{0,4},{4,0},{8,12},{12,8},{16,20},{20,16},{24,28},{28,24},{1,5},{5... | collective-permute-start | bytes 1572872 | tf_op jit(solution)/shard_map/core_self/ppermute | solution.py:376
  10.7 20.1 %collective-permute-start.3 = (f32[256,512]{1,0:T(8,128)S(1)}, f32[256,512]{1,0:T(8,128)S(1)}, u32[]{:S(2)}, u32[]{:S(2)}) collective-permute-start(f32[256,512]{1,0:T(8,128)S(1)} %add.11), channel_id=1, source_target_pairs={{0,8},{4,20},{8,0},{12,28},{16,24},{20,4},{24,16},{28,12},{1,9},{5... | collective-permute-start | bytes 1572872 | tf_op jit(solution)/shard_map/link_straight/ppermute | solution.py:376
  12.2 20.1 %collective-permute-start.8 = (f32[256,512]{1,0:T(8,128)S(1)}, f32[256,512]{1,0:T(8,128)S(1)}, u32[]{:S(2)}, u32[]{:S(2)}) collective-permute-start(f32[256,512]{1,0:T(8,128)S(1)} %get-tuple-element.66), channel_id=1, source_target_pairs={{0,4},{4,0},{8,12},{12,8},{16,20},{20,16},{24,28},{28,24},{1,5},{5... | collective-permute-start | bytes 1572872 | tf_op jit(solution)/shard_map/core_self/ppermute | solution.py:376
  16.2 25.8 %collective-permute-start.10 = (f32[256,512]{1,0:T(8,128)S(1)}, f32[256,512]{1,0:T(8,128)S(1)}, u32[]{:S(2)}, u32[]{:S(2)}) collective-permute-start(f32[256,512]{1,0:T(8,128)S(1)} %add.15), channel_id=1, source_target_pairs={{0,8},{4,20},{8,0},{12,28},{16,24},{20,4},{24,16},{28,12},{1,9},{5... | collective-permute-start | bytes 1572872 | tf_op jit(solution)/shard_map/link_straight/ppermute | solution.py:376
  21.8 20.3 %collective-permute-start.7 = (f32[256,512]{1,0:T(8,128)S(1)}, f32[256,512]{1,0:T(8,128)S(1)}, u32[]{:S(2)}, u32[]{:S(2)}) collective-permute-start(f32[256,512]{1,0:T(8,128)S(1)} %add.14), channel_id=1, source_target_pairs={{0,16},{4,12},{8,24},{12,4},{16,0},{20,28},{24,8},{28,20},{1,17},{... | collective-permute-start | bytes 1572872 | tf_op jit(solution)/shard_map/side_side/ppermute | solution.py:376
  24.0 19.8 %collective-permute-start.13 = (f32[256,512]{1,0:T(8,128)S(1)}, f32[256,512]{1,0:T(8,128)S(1)}, u32[]{:S(2)}, u32[]{:S(2)}) collective-permute-start(f32[256,512]{1,0:T(8,128)S(1)} %add.17), channel_id=1, source_target_pairs={{0,16},{4,12},{8,24},{12,4},{16,0},{20,28},{24,8},{28,20},{1,17},{... | collective-permute-start | bytes 1572872 | tf_op jit(solution)/shard_map/side_side/ppermute | solution.py:376
  44.0 1.2 %collective-permute-start.14 = (f32[8,128]{1,0:T(8,128)S(1)}, f32[8,128]{1,0:T(8,128)S(1)}, u32[]{:S(2)}, u32[]{:S(2)}) collective-permute-start(f32[8,128]{1,0:T(8,128)S(1)} %get-tuple-element.73.refs_0_.block_norm_ref), channel_id=1, source_target_pairs={{0,4},{4,0},{8,12},{12,8},{16,20},{20,16},{24,28},{28,24},{1,5},{5... | collective-permute-start | bytes 12296 | tf_op jit(solution)/shard_map/core_norm/ppermute | solution.py:376
  45.2 6.8 %collective-permute-start.15 = (f32[8,128]{1,0:T(8,128)S(1)}, f32[8,128]{1,0:T(8,128)S(1)}, u32[]{:S(2)}, u32[]{:S(2)}) collective-permute-start(f32[8,128]{1,0:T(8,128)S(1)} %sum.2.refs_0_), channel_id=1, source_target_pairs={{0,24},{4,28},{8,16},{12,20},{16,8},{20,12},{24,0},{28,4},{1,25},{... | collective-permute-start | bytes 12296 | tf_op jit(solution)/shard_map/chip_norm/ppermute | solution.py:376
  48.2 3.8 %collective-permute-start.16 = (f32[8,128]{1,0:T(8,128)S(1)}, f32[8,128]{1,0:T(8,128)S(1)}, u32[]{:S(2)}, u32[]{:S(2)}) collective-permute-start(f32[8,128]{1,0:T(8,128)S(1)} %sum.2.refs_0_), channel_id=1, source_target_pairs={{0,16},{4,20},{8,24},{12,28},{16,0},{20,4},{24,8},{28,12},{1,17},{... | collective-permute-start | bytes 12296 | tf_op jit(solution)/shard_map/chip_norm/ppermute | solution.py:376
  48.7 3.6 %collective-permute-start.17 = (f32[8,128]{1,0:T(8,128)S(1)}, f32[8,128]{1,0:T(8,128)S(1)}, u32[]{:S(2)}, u32[]{:S(2)}) collective-permute-start(f32[8,128]{1,0:T(8,128)S(1)} %sum.2.refs_0_), channel_id=1, source_target_pairs={{0,8},{4,12},{8,0},{12,4},{16,24},{20,28},{24,16},{28,20},{1,9},{5... | collective-permute-start | bytes 12296 | tf_op jit(solution)/shard_map/chip_norm/ppermute | solution.py:376
  52.3 6.3 %collective-permute-start.18 = (f32[8,128]{1,0:T(8,128)S(1)}, f32[8,128]{1,0:T(8,128)S(1)}, u32[]{:S(2)}, u32[]{:S(2)}) collective-permute-start(f32[8,128]{1,0:T(8,128)S(1)} %sum.3.refs_10_), channel_id=1, source_target_pairs={{0,3},{1,2},{2,1},{3,0},{4,7},{5,6},{6,5},{7,4},{8,11},{9,10},{10,... | collective-permute-start | bytes 12296 | tf_op jit(solution)/shard_map/group_norm/ppermute | solution.py:432
  56.2 4.5 %collective-permute-start.19 = (f32[8,128]{1,0:T(8,128)S(1)}, f32[8,128]{1,0:T(8,128)S(1)}, u32[]{:S(2)}, u32[]{:S(2)}) collective-permute-start(f32[8,128]{1,0:T(8,128)S(1)} %sum.3.refs_10_), channel_id=1, source_target_pairs={{0,2},{1,3},{2,0},{3,1},{4,6},{5,7},{6,4},{7,5},{8,10},{9,11},{10,... | collective-permute-start | bytes 12296 | tf_op jit(solution)/shard_map/group_norm/ppermute | solution.py:432
  56.2 4.5 %collective-permute-start.20 = (f32[8,128]{1,0:T(8,128)S(1)}, f32[8,128]{1,0:T(8,128)S(1)}, u32[]{:S(2)}, u32[]{:S(2)}) collective-permute-start(f32[8,128]{1,0:T(8,128)S(1)} %sum.3.refs_10_), channel_id=1, source_target_pairs={{0,1},{1,0},{2,3},{3,2},{4,5},{5,4},{6,7},{7,6},{8,9},{9,8},{10,11... | collective-permute-start | bytes 12296 | tf_op jit(solution)/shard_map/group_norm/ppermute | solution.py:432
  66.7 9.3 %collective-permute-start.22 = (f32[512,512]{1,0:T(8,128)S(1)}, f32[512,512]{1,0:T(8,128)S(1)}, u32[]{:S(2)}, u32[]{:S(2)}) collective-permute-start(f32[512,512]{1,0:T(8,128)S(1)} %get-tuple-element.83.refs_0_), channel_id=1, source_target_pairs={{0,4},{4,0},{8,12},{12,8},{16,20},{20,16},{24,28},{28,24},{1,5},{5... | collective-permute-start | bytes 3145736 | tf_op jit(solution)/shard_map/core_own/ppermute | solution.py:376
  66.8 9.2 %collective-permute-start.21 = (f32[256,512]{1,0:T(8,128)S(1)}, f32[256,512]{1,0:T(8,128)S(1)}, u32[]{:S(2)}, u32[]{:S(2)}) collective-permute-start(f32[256,512]{1,0:T(8,128)S(1)} %get-tuple-element.82), channel_id=1, source_target_pairs={{0,8},{4,20},{8,0},{12,28},{16,24},{20,4},{24,16},{28,12},{1,9},{5... | collective-permute-start | bytes 1572872 | tf_op jit(solution)/shard_map/link_own/ppermute | solution.py:376
  68.4 13.3 %collective-permute-start.25 = (f32[256,512]{1,0:T(8,128)S(1)}, f32[256,512]{1,0:T(8,128)S(1)}, u32[]{:S(2)}, u32[]{:S(2)}) collective-permute-start(f32[256,512]{1,0:T(8,128)S(1)} %get-tuple-element.85), channel_id=1, source_target_pairs={{0,8},{4,20},{8,0},{12,28},{16,24},{20,4},{24,16},{28,12},{1,9},{5... | collective-permute-start | bytes 1572872 | tf_op jit(solution)/shard_map/link_own/ppermute | solution.py:376
  76.0 16.8 %collective-permute-start.30 = (f32[512,512]{1,0:T(8,128)S(1)}, f32[512,512]{1,0:T(8,128)S(1)}, u32[]{:S(2)}, u32[]{:S(2)}) collective-permute-start(f32[512,512]{1,0:T(8,128)S(1)} %collective-permute-done.22.refs_1_), channel_id=1, source_target_pairs={{0,8},{4,20},{8,0},{12,28},{16,24},{20,4},{24,16},{28,12},{1,9},{5... | collective-permute-start | bytes 3145736 | tf_op jit(solution)/shard_map/link_sibling/ppermute | solution.py:376
  77.6 4.1 %collective-permute-start.23 = (f32[256,512]{1,0:T(8,128)S(1)}, f32[256,512]{1,0:T(8,128)S(1)}, u32[]{:S(2)}, u32[]{:S(2)}) collective-permute-start(f32[256,512]{1,0:T(8,128)S(1)} %collective-permute-done.21.refs_2_), channel_id=1, source_target_pairs={{0,4},{4,0},{8,12},{12,8},{16,20},{20,16},{24,28},{28,24},{1,5},{5... | collective-permute-start | bytes 1572872 | tf_op jit(solution)/shard_map/core_first/ppermute | solution.py:376
  81.7 11.2 %collective-permute-start.26 = (f32[256,512]{1,0:T(8,128)S(1)}, f32[256,512]{1,0:T(8,128)S(1)}, u32[]{:S(2)}, u32[]{:S(2)}) collective-permute-start(f32[256,512]{1,0:T(8,128)S(1)} %collective-permute-done.25.refs_3_), channel_id=1, source_target_pairs={{0,4},{4,0},{8,12},{12,8},{16,20},{20,16},{24,28},{28,24},{1,5},{5... | collective-permute-start | bytes 1572872 | tf_op jit(solution)/shard_map/core_first/ppermute | solution.py:376
  81.7 16.8 %collective-permute-start.24 = (f32[256,512]{1,0:T(8,128)S(1)}, f32[256,512]{1,0:T(8,128)S(1)}, u32[]{:S(2)}, u32[]{:S(2)}) collective-permute-start(f32[256,512]{1,0:T(8,128)S(1)} %collective-permute-done.23.refs_4_), channel_id=1, source_target_pairs={{0,8},{4,20},{8,0},{12,28},{16,24},{20,4},{24,16},{28,12},{1,9},{5... | collective-permute-start | bytes 1572872 | tf_op jit(solution)/shard_map/link_relayed/ppermute | solution.py:376
  92.9 11.2 %collective-permute-start.31 = (f32[512,512]{1,0:T(8,128)S(1)}, f32[512,512]{1,0:T(8,128)S(1)}, u32[]{:S(2)}, u32[]{:S(2)}) collective-permute-start(f32[512,512]{1,0:T(8,128)S(1)} %collective-permute-done.30.refs_0_), channel_id=1, source_target_pairs={{0,4},{4,0},{8,12},{12,8},{16,20},{20,16},{24,28},{28,24},{1,5},{5... | collective-permute-start | bytes 3145736 | tf_op jit(solution)/shard_map/core_second/ppermute | solution.py:376
  92.9 11.2 %collective-permute-start.28 = (f32[256,512]{1,0:T(8,128)S(1)}, f32[256,512]{1,0:T(8,128)S(1)}, u32[]{:S(2)}, u32[]{:S(2)}) collective-permute-start(f32[256,512]{1,0:T(8,128)S(1)} %collective-permute-done.26.refs_5_), channel_id=1, source_target_pairs={{0,8},{4,20},{8,0},{12,28},{16,24},{20,4},{24,16},{28,12},{1,9},{5... | collective-permute-start | bytes 1572872 | tf_op jit(solution)/shard_map/link_relayed/ppermute | solution.py:376
  98.5 7.9 %collective-permute-start.27 = (f32[256,512]{1,0:T(8,128)S(1)}, f32[256,512]{1,0:T(8,128)S(1)}, u32[]{:S(2)}, u32[]{:S(2)}) collective-permute-start(f32[256,512]{1,0:T(8,128)S(1)} %collective-permute-done.24.refs_2_), channel_id=1, source_target_pairs={{0,4},{4,0},{8,12},{12,8},{16,20},{20,16},{24,28},{28,24},{1,5},{5... | collective-permute-start | bytes 1572872 | tf_op jit(solution)/shard_map/core_relayed/ppermute | solution.py:376
  104.1 2.3 %collective-permute-start.29 = (f32[256,512]{1,0:T(8,128)S(1)}, f32[256,512]{1,0:T(8,128)S(1)}, u32[]{:S(2)}, u32[]{:S(2)}) collective-permute-start(f32[256,512]{1,0:T(8,128)S(1)} %collective-permute-done.28.refs_3_), channel_id=1, source_target_pairs={{0,4},{4,0},{8,12},{12,8},{16,20},{20,16},{24,28},{28,24},{1,5},{5... | collective-permute-start | bytes 1572872 | tf_op jit(solution)/shard_map/core_relayed/ppermute | solution.py:376
  (4 other events, 51.3 us)

commit v16 on v15

--- a/solution.py
+++ b/solution.py
@@ -443,9 +443,9 @@
     held += [(("straight", 0, half), first[half]) for half in HALVES]
     held += [(("straight", 1, half), core_first[half]) for half in HALVES]
     crossed = [(("cross", 0, None), second), (("cross", 1, None), core_second)]
-    result = assemble(None, *held)
+    result = assemble(None, *held, crossed[0])
     core_relayed = [to_core(after(relayed[0], result), "relayed"), to_core(relayed[1], "relayed")]
-    result = assemble(result, *crossed, *[(("diagonal", 0, half), relayed[half]) for half in HALVES])
+    result = assemble(result, crossed[1], *[(("diagonal", 0, half), relayed[half]) for half in HALVES])
     return assemble(result, *[(("diagonal", 1, half), core_relayed[half]) for half in HALVES])
 
 

time: 108 us -> 108 us (level)
  no operation moved by 1% of the time
where the time goes in v16:
time: 108 us; the launch traced here: 107 us
  waiting for transfers between devices  56.6 us (52%)
  starting transfers between devices  26.4 us (24%)
  Pallas kernels  20.7 us (19%)
  local copies, waits for them, and re-layouts  1.9 us (2%)
    ppermute x29, waiting for transfers between devices, over(): return lax.ppermute(value, 'dp', pairs)  54.4 us
    ppermute x29, starting transfers between devices, over(): return lax.ppermute(value, 'dp', pairs)  21.9 us
    pallas_call x20, Pallas kernels, local_call(): pl.pallas_call(kernel, in_specs=[pl.BlockSpec(memory_space=pltpu.SMEM)] *...  15.6 us
    pallas_call x3, Pallas kernels, assemble_call(): pl.pallas_call(kernel, in_specs=in_specs, out_specs=pl.BlockSpec(memory_s...  5.09 us
    ppermute x3, starting transfers between devices, paired_body(): norms.append(lax.ppermute(norm, 'mp', pairs))  4.54 us
  transfers between devices with their start and end apart: 32, of which 14 were waited for; matrix products, arithmetic and copies ran while one was open for 0% of the time, Pallas kernels for 12%

profile of v16, /device:TPU:0, one launch (start us, length us, event | category | flops | bytes accessed | tf_op | source)
XLA Modules:
  0.0 106.7 jit_solution(3768618207669043371)
XLA Ops:
  0.7 1.9 %copy-done = bf16[1,512,3072]{2,1,0:T(8,128)(2,1)S(1)} copy-done((bf16[1,512,3072]{2,1,0:T(8,128)(2,1)S(1)}, bf16[1,512,3072]{2,1,0:T(8,128)(2,1)}, u32[]{:S(2)}) %copy-start) | copy-done | bytes 3145752
  2.6 0.8 pack.3
  6.2 2.9 %collective-permute-start.6 = (f32[256,512]{1,0:T(8,128)S(1)}, f32[256,512]{1,0:T(8,128)S(1)}, u32[]{:S(2)}, u32[]{:S(2)}) collective-permute-start(f32[256,512]{1,0:T(8,128)S(1)} %add.13), channel_id=1, source_target_pairs={{0,8},{4,20},{8,0},{12,28},{16,24},{20,4},{24,16},{28,12},{1,9},{5... | collective-permute-start | bytes 1572872 | tf_op jit(solution)/shard_map/link_corner/ppermute | solution.py:376
  9.8 0.8 pack.4
  10.7 1.5 %collective-permute-start.3 = (f32[256,512]{1,0:T(8,128)S(1)}, f32[256,512]{1,0:T(8,128)S(1)}, u32[]{:S(2)}, u32[]{:S(2)}) collective-permute-start(f32[256,512]{1,0:T(8,128)S(1)} %add.11), channel_id=1, source_target_pairs={{0,8},{4,20},{8,0},{12,28},{16,24},{20,4},{24,16},{28,12},{1,9},{5... | collective-permute-start | bytes 1572872 | tf_op jit(solution)/shard_map/link_straight/ppermute | solution.py:376
  12.6 3.6 %collective-permute-done.6.refs_2_ = f32[256,512]{1,0:T(8,128)S(1)} collective-permute-done((f32[256,512]{1,0:T(8,128)S(1)}, f32[256,512]{1,0:T(8,128)S(1)}, u32[]{:S(2)}, u32[]{:S(2)}) %collective-permute-start.6) | collective-permute-done | bytes 524320 | tf_op jit(solution)/shard_map/link_corner/ppermute | solution.py:376
  16.2 2.0 %collective-permute-start.10 = (f32[256,512]{1,0:T(8,128)S(1)}, f32[256,512]{1,0:T(8,128)S(1)}, u32[]{:S(2)}, u32[]{:S(2)}) collective-permute-start(f32[256,512]{1,0:T(8,128)S(1)} %add.15), channel_id=1, source_target_pairs={{0,8},{4,20},{8,0},{12,28},{16,24},{20,4},{24,16},{28,12},{1,9},{5... | collective-permute-start | bytes 1572872 | tf_op jit(solution)/shard_map/link_straight/ppermute | solution.py:376
  18.3 3.5 %collective-permute-done.12.refs_2_ = f32[256,512]{1,0:T(8,128)S(1)} collective-permute-done((f32[256,512]{1,0:T(8,128)S(1)}, f32[256,512]{1,0:T(8,128)S(1)}, u32[]{:S(2)}, u32[]{:S(2)}) %collective-permute-start.12) | collective-permute-done | bytes 524320 | tf_op jit(solution)/shard_map/link_corner/ppermute | solution.py:376
  21.8 2.1 %collective-permute-start.7 = (f32[256,512]{1,0:T(8,128)S(1)}, f32[256,512]{1,0:T(8,128)S(1)}, u32[]{:S(2)}, u32[]{:S(2)}) collective-permute-start(f32[256,512]{1,0:T(8,128)S(1)} %add.14), channel_id=1, source_target_pairs={{0,16},{4,12},{8,24},{12,4},{16,0},{20,28},{24,8},{28,20},{1,17},{... | collective-permute-start | bytes 1572872 | tf_op jit(solution)/shard_map/side_side/ppermute | solution.py:376
  24.1 6.7 %collective-permute-done.3.refs_2_ = f32[256,512]{1,0:T(8,128)S(1)} collective-permute-done((f32[256,512]{1,0:T(8,128)S(1)}, f32[256,512]{1,0:T(8,128)S(1)}, u32[]{:S(2)}, u32[]{:S(2)}) %collective-permute-start.3) | collective-permute-done | bytes 524320 | tf_op jit(solution)/shard_map/link_straight/ppermute | solution.py:376
  30.9 1.5 %square.1 = (f32[512,512]{1,0:T(8,128)S(1)}, f32[512,512]{1,0:T(8,128)S(1)}) custom-call(f32[512,512]{1,0:T(8,128)S(1)} %bitcast.8, f32[512,512]{1,0:T(8,128)S(1)} %bitcast.11), custom_call_target="tpu_custom_call" | custom-call | flops 1610612736 | bytes 4194304 | tf_op jit(solution)/shard_map/square/pallas_call | solution.py:129
  32.4 9.7 %collective-permute-done.10.refs_2_ = f32[256,512]{1,0:T(8,128)S(1)} collective-permute-done((f32[256,512]{1,0:T(8,128)S(1)}, f32[256,512]{1,0:T(8,128)S(1)}, u32[]{:S(2)}, u32[]{:S(2)}) %collective-permute-start.10) | collective-permute-done | bytes 524320 | tf_op jit(solution)/shard_map/link_straight/ppermute | solution.py:376
  42.3 1.4 %collective-permute-done.13.arrival_ref = f32[256,512]{1,0:T(8,128)S(1)} collective-permute-done((f32[256,512]{1,0:T(8,128)S(1)}, f32[256,512]{1,0:T(8,128)S(1)}, u32[]{:S(2)}, u32[]{:S(2)}) %collective-permute-start.13) | collective-permute-done | bytes 524320 | tf_op jit(solution)/shard_map/side_side/ppermute | solution.py:376
  44.4 0.8 collective-permute-done.14.refs_1_
  45.2 3.0 %collective-permute-start.15 = (f32[8,128]{1,0:T(8,128)S(1)}, f32[8,128]{1,0:T(8,128)S(1)}, u32[]{:S(2)}, u32[]{:S(2)}) collective-permute-start(f32[8,128]{1,0:T(8,128)S(1)} %sum.2.refs_0_), channel_id=1, source_target_pairs={{0,24},{4,28},{8,16},{12,20},{16,8},{20,12},{24,0},{28,4},{1,25},{... | collective-permute-start | bytes 12296 | tf_op jit(solution)/shard_map/chip_norm/ppermute | solution.py:376
  48.8 1.5 %gram.1 = (f32[512,512]{1,0:T(8,128)S(1)}, f32[512,512]{1,0:T(8,128)S(1)}) custom-call(f32[256,512]{1,0:T(8,128)S(1)} %get-tuple-element.74.upper_ref, f32[256,512]{1,0:T(8,128)S(1)} %get-tuple-element.72.lower_ref), custom_call_target="tpu_custom_call" | custom-call | flops 1610612736 | bytes 3145728 | tf_op jit(solution)/shard_map/gram/pallas_call | solution.py:129
  50.3 1.7 %mix.2 = (f32[512,512]{1,0:T(8,128)S(1)}, f32[512,512]{1,0:T(8,128)S(1)}) custom-call(f32[512,512]{1,0:T(8,128)S(1)} %bitcast.9, f32[512,512]{1,0:T(8,128)S(1)} %get-tuple-element.75.gram_ref.refs_1_), custom_call_target="tpu_custom_call" | custom-call | flops 1610612736 | bytes 4194304 | tf_op jit(solution)/shard_map/mix/pallas_call | solution.py:129
  52.3 3.9 %collective-permute-start.18 = (f32[8,128]{1,0:T(8,128)S(1)}, f32[8,128]{1,0:T(8,128)S(1)}, u32[]{:S(2)}, u32[]{:S(2)}) collective-permute-start(f32[8,128]{1,0:T(8,128)S(1)} %sum.3.refs_10_), channel_id=1, source_target_pairs={{0,3},{1,2},{2,1},{3,0},{4,7},{5,6},{6,5},{7,4},{8,11},{9,10},{10,... | collective-permute-start | bytes 12296 | tf_op jit(solution)/shard_map/group_norm/ppermute | solution.py:432
  56.9 1.7 %mix.3 = (f32[512,512]{1,0:T(8,128)S(1)}, f32[512,512]{1,0:T(8,128)S(1)}) custom-call(f32[512,512]{1,0:T(8,128)S(1)} %bitcast.12, f32[512,512]{1,0:T(8,128)S(1)} %get-tuple-element.78.gram_ref.refs_6_), custom_call_target="tpu_custom_call" | custom-call | flops 1610612736 | bytes 4194304 | tf_op jit(solution)/shard_map/mix/pallas_call | solution.py:129
  58.6 2.1 %collective-permute-done.19.refs_12_ = f32[8,128]{1,0:T(8,128)S(1)} collective-permute-done((f32[8,128]{1,0:T(8,128)S(1)}, f32[8,128]{1,0:T(8,128)S(1)}, u32[]{:S(2)}, u32[]{:S(2)}) %collective-permute-start.19) | collective-permute-done | bytes 4128 | tf_op jit(solution)/shard_map/group_norm/ppermute | solution.py:432
  60.7 6.0 %update.1 = (f32[512,512]{1,0:T(8,128)S(1)}, f32[256,512]{1,0:T(8,128)S(1)}, f32[256,512]{1,0:T(8,128)S(1)}) custom-call(f32[256,512]{1,0:T(8,128)S(1)} %get-tuple-element.74.upper_ref, f32[256,512]{1,0:T(8,128)S(1)} %get-tuple-element.72.lower_ref, f32[8,128]{1,0:T(8,128)S(1)} %get-tuple-element.73.refs_0_.block_norm_ref, f32[512,512]{1,0:T(8,128)S(1)} %bitcast.10, ...), custom_call_target="tpu_custom_call" | custom-call | flops 4831838208 | bytes 13651968 | tf_op jit(solution)/shard_map/update/pallas_call | solution.py:129
  66.8 1.6 %collective-permute-start.21 = (f32[256,512]{1,0:T(8,128)S(1)}, f32[256,512]{1,0:T(8,128)S(1)}, u32[]{:S(2)}, u32[]{:S(2)}) collective-permute-start(f32[256,512]{1,0:T(8,128)S(1)} %get-tuple-element.82), channel_id=1, source_target_pairs={{0,8},{4,20},{8,0},{12,28},{16,24},{20,4},{24,16},{28,12},{1,9},{5... | collective-permute-start | bytes 1572872 | tf_op jit(solution)/shard_map/link_own/ppermute | solution.py:376
  68.9 7.2 %collective-permute-done.21.refs_2_ = f32[256,512]{1,0:T(8,128)S(1)} collective-permute-done((f32[256,512]{1,0:T(8,128)S(1)}, f32[256,512]{1,0:T(8,128)S(1)}, u32[]{:S(2)}, u32[]{:S(2)}) %collective-permute-start.21) | collective-permute-done | bytes 524320 | tf_op jit(solution)/shard_map/link_own/ppermute | solution.py:376
  76.0 1.5 %collective-permute-start.27 = (f32[512,512]{1,0:T(8,128)S(1)}, f32[512,512]{1,0:T(8,128)S(1)}, u32[]{:S(2)}, u32[]{:S(2)}) collective-permute-start(f32[512,512]{1,0:T(8,128)S(1)} %collective-permute-done.22.refs_1_), channel_id=1, source_target_pairs={{0,8},{4,20},{8,0},{12,28},{16,24},{20,4},{24,16},{28,12},{1,9},{5... | collective-permute-start | bytes 3145736 | tf_op jit(solution)/shard_map/link_sibling/ppermute | solution.py:376
  77.6 4.1 %collective-permute-done.25.refs_3_ = f32[256,512]{1,0:T(8,128)S(1)} collective-permute-done((f32[256,512]{1,0:T(8,128)S(1)}, f32[256,512]{1,0:T(8,128)S(1)}, u32[]{:S(2)}, u32[]{:S(2)}) %collective-permute-start.25) | collective-permute-done | bytes 524320 | tf_op jit(solution)/shard_map/link_own/ppermute | solution.py:376
  81.7 1.5 %collective-permute-start.24 = (f32[256,512]{1,0:T(8,128)S(1)}, f32[256,512]{1,0:T(8,128)S(1)}, u32[]{:S(2)}, u32[]{:S(2)}) collective-permute-start(f32[256,512]{1,0:T(8,128)S(1)} %collective-permute-done.23.refs_4_), channel_id=1, source_target_pairs={{0,8},{4,20},{8,0},{12,28},{16,24},{20,4},{24,16},{28,12},{1,9},{5... | collective-permute-start | bytes 1572872 | tf_op jit(solution)/shard_map/link_relayed/ppermute | solution.py:376
  83.2 9.7 %collective-permute-done.27.refs_6_ = f32[512,512]{1,0:T(8,128)S(1)} collective-permute-done((f32[512,512]{1,0:T(8,128)S(1)}, f32[512,512]{1,0:T(8,128)S(1)}, u32[]{:S(2)}, u32[]{:S(2)}) %collective-permute-start.27) | collective-permute-done | bytes 1048608 | tf_op jit(solution)/shard_map/link_sibling/ppermute | solution.py:376
  92.9 1.5 %collective-permute-start.29 = (f32[256,512]{1,0:T(8,128)S(1)}, f32[256,512]{1,0:T(8,128)S(1)}, u32[]{:S(2)}, u32[]{:S(2)}) collective-permute-start(f32[256,512]{1,0:T(8,128)S(1)} %collective-permute-done.26.refs_5_), channel_id=1, source_target_pairs={{0,8},{4,20},{8,0},{12,28},{16,24},{20,4},{24,16},{28,12},{1,9},{5... | collective-permute-start | bytes 1572872 | tf_op jit(solution)/shard_map/link_relayed/ppermute | solution.py:376
  94.4 2.6 %assemble.3.refs_3_ = f32[512,3072]{1,0:T(8,128)} custom-call(s32[7]{0:T(128)S(1)} %pad_add_fusion.places_ref, f32[512,512]{1,0:T(8,128)S(1)} %get-tuple-element.83.refs_0_, f32[512,512]{1,0:T(8,128)S(1)} %collective-permute-done.22.refs_1_, f32[256,512]{1,0:T(8,128)S(1)} %collective-permute-done.21.refs_2_, f32[256,512]{1,0:T(8,128)S(1)} %collective-permute-done.25.refs_3_, ...), custom_call_target="tpu_custom_call" | custom-call | bytes 14680064 | tf_op jit(solution)/shard_map/assemble/pallas_call | solution.py:347
  97.0 1.5 %collective-permute-done.24.refs_1_ = f32[256,512]{1,0:T(8,128)S(1)} collective-permute-done((f32[256,512]{1,0:T(8,128)S(1)}, f32[256,512]{1,0:T(8,128)S(1)}, u32[]{:S(2)}, u32[]{:S(2)}) %collective-permute-start.24) | collective-permute-done | bytes 524320 | tf_op jit(solution)/shard_map/link_relayed/ppermute | solution.py:376
  98.5 5.6 %collective-permute-done.29.refs_2_ = f32[256,512]{1,0:T(8,128)S(1)} collective-permute-done((f32[256,512]{1,0:T(8,128)S(1)}, f32[256,512]{1,0:T(8,128)S(1)}, u32[]{:S(2)}, u32[]{:S(2)}) %collective-permute-start.29) | collective-permute-done | bytes 524320 | tf_op jit(solution)/shard_map/link_relayed/ppermute | solution.py:376
  104.1 1.9 %assemble.4.refs_2_ = f32[512,3072]{1,0:T(8,128)} custom-call(s32[7]{0:T(128)S(1)} %pad_add_fusion.places_ref, f32[512,512]{1,0:T(8,128)S(1)} %collective-permute-done.31.refs_0_, f32[256,512]{1,0:T(8,128)S(1)} %collective-permute-done.24.refs_1_, f32[256,512]{1,0:T(8,128)S(1)} %collective-permute-done.29.refs_2_, ...), custom_call_target="tpu_custom_call", output_to_operand_aliasing={{}: (4, {})} | custom-call | bytes 6291456 | tf_op jit(solution)/shard_map/assemble/pallas_call | solution.py:347
  (64 shorter events, 8.7 us)
Async XLA Ops:
  3.4 2.3 %collective-permute-start.5 = (f32[256,512]{1,0:T(8,128)S(1)}, f32[256,512]{1,0:T(8,128)S(1)}, u32[]{:S(2)}, u32[]{:S(2)}) collective-permute-start(f32[256,512]{1,0:T(8,128)S(1)} %get-tuple-element.62), channel_id=1, source_target_pairs={{0,4},{4,0},{8,12},{12,8},{16,20},{20,16},{24,28},{28,24},{1,5},{5... | collective-permute-start | bytes 1572872 | tf_op jit(solution)/shard_map/core_corner/ppermute | solution.py:376
  3.9 2.3 %collective-permute-start = (f32[256,512]{1,0:T(8,128)S(1)}, f32[256,512]{1,0:T(8,128)S(1)}, u32[]{:S(2)}, u32[]{:S(2)}) collective-permute-start(f32[256,512]{1,0:T(8,128)S(1)} %get-tuple-element.48), channel_id=1, source_target_pairs={{0,4},{4,0},{8,12},{12,8},{16,20},{20,16},{24,28},{28,24},{1,5},{5... | collective-permute-start | bytes 1572872 | tf_op jit(solution)/shard_map/core_corner/ppermute | solution.py:376
  4.0 5.1 %collective-permute-start.2 = (f32[256,512]{1,0:T(8,128)S(1)}, f32[256,512]{1,0:T(8,128)S(1)}, u32[]{:S(2)}, u32[]{:S(2)}) collective-permute-start(f32[256,512]{1,0:T(8,128)S(1)} %get-tuple-element.53), channel_id=1, source_target_pairs={{0,4},{4,0},{8,12},{12,8},{16,20},{20,16},{24,28},{28,24},{1,5},{5... | collective-permute-start | bytes 1572872 | tf_op jit(solution)/shard_map/core_straight/ppermute | solution.py:376
  5.1 4.7 %collective-permute-start.4 = (f32[256,512]{1,0:T(8,128)S(1)}, f32[256,512]{1,0:T(8,128)S(1)}, u32[]{:S(2)}, u32[]{:S(2)}) collective-permute-start(f32[256,512]{1,0:T(8,128)S(1)} %get-tuple-element.60), channel_id=1, source_target_pairs={{0,4},{4,0},{8,12},{12,8},{16,20},{20,16},{24,28},{28,24},{1,5},{5... | collective-permute-start | bytes 1572872 | tf_op jit(solution)/shard_map/core_side/ppermute | solution.py:376
  5.3 5.4 %collective-permute-start.9 = (f32[256,512]{1,0:T(8,128)S(1)}, f32[256,512]{1,0:T(8,128)S(1)}, u32[]{:S(2)}, u32[]{:S(2)}) collective-permute-start(f32[256,512]{1,0:T(8,128)S(1)} %get-tuple-element.68), channel_id=1, source_target_pairs={{0,4},{4,0},{8,12},{12,8},{16,20},{20,16},{24,28},{28,24},{1,5},{5... | collective-permute-start | bytes 1572872 | tf_op jit(solution)/shard_map/core_straight/ppermute | solution.py:376
  5.7 6.5 %collective-permute-start.11 = (f32[256,512]{1,0:T(8,128)S(1)}, f32[256,512]{1,0:T(8,128)S(1)}, u32[]{:S(2)}, u32[]{:S(2)}) collective-permute-start(f32[256,512]{1,0:T(8,128)S(1)} %get-tuple-element.70), channel_id=1, source_target_pairs={{0,4},{4,0},{8,12},{12,8},{16,20},{20,16},{24,28},{28,24},{1,5},{5... | collective-permute-start | bytes 1572872 | tf_op jit(solution)/shard_map/core_side/ppermute | solution.py:376
  6.2 10.0 %collective-permute-start.6 = (f32[256,512]{1,0:T(8,128)S(1)}, f32[256,512]{1,0:T(8,128)S(1)}, u32[]{:S(2)}, u32[]{:S(2)}) collective-permute-start(f32[256,512]{1,0:T(8,128)S(1)} %add.13), channel_id=1, source_target_pairs={{0,8},{4,20},{8,0},{12,28},{16,24},{20,4},{24,16},{28,12},{1,9},{5... | collective-permute-start | bytes 1572872 | tf_op jit(solution)/shard_map/link_corner/ppermute | solution.py:376
  9.1 12.7 %collective-permute-start.12 = (f32[256,512]{1,0:T(8,128)S(1)}, f32[256,512]{1,0:T(8,128)S(1)}, u32[]{:S(2)}, u32[]{:S(2)}) collective-permute-start(f32[256,512]{1,0:T(8,128)S(1)} %add.10), channel_id=1, source_target_pairs={{0,8},{4,20},{8,0},{12,28},{16,24},{20,4},{24,16},{28,12},{1,9},{5... | collective-permute-start | bytes 1572872 | tf_op jit(solution)/shard_map/link_corner/ppermute | solution.py:376
  9.8 14.2 %collective-permute-start.1 = (f32[256,512]{1,0:T(8,128)S(1)}, f32[256,512]{1,0:T(8,128)S(1)}, u32[]{:S(2)}, u32[]{:S(2)}) collective-permute-start(f32[256,512]{1,0:T(8,128)S(1)} %get-tuple-element.51), channel_id=1, source_target_pairs={{0,4},{4,0},{8,12},{12,8},{16,20},{20,16},{24,28},{28,24},{1,5},{5... | collective-permute-start | bytes 1572872 | tf_op jit(solution)/shard_map/core_self/ppermute | solution.py:376
  10.7 20.1 %collective-permute-start.3 = (f32[256,512]{1,0:T(8,128)S(1)}, f32[256,512]{1,0:T(8,128)S(1)}, u32[]{:S(2)}, u32[]{:S(2)}) collective-permute-start(f32[256,512]{1,0:T(8,128)S(1)} %add.11), channel_id=1, source_target_pairs={{0,8},{4,20},{8,0},{12,28},{16,24},{20,4},{24,16},{28,12},{1,9},{5... | collective-permute-start | bytes 1572872 | tf_op jit(solution)/shard_map/link_straight/ppermute | solution.py:376
  12.2 20.1 %collective-permute-start.8 = (f32[256,512]{1,0:T(8,128)S(1)}, f32[256,512]{1,0:T(8,128)S(1)}, u32[]{:S(2)}, u32[]{:S(2)}) collective-permute-start(f32[256,512]{1,0:T(8,128)S(1)} %get-tuple-element.66), channel_id=1, source_target_pairs={{0,4},{4,0},{8,12},{12,8},{16,20},{20,16},{24,28},{28,24},{1,5},{5... | collective-permute-start | bytes 1572872 | tf_op jit(solution)/shard_map/core_self/ppermute | solution.py:376
  16.2 25.8 %collective-permute-start.10 = (f32[256,512]{1,0:T(8,128)S(1)}, f32[256,512]{1,0:T(8,128)S(1)}, u32[]{:S(2)}, u32[]{:S(2)}) collective-permute-start(f32[256,512]{1,0:T(8,128)S(1)} %add.15), channel_id=1, source_target_pairs={{0,8},{4,20},{8,0},{12,28},{16,24},{20,4},{24,16},{28,12},{1,9},{5... | collective-permute-start | bytes 1572872 | tf_op jit(solution)/shard_map/link_straight/ppermute | solution.py:376
  21.8 20.3 %collective-permute-start.7 = (f32[256,512]{1,0:T(8,128)S(1)}, f32[256,512]{1,0:T(8,128)S(1)}, u32[]{:S(2)}, u32[]{:S(2)}) collective-permute-start(f32[256,512]{1,0:T(8,128)S(1)} %add.14), channel_id=1, source_target_pairs={{0,16},{4,12},{8,24},{12,4},{16,0},{20,28},{24,8},{28,20},{1,17},{... | collective-permute-start | bytes 1572872 | tf_op jit(solution)/shard_map/side_side/ppermute | solution.py:376
  24.0 19.8 %collective-permute-start.13 = (f32[256,512]{1,0:T(8,128)S(1)}, f32[256,512]{1,0:T(8,128)S(1)}, u32[]{:S(2)}, u32[]{:S(2)}) collective-permute-start(f32[256,512]{1,0:T(8,128)S(1)} %add.17), channel_id=1, source_target_pairs={{0,16},{4,12},{8,24},{12,4},{16,0},{20,28},{24,8},{28,20},{1,17},{... | collective-permute-start | bytes 1572872 | tf_op jit(solution)/shard_map/side_side/ppermute | solution.py:376
  44.0 1.2 %collective-permute-start.14 = (f32[8,128]{1,0:T(8,128)S(1)}, f32[8,128]{1,0:T(8,128)S(1)}, u32[]{:S(2)}, u32[]{:S(2)}) collective-permute-start(f32[8,128]{1,0:T(8,128)S(1)} %get-tuple-element.73.refs_0_.block_norm_ref), channel_id=1, source_target_pairs={{0,4},{4,0},{8,12},{12,8},{16,20},{20,16},{24,28},{28,24},{1,5},{5... | collective-permute-start | bytes 12296 | tf_op jit(solution)/shard_map/core_norm/ppermute | solution.py:376
  45.2 6.8 %collective-permute-start.15 = (f32[8,128]{1,0:T(8,128)S(1)}, f32[8,128]{1,0:T(8,128)S(1)}, u32[]{:S(2)}, u32[]{:S(2)}) collective-permute-start(f32[8,128]{1,0:T(8,128)S(1)} %sum.2.refs_0_), channel_id=1, source_target_pairs={{0,24},{4,28},{8,16},{12,20},{16,8},{20,12},{24,0},{28,4},{1,25},{... | collective-permute-start | bytes 12296 | tf_op jit(solution)/shard_map/chip_norm/ppermute | solution.py:376
  48.2 3.8 %collective-permute-start.16 = (f32[8,128]{1,0:T(8,128)S(1)}, f32[8,128]{1,0:T(8,128)S(1)}, u32[]{:S(2)}, u32[]{:S(2)}) collective-permute-start(f32[8,128]{1,0:T(8,128)S(1)} %sum.2.refs_0_), channel_id=1, source_target_pairs={{0,16},{4,20},{8,24},{12,28},{16,0},{20,4},{24,8},{28,12},{1,17},{... | collective-permute-start | bytes 12296 | tf_op jit(solution)/shard_map/chip_norm/ppermute | solution.py:376
  48.7 3.6 %collective-permute-start.17 = (f32[8,128]{1,0:T(8,128)S(1)}, f32[8,128]{1,0:T(8,128)S(1)}, u32[]{:S(2)}, u32[]{:S(2)}) collective-permute-start(f32[8,128]{1,0:T(8,128)S(1)} %sum.2.refs_0_), channel_id=1, source_target_pairs={{0,8},{4,12},{8,0},{12,4},{16,24},{20,28},{24,16},{28,20},{1,9},{5... | collective-permute-start | bytes 12296 | tf_op jit(solution)/shard_map/chip_norm/ppermute | solution.py:376
  52.3 6.3 %collective-permute-start.18 = (f32[8,128]{1,0:T(8,128)S(1)}, f32[8,128]{1,0:T(8,128)S(1)}, u32[]{:S(2)}, u32[]{:S(2)}) collective-permute-start(f32[8,128]{1,0:T(8,128)S(1)} %sum.3.refs_10_), channel_id=1, source_target_pairs={{0,3},{1,2},{2,1},{3,0},{4,7},{5,6},{6,5},{7,4},{8,11},{9,10},{10,... | collective-permute-start | bytes 12296 | tf_op jit(solution)/shard_map/group_norm/ppermute | solution.py:432
  56.2 4.5 %collective-permute-start.19 = (f32[8,128]{1,0:T(8,128)S(1)}, f32[8,128]{1,0:T(8,128)S(1)}, u32[]{:S(2)}, u32[]{:S(2)}) collective-permute-start(f32[8,128]{1,0:T(8,128)S(1)} %sum.3.refs_10_), channel_id=1, source_target_pairs={{0,2},{1,3},{2,0},{3,1},{4,6},{5,7},{6,4},{7,5},{8,10},{9,11},{10,... | collective-permute-start | bytes 12296 | tf_op jit(solution)/shard_map/group_norm/ppermute | solution.py:432
  56.2 4.5 %collective-permute-start.20 = (f32[8,128]{1,0:T(8,128)S(1)}, f32[8,128]{1,0:T(8,128)S(1)}, u32[]{:S(2)}, u32[]{:S(2)}) collective-permute-start(f32[8,128]{1,0:T(8,128)S(1)} %sum.3.refs_10_), channel_id=1, source_target_pairs={{0,1},{1,0},{2,3},{3,2},{4,5},{5,4},{6,7},{7,6},{8,9},{9,8},{10,11... | collective-permute-start | bytes 12296 | tf_op jit(solution)/shard_map/group_norm/ppermute | solution.py:432
  66.7 9.3 %collective-permute-start.22 = (f32[512,512]{1,0:T(8,128)S(1)}, f32[512,512]{1,0:T(8,128)S(1)}, u32[]{:S(2)}, u32[]{:S(2)}) collective-permute-start(f32[512,512]{1,0:T(8,128)S(1)} %get-tuple-element.83.refs_0_), channel_id=1, source_target_pairs={{0,4},{4,0},{8,12},{12,8},{16,20},{20,16},{24,28},{28,24},{1,5},{5... | collective-permute-start | bytes 3145736 | tf_op jit(solution)/shard_map/core_own/ppermute | solution.py:376
  66.8 9.2 %collective-permute-start.21 = (f32[256,512]{1,0:T(8,128)S(1)}, f32[256,512]{1,0:T(8,128)S(1)}, u32[]{:S(2)}, u32[]{:S(2)}) collective-permute-start(f32[256,512]{1,0:T(8,128)S(1)} %get-tuple-element.82), channel_id=1, source_target_pairs={{0,8},{4,20},{8,0},{12,28},{16,24},{20,4},{24,16},{28,12},{1,9},{5... | collective-permute-start | bytes 1572872 | tf_op jit(solution)/shard_map/link_own/ppermute | solution.py:376
  68.4 13.3 %collective-permute-start.25 = (f32[256,512]{1,0:T(8,128)S(1)}, f32[256,512]{1,0:T(8,128)S(1)}, u32[]{:S(2)}, u32[]{:S(2)}) collective-permute-start(f32[256,512]{1,0:T(8,128)S(1)} %get-tuple-element.85), channel_id=1, source_target_pairs={{0,8},{4,20},{8,0},{12,28},{16,24},{20,4},{24,16},{28,12},{1,9},{5... | collective-permute-start | bytes 1572872 | tf_op jit(solution)/shard_map/link_own/ppermute | solution.py:376
  76.0 16.8 %collective-permute-start.27 = (f32[512,512]{1,0:T(8,128)S(1)}, f32[512,512]{1,0:T(8,128)S(1)}, u32[]{:S(2)}, u32[]{:S(2)}) collective-permute-start(f32[512,512]{1,0:T(8,128)S(1)} %collective-permute-done.22.refs_1_), channel_id=1, source_target_pairs={{0,8},{4,20},{8,0},{12,28},{16,24},{20,4},{24,16},{28,12},{1,9},{5... | collective-permute-start | bytes 3145736 | tf_op jit(solution)/shard_map/link_sibling/ppermute | solution.py:376
  77.6 4.1 %collective-permute-start.23 = (f32[256,512]{1,0:T(8,128)S(1)}, f32[256,512]{1,0:T(8,128)S(1)}, u32[]{:S(2)}, u32[]{:S(2)}) collective-permute-start(f32[256,512]{1,0:T(8,128)S(1)} %collective-permute-done.21.refs_2_), channel_id=1, source_target_pairs={{0,4},{4,0},{8,12},{12,8},{16,20},{20,16},{24,28},{28,24},{1,5},{5... | collective-permute-start | bytes 1572872 | tf_op jit(solution)/shard_map/core_first/ppermute | solution.py:376
  81.7 11.2 %collective-permute-start.26 = (f32[256,512]{1,0:T(8,128)S(1)}, f32[256,512]{1,0:T(8,128)S(1)}, u32[]{:S(2)}, u32[]{:S(2)}) collective-permute-start(f32[256,512]{1,0:T(8,128)S(1)} %collective-permute-done.25.refs_3_), channel_id=1, source_target_pairs={{0,4},{4,0},{8,12},{12,8},{16,20},{20,16},{24,28},{28,24},{1,5},{5... | collective-permute-start | bytes 1572872 | tf_op jit(solution)/shard_map/core_first/ppermute | solution.py:376
  81.7 16.8 %collective-permute-start.24 = (f32[256,512]{1,0:T(8,128)S(1)}, f32[256,512]{1,0:T(8,128)S(1)}, u32[]{:S(2)}, u32[]{:S(2)}) collective-permute-start(f32[256,512]{1,0:T(8,128)S(1)} %collective-permute-done.23.refs_4_), channel_id=1, source_target_pairs={{0,8},{4,20},{8,0},{12,28},{16,24},{20,4},{24,16},{28,12},{1,9},{5... | collective-permute-start | bytes 1572872 | tf_op jit(solution)/shard_map/link_relayed/ppermute | solution.py:376
  92.9 11.2 %collective-permute-start.31 = (f32[512,512]{1,0:T(8,128)S(1)}, f32[512,512]{1,0:T(8,128)S(1)}, u32[]{:S(2)}, u32[]{:S(2)}) collective-permute-start(f32[512,512]{1,0:T(8,128)S(1)} %collective-permute-done.27.refs_6_), channel_id=1, source_target_pairs={{0,4},{4,0},{8,12},{12,8},{16,20},{20,16},{24,28},{28,24},{1,5},{5... | collective-permute-start | bytes 3145736 | tf_op jit(solution)/shard_map/core_second/ppermute | solution.py:376
  92.9 11.2 %collective-permute-start.29 = (f32[256,512]{1,0:T(8,128)S(1)}, f32[256,512]{1,0:T(8,128)S(1)}, u32[]{:S(2)}, u32[]{:S(2)}) collective-permute-start(f32[256,512]{1,0:T(8,128)S(1)} %collective-permute-done.26.refs_5_), channel_id=1, source_target_pairs={{0,8},{4,20},{8,0},{12,28},{16,24},{20,4},{24,16},{28,12},{1,9},{5... | collective-permute-start | bytes 1572872 | tf_op jit(solution)/shard_map/link_relayed/ppermute | solution.py:376
  98.5 7.5 %collective-permute-start.28 = (f32[256,512]{1,0:T(8,128)S(1)}, f32[256,512]{1,0:T(8,128)S(1)}, u32[]{:S(2)}, u32[]{:S(2)}) collective-permute-start(f32[256,512]{1,0:T(8,128)S(1)} %collective-permute-done.24.refs_1_), channel_id=1, source_target_pairs={{0,4},{4,0},{8,12},{12,8},{16,20},{20,16},{24,28},{28,24},{1,5},{5... | collective-permute-start | bytes 1572872 | tf_op jit(solution)/shard_map/core_relayed/ppermute | solution.py:376
  104.1 1.9 %collective-permute-start.30 = (f32[256,512]{1,0:T(8,128)S(1)}, f32[256,512]{1,0:T(8,128)S(1)}, u32[]{:S(2)}, u32[]{:S(2)}) collective-permute-start(f32[256,512]{1,0:T(8,128)S(1)} %collective-permute-done.29.refs_2_), channel_id=1, source_target_pairs={{0,4},{4,0},{8,12},{12,8},{16,20},{20,16},{24,28},{28,24},{1,5},{5... | collective-permute-start | bytes 1572872 | tf_op jit(solution)/shard_map/core_relayed/ppermute | solution.py:376
  (4 other events, 51.3 us)

commit v17 on v16

--- a/solution.py
+++ b/solution.py
@@ -425,7 +425,8 @@
     sides[0] += tuple(mix_call(*sides[0][:2]))
     norm = sum_call(after(norm, sides[0][4]), *chip_norms)
     norms = [norm]
-    for shift in reversed(range(1, group_count)):
+    far_first = sorted(range(1, group_count), key=lambda shift: (2 * shift != group_count, -shift))
+    for shift in far_first:
         both_ways = group_count & (group_count - 1) == 0
         pairs = [(i, i ^ shift if both_ways else (i + shift) % group_count) for i in range(group_count)]
         with jax.named_scope("group_norm"):
@@ -445,8 +446,10 @@
     crossed = [(("cross", 0, None), second), (("cross", 1, None), core_second)]
     result = assemble(None, *held, crossed[0])
     core_relayed = [to_core(after(relayed[0], result), "relayed"), to_core(relayed[1], "relayed")]
-    result = assemble(result, crossed[1], *[(("diagonal", 0, half), relayed[half]) for half in HALVES])
-    return assemble(result, *[(("diagonal", 1, half), core_relayed[half]) for half in HALVES])
+    result = assemble(
+        result, crossed[1], *[(("diagonal", 0, half), relayed[half]) for half in HALVES], (("diagonal", 1, 0), core_relayed[0])
+    )
+    return assemble(result, (("diagonal", 1, 1), core_relayed[1]))
 
 
 def solution(mesh):

time: 108 us -> 108 us (level)
  no operation moved by 1% of the time
where the time goes in v17:
time: 108 us
  waiting for transfers between devices  56.9 us (53%)
  starting transfers between devices  26.4 us (24%)
  Pallas kernels  21.4 us (20%)
  local copies, waits for them, and re-layouts  1.9 us (2%)
    ppermute x29, waiting for transfers between devices, over(): return lax.ppermute(value, 'dp', pairs)  54.8 us
    ppermute x29, starting transfers between devices, over(): return lax.ppermute(value, 'dp', pairs)  21.9 us
    pallas_call x20, Pallas kernels, local_call(): pl.pallas_call(kernel, in_specs=[pl.BlockSpec(memory_space=pltpu.SMEM)] *...  15.6 us
    pallas_call x3, Pallas kernels, assemble_call(): pl.pallas_call(kernel, in_specs=in_specs, out_specs=pl.BlockSpec(memory_s...  5.74 us
    ppermute x3, starting transfers between devices, paired_body(): norms.append(lax.ppermute(norm, 'mp', pairs))  4.46 us
  transfers between devices with their start and end apart: 32, of which 14 were waited for; matrix products, arithmetic and copies ran while one was open for 0% of the time, Pallas kernels for 12%

profile of v17, /device:TPU:0, one launch (start us, length us, event | category | flops | bytes accessed | tf_op | source)
XLA Modules:
  0.0 107.5 jit_solution(9280278487869771040)
XLA Ops:
  0.7 1.9 %copy-done = bf16[1,512,3072]{2,1,0:T(8,128)(2,1)S(1)} copy-done((bf16[1,512,3072]{2,1,0:T(8,128)(2,1)S(1)}, bf16[1,512,3072]{2,1,0:T(8,128)(2,1)}, u32[]{:S(2)}) %copy-start) | copy-done | bytes 3145752
  6.2 2.9 %collective-permute-start.6 = (f32[256,512]{1,0:T(8,128)S(1)}, f32[256,512]{1,0:T(8,128)S(1)}, u32[]{:S(2)}, u32[]{:S(2)}) collective-permute-start(f32[256,512]{1,0:T(8,128)S(1)} %add.13), channel_id=1, source_target_pairs={{0,8},{4,20},{8,0},{12,28},{16,24},{20,4},{24,16},{28,12},{1,9},{5... | collective-permute-start | bytes 1572872 | tf_op jit(solution)/shard_map/link_corner/ppermute | solution.py:376
  10.7 1.5 %collective-permute-start.3 = (f32[256,512]{1,0:T(8,128)S(1)}, f32[256,512]{1,0:T(8,128)S(1)}, u32[]{:S(2)}, u32[]{:S(2)}) collective-permute-start(f32[256,512]{1,0:T(8,128)S(1)} %add.11), channel_id=1, source_target_pairs={{0,8},{4,20},{8,0},{12,28},{16,24},{20,4},{24,16},{28,12},{1,9},{5... | collective-permute-start | bytes 1572872 | tf_op jit(solution)/shard_map/link_straight/ppermute | solution.py:376
  12.6 3.6 %collective-permute-done.6.refs_2_ = f32[256,512]{1,0:T(8,128)S(1)} collective-permute-done((f32[256,512]{1,0:T(8,128)S(1)}, f32[256,512]{1,0:T(8,128)S(1)}, u32[]{:S(2)}, u32[]{:S(2)}) %collective-permute-start.6) | collective-permute-done | bytes 524320 | tf_op jit(solution)/shard_map/link_corner/ppermute | solution.py:376
  16.2 2.0 %collective-permute-start.10 = (f32[256,512]{1,0:T(8,128)S(1)}, f32[256,512]{1,0:T(8,128)S(1)}, u32[]{:S(2)}, u32[]{:S(2)}) collective-permute-start(f32[256,512]{1,0:T(8,128)S(1)} %add.15), channel_id=1, source_target_pairs={{0,8},{4,20},{8,0},{12,28},{16,24},{20,4},{24,16},{28,12},{1,9},{5... | collective-permute-start | bytes 1572872 | tf_op jit(solution)/shard_map/link_straight/ppermute | solution.py:376
  18.3 3.5 %collective-permute-done.12.refs_2_ = f32[256,512]{1,0:T(8,128)S(1)} collective-permute-done((f32[256,512]{1,0:T(8,128)S(1)}, f32[256,512]{1,0:T(8,128)S(1)}, u32[]{:S(2)}, u32[]{:S(2)}) %collective-permute-start.12) | collective-permute-done | bytes 524320 | tf_op jit(solution)/shard_map/link_corner/ppermute | solution.py:376
  21.8 2.1 %collective-permute-start.7 = (f32[256,512]{1,0:T(8,128)S(1)}, f32[256,512]{1,0:T(8,128)S(1)}, u32[]{:S(2)}, u32[]{:S(2)}) collective-permute-start(f32[256,512]{1,0:T(8,128)S(1)} %add.14), channel_id=1, source_target_pairs={{0,16},{4,12},{8,24},{12,4},{16,0},{20,28},{24,8},{28,20},{1,17},{... | collective-permute-start | bytes 1572872 | tf_op jit(solution)/shard_map/side_side/ppermute | solution.py:376
  24.1 6.7 %collective-permute-done.3.refs_2_ = f32[256,512]{1,0:T(8,128)S(1)} collective-permute-done((f32[256,512]{1,0:T(8,128)S(1)}, f32[256,512]{1,0:T(8,128)S(1)}, u32[]{:S(2)}, u32[]{:S(2)}) %collective-permute-start.3) | collective-permute-done | bytes 524320 | tf_op jit(solution)/shard_map/link_straight/ppermute | solution.py:376
  30.9 1.5 %square.1 = (f32[512,512]{1,0:T(8,128)S(1)}, f32[512,512]{1,0:T(8,128)S(1)}) custom-call(f32[512,512]{1,0:T(8,128)S(1)} %bitcast.8, f32[512,512]{1,0:T(8,128)S(1)} %bitcast.11), custom_call_target="tpu_custom_call" | custom-call | flops 1610612736 | bytes 4194304 | tf_op jit(solution)/shard_map/square/pallas_call | solution.py:129
  32.4 9.7 %collective-permute-done.10.refs_2_ = f32[256,512]{1,0:T(8,128)S(1)} collective-permute-done((f32[256,512]{1,0:T(8,128)S(1)}, f32[256,512]{1,0:T(8,128)S(1)}, u32[]{:S(2)}, u32[]{:S(2)}) %collective-permute-start.10) | collective-permute-done | bytes 524320 | tf_op jit(solution)/shard_map/link_straight/ppermute | solution.py:376
  42.3 1.4 %collective-permute-done.13.arrival_ref = f32[256,512]{1,0:T(8,128)S(1)} collective-permute-done((f32[256,512]{1,0:T(8,128)S(1)}, f32[256,512]{1,0:T(8,128)S(1)}, u32[]{:S(2)}, u32[]{:S(2)}) %collective-permute-start.13) | collective-permute-done | bytes 524320 | tf_op jit(solution)/shard_map/side_side/ppermute | solution.py:376
  44.4 0.8 collective-permute-done.14.refs_1_
  45.2 3.0 %collective-permute-start.15 = (f32[8,128]{1,0:T(8,128)S(1)}, f32[8,128]{1,0:T(8,128)S(1)}, u32[]{:S(2)}, u32[]{:S(2)}) collective-permute-start(f32[8,128]{1,0:T(8,128)S(1)} %sum.2.refs_0_), channel_id=1, source_target_pairs={{0,24},{4,28},{8,16},{12,20},{16,8},{20,12},{24,0},{28,4},{1,25},{... | collective-permute-start | bytes 12296 | tf_op jit(solution)/shard_map/chip_norm/ppermute | solution.py:376
  48.8 1.5 %gram.1 = (f32[512,512]{1,0:T(8,128)S(1)}, f32[512,512]{1,0:T(8,128)S(1)}) custom-call(f32[256,512]{1,0:T(8,128)S(1)} %get-tuple-element.74.upper_ref, f32[256,512]{1,0:T(8,128)S(1)} %get-tuple-element.72.lower_ref), custom_call_target="tpu_custom_call" | custom-call | flops 1610612736 | bytes 3145728 | tf_op jit(solution)/shard_map/gram/pallas_call | solution.py:129
  50.3 1.7 %mix.2 = (f32[512,512]{1,0:T(8,128)S(1)}, f32[512,512]{1,0:T(8,128)S(1)}) custom-call(f32[512,512]{1,0:T(8,128)S(1)} %bitcast.9, f32[512,512]{1,0:T(8,128)S(1)} %get-tuple-element.75.gram_ref.refs_1_), custom_call_target="tpu_custom_call" | custom-call | flops 1610612736 | bytes 4194304 | tf_op jit(solution)/shard_map/mix/pallas_call | solution.py:129
  52.3 2.9 %collective-permute-start.18 = (f32[8,128]{1,0:T(8,128)S(1)}, f32[8,128]{1,0:T(8,128)S(1)}, u32[]{:S(2)}, u32[]{:S(2)}) collective-permute-start(f32[8,128]{1,0:T(8,128)S(1)} %sum.3.refs_10_), channel_id=1, source_target_pairs={{0,2},{1,3},{2,0},{3,1},{4,6},{5,7},{6,4},{7,5},{8,10},{9,11},{10,... | collective-permute-start | bytes 12296 | tf_op jit(solution)/shard_map/group_norm/ppermute | solution.py:433
  55.2 1.3 %collective-permute-start.19 = (f32[8,128]{1,0:T(8,128)S(1)}, f32[8,128]{1,0:T(8,128)S(1)}, u32[]{:S(2)}, u32[]{:S(2)}) collective-permute-start(f32[8,128]{1,0:T(8,128)S(1)} %sum.3.refs_10_), channel_id=1, source_target_pairs={{0,3},{1,2},{2,1},{3,0},{4,7},{5,6},{6,5},{7,4},{8,11},{9,10},{10,... | collective-permute-start | bytes 12296 | tf_op jit(solution)/shard_map/group_norm/ppermute | solution.py:433
  56.8 1.7 %mix.3 = (f32[512,512]{1,0:T(8,128)S(1)}, f32[512,512]{1,0:T(8,128)S(1)}) custom-call(f32[512,512]{1,0:T(8,128)S(1)} %bitcast.12, f32[512,512]{1,0:T(8,128)S(1)} %get-tuple-element.78.gram_ref.refs_6_), custom_call_target="tpu_custom_call" | custom-call | flops 1610612736 | bytes 4194304 | tf_op jit(solution)/shard_map/mix/pallas_call | solution.py:129
  58.5 2.1 %collective-permute-done.19.refs_12_ = f32[8,128]{1,0:T(8,128)S(1)} collective-permute-done((f32[8,128]{1,0:T(8,128)S(1)}, f32[8,128]{1,0:T(8,128)S(1)}, u32[]{:S(2)}, u32[]{:S(2)}) %collective-permute-start.19) | collective-permute-done | bytes 4128 | tf_op jit(solution)/shard_map/group_norm/ppermute | solution.py:433
  60.6 6.0 %update.1 = (f32[512,512]{1,0:T(8,128)S(1)}, f32[256,512]{1,0:T(8,128)S(1)}, f32[256,512]{1,0:T(8,128)S(1)}) custom-call(f32[256,512]{1,0:T(8,128)S(1)} %get-tuple-element.74.upper_ref, f32[256,512]{1,0:T(8,128)S(1)} %get-tuple-element.72.lower_ref, f32[8,128]{1,0:T(8,128)S(1)} %get-tuple-element.73.refs_0_.block_norm_ref, f32[512,512]{1,0:T(8,128)S(1)} %bitcast.10, ...), custom_call_target="tpu_custom_call" | custom-call | flops 4831838208 | bytes 13651968 | tf_op jit(solution)/shard_map/update/pallas_call | solution.py:129
  66.7 1.6 %collective-permute-start.26 = (f32[256,512]{1,0:T(8,128)S(1)}, f32[256,512]{1,0:T(8,128)S(1)}, u32[]{:S(2)}, u32[]{:S(2)}) collective-permute-start(f32[256,512]{1,0:T(8,128)S(1)} %get-tuple-element.85), channel_id=1, source_target_pairs={{0,8},{4,20},{8,0},{12,28},{16,24},{20,4},{24,16},{28,12},{1,9},{5... | collective-permute-start | bytes 1572872 | tf_op jit(solution)/shard_map/link_own/ppermute | solution.py:376
  68.8 7.2 %collective-permute-done.26.refs_2_ = f32[256,512]{1,0:T(8,128)S(1)} collective-permute-done((f32[256,512]{1,0:T(8,128)S(1)}, f32[256,512]{1,0:T(8,128)S(1)}, u32[]{:S(2)}, u32[]{:S(2)}) %collective-permute-start.26) | collective-permute-done | bytes 524320 | tf_op jit(solution)/shard_map/link_own/ppermute | solution.py:376
  75.9 1.5 %collective-permute-start.27 = (f32[512,512]{1,0:T(8,128)S(1)}, f32[512,512]{1,0:T(8,128)S(1)}, u32[]{:S(2)}, u32[]{:S(2)}) collective-permute-start(f32[512,512]{1,0:T(8,128)S(1)} %collective-permute-done.22.refs_1_), channel_id=1, source_target_pairs={{0,8},{4,20},{8,0},{12,28},{16,24},{20,4},{24,16},{28,12},{1,9},{5... | collective-permute-start | bytes 3145736 | tf_op jit(solution)/shard_map/link_sibling/ppermute | solution.py:376
  77.4 4.1 %collective-permute-done.21.refs_3_ = f32[256,512]{1,0:T(8,128)S(1)} collective-permute-done((f32[256,512]{1,0:T(8,128)S(1)}, f32[256,512]{1,0:T(8,128)S(1)}, u32[]{:S(2)}, u32[]{:S(2)}) %collective-permute-start.21) | collective-permute-done | bytes 524320 | tf_op jit(solution)/shard_map/link_own/ppermute | solution.py:376
  81.6 1.5 %collective-permute-start.30 = (f32[256,512]{1,0:T(8,128)S(1)}, f32[256,512]{1,0:T(8,128)S(1)}, u32[]{:S(2)}, u32[]{:S(2)}) collective-permute-start(f32[256,512]{1,0:T(8,128)S(1)} %collective-permute-done.29.refs_4_), channel_id=1, source_target_pairs={{0,8},{4,20},{8,0},{12,28},{16,24},{20,4},{24,16},{28,12},{1,9},{5... | collective-permute-start | bytes 1572872 | tf_op jit(solution)/shard_map/link_relayed/ppermute | solution.py:376
  83.1 9.7 %collective-permute-done.27.refs_6_ = f32[512,512]{1,0:T(8,128)S(1)} collective-permute-done((f32[512,512]{1,0:T(8,128)S(1)}, f32[512,512]{1,0:T(8,128)S(1)}, u32[]{:S(2)}, u32[]{:S(2)}) %collective-permute-start.27) | collective-permute-done | bytes 1048608 | tf_op jit(solution)/shard_map/link_sibling/ppermute | solution.py:376
  92.8 1.5 %collective-permute-start.24 = (f32[256,512]{1,0:T(8,128)S(1)}, f32[256,512]{1,0:T(8,128)S(1)}, u32[]{:S(2)}, u32[]{:S(2)}) collective-permute-start(f32[256,512]{1,0:T(8,128)S(1)} %collective-permute-done.23.refs_5_), channel_id=1, source_target_pairs={{0,8},{4,20},{8,0},{12,28},{16,24},{20,4},{24,16},{28,12},{1,9},{5... | collective-permute-start | bytes 1572872 | tf_op jit(solution)/shard_map/link_relayed/ppermute | solution.py:376
  94.3 2.3 %assemble.3.refs_4_ = f32[512,3072]{1,0:T(8,128)} custom-call(s32[7]{0:T(128)S(1)} %pad_add_fusion.places_ref, f32[512,512]{1,0:T(8,128)S(1)} %get-tuple-element.83.refs_0_, f32[512,512]{1,0:T(8,128)S(1)} %collective-permute-done.22.refs_1_, f32[256,512]{1,0:T(8,128)S(1)} %collective-permute-done.26.refs_2_, f32[256,512]{1,0:T(8,128)S(1)} %collective-permute-done.21.refs_3_, ...), custom_call_target="tpu_custom_call" | custom-call | bytes 14680064 | tf_op jit(solution)/shard_map/assemble/pallas_call | solution.py:347
  96.6 1.8 %collective-permute-done.30.refs_1_ = f32[256,512]{1,0:T(8,128)S(1)} collective-permute-done((f32[256,512]{1,0:T(8,128)S(1)}, f32[256,512]{1,0:T(8,128)S(1)}, u32[]{:S(2)}, u32[]{:S(2)}) %collective-permute-start.30) | collective-permute-done | bytes 524320 | tf_op jit(solution)/shard_map/link_relayed/ppermute | solution.py:376
  98.4 5.6 %collective-permute-done.24.refs_2_ = f32[256,512]{1,0:T(8,128)S(1)} collective-permute-done((f32[256,512]{1,0:T(8,128)S(1)}, f32[256,512]{1,0:T(8,128)S(1)}, u32[]{:S(2)}, u32[]{:S(2)}) %collective-permute-start.24) | collective-permute-done | bytes 524320 | tf_op jit(solution)/shard_map/link_relayed/ppermute | solution.py:376
  104.0 2.1 %assemble.4.refs_1_ = f32[512,3072]{1,0:T(8,128)} custom-call(s32[7]{0:T(128)S(1)} %pad_add_fusion.places_ref, f32[512,512]{1,0:T(8,128)S(1)} %collective-permute-done.28.refs_0_, f32[256,512]{1,0:T(8,128)S(1)} %collective-permute-done.30.refs_1_, f32[256,512]{1,0:T(8,128)S(1)} %collective-permute-done.24.refs_2_, ...), custom_call_target="tpu_custom_call", output_to_operand_aliasing={{}: (5, {})} | custom-call | bytes 8388608 | tf_op jit(solution)/shard_map/assemble/pallas_call | solution.py:347
  106.1 1.4 %assemble.5 = f32[512,3072]{1,0:T(8,128)} custom-call(s32[7]{0:T(128)S(1)} %pad_add_fusion.places_ref, f32[256,512]{1,0:T(8,128)S(1)} %collective-permute-done.25.refs_0_, f32[512,3072]{1,0:T(8,128)} %assemble.4.refs_1_), custom_call_target="tpu_custom_call", output_to_operand_aliasing={{}: (2, {})} | custom-call | bytes 1048576 | tf_op jit(solution)/shard_map/assemble/pallas_call | solution.py:347
  (64 shorter events, 9.2 us)
Async XLA Ops:
  3.4 2.3 %collective-permute-start.5 = (f32[256,512]{1,0:T(8,128)S(1)}, f32[256,512]{1,0:T(8,128)S(1)}, u32[]{:S(2)}, u32[]{:S(2)}) collective-permute-start(f32[256,512]{1,0:T(8,128)S(1)} %get-tuple-element.62), channel_id=1, source_target_pairs={{0,4},{4,0},{8,12},{12,8},{16,20},{20,16},{24,28},{28,24},{1,5},{5... | collective-permute-start | bytes 1572872 | tf_op jit(solution)/shard_map/core_corner/ppermute | solution.py:376
  3.9 2.3 %collective-permute-start = (f32[256,512]{1,0:T(8,128)S(1)}, f32[256,512]{1,0:T(8,128)S(1)}, u32[]{:S(2)}, u32[]{:S(2)}) collective-permute-start(f32[256,512]{1,0:T(8,128)S(1)} %get-tuple-element.48), channel_id=1, source_target_pairs={{0,4},{4,0},{8,12},{12,8},{16,20},{20,16},{24,28},{28,24},{1,5},{5... | collective-permute-start | bytes 1572872 | tf_op jit(solution)/shard_map/core_corner/ppermute | solution.py:376
  4.0 5.1 %collective-permute-start.2 = (f32[256,512]{1,0:T(8,128)S(1)}, f32[256,512]{1,0:T(8,128)S(1)}, u32[]{:S(2)}, u32[]{:S(2)}) collective-permute-start(f32[256,512]{1,0:T(8,128)S(1)} %get-tuple-element.53), channel_id=1, source_target_pairs={{0,4},{4,0},{8,12},{12,8},{16,20},{20,16},{24,28},{28,24},{1,5},{5... | collective-permute-start | bytes 1572872 | tf_op jit(solution)/shard_map/core_straight/ppermute | solution.py:376
  5.1 4.7 %collective-permute-start.4 = (f32[256,512]{1,0:T(8,128)S(1)}, f32[256,512]{1,0:T(8,128)S(1)}, u32[]{:S(2)}, u32[]{:S(2)}) collective-permute-start(f32[256,512]{1,0:T(8,128)S(1)} %get-tuple-element.60), channel_id=1, source_target_pairs={{0,4},{4,0},{8,12},{12,8},{16,20},{20,16},{24,28},{28,24},{1,5},{5... | collective-permute-start | bytes 1572872 | tf_op jit(solution)/shard_map/core_side/ppermute | solution.py:376
  5.3 5.4 %collective-permute-start.9 = (f32[256,512]{1,0:T(8,128)S(1)}, f32[256,512]{1,0:T(8,128)S(1)}, u32[]{:S(2)}, u32[]{:S(2)}) collective-permute-start(f32[256,512]{1,0:T(8,128)S(1)} %get-tuple-element.68), channel_id=1, source_target_pairs={{0,4},{4,0},{8,12},{12,8},{16,20},{20,16},{24,28},{28,24},{1,5},{5... | collective-permute-start | bytes 1572872 | tf_op jit(solution)/shard_map/core_straight/ppermute | solution.py:376
  5.7 6.5 %collective-permute-start.11 = (f32[256,512]{1,0:T(8,128)S(1)}, f32[256,512]{1,0:T(8,128)S(1)}, u32[]{:S(2)}, u32[]{:S(2)}) collective-permute-start(f32[256,512]{1,0:T(8,128)S(1)} %get-tuple-element.70), channel_id=1, source_target_pairs={{0,4},{4,0},{8,12},{12,8},{16,20},{20,16},{24,28},{28,24},{1,5},{5... | collective-permute-start | bytes 1572872 | tf_op jit(solution)/shard_map/core_side/ppermute | solution.py:376
  6.2 10.0 %collective-permute-start.6 = (f32[256,512]{1,0:T(8,128)S(1)}, f32[256,512]{1,0:T(8,128)S(1)}, u32[]{:S(2)}, u32[]{:S(2)}) collective-permute-start(f32[256,512]{1,0:T(8,128)S(1)} %add.13), channel_id=1, source_target_pairs={{0,8},{4,20},{8,0},{12,28},{16,24},{20,4},{24,16},{28,12},{1,9},{5... | collective-permute-start | bytes 1572872 | tf_op jit(solution)/shard_map/link_corner/ppermute | solution.py:376
  9.1 12.7 %collective-permute-start.12 = (f32[256,512]{1,0:T(8,128)S(1)}, f32[256,512]{1,0:T(8,128)S(1)}, u32[]{:S(2)}, u32[]{:S(2)}) collective-permute-start(f32[256,512]{1,0:T(8,128)S(1)} %add.10), channel_id=1, source_target_pairs={{0,8},{4,20},{8,0},{12,28},{16,24},{20,4},{24,16},{28,12},{1,9},{5... | collective-permute-start | bytes 1572872 | tf_op jit(solution)/shard_map/link_corner/ppermute | solution.py:376
  9.8 14.2 %collective-permute-start.1 = (f32[256,512]{1,0:T(8,128)S(1)}, f32[256,512]{1,0:T(8,128)S(1)}, u32[]{:S(2)}, u32[]{:S(2)}) collective-permute-start(f32[256,512]{1,0:T(8,128)S(1)} %get-tuple-element.51), channel_id=1, source_target_pairs={{0,4},{4,0},{8,12},{12,8},{16,20},{20,16},{24,28},{28,24},{1,5},{5... | collective-permute-start | bytes 1572872 | tf_op jit(solution)/shard_map/core_self/ppermute | solution.py:376
  10.7 20.1 %collective-permute-start.3 = (f32[256,512]{1,0:T(8,128)S(1)}, f32[256,512]{1,0:T(8,128)S(1)}, u32[]{:S(2)}, u32[]{:S(2)}) collective-permute-start(f32[256,512]{1,0:T(8,128)S(1)} %add.11), channel_id=1, source_target_pairs={{0,8},{4,20},{8,0},{12,28},{16,24},{20,4},{24,16},{28,12},{1,9},{5... | collective-permute-start | bytes 1572872 | tf_op jit(solution)/shard_map/link_straight/ppermute | solution.py:376
  12.2 20.1 %collective-permute-start.8 = (f32[256,512]{1,0:T(8,128)S(1)}, f32[256,512]{1,0:T(8,128)S(1)}, u32[]{:S(2)}, u32[]{:S(2)}) collective-permute-start(f32[256,512]{1,0:T(8,128)S(1)} %get-tuple-element.66), channel_id=1, source_target_pairs={{0,4},{4,0},{8,12},{12,8},{16,20},{20,16},{24,28},{28,24},{1,5},{5... | collective-permute-start | bytes 1572872 | tf_op jit(solution)/shard_map/core_self/ppermute | solution.py:376
  16.2 25.8 %collective-permute-start.10 = (f32[256,512]{1,0:T(8,128)S(1)}, f32[256,512]{1,0:T(8,128)S(1)}, u32[]{:S(2)}, u32[]{:S(2)}) collective-permute-start(f32[256,512]{1,0:T(8,128)S(1)} %add.15), channel_id=1, source_target_pairs={{0,8},{4,20},{8,0},{12,28},{16,24},{20,4},{24,16},{28,12},{1,9},{5... | collective-permute-start | bytes 1572872 | tf_op jit(solution)/shard_map/link_straight/ppermute | solution.py:376
  21.8 20.3 %collective-permute-start.7 = (f32[256,512]{1,0:T(8,128)S(1)}, f32[256,512]{1,0:T(8,128)S(1)}, u32[]{:S(2)}, u32[]{:S(2)}) collective-permute-start(f32[256,512]{1,0:T(8,128)S(1)} %add.14), channel_id=1, source_target_pairs={{0,16},{4,12},{8,24},{12,4},{16,0},{20,28},{24,8},{28,20},{1,17},{... | collective-permute-start | bytes 1572872 | tf_op jit(solution)/shard_map/side_side/ppermute | solution.py:376
  24.0 19.8 %collective-permute-start.13 = (f32[256,512]{1,0:T(8,128)S(1)}, f32[256,512]{1,0:T(8,128)S(1)}, u32[]{:S(2)}, u32[]{:S(2)}) collective-permute-start(f32[256,512]{1,0:T(8,128)S(1)} %add.17), channel_id=1, source_target_pairs={{0,16},{4,12},{8,24},{12,4},{16,0},{20,28},{24,8},{28,20},{1,17},{... | collective-permute-start | bytes 1572872 | tf_op jit(solution)/shard_map/side_side/ppermute | solution.py:376
  44.0 1.2 %collective-permute-start.14 = (f32[8,128]{1,0:T(8,128)S(1)}, f32[8,128]{1,0:T(8,128)S(1)}, u32[]{:S(2)}, u32[]{:S(2)}) collective-permute-start(f32[8,128]{1,0:T(8,128)S(1)} %get-tuple-element.73.refs_0_.block_norm_ref), channel_id=1, source_target_pairs={{0,4},{4,0},{8,12},{12,8},{16,20},{20,16},{24,28},{28,24},{1,5},{5... | collective-permute-start | bytes 12296 | tf_op jit(solution)/shard_map/core_norm/ppermute | solution.py:376
  45.2 6.8 %collective-permute-start.15 = (f32[8,128]{1,0:T(8,128)S(1)}, f32[8,128]{1,0:T(8,128)S(1)}, u32[]{:S(2)}, u32[]{:S(2)}) collective-permute-start(f32[8,128]{1,0:T(8,128)S(1)} %sum.2.refs_0_), channel_id=1, source_target_pairs={{0,24},{4,28},{8,16},{12,20},{16,8},{20,12},{24,0},{28,4},{1,25},{... | collective-permute-start | bytes 12296 | tf_op jit(solution)/shard_map/chip_norm/ppermute | solution.py:376
  48.2 3.8 %collective-permute-start.16 = (f32[8,128]{1,0:T(8,128)S(1)}, f32[8,128]{1,0:T(8,128)S(1)}, u32[]{:S(2)}, u32[]{:S(2)}) collective-permute-start(f32[8,128]{1,0:T(8,128)S(1)} %sum.2.refs_0_), channel_id=1, source_target_pairs={{0,16},{4,20},{8,24},{12,28},{16,0},{20,4},{24,8},{28,12},{1,17},{... | collective-permute-start | bytes 12296 | tf_op jit(solution)/shard_map/chip_norm/ppermute | solution.py:376
  48.7 3.6 %collective-permute-start.17 = (f32[8,128]{1,0:T(8,128)S(1)}, f32[8,128]{1,0:T(8,128)S(1)}, u32[]{:S(2)}, u32[]{:S(2)}) collective-permute-start(f32[8,128]{1,0:T(8,128)S(1)} %sum.2.refs_0_), channel_id=1, source_target_pairs={{0,8},{4,12},{8,0},{12,4},{16,24},{20,28},{24,16},{28,20},{1,9},{5... | collective-permute-start | bytes 12296 | tf_op jit(solution)/shard_map/chip_norm/ppermute | solution.py:376
  52.3 6.2 %collective-permute-start.18 = (f32[8,128]{1,0:T(8,128)S(1)}, f32[8,128]{1,0:T(8,128)S(1)}, u32[]{:S(2)}, u32[]{:S(2)}) collective-permute-start(f32[8,128]{1,0:T(8,128)S(1)} %sum.3.refs_10_), channel_id=1, source_target_pairs={{0,2},{1,3},{2,0},{3,1},{4,6},{5,7},{6,4},{7,5},{8,10},{9,11},{10,... | collective-permute-start | bytes 12296 | tf_op jit(solution)/shard_map/group_norm/ppermute | solution.py:433
  55.2 5.4 %collective-permute-start.19 = (f32[8,128]{1,0:T(8,128)S(1)}, f32[8,128]{1,0:T(8,128)S(1)}, u32[]{:S(2)}, u32[]{:S(2)}) collective-permute-start(f32[8,128]{1,0:T(8,128)S(1)} %sum.3.refs_10_), channel_id=1, source_target_pairs={{0,3},{1,2},{2,1},{3,0},{4,7},{5,6},{6,5},{7,4},{8,11},{9,10},{10,... | collective-permute-start | bytes 12296 | tf_op jit(solution)/shard_map/group_norm/ppermute | solution.py:433
  56.5 4.1 %collective-permute-start.20 = (f32[8,128]{1,0:T(8,128)S(1)}, f32[8,128]{1,0:T(8,128)S(1)}, u32[]{:S(2)}, u32[]{:S(2)}) collective-permute-start(f32[8,128]{1,0:T(8,128)S(1)} %sum.3.refs_10_), channel_id=1, source_target_pairs={{0,1},{1,0},{2,3},{3,2},{4,5},{5,4},{6,7},{7,6},{8,9},{9,8},{10,11... | collective-permute-start | bytes 12296 | tf_op jit(solution)/shard_map/group_norm/ppermute | solution.py:433
  66.6 9.3 %collective-permute-start.22 = (f32[512,512]{1,0:T(8,128)S(1)}, f32[512,512]{1,0:T(8,128)S(1)}, u32[]{:S(2)}, u32[]{:S(2)}) collective-permute-start(f32[512,512]{1,0:T(8,128)S(1)} %get-tuple-element.83.refs_0_), channel_id=1, source_target_pairs={{0,4},{4,0},{8,12},{12,8},{16,20},{20,16},{24,28},{28,24},{1,5},{5... | collective-permute-start | bytes 3145736 | tf_op jit(solution)/shard_map/core_own/ppermute | solution.py:376
  66.7 9.2 %collective-permute-start.26 = (f32[256,512]{1,0:T(8,128)S(1)}, f32[256,512]{1,0:T(8,128)S(1)}, u32[]{:S(2)}, u32[]{:S(2)}) collective-permute-start(f32[256,512]{1,0:T(8,128)S(1)} %get-tuple-element.85), channel_id=1, source_target_pairs={{0,8},{4,20},{8,0},{12,28},{16,24},{20,4},{24,16},{28,12},{1,9},{5... | collective-permute-start | bytes 1572872 | tf_op jit(solution)/shard_map/link_own/ppermute | solution.py:376
  68.3 13.3 %collective-permute-start.21 = (f32[256,512]{1,0:T(8,128)S(1)}, f32[256,512]{1,0:T(8,128)S(1)}, u32[]{:S(2)}, u32[]{:S(2)}) collective-permute-start(f32[256,512]{1,0:T(8,128)S(1)} %get-tuple-element.82), channel_id=1, source_target_pairs={{0,8},{4,20},{8,0},{12,28},{16,24},{20,4},{24,16},{28,12},{1,9},{5... | collective-permute-start | bytes 1572872 | tf_op jit(solution)/shard_map/link_own/ppermute | solution.py:376
  75.9 16.8 %collective-permute-start.27 = (f32[512,512]{1,0:T(8,128)S(1)}, f32[512,512]{1,0:T(8,128)S(1)}, u32[]{:S(2)}, u32[]{:S(2)}) collective-permute-start(f32[512,512]{1,0:T(8,128)S(1)} %collective-permute-done.22.refs_1_), channel_id=1, source_target_pairs={{0,8},{4,20},{8,0},{12,28},{16,24},{20,4},{24,16},{28,12},{1,9},{5... | collective-permute-start | bytes 3145736 | tf_op jit(solution)/shard_map/link_sibling/ppermute | solution.py:376
  77.4 4.1 %collective-permute-start.29 = (f32[256,512]{1,0:T(8,128)S(1)}, f32[256,512]{1,0:T(8,128)S(1)}, u32[]{:S(2)}, u32[]{:S(2)}) collective-permute-start(f32[256,512]{1,0:T(8,128)S(1)} %collective-permute-done.26.refs_2_), channel_id=1, source_target_pairs={{0,4},{4,0},{8,12},{12,8},{16,20},{20,16},{24,28},{28,24},{1,5},{5... | collective-permute-start | bytes 1572872 | tf_op jit(solution)/shard_map/core_first/ppermute | solution.py:376
  81.6 11.2 %collective-permute-start.23 = (f32[256,512]{1,0:T(8,128)S(1)}, f32[256,512]{1,0:T(8,128)S(1)}, u32[]{:S(2)}, u32[]{:S(2)}) collective-permute-start(f32[256,512]{1,0:T(8,128)S(1)} %collective-permute-done.21.refs_3_), channel_id=1, source_target_pairs={{0,4},{4,0},{8,12},{12,8},{16,20},{20,16},{24,28},{28,24},{1,5},{5... | collective-permute-start | bytes 1572872 | tf_op jit(solution)/shard_map/core_first/ppermute | solution.py:376
  81.6 16.8 %collective-permute-start.30 = (f32[256,512]{1,0:T(8,128)S(1)}, f32[256,512]{1,0:T(8,128)S(1)}, u32[]{:S(2)}, u32[]{:S(2)}) collective-permute-start(f32[256,512]{1,0:T(8,128)S(1)} %collective-permute-done.29.refs_4_), channel_id=1, source_target_pairs={{0,8},{4,20},{8,0},{12,28},{16,24},{20,4},{24,16},{28,12},{1,9},{5... | collective-permute-start | bytes 1572872 | tf_op jit(solution)/shard_map/link_relayed/ppermute | solution.py:376
  92.8 11.2 %collective-permute-start.28 = (f32[512,512]{1,0:T(8,128)S(1)}, f32[512,512]{1,0:T(8,128)S(1)}, u32[]{:S(2)}, u32[]{:S(2)}) collective-permute-start(f32[512,512]{1,0:T(8,128)S(1)} %collective-permute-done.27.refs_6_), channel_id=1, source_target_pairs={{0,4},{4,0},{8,12},{12,8},{16,20},{20,16},{24,28},{28,24},{1,5},{5... | collective-permute-start | bytes 3145736 | tf_op jit(solution)/shard_map/core_second/ppermute | solution.py:376
  92.8 11.2 %collective-permute-start.24 = (f32[256,512]{1,0:T(8,128)S(1)}, f32[256,512]{1,0:T(8,128)S(1)}, u32[]{:S(2)}, u32[]{:S(2)}) collective-permute-start(f32[256,512]{1,0:T(8,128)S(1)} %collective-permute-done.23.refs_5_), channel_id=1, source_target_pairs={{0,8},{4,20},{8,0},{12,28},{16,24},{20,4},{24,16},{28,12},{1,9},{5... | collective-permute-start | bytes 1572872 | tf_op jit(solution)/shard_map/link_relayed/ppermute | solution.py:376
  98.4 5.6 %collective-permute-start.31 = (f32[256,512]{1,0:T(8,128)S(1)}, f32[256,512]{1,0:T(8,128)S(1)}, u32[]{:S(2)}, u32[]{:S(2)}) collective-permute-start(f32[256,512]{1,0:T(8,128)S(1)} %collective-permute-done.30.refs_1_), channel_id=1, source_target_pairs={{0,4},{4,0},{8,12},{12,8},{16,20},{20,16},{24,28},{28,24},{1,5},{5... | collective-permute-start | bytes 1572872 | tf_op jit(solution)/shard_map/core_relayed/ppermute | solution.py:376
  104.0 2.1 %collective-permute-start.25 = (f32[256,512]{1,0:T(8,128)S(1)}, f32[256,512]{1,0:T(8,128)S(1)}, u32[]{:S(2)}, u32[]{:S(2)}) collective-permute-start(f32[256,512]{1,0:T(8,128)S(1)} %collective-permute-done.24.refs_2_), channel_id=1, source_target_pairs={{0,4},{4,0},{8,12},{12,8},{16,20},{20,16},{24,28},{28,24},{1,5},{5... | collective-permute-start | bytes 1572872 | tf_op jit(solution)/shard_map/core_relayed/ppermute | solution.py:376
  (4 other events, 51.3 us)

commit v18 on v17

--- a/solution.py
+++ b/solution.py
@@ -159,7 +159,7 @@
     return jax.ShapeDtypeStruct((width if half is None else width // 2, width), F32)
 
 
-def pack_call(places, grads, pieces, width, with_owned=False):
+def pack_call(places, grads, pieces, width, with_flags=False):
     block_count = grads.shape[1] // width
 
     def kernel(places_ref, grad_ref, *out_refs):
@@ -168,15 +168,16 @@
             columns = owner_columns(places_ref, grad_ref, width, piece_target(kind, me ^ flip))
             for block_rows, piece_rows in row_chunks(half, width):
                 out_ref[piece_rows, :] = grad_ref[block_rows, columns].astype(F32)
-        if with_owned:
+        if with_flags:
             owned = 0
             for index in range(block_count):
                 owned = owned + jnp.where(places_ref[index] == me, 1, 0)
-            out_refs[-1][...] = jnp.full((8, 128), owned.astype(F32))
+            out_refs[-2][...] = jnp.full((8, 128), owned.astype(F32))
+            out_refs[-1][...] = jnp.full((8, 128), (me & 1).astype(F32))
 
     shapes = [piece_shape(half, width) for _, _, half in pieces]
-    if with_owned:
-        shapes.append(jax.ShapeDtypeStruct((8, 128), F32))
+    if with_flags:
+        shapes += [jax.ShapeDtypeStruct((8, 128), F32)] * 2
     return local_call(kernel, "pack", shapes, (grads,), (places,))
 
 
@@ -296,7 +297,8 @@
 
     def kernel(upper_ref, lower_ref, block_norm_ref, *refs):
         left_refs, right_refs, norm_refs, out_refs = refs[:5], refs[5:10], refs[10:-3], refs[-3:]
-        squares = sum(ref[:1, :1] for ref in norm_refs)
+        group_ref, handed_ref, second_core_ref = norm_refs
+        squares = group_ref[:1, :1] * second_core_ref[:1, :1] + handed_ref[:1, :1]
         clip_factor = jnp.minimum(1.0, clip_level / jnp.sqrt(squares / entry_count))
         gram_scale = clip_factor * clip_factor / width
         roots, scales = roots_of((left_refs, right_refs), gram_scale)
@@ -401,7 +403,7 @@
     pieces += cut(places, keys[4:], [])
     from_core = {key: to_core(value, key[0]) for key, value in zip(keys, pieces)}
     sums = [add_call(own_first, from_core[keys[0]]), add_call(own_second, from_core[keys[1]])]
-    *own, owned = cut(after(places, sums[1]), [], keys[2:], with_owned=True)
+    *own, owned, second_core = cut(after(places, sums[1]), [], keys[2:], with_flags=True)
     own = dict(zip(keys[2:], own))
     sums += [add_call(own[key], from_core[key]) for key in keys[2:4]]
     from_link = {key: to_link(value, key[0]) for key, value in zip(keys[:4], sums)}
@@ -424,14 +426,21 @@
     sides = [(previous, gram, square) for (previous,), gram, square in zip(sides, grams, squares)]
     sides[0] += tuple(mix_call(*sides[0][:2]))
     norm = sum_call(after(norm, sides[0][4]), *chip_norms)
-    norms = [norm]
+    tiles = [norm]
+    both_ways = group_count & (group_count - 1) == 0
     far_first = sorted(range(1, group_count), key=lambda shift: (2 * shift != group_count, -shift))
     for shift in far_first:
-        both_ways = group_count & (group_count - 1) == 0
-        pairs = [(i, i ^ shift if both_ways else (i + shift) % group_count) for i in range(group_count)]
+        pairs = []
+        for device in range(1, 8, 2):
+            for group in range(group_count):
+                other = group ^ shift if both_ways else (group + shift) % group_count
+                pairs.append((device * group_count + group, device * group_count + other))
         with jax.named_scope("group_norm"):
-            norms.append(lax.ppermute(norm, "mp", pairs))
+            tiles.append(lax.ppermute(norm, ("dp", "mp"), pairs))
     sides[1] += tuple(mix_call(*sides[1][:2]))
+    group_norm = sum_call(after(tiles[0], sides[1][3]), *tiles[1:])
+    handed = over([(device, device ^ 1) for device in range(1, 8, 2)], group_norm, "core_norm")
+    norms = [group_norm, handed, second_core]
     whole, *own = update_call(block, block_norm, *sides, norms, entry_count)
 
     core_own = to_core(whole, "own")

time: 108 us -> 113 us (1.046)
  waiting for transfers between devices: 56.9 us -> 62.4 us
    ppermute x29 -> x30, waiting for transfers between devices: 54.8 us -> 62.4 us  [over(): return lax.ppermute(value, 'dp', pairs)]
    ppermute x3, starting transfers between devices: 4.46 us -> 1.97 us  [paired_body(): tiles.append(lax.ppermute(norm, ('dp', 'mp'), pairs))]
    ppermute x3, waiting for transfers between devices: 2.11 us -> 0.01 us  [paired_body(): tiles.append(lax.ppermute(norm, ('dp', 'mp'), pairs))]
    ppermute x29 -> x30, starting transfers between devices: 21.9 us -> 23.4 us  [over(): return lax.ppermute(value, 'dp', pairs)]
    pallas_call x20 -> x21, Pallas kernels: 15.6 us -> 15.8 us  [local_call(): pl.pallas_call(kernel, in_specs=[pl.BlockSpec(memory_space=pltpu.SMEM)] *...]
  transfers between devices with their start and end apart: 32 -> 33, of which waited for: 14 -> 15; matrix products, arithmetic and copies ran while one was open for 0% -> 0% of each run, Pallas kernels for 12% -> 12%
where the time goes in v18:
time: 113 us; the launch traced here: 112 us
  waiting for transfers between devices  62.4 us (55%)
  starting transfers between devices  25.4 us (22%)
  Pallas kernels  20.9 us (18%)
  local copies, waits for them, and re-layouts  1.9 us (2%)
    ppermute x30, waiting for transfers between devices, over(): return lax.ppermute(value, 'dp', pairs)  62.4 us
    ppermute x30, starting transfers between devices, over(): return lax.ppermute(value, 'dp', pairs)  23.4 us
    pallas_call x21, Pallas kernels, local_call(): pl.pallas_call(kernel, in_specs=[pl.BlockSpec(memory_space=pltpu.SMEM)] *...  15.8 us
    pallas_call x3, Pallas kernels, assemble_call(): pl.pallas_call(kernel, in_specs=in_specs, out_specs=pl.BlockSpec(memory_s...  5.1 us
  transfers between devices with their start and end apart: 33, of which 15 were waited for; matrix products, arithmetic and copies ran while one was open for 0% of the time, Pallas kernels for 12%

profile of v18, /device:TPU:0, one launch (start us, length us, event | category | flops | bytes accessed | tf_op | source)
XLA Modules:
  0.0 111.8 jit_solution(7861019837486834413)
XLA Ops:
  0.7 1.9 %copy-done = bf16[1,512,3072]{2,1,0:T(8,128)(2,1)S(1)} copy-done((bf16[1,512,3072]{2,1,0:T(8,128)(2,1)S(1)}, bf16[1,512,3072]{2,1,0:T(8,128)(2,1)}, u32[]{:S(2)}) %copy-start) | copy-done | bytes 3145752
  2.6 0.8 pack.3
  6.2 2.9 %collective-permute-start.6 = (f32[256,512]{1,0:T(8,128)S(1)}, f32[256,512]{1,0:T(8,128)S(1)}, u32[]{:S(2)}, u32[]{:S(2)}) collective-permute-start(f32[256,512]{1,0:T(8,128)S(1)} %add.13), channel_id=1, source_target_pairs={{0,8},{4,20},{8,0},{12,28},{16,24},{20,4},{24,16},{28,12},{1,9},{5... | collective-permute-start | bytes 1572872 | tf_op jit(solution)/shard_map/link_corner/ppermute | solution.py:378
  9.8 0.8 pack.4
  10.7 1.5 %collective-permute-start.3 = (f32[256,512]{1,0:T(8,128)S(1)}, f32[256,512]{1,0:T(8,128)S(1)}, u32[]{:S(2)}, u32[]{:S(2)}) collective-permute-start(f32[256,512]{1,0:T(8,128)S(1)} %add.11), channel_id=1, source_target_pairs={{0,8},{4,20},{8,0},{12,28},{16,24},{20,4},{24,16},{28,12},{1,9},{5... | collective-permute-start | bytes 1572872 | tf_op jit(solution)/shard_map/link_straight/ppermute | solution.py:378
  12.6 3.6 %collective-permute-done.6.refs_2_ = f32[256,512]{1,0:T(8,128)S(1)} collective-permute-done((f32[256,512]{1,0:T(8,128)S(1)}, f32[256,512]{1,0:T(8,128)S(1)}, u32[]{:S(2)}, u32[]{:S(2)}) %collective-permute-start.6) | collective-permute-done | bytes 524320 | tf_op jit(solution)/shard_map/link_corner/ppermute | solution.py:378
  16.2 2.0 %collective-permute-start.10 = (f32[256,512]{1,0:T(8,128)S(1)}, f32[256,512]{1,0:T(8,128)S(1)}, u32[]{:S(2)}, u32[]{:S(2)}) collective-permute-start(f32[256,512]{1,0:T(8,128)S(1)} %add.15), channel_id=1, source_target_pairs={{0,8},{4,20},{8,0},{12,28},{16,24},{20,4},{24,16},{28,12},{1,9},{5... | collective-permute-start | bytes 1572872 | tf_op jit(solution)/shard_map/link_straight/ppermute | solution.py:378
  18.3 3.5 %collective-permute-done.12.refs_2_ = f32[256,512]{1,0:T(8,128)S(1)} collective-permute-done((f32[256,512]{1,0:T(8,128)S(1)}, f32[256,512]{1,0:T(8,128)S(1)}, u32[]{:S(2)}, u32[]{:S(2)}) %collective-permute-start.12) | collective-permute-done | bytes 524320 | tf_op jit(solution)/shard_map/link_corner/ppermute | solution.py:378
  21.8 2.1 %collective-permute-start.7 = (f32[256,512]{1,0:T(8,128)S(1)}, f32[256,512]{1,0:T(8,128)S(1)}, u32[]{:S(2)}, u32[]{:S(2)}) collective-permute-start(f32[256,512]{1,0:T(8,128)S(1)} %add.14), channel_id=1, source_target_pairs={{0,16},{4,12},{8,24},{12,4},{16,0},{20,28},{24,8},{28,20},{1,17},{... | collective-permute-start | bytes 1572872 | tf_op jit(solution)/shard_map/side_side/ppermute | solution.py:378
  24.1 6.7 %collective-permute-done.3.refs_2_ = f32[256,512]{1,0:T(8,128)S(1)} collective-permute-done((f32[256,512]{1,0:T(8,128)S(1)}, f32[256,512]{1,0:T(8,128)S(1)}, u32[]{:S(2)}, u32[]{:S(2)}) %collective-permute-start.3) | collective-permute-done | bytes 524320 | tf_op jit(solution)/shard_map/link_straight/ppermute | solution.py:378
  30.9 1.5 %square.1 = (f32[512,512]{1,0:T(8,128)S(1)}, f32[512,512]{1,0:T(8,128)S(1)}) custom-call(f32[512,512]{1,0:T(8,128)S(1)} %bitcast.8, f32[512,512]{1,0:T(8,128)S(1)} %bitcast.11), custom_call_target="tpu_custom_call" | custom-call | flops 1610612736 | bytes 4194304 | tf_op jit(solution)/shard_map/square/pallas_call | solution.py:129
  32.4 9.6 %collective-permute-done.10.refs_2_ = f32[256,512]{1,0:T(8,128)S(1)} collective-permute-done((f32[256,512]{1,0:T(8,128)S(1)}, f32[256,512]{1,0:T(8,128)S(1)}, u32[]{:S(2)}, u32[]{:S(2)}) %collective-permute-start.10) | collective-permute-done | bytes 524320 | tf_op jit(solution)/shard_map/link_straight/ppermute | solution.py:378
  42.3 1.4 %collective-permute-done.13.arrival_ref = f32[256,512]{1,0:T(8,128)S(1)} collective-permute-done((f32[256,512]{1,0:T(8,128)S(1)}, f32[256,512]{1,0:T(8,128)S(1)}, u32[]{:S(2)}, u32[]{:S(2)}) %collective-permute-start.13) | collective-permute-done | bytes 524320 | tf_op jit(solution)/shard_map/side_side/ppermute | solution.py:378
  44.4 0.8 collective-permute-done.14.refs_1_
  45.2 3.0 %collective-permute-start.15 = (f32[8,128]{1,0:T(8,128)S(1)}, f32[8,128]{1,0:T(8,128)S(1)}, u32[]{:S(2)}, u32[]{:S(2)}) collective-permute-start(f32[8,128]{1,0:T(8,128)S(1)} %sum.3.refs_0_), channel_id=1, source_target_pairs={{0,24},{4,28},{8,16},{12,20},{16,8},{20,12},{24,0},{28,4},{1,25},{... | collective-permute-start | bytes 12296 | tf_op jit(solution)/shard_map/chip_norm/ppermute | solution.py:378
  48.8 1.5 %gram.1 = (f32[512,512]{1,0:T(8,128)S(1)}, f32[512,512]{1,0:T(8,128)S(1)}) custom-call(f32[256,512]{1,0:T(8,128)S(1)} %get-tuple-element.76.upper_ref, f32[256,512]{1,0:T(8,128)S(1)} %get-tuple-element.74.lower_ref), custom_call_target="tpu_custom_call" | custom-call | flops 1610612736 | bytes 3145728 | tf_op jit(solution)/shard_map/gram/pallas_call | solution.py:129
  50.3 1.7 %mix.2 = (f32[512,512]{1,0:T(8,128)S(1)}, f32[512,512]{1,0:T(8,128)S(1)}) custom-call(f32[512,512]{1,0:T(8,128)S(1)} %bitcast.9, f32[512,512]{1,0:T(8,128)S(1)} %get-tuple-element.77.gram_ref.refs_1_), custom_call_target="tpu_custom_call" | custom-call | flops 1610612736 | bytes 4194304 | tf_op jit(solution)/shard_map/mix/pallas_call | solution.py:129
  54.3 1.8 %mix.3 = (f32[512,512]{1,0:T(8,128)S(1)}, f32[512,512]{1,0:T(8,128)S(1)}) custom-call(f32[512,512]{1,0:T(8,128)S(1)} %bitcast.12, f32[512,512]{1,0:T(8,128)S(1)} %get-tuple-element.80.gram_ref.refs_6_), custom_call_target="tpu_custom_call" | custom-call | flops 1610612736 | bytes 4194304 | tf_op jit(solution)/shard_map/mix/pallas_call | solution.py:129
  56.1 1.5 %collective-permute-start.21 = (f32[8,128]{1,0:T(8,128)S(1)}, f32[8,128]{1,0:T(8,128)S(1)}, u32[]{:S(2)}, u32[]{:S(2)}) collective-permute-start(f32[8,128]{1,0:T(8,128)S(1)} %sum.5.refs_10_), channel_id=1, source_target_pairs={{4,0},{12,8},{20,16},{28,24},{5,1},{13,9},{21,17},{29,25},{6,2},{1... | collective-permute-start | bytes 12296 | tf_op jit(solution)/shard_map/core_norm/ppermute | solution.py:378
  57.6 8.0 %collective-permute-done.21.refs_11_ = f32[8,128]{1,0:T(8,128)S(1)} collective-permute-done((f32[8,128]{1,0:T(8,128)S(1)}, f32[8,128]{1,0:T(8,128)S(1)}, u32[]{:S(2)}, u32[]{:S(2)}) %collective-permute-start.21) | collective-permute-done | bytes 4128 | tf_op jit(solution)/shard_map/core_norm/ppermute | solution.py:378
  65.6 6.1 %update.1 = (f32[512,512]{1,0:T(8,128)S(1)}, f32[256,512]{1,0:T(8,128)S(1)}, f32[256,512]{1,0:T(8,128)S(1)}) custom-call(f32[256,512]{1,0:T(8,128)S(1)} %get-tuple-element.76.upper_ref, f32[256,512]{1,0:T(8,128)S(1)} %get-tuple-element.74.lower_ref, f32[8,128]{1,0:T(8,128)S(1)} %get-tuple-element.75.refs_0_.block_norm_ref, f32[512,512]{1,0:T(8,128)S(1)} %bitcast.10, ...), custom_call_target="tpu_custom_call" | custom-call | flops 4831838208 | bytes 13647872 | tf_op jit(solution)/shard_map/update/pallas_call | solution.py:129
  71.9 1.5 %collective-permute-start.27 = (f32[256,512]{1,0:T(8,128)S(1)}, f32[256,512]{1,0:T(8,128)S(1)}, u32[]{:S(2)}, u32[]{:S(2)}) collective-permute-start(f32[256,512]{1,0:T(8,128)S(1)} %get-tuple-element.89), channel_id=1, source_target_pairs={{0,8},{4,20},{8,0},{12,28},{16,24},{20,4},{24,16},{28,12},{1,9},{5... | collective-permute-start | bytes 1572872 | tf_op jit(solution)/shard_map/link_own/ppermute | solution.py:378
  73.9 7.2 %collective-permute-done.27.refs_2_ = f32[256,512]{1,0:T(8,128)S(1)} collective-permute-done((f32[256,512]{1,0:T(8,128)S(1)}, f32[256,512]{1,0:T(8,128)S(1)}, u32[]{:S(2)}, u32[]{:S(2)}) %collective-permute-start.27) | collective-permute-done | bytes 524320 | tf_op jit(solution)/shard_map/link_own/ppermute | solution.py:378
  81.0 1.5 %collective-permute-start.28 = (f32[512,512]{1,0:T(8,128)S(1)}, f32[512,512]{1,0:T(8,128)S(1)}, u32[]{:S(2)}, u32[]{:S(2)}) collective-permute-start(f32[512,512]{1,0:T(8,128)S(1)} %collective-permute-done.23.refs_1_), channel_id=1, source_target_pairs={{0,8},{4,20},{8,0},{12,28},{16,24},{20,4},{24,16},{28,12},{1,9},{5... | collective-permute-start | bytes 3145736 | tf_op jit(solution)/shard_map/link_sibling/ppermute | solution.py:378
  82.5 4.1 %collective-permute-done.22.refs_3_ = f32[256,512]{1,0:T(8,128)S(1)} collective-permute-done((f32[256,512]{1,0:T(8,128)S(1)}, f32[256,512]{1,0:T(8,128)S(1)}, u32[]{:S(2)}, u32[]{:S(2)}) %collective-permute-start.22) | collective-permute-done | bytes 524320 | tf_op jit(solution)/shard_map/link_own/ppermute | solution.py:378
  86.7 1.5 %collective-permute-start.31 = (f32[256,512]{1,0:T(8,128)S(1)}, f32[256,512]{1,0:T(8,128)S(1)}, u32[]{:S(2)}, u32[]{:S(2)}) collective-permute-start(f32[256,512]{1,0:T(8,128)S(1)} %collective-permute-done.30.refs_4_), channel_id=1, source_target_pairs={{0,8},{4,20},{8,0},{12,28},{16,24},{20,4},{24,16},{28,12},{1,9},{5... | collective-permute-start | bytes 1572872 | tf_op jit(solution)/shard_map/link_relayed/ppermute | solution.py:378
  88.1 9.7 %collective-permute-done.28.refs_6_ = f32[512,512]{1,0:T(8,128)S(1)} collective-permute-done((f32[512,512]{1,0:T(8,128)S(1)}, f32[512,512]{1,0:T(8,128)S(1)}, u32[]{:S(2)}, u32[]{:S(2)}) %collective-permute-start.28) | collective-permute-done | bytes 1048608 | tf_op jit(solution)/shard_map/link_sibling/ppermute | solution.py:378
  97.9 1.5 %collective-permute-start.25 = (f32[256,512]{1,0:T(8,128)S(1)}, f32[256,512]{1,0:T(8,128)S(1)}, u32[]{:S(2)}, u32[]{:S(2)}) collective-permute-start(f32[256,512]{1,0:T(8,128)S(1)} %collective-permute-done.24.refs_5_), channel_id=1, source_target_pairs={{0,8},{4,20},{8,0},{12,28},{16,24},{20,4},{24,16},{28,12},{1,9},{5... | collective-permute-start | bytes 1572872 | tf_op jit(solution)/shard_map/link_relayed/ppermute | solution.py:378
  99.4 3.0 %assemble.3.refs_4_ = f32[512,3072]{1,0:T(8,128)} custom-call(s32[7]{0:T(128)S(1)} %pad_add_fusion.places_ref, f32[512,512]{1,0:T(8,128)S(1)} %get-tuple-element.87.refs_0_, f32[512,512]{1,0:T(8,128)S(1)} %collective-permute-done.23.refs_1_, f32[256,512]{1,0:T(8,128)S(1)} %collective-permute-done.27.refs_2_, f32[256,512]{1,0:T(8,128)S(1)} %collective-permute-done.22.refs_3_, ...), custom_call_target="tpu_custom_call" | custom-call | bytes 14680064 | tf_op jit(solution)/shard_map/assemble/pallas_call | solution.py:349
  102.4 1.2 %collective-permute-done.31.refs_1_ = f32[256,512]{1,0:T(8,128)S(1)} collective-permute-done((f32[256,512]{1,0:T(8,128)S(1)}, f32[256,512]{1,0:T(8,128)S(1)}, u32[]{:S(2)}, u32[]{:S(2)}) %collective-permute-start.31) | collective-permute-done | bytes 524320 | tf_op jit(solution)/shard_map/link_relayed/ppermute | solution.py:378
  103.5 5.6 %collective-permute-done.25.refs_2_ = f32[256,512]{1,0:T(8,128)S(1)} collective-permute-done((f32[256,512]{1,0:T(8,128)S(1)}, f32[256,512]{1,0:T(8,128)S(1)}, u32[]{:S(2)}, u32[]{:S(2)}) %collective-permute-start.25) | collective-permute-done | bytes 524320 | tf_op jit(solution)/shard_map/link_relayed/ppermute | solution.py:378
  109.1 1.6 %assemble.4.refs_1_ = f32[512,3072]{1,0:T(8,128)} custom-call(s32[7]{0:T(128)S(1)} %pad_add_fusion.places_ref, f32[512,512]{1,0:T(8,128)S(1)} %collective-permute-done.29.refs_0_, f32[256,512]{1,0:T(8,128)S(1)} %collective-permute-done.31.refs_1_, f32[256,512]{1,0:T(8,128)S(1)} %collective-permute-done.25.refs_2_, ...), custom_call_target="tpu_custom_call", output_to_operand_aliasing={{}: (5, {})} | custom-call | bytes 8388608 | tf_op jit(solution)/shard_map/assemble/pallas_call | solution.py:349
  (67 shorter events, 10.5 us)
Async XLA Ops:
  3.4 2.3 %collective-permute-start.5 = (f32[256,512]{1,0:T(8,128)S(1)}, f32[256,512]{1,0:T(8,128)S(1)}, u32[]{:S(2)}, u32[]{:S(2)}) collective-permute-start(f32[256,512]{1,0:T(8,128)S(1)} %get-tuple-element.64), channel_id=1, source_target_pairs={{0,4},{4,0},{8,12},{12,8},{16,20},{20,16},{24,28},{28,24},{1,5},{5... | collective-permute-start | bytes 1572872 | tf_op jit(solution)/shard_map/core_corner/ppermute | solution.py:378
  3.9 2.3 %collective-permute-start = (f32[256,512]{1,0:T(8,128)S(1)}, f32[256,512]{1,0:T(8,128)S(1)}, u32[]{:S(2)}, u32[]{:S(2)}) collective-permute-start(f32[256,512]{1,0:T(8,128)S(1)} %get-tuple-element.50), channel_id=1, source_target_pairs={{0,4},{4,0},{8,12},{12,8},{16,20},{20,16},{24,28},{28,24},{1,5},{5... | collective-permute-start | bytes 1572872 | tf_op jit(solution)/shard_map/core_corner/ppermute | solution.py:378
  4.0 5.1 %collective-permute-start.2 = (f32[256,512]{1,0:T(8,128)S(1)}, f32[256,512]{1,0:T(8,128)S(1)}, u32[]{:S(2)}, u32[]{:S(2)}) collective-permute-start(f32[256,512]{1,0:T(8,128)S(1)} %get-tuple-element.55), channel_id=1, source_target_pairs={{0,4},{4,0},{8,12},{12,8},{16,20},{20,16},{24,28},{28,24},{1,5},{5... | collective-permute-start | bytes 1572872 | tf_op jit(solution)/shard_map/core_straight/ppermute | solution.py:378
  5.1 4.7 %collective-permute-start.4 = (f32[256,512]{1,0:T(8,128)S(1)}, f32[256,512]{1,0:T(8,128)S(1)}, u32[]{:S(2)}, u32[]{:S(2)}) collective-permute-start(f32[256,512]{1,0:T(8,128)S(1)} %get-tuple-element.62), channel_id=1, source_target_pairs={{0,4},{4,0},{8,12},{12,8},{16,20},{20,16},{24,28},{28,24},{1,5},{5... | collective-permute-start | bytes 1572872 | tf_op jit(solution)/shard_map/core_side/ppermute | solution.py:378
  5.3 5.4 %collective-permute-start.9 = (f32[256,512]{1,0:T(8,128)S(1)}, f32[256,512]{1,0:T(8,128)S(1)}, u32[]{:S(2)}, u32[]{:S(2)}) collective-permute-start(f32[256,512]{1,0:T(8,128)S(1)} %get-tuple-element.70), channel_id=1, source_target_pairs={{0,4},{4,0},{8,12},{12,8},{16,20},{20,16},{24,28},{28,24},{1,5},{5... | collective-permute-start | bytes 1572872 | tf_op jit(solution)/shard_map/core_straight/ppermute | solution.py:378
  5.7 6.5 %collective-permute-start.11 = (f32[256,512]{1,0:T(8,128)S(1)}, f32[256,512]{1,0:T(8,128)S(1)}, u32[]{:S(2)}, u32[]{:S(2)}) collective-permute-start(f32[256,512]{1,0:T(8,128)S(1)} %get-tuple-element.72), channel_id=1, source_target_pairs={{0,4},{4,0},{8,12},{12,8},{16,20},{20,16},{24,28},{28,24},{1,5},{5... | collective-permute-start | bytes 1572872 | tf_op jit(solution)/shard_map/core_side/ppermute | solution.py:378
  6.2 10.0 %collective-permute-start.6 = (f32[256,512]{1,0:T(8,128)S(1)}, f32[256,512]{1,0:T(8,128)S(1)}, u32[]{:S(2)}, u32[]{:S(2)}) collective-permute-start(f32[256,512]{1,0:T(8,128)S(1)} %add.13), channel_id=1, source_target_pairs={{0,8},{4,20},{8,0},{12,28},{16,24},{20,4},{24,16},{28,12},{1,9},{5... | collective-permute-start | bytes 1572872 | tf_op jit(solution)/shard_map/link_corner/ppermute | solution.py:378
  9.1 12.7 %collective-permute-start.12 = (f32[256,512]{1,0:T(8,128)S(1)}, f32[256,512]{1,0:T(8,128)S(1)}, u32[]{:S(2)}, u32[]{:S(2)}) collective-permute-start(f32[256,512]{1,0:T(8,128)S(1)} %add.10), channel_id=1, source_target_pairs={{0,8},{4,20},{8,0},{12,28},{16,24},{20,4},{24,16},{28,12},{1,9},{5... | collective-permute-start | bytes 1572872 | tf_op jit(solution)/shard_map/link_corner/ppermute | solution.py:378
  9.8 14.2 %collective-permute-start.1 = (f32[256,512]{1,0:T(8,128)S(1)}, f32[256,512]{1,0:T(8,128)S(1)}, u32[]{:S(2)}, u32[]{:S(2)}) collective-permute-start(f32[256,512]{1,0:T(8,128)S(1)} %get-tuple-element.53), channel_id=1, source_target_pairs={{0,4},{4,0},{8,12},{12,8},{16,20},{20,16},{24,28},{28,24},{1,5},{5... | collective-permute-start | bytes 1572872 | tf_op jit(solution)/shard_map/core_self/ppermute | solution.py:378
  10.7 20.1 %collective-permute-start.3 = (f32[256,512]{1,0:T(8,128)S(1)}, f32[256,512]{1,0:T(8,128)S(1)}, u32[]{:S(2)}, u32[]{:S(2)}) collective-permute-start(f32[256,512]{1,0:T(8,128)S(1)} %add.11), channel_id=1, source_target_pairs={{0,8},{4,20},{8,0},{12,28},{16,24},{20,4},{24,16},{28,12},{1,9},{5... | collective-permute-start | bytes 1572872 | tf_op jit(solution)/shard_map/link_straight/ppermute | solution.py:378
  12.2 20.2 %collective-permute-start.8 = (f32[256,512]{1,0:T(8,128)S(1)}, f32[256,512]{1,0:T(8,128)S(1)}, u32[]{:S(2)}, u32[]{:S(2)}) collective-permute-start(f32[256,512]{1,0:T(8,128)S(1)} %get-tuple-element.68), channel_id=1, source_target_pairs={{0,4},{4,0},{8,12},{12,8},{16,20},{20,16},{24,28},{28,24},{1,5},{5... | collective-permute-start | bytes 1572872 | tf_op jit(solution)/shard_map/core_self/ppermute | solution.py:378
  16.2 25.8 %collective-permute-start.10 = (f32[256,512]{1,0:T(8,128)S(1)}, f32[256,512]{1,0:T(8,128)S(1)}, u32[]{:S(2)}, u32[]{:S(2)}) collective-permute-start(f32[256,512]{1,0:T(8,128)S(1)} %add.15), channel_id=1, source_target_pairs={{0,8},{4,20},{8,0},{12,28},{16,24},{20,4},{24,16},{28,12},{1,9},{5... | collective-permute-start | bytes 1572872 | tf_op jit(solution)/shard_map/link_straight/ppermute | solution.py:378
  21.8 20.3 %collective-permute-start.7 = (f32[256,512]{1,0:T(8,128)S(1)}, f32[256,512]{1,0:T(8,128)S(1)}, u32[]{:S(2)}, u32[]{:S(2)}) collective-permute-start(f32[256,512]{1,0:T(8,128)S(1)} %add.14), channel_id=1, source_target_pairs={{0,16},{4,12},{8,24},{12,4},{16,0},{20,28},{24,8},{28,20},{1,17},{... | collective-permute-start | bytes 1572872 | tf_op jit(solution)/shard_map/side_side/ppermute | solution.py:378
  24.0 19.8 %collective-permute-start.13 = (f32[256,512]{1,0:T(8,128)S(1)}, f32[256,512]{1,0:T(8,128)S(1)}, u32[]{:S(2)}, u32[]{:S(2)}) collective-permute-start(f32[256,512]{1,0:T(8,128)S(1)} %add.17), channel_id=1, source_target_pairs={{0,16},{4,12},{8,24},{12,4},{16,0},{20,28},{24,8},{28,20},{1,17},{... | collective-permute-start | bytes 1572872 | tf_op jit(solution)/shard_map/side_side/ppermute | solution.py:378
  45.2 6.8 %collective-permute-start.15 = (f32[8,128]{1,0:T(8,128)S(1)}, f32[8,128]{1,0:T(8,128)S(1)}, u32[]{:S(2)}, u32[]{:S(2)}) collective-permute-start(f32[8,128]{1,0:T(8,128)S(1)} %sum.3.refs_0_), channel_id=1, source_target_pairs={{0,24},{4,28},{8,16},{12,20},{16,8},{20,12},{24,0},{28,4},{1,25},{... | collective-permute-start | bytes 12296 | tf_op jit(solution)/shard_map/chip_norm/ppermute | solution.py:378
  48.2 3.9 %collective-permute-start.16 = (f32[8,128]{1,0:T(8,128)S(1)}, f32[8,128]{1,0:T(8,128)S(1)}, u32[]{:S(2)}, u32[]{:S(2)}) collective-permute-start(f32[8,128]{1,0:T(8,128)S(1)} %sum.3.refs_0_), channel_id=1, source_target_pairs={{0,16},{4,20},{8,24},{12,28},{16,0},{20,4},{24,8},{28,12},{1,17},{... | collective-permute-start | bytes 12296 | tf_op jit(solution)/shard_map/chip_norm/ppermute | solution.py:378
  48.7 3.6 %collective-permute-start.17 = (f32[8,128]{1,0:T(8,128)S(1)}, f32[8,128]{1,0:T(8,128)S(1)}, u32[]{:S(2)}, u32[]{:S(2)}) collective-permute-start(f32[8,128]{1,0:T(8,128)S(1)} %sum.3.refs_0_), channel_id=1, source_target_pairs={{0,8},{4,12},{8,0},{12,4},{16,24},{20,28},{24,16},{28,20},{1,9},{5... | collective-permute-start | bytes 12296 | tf_op jit(solution)/shard_map/chip_norm/ppermute | solution.py:378
  52.3 3.8 %collective-permute-start.18 = (f32[8,128]{1,0:T(8,128)S(1)}, f32[8,128]{1,0:T(8,128)S(1)}, u32[]{:S(2)}, u32[]{:S(2)}) collective-permute-start(f32[8,128]{1,0:T(8,128)S(1)} %sum.4.refs_0_), channel_id=1, source_target_pairs={{4,6},{5,7},{6,4},{7,5},{12,14},{13,15},{14,12},{15,13},{20,22},{2... | collective-permute-start | bytes 12296 | tf_op jit(solution)/shard_map/group_norm/ppermute | solution.py:439
  53.0 3.1 %collective-permute-start.19 = (f32[8,128]{1,0:T(8,128)S(1)}, f32[8,128]{1,0:T(8,128)S(1)}, u32[]{:S(2)}, u32[]{:S(2)}) collective-permute-start(f32[8,128]{1,0:T(8,128)S(1)} %sum.4.refs_0_), channel_id=1, source_target_pairs={{4,7},{5,6},{6,5},{7,4},{12,15},{13,14},{14,13},{15,12},{20,23},{2... | collective-permute-start | bytes 12296 | tf_op jit(solution)/shard_map/group_norm/ppermute | solution.py:439
  53.6 2.5 %collective-permute-start.20 = (f32[8,128]{1,0:T(8,128)S(1)}, f32[8,128]{1,0:T(8,128)S(1)}, u32[]{:S(2)}, u32[]{:S(2)}) collective-permute-start(f32[8,128]{1,0:T(8,128)S(1)} %sum.4.refs_0_), channel_id=1, source_target_pairs={{4,5},{5,4},{6,7},{7,6},{12,13},{13,12},{14,15},{15,14},{20,21},{2... | collective-permute-start | bytes 12296 | tf_op jit(solution)/shard_map/group_norm/ppermute | solution.py:439
  56.1 9.4 %collective-permute-start.21 = (f32[8,128]{1,0:T(8,128)S(1)}, f32[8,128]{1,0:T(8,128)S(1)}, u32[]{:S(2)}, u32[]{:S(2)}) collective-permute-start(f32[8,128]{1,0:T(8,128)S(1)} %sum.5.refs_10_), channel_id=1, source_target_pairs={{4,0},{12,8},{20,16},{28,24},{5,1},{13,9},{21,17},{29,25},{6,2},{1... | collective-permute-start | bytes 12296 | tf_op jit(solution)/shard_map/core_norm/ppermute | solution.py:378
  71.6 9.4 %collective-permute-start.23 = (f32[512,512]{1,0:T(8,128)S(1)}, f32[512,512]{1,0:T(8,128)S(1)}, u32[]{:S(2)}, u32[]{:S(2)}) collective-permute-start(f32[512,512]{1,0:T(8,128)S(1)} %get-tuple-element.87.refs_0_), channel_id=1, source_target_pairs={{0,4},{4,0},{8,12},{12,8},{16,20},{20,16},{24,28},{28,24},{1,5},{5... | collective-permute-start | bytes 3145736 | tf_op jit(solution)/shard_map/core_own/ppermute | solution.py:378
  71.9 9.2 %collective-permute-start.27 = (f32[256,512]{1,0:T(8,128)S(1)}, f32[256,512]{1,0:T(8,128)S(1)}, u32[]{:S(2)}, u32[]{:S(2)}) collective-permute-start(f32[256,512]{1,0:T(8,128)S(1)} %get-tuple-element.89), channel_id=1, source_target_pairs={{0,8},{4,20},{8,0},{12,28},{16,24},{20,4},{24,16},{28,12},{1,9},{5... | collective-permute-start | bytes 1572872 | tf_op jit(solution)/shard_map/link_own/ppermute | solution.py:378
  73.3 13.3 %collective-permute-start.22 = (f32[256,512]{1,0:T(8,128)S(1)}, f32[256,512]{1,0:T(8,128)S(1)}, u32[]{:S(2)}, u32[]{:S(2)}) collective-permute-start(f32[256,512]{1,0:T(8,128)S(1)} %get-tuple-element.86), channel_id=1, source_target_pairs={{0,8},{4,20},{8,0},{12,28},{16,24},{20,4},{24,16},{28,12},{1,9},{5... | collective-permute-start | bytes 1572872 | tf_op jit(solution)/shard_map/link_own/ppermute | solution.py:378
  81.0 16.8 %collective-permute-start.28 = (f32[512,512]{1,0:T(8,128)S(1)}, f32[512,512]{1,0:T(8,128)S(1)}, u32[]{:S(2)}, u32[]{:S(2)}) collective-permute-start(f32[512,512]{1,0:T(8,128)S(1)} %collective-permute-done.23.refs_1_), channel_id=1, source_target_pairs={{0,8},{4,20},{8,0},{12,28},{16,24},{20,4},{24,16},{28,12},{1,9},{5... | collective-permute-start | bytes 3145736 | tf_op jit(solution)/shard_map/link_sibling/ppermute | solution.py:378
  82.5 4.1 %collective-permute-start.30 = (f32[256,512]{1,0:T(8,128)S(1)}, f32[256,512]{1,0:T(8,128)S(1)}, u32[]{:S(2)}, u32[]{:S(2)}) collective-permute-start(f32[256,512]{1,0:T(8,128)S(1)} %collective-permute-done.27.refs_2_), channel_id=1, source_target_pairs={{0,4},{4,0},{8,12},{12,8},{16,20},{20,16},{24,28},{28,24},{1,5},{5... | collective-permute-start | bytes 1572872 | tf_op jit(solution)/shard_map/core_first/ppermute | solution.py:378
  86.7 11.2 %collective-permute-start.24 = (f32[256,512]{1,0:T(8,128)S(1)}, f32[256,512]{1,0:T(8,128)S(1)}, u32[]{:S(2)}, u32[]{:S(2)}) collective-permute-start(f32[256,512]{1,0:T(8,128)S(1)} %collective-permute-done.22.refs_3_), channel_id=1, source_target_pairs={{0,4},{4,0},{8,12},{12,8},{16,20},{20,16},{24,28},{28,24},{1,5},{5... | collective-permute-start | bytes 1572872 | tf_op jit(solution)/shard_map/core_first/ppermute | solution.py:378
  86.7 16.8 %collective-permute-start.31 = (f32[256,512]{1,0:T(8,128)S(1)}, f32[256,512]{1,0:T(8,128)S(1)}, u32[]{:S(2)}, u32[]{:S(2)}) collective-permute-start(f32[256,512]{1,0:T(8,128)S(1)} %collective-permute-done.30.refs_4_), channel_id=1, source_target_pairs={{0,8},{4,20},{8,0},{12,28},{16,24},{20,4},{24,16},{28,12},{1,9},{5... | collective-permute-start | bytes 1572872 | tf_op jit(solution)/shard_map/link_relayed/ppermute | solution.py:378
  97.9 11.2 %collective-permute-start.29 = (f32[512,512]{1,0:T(8,128)S(1)}, f32[512,512]{1,0:T(8,128)S(1)}, u32[]{:S(2)}, u32[]{:S(2)}) collective-permute-start(f32[512,512]{1,0:T(8,128)S(1)} %collective-permute-done.28.refs_6_), channel_id=1, source_target_pairs={{0,4},{4,0},{8,12},{12,8},{16,20},{20,16},{24,28},{28,24},{1,5},{5... | collective-permute-start | bytes 3145736 | tf_op jit(solution)/shard_map/core_second/ppermute | solution.py:378
  97.9 11.2 %collective-permute-start.25 = (f32[256,512]{1,0:T(8,128)S(1)}, f32[256,512]{1,0:T(8,128)S(1)}, u32[]{:S(2)}, u32[]{:S(2)}) collective-permute-start(f32[256,512]{1,0:T(8,128)S(1)} %collective-permute-done.24.refs_5_), channel_id=1, source_target_pairs={{0,8},{4,20},{8,0},{12,28},{16,24},{20,4},{24,16},{28,12},{1,9},{5... | collective-permute-start | bytes 1572872 | tf_op jit(solution)/shard_map/link_relayed/ppermute | solution.py:378
  103.5 5.6 %collective-permute-start.32 = (f32[256,512]{1,0:T(8,128)S(1)}, f32[256,512]{1,0:T(8,128)S(1)}, u32[]{:S(2)}, u32[]{:S(2)}) collective-permute-start(f32[256,512]{1,0:T(8,128)S(1)} %collective-permute-done.31.refs_1_), channel_id=1, source_target_pairs={{0,4},{4,0},{8,12},{12,8},{16,20},{20,16},{24,28},{28,24},{1,5},{5... | collective-permute-start | bytes 1572872 | tf_op jit(solution)/shard_map/core_relayed/ppermute | solution.py:378
  109.1 1.9 %collective-permute-start.26 = (f32[256,512]{1,0:T(8,128)S(1)}, f32[256,512]{1,0:T(8,128)S(1)}, u32[]{:S(2)}, u32[]{:S(2)}) collective-permute-start(f32[256,512]{1,0:T(8,128)S(1)} %collective-permute-done.25.refs_2_), channel_id=1, source_target_pairs={{0,4},{4,0},{8,12},{12,8},{16,20},{20,16},{24,28},{28,24},{1,5},{5... | collective-permute-start | bytes 1572872 | tf_op jit(solution)/shard_map/core_relayed/ppermute | solution.py:378
  (5 other events, 52.5 us)

commit v19 on v17

--- a/solution.py
+++ b/solution.py
@@ -434,20 +434,24 @@
     sides[1] += tuple(mix_call(*sides[1][:2]))
     whole, *own = update_call(block, block_norm, *sides, norms, entry_count)
 
-    core_own = to_core(whole, "own")
     first = [to_link(value, "own") for value in own]
-    core_first = [to_core(after(value, core_own), "first") for value in first]
-    second = to_link(after(core_own, first[0]), "sibling")
-    core_second = to_core(second, "second")
+    core_own = [to_core(value, "own") for value in own]
+    core_first = [to_core(value, "first") for value in first]
+    second = [to_link(core_own[0], "sibling"), to_link(core_own[1], "sibling")]
+    core_second = [to_core(value, "second") for value in second]
     relayed = [to_link(value, "relayed") for value in core_first]
-    held = [(("self", 0, None), whole), (("self", 1, None), core_own)]
+    held = [(("self", 0, None), whole)]
+    held += [(("self", 1, half), core_own[half]) for half in HALVES]
     held += [(("straight", 0, half), first[half]) for half in HALVES]
     held += [(("straight", 1, half), core_first[half]) for half in HALVES]
-    crossed = [(("cross", 0, None), second), (("cross", 1, None), core_second)]
-    result = assemble(None, *held, crossed[0])
+    held += [(("cross", 0, half), second[half]) for half in HALVES]
+    result = assemble(None, *held)
     core_relayed = [to_core(after(relayed[0], result), "relayed"), to_core(relayed[1], "relayed")]
     result = assemble(
-        result, crossed[1], *[(("diagonal", 0, half), relayed[half]) for half in HALVES], (("diagonal", 1, 0), core_relayed[0])
+        result,
+        *[(("cross", 1, half), core_second[half]) for half in HALVES],
+        *[(("diagonal", 0, half), relayed[half]) for half in HALVES],
+        (("diagonal", 1, 0), core_relayed[0]),
     )
     return assemble(result, (("diagonal", 1, 1), core_relayed[1]))
 

time: 108 us -> 111 us (1.028)
  waiting for transfers between devices: 56.9 us -> 60.2 us
    ppermute x29 -> x32, waiting for transfers between devices: 54.8 us -> 58.1 us  [over(): return lax.ppermute(value, 'dp', pairs)]
    ppermute x29 -> x32, starting transfers between devices: 21.9 us -> 21.9 us  [over(): return lax.ppermute(value, 'dp', pairs)]
  transfers between devices with their start and end apart: 32 -> 35, of which waited for: 14 -> 16; matrix products, arithmetic and copies ran while one was open for 0% -> 0% of each run, Pallas kernels for 12% -> 12%
where the time goes in v19:
time: 111 us
  waiting for transfers between devices  60.2 us (54%)
  starting transfers between devices  26.3 us (24%)
  Pallas kernels  21.6 us (19%)
  local copies, waits for them, and re-layouts  1.9 us (2%)
    ppermute x32, waiting for transfers between devices, over(): return lax.ppermute(value, 'dp', pairs)  58.1 us
    ppermute x32, starting transfers between devices, over(): return lax.ppermute(value, 'dp', pairs)  21.9 us
    pallas_call x20, Pallas kernels, local_call(): pl.pallas_call(kernel, in_specs=[pl.BlockSpec(memory_space=pltpu.SMEM)] *...  15.8 us
    pallas_call x3, Pallas kernels, assemble_call(): pl.pallas_call(kernel, in_specs=in_specs, out_specs=pl.BlockSpec(memory_s...  5.75 us
    ppermute x3, starting transfers between devices, paired_body(): norms.append(lax.ppermute(norm, 'mp', pairs))  4.46 us
  transfers between devices with their start and end apart: 35, of which 16 were waited for; matrix products, arithmetic and copies ran while one was open for 0% of the time, Pallas kernels for 12%

profile of v19, /device:TPU:0, one launch (start us, length us, event | category | flops | bytes accessed | tf_op | source)
XLA Modules:
  0.0 111.2 jit_solution(634681611613182047)
XLA Ops:
  0.7 1.9 %copy-done = bf16[1,512,3072]{2,1,0:T(8,128)(2,1)S(1)} copy-done((bf16[1,512,3072]{2,1,0:T(8,128)(2,1)S(1)}, bf16[1,512,3072]{2,1,0:T(8,128)(2,1)}, u32[]{:S(2)}) %copy-start) | copy-done | bytes 3145752
  6.2 2.9 %collective-permute-start.6 = (f32[256,512]{1,0:T(8,128)S(1)}, f32[256,512]{1,0:T(8,128)S(1)}, u32[]{:S(2)}, u32[]{:S(2)}) collective-permute-start(f32[256,512]{1,0:T(8,128)S(1)} %add.13), channel_id=1, source_target_pairs={{0,8},{4,20},{8,0},{12,28},{16,24},{20,4},{24,16},{28,12},{1,9},{5... | collective-permute-start | bytes 1572872 | tf_op jit(solution)/shard_map/link_corner/ppermute | solution.py:376
  10.7 1.5 %collective-permute-start.3 = (f32[256,512]{1,0:T(8,128)S(1)}, f32[256,512]{1,0:T(8,128)S(1)}, u32[]{:S(2)}, u32[]{:S(2)}) collective-permute-start(f32[256,512]{1,0:T(8,128)S(1)} %add.11), channel_id=1, source_target_pairs={{0,8},{4,20},{8,0},{12,28},{16,24},{20,4},{24,16},{28,12},{1,9},{5... | collective-permute-start | bytes 1572872 | tf_op jit(solution)/shard_map/link_straight/ppermute | solution.py:376
  12.6 3.6 %collective-permute-done.6.refs_2_ = f32[256,512]{1,0:T(8,128)S(1)} collective-permute-done((f32[256,512]{1,0:T(8,128)S(1)}, f32[256,512]{1,0:T(8,128)S(1)}, u32[]{:S(2)}, u32[]{:S(2)}) %collective-permute-start.6) | collective-permute-done | bytes 524320 | tf_op jit(solution)/shard_map/link_corner/ppermute | solution.py:376
  16.2 2.0 %collective-permute-start.10 = (f32[256,512]{1,0:T(8,128)S(1)}, f32[256,512]{1,0:T(8,128)S(1)}, u32[]{:S(2)}, u32[]{:S(2)}) collective-permute-start(f32[256,512]{1,0:T(8,128)S(1)} %add.15), channel_id=1, source_target_pairs={{0,8},{4,20},{8,0},{12,28},{16,24},{20,4},{24,16},{28,12},{1,9},{5... | collective-permute-start | bytes 1572872 | tf_op jit(solution)/shard_map/link_straight/ppermute | solution.py:376
  18.3 3.5 %collective-permute-done.12.refs_2_ = f32[256,512]{1,0:T(8,128)S(1)} collective-permute-done((f32[256,512]{1,0:T(8,128)S(1)}, f32[256,512]{1,0:T(8,128)S(1)}, u32[]{:S(2)}, u32[]{:S(2)}) %collective-permute-start.12) | collective-permute-done | bytes 524320 | tf_op jit(solution)/shard_map/link_corner/ppermute | solution.py:376
  21.8 2.1 %collective-permute-start.7 = (f32[256,512]{1,0:T(8,128)S(1)}, f32[256,512]{1,0:T(8,128)S(1)}, u32[]{:S(2)}, u32[]{:S(2)}) collective-permute-start(f32[256,512]{1,0:T(8,128)S(1)} %add.14), channel_id=1, source_target_pairs={{0,16},{4,12},{8,24},{12,4},{16,0},{20,28},{24,8},{28,20},{1,17},{... | collective-permute-start | bytes 1572872 | tf_op jit(solution)/shard_map/side_side/ppermute | solution.py:376
  24.1 6.7 %collective-permute-done.3.refs_2_ = f32[256,512]{1,0:T(8,128)S(1)} collective-permute-done((f32[256,512]{1,0:T(8,128)S(1)}, f32[256,512]{1,0:T(8,128)S(1)}, u32[]{:S(2)}, u32[]{:S(2)}) %collective-permute-start.3) | collective-permute-done | bytes 524320 | tf_op jit(solution)/shard_map/link_straight/ppermute | solution.py:376
  30.9 1.5 %square.1 = (f32[512,512]{1,0:T(8,128)S(1)}, f32[512,512]{1,0:T(8,128)S(1)}) custom-call(f32[512,512]{1,0:T(8,128)S(1)} %bitcast.8, f32[512,512]{1,0:T(8,128)S(1)} %bitcast.11), custom_call_target="tpu_custom_call" | custom-call | flops 1610612736 | bytes 4194304 | tf_op jit(solution)/shard_map/square/pallas_call | solution.py:129
  32.4 9.7 %collective-permute-done.10.refs_2_ = f32[256,512]{1,0:T(8,128)S(1)} collective-permute-done((f32[256,512]{1,0:T(8,128)S(1)}, f32[256,512]{1,0:T(8,128)S(1)}, u32[]{:S(2)}, u32[]{:S(2)}) %collective-permute-start.10) | collective-permute-done | bytes 524320 | tf_op jit(solution)/shard_map/link_straight/ppermute | solution.py:376
  42.3 1.4 %collective-permute-done.13.arrival_ref = f32[256,512]{1,0:T(8,128)S(1)} collective-permute-done((f32[256,512]{1,0:T(8,128)S(1)}, f32[256,512]{1,0:T(8,128)S(1)}, u32[]{:S(2)}, u32[]{:S(2)}) %collective-permute-start.13) | collective-permute-done | bytes 524320 | tf_op jit(solution)/shard_map/side_side/ppermute | solution.py:376
  44.4 0.8 collective-permute-done.14.refs_1_
  45.2 3.0 %collective-permute-start.15 = (f32[8,128]{1,0:T(8,128)S(1)}, f32[8,128]{1,0:T(8,128)S(1)}, u32[]{:S(2)}, u32[]{:S(2)}) collective-permute-start(f32[8,128]{1,0:T(8,128)S(1)} %sum.2.refs_0_), channel_id=1, source_target_pairs={{0,24},{4,28},{8,16},{12,20},{16,8},{20,12},{24,0},{28,4},{1,25},{... | collective-permute-start | bytes 12296 | tf_op jit(solution)/shard_map/chip_norm/ppermute | solution.py:376
  48.8 1.5 %gram.1 = (f32[512,512]{1,0:T(8,128)S(1)}, f32[512,512]{1,0:T(8,128)S(1)}) custom-call(f32[256,512]{1,0:T(8,128)S(1)} %get-tuple-element.71.upper_ref, f32[256,512]{1,0:T(8,128)S(1)} %get-tuple-element.69.lower_ref), custom_call_target="tpu_custom_call" | custom-call | flops 1610612736 | bytes 3145728 | tf_op jit(solution)/shard_map/gram/pallas_call | solution.py:129
  50.3 1.7 %mix.2 = (f32[512,512]{1,0:T(8,128)S(1)}, f32[512,512]{1,0:T(8,128)S(1)}) custom-call(f32[512,512]{1,0:T(8,128)S(1)} %bitcast.9, f32[512,512]{1,0:T(8,128)S(1)} %get-tuple-element.72.gram_ref.refs_1_), custom_call_target="tpu_custom_call" | custom-call | flops 1610612736 | bytes 4194304 | tf_op jit(solution)/shard_map/mix/pallas_call | solution.py:129
  52.3 2.9 %collective-permute-start.18 = (f32[8,128]{1,0:T(8,128)S(1)}, f32[8,128]{1,0:T(8,128)S(1)}, u32[]{:S(2)}, u32[]{:S(2)}) collective-permute-start(f32[8,128]{1,0:T(8,128)S(1)} %sum.3.refs_10_), channel_id=1, source_target_pairs={{0,2},{1,3},{2,0},{3,1},{4,6},{5,7},{6,4},{7,5},{8,10},{9,11},{10,... | collective-permute-start | bytes 12296 | tf_op jit(solution)/shard_map/group_norm/ppermute | solution.py:433
  55.2 1.4 %collective-permute-start.19 = (f32[8,128]{1,0:T(8,128)S(1)}, f32[8,128]{1,0:T(8,128)S(1)}, u32[]{:S(2)}, u32[]{:S(2)}) collective-permute-start(f32[8,128]{1,0:T(8,128)S(1)} %sum.3.refs_10_), channel_id=1, source_target_pairs={{0,3},{1,2},{2,1},{3,0},{4,7},{5,6},{6,5},{7,4},{8,11},{9,10},{10,... | collective-permute-start | bytes 12296 | tf_op jit(solution)/shard_map/group_norm/ppermute | solution.py:433
  56.8 1.7 %mix.3 = (f32[512,512]{1,0:T(8,128)S(1)}, f32[512,512]{1,0:T(8,128)S(1)}) custom-call(f32[512,512]{1,0:T(8,128)S(1)} %bitcast.12, f32[512,512]{1,0:T(8,128)S(1)} %get-tuple-element.75.gram_ref.refs_6_), custom_call_target="tpu_custom_call" | custom-call | flops 1610612736 | bytes 4194304 | tf_op jit(solution)/shard_map/mix/pallas_call | solution.py:129
  58.5 2.1 %collective-permute-done.19.refs_12_ = f32[8,128]{1,0:T(8,128)S(1)} collective-permute-done((f32[8,128]{1,0:T(8,128)S(1)}, f32[8,128]{1,0:T(8,128)S(1)}, u32[]{:S(2)}, u32[]{:S(2)}) %collective-permute-start.19) | collective-permute-done | bytes 4128 | tf_op jit(solution)/shard_map/group_norm/ppermute | solution.py:433
  60.6 6.2 %update.1 = (f32[512,512]{1,0:T(8,128)S(1)}, f32[256,512]{1,0:T(8,128)S(1)}, f32[256,512]{1,0:T(8,128)S(1)}) custom-call(f32[256,512]{1,0:T(8,128)S(1)} %get-tuple-element.71.upper_ref, f32[256,512]{1,0:T(8,128)S(1)} %get-tuple-element.69.lower_ref, f32[8,128]{1,0:T(8,128)S(1)} %get-tuple-element.70.refs_0_.block_norm_ref, f32[512,512]{1,0:T(8,128)S(1)} %bitcast.10, ...), custom_call_target="tpu_custom_call" | custom-call | flops 4831838208 | bytes 13651968 | tf_op jit(solution)/shard_map/update/pallas_call | solution.py:129
  66.8 1.6 %collective-permute-start.31 = (f32[256,512]{1,0:T(8,128)S(1)}, f32[256,512]{1,0:T(8,128)S(1)}, u32[]{:S(2)}, u32[]{:S(2)}) collective-permute-start(f32[256,512]{1,0:T(8,128)S(1)} %get-tuple-element.80), channel_id=1, source_target_pairs={{0,8},{4,20},{8,0},{12,28},{16,24},{20,4},{24,16},{28,12},{1,9},{5... | collective-permute-start | bytes 1572872 | tf_op jit(solution)/shard_map/link_own/ppermute | solution.py:376
  69.4 6.6 %collective-permute-done.31.refs_3_ = f32[256,512]{1,0:T(8,128)S(1)} collective-permute-done((f32[256,512]{1,0:T(8,128)S(1)}, f32[256,512]{1,0:T(8,128)S(1)}, u32[]{:S(2)}, u32[]{:S(2)}) %collective-permute-start.31) | collective-permute-done | bytes 524320 | tf_op jit(solution)/shard_map/link_own/ppermute | solution.py:376
  76.1 5.6 %collective-permute-done.21.refs_4_ = f32[256,512]{1,0:T(8,128)S(1)} collective-permute-done((f32[256,512]{1,0:T(8,128)S(1)}, f32[256,512]{1,0:T(8,128)S(1)}, u32[]{:S(2)}, u32[]{:S(2)}) %collective-permute-start.21) | collective-permute-done | bytes 524320 | tf_op jit(solution)/shard_map/link_own/ppermute | solution.py:376
  81.7 1.5 %collective-permute-start.26 = (f32[256,512]{1,0:T(8,128)S(1)}, f32[256,512]{1,0:T(8,128)S(1)}, u32[]{:S(2)}, u32[]{:S(2)}) collective-permute-start(f32[256,512]{1,0:T(8,128)S(1)} %collective-permute-done.25.refs_1_), channel_id=1, source_target_pairs={{0,8},{4,20},{8,0},{12,28},{16,24},{20,4},{24,16},{28,12},{1,9},{5... | collective-permute-start | bytes 1572872 | tf_op jit(solution)/shard_map/link_sibling/ppermute | solution.py:376
  83.7 1.5 %collective-permute-start.33 = (f32[256,512]{1,0:T(8,128)S(1)}, f32[256,512]{1,0:T(8,128)S(1)}, u32[]{:S(2)}, u32[]{:S(2)}) collective-permute-start(f32[256,512]{1,0:T(8,128)S(1)} %collective-permute-done.32.refs_5_), channel_id=1, source_target_pairs={{0,8},{4,20},{8,0},{12,28},{16,24},{20,4},{24,16},{28,12},{1,9},{5... | collective-permute-start | bytes 1572872 | tf_op jit(solution)/shard_map/link_relayed/ppermute | solution.py:376
  85.8 5.1 %collective-permute-done.26.refs_7_ = f32[256,512]{1,0:T(8,128)S(1)} collective-permute-done((f32[256,512]{1,0:T(8,128)S(1)}, f32[256,512]{1,0:T(8,128)S(1)}, u32[]{:S(2)}, u32[]{:S(2)}) %collective-permute-start.26) | collective-permute-done | bytes 524320 | tf_op jit(solution)/shard_map/link_sibling/ppermute | solution.py:376
  90.9 5.6 %collective-permute-done.29.refs_8_ = f32[256,512]{1,0:T(8,128)S(1)} collective-permute-done((f32[256,512]{1,0:T(8,128)S(1)}, f32[256,512]{1,0:T(8,128)S(1)}, u32[]{:S(2)}, u32[]{:S(2)}) %collective-permute-start.29) | collective-permute-done | bytes 524320 | tf_op jit(solution)/shard_map/link_sibling/ppermute | solution.py:376
  96.5 2.6 %assemble.3.refs_5_ = f32[512,3072]{1,0:T(8,128)} custom-call(s32[7]{0:T(128)S(1)} %pad_add_fusion.places_ref, f32[512,512]{1,0:T(8,128)S(1)} %get-tuple-element.81.refs_0_, f32[256,512]{1,0:T(8,128)S(1)} %collective-permute-done.25.refs_1_, f32[256,512]{1,0:T(8,128)S(1)} %collective-permute-done.28.refs_2_, f32[256,512]{1,0:T(8,128)S(1)} %collective-permute-done.31.refs_3_, ...), custom_call_target="tpu_custom_call" | custom-call | bytes 18874368 | tf_op jit(solution)/shard_map/assemble/pallas_call | solution.py:347
  99.1 3.0 %collective-permute-done.33.refs_2_ = f32[256,512]{1,0:T(8,128)S(1)} collective-permute-done((f32[256,512]{1,0:T(8,128)S(1)}, f32[256,512]{1,0:T(8,128)S(1)}, u32[]{:S(2)}, u32[]{:S(2)}) %collective-permute-start.33) | collective-permute-done | bytes 524320 | tf_op jit(solution)/shard_map/link_relayed/ppermute | solution.py:376
  102.1 5.6 %collective-permute-done.23.refs_3_ = f32[256,512]{1,0:T(8,128)S(1)} collective-permute-done((f32[256,512]{1,0:T(8,128)S(1)}, f32[256,512]{1,0:T(8,128)S(1)}, u32[]{:S(2)}, u32[]{:S(2)}) %collective-permute-start.23) | collective-permute-done | bytes 524320 | tf_op jit(solution)/shard_map/link_relayed/ppermute | solution.py:376
  107.7 1.8 %assemble.4.refs_1_ = f32[512,3072]{1,0:T(8,128)} custom-call(s32[7]{0:T(128)S(1)} %pad_add_fusion.places_ref, f32[256,512]{1,0:T(8,128)S(1)} %collective-permute-done.27.refs_0_, f32[256,512]{1,0:T(8,128)S(1)} %collective-permute-done.30.refs_1_, f32[256,512]{1,0:T(8,128)S(1)} %collective-permute-done.33.refs_2_, ...), custom_call_target="tpu_custom_call", output_to_operand_aliasing={{}: (6, {})} | custom-call | bytes 5242880 | tf_op jit(solution)/shard_map/assemble/pallas_call | solution.py:347
  109.6 1.4 %assemble.5 = f32[512,3072]{1,0:T(8,128)} custom-call(s32[7]{0:T(128)S(1)} %pad_add_fusion.places_ref, f32[256,512]{1,0:T(8,128)S(1)} %collective-permute-done.24.refs_0_, f32[512,3072]{1,0:T(8,128)} %assemble.4.refs_1_), custom_call_target="tpu_custom_call", output_to_operand_aliasing={{}: (2, {})} | custom-call | bytes 1048576 | tf_op jit(solution)/shard_map/assemble/pallas_call | solution.py:347
  (70 shorter events, 10.9 us)
Async XLA Ops:
  3.4 2.3 %collective-permute-start.5 = (f32[256,512]{1,0:T(8,128)S(1)}, f32[256,512]{1,0:T(8,128)S(1)}, u32[]{:S(2)}, u32[]{:S(2)}) collective-permute-start(f32[256,512]{1,0:T(8,128)S(1)} %get-tuple-element.59), channel_id=1, source_target_pairs={{0,4},{4,0},{8,12},{12,8},{16,20},{20,16},{24,28},{28,24},{1,5},{5... | collective-permute-start | bytes 1572872 | tf_op jit(solution)/shard_map/core_corner/ppermute | solution.py:376
  4.0 5.1 %collective-permute-start.2 = (f32[256,512]{1,0:T(8,128)S(1)}, f32[256,512]{1,0:T(8,128)S(1)}, u32[]{:S(2)}, u32[]{:S(2)}) collective-permute-start(f32[256,512]{1,0:T(8,128)S(1)} %get-tuple-element.50), channel_id=1, source_target_pairs={{0,4},{4,0},{8,12},{12,8},{16,20},{20,16},{24,28},{28,24},{1,5},{5... | collective-permute-start | bytes 1572872 | tf_op jit(solution)/shard_map/core_straight/ppermute | solution.py:376
  5.1 4.7 %collective-permute-start.4 = (f32[256,512]{1,0:T(8,128)S(1)}, f32[256,512]{1,0:T(8,128)S(1)}, u32[]{:S(2)}, u32[]{:S(2)}) collective-permute-start(f32[256,512]{1,0:T(8,128)S(1)} %get-tuple-element.57), channel_id=1, source_target_pairs={{0,4},{4,0},{8,12},{12,8},{16,20},{20,16},{24,28},{28,24},{1,5},{5... | collective-permute-start | bytes 1572872 | tf_op jit(solution)/shard_map/core_side/ppermute | solution.py:376
  5.3 5.4 %collective-permute-start.9 = (f32[256,512]{1,0:T(8,128)S(1)}, f32[256,512]{1,0:T(8,128)S(1)}, u32[]{:S(2)}, u32[]{:S(2)}) collective-permute-start(f32[256,512]{1,0:T(8,128)S(1)} %get-tuple-element.65), channel_id=1, source_target_pairs={{0,4},{4,0},{8,12},{12,8},{16,20},{20,16},{24,28},{28,24},{1,5},{5... | collective-permute-start | bytes 1572872 | tf_op jit(solution)/shard_map/core_straight/ppermute | solution.py:376
  5.7 6.5 %collective-permute-start.11 = (f32[256,512]{1,0:T(8,128)S(1)}, f32[256,512]{1,0:T(8,128)S(1)}, u32[]{:S(2)}, u32[]{:S(2)}) collective-permute-start(f32[256,512]{1,0:T(8,128)S(1)} %get-tuple-element.67), channel_id=1, source_target_pairs={{0,4},{4,0},{8,12},{12,8},{16,20},{20,16},{24,28},{28,24},{1,5},{5... | collective-permute-start | bytes 1572872 | tf_op jit(solution)/shard_map/core_side/ppermute | solution.py:376
  6.2 10.0 %collective-permute-start.6 = (f32[256,512]{1,0:T(8,128)S(1)}, f32[256,512]{1,0:T(8,128)S(1)}, u32[]{:S(2)}, u32[]{:S(2)}) collective-permute-start(f32[256,512]{1,0:T(8,128)S(1)} %add.13), channel_id=1, source_target_pairs={{0,8},{4,20},{8,0},{12,28},{16,24},{20,4},{24,16},{28,12},{1,9},{5... | collective-permute-start | bytes 1572872 | tf_op jit(solution)/shard_map/link_corner/ppermute | solution.py:376
  9.1 12.7 %collective-permute-start.12 = (f32[256,512]{1,0:T(8,128)S(1)}, f32[256,512]{1,0:T(8,128)S(1)}, u32[]{:S(2)}, u32[]{:S(2)}) collective-permute-start(f32[256,512]{1,0:T(8,128)S(1)} %add.10), channel_id=1, source_target_pairs={{0,8},{4,20},{8,0},{12,28},{16,24},{20,4},{24,16},{28,12},{1,9},{5... | collective-permute-start | bytes 1572872 | tf_op jit(solution)/shard_map/link_corner/ppermute | solution.py:376
  9.8 14.2 %collective-permute-start.1 = (f32[256,512]{1,0:T(8,128)S(1)}, f32[256,512]{1,0:T(8,128)S(1)}, u32[]{:S(2)}, u32[]{:S(2)}) collective-permute-start(f32[256,512]{1,0:T(8,128)S(1)} %get-tuple-element.48), channel_id=1, source_target_pairs={{0,4},{4,0},{8,12},{12,8},{16,20},{20,16},{24,28},{28,24},{1,5},{5... | collective-permute-start | bytes 1572872 | tf_op jit(solution)/shard_map/core_self/ppermute | solution.py:376
  10.7 20.1 %collective-permute-start.3 = (f32[256,512]{1,0:T(8,128)S(1)}, f32[256,512]{1,0:T(8,128)S(1)}, u32[]{:S(2)}, u32[]{:S(2)}) collective-permute-start(f32[256,512]{1,0:T(8,128)S(1)} %add.11), channel_id=1, source_target_pairs={{0,8},{4,20},{8,0},{12,28},{16,24},{20,4},{24,16},{28,12},{1,9},{5... | collective-permute-start | bytes 1572872 | tf_op jit(solution)/shard_map/link_straight/ppermute | solution.py:376
  12.2 20.1 %collective-permute-start.8 = (f32[256,512]{1,0:T(8,128)S(1)}, f32[256,512]{1,0:T(8,128)S(1)}, u32[]{:S(2)}, u32[]{:S(2)}) collective-permute-start(f32[256,512]{1,0:T(8,128)S(1)} %get-tuple-element.63), channel_id=1, source_target_pairs={{0,4},{4,0},{8,12},{12,8},{16,20},{20,16},{24,28},{28,24},{1,5},{5... | collective-permute-start | bytes 1572872 | tf_op jit(solution)/shard_map/core_self/ppermute | solution.py:376
  16.2 25.8 %collective-permute-start.10 = (f32[256,512]{1,0:T(8,128)S(1)}, f32[256,512]{1,0:T(8,128)S(1)}, u32[]{:S(2)}, u32[]{:S(2)}) collective-permute-start(f32[256,512]{1,0:T(8,128)S(1)} %add.15), channel_id=1, source_target_pairs={{0,8},{4,20},{8,0},{12,28},{16,24},{20,4},{24,16},{28,12},{1,9},{5... | collective-permute-start | bytes 1572872 | tf_op jit(solution)/shard_map/link_straight/ppermute | solution.py:376
  21.8 20.3 %collective-permute-start.7 = (f32[256,512]{1,0:T(8,128)S(1)}, f32[256,512]{1,0:T(8,128)S(1)}, u32[]{:S(2)}, u32[]{:S(2)}) collective-permute-start(f32[256,512]{1,0:T(8,128)S(1)} %add.14), channel_id=1, source_target_pairs={{0,16},{4,12},{8,24},{12,4},{16,0},{20,28},{24,8},{28,20},{1,17},{... | collective-permute-start | bytes 1572872 | tf_op jit(solution)/shard_map/side_side/ppermute | solution.py:376
  24.0 19.8 %collective-permute-start.13 = (f32[256,512]{1,0:T(8,128)S(1)}, f32[256,512]{1,0:T(8,128)S(1)}, u32[]{:S(2)}, u32[]{:S(2)}) collective-permute-start(f32[256,512]{1,0:T(8,128)S(1)} %add.17), channel_id=1, source_target_pairs={{0,16},{4,12},{8,24},{12,4},{16,0},{20,28},{24,8},{28,20},{1,17},{... | collective-permute-start | bytes 1572872 | tf_op jit(solution)/shard_map/side_side/ppermute | solution.py:376
  45.2 6.8 %collective-permute-start.15 = (f32[8,128]{1,0:T(8,128)S(1)}, f32[8,128]{1,0:T(8,128)S(1)}, u32[]{:S(2)}, u32[]{:S(2)}) collective-permute-start(f32[8,128]{1,0:T(8,128)S(1)} %sum.2.refs_0_), channel_id=1, source_target_pairs={{0,24},{4,28},{8,16},{12,20},{16,8},{20,12},{24,0},{28,4},{1,25},{... | collective-permute-start | bytes 12296 | tf_op jit(solution)/shard_map/chip_norm/ppermute | solution.py:376
  48.2 3.8 %collective-permute-start.16 = (f32[8,128]{1,0:T(8,128)S(1)}, f32[8,128]{1,0:T(8,128)S(1)}, u32[]{:S(2)}, u32[]{:S(2)}) collective-permute-start(f32[8,128]{1,0:T(8,128)S(1)} %sum.2.refs_0_), channel_id=1, source_target_pairs={{0,16},{4,20},{8,24},{12,28},{16,0},{20,4},{24,8},{28,12},{1,17},{... | collective-permute-start | bytes 12296 | tf_op jit(solution)/shard_map/chip_norm/ppermute | solution.py:376
  48.7 3.6 %collective-permute-start.17 = (f32[8,128]{1,0:T(8,128)S(1)}, f32[8,128]{1,0:T(8,128)S(1)}, u32[]{:S(2)}, u32[]{:S(2)}) collective-permute-start(f32[8,128]{1,0:T(8,128)S(1)} %sum.2.refs_0_), channel_id=1, source_target_pairs={{0,8},{4,12},{8,0},{12,4},{16,24},{20,28},{24,16},{28,20},{1,9},{5... | collective-permute-start | bytes 12296 | tf_op jit(solution)/shard_map/chip_norm/ppermute | solution.py:376
  52.3 6.2 %collective-permute-start.18 = (f32[8,128]{1,0:T(8,128)S(1)}, f32[8,128]{1,0:T(8,128)S(1)}, u32[]{:S(2)}, u32[]{:S(2)}) collective-permute-start(f32[8,128]{1,0:T(8,128)S(1)} %sum.3.refs_10_), channel_id=1, source_target_pairs={{0,2},{1,3},{2,0},{3,1},{4,6},{5,7},{6,4},{7,5},{8,10},{9,11},{10,... | collective-permute-start | bytes 12296 | tf_op jit(solution)/shard_map/group_norm/ppermute | solution.py:433
  55.2 5.4 %collective-permute-start.19 = (f32[8,128]{1,0:T(8,128)S(1)}, f32[8,128]{1,0:T(8,128)S(1)}, u32[]{:S(2)}, u32[]{:S(2)}) collective-permute-start(f32[8,128]{1,0:T(8,128)S(1)} %sum.3.refs_10_), channel_id=1, source_target_pairs={{0,3},{1,2},{2,1},{3,0},{4,7},{5,6},{6,5},{7,4},{8,11},{9,10},{10,... | collective-permute-start | bytes 12296 | tf_op jit(solution)/shard_map/group_norm/ppermute | solution.py:433
  56.5 4.1 %collective-permute-start.20 = (f32[8,128]{1,0:T(8,128)S(1)}, f32[8,128]{1,0:T(8,128)S(1)}, u32[]{:S(2)}, u32[]{:S(2)}) collective-permute-start(f32[8,128]{1,0:T(8,128)S(1)} %sum.3.refs_10_), channel_id=1, source_target_pairs={{0,1},{1,0},{2,3},{3,2},{4,5},{5,4},{6,7},{7,6},{8,9},{9,8},{10,11... | collective-permute-start | bytes 12296 | tf_op jit(solution)/shard_map/group_norm/ppermute | solution.py:433
  66.8 9.2 %collective-permute-start.31 = (f32[256,512]{1,0:T(8,128)S(1)}, f32[256,512]{1,0:T(8,128)S(1)}, u32[]{:S(2)}, u32[]{:S(2)}) collective-permute-start(f32[256,512]{1,0:T(8,128)S(1)} %get-tuple-element.80), channel_id=1, source_target_pairs={{0,8},{4,20},{8,0},{12,28},{16,24},{20,4},{24,16},{28,12},{1,9},{5... | collective-permute-start | bytes 1572872 | tf_op jit(solution)/shard_map/link_own/ppermute | solution.py:376
  68.4 13.3 %collective-permute-start.21 = (f32[256,512]{1,0:T(8,128)S(1)}, f32[256,512]{1,0:T(8,128)S(1)}, u32[]{:S(2)}, u32[]{:S(2)}) collective-permute-start(f32[256,512]{1,0:T(8,128)S(1)} %get-tuple-element.79), channel_id=1, source_target_pairs={{0,8},{4,20},{8,0},{12,28},{16,24},{20,4},{24,16},{28,12},{1,9},{5... | collective-permute-start | bytes 1572872 | tf_op jit(solution)/shard_map/link_own/ppermute | solution.py:376
  68.9 12.8 %collective-permute-start.25 = (f32[256,512]{1,0:T(8,128)S(1)}, f32[256,512]{1,0:T(8,128)S(1)}, u32[]{:S(2)}, u32[]{:S(2)}) collective-permute-start(f32[256,512]{1,0:T(8,128)S(1)} %get-tuple-element.80), channel_id=1, source_target_pairs={{0,4},{4,0},{8,12},{12,8},{16,20},{20,16},{24,28},{28,24},{1,5},{5... | collective-permute-start | bytes 1572872 | tf_op jit(solution)/shard_map/core_own/ppermute | solution.py:376
  68.9 14.3 %collective-permute-start.28 = (f32[256,512]{1,0:T(8,128)S(1)}, f32[256,512]{1,0:T(8,128)S(1)}, u32[]{:S(2)}, u32[]{:S(2)}) collective-permute-start(f32[256,512]{1,0:T(8,128)S(1)} %get-tuple-element.79), channel_id=1, source_target_pairs={{0,4},{4,0},{8,12},{12,8},{16,20},{20,16},{24,28},{28,24},{1,5},{5... | collective-permute-start | bytes 1572872 | tf_op jit(solution)/shard_map/core_own/ppermute | solution.py:376
  76.1 7.7 %collective-permute-start.32 = (f32[256,512]{1,0:T(8,128)S(1)}, f32[256,512]{1,0:T(8,128)S(1)}, u32[]{:S(2)}, u32[]{:S(2)}) collective-permute-start(f32[256,512]{1,0:T(8,128)S(1)} %collective-permute-done.31.refs_3_), channel_id=1, source_target_pairs={{0,4},{4,0},{8,12},{12,8},{16,20},{20,16},{24,28},{28,24},{1,5},{5... | collective-permute-start | bytes 1572872 | tf_op jit(solution)/shard_map/core_first/ppermute | solution.py:376
  81.7 3.5 %collective-permute-start.22 = (f32[256,512]{1,0:T(8,128)S(1)}, f32[256,512]{1,0:T(8,128)S(1)}, u32[]{:S(2)}, u32[]{:S(2)}) collective-permute-start(f32[256,512]{1,0:T(8,128)S(1)} %collective-permute-done.21.refs_4_), channel_id=1, source_target_pairs={{0,4},{4,0},{8,12},{12,8},{16,20},{20,16},{24,28},{28,24},{1,5},{5... | collective-permute-start | bytes 1572872 | tf_op jit(solution)/shard_map/core_first/ppermute | solution.py:376
  81.7 9.2 %collective-permute-start.26 = (f32[256,512]{1,0:T(8,128)S(1)}, f32[256,512]{1,0:T(8,128)S(1)}, u32[]{:S(2)}, u32[]{:S(2)}) collective-permute-start(f32[256,512]{1,0:T(8,128)S(1)} %collective-permute-done.25.refs_1_), channel_id=1, source_target_pairs={{0,8},{4,20},{8,0},{12,28},{16,24},{20,4},{24,16},{28,12},{1,9},{5... | collective-permute-start | bytes 1572872 | tf_op jit(solution)/shard_map/link_sibling/ppermute | solution.py:376
  83.2 13.3 %collective-permute-start.29 = (f32[256,512]{1,0:T(8,128)S(1)}, f32[256,512]{1,0:T(8,128)S(1)}, u32[]{:S(2)}, u32[]{:S(2)}) collective-permute-start(f32[256,512]{1,0:T(8,128)S(1)} %collective-permute-done.28.refs_2_), channel_id=1, source_target_pairs={{0,8},{4,20},{8,0},{12,28},{16,24},{20,4},{24,16},{28,12},{1,9},{5... | collective-permute-start | bytes 1572872 | tf_op jit(solution)/shard_map/link_sibling/ppermute | solution.py:376
  83.7 18.4 %collective-permute-start.33 = (f32[256,512]{1,0:T(8,128)S(1)}, f32[256,512]{1,0:T(8,128)S(1)}, u32[]{:S(2)}, u32[]{:S(2)}) collective-permute-start(f32[256,512]{1,0:T(8,128)S(1)} %collective-permute-done.32.refs_5_), channel_id=1, source_target_pairs={{0,8},{4,20},{8,0},{12,28},{16,24},{20,4},{24,16},{28,12},{1,9},{5... | collective-permute-start | bytes 1572872 | tf_op jit(solution)/shard_map/link_relayed/ppermute | solution.py:376
  85.2 22.5 %collective-permute-start.23 = (f32[256,512]{1,0:T(8,128)S(1)}, f32[256,512]{1,0:T(8,128)S(1)}, u32[]{:S(2)}, u32[]{:S(2)}) collective-permute-start(f32[256,512]{1,0:T(8,128)S(1)} %collective-permute-done.22.refs_6_), channel_id=1, source_target_pairs={{0,8},{4,20},{8,0},{12,28},{16,24},{20,4},{24,16},{28,12},{1,9},{5... | collective-permute-start | bytes 1572872 | tf_op jit(solution)/shard_map/link_relayed/ppermute | solution.py:376
  90.9 16.9 %collective-permute-start.27 = (f32[256,512]{1,0:T(8,128)S(1)}, f32[256,512]{1,0:T(8,128)S(1)}, u32[]{:S(2)}, u32[]{:S(2)}) collective-permute-start(f32[256,512]{1,0:T(8,128)S(1)} %collective-permute-done.26.refs_7_), channel_id=1, source_target_pairs={{0,4},{4,0},{8,12},{12,8},{16,20},{20,16},{24,28},{28,24},{1,5},{5... | collective-permute-start | bytes 1572872 | tf_op jit(solution)/shard_map/core_second/ppermute | solution.py:376
  96.5 11.2 %collective-permute-start.30 = (f32[256,512]{1,0:T(8,128)S(1)}, f32[256,512]{1,0:T(8,128)S(1)}, u32[]{:S(2)}, u32[]{:S(2)}) collective-permute-start(f32[256,512]{1,0:T(8,128)S(1)} %collective-permute-done.29.refs_8_), channel_id=1, source_target_pairs={{0,4},{4,0},{8,12},{12,8},{16,20},{20,16},{24,28},{28,24},{1,5},{5... | collective-permute-start | bytes 1572872 | tf_op jit(solution)/shard_map/core_second/ppermute | solution.py:376
  102.1 5.6 %collective-permute-start.34 = (f32[256,512]{1,0:T(8,128)S(1)}, f32[256,512]{1,0:T(8,128)S(1)}, u32[]{:S(2)}, u32[]{:S(2)}) collective-permute-start(f32[256,512]{1,0:T(8,128)S(1)} %collective-permute-done.33.refs_2_), channel_id=1, source_target_pairs={{0,4},{4,0},{8,12},{12,8},{16,20},{20,16},{24,28},{28,24},{1,5},{5... | collective-permute-start | bytes 1572872 | tf_op jit(solution)/shard_map/core_relayed/ppermute | solution.py:376
  (7 other events, 56.7 us)

commit v20 on v17

--- a/solution.py
+++ b/solution.py
@@ -300,15 +300,20 @@
         clip_factor = jnp.minimum(1.0, clip_level / jnp.sqrt(squares / entry_count))
         gram_scale = clip_factor * clip_factor / width
         roots, scales = roots_of((left_refs, right_refs), gram_scale)
-        halfway = triple_dot(left_operand(roots[0]), right_operand(whole_block((upper_ref, lower_ref))))
-        pre = triple_dot(left_operand(halfway), right_operand(roots[1]))
+        rows = width // 2
+        block_side = right_operand(whole_block((upper_ref, lower_ref)))
+        halfway = [triple_dot(left_operand(roots[0][h * rows : (h + 1) * rows]), block_side) for h in HALVES]
+        root_side = right_operand(roots[1])
+        pre = [triple_dot(left_operand(value), root_side) for value in halfway]
         pre_scale = scales[0] * scales[1] * clip_factor
-        pre_norm = jnp.sum(pre * pre, keepdims=True).reshape(1, 1) * (pre_scale * pre_scale)
+        pre_norm = sum(jnp.sum(value * value, keepdims=True).reshape(1, 1) for value in pre)
+        pre_norm = pre_norm * (pre_scale * pre_scale)
         clipped_norm = block_norm_ref[:1, :1] * (clip_factor * clip_factor)
-        update = pre * (pre_scale * jnp.sqrt(clipped_norm / (pre_norm + graft_eps)))
-        out_refs[0][...] = update
+        scale = pre_scale * jnp.sqrt(clipped_norm / (pre_norm + graft_eps))
         for half in HALVES:
-            out_refs[1 + half][...] = update[half * (width // 2) : (half + 1) * (width // 2)]
+            update = pre[half] * scale
+            out_refs[0][half * rows : (half + 1) * rows, :] = update
+            out_refs[1 + half][...] = update
 
     operands = (*block, block_norm, *left, *right, *norms)
     shapes = [piece_shape(half, width) for half in (None, *HALVES)]

time: 108 us -> 108 us (level)
  transfers between devices with their start and end apart: 32 -> 32, of which waited for: 14 -> 15; matrix products, arithmetic and copies ran while one was open for 0% -> 0% of each run, Pallas kernels for 12% -> 12%
where the time goes in v20:
time: 108 us
  waiting for transfers between devices  56.7 us (52%)
  starting transfers between devices  26.3 us (24%)
  Pallas kernels  21.5 us (20%)
  local copies, waits for them, and re-layouts  1.9 us (2%)
    ppermute x29, waiting for transfers between devices, over(): return lax.ppermute(value, 'dp', pairs)  54.6 us
    ppermute x29, starting transfers between devices, over(): return lax.ppermute(value, 'dp', pairs)  21.9 us
    pallas_call x20, Pallas kernels, local_call(): pl.pallas_call(kernel, in_specs=[pl.BlockSpec(memory_space=pltpu.SMEM)] *...  15.8 us
    pallas_call x3, Pallas kernels, assemble_call(): pl.pallas_call(kernel, in_specs=in_specs, out_specs=pl.BlockSpec(memory_s...  5.73 us
    ppermute x3, starting transfers between devices, paired_body(): norms.append(lax.ppermute(norm, 'mp', pairs))  4.46 us
  transfers between devices with their start and end apart: 32, of which 15 were waited for; matrix products, arithmetic and copies ran while one was open for 0% of the time, Pallas kernels for 12%

profile of v20, /device:TPU:0, one launch (start us, length us, event | category | flops | bytes accessed | tf_op | source)
XLA Modules:
  0.0 107.6 jit_solution(3340328084315709969)
XLA Ops:
  0.7 1.9 %copy-done = bf16[1,512,3072]{2,1,0:T(8,128)(2,1)S(1)} copy-done((bf16[1,512,3072]{2,1,0:T(8,128)(2,1)S(1)}, bf16[1,512,3072]{2,1,0:T(8,128)(2,1)}, u32[]{:S(2)}) %copy-start) | copy-done | bytes 3145752
  6.2 2.9 %collective-permute-start.6 = (f32[256,512]{1,0:T(8,128)S(1)}, f32[256,512]{1,0:T(8,128)S(1)}, u32[]{:S(2)}, u32[]{:S(2)}) collective-permute-start(f32[256,512]{1,0:T(8,128)S(1)} %add.13), channel_id=1, source_target_pairs={{0,8},{4,20},{8,0},{12,28},{16,24},{20,4},{24,16},{28,12},{1,9},{5... | collective-permute-start | bytes 1572872 | tf_op jit(solution)/shard_map/link_corner/ppermute | solution.py:381
  10.7 1.5 %collective-permute-start.3 = (f32[256,512]{1,0:T(8,128)S(1)}, f32[256,512]{1,0:T(8,128)S(1)}, u32[]{:S(2)}, u32[]{:S(2)}) collective-permute-start(f32[256,512]{1,0:T(8,128)S(1)} %add.11), channel_id=1, source_target_pairs={{0,8},{4,20},{8,0},{12,28},{16,24},{20,4},{24,16},{28,12},{1,9},{5... | collective-permute-start | bytes 1572872 | tf_op jit(solution)/shard_map/link_straight/ppermute | solution.py:381
  12.6 3.6 %collective-permute-done.6.refs_2_ = f32[256,512]{1,0:T(8,128)S(1)} collective-permute-done((f32[256,512]{1,0:T(8,128)S(1)}, f32[256,512]{1,0:T(8,128)S(1)}, u32[]{:S(2)}, u32[]{:S(2)}) %collective-permute-start.6) | collective-permute-done | bytes 524320 | tf_op jit(solution)/shard_map/link_corner/ppermute | solution.py:381
  16.2 2.0 %collective-permute-start.10 = (f32[256,512]{1,0:T(8,128)S(1)}, f32[256,512]{1,0:T(8,128)S(1)}, u32[]{:S(2)}, u32[]{:S(2)}) collective-permute-start(f32[256,512]{1,0:T(8,128)S(1)} %add.15), channel_id=1, source_target_pairs={{0,8},{4,20},{8,0},{12,28},{16,24},{20,4},{24,16},{28,12},{1,9},{5... | collective-permute-start | bytes 1572872 | tf_op jit(solution)/shard_map/link_straight/ppermute | solution.py:381
  18.3 3.5 %collective-permute-done.12.refs_2_ = f32[256,512]{1,0:T(8,128)S(1)} collective-permute-done((f32[256,512]{1,0:T(8,128)S(1)}, f32[256,512]{1,0:T(8,128)S(1)}, u32[]{:S(2)}, u32[]{:S(2)}) %collective-permute-start.12) | collective-permute-done | bytes 524320 | tf_op jit(solution)/shard_map/link_corner/ppermute | solution.py:381
  21.8 2.1 %collective-permute-start.7 = (f32[256,512]{1,0:T(8,128)S(1)}, f32[256,512]{1,0:T(8,128)S(1)}, u32[]{:S(2)}, u32[]{:S(2)}) collective-permute-start(f32[256,512]{1,0:T(8,128)S(1)} %add.14), channel_id=1, source_target_pairs={{0,16},{4,12},{8,24},{12,4},{16,0},{20,28},{24,8},{28,20},{1,17},{... | collective-permute-start | bytes 1572872 | tf_op jit(solution)/shard_map/side_side/ppermute | solution.py:381
  24.1 6.7 %collective-permute-done.3.refs_2_ = f32[256,512]{1,0:T(8,128)S(1)} collective-permute-done((f32[256,512]{1,0:T(8,128)S(1)}, f32[256,512]{1,0:T(8,128)S(1)}, u32[]{:S(2)}, u32[]{:S(2)}) %collective-permute-start.3) | collective-permute-done | bytes 524320 | tf_op jit(solution)/shard_map/link_straight/ppermute | solution.py:381
  30.9 1.5 %square.1 = (f32[512,512]{1,0:T(8,128)S(1)}, f32[512,512]{1,0:T(8,128)S(1)}) custom-call(f32[512,512]{1,0:T(8,128)S(1)} %bitcast.8, f32[512,512]{1,0:T(8,128)S(1)} %bitcast.11), custom_call_target="tpu_custom_call" | custom-call | flops 1610612736 | bytes 4194304 | tf_op jit(solution)/shard_map/square/pallas_call | solution.py:129
  32.4 9.7 %collective-permute-done.10.refs_2_ = f32[256,512]{1,0:T(8,128)S(1)} collective-permute-done((f32[256,512]{1,0:T(8,128)S(1)}, f32[256,512]{1,0:T(8,128)S(1)}, u32[]{:S(2)}, u32[]{:S(2)}) %collective-permute-start.10) | collective-permute-done | bytes 524320 | tf_op jit(solution)/shard_map/link_straight/ppermute | solution.py:381
  42.3 1.4 %collective-permute-done.13.arrival_ref = f32[256,512]{1,0:T(8,128)S(1)} collective-permute-done((f32[256,512]{1,0:T(8,128)S(1)}, f32[256,512]{1,0:T(8,128)S(1)}, u32[]{:S(2)}, u32[]{:S(2)}) %collective-permute-start.13) | collective-permute-done | bytes 524320 | tf_op jit(solution)/shard_map/side_side/ppermute | solution.py:381
  44.4 0.8 collective-permute-done.14.refs_1_
  45.2 3.0 %collective-permute-start.15 = (f32[8,128]{1,0:T(8,128)S(1)}, f32[8,128]{1,0:T(8,128)S(1)}, u32[]{:S(2)}, u32[]{:S(2)}) collective-permute-start(f32[8,128]{1,0:T(8,128)S(1)} %sum.2.refs_0_), channel_id=1, source_target_pairs={{0,24},{4,28},{8,16},{12,20},{16,8},{20,12},{24,0},{28,4},{1,25},{... | collective-permute-start | bytes 12296 | tf_op jit(solution)/shard_map/chip_norm/ppermute | solution.py:381
  48.8 1.5 %gram.1 = (f32[512,512]{1,0:T(8,128)S(1)}, f32[512,512]{1,0:T(8,128)S(1)}) custom-call(f32[256,512]{1,0:T(8,128)S(1)} %get-tuple-element.74.upper_ref, f32[256,512]{1,0:T(8,128)S(1)} %get-tuple-element.72.lower_ref), custom_call_target="tpu_custom_call" | custom-call | flops 1610612736 | bytes 3145728 | tf_op jit(solution)/shard_map/gram/pallas_call | solution.py:129
  50.3 1.7 %mix.2 = (f32[512,512]{1,0:T(8,128)S(1)}, f32[512,512]{1,0:T(8,128)S(1)}) custom-call(f32[512,512]{1,0:T(8,128)S(1)} %bitcast.9, f32[512,512]{1,0:T(8,128)S(1)} %get-tuple-element.75.gram_ref.refs_1_), custom_call_target="tpu_custom_call" | custom-call | flops 1610612736 | bytes 4194304 | tf_op jit(solution)/shard_map/mix/pallas_call | solution.py:129
  52.3 2.9 %collective-permute-start.18 = (f32[8,128]{1,0:T(8,128)S(1)}, f32[8,128]{1,0:T(8,128)S(1)}, u32[]{:S(2)}, u32[]{:S(2)}) collective-permute-start(f32[8,128]{1,0:T(8,128)S(1)} %sum.3.refs_10_), channel_id=1, source_target_pairs={{0,2},{1,3},{2,0},{3,1},{4,6},{5,7},{6,4},{7,5},{8,10},{9,11},{10,... | collective-permute-start | bytes 12296 | tf_op jit(solution)/shard_map/group_norm/ppermute | solution.py:438
  55.2 1.4 %collective-permute-start.19 = (f32[8,128]{1,0:T(8,128)S(1)}, f32[8,128]{1,0:T(8,128)S(1)}, u32[]{:S(2)}, u32[]{:S(2)}) collective-permute-start(f32[8,128]{1,0:T(8,128)S(1)} %sum.3.refs_10_), channel_id=1, source_target_pairs={{0,3},{1,2},{2,1},{3,0},{4,7},{5,6},{6,5},{7,4},{8,11},{9,10},{10,... | collective-permute-start | bytes 12296 | tf_op jit(solution)/shard_map/group_norm/ppermute | solution.py:438
  56.8 1.7 %mix.3 = (f32[512,512]{1,0:T(8,128)S(1)}, f32[512,512]{1,0:T(8,128)S(1)}) custom-call(f32[512,512]{1,0:T(8,128)S(1)} %bitcast.12, f32[512,512]{1,0:T(8,128)S(1)} %get-tuple-element.78.gram_ref.refs_6_), custom_call_target="tpu_custom_call" | custom-call | flops 1610612736 | bytes 4194304 | tf_op jit(solution)/shard_map/mix/pallas_call | solution.py:129
  58.5 2.1 %collective-permute-done.19.refs_12_ = f32[8,128]{1,0:T(8,128)S(1)} collective-permute-done((f32[8,128]{1,0:T(8,128)S(1)}, f32[8,128]{1,0:T(8,128)S(1)}, u32[]{:S(2)}, u32[]{:S(2)}) %collective-permute-start.19) | collective-permute-done | bytes 4128 | tf_op jit(solution)/shard_map/group_norm/ppermute | solution.py:438
  60.6 6.1 %update.1 = (f32[512,512]{1,0:T(8,128)S(1)}, f32[256,512]{1,0:T(8,128)S(1)}, f32[256,512]{1,0:T(8,128)S(1)}) custom-call(f32[256,512]{1,0:T(8,128)S(1)} %get-tuple-element.74.upper_ref, f32[256,512]{1,0:T(8,128)S(1)} %get-tuple-element.72.lower_ref, f32[8,128]{1,0:T(8,128)S(1)} %get-tuple-element.73.refs_0_.block_norm_ref, f32[512,512]{1,0:T(8,128)S(1)} %bitcast.10, ...), custom_call_target="tpu_custom_call" | custom-call | flops 4831838208 | bytes 13651968 | tf_op jit(solution)/shard_map/update/pallas_call | solution.py:129
  66.8 1.6 %collective-permute-start.26 = (f32[256,512]{1,0:T(8,128)S(1)}, f32[256,512]{1,0:T(8,128)S(1)}, u32[]{:S(2)}, u32[]{:S(2)}) collective-permute-start(f32[256,512]{1,0:T(8,128)S(1)} %get-tuple-element.85), channel_id=1, source_target_pairs={{0,8},{4,20},{8,0},{12,28},{16,24},{20,4},{24,16},{28,12},{1,9},{5... | collective-permute-start | bytes 1572872 | tf_op jit(solution)/shard_map/link_own/ppermute | solution.py:381
  68.9 7.2 %collective-permute-done.26.refs_2_ = f32[256,512]{1,0:T(8,128)S(1)} collective-permute-done((f32[256,512]{1,0:T(8,128)S(1)}, f32[256,512]{1,0:T(8,128)S(1)}, u32[]{:S(2)}, u32[]{:S(2)}) %collective-permute-start.26) | collective-permute-done | bytes 524320 | tf_op jit(solution)/shard_map/link_own/ppermute | solution.py:381
  76.1 1.5 %collective-permute-start.27 = (f32[512,512]{1,0:T(8,128)S(1)}, f32[512,512]{1,0:T(8,128)S(1)}, u32[]{:S(2)}, u32[]{:S(2)}) collective-permute-start(f32[512,512]{1,0:T(8,128)S(1)} %collective-permute-done.22.refs_1_), channel_id=1, source_target_pairs={{0,8},{4,20},{8,0},{12,28},{16,24},{20,4},{24,16},{28,12},{1,9},{5... | collective-permute-start | bytes 3145736 | tf_op jit(solution)/shard_map/link_sibling/ppermute | solution.py:381
  77.6 4.1 %collective-permute-done.21.refs_3_ = f32[256,512]{1,0:T(8,128)S(1)} collective-permute-done((f32[256,512]{1,0:T(8,128)S(1)}, f32[256,512]{1,0:T(8,128)S(1)}, u32[]{:S(2)}, u32[]{:S(2)}) %collective-permute-start.21) | collective-permute-done | bytes 524320 | tf_op jit(solution)/shard_map/link_own/ppermute | solution.py:381
  81.7 1.5 %collective-permute-start.30 = (f32[256,512]{1,0:T(8,128)S(1)}, f32[256,512]{1,0:T(8,128)S(1)}, u32[]{:S(2)}, u32[]{:S(2)}) collective-permute-start(f32[256,512]{1,0:T(8,128)S(1)} %collective-permute-done.29.refs_4_), channel_id=1, source_target_pairs={{0,8},{4,20},{8,0},{12,28},{16,24},{20,4},{24,16},{28,12},{1,9},{5... | collective-permute-start | bytes 1572872 | tf_op jit(solution)/shard_map/link_relayed/ppermute | solution.py:381
  83.2 9.7 %collective-permute-done.27.refs_6_ = f32[512,512]{1,0:T(8,128)S(1)} collective-permute-done((f32[512,512]{1,0:T(8,128)S(1)}, f32[512,512]{1,0:T(8,128)S(1)}, u32[]{:S(2)}, u32[]{:S(2)}) %collective-permute-start.27) | collective-permute-done | bytes 1048608 | tf_op jit(solution)/shard_map/link_sibling/ppermute | solution.py:381
  92.9 1.5 %collective-permute-start.24 = (f32[256,512]{1,0:T(8,128)S(1)}, f32[256,512]{1,0:T(8,128)S(1)}, u32[]{:S(2)}, u32[]{:S(2)}) collective-permute-start(f32[256,512]{1,0:T(8,128)S(1)} %collective-permute-done.23.refs_5_), channel_id=1, source_target_pairs={{0,8},{4,20},{8,0},{12,28},{16,24},{20,4},{24,16},{28,12},{1,9},{5... | collective-permute-start | bytes 1572872 | tf_op jit(solution)/shard_map/link_relayed/ppermute | solution.py:381
  94.4 2.6 %assemble.3.refs_4_ = f32[512,3072]{1,0:T(8,128)} custom-call(s32[7]{0:T(128)S(1)} %pad_add_fusion.places_ref, f32[512,512]{1,0:T(8,128)S(1)} %get-tuple-element.83.refs_0_, f32[512,512]{1,0:T(8,128)S(1)} %collective-permute-done.22.refs_1_, f32[256,512]{1,0:T(8,128)S(1)} %collective-permute-done.26.refs_2_, f32[256,512]{1,0:T(8,128)S(1)} %collective-permute-done.21.refs_3_, ...), custom_call_target="tpu_custom_call" | custom-call | bytes 14680064 | tf_op jit(solution)/shard_map/assemble/pallas_call | solution.py:352
  97.1 1.5 %collective-permute-done.30.refs_1_ = f32[256,512]{1,0:T(8,128)S(1)} collective-permute-done((f32[256,512]{1,0:T(8,128)S(1)}, f32[256,512]{1,0:T(8,128)S(1)}, u32[]{:S(2)}, u32[]{:S(2)}) %collective-permute-start.30) | collective-permute-done | bytes 524320 | tf_op jit(solution)/shard_map/link_relayed/ppermute | solution.py:381
  98.5 5.6 %collective-permute-done.24.refs_2_ = f32[256,512]{1,0:T(8,128)S(1)} collective-permute-done((f32[256,512]{1,0:T(8,128)S(1)}, f32[256,512]{1,0:T(8,128)S(1)}, u32[]{:S(2)}, u32[]{:S(2)}) %collective-permute-start.24) | collective-permute-done | bytes 524320 | tf_op jit(solution)/shard_map/link_relayed/ppermute | solution.py:381
  104.2 1.7 %assemble.4.refs_1_ = f32[512,3072]{1,0:T(8,128)} custom-call(s32[7]{0:T(128)S(1)} %pad_add_fusion.places_ref, f32[512,512]{1,0:T(8,128)S(1)} %collective-permute-done.28.refs_0_, f32[256,512]{1,0:T(8,128)S(1)} %collective-permute-done.30.refs_1_, f32[256,512]{1,0:T(8,128)S(1)} %collective-permute-done.24.refs_2_, ...), custom_call_target="tpu_custom_call", output_to_operand_aliasing={{}: (5, {})} | custom-call | bytes 8388608 | tf_op jit(solution)/shard_map/assemble/pallas_call | solution.py:352
  106.1 1.4 %assemble.5 = f32[512,3072]{1,0:T(8,128)} custom-call(s32[7]{0:T(128)S(1)} %pad_add_fusion.places_ref, f32[256,512]{1,0:T(8,128)S(1)} %collective-permute-done.25.refs_0_, f32[512,3072]{1,0:T(8,128)} %assemble.4.refs_1_), custom_call_target="tpu_custom_call", output_to_operand_aliasing={{}: (2, {})} | custom-call | bytes 1048576 | tf_op jit(solution)/shard_map/assemble/pallas_call | solution.py:352
  (64 shorter events, 9.4 us)
Async XLA Ops:
  3.4 2.3 %collective-permute-start.5 = (f32[256,512]{1,0:T(8,128)S(1)}, f32[256,512]{1,0:T(8,128)S(1)}, u32[]{:S(2)}, u32[]{:S(2)}) collective-permute-start(f32[256,512]{1,0:T(8,128)S(1)} %get-tuple-element.62), channel_id=1, source_target_pairs={{0,4},{4,0},{8,12},{12,8},{16,20},{20,16},{24,28},{28,24},{1,5},{5... | collective-permute-start | bytes 1572872 | tf_op jit(solution)/shard_map/core_corner/ppermute | solution.py:381
  3.9 2.3 %collective-permute-start = (f32[256,512]{1,0:T(8,128)S(1)}, f32[256,512]{1,0:T(8,128)S(1)}, u32[]{:S(2)}, u32[]{:S(2)}) collective-permute-start(f32[256,512]{1,0:T(8,128)S(1)} %get-tuple-element.48), channel_id=1, source_target_pairs={{0,4},{4,0},{8,12},{12,8},{16,20},{20,16},{24,28},{28,24},{1,5},{5... | collective-permute-start | bytes 1572872 | tf_op jit(solution)/shard_map/core_corner/ppermute | solution.py:381
  4.0 5.1 %collective-permute-start.2 = (f32[256,512]{1,0:T(8,128)S(1)}, f32[256,512]{1,0:T(8,128)S(1)}, u32[]{:S(2)}, u32[]{:S(2)}) collective-permute-start(f32[256,512]{1,0:T(8,128)S(1)} %get-tuple-element.53), channel_id=1, source_target_pairs={{0,4},{4,0},{8,12},{12,8},{16,20},{20,16},{24,28},{28,24},{1,5},{5... | collective-permute-start | bytes 1572872 | tf_op jit(solution)/shard_map/core_straight/ppermute | solution.py:381
  5.1 4.7 %collective-permute-start.4 = (f32[256,512]{1,0:T(8,128)S(1)}, f32[256,512]{1,0:T(8,128)S(1)}, u32[]{:S(2)}, u32[]{:S(2)}) collective-permute-start(f32[256,512]{1,0:T(8,128)S(1)} %get-tuple-element.60), channel_id=1, source_target_pairs={{0,4},{4,0},{8,12},{12,8},{16,20},{20,16},{24,28},{28,24},{1,5},{5... | collective-permute-start | bytes 1572872 | tf_op jit(solution)/shard_map/core_side/ppermute | solution.py:381
  5.3 5.4 %collective-permute-start.9 = (f32[256,512]{1,0:T(8,128)S(1)}, f32[256,512]{1,0:T(8,128)S(1)}, u32[]{:S(2)}, u32[]{:S(2)}) collective-permute-start(f32[256,512]{1,0:T(8,128)S(1)} %get-tuple-element.68), channel_id=1, source_target_pairs={{0,4},{4,0},{8,12},{12,8},{16,20},{20,16},{24,28},{28,24},{1,5},{5... | collective-permute-start | bytes 1572872 | tf_op jit(solution)/shard_map/core_straight/ppermute | solution.py:381
  5.7 6.5 %collective-permute-start.11 = (f32[256,512]{1,0:T(8,128)S(1)}, f32[256,512]{1,0:T(8,128)S(1)}, u32[]{:S(2)}, u32[]{:S(2)}) collective-permute-start(f32[256,512]{1,0:T(8,128)S(1)} %get-tuple-element.70), channel_id=1, source_target_pairs={{0,4},{4,0},{8,12},{12,8},{16,20},{20,16},{24,28},{28,24},{1,5},{5... | collective-permute-start | bytes 1572872 | tf_op jit(solution)/shard_map/core_side/ppermute | solution.py:381
  6.2 10.0 %collective-permute-start.6 = (f32[256,512]{1,0:T(8,128)S(1)}, f32[256,512]{1,0:T(8,128)S(1)}, u32[]{:S(2)}, u32[]{:S(2)}) collective-permute-start(f32[256,512]{1,0:T(8,128)S(1)} %add.13), channel_id=1, source_target_pairs={{0,8},{4,20},{8,0},{12,28},{16,24},{20,4},{24,16},{28,12},{1,9},{5... | collective-permute-start | bytes 1572872 | tf_op jit(solution)/shard_map/link_corner/ppermute | solution.py:381
  9.1 12.7 %collective-permute-start.12 = (f32[256,512]{1,0:T(8,128)S(1)}, f32[256,512]{1,0:T(8,128)S(1)}, u32[]{:S(2)}, u32[]{:S(2)}) collective-permute-start(f32[256,512]{1,0:T(8,128)S(1)} %add.10), channel_id=1, source_target_pairs={{0,8},{4,20},{8,0},{12,28},{16,24},{20,4},{24,16},{28,12},{1,9},{5... | collective-permute-start | bytes 1572872 | tf_op jit(solution)/shard_map/link_corner/ppermute | solution.py:381
  9.8 14.2 %collective-permute-start.1 = (f32[256,512]{1,0:T(8,128)S(1)}, f32[256,512]{1,0:T(8,128)S(1)}, u32[]{:S(2)}, u32[]{:S(2)}) collective-permute-start(f32[256,512]{1,0:T(8,128)S(1)} %get-tuple-element.51), channel_id=1, source_target_pairs={{0,4},{4,0},{8,12},{12,8},{16,20},{20,16},{24,28},{28,24},{1,5},{5... | collective-permute-start | bytes 1572872 | tf_op jit(solution)/shard_map/core_self/ppermute | solution.py:381
  10.7 20.1 %collective-permute-start.3 = (f32[256,512]{1,0:T(8,128)S(1)}, f32[256,512]{1,0:T(8,128)S(1)}, u32[]{:S(2)}, u32[]{:S(2)}) collective-permute-start(f32[256,512]{1,0:T(8,128)S(1)} %add.11), channel_id=1, source_target_pairs={{0,8},{4,20},{8,0},{12,28},{16,24},{20,4},{24,16},{28,12},{1,9},{5... | collective-permute-start | bytes 1572872 | tf_op jit(solution)/shard_map/link_straight/ppermute | solution.py:381
  12.2 20.1 %collective-permute-start.8 = (f32[256,512]{1,0:T(8,128)S(1)}, f32[256,512]{1,0:T(8,128)S(1)}, u32[]{:S(2)}, u32[]{:S(2)}) collective-permute-start(f32[256,512]{1,0:T(8,128)S(1)} %get-tuple-element.66), channel_id=1, source_target_pairs={{0,4},{4,0},{8,12},{12,8},{16,20},{20,16},{24,28},{28,24},{1,5},{5... | collective-permute-start | bytes 1572872 | tf_op jit(solution)/shard_map/core_self/ppermute | solution.py:381
  16.2 25.8 %collective-permute-start.10 = (f32[256,512]{1,0:T(8,128)S(1)}, f32[256,512]{1,0:T(8,128)S(1)}, u32[]{:S(2)}, u32[]{:S(2)}) collective-permute-start(f32[256,512]{1,0:T(8,128)S(1)} %add.15), channel_id=1, source_target_pairs={{0,8},{4,20},{8,0},{12,28},{16,24},{20,4},{24,16},{28,12},{1,9},{5... | collective-permute-start | bytes 1572872 | tf_op jit(solution)/shard_map/link_straight/ppermute | solution.py:381
  21.8 20.3 %collective-permute-start.7 = (f32[256,512]{1,0:T(8,128)S(1)}, f32[256,512]{1,0:T(8,128)S(1)}, u32[]{:S(2)}, u32[]{:S(2)}) collective-permute-start(f32[256,512]{1,0:T(8,128)S(1)} %add.14), channel_id=1, source_target_pairs={{0,16},{4,12},{8,24},{12,4},{16,0},{20,28},{24,8},{28,20},{1,17},{... | collective-permute-start | bytes 1572872 | tf_op jit(solution)/shard_map/side_side/ppermute | solution.py:381
  24.0 19.8 %collective-permute-start.13 = (f32[256,512]{1,0:T(8,128)S(1)}, f32[256,512]{1,0:T(8,128)S(1)}, u32[]{:S(2)}, u32[]{:S(2)}) collective-permute-start(f32[256,512]{1,0:T(8,128)S(1)} %add.17), channel_id=1, source_target_pairs={{0,16},{4,12},{8,24},{12,4},{16,0},{20,28},{24,8},{28,20},{1,17},{... | collective-permute-start | bytes 1572872 | tf_op jit(solution)/shard_map/side_side/ppermute | solution.py:381
  44.0 1.2 %collective-permute-start.14 = (f32[8,128]{1,0:T(8,128)S(1)}, f32[8,128]{1,0:T(8,128)S(1)}, u32[]{:S(2)}, u32[]{:S(2)}) collective-permute-start(f32[8,128]{1,0:T(8,128)S(1)} %get-tuple-element.73.refs_0_.block_norm_ref), channel_id=1, source_target_pairs={{0,4},{4,0},{8,12},{12,8},{16,20},{20,16},{24,28},{28,24},{1,5},{5... | collective-permute-start | bytes 12296 | tf_op jit(solution)/shard_map/core_norm/ppermute | solution.py:381
  45.2 6.8 %collective-permute-start.15 = (f32[8,128]{1,0:T(8,128)S(1)}, f32[8,128]{1,0:T(8,128)S(1)}, u32[]{:S(2)}, u32[]{:S(2)}) collective-permute-start(f32[8,128]{1,0:T(8,128)S(1)} %sum.2.refs_0_), channel_id=1, source_target_pairs={{0,24},{4,28},{8,16},{12,20},{16,8},{20,12},{24,0},{28,4},{1,25},{... | collective-permute-start | bytes 12296 | tf_op jit(solution)/shard_map/chip_norm/ppermute | solution.py:381
  48.2 3.8 %collective-permute-start.16 = (f32[8,128]{1,0:T(8,128)S(1)}, f32[8,128]{1,0:T(8,128)S(1)}, u32[]{:S(2)}, u32[]{:S(2)}) collective-permute-start(f32[8,128]{1,0:T(8,128)S(1)} %sum.2.refs_0_), channel_id=1, source_target_pairs={{0,16},{4,20},{8,24},{12,28},{16,0},{20,4},{24,8},{28,12},{1,17},{... | collective-permute-start | bytes 12296 | tf_op jit(solution)/shard_map/chip_norm/ppermute | solution.py:381
  48.7 3.6 %collective-permute-start.17 = (f32[8,128]{1,0:T(8,128)S(1)}, f32[8,128]{1,0:T(8,128)S(1)}, u32[]{:S(2)}, u32[]{:S(2)}) collective-permute-start(f32[8,128]{1,0:T(8,128)S(1)} %sum.2.refs_0_), channel_id=1, source_target_pairs={{0,8},{4,12},{8,0},{12,4},{16,24},{20,28},{24,16},{28,20},{1,9},{5... | collective-permute-start | bytes 12296 | tf_op jit(solution)/shard_map/chip_norm/ppermute | solution.py:381
  52.3 6.2 %collective-permute-start.18 = (f32[8,128]{1,0:T(8,128)S(1)}, f32[8,128]{1,0:T(8,128)S(1)}, u32[]{:S(2)}, u32[]{:S(2)}) collective-permute-start(f32[8,128]{1,0:T(8,128)S(1)} %sum.3.refs_10_), channel_id=1, source_target_pairs={{0,2},{1,3},{2,0},{3,1},{4,6},{5,7},{6,4},{7,5},{8,10},{9,11},{10,... | collective-permute-start | bytes 12296 | tf_op jit(solution)/shard_map/group_norm/ppermute | solution.py:438
  55.2 5.4 %collective-permute-start.19 = (f32[8,128]{1,0:T(8,128)S(1)}, f32[8,128]{1,0:T(8,128)S(1)}, u32[]{:S(2)}, u32[]{:S(2)}) collective-permute-start(f32[8,128]{1,0:T(8,128)S(1)} %sum.3.refs_10_), channel_id=1, source_target_pairs={{0,3},{1,2},{2,1},{3,0},{4,7},{5,6},{6,5},{7,4},{8,11},{9,10},{10,... | collective-permute-start | bytes 12296 | tf_op jit(solution)/shard_map/group_norm/ppermute | solution.py:438
  56.5 4.1 %collective-permute-start.20 = (f32[8,128]{1,0:T(8,128)S(1)}, f32[8,128]{1,0:T(8,128)S(1)}, u32[]{:S(2)}, u32[]{:S(2)}) collective-permute-start(f32[8,128]{1,0:T(8,128)S(1)} %sum.3.refs_10_), channel_id=1, source_target_pairs={{0,1},{1,0},{2,3},{3,2},{4,5},{5,4},{6,7},{7,6},{8,9},{9,8},{10,11... | collective-permute-start | bytes 12296 | tf_op jit(solution)/shard_map/group_norm/ppermute | solution.py:438
  66.7 9.3 %collective-permute-start.22 = (f32[512,512]{1,0:T(8,128)S(1)}, f32[512,512]{1,0:T(8,128)S(1)}, u32[]{:S(2)}, u32[]{:S(2)}) collective-permute-start(f32[512,512]{1,0:T(8,128)S(1)} %get-tuple-element.83.refs_0_), channel_id=1, source_target_pairs={{0,4},{4,0},{8,12},{12,8},{16,20},{20,16},{24,28},{28,24},{1,5},{5... | collective-permute-start | bytes 3145736 | tf_op jit(solution)/shard_map/core_own/ppermute | solution.py:381
  66.8 9.2 %collective-permute-start.26 = (f32[256,512]{1,0:T(8,128)S(1)}, f32[256,512]{1,0:T(8,128)S(1)}, u32[]{:S(2)}, u32[]{:S(2)}) collective-permute-start(f32[256,512]{1,0:T(8,128)S(1)} %get-tuple-element.85), channel_id=1, source_target_pairs={{0,8},{4,20},{8,0},{12,28},{16,24},{20,4},{24,16},{28,12},{1,9},{5... | collective-permute-start | bytes 1572872 | tf_op jit(solution)/shard_map/link_own/ppermute | solution.py:381
  68.4 13.3 %collective-permute-start.21 = (f32[256,512]{1,0:T(8,128)S(1)}, f32[256,512]{1,0:T(8,128)S(1)}, u32[]{:S(2)}, u32[]{:S(2)}) collective-permute-start(f32[256,512]{1,0:T(8,128)S(1)} %get-tuple-element.82), channel_id=1, source_target_pairs={{0,8},{4,20},{8,0},{12,28},{16,24},{20,4},{24,16},{28,12},{1,9},{5... | collective-permute-start | bytes 1572872 | tf_op jit(solution)/shard_map/link_own/ppermute | solution.py:381
  76.1 16.8 %collective-permute-start.27 = (f32[512,512]{1,0:T(8,128)S(1)}, f32[512,512]{1,0:T(8,128)S(1)}, u32[]{:S(2)}, u32[]{:S(2)}) collective-permute-start(f32[512,512]{1,0:T(8,128)S(1)} %collective-permute-done.22.refs_1_), channel_id=1, source_target_pairs={{0,8},{4,20},{8,0},{12,28},{16,24},{20,4},{24,16},{28,12},{1,9},{5... | collective-permute-start | bytes 3145736 | tf_op jit(solution)/shard_map/link_sibling/ppermute | solution.py:381
  77.6 4.1 %collective-permute-start.29 = (f32[256,512]{1,0:T(8,128)S(1)}, f32[256,512]{1,0:T(8,128)S(1)}, u32[]{:S(2)}, u32[]{:S(2)}) collective-permute-start(f32[256,512]{1,0:T(8,128)S(1)} %collective-permute-done.26.refs_2_), channel_id=1, source_target_pairs={{0,4},{4,0},{8,12},{12,8},{16,20},{20,16},{24,28},{28,24},{1,5},{5... | collective-permute-start | bytes 1572872 | tf_op jit(solution)/shard_map/core_first/ppermute | solution.py:381
  81.7 11.2 %collective-permute-start.23 = (f32[256,512]{1,0:T(8,128)S(1)}, f32[256,512]{1,0:T(8,128)S(1)}, u32[]{:S(2)}, u32[]{:S(2)}) collective-permute-start(f32[256,512]{1,0:T(8,128)S(1)} %collective-permute-done.21.refs_3_), channel_id=1, source_target_pairs={{0,4},{4,0},{8,12},{12,8},{16,20},{20,16},{24,28},{28,24},{1,5},{5... | collective-permute-start | bytes 1572872 | tf_op jit(solution)/shard_map/core_first/ppermute | solution.py:381
  81.7 16.8 %collective-permute-start.30 = (f32[256,512]{1,0:T(8,128)S(1)}, f32[256,512]{1,0:T(8,128)S(1)}, u32[]{:S(2)}, u32[]{:S(2)}) collective-permute-start(f32[256,512]{1,0:T(8,128)S(1)} %collective-permute-done.29.refs_4_), channel_id=1, source_target_pairs={{0,8},{4,20},{8,0},{12,28},{16,24},{20,4},{24,16},{28,12},{1,9},{5... | collective-permute-start | bytes 1572872 | tf_op jit(solution)/shard_map/link_relayed/ppermute | solution.py:381
  92.9 11.2 %collective-permute-start.28 = (f32[512,512]{1,0:T(8,128)S(1)}, f32[512,512]{1,0:T(8,128)S(1)}, u32[]{:S(2)}, u32[]{:S(2)}) collective-permute-start(f32[512,512]{1,0:T(8,128)S(1)} %collective-permute-done.27.refs_6_), channel_id=1, source_target_pairs={{0,4},{4,0},{8,12},{12,8},{16,20},{20,16},{24,28},{28,24},{1,5},{5... | collective-permute-start | bytes 3145736 | tf_op jit(solution)/shard_map/core_second/ppermute | solution.py:381
  92.9 11.2 %collective-permute-start.24 = (f32[256,512]{1,0:T(8,128)S(1)}, f32[256,512]{1,0:T(8,128)S(1)}, u32[]{:S(2)}, u32[]{:S(2)}) collective-permute-start(f32[256,512]{1,0:T(8,128)S(1)} %collective-permute-done.23.refs_5_), channel_id=1, source_target_pairs={{0,8},{4,20},{8,0},{12,28},{16,24},{20,4},{24,16},{28,12},{1,9},{5... | collective-permute-start | bytes 1572872 | tf_op jit(solution)/shard_map/link_relayed/ppermute | solution.py:381
  98.5 5.6 %collective-permute-start.31 = (f32[256,512]{1,0:T(8,128)S(1)}, f32[256,512]{1,0:T(8,128)S(1)}, u32[]{:S(2)}, u32[]{:S(2)}) collective-permute-start(f32[256,512]{1,0:T(8,128)S(1)} %collective-permute-done.30.refs_1_), channel_id=1, source_target_pairs={{0,4},{4,0},{8,12},{12,8},{16,20},{20,16},{24,28},{28,24},{1,5},{5... | collective-permute-start | bytes 1572872 | tf_op jit(solution)/shard_map/core_relayed/ppermute | solution.py:381
  104.2 1.9 %collective-permute-start.25 = (f32[256,512]{1,0:T(8,128)S(1)}, f32[256,512]{1,0:T(8,128)S(1)}, u32[]{:S(2)}, u32[]{:S(2)}) collective-permute-start(f32[256,512]{1,0:T(8,128)S(1)} %collective-permute-done.24.refs_2_), channel_id=1, source_target_pairs={{0,4},{4,0},{8,12},{12,8},{16,20},{20,16},{24,28},{28,24},{1,5},{5... | collective-permute-start | bytes 1572872 | tf_op jit(solution)/shard_map/core_relayed/ppermute | solution.py:381
  (4 other events, 51.3 us)

commit v21 on v17

--- a/solution.py
+++ b/solution.py
@@ -419,7 +419,7 @@
         block.append(joined)
     block_norm = norm
     norm = sum_call(norm, to_core(norm, "norm"))
-    chip_norms = [over(flipped(mask), norm, "chip_norm") for mask in (6, 4, 2)]
+    chip_norms = [over(flipped(mask), norm, "chip_norm") for mask in (4, 6, 2)]
     grams = gram_call([after(block[0], norm), block[1]])
     sides = [(previous, gram, square) for (previous,), gram, square in zip(sides, grams, squares)]
     sides[0] += tuple(mix_call(*sides[0][:2]))

time: 108 us -> 107 us (level)
  no operation moved by 1% of the time
where the time goes in v21:
time: 107 us
  waiting for transfers between devices  56.6 us (53%)
  starting transfers between devices  26.4 us (25%)
  Pallas kernels  20.7 us (19%)
  local copies, waits for them, and re-layouts  1.9 us (2%)
    ppermute x29, waiting for transfers between devices, over(): return lax.ppermute(value, 'dp', pairs)  54.5 us
    ppermute x29, starting transfers between devices, over(): return lax.ppermute(value, 'dp', pairs)  21.9 us
    pallas_call x20, Pallas kernels, local_call(): pl.pallas_call(kernel, in_specs=[pl.BlockSpec(memory_space=pltpu.SMEM)] *...  15.6 us
    pallas_call x3, Pallas kernels, assemble_call(): pl.pallas_call(kernel, in_specs=in_specs, out_specs=pl.BlockSpec(memory_s...  5.1 us
    ppermute x3, starting transfers between devices, paired_body(): norms.append(lax.ppermute(norm, 'mp', pairs))  4.46 us
  transfers between devices with their start and end apart: 32, of which 14 were waited for; matrix products, arithmetic and copies ran while one was open for 0% of the time, Pallas kernels for 12%

profile of v21, /device:TPU:0, one launch (start us, length us, event | category | flops | bytes accessed | tf_op | source)
XLA Modules:
  0.0 106.5 jit_solution(12849629579088305080)
XLA Ops:
  0.7 1.9 %copy-done = bf16[1,512,3072]{2,1,0:T(8,128)(2,1)S(1)} copy-done((bf16[1,512,3072]{2,1,0:T(8,128)(2,1)S(1)}, bf16[1,512,3072]{2,1,0:T(8,128)(2,1)}, u32[]{:S(2)}) %copy-start) | copy-done | bytes 3145752
  6.2 2.9 %collective-permute-start.6 = (f32[256,512]{1,0:T(8,128)S(1)}, f32[256,512]{1,0:T(8,128)S(1)}, u32[]{:S(2)}, u32[]{:S(2)}) collective-permute-start(f32[256,512]{1,0:T(8,128)S(1)} %add.13), channel_id=1, source_target_pairs={{0,8},{4,20},{8,0},{12,28},{16,24},{20,4},{24,16},{28,12},{1,9},{5... | collective-permute-start | bytes 1572872 | tf_op jit(solution)/shard_map/link_corner/ppermute | solution.py:376
  10.7 1.5 %collective-permute-start.3 = (f32[256,512]{1,0:T(8,128)S(1)}, f32[256,512]{1,0:T(8,128)S(1)}, u32[]{:S(2)}, u32[]{:S(2)}) collective-permute-start(f32[256,512]{1,0:T(8,128)S(1)} %add.11), channel_id=1, source_target_pairs={{0,8},{4,20},{8,0},{12,28},{16,24},{20,4},{24,16},{28,12},{1,9},{5... | collective-permute-start | bytes 1572872 | tf_op jit(solution)/shard_map/link_straight/ppermute | solution.py:376
  12.6 3.6 %collective-permute-done.6.refs_2_ = f32[256,512]{1,0:T(8,128)S(1)} collective-permute-done((f32[256,512]{1,0:T(8,128)S(1)}, f32[256,512]{1,0:T(8,128)S(1)}, u32[]{:S(2)}, u32[]{:S(2)}) %collective-permute-start.6) | collective-permute-done | bytes 524320 | tf_op jit(solution)/shard_map/link_corner/ppermute | solution.py:376
  16.2 2.0 %collective-permute-start.10 = (f32[256,512]{1,0:T(8,128)S(1)}, f32[256,512]{1,0:T(8,128)S(1)}, u32[]{:S(2)}, u32[]{:S(2)}) collective-permute-start(f32[256,512]{1,0:T(8,128)S(1)} %add.15), channel_id=1, source_target_pairs={{0,8},{4,20},{8,0},{12,28},{16,24},{20,4},{24,16},{28,12},{1,9},{5... | collective-permute-start | bytes 1572872 | tf_op jit(solution)/shard_map/link_straight/ppermute | solution.py:376
  18.3 3.5 %collective-permute-done.12.refs_2_ = f32[256,512]{1,0:T(8,128)S(1)} collective-permute-done((f32[256,512]{1,0:T(8,128)S(1)}, f32[256,512]{1,0:T(8,128)S(1)}, u32[]{:S(2)}, u32[]{:S(2)}) %collective-permute-start.12) | collective-permute-done | bytes 524320 | tf_op jit(solution)/shard_map/link_corner/ppermute | solution.py:376
  21.8 2.1 %collective-permute-start.7 = (f32[256,512]{1,0:T(8,128)S(1)}, f32[256,512]{1,0:T(8,128)S(1)}, u32[]{:S(2)}, u32[]{:S(2)}) collective-permute-start(f32[256,512]{1,0:T(8,128)S(1)} %add.14), channel_id=1, source_target_pairs={{0,16},{4,12},{8,24},{12,4},{16,0},{20,28},{24,8},{28,20},{1,17},{... | collective-permute-start | bytes 1572872 | tf_op jit(solution)/shard_map/side_side/ppermute | solution.py:376
  24.1 6.7 %collective-permute-done.3.refs_2_ = f32[256,512]{1,0:T(8,128)S(1)} collective-permute-done((f32[256,512]{1,0:T(8,128)S(1)}, f32[256,512]{1,0:T(8,128)S(1)}, u32[]{:S(2)}, u32[]{:S(2)}) %collective-permute-start.3) | collective-permute-done | bytes 524320 | tf_op jit(solution)/shard_map/link_straight/ppermute | solution.py:376
  30.9 1.5 %square.1 = (f32[512,512]{1,0:T(8,128)S(1)}, f32[512,512]{1,0:T(8,128)S(1)}) custom-call(f32[512,512]{1,0:T(8,128)S(1)} %bitcast.8, f32[512,512]{1,0:T(8,128)S(1)} %bitcast.11), custom_call_target="tpu_custom_call" | custom-call | flops 1610612736 | bytes 4194304 | tf_op jit(solution)/shard_map/square/pallas_call | solution.py:129
  32.4 9.7 %collective-permute-done.10.refs_2_ = f32[256,512]{1,0:T(8,128)S(1)} collective-permute-done((f32[256,512]{1,0:T(8,128)S(1)}, f32[256,512]{1,0:T(8,128)S(1)}, u32[]{:S(2)}, u32[]{:S(2)}) %collective-permute-start.10) | collective-permute-done | bytes 524320 | tf_op jit(solution)/shard_map/link_straight/ppermute | solution.py:376
  42.3 1.4 %collective-permute-done.13.arrival_ref = f32[256,512]{1,0:T(8,128)S(1)} collective-permute-done((f32[256,512]{1,0:T(8,128)S(1)}, f32[256,512]{1,0:T(8,128)S(1)}, u32[]{:S(2)}, u32[]{:S(2)}) %collective-permute-start.13) | collective-permute-done | bytes 524320 | tf_op jit(solution)/shard_map/side_side/ppermute | solution.py:376
  44.4 0.8 collective-permute-done.14.refs_1_
  45.2 2.1 %collective-permute-start.15 = (f32[8,128]{1,0:T(8,128)S(1)}, f32[8,128]{1,0:T(8,128)S(1)}, u32[]{:S(2)}, u32[]{:S(2)}) collective-permute-start(f32[8,128]{1,0:T(8,128)S(1)} %sum.2.refs_0_), channel_id=1, source_target_pairs={{0,16},{4,20},{8,24},{12,28},{16,0},{20,4},{24,8},{28,12},{1,17},{... | collective-permute-start | bytes 12296 | tf_op jit(solution)/shard_map/chip_norm/ppermute | solution.py:376
  47.3 1.4 %collective-permute-start.16 = (f32[8,128]{1,0:T(8,128)S(1)}, f32[8,128]{1,0:T(8,128)S(1)}, u32[]{:S(2)}, u32[]{:S(2)}) collective-permute-start(f32[8,128]{1,0:T(8,128)S(1)} %sum.2.refs_0_), channel_id=1, source_target_pairs={{0,24},{4,28},{8,16},{12,20},{16,8},{20,12},{24,0},{28,4},{1,25},{... | collective-permute-start | bytes 12296 | tf_op jit(solution)/shard_map/chip_norm/ppermute | solution.py:376
  48.8 1.5 %gram.1 = (f32[512,512]{1,0:T(8,128)S(1)}, f32[512,512]{1,0:T(8,128)S(1)}) custom-call(f32[256,512]{1,0:T(8,128)S(1)} %get-tuple-element.74.upper_ref, f32[256,512]{1,0:T(8,128)S(1)} %get-tuple-element.72.lower_ref), custom_call_target="tpu_custom_call" | custom-call | flops 1610612736 | bytes 3145728 | tf_op jit(solution)/shard_map/gram/pallas_call | solution.py:129
  50.3 1.7 %mix.2 = (f32[512,512]{1,0:T(8,128)S(1)}, f32[512,512]{1,0:T(8,128)S(1)}) custom-call(f32[512,512]{1,0:T(8,128)S(1)} %bitcast.9, f32[512,512]{1,0:T(8,128)S(1)} %get-tuple-element.75.gram_ref.refs_1_), custom_call_target="tpu_custom_call" | custom-call | flops 1610612736 | bytes 4194304 | tf_op jit(solution)/shard_map/mix/pallas_call | solution.py:129
  52.3 2.9 %collective-permute-start.18 = (f32[8,128]{1,0:T(8,128)S(1)}, f32[8,128]{1,0:T(8,128)S(1)}, u32[]{:S(2)}, u32[]{:S(2)}) collective-permute-start(f32[8,128]{1,0:T(8,128)S(1)} %sum.3.refs_10_), channel_id=1, source_target_pairs={{0,2},{1,3},{2,0},{3,1},{4,6},{5,7},{6,4},{7,5},{8,10},{9,11},{10,... | collective-permute-start | bytes 12296 | tf_op jit(solution)/shard_map/group_norm/ppermute | solution.py:433
  55.2 1.3 %collective-permute-start.19 = (f32[8,128]{1,0:T(8,128)S(1)}, f32[8,128]{1,0:T(8,128)S(1)}, u32[]{:S(2)}, u32[]{:S(2)}) collective-permute-start(f32[8,128]{1,0:T(8,128)S(1)} %sum.3.refs_10_), channel_id=1, source_target_pairs={{0,3},{1,2},{2,1},{3,0},{4,7},{5,6},{6,5},{7,4},{8,11},{9,10},{10,... | collective-permute-start | bytes 12296 | tf_op jit(solution)/shard_map/group_norm/ppermute | solution.py:433
  56.8 1.7 %mix.3 = (f32[512,512]{1,0:T(8,128)S(1)}, f32[512,512]{1,0:T(8,128)S(1)}) custom-call(f32[512,512]{1,0:T(8,128)S(1)} %bitcast.12, f32[512,512]{1,0:T(8,128)S(1)} %get-tuple-element.78.gram_ref.refs_6_), custom_call_target="tpu_custom_call" | custom-call | flops 1610612736 | bytes 4194304 | tf_op jit(solution)/shard_map/mix/pallas_call | solution.py:129
  58.5 2.1 %collective-permute-done.19.refs_12_ = f32[8,128]{1,0:T(8,128)S(1)} collective-permute-done((f32[8,128]{1,0:T(8,128)S(1)}, f32[8,128]{1,0:T(8,128)S(1)}, u32[]{:S(2)}, u32[]{:S(2)}) %collective-permute-start.19) | collective-permute-done | bytes 4128 | tf_op jit(solution)/shard_map/group_norm/ppermute | solution.py:433
  60.6 6.0 %update.1 = (f32[512,512]{1,0:T(8,128)S(1)}, f32[256,512]{1,0:T(8,128)S(1)}, f32[256,512]{1,0:T(8,128)S(1)}) custom-call(f32[256,512]{1,0:T(8,128)S(1)} %get-tuple-element.74.upper_ref, f32[256,512]{1,0:T(8,128)S(1)} %get-tuple-element.72.lower_ref, f32[8,128]{1,0:T(8,128)S(1)} %get-tuple-element.73.refs_0_.block_norm_ref, f32[512,512]{1,0:T(8,128)S(1)} %bitcast.10, ...), custom_call_target="tpu_custom_call" | custom-call | flops 4831838208 | bytes 13651968 | tf_op jit(solution)/shard_map/update/pallas_call | solution.py:129
  66.7 1.6 %collective-permute-start.26 = (f32[256,512]{1,0:T(8,128)S(1)}, f32[256,512]{1,0:T(8,128)S(1)}, u32[]{:S(2)}, u32[]{:S(2)}) collective-permute-start(f32[256,512]{1,0:T(8,128)S(1)} %get-tuple-element.85), channel_id=1, source_target_pairs={{0,8},{4,20},{8,0},{12,28},{16,24},{20,4},{24,16},{28,12},{1,9},{5... | collective-permute-start | bytes 1572872 | tf_op jit(solution)/shard_map/link_own/ppermute | solution.py:376
  68.8 7.2 %collective-permute-done.26.refs_2_ = f32[256,512]{1,0:T(8,128)S(1)} collective-permute-done((f32[256,512]{1,0:T(8,128)S(1)}, f32[256,512]{1,0:T(8,128)S(1)}, u32[]{:S(2)}, u32[]{:S(2)}) %collective-permute-start.26) | collective-permute-done | bytes 524320 | tf_op jit(solution)/shard_map/link_own/ppermute | solution.py:376
  75.9 1.5 %collective-permute-start.27 = (f32[512,512]{1,0:T(8,128)S(1)}, f32[512,512]{1,0:T(8,128)S(1)}, u32[]{:S(2)}, u32[]{:S(2)}) collective-permute-start(f32[512,512]{1,0:T(8,128)S(1)} %collective-permute-done.22.refs_1_), channel_id=1, source_target_pairs={{0,8},{4,20},{8,0},{12,28},{16,24},{20,4},{24,16},{28,12},{1,9},{5... | collective-permute-start | bytes 3145736 | tf_op jit(solution)/shard_map/link_sibling/ppermute | solution.py:376
  77.4 4.1 %collective-permute-done.21.refs_3_ = f32[256,512]{1,0:T(8,128)S(1)} collective-permute-done((f32[256,512]{1,0:T(8,128)S(1)}, f32[256,512]{1,0:T(8,128)S(1)}, u32[]{:S(2)}, u32[]{:S(2)}) %collective-permute-start.21) | collective-permute-done | bytes 524320 | tf_op jit(solution)/shard_map/link_own/ppermute | solution.py:376
  81.6 1.5 %collective-permute-start.30 = (f32[256,512]{1,0:T(8,128)S(1)}, f32[256,512]{1,0:T(8,128)S(1)}, u32[]{:S(2)}, u32[]{:S(2)}) collective-permute-start(f32[256,512]{1,0:T(8,128)S(1)} %collective-permute-done.29.refs_4_), channel_id=1, source_target_pairs={{0,8},{4,20},{8,0},{12,28},{16,24},{20,4},{24,16},{28,12},{1,9},{5... | collective-permute-start | bytes 1572872 | tf_op jit(solution)/shard_map/link_relayed/ppermute | solution.py:376
  83.1 9.7 %collective-permute-done.27.refs_6_ = f32[512,512]{1,0:T(8,128)S(1)} collective-permute-done((f32[512,512]{1,0:T(8,128)S(1)}, f32[512,512]{1,0:T(8,128)S(1)}, u32[]{:S(2)}, u32[]{:S(2)}) %collective-permute-start.27) | collective-permute-done | bytes 1048608 | tf_op jit(solution)/shard_map/link_sibling/ppermute | solution.py:376
  92.8 1.5 %collective-permute-start.24 = (f32[256,512]{1,0:T(8,128)S(1)}, f32[256,512]{1,0:T(8,128)S(1)}, u32[]{:S(2)}, u32[]{:S(2)}) collective-permute-start(f32[256,512]{1,0:T(8,128)S(1)} %collective-permute-done.23.refs_5_), channel_id=1, source_target_pairs={{0,8},{4,20},{8,0},{12,28},{16,24},{20,4},{24,16},{28,12},{1,9},{5... | collective-permute-start | bytes 1572872 | tf_op jit(solution)/shard_map/link_relayed/ppermute | solution.py:376
  94.3 2.6 %assemble.3.refs_4_ = f32[512,3072]{1,0:T(8,128)} custom-call(s32[7]{0:T(128)S(1)} %pad_add_fusion.places_ref, f32[512,512]{1,0:T(8,128)S(1)} %get-tuple-element.83.refs_0_, f32[512,512]{1,0:T(8,128)S(1)} %collective-permute-done.22.refs_1_, f32[256,512]{1,0:T(8,128)S(1)} %collective-permute-done.26.refs_2_, f32[256,512]{1,0:T(8,128)S(1)} %collective-permute-done.21.refs_3_, ...), custom_call_target="tpu_custom_call" | custom-call | bytes 14680064 | tf_op jit(solution)/shard_map/assemble/pallas_call | solution.py:347
  96.9 1.5 %collective-permute-done.30.refs_1_ = f32[256,512]{1,0:T(8,128)S(1)} collective-permute-done((f32[256,512]{1,0:T(8,128)S(1)}, f32[256,512]{1,0:T(8,128)S(1)}, u32[]{:S(2)}, u32[]{:S(2)}) %collective-permute-start.30) | collective-permute-done | bytes 524320 | tf_op jit(solution)/shard_map/link_relayed/ppermute | solution.py:376
  98.4 5.6 %collective-permute-done.24.refs_2_ = f32[256,512]{1,0:T(8,128)S(1)} collective-permute-done((f32[256,512]{1,0:T(8,128)S(1)}, f32[256,512]{1,0:T(8,128)S(1)}, u32[]{:S(2)}, u32[]{:S(2)}) %collective-permute-start.24) | collective-permute-done | bytes 524320 | tf_op jit(solution)/shard_map/link_relayed/ppermute | solution.py:376
  104.0 1.9 %assemble.4.refs_1_ = f32[512,3072]{1,0:T(8,128)} custom-call(s32[7]{0:T(128)S(1)} %pad_add_fusion.places_ref, f32[512,512]{1,0:T(8,128)S(1)} %collective-permute-done.28.refs_0_, f32[256,512]{1,0:T(8,128)S(1)} %collective-permute-done.30.refs_1_, f32[256,512]{1,0:T(8,128)S(1)} %collective-permute-done.24.refs_2_, ...), custom_call_target="tpu_custom_call", output_to_operand_aliasing={{}: (5, {})} | custom-call | bytes 8388608 | tf_op jit(solution)/shard_map/assemble/pallas_call | solution.py:347
  (64 shorter events, 9.3 us)
Async XLA Ops:
  3.4 2.3 %collective-permute-start.5 = (f32[256,512]{1,0:T(8,128)S(1)}, f32[256,512]{1,0:T(8,128)S(1)}, u32[]{:S(2)}, u32[]{:S(2)}) collective-permute-start(f32[256,512]{1,0:T(8,128)S(1)} %get-tuple-element.62), channel_id=1, source_target_pairs={{0,4},{4,0},{8,12},{12,8},{16,20},{20,16},{24,28},{28,24},{1,5},{5... | collective-permute-start | bytes 1572872 | tf_op jit(solution)/shard_map/core_corner/ppermute | solution.py:376
  3.9 2.3 %collective-permute-start = (f32[256,512]{1,0:T(8,128)S(1)}, f32[256,512]{1,0:T(8,128)S(1)}, u32[]{:S(2)}, u32[]{:S(2)}) collective-permute-start(f32[256,512]{1,0:T(8,128)S(1)} %get-tuple-element.48), channel_id=1, source_target_pairs={{0,4},{4,0},{8,12},{12,8},{16,20},{20,16},{24,28},{28,24},{1,5},{5... | collective-permute-start | bytes 1572872 | tf_op jit(solution)/shard_map/core_corner/ppermute | solution.py:376
  4.0 5.1 %collective-permute-start.2 = (f32[256,512]{1,0:T(8,128)S(1)}, f32[256,512]{1,0:T(8,128)S(1)}, u32[]{:S(2)}, u32[]{:S(2)}) collective-permute-start(f32[256,512]{1,0:T(8,128)S(1)} %get-tuple-element.53), channel_id=1, source_target_pairs={{0,4},{4,0},{8,12},{12,8},{16,20},{20,16},{24,28},{28,24},{1,5},{5... | collective-permute-start | bytes 1572872 | tf_op jit(solution)/shard_map/core_straight/ppermute | solution.py:376
  5.1 4.7 %collective-permute-start.4 = (f32[256,512]{1,0:T(8,128)S(1)}, f32[256,512]{1,0:T(8,128)S(1)}, u32[]{:S(2)}, u32[]{:S(2)}) collective-permute-start(f32[256,512]{1,0:T(8,128)S(1)} %get-tuple-element.60), channel_id=1, source_target_pairs={{0,4},{4,0},{8,12},{12,8},{16,20},{20,16},{24,28},{28,24},{1,5},{5... | collective-permute-start | bytes 1572872 | tf_op jit(solution)/shard_map/core_side/ppermute | solution.py:376
  5.3 5.4 %collective-permute-start.9 = (f32[256,512]{1,0:T(8,128)S(1)}, f32[256,512]{1,0:T(8,128)S(1)}, u32[]{:S(2)}, u32[]{:S(2)}) collective-permute-start(f32[256,512]{1,0:T(8,128)S(1)} %get-tuple-element.68), channel_id=1, source_target_pairs={{0,4},{4,0},{8,12},{12,8},{16,20},{20,16},{24,28},{28,24},{1,5},{5... | collective-permute-start | bytes 1572872 | tf_op jit(solution)/shard_map/core_straight/ppermute | solution.py:376
  5.7 6.5 %collective-permute-start.11 = (f32[256,512]{1,0:T(8,128)S(1)}, f32[256,512]{1,0:T(8,128)S(1)}, u32[]{:S(2)}, u32[]{:S(2)}) collective-permute-start(f32[256,512]{1,0:T(8,128)S(1)} %get-tuple-element.70), channel_id=1, source_target_pairs={{0,4},{4,0},{8,12},{12,8},{16,20},{20,16},{24,28},{28,24},{1,5},{5... | collective-permute-start | bytes 1572872 | tf_op jit(solution)/shard_map/core_side/ppermute | solution.py:376
  6.2 10.0 %collective-permute-start.6 = (f32[256,512]{1,0:T(8,128)S(1)}, f32[256,512]{1,0:T(8,128)S(1)}, u32[]{:S(2)}, u32[]{:S(2)}) collective-permute-start(f32[256,512]{1,0:T(8,128)S(1)} %add.13), channel_id=1, source_target_pairs={{0,8},{4,20},{8,0},{12,28},{16,24},{20,4},{24,16},{28,12},{1,9},{5... | collective-permute-start | bytes 1572872 | tf_op jit(solution)/shard_map/link_corner/ppermute | solution.py:376
  9.1 12.7 %collective-permute-start.12 = (f32[256,512]{1,0:T(8,128)S(1)}, f32[256,512]{1,0:T(8,128)S(1)}, u32[]{:S(2)}, u32[]{:S(2)}) collective-permute-start(f32[256,512]{1,0:T(8,128)S(1)} %add.10), channel_id=1, source_target_pairs={{0,8},{4,20},{8,0},{12,28},{16,24},{20,4},{24,16},{28,12},{1,9},{5... | collective-permute-start | bytes 1572872 | tf_op jit(solution)/shard_map/link_corner/ppermute | solution.py:376
  9.8 14.2 %collective-permute-start.1 = (f32[256,512]{1,0:T(8,128)S(1)}, f32[256,512]{1,0:T(8,128)S(1)}, u32[]{:S(2)}, u32[]{:S(2)}) collective-permute-start(f32[256,512]{1,0:T(8,128)S(1)} %get-tuple-element.51), channel_id=1, source_target_pairs={{0,4},{4,0},{8,12},{12,8},{16,20},{20,16},{24,28},{28,24},{1,5},{5... | collective-permute-start | bytes 1572872 | tf_op jit(solution)/shard_map/core_self/ppermute | solution.py:376
  10.7 20.1 %collective-permute-start.3 = (f32[256,512]{1,0:T(8,128)S(1)}, f32[256,512]{1,0:T(8,128)S(1)}, u32[]{:S(2)}, u32[]{:S(2)}) collective-permute-start(f32[256,512]{1,0:T(8,128)S(1)} %add.11), channel_id=1, source_target_pairs={{0,8},{4,20},{8,0},{12,28},{16,24},{20,4},{24,16},{28,12},{1,9},{5... | collective-permute-start | bytes 1572872 | tf_op jit(solution)/shard_map/link_straight/ppermute | solution.py:376
  12.2 20.1 %collective-permute-start.8 = (f32[256,512]{1,0:T(8,128)S(1)}, f32[256,512]{1,0:T(8,128)S(1)}, u32[]{:S(2)}, u32[]{:S(2)}) collective-permute-start(f32[256,512]{1,0:T(8,128)S(1)} %get-tuple-element.66), channel_id=1, source_target_pairs={{0,4},{4,0},{8,12},{12,8},{16,20},{20,16},{24,28},{28,24},{1,5},{5... | collective-permute-start | bytes 1572872 | tf_op jit(solution)/shard_map/core_self/ppermute | solution.py:376
  16.2 25.8 %collective-permute-start.10 = (f32[256,512]{1,0:T(8,128)S(1)}, f32[256,512]{1,0:T(8,128)S(1)}, u32[]{:S(2)}, u32[]{:S(2)}) collective-permute-start(f32[256,512]{1,0:T(8,128)S(1)} %add.15), channel_id=1, source_target_pairs={{0,8},{4,20},{8,0},{12,28},{16,24},{20,4},{24,16},{28,12},{1,9},{5... | collective-permute-start | bytes 1572872 | tf_op jit(solution)/shard_map/link_straight/ppermute | solution.py:376
  21.8 20.3 %collective-permute-start.7 = (f32[256,512]{1,0:T(8,128)S(1)}, f32[256,512]{1,0:T(8,128)S(1)}, u32[]{:S(2)}, u32[]{:S(2)}) collective-permute-start(f32[256,512]{1,0:T(8,128)S(1)} %add.14), channel_id=1, source_target_pairs={{0,16},{4,12},{8,24},{12,4},{16,0},{20,28},{24,8},{28,20},{1,17},{... | collective-permute-start | bytes 1572872 | tf_op jit(solution)/shard_map/side_side/ppermute | solution.py:376
  24.0 19.8 %collective-permute-start.13 = (f32[256,512]{1,0:T(8,128)S(1)}, f32[256,512]{1,0:T(8,128)S(1)}, u32[]{:S(2)}, u32[]{:S(2)}) collective-permute-start(f32[256,512]{1,0:T(8,128)S(1)} %add.17), channel_id=1, source_target_pairs={{0,16},{4,12},{8,24},{12,4},{16,0},{20,28},{24,8},{28,20},{1,17},{... | collective-permute-start | bytes 1572872 | tf_op jit(solution)/shard_map/side_side/ppermute | solution.py:376
  44.0 1.2 %collective-permute-start.14 = (f32[8,128]{1,0:T(8,128)S(1)}, f32[8,128]{1,0:T(8,128)S(1)}, u32[]{:S(2)}, u32[]{:S(2)}) collective-permute-start(f32[8,128]{1,0:T(8,128)S(1)} %get-tuple-element.73.refs_0_.block_norm_ref), channel_id=1, source_target_pairs={{0,4},{4,0},{8,12},{12,8},{16,20},{20,16},{24,28},{28,24},{1,5},{5... | collective-permute-start | bytes 12296 | tf_op jit(solution)/shard_map/core_norm/ppermute | solution.py:376
  45.2 6.8 %collective-permute-start.15 = (f32[8,128]{1,0:T(8,128)S(1)}, f32[8,128]{1,0:T(8,128)S(1)}, u32[]{:S(2)}, u32[]{:S(2)}) collective-permute-start(f32[8,128]{1,0:T(8,128)S(1)} %sum.2.refs_0_), channel_id=1, source_target_pairs={{0,16},{4,20},{8,24},{12,28},{16,0},{20,4},{24,8},{28,12},{1,17},{... | collective-permute-start | bytes 12296 | tf_op jit(solution)/shard_map/chip_norm/ppermute | solution.py:376
  47.3 4.8 %collective-permute-start.16 = (f32[8,128]{1,0:T(8,128)S(1)}, f32[8,128]{1,0:T(8,128)S(1)}, u32[]{:S(2)}, u32[]{:S(2)}) collective-permute-start(f32[8,128]{1,0:T(8,128)S(1)} %sum.2.refs_0_), channel_id=1, source_target_pairs={{0,24},{4,28},{8,16},{12,20},{16,8},{20,12},{24,0},{28,4},{1,25},{... | collective-permute-start | bytes 12296 | tf_op jit(solution)/shard_map/chip_norm/ppermute | solution.py:376
  48.7 3.6 %collective-permute-start.17 = (f32[8,128]{1,0:T(8,128)S(1)}, f32[8,128]{1,0:T(8,128)S(1)}, u32[]{:S(2)}, u32[]{:S(2)}) collective-permute-start(f32[8,128]{1,0:T(8,128)S(1)} %sum.2.refs_0_), channel_id=1, source_target_pairs={{0,8},{4,12},{8,0},{12,4},{16,24},{20,28},{24,16},{28,20},{1,9},{5... | collective-permute-start | bytes 12296 | tf_op jit(solution)/shard_map/chip_norm/ppermute | solution.py:376
  52.3 6.2 %collective-permute-start.18 = (f32[8,128]{1,0:T(8,128)S(1)}, f32[8,128]{1,0:T(8,128)S(1)}, u32[]{:S(2)}, u32[]{:S(2)}) collective-permute-start(f32[8,128]{1,0:T(8,128)S(1)} %sum.3.refs_10_), channel_id=1, source_target_pairs={{0,2},{1,3},{2,0},{3,1},{4,6},{5,7},{6,4},{7,5},{8,10},{9,11},{10,... | collective-permute-start | bytes 12296 | tf_op jit(solution)/shard_map/group_norm/ppermute | solution.py:433
  55.2 5.4 %collective-permute-start.19 = (f32[8,128]{1,0:T(8,128)S(1)}, f32[8,128]{1,0:T(8,128)S(1)}, u32[]{:S(2)}, u32[]{:S(2)}) collective-permute-start(f32[8,128]{1,0:T(8,128)S(1)} %sum.3.refs_10_), channel_id=1, source_target_pairs={{0,3},{1,2},{2,1},{3,0},{4,7},{5,6},{6,5},{7,4},{8,11},{9,10},{10,... | collective-permute-start | bytes 12296 | tf_op jit(solution)/shard_map/group_norm/ppermute | solution.py:433
  56.5 4.1 %collective-permute-start.20 = (f32[8,128]{1,0:T(8,128)S(1)}, f32[8,128]{1,0:T(8,128)S(1)}, u32[]{:S(2)}, u32[]{:S(2)}) collective-permute-start(f32[8,128]{1,0:T(8,128)S(1)} %sum.3.refs_10_), channel_id=1, source_target_pairs={{0,1},{1,0},{2,3},{3,2},{4,5},{5,4},{6,7},{7,6},{8,9},{9,8},{10,11... | collective-permute-start | bytes 12296 | tf_op jit(solution)/shard_map/group_norm/ppermute | solution.py:433
  66.6 9.3 %collective-permute-start.22 = (f32[512,512]{1,0:T(8,128)S(1)}, f32[512,512]{1,0:T(8,128)S(1)}, u32[]{:S(2)}, u32[]{:S(2)}) collective-permute-start(f32[512,512]{1,0:T(8,128)S(1)} %get-tuple-element.83.refs_0_), channel_id=1, source_target_pairs={{0,4},{4,0},{8,12},{12,8},{16,20},{20,16},{24,28},{28,24},{1,5},{5... | collective-permute-start | bytes 3145736 | tf_op jit(solution)/shard_map/core_own/ppermute | solution.py:376
  66.7 9.2 %collective-permute-start.26 = (f32[256,512]{1,0:T(8,128)S(1)}, f32[256,512]{1,0:T(8,128)S(1)}, u32[]{:S(2)}, u32[]{:S(2)}) collective-permute-start(f32[256,512]{1,0:T(8,128)S(1)} %get-tuple-element.85), channel_id=1, source_target_pairs={{0,8},{4,20},{8,0},{12,28},{16,24},{20,4},{24,16},{28,12},{1,9},{5... | collective-permute-start | bytes 1572872 | tf_op jit(solution)/shard_map/link_own/ppermute | solution.py:376
  68.3 13.3 %collective-permute-start.21 = (f32[256,512]{1,0:T(8,128)S(1)}, f32[256,512]{1,0:T(8,128)S(1)}, u32[]{:S(2)}, u32[]{:S(2)}) collective-permute-start(f32[256,512]{1,0:T(8,128)S(1)} %get-tuple-element.82), channel_id=1, source_target_pairs={{0,8},{4,20},{8,0},{12,28},{16,24},{20,4},{24,16},{28,12},{1,9},{5... | collective-permute-start | bytes 1572872 | tf_op jit(solution)/shard_map/link_own/ppermute | solution.py:376
  75.9 16.8 %collective-permute-start.27 = (f32[512,512]{1,0:T(8,128)S(1)}, f32[512,512]{1,0:T(8,128)S(1)}, u32[]{:S(2)}, u32[]{:S(2)}) collective-permute-start(f32[512,512]{1,0:T(8,128)S(1)} %collective-permute-done.22.refs_1_), channel_id=1, source_target_pairs={{0,8},{4,20},{8,0},{12,28},{16,24},{20,4},{24,16},{28,12},{1,9},{5... | collective-permute-start | bytes 3145736 | tf_op jit(solution)/shard_map/link_sibling/ppermute | solution.py:376
  77.4 4.1 %collective-permute-start.29 = (f32[256,512]{1,0:T(8,128)S(1)}, f32[256,512]{1,0:T(8,128)S(1)}, u32[]{:S(2)}, u32[]{:S(2)}) collective-permute-start(f32[256,512]{1,0:T(8,128)S(1)} %collective-permute-done.26.refs_2_), channel_id=1, source_target_pairs={{0,4},{4,0},{8,12},{12,8},{16,20},{20,16},{24,28},{28,24},{1,5},{5... | collective-permute-start | bytes 1572872 | tf_op jit(solution)/shard_map/core_first/ppermute | solution.py:376
  81.6 11.2 %collective-permute-start.23 = (f32[256,512]{1,0:T(8,128)S(1)}, f32[256,512]{1,0:T(8,128)S(1)}, u32[]{:S(2)}, u32[]{:S(2)}) collective-permute-start(f32[256,512]{1,0:T(8,128)S(1)} %collective-permute-done.21.refs_3_), channel_id=1, source_target_pairs={{0,4},{4,0},{8,12},{12,8},{16,20},{20,16},{24,28},{28,24},{1,5},{5... | collective-permute-start | bytes 1572872 | tf_op jit(solution)/shard_map/core_first/ppermute | solution.py:376
  81.6 16.8 %collective-permute-start.30 = (f32[256,512]{1,0:T(8,128)S(1)}, f32[256,512]{1,0:T(8,128)S(1)}, u32[]{:S(2)}, u32[]{:S(2)}) collective-permute-start(f32[256,512]{1,0:T(8,128)S(1)} %collective-permute-done.29.refs_4_), channel_id=1, source_target_pairs={{0,8},{4,20},{8,0},{12,28},{16,24},{20,4},{24,16},{28,12},{1,9},{5... | collective-permute-start | bytes 1572872 | tf_op jit(solution)/shard_map/link_relayed/ppermute | solution.py:376
  92.8 11.2 %collective-permute-start.28 = (f32[512,512]{1,0:T(8,128)S(1)}, f32[512,512]{1,0:T(8,128)S(1)}, u32[]{:S(2)}, u32[]{:S(2)}) collective-permute-start(f32[512,512]{1,0:T(8,128)S(1)} %collective-permute-done.27.refs_6_), channel_id=1, source_target_pairs={{0,4},{4,0},{8,12},{12,8},{16,20},{20,16},{24,28},{28,24},{1,5},{5... | collective-permute-start | bytes 3145736 | tf_op jit(solution)/shard_map/core_second/ppermute | solution.py:376
  92.8 11.2 %collective-permute-start.24 = (f32[256,512]{1,0:T(8,128)S(1)}, f32[256,512]{1,0:T(8,128)S(1)}, u32[]{:S(2)}, u32[]{:S(2)}) collective-permute-start(f32[256,512]{1,0:T(8,128)S(1)} %collective-permute-done.23.refs_5_), channel_id=1, source_target_pairs={{0,8},{4,20},{8,0},{12,28},{16,24},{20,4},{24,16},{28,12},{1,9},{5... | collective-permute-start | bytes 1572872 | tf_op jit(solution)/shard_map/link_relayed/ppermute | solution.py:376
  98.4 5.6 %collective-permute-start.31 = (f32[256,512]{1,0:T(8,128)S(1)}, f32[256,512]{1,0:T(8,128)S(1)}, u32[]{:S(2)}, u32[]{:S(2)}) collective-permute-start(f32[256,512]{1,0:T(8,128)S(1)} %collective-permute-done.30.refs_1_), channel_id=1, source_target_pairs={{0,4},{4,0},{8,12},{12,8},{16,20},{20,16},{24,28},{28,24},{1,5},{5... | collective-permute-start | bytes 1572872 | tf_op jit(solution)/shard_map/core_relayed/ppermute | solution.py:376
  104.0 1.9 %collective-permute-start.25 = (f32[256,512]{1,0:T(8,128)S(1)}, f32[256,512]{1,0:T(8,128)S(1)}, u32[]{:S(2)}, u32[]{:S(2)}) collective-permute-start(f32[256,512]{1,0:T(8,128)S(1)} %collective-permute-done.24.refs_2_), channel_id=1, source_target_pairs={{0,4},{4,0},{8,12},{12,8},{16,20},{20,16},{24,28},{28,24},{1,5},{5... | collective-permute-start | bytes 1572872 | tf_op jit(solution)/shard_map/core_relayed/ppermute | solution.py:376
  (4 other events, 51.3 us)
